TPU v7x, 32 devices: a whole 2x2x4 slice. The times are simulated.
32 devices in a mesh: batch: 8 (over z, y), proto: 4 (over x, core).
Axes of the slice: x: 2, y: 2, z: 4, core: 2. Of those that a mesh axis runs over, the one named last changes fastest.
Arguments:
- crops: bfloat16 [1536, 1536], P(('batch', 'proto')), may hold values from -6 to 6
- teacher_emb: bfloat16 [1536, 256], P('batch'), may hold values from -4 to 4
- w_first: bfloat16 [1536, 2048], P(None, 'proto'), may hold values from -0.15625 to 0.15625
- b_first: float32 [2048], replicated, may hold values from -3 to 3
- w_second: bfloat16 [2048, 2048], P('proto'), may hold values from -0.125 to 0.125
- b_second: float32 [2048], replicated, may hold values from -3 to 3
- w_third: bfloat16 [2048, 256], P('proto'), may hold values from -0.125 to 0.125
- b_third: float32 [256], replicated, may hold values from -3 to 3
- protos: bfloat16 [65536, 256], P('proto'), may hold values from -60 to 60
Outputs:
- crop_grad: float32 [1536, 256], P(('batch', 'proto'))
All inputs are finite; a program needn't handle non-finite values.
Results may differ from a plain program's by a relative error of at most 0.018.
The roundings to bfloat16 on the way count: a program that leaves them out, or rounds other values in their place, can miss the bound.
Values may be sent and summed in bfloat16 or wider, within the bound.
No kernel may reach another device: no remote copies, remote signals or barrier semaphores. Data moves between devices by JAX's collectives and lax.ppermute only.
A program may use at most 128 MiB of HBM per device.

v0:
```python
import jax
import jax.numpy as jnp
from jax import lax
from jax.sharding import PartitionSpec as P

ITERS = 3


student_temp = 0.1
teacher_temp = 0.07
norm_eps = 1e-06


def scores(left_rows, right_rows):
    return lax.dot_general(
        left_rows, right_rows, (((1,), (1,)), ((), ())), preferred_element_type=jnp.float32
    )


def unit_rows(values):
    lengths = jnp.sqrt(jnp.sum(values * values, axis=1, keepdims=True) + norm_eps)
    return (values / lengths, lengths)


def proto_scales(local_rows, protos_total):
    row_total = lax.psum(local_rows, "batch")
    return 1.0 / (protos_total * row_total)


def body(crops, teacher_emb, w_first, b_first, w_second, b_second, w_third, b_third, protos):
    proto_index = lax.axis_index("proto")
    share_rows = crops.shape[0]
    all_crops = lax.all_gather(crops, "proto", axis=0, tiled=True)
    hidden_share = w_first.shape[1]
    first_bias = lax.dynamic_slice_in_dim(b_first, proto_index * hidden_share, hidden_share)
    h_first = jax.nn.gelu(
        jnp.dot(all_crops, w_first, preferred_element_type=jnp.float32) + first_bias,
        approximate=False,
    ).astype(jnp.bfloat16)
    partial_value = jnp.dot(h_first, w_second, preferred_element_type=jnp.float32)
    pre_second = lax.psum_scatter(partial_value, "proto", scatter_dimension=1, tiled=True)
    second_bias = lax.dynamic_slice_in_dim(b_second, proto_index * hidden_share, hidden_share)
    h_second = jax.nn.gelu(pre_second + second_bias, approximate=False).astype(jnp.bfloat16)
    bottleneck = (
        lax.psum(jnp.dot(h_second, w_third, preferred_element_type=jnp.float32), "proto") + b_third
    )
    unit_all, lengths_all = unit_rows(bottleneck)
    student_emb = unit_all.astype(jnp.bfloat16)
    unit = lax.dynamic_slice_in_dim(unit_all, proto_index * share_rows, share_rows, 0)
    lengths = lax.dynamic_slice_in_dim(lengths_all, proto_index * share_rows, share_rows, 0)
    crops_total = teacher_emb.shape[0] * lax.axis_size("batch")
    protos_total = protos.shape[0] * lax.axis_size("proto")
    teacher_unit = unit_rows(teacher_emb.astype(jnp.float32))[0].astype(jnp.bfloat16)
    teacher_logits = scores(teacher_unit, protos) / teacher_temp
    teacher_top = lax.pmax(jnp.max(teacher_logits, axis=1), "proto")
    weights_e = jnp.exp(teacher_logits - teacher_top[:, None])
    local_rows = jnp.sum(weights_e, axis=0)
    proto_scale = None
    crop_scale = None
    for sweep_step in range(ITERS):
        proto_scale = proto_scales(local_rows, protos_total)
        column_total = lax.psum(
            jnp.dot(weights_e, proto_scale, precision=lax.Precision.HIGHEST), "proto"
        )
        crop_scale = 1.0 / (crops_total * column_total)
        if sweep_step + 1 < ITERS:
            local_rows = jnp.dot(crop_scale, weights_e, precision=lax.Precision.HIGHEST)
    targets = crops_total * weights_e * proto_scale[None, :] * crop_scale[:, None]
    logits = scores(student_emb, protos) / student_temp
    local_top = jnp.max(logits, axis=1)
    row_top = lax.pmax(local_top, "proto")
    shifted = jnp.exp(logits - row_top[:, None])
    row_sum = lax.psum(jnp.sum(shifted, axis=1), "proto")
    probs = shifted / row_sum[:, None]
    difference = (probs - targets).astype(jnp.bfloat16)
    partial_grad = jnp.dot(difference, protos, preferred_element_type=jnp.float32)
    emb_grad = (
        lax.psum_scatter(partial_grad, "proto", scatter_dimension=0, tiled=True) / student_temp
    )
    crop_grad = (emb_grad - unit * jnp.sum(unit * emb_grad, axis=1, keepdims=True)) / lengths
    return crop_grad


def solution(mesh):
    in_specs = (
        P(("batch", "proto"), None),
        P("batch", None),
        P(None, "proto"),
        P(),
        P("proto", None),
        P(),
        P("proto", None),
        P(),
        P("proto", None),
    )
    out_specs = P(("batch", "proto"), None)
    return jax.shard_map(body, mesh=mesh, in_specs=in_specs, out_specs=out_specs, check_vma=False)
```

profile of v0, /device:TPU:0, one launch (start us, length us, event | category | flops | bytes accessed | tf_op | source)
XLA Modules:
  0.0 441.3 jit_solution(18313922657477814900)
XLA Ops:
  6.5 0.0 copy-start
  6.5 0.0 copy-start.1
  6.5 0.0 copy-start.3
  6.5 0.0 reduce-scatter.3.cloned.1.call-start
  6.6 9.3 %all_gather.3 = bf16[192,1536]{1,0:T(8,128)(2,1)S(1)} all-gather(bf16[48,1536]{1,0:T(8,128)(2,1)} %param.9), channel_id=1, replica_groups=mesh['batch'=8,'proto'=4] {'proto'}, dimensions={0}, use_global_device_ids=true | all-gather | bytes 737280 | tf_op jit(solution)/shard_map/all_gather | solution.py:33
  15.9 0.8 dynamic_slice.10
  16.6 0.0 copy-done
  16.6 4.4 fusion.22
  21.0 0.0 reduce-scatter.3.cloned.1.call-update
  21.1 0.0 all-reduce.7.cloned.1.call-start
  21.1 0.8 dynamic_slice.11
  21.9 0.0 copy-done.1
  21.9 0.1 fusion.23
  22.0 28.3 %reduce-scatter.3.cloned.1.call-done = f32[192,512]{1,0:T(8,128)} async-done(((f32[192,2048]{1,0:T(8,128)}), f32[192,512]{1,0:T(8,128)}) %reduce-scatter.3.cloned.1.call-update) | async-done | bytes 393232 | tf_op jit(solution)/shard_map/reduce_scatter | solution.py:41
  50.3 0.0 copy-done.3
  50.3 2.7 fusion.56
  52.9 0.0 all-reduce.7.cloned.1.call-update
  53.0 0.0 copy-start.2
  53.0 0.0 all-reduce.9.cloned.1.call-start
  53.0 10.9 %fusion.127 = (f32[192]{0:T(256)S(1)}, f32[192,16384]{1,0:T(8,128)}) fusion(bf16[16384,256]{1,0:T(8,128)(2,1)} %param.17, bf16[192,256]{1,0:T(8,128)(2,1)S(1)} %copy-done.1, f32[192]{0:T(256)S(1)} %add_sqrt_fusion), kind=kOutput, calls=%fused_computation.164 | convolution fusion | flops 1617051392 | bytes 21071360 | tf_op jit(solution)/shard_map/dot_general | solution.py:15
  63.9 20.9 %all-reduce.7.cloned.1.call-done = f32[192,256]{1,0:T(8,128)} async-done(((f32[192,256]{1,0:T(8,128)}), f32[192,256]{1,0:T(8,128)}) %all-reduce.7.cloned.1.call-update) | async-done | bytes 196624 | tf_op jit(solution)/shard_map/psum | solution.py:45
  84.8 0.0 copy-done.2
  84.8 1.0 multiply_reduce_fusion
  85.9 1.0 add_divide_fusion
  86.9 10.7 %fusion.128 = (f32[192]{0:T(256)S(1)}, f32[192,16384]{1,0:T(8,128)}) fusion(bf16[16384,256]{1,0:T(8,128)(2,1)} %param.17, f32[192,256]{1,0:T(8,128)S(1)} %add_divide_fusion), kind=kOutput, calls=%fused_computation.165 | convolution fusion | flops 1616953088 | bytes 21168896 | tf_op jit(solution)/shard_map/dot_general | solution.py:15
  97.6 5.7 %all-reduce.1 = (f32[192]{0:T(256)S(1)}, f32[192]{0:T(256)S(1)}) all-reduce(f32[192]{0:T(256)S(1)} %get-tuple-element.11, f32[192]{0:T(256)S(1)} %get-tuple-element.13), channel_id=1, replica_groups=mesh['batch'=8,'proto'=4] {'proto'}, use_global_device_ids=true, to_apply=%region_9.0 | all-reduce | flops 384 | bytes 3072 | tf_op jit(solution)/shard_map/pmax | solution.py:55
  103.4 7.3 %fusion.126 = f32[16384]{0:T(1024)} fusion(f32[192,16384]{1,0:T(8,128)} %get-tuple-element.12, f32[192]{0:T(256)S(1)} %get-tuple-element.7), kind=kLoop, calls=%fused_computation.163 | loop fusion | flops 6275072 | bytes 12649216 | tf_op jit(solution)/shard_map/reduce_sum | solution.py:57
  110.7 0.0 all-reduce.9.cloned.1.call-update
  110.7 0.2 all-reduce.11.cloned.1.call-start
  110.9 68.5 %all-reduce.9.cloned.1.call-done = f32[16384]{0:T(1024)} async-done(((f32[16384]{0:T(1024)}), f32[16384]{0:T(1024)}) %all-reduce.9.cloned.1.call-update) | async-done | bytes 65552 | tf_op jit(solution)/shard_map/psum | solution.py:26
  179.4 0.9 multiply_divide_fusion.2
  180.3 13.4 %fusion.125 = f32[1,192]{1,0:T(1,128)S(1)} fusion(f32[16384,1]{0,1:T(1,128)S(1)} %bitcast.25, f32[192,16384]{1,0:T(8,128)} %get-tuple-element.12, f32[192]{0:T(256)S(1)} %get-tuple-element.7), kind=kOutput, calls=%fused_computation.162 | convolution fusion | flops 40894464 | bytes 12649984 | tf_op jit(solution)/shard_map/dot_general | solution.py:63
  193.7 5.7 %psum.59 = f32[192]{0:T(256)S(1)} all-reduce(f32[192]{0:T(256)S(1)} %bitcast.28), channel_id=1, replica_groups=mesh['batch'=8,'proto'=4] {'proto'}, use_global_device_ids=true, to_apply=%region_12.0 | all-reduce | flops 192 | bytes 1536 | tf_op jit(solution)/shard_map/psum | solution.py:62
  199.3 10.7 %fusion.124 = f32[1,16384]{1,0:T(1,128)} fusion(f32[192,1]{0,1:T(1,128)S(1)} %bitcast.29, f32[192,16384]{1,0:T(8,128)} %get-tuple-element.12, f32[192]{0:T(256)S(1)} %get-tuple-element.7), kind=kOutput, calls=%fused_computation.161 | convolution fusion | flops 40894464 | bytes 12649984 | tf_op jit(solution)/shard_map/dot_general | solution.py:67
  210.1 0.0 all-reduce.11.cloned.1.call-update
  210.1 0.3 all-reduce.13.cloned.1.call-start
  210.4 68.5 %all-reduce.11.cloned.1.call-done = f32[16384]{0:T(1024)} async-done(((f32[16384]{0:T(1024)}), f32[16384]{0:T(1024)}) %all-reduce.11.cloned.1.call-update) | async-done | bytes 65552 | tf_op jit(solution)/shard_map/psum | solution.py:26
  278.9 0.9 multiply_divide_fusion.1
  279.8 13.4 %fusion.123 = f32[1,192]{1,0:T(1,128)S(1)} fusion(f32[16384,1]{0,1:T(1,128)S(1)} %bitcast.26, f32[192,16384]{1,0:T(8,128)} %get-tuple-element.12, f32[192]{0:T(256)S(1)} %get-tuple-element.7), kind=kOutput, calls=%fused_computation.160 | convolution fusion | flops 40894464 | bytes 12649984 | tf_op jit(solution)/shard_map/dot_general | solution.py:63
  293.2 5.7 %psum.61 = f32[192]{0:T(256)S(1)} all-reduce(f32[192]{0:T(256)S(1)} %bitcast.30), channel_id=1, replica_groups=mesh['batch'=8,'proto'=4] {'proto'}, use_global_device_ids=true, to_apply=%region_14.0 | all-reduce | flops 192 | bytes 1536 | tf_op jit(solution)/shard_map/psum | solution.py:62
  298.8 10.7 %fusion.122 = f32[1,16384]{1,0:T(1,128)} fusion(f32[192,1]{0,1:T(1,128)S(1)} %bitcast.31, f32[192,16384]{1,0:T(8,128)} %get-tuple-element.12, f32[192]{0:T(256)S(1)} %get-tuple-element.7), kind=kOutput, calls=%fused_computation.159 | convolution fusion | flops 40894464 | bytes 12649984 | tf_op jit(solution)/shard_map/dot_general | solution.py:67
  309.6 0.0 all-reduce.13.cloned.1.call-update
  309.6 0.3 reduce-scatter.5.cloned.1.call-start
  309.9 6.4 %fusion = f32[192]{0:T(256)S(1)} fusion(f32[192,16384]{1,0:T(8,128)} %get-tuple-element.14, f32[192]{0:T(256)S(1)} %get-tuple-element.8), kind=kLoop, calls=%fused_computation.5 | loop fusion | flops 6291264 | bytes 12584448 | tf_op jit(solution)/shard_map/reduce_sum | solution.py:73
  316.3 62.1 %all-reduce.13.cloned.1.call-done = f32[16384]{0:T(1024)} async-done(((f32[16384]{0:T(1024)}), f32[16384]{0:T(1024)}) %all-reduce.13.cloned.1.call-update) | async-done | bytes 65552 | tf_op jit(solution)/shard_map/psum | solution.py:26
  378.4 0.9 broadcast_multiply_fusion
  379.3 13.4 %fusion.121 = f32[1,192]{1,0:T(1,128)S(1)} fusion(f32[16384,1]{0,1:T(1,128)S(1)} %bitcast.22, f32[192,16384]{1,0:T(8,128)} %get-tuple-element.12, f32[192]{0:T(256)S(1)} %get-tuple-element.7), kind=kOutput, calls=%fused_computation.158 | convolution fusion | flops 40894464 | bytes 12649984 | tf_op jit(solution)/shard_map/dot_general | solution.py:63
  392.7 5.7 %all-reduce = (f32[192]{0:T(256)S(1)}, f32[192]{0:T(256)S(1)}) all-reduce(f32[192]{0:T(256)S(1)} %bitcast.27, f32[192]{0:T(256)S(1)} %fusion), channel_id=1, replica_groups=mesh['batch'=8,'proto'=4] {'proto'}, use_global_device_ids=true, to_apply=%region_16.0 | all-reduce | flops 384 | bytes 3072 | tf_op jit(solution)/shard_map/psum | solution.py:62
  398.4 13.6 %fusion.1 = f32[192,256]{1,0:T(8,128)} fusion(bf16[16384,256]{1,0:T(8,128)(2,1)} %param.17, f32[192,16384]{1,0:T(8,128)} %get-tuple-element.14, f32[192]{0:T(256)S(1)} %multiply_divide_fusion.3, f32[16384]{0:T(1024)S(1)} %get-tuple-element.9, f32[192]{0:T(256)S(1)} %get-tuple-element.6, f32[192]{0:T(256)S(1)} %get-tuple-element.8, ...), kind=kOutput, calls=%fused_computation.6 | convolution fusion | flops 1632632832 | bytes 33819648 | tf_op jit(solution)/shard_map/dot_general | solution.py:76
  411.9 0.0 reduce-scatter.5.cloned.1.call-update
  412.0 0.1 dynamic-slice.3
  412.0 20.0 %reduce-scatter.5.cloned.1.call-done = f32[48,256]{1,0:T(8,128)} async-done(((f32[192,256]{1,0:T(8,128)}), f32[48,256]{1,0:T(8,128)}) %reduce-scatter.5.cloned.1.call-update) | async-done | bytes 49168 | tf_op jit(solution)/shard_map/reduce_scatter | solution.py:78
  432.1 0.9 multiply_reduce_fusion.1
  433.0 1.5 subtract_divide_fusion
  (5 shorter events, 0.0 us)
Async XLA Ops:
  6.5 10.1 %copy-start = (bf16[512,2048]{1,0:T(8,128)(2,1)S(1)}, bf16[512,2048]{1,0:T(8,128)(2,1)}, u32[]{:S(2)}) copy-start(bf16[512,2048]{1,0:T(8,128)(2,1)} %param.13) | copy-start | bytes 6291460
  6.5 15.3 %copy-start.1 = (bf16[192,256]{1,0:T(8,128)(2,1)S(1)}, bf16[192,256]{1,0:T(8,128)(2,1)}, u32[]{:S(2)}) copy-start(bf16[192,256]{1,0:T(8,128)(2,1)} %param.10) | copy-start | bytes 294916
  6.5 43.7 %copy-start.3 = (bf16[512,256]{1,0:T(8,128)(2,1)S(1)}, bf16[512,256]{1,0:T(8,128)(2,1)}, u32[]{:S(2)}) copy-start(bf16[512,256]{1,0:T(8,128)(2,1)} %param.15) | copy-start | bytes 786436
  6.5 43.7 %reduce-scatter.3.cloned.1.call-start = ((), (), s32[]{:S(2)}) async-start(), calls=%async_computation.2 | async-start | bytes 1966080 | tf_op jit(solution)/shard_map/reduce_scatter | solution.py:41
  21.1 63.8 %all-reduce.7.cloned.1.call-start = ((), (), s32[]{:S(2)}) async-start(), calls=%async_computation.3 | async-start | bytes 393216 | tf_op jit(solution)/shard_map/psum | solution.py:45
  53.0 31.9 %copy-start.2 = (f32[256]{0:T(256)S(1)}, f32[256]{0:T(256)}, u32[]{:S(2)}) copy-start(f32[256]{0:T(256)} %param.16) | copy-start | bytes 3076
  53.0 126.4 %all-reduce.9.cloned.1.call-start = ((), (), s32[]{:S(2)}) async-start(), calls=%async_computation.4 | async-start | bytes 131072 | tf_op jit(solution)/shard_map/psum | solution.py:26
  110.7 168.2 %all-reduce.11.cloned.1.call-start = ((), (), s32[]{:S(2)}) async-start(), calls=%async_computation.5 | async-start | bytes 131072 | tf_op jit(solution)/shard_map/psum | solution.py:26
  210.1 168.3 %all-reduce.13.cloned.1.call-start = ((), (), s32[]{:S(2)}) async-start(), calls=%async_computation.6 | async-start | bytes 131072 | tf_op jit(solution)/shard_map/psum | solution.py:26
  309.6 122.4 %reduce-scatter.5.cloned.1.call-start = ((), (), s32[]{:S(2)}) async-start(), calls=%async_computation.7 | async-start | bytes 245760 | tf_op jit(solution)/shard_map/reduce_scatter | solution.py:78
Sparse Core Ops, SparseCore 0:
  21.2 29.0 reduce-scatter.2
  53.1 31.6 all-reduce.6
  110.8 68.5 all-reduce.8
  210.2 68.6 all-reduce.10
  309.7 68.6 all-reduce.12
  412.1 19.9 reduce-scatter.4
where the time goes:
time: 442 us; the launch traced here: 441 us
  waiting for transfers between devices  268 us (61%)
  matrix products  104 us (24%)
  blocking collectives  32 us (7%)
  other arithmetic  20.9 us (5%)
  between operations  13.5 us (3%)
    psum x3, waiting for transfers between devices, proto_scales(): row_total = lax.psum(local_rows, 'batch')  199 us
    dot_general x3, matrix products, body(): jnp.dot(weights_e, proto_scale, precision=lax.Precision.HIGHEST)  40.2 us
    reduce_scatter x1, waiting for transfers between devices, body(): lax.psum_scatter(partial_value, 'proto', scatter_dimension=1, tiled=True)  28.3 us
    dot_general x2, matrix products, scores(): lax.dot_general(left_rows, right_rows, (((1,), (1,)), ((), ())), preferre...  21.6 us
    dot_general x2, matrix products, body(): local_rows = jnp.dot(crop_scale, weights_e, precision=lax.Precision.HIGHEST)  21.5 us
    psum x1, waiting for transfers between devices, body(): lax.psum(jnp.dot(h_second, w_third, preferred_element_type=jnp.float32),...  20.9 us
    reduce_scatter x1, waiting for transfers between devices, body(): lax.psum_scatter(partial_grad, 'proto', scatter_dimension=0, tiled=True)  20 us
    psum x3, blocking collectives, body(): lax.psum(jnp.dot(weights_e, proto_scale, precision=lax.Precision.HIGHEST)...  17 us
  transfers between devices with their start and end apart: 6, of which 6 were waited for; matrix products, arithmetic and copies ran while one was open for 4% of the time, Pallas kernels for 0%

commit v1 on v0

v1 whole, which is shorter than its diff:
```python
import jax
import jax.numpy as jnp
from jax import lax
from jax.sharding import PartitionSpec as P

ITERS = 3

student_temp = 0.1
teacher_temp = 0.07
norm_eps = 1e-06


def scores(left_rows, right_rows):
    return lax.dot_general(
        left_rows, right_rows, (((1,), (1,)), ((), ())), preferred_element_type=jnp.float32
    )


def unit_rows(values):
    lengths = jnp.sqrt(jnp.sum(values * values, axis=1, keepdims=True) + norm_eps)
    return (values / lengths, lengths)


def exchange_rows(blocks, axis):
    count = lax.axis_size(axis)
    own = lax.axis_index(axis)
    rows = blocks.shape[0] // count
    parts = [lax.dynamic_slice_in_dim(blocks, own * rows, rows, 0)]
    for step in range(1, count):
        target = lax.rem(own + step, count)
        sent = lax.dynamic_slice_in_dim(blocks, target * rows, rows, 0)
        parts.append(lax.ppermute(sent, axis, [(i, (i + step) % count) for i in range(count)]))
    return parts


def body(crops, teacher_emb, w_first, b_first, w_second, b_second, w_third, b_third, protos):
    batch_index = lax.axis_index("batch")
    proto_index = lax.axis_index("proto")
    batch_size = lax.axis_size("batch")
    proto_size = lax.axis_size("proto")
    share_rows = crops.shape[0]
    group_rows = teacher_emb.shape[0]
    crops_total = group_rows * batch_size
    protos_total = protos.shape[0] * proto_size
    thin = protos.shape[0] // batch_size
    hidden_share = w_first.shape[1]

    all_crops = lax.all_gather(crops, "proto", axis=0, tiled=True)
    w_third_all = lax.all_gather(w_third, "proto", axis=0, tiled=True)
    first_bias = lax.dynamic_slice_in_dim(b_first, proto_index * hidden_share, hidden_share)
    h_first = jax.nn.gelu(
        jnp.dot(all_crops, w_first, preferred_element_type=jnp.float32) + first_bias,
        approximate=False,
    ).astype(jnp.bfloat16)
    partial_value = jnp.dot(h_first, w_second, preferred_element_type=jnp.float32)

    teacher_unit = unit_rows(teacher_emb.astype(jnp.float32))[0].astype(jnp.bfloat16)
    unit_share = lax.dynamic_slice_in_dim(teacher_unit, proto_index * share_rows, share_rows, 0)
    all_unit = lax.all_gather(unit_share, ("batch", "proto"), axis=0, tiled=True)
    thin_protos = lax.dynamic_slice_in_dim(protos, batch_index * thin, thin, 0)
    thin_logits = scores(thin_protos, all_unit) / teacher_temp
    teacher_top = lax.pmax(jnp.max(thin_logits, axis=0), ("batch", "proto"))
    thin_weights = jnp.exp(thin_logits - teacher_top[None, :])

    pre_second = sum(exchange_rows(partial_value, "proto"))
    h_second = jax.nn.gelu(pre_second + b_second, approximate=False).astype(jnp.bfloat16)
    bottleneck = jnp.dot(h_second, w_third_all, preferred_element_type=jnp.float32) + b_third
    unit, lengths = unit_rows(bottleneck)
    student_emb = lax.all_gather(unit.astype(jnp.bfloat16), "proto", axis=0, tiled=True)
    logits = scores(student_emb, protos) / student_temp
    local_top = jnp.max(logits, axis=1, keepdims=True)
    shifted = jnp.exp(logits - local_top)
    local_total = jnp.sum(shifted, axis=1, keepdims=True)
    attract = jnp.dot(shifted.astype(jnp.bfloat16), protos, preferred_element_type=jnp.float32)
    attract = jnp.concatenate(
        [attract, jnp.broadcast_to(local_total, (group_rows, 128)), jnp.broadcast_to(local_top, (group_rows, 128))],
        axis=1,
    )
    attract_parts = exchange_rows(attract, "proto")

    row_total = jnp.sum(thin_weights, axis=1)
    for sweep_step in range(ITERS):
        proto_scale = 1.0 / (protos_total * row_total)
        if sweep_step + 1 < ITERS:
            column_total = lax.psum(
                jnp.sum(thin_weights * proto_scale[:, None], axis=0), ("batch", "proto")
            )
            crop_scale = 1.0 / (crops_total * column_total)
            row_total = jnp.sum(thin_weights * crop_scale[None, :], axis=1)
    all_scale = lax.all_gather(proto_scale, "batch", axis=0, tiled=True)

    own_top = lax.dynamic_slice_in_dim(teacher_top, batch_index * group_rows, group_rows, 0)
    weights_e = jnp.exp(scores(teacher_unit, protos) / teacher_temp - own_top[:, None])
    scaled = weights_e * all_scale[None, :]
    column_part = jnp.sum(scaled, axis=1, keepdims=True)
    repel = jnp.dot(scaled.astype(jnp.bfloat16), protos, preferred_element_type=jnp.float32)
    repel = jnp.concatenate([repel, jnp.broadcast_to(column_part, (group_rows, 128))], axis=1)
    repel_sum = sum(exchange_rows(repel, "proto"))

    width = protos.shape[1]
    tops = [part[:, width + 128 : width + 129] for part in attract_parts]
    row_top = tops[0]
    for top in tops[1:]:
        row_top = jnp.maximum(row_top, top)
    attract_sum = sum(part[:, :width] * jnp.exp(top - row_top) for part, top in zip(attract_parts, tops))
    row_sum = sum(part[:, width : width + 1] * jnp.exp(top - row_top) for part, top in zip(attract_parts, tops))
    emb_grad = (
        attract_sum / row_sum - repel_sum[:, :width] / repel_sum[:, width : width + 1]
    ) / student_temp
    crop_grad = (emb_grad - unit * jnp.sum(unit * emb_grad, axis=1, keepdims=True)) / lengths
    return crop_grad


def solution(mesh):
    in_specs = (
        P(("batch", "proto"), None),
        P("batch", None),
        P(None, "proto"),
        P(),
        P("proto", None),
        P(),
        P("proto", None),
        P(),
        P("proto", None),
    )
    out_specs = P(("batch", "proto"), None)
    return jax.shard_map(body, mesh=mesh, in_specs=in_specs, out_specs=out_specs, check_vma=False)
```

time: 442 us -> 327 us (0.74)
  waiting for transfers between devices: 268 us -> 7.72 us
  blocking collectives: 32 us -> 218 us
  matrix products: 104 us -> 39 us
  other arithmetic: 20.9 us -> 34.1 us
  starting transfers between devices: 0.87 us -> 9.27 us
    psum x4 -> x0, waiting for transfers between devices: 220 us -> none  [the longest x3 199 us: proto_scales(): row_total = lax.psum(local_rows, 'batch')]
    all_gather x0 -> x3, blocking collectives: none -> 90.6 us  [the longest x1 54.3 us: body(): lax.all_gather(unit_share, ('batch', 'proto'), axis=0, tiled=True)]
    dot_general x7 -> x3, matrix products: 78 us -> 13.4 us  [the longest x1 5.31 us: body(): jnp.dot(scaled.astype(jnp.bfloat16), protos, preferred_element_type=jnp.f...]
    psum x3 -> x2, blocking collectives: 17 us -> 81.1 us  [body(): lax.psum(jnp.sum(thin_weights * proto_scale[:, None], axis=0), ('batch',...]
    reduce_scatter x2 -> x0, waiting for transfers between devices: 48.3 us -> none  [the longest x1 28.3 us: body(): lax.psum_scatter(partial_value, 'proto', scatter_dimension=1, tiled=True)]
    pmax x1, blocking collectives: 5.73 us -> 36.9 us  [body(): teacher_top = lax.pmax(jnp.max(thin_logits, axis=0), ('batch', 'proto'))]
    reduce_sum x2 -> x6, other arithmetic: 13.7 us -> 32.6 us  [the longest x2 14.2 us: body(): row_total = jnp.sum(thin_weights * crop_scale[None, :], axis=1)]
    ppermute x0 -> x9, starting transfers between devices: none -> 9.26 us  [exchange_rows(): lax.ppermute(sent, axis, [(i, (i + step) % count) for i in range(count)])]
  transfers between devices with their start and end apart: 6 -> 10, of which waited for: 6 -> 4; matrix products, arithmetic and copies ran while one was open for 4% -> 18% of each run, Pallas kernels for 0% -> 0%
where the time goes in v1:
time: 327 us; the launch traced here: 326 us
  blocking collectives  218 us (67%)
  matrix products  39 us (12%)
  other arithmetic  34.1 us (10%)
  between operations  13.6 us (4%)
  starting transfers between devices  9.27 us (3%)
  waiting for transfers between devices  7.72 us (2%)
  local copies, waits for them, and re-layouts  4.76 us (1%)
    psum x2, blocking collectives, body(): lax.psum(jnp.sum(thin_weights * proto_scale[:, None], axis=0), ('batch',...  81.1 us
    all_gather x1, blocking collectives, body(): lax.all_gather(unit_share, ('batch', 'proto'), axis=0, tiled=True)  54.3 us
    pmax x1, blocking collectives, body(): teacher_top = lax.pmax(jnp.max(thin_logits, axis=0), ('batch', 'proto'))  36.9 us
    all_gather x1, blocking collectives, body(): all_scale = lax.all_gather(proto_scale, 'batch', axis=0, tiled=True)  30.7 us
    dot_general x3, matrix products, scores(): lax.dot_general(left_rows, right_rows, (((1,), (1,)), ((), ())), preferre...  21.1 us
    reduce_sum x2, other arithmetic, body(): row_total = jnp.sum(thin_weights * crop_scale[None, :], axis=1)  14.2 us
    reduce_sum x2, other arithmetic, body(): jnp.sum(thin_weights * proto_scale[:, None], axis=0)  9.51 us
    ppermute x9, starting transfers between devices, exchange_rows(): lax.ppermute(sent, axis, [(i, (i + step) % count) for i in range(count)])  9.26 us
  transfers between devices with their start and end apart: 10, of which 4 were waited for; matrix products, arithmetic and copies ran while one was open for 18% of the time, Pallas kernels for 0%

profile of v1, /device:TPU:0, one launch (start us, length us, event | category | flops | bytes accessed | tf_op | source)
XLA Modules:
  0.0 326.3 jit_solution(13133625999502515596)
XLA Ops:
  6.5 0.0 copy-start
  6.5 0.0 copy-start.2
  6.5 0.0 all-gather.2.cloned.1.call-start
  6.5 0.7 all-gather.2.cloned.1.call-update
  7.3 9.2 %all_gather.15 = bf16[192,1536]{1,0:T(8,128)(2,1)S(1)} all-gather(bf16[48,1536]{1,0:T(8,128)(2,1)} %param.9), channel_id=1, replica_groups=mesh['batch'=8,'proto'=4] {'proto'}, dimensions={0}, use_global_device_ids=true | all-gather | bytes 737280 | tf_op jit(solution)/shard_map/all_gather | solution.py:48
  16.5 0.8 dynamic_slice.48
  17.2 0.0 copy-done
  17.2 4.5 %fusion.33 = f32[192,2048]{1,0:T(8,128)} fusion(bf16[512,2048]{1,0:T(8,128)(2,1)S(1)} %copy-done, bf16[192,1536]{1,0:T(8,128)(2,1)S(1)} %all_gather.15, bf16[1536,512]{1,0:T(8,128)(2,1)} %param.11, f32[512]{0:T(512)S(1)} %dynamic_slice.48), kind=kOutput, calls=%fused_computation.67 | convolution fusion | flops 711131136 | bytes 5834752 | tf_op jit(solution)/shard_map/dot_general | solution.py:55
  21.7 2.2 constant_dynamic-slice_fusion.6
  23.9 1.1 collective-permute-start.2
  25.0 0.9 collective-permute-start.1
  25.9 0.0 collective-permute-start
  25.9 0.0 copy-done.2
  25.9 0.1 fusion.34
  26.1 0.1 fusion.35
  26.2 54.3 %all_gather.18 = bf16[1536,256]{1,0:T(8,128)(2,1)S(1)} all-gather(bf16[48,256]{1,0:T(8,128)(2,1)S(1)} %constant_dynamic-slice_fusion), channel_id=1, replica_groups=mesh['batch'=8,'proto'=4] {'batch','proto'}, dimensions={0}, use_global_device_ids=true | all-gather | bytes 811008 | tf_op jit(solution)/shard_map/all_gather | solution.py:59
  80.4 7.6 %multiply_reduce_fusion.4 = (f32[1536]{0:T(1024)S(1)}, f32[2048,1536]{1,0:T(8,128)}) fusion(bf16[1536,256]{1,0:T(8,128)(2,1)S(1)} %all_gather.18, bf16[16384,256]{1,0:T(8,128)(2,1)} %param.17, s32[]{:T(128)S(6)} %select_n.35), kind=kOutput, calls=%fused_computation.11 | convolution fusion | flops 1616902656 | bytes 14424068 | tf_op jit(solution)/shard_map/dot_general | solution.py:14
  88.1 36.9 %pmax.7 = f32[1536]{0:T(1024)S(1)} all-reduce(f32[1536]{0:T(1024)S(1)} %get-tuple-element.23), channel_id=1, replica_groups=mesh['batch'=8,'proto'=4] {'batch','proto'}, use_global_device_ids=true, to_apply=%region_5.0 | all-reduce | flops 1536 | bytes 12288 | tf_op jit(solution)/shard_map/pmax | solution.py:62
  124.9 0.0 copy-start.1
  124.9 6.8 %fusion.10 = f32[2048]{0:T(1024)S(1)} fusion(f32[1536]{0:T(1024)S(1)} %pmax.7, f32[2048,1536]{1,0:T(8,128)} %get-tuple-element.24), kind=kLoop, calls=%fused_computation.18 | loop fusion | flops 9435136 | bytes 12597248 | tf_op jit(solution)/shard_map/reduce_sum | solution.py:81
  131.8 1.3 copy-done.1
  133.1 3.1 multiply_reduce_fusion.3
  136.2 41.5 %psum.14 = f32[1536]{0:T(1024)S(1)} all-reduce(f32[1536]{0:T(1024)S(1)} %multiply_reduce_fusion.3), channel_id=1, replica_groups=mesh['batch'=8,'proto'=4] {'batch','proto'}, use_global_device_ids=true, to_apply=%region_8.0 | all-reduce | flops 1536 | bytes 12288 | tf_op jit(solution)/shard_map/psum | solution.py:85
  177.7 7.1 %multiply_reduce_fusion.2 = f32[2048]{0:T(1024)S(1)} fusion(f32[1536]{0:T(1024)S(1)} %multiply_divide_fusion.3, f32[1536]{0:T(1024)S(1)} %pmax.7, f32[2048,1536]{1,0:T(8,128)} %get-tuple-element.24), kind=kLoop, calls=%fused_computation.7 | loop fusion | flops 12580864 | bytes 12603392 | tf_op jit(solution)/shard_map/reduce_sum | solution.py:89
  184.8 6.4 %multiply_reduce_fusion.1 = f32[1536]{0:T(1024)S(1)} fusion(f32[2048]{0:T(1024)S(1)} %multiply_divide_fusion.2, f32[1536]{0:T(1024)S(1)} %pmax.7, f32[2048,1536]{1,0:T(8,128)} %get-tuple-element.24), kind=kLoop, calls=%fused_computation.6 | loop fusion | flops 12581376 | bytes 12603392 | tf_op jit(solution)/shard_map/reduce_sum | solution.py:86
  191.2 39.7 %psum.15 = f32[1536]{0:T(1024)S(1)} all-reduce(f32[1536]{0:T(1024)S(1)} %multiply_reduce_fusion.1), channel_id=1, replica_groups=mesh['batch'=8,'proto'=4] {'batch','proto'}, use_global_device_ids=true, to_apply=%region_11.0 | all-reduce | flops 1536 | bytes 12288 | tf_op jit(solution)/shard_map/psum | solution.py:85
  230.8 7.1 %multiply_reduce_fusion = f32[2048]{0:T(1024)S(1)} fusion(f32[1536]{0:T(1024)S(1)} %multiply_divide_fusion.1, f32[1536]{0:T(1024)S(1)} %pmax.7, f32[2048,1536]{1,0:T(8,128)} %get-tuple-element.24), kind=kLoop, calls=%fused_computation.5 | loop fusion | flops 12580864 | bytes 12603392 | tf_op jit(solution)/shard_map/reduce_sum | solution.py:89
  238.0 30.7 %all_gather.19 = f32[16384]{0:T(1024)S(1)} all-gather(f32[2048]{0:T(1024)S(1)} %multiply_divide_fusion), channel_id=1, replica_groups=mesh['batch'=8,'proto'=4] {'batch'}, dimensions={0}, use_global_device_ids=true | all-gather | bytes 73728 | tf_op jit(solution)/shard_map/all_gather | solution.py:90
  268.7 0.1 dynamic_slice.59
  268.7 7.2 %fusion.153 = (f32[192]{0:T(256)S(1)}, bf16[192,16384]{1,0:T(8,128)(2,1)S(1)}) fusion(f32[16384]{0:T(1024)S(1)} %all_gather.19, f32[192]{0:T(256)S(1)} %dynamic_slice.59, bf16[192,256]{1,0:T(8,128)(2,1)S(1)} %fusion.35, bf16[16384,256]{1,0:T(8,128)(2,1)} %param.17), kind=kOutput, calls=%fused_computation.224 | convolution fusion | flops 1626341120 | bytes 14845440 | tf_op jit(solution)/shard_map/dot_general | solution.py:14
  275.9 0.0 copy-start.3
  276.0 0.0 copy-start.4
  276.0 5.3 %fusion.7 = f32[192,256]{1,0:T(8,128)S(1)} fusion(bf16[16384,256]{1,0:T(8,128)(2,1)} %param.17, bf16[192,16384]{1,0:T(8,128)(2,1)S(1)} %get-tuple-element.26), kind=kOutput, calls=%fused_computation.15 | convolution fusion | flops 1610612736 | bytes 14876672 | tf_op jit(solution)/shard_map/dot_general | solution.py:96
  281.3 0.1 broadcast_in_dim.8
  281.4 0.1 collective-permute-start.8
  281.5 2.3 collective-permute-start.7
  283.8 0.0 collective-permute-done.8
  283.8 2.7 collective-permute-start.6
  286.5 1.6 collective-permute-done.7
  288.1 0.2 collective-permute-done.6
  288.3 0.0 collective-permute-done.2
  288.3 0.0 collective-permute-done.1
  288.3 0.0 collective-permute-done
  288.3 0.0 all-gather.2.cloned.1.call-done
  288.3 0.0 copy-done.3
  288.3 0.0 copy-done.4
  288.4 2.8 multiply_reduce_fusion.6
  291.2 0.1 fusion.151
  291.3 5.6 %all_gather.17 = bf16[192,256]{1,0:T(8,128)(2,1)S(1)} all-gather(bf16[48,256]{1,0:T(8,128)(2,1)S(1)} %fusion.151), channel_id=1, replica_groups=mesh['batch'=8,'proto'=4] {'proto'}, dimensions={0}, use_global_device_ids=true | all-gather | bytes 122880 | tf_op jit(solution)/shard_map/all_gather | solution.py:69
  296.9 6.3 %fusion.154 = (f32[192]{0:T(256)S(1)}, f32[192,16384]{1,0:T(8,128)S(1)}) fusion(bf16[192,256]{1,0:T(8,128)(2,1)S(1)} %all_gather.17, bf16[16384,256]{1,0:T(8,128)(2,1)} %param.17), kind=kOutput, calls=%fused_computation.225 | convolution fusion | flops 1616903936 | bytes 21070592 | tf_op jit(solution)/shard_map/dot_general | solution.py:14
  303.2 2.0 fusion.3
  305.3 5.2 %fusion.5 = f32[192,256]{1,0:T(8,128)S(1)} fusion(bf16[16384,256]{1,0:T(8,128)(2,1)} %param.17, f32[192,16384]{1,0:T(8,128)S(1)} %get-tuple-element.28, f32[192]{0:T(256)S(1)} %get-tuple-element.27), kind=kOutput, calls=%fused_computation.14 | convolution fusion | flops 1616904192 | bytes 21168896 | tf_op jit(solution)/shard_map/dot_general | solution.py:74
  310.5 0.1 broadcast_in_dim.7
  310.6 0.1 broadcast_in_dim.6
  310.7 1.9 collective-permute-start.5
  312.7 0.1 collective-permute-start.4
  312.8 0.2 collective-permute-start.3
  313.0 0.1 slice_reduce_fusion
  313.1 2.6 collective-permute-done.5
  315.7 2.6 collective-permute-done.4
  318.3 0.0 collective-permute-done.3
  318.3 0.2 fusion.88
  318.5 0.2 multiply_reduce_fusion.5
  318.7 0.7 subtract_divide_fusion
  (12 shorter events, 0.2 us)
Async XLA Ops:
  6.5 10.7 %copy-start = (bf16[512,2048]{1,0:T(8,128)(2,1)S(1)}, bf16[512,2048]{1,0:T(8,128)(2,1)}, u32[]{:S(2)}) copy-start(bf16[512,2048]{1,0:T(8,128)(2,1)} %param.13) | copy-start | bytes 6291460
  6.5 19.4 %copy-start.2 = (bf16[192,256]{1,0:T(8,128)(2,1)S(1)}, bf16[192,256]{1,0:T(8,128)(2,1)}, u32[]{:S(2)}) copy-start(bf16[192,256]{1,0:T(8,128)(2,1)} %param.10) | copy-start | bytes 294916
  6.5 281.8 %all-gather.2.cloned.1.call-start = ((), (), s32[]{:S(2)}) async-start(), calls=%async_computation | async-start | bytes 1310720 | tf_op jit(solution)/shard_map/all_gather | solution.py:49
  23.9 264.3 %collective-permute-start.2 = (f32[48,2048]{1,0:T(8,128)}, f32[48,2048]{1,0:T(8,128)}, u32[]{:S(2)}, u32[]{:S(2)}) collective-permute-start(f32[48,2048]{1,0:T(8,128)} %get-tuple-element.13), channel_id=1, source_target_pairs={{0,3},{1,0},{2,1},{3,2},{4,7},{5,4},{6,5},{7,6},{8,11},{9,8},{10,9... | collective-permute-start | bytes 1179656 | tf_op jit(solution)/shard_map/ppermute | solution.py:32
  25.0 263.3 %collective-permute-start.1 = (f32[48,2048]{1,0:T(8,128)}, f32[48,2048]{1,0:T(8,128)}, u32[]{:S(2)}, u32[]{:S(2)}) collective-permute-start(f32[48,2048]{1,0:T(8,128)} %get-tuple-element.14), channel_id=1, source_target_pairs={{0,2},{1,3},{2,0},{3,1},{4,6},{5,7},{6,4},{7,5},{8,10},{9,11},{10,... | collective-permute-start | bytes 1179656 | tf_op jit(solution)/shard_map/ppermute | solution.py:32
  25.9 262.4 %collective-permute-start = (f32[48,2048]{1,0:T(8,128)S(1)}, f32[48,2048]{1,0:T(8,128)}, u32[]{:S(2)}, u32[]{:S(2)}) collective-permute-start(f32[48,2048]{1,0:T(8,128)S(1)} %get-tuple-element.12), channel_id=1, source_target_pairs={{0,1},{1,2},{2,3},{3,0},{4,5},{5,6},{6,7},{7,4},{8,9},{9,10},{10,1... | collective-permute-start | bytes 1179656 | tf_op jit(solution)/shard_map/ppermute | solution.py:32
  124.9 8.2 %copy-start.1 = (f32[2048,1536]{1,0:T(8,128)S(1)}, f32[2048,1536]{1,0:T(8,128)}, u32[]{:S(2)}) copy-start(f32[2048,1536]{1,0:T(8,128)} %get-tuple-element.24) | copy-start | bytes 37748740
  275.9 12.4 %copy-start.3 = (f32[2048]{0:T(1024)S(1)}, f32[2048]{0:T(1024)}, u32[]{:S(2)}) copy-start(f32[2048]{0:T(1024)} %param.14) | copy-start | bytes 24580
  276.0 12.4 %copy-start.4 = (f32[256]{0:T(256)S(1)}, f32[256]{0:T(256)}, u32[]{:S(2)}) copy-start(f32[256]{0:T(256)} %param.16) | copy-start | bytes 3076
  281.4 2.4 collective-permute-start.8
  281.5 6.6 %collective-permute-start.7 = (f32[48,384]{1,0:T(8,128)S(1)}, f32[48,384]{1,0:T(8,128)S(1)}, u32[]{:S(2)}, u32[]{:S(2)}) collective-permute-start(f32[48,384]{1,0:T(8,128)S(1)} %get-tuple-element.19), channel_id=1, source_target_pairs={{0,2},{1,3},{2,0},{3,1},{4,6},{5,7},{6,4},{7,5},{8,10},{9,11},{10,... | collective-permute-start | bytes 221192 | tf_op jit(solution)/shard_map/ppermute | solution.py:32
  283.8 4.4 %collective-permute-start.6 = (f32[48,384]{1,0:T(8,128)S(1)}, f32[48,384]{1,0:T(8,128)S(1)}, u32[]{:S(2)}, u32[]{:S(2)}) collective-permute-start(f32[48,384]{1,0:T(8,128)S(1)} %get-tuple-element.18), channel_id=1, source_target_pairs={{0,1},{1,2},{2,3},{3,0},{4,5},{5,6},{6,7},{7,4},{8,9},{9,10},{10,1... | collective-permute-start | bytes 221192 | tf_op jit(solution)/shard_map/ppermute | solution.py:32
  310.7 4.9 %collective-permute-start.5 = (f32[48,512]{1,0:T(8,128)S(1)}, f32[48,512]{1,0:T(8,128)S(1)}, u32[]{:S(2)}, u32[]{:S(2)}) collective-permute-start(f32[48,512]{1,0:T(8,128)S(1)} %get-tuple-element.16), channel_id=1, source_target_pairs={{0,3},{1,0},{2,1},{3,2},{4,7},{5,4},{6,5},{7,6},{8,11},{9,8},{10,9... | collective-permute-start | bytes 294920 | tf_op jit(solution)/shard_map/ppermute | solution.py:32
  312.7 5.6 %collective-permute-start.4 = (f32[48,512]{1,0:T(8,128)S(1)}, f32[48,512]{1,0:T(8,128)S(1)}, u32[]{:S(2)}, u32[]{:S(2)}) collective-permute-start(f32[48,512]{1,0:T(8,128)S(1)} %get-tuple-element.17), channel_id=1, source_target_pairs={{0,2},{1,3},{2,0},{3,1},{4,6},{5,7},{6,4},{7,5},{8,10},{9,11},{10,... | collective-permute-start | bytes 294920 | tf_op jit(solution)/shard_map/ppermute | solution.py:32
  312.8 5.5 %collective-permute-start.3 = (f32[48,512]{1,0:T(8,128)S(1)}, f32[48,512]{1,0:T(8,128)S(1)}, u32[]{:S(2)}, u32[]{:S(2)}) collective-permute-start(f32[48,512]{1,0:T(8,128)S(1)} %get-tuple-element.15), channel_id=1, source_target_pairs={{0,1},{1,2},{2,3},{3,0},{4,5},{5,6},{6,7},{7,4},{8,9},{9,10},{10,1... | collective-permute-start | bytes 294920 | tf_op jit(solution)/shard_map/ppermute | solution.py:32
Sparse Core Ops, SparseCore 0:
  8.9 19.4 all-gather.1

commit v2 on v1

--- a/solution.py
+++ b/solution.py
@@ -33,6 +33,26 @@
     return parts
 
 
+def spread(values, axes):
+    count = lax.axis_size(axes)
+    copies = jnp.broadcast_to(values[None], (count,) + values.shape)
+    return lax.all_to_all(copies, axes, 0, 0, tiled=True)
+
+
+def butterfly(values, axis, combine):
+    count = lax.axis_size(axis)
+    step = 1
+    while step < count:
+        other = lax.ppermute(values, axis, [(i, i ^ step) for i in range(count)])
+        values = combine(values, other, (lax.axis_index(axis) // step) % 2)
+        step *= 2
+    return values
+
+
+def in_order(mine, other, upper):
+    return jnp.where(upper == 0, jnp.concatenate([mine, other]), jnp.concatenate([other, mine]))
+
+
 def body(crops, teacher_emb, w_first, b_first, w_second, b_second, w_third, b_third, protos):
     batch_index = lax.axis_index("batch")
     proto_index = lax.axis_index("proto")
@@ -56,10 +76,11 @@
 
     teacher_unit = unit_rows(teacher_emb.astype(jnp.float32))[0].astype(jnp.bfloat16)
     unit_share = lax.dynamic_slice_in_dim(teacher_unit, proto_index * share_rows, share_rows, 0)
-    all_unit = lax.all_gather(unit_share, ("batch", "proto"), axis=0, tiled=True)
+    lanes = butterfly(unit_share[None], "batch", in_order)
+    all_unit = lax.all_gather(lanes, "proto", axis=1, tiled=True).reshape(crops_total, -1)
     thin_protos = lax.dynamic_slice_in_dim(protos, batch_index * thin, thin, 0)
     thin_logits = scores(thin_protos, all_unit) / teacher_temp
-    teacher_top = lax.pmax(jnp.max(thin_logits, axis=0), ("batch", "proto"))
+    teacher_top = jnp.max(spread(jnp.max(thin_logits, axis=0), ("batch", "proto")), axis=0)
     thin_weights = jnp.exp(thin_logits - teacher_top[None, :])
 
     pre_second = sum(exchange_rows(partial_value, "proto"))
@@ -82,12 +103,16 @@
     for sweep_step in range(ITERS):
         proto_scale = 1.0 / (protos_total * row_total)
         if sweep_step + 1 < ITERS:
-            column_total = lax.psum(
-                jnp.sum(thin_weights * proto_scale[:, None], axis=0), ("batch", "proto")
-            )
+            column_part = jnp.sum(thin_weights * proto_scale[:, None], axis=0)
+            if sweep_step == 0:
+                column_total = jnp.sum(spread(column_part, ("batch", "proto")), axis=0)
+            else:
+                column_total = butterfly(
+                    lax.psum(column_part, "proto"), "batch", lambda mine, other, upper: mine + other
+                )
             crop_scale = 1.0 / (crops_total * column_total)
             row_total = jnp.sum(thin_weights * crop_scale[None, :], axis=1)
-    all_scale = lax.all_gather(proto_scale, "batch", axis=0, tiled=True)
+    all_scale = spread(proto_scale, "batch").reshape(-1)
 
     own_top = lax.dynamic_slice_in_dim(teacher_top, batch_index * group_rows, group_rows, 0)
     weights_e = jnp.exp(scores(teacher_unit, protos) / teacher_temp - own_top[:, None])

time: 327 us -> 196 us (0.60)
  blocking collectives: 218 us -> 57 us
  waiting for transfers between devices: 7.72 us -> 22.3 us
  starting transfers between devices: 9.27 us -> 20.7 us
    all_gather x2 -> x1, blocking collectives: 85 us -> 8.94 us  [body(): lax.all_gather(lanes, 'proto', axis=1, tiled=True).reshape(crops_total, -1)]
    psum x2 -> x1, blocking collectives: 81.1 us -> 6.41 us  [body(): lax.psum(column_part, 'proto')]
    pmax x1 -> x0, blocking collectives: 36.9 us -> none  [body(): teacher_top = lax.pmax(jnp.max(thin_logits, axis=0), ('batch', 'proto'))]
    all_to_all x0 -> x2, blocking collectives: none -> 26 us  [spread(): return lax.all_to_all(copies, axes, 0, 0, tiled=True)]
    ppermute x0 -> x6, starting transfers between devices: none -> 10.3 us  [butterfly(): other = lax.ppermute(values, axis, [(i, i ^ step) for i in range(count)])]
    ppermute x0 -> x6, waiting for transfers between devices: none -> 8.98 us  [butterfly(): other = lax.ppermute(values, axis, [(i, i ^ step) for i in range(count)])]
    all_to_all x0 -> x1, starting transfers between devices: none -> 5.32 us  [spread(): return lax.all_to_all(copies, axes, 0, 0, tiled=True)]
    ppermute x9, starting transfers between devices: 9.26 us -> 5.07 us  [exchange_rows(): lax.ppermute(sent, axis, [(i, (i + step) % count) for i in range(count)])]
  transfers between devices with their start and end apart: 10 -> 17, of which waited for: 4 -> 11; matrix products, arithmetic and copies ran while one was open for 18% -> 14% of each run, Pallas kernels for 0% -> 0%
where the time goes in v2:
time: 196 us; the launch traced here: 195 us
  blocking collectives  57 us (29%)
  matrix products  39.3 us (20%)
  other arithmetic  36.7 us (19%)
  waiting for transfers between devices  22.3 us (11%)
  starting transfers between devices  20.7 us (11%)
  between operations  13.7 us (7%)
  local copies, waits for them, and re-layouts  5.5 us (3%)
    all_to_all x2, blocking collectives, spread(): return lax.all_to_all(copies, axes, 0, 0, tiled=True)  26 us
    dot_general x3, matrix products, scores(): lax.dot_general(left_rows, right_rows, (((1,), (1,)), ((), ())), preferre...  21.2 us
    reduce_sum x2, other arithmetic, body(): row_total = jnp.sum(thin_weights * crop_scale[None, :], axis=1)  14.3 us
    ppermute x6, starting transfers between devices, butterfly(): other = lax.ppermute(values, axis, [(i, i ^ step) for i in range(count)])  10.3 us
    all_gather x1, blocking collectives, body(): all_crops = lax.all_gather(crops, 'proto', axis=0, tiled=True)  10.2 us
    ppermute x9, waiting for transfers between devices, exchange_rows(): lax.ppermute(sent, axis, [(i, (i + step) % count) for i in range(count)])  9.98 us
    reduce_sum x2, other arithmetic, body(): column_part = jnp.sum(thin_weights * proto_scale[:, None], axis=0)  9.52 us
    ppermute x6, waiting for transfers between devices, butterfly(): other = lax.ppermute(values, axis, [(i, i ^ step) for i in range(count)])  8.98 us
  transfers between devices with their start and end apart: 17, of which 11 were waited for; matrix products, arithmetic and copies ran while one was open for 14% of the time, Pallas kernels for 0%

profile of v2, /device:TPU:0, one launch (start us, length us, event | category | flops | bytes accessed | tf_op | source)
XLA Modules:
  0.0 195.3 jit_solution(9497467714618280081)
XLA Ops:
  6.5 1.2 fusion.34
  7.7 1.0 fusion.35
  8.7 3.0 %collective-permute-start.6 = (bf16[1,48,256]{2,1,0:T(8,128)(2,1)S(1)}, bf16[1,48,256]{2,1,0:T(8,128)(2,1)S(1)}, u32[]{:S(2)}, u32[]{:S(2)}) collective-permute-start(bf16[1,48,256]{2,1,0:T(8,128)(2,1)S(1)} %dynamic-slice_bitcast_fusion), channel_id=1, source_target_pairs={{0,4},{4,0},{8,12},{12,8},{16,20},{20,16},{24,28},{28,24},{1,5},{5... | collective-permute-start | bytes 73736 | tf_op jit(solution)/shard_map/ppermute | solution.py:46
  11.8 1.8 collective-permute-done.6
  13.6 2.1 %collective-permute-start.7 = (bf16[2,48,256]{2,1,0:T(8,128)(2,1)S(1)}, bf16[2,48,256]{2,1,0:T(8,128)(2,1)S(1)}, u32[]{:S(2)}, u32[]{:S(2)}) collective-permute-start(bf16[2,48,256]{2,1,0:T(8,128)(2,1)S(1)} %maximum_select_fusion.2), channel_id=1, source_target_pairs={{0,8},{4,12},{8,0},{12,4},{16,24},{20,28},{24,16},{28,20},{1,9},{5... | collective-permute-start | bytes 147464 | tf_op jit(solution)/shard_map/ppermute | solution.py:46
  15.7 2.1 %collective-permute-done.7 = bf16[2,48,256]{2,1,0:T(8,128)(2,1)S(1)} collective-permute-done((bf16[2,48,256]{2,1,0:T(8,128)(2,1)S(1)}, bf16[2,48,256]{2,1,0:T(8,128)(2,1)S(1)}, u32[]{:S(2)}, u32[]{:S(2)}) %collective-permute-start.7) | collective-permute-done | bytes 49184 | tf_op jit(solution)/shard_map/ppermute | solution.py:46
  17.8 3.1 %collective-permute-start.8 = (bf16[4,48,256]{2,1,0:T(8,128)(2,1)S(1)}, bf16[4,48,256]{2,1,0:T(8,128)(2,1)S(1)}, u32[]{:S(2)}, u32[]{:S(2)}) collective-permute-start(bf16[4,48,256]{2,1,0:T(8,128)(2,1)S(1)} %maximum_select_fusion.1), channel_id=1, source_target_pairs={{0,16},{4,20},{8,24},{12,28},{16,0},{20,4},{24,8},{28,12},{1,17},{... | collective-permute-start | bytes 294920 | tf_op jit(solution)/shard_map/ppermute | solution.py:46
  20.9 2.6 %collective-permute-done.8 = bf16[4,48,256]{2,1,0:T(8,128)(2,1)S(1)} collective-permute-done((bf16[4,48,256]{2,1,0:T(8,128)(2,1)S(1)}, bf16[4,48,256]{2,1,0:T(8,128)(2,1)S(1)}, u32[]{:S(2)}, u32[]{:S(2)}) %collective-permute-start.8) | collective-permute-done | bytes 98336 | tf_op jit(solution)/shard_map/ppermute | solution.py:46
  23.5 8.9 %all_gather.15 = bf16[8,192,256]{2,1,0:T(8,128)(2,1)S(1)} all-gather(bf16[8,48,256]{2,1,0:T(8,128)(2,1)S(1)} %maximum_select_fusion), channel_id=1, replica_groups=mesh['batch'=8,'proto'=4] {'proto'}, dimensions={1}, use_global_device_ids=true | all-gather | bytes 983040 | tf_op jit(solution)/shard_map/all_gather | solution.py:80
  32.5 7.6 %multiply_reduce_fusion.4 = (f32[1536]{0:T(1024)S(1)}, f32[2048,1536]{1,0:T(8,128)}) fusion(bf16[1536,256]{1,0:T(8,128)(2,1)S(1)} %bitcast.16, bf16[16384,256]{1,0:T(8,128)(2,1)} %param.17, s32[]{:T(128)S(6)} %select_n.82), kind=kOutput, calls=%fused_computation.11 | convolution fusion | flops 1616902656 | bytes 14424068 | tf_op jit(solution)/shard_map/dot_general | solution.py:14
  40.1 0.1 broadcast_in_dim.17
  40.2 14.5 %all_to_all.18 = f32[32,1,1536]{2,1,0:T(1,128)S(1)} all-to-all(f32[32,1,1536]{2,1,0:T(1,128)S(1)} %broadcast_in_dim.17), channel_id=1, replica_groups=mesh['batch'=8,'proto'=4] {'batch','proto'}, dimensions={0} | all-to-all | bytes 393216 | tf_op jit(solution)/shard_map/all_to_all | solution.py:39
  54.7 0.1 reduce_max.29
  54.9 6.8 %fusion.10 = f32[2048]{0:T(1024)S(1)} fusion(f32[1536]{0:T(1024)S(1)} %reduce_max.29, f32[2048,1536]{1,0:T(8,128)} %get-tuple-element.24), kind=kLoop, calls=%fused_computation.18 | loop fusion | flops 9435136 | bytes 12597248 | tf_op jit(solution)/shard_map/reduce_sum | solution.py:102
  61.7 1.3 copy-done.1
  63.0 3.1 %multiply_reduce_fusion.3 = f32[1536]{0:T(1024)S(1)} fusion(f32[2048]{0:T(1024)S(1)} %multiply_divide_fusion.4, f32[1536]{0:T(1024)S(1)} %reduce_max.29, f32[2048,1536]{1,0:T(8,128)S(1)} %copy-done.1), kind=kLoop, calls=%fused_computation.8 | loop fusion | flops 12581376 | bytes 12603392 | tf_op jit(solution)/shard_map/reduce_sum | solution.py:106
  66.2 0.1 broadcast_in_dim.18
  66.3 11.4 %all_to_all.19 = f32[32,1,1536]{2,1,0:T(1,128)S(1)} all-to-all(f32[32,1,1536]{2,1,0:T(1,128)S(1)} %broadcast_in_dim.18), channel_id=1, replica_groups=mesh['batch'=8,'proto'=4] {'batch','proto'}, dimensions={0} | all-to-all | bytes 393216 | tf_op jit(solution)/shard_map/all_to_all | solution.py:39
  77.7 0.1 reduce_sum.104
  77.8 7.1 %multiply_reduce_fusion.2 = f32[2048]{0:T(1024)S(1)} fusion(f32[1536]{0:T(1024)S(1)} %multiply_divide_fusion.3, f32[1536]{0:T(1024)S(1)} %reduce_max.29, f32[2048,1536]{1,0:T(8,128)} %get-tuple-element.24), kind=kLoop, calls=%fused_computation.7 | loop fusion | flops 12580864 | bytes 12603392 | tf_op jit(solution)/shard_map/reduce_sum | solution.py:114
  85.0 6.4 %multiply_reduce_fusion.1 = f32[1536]{0:T(1024)S(1)} fusion(f32[2048]{0:T(1024)S(1)} %multiply_divide_fusion.2, f32[1536]{0:T(1024)S(1)} %reduce_max.29, f32[2048,1536]{1,0:T(8,128)} %get-tuple-element.24), kind=kLoop, calls=%fused_computation.6 | loop fusion | flops 12581376 | bytes 12603392 | tf_op jit(solution)/shard_map/reduce_sum | solution.py:106
  91.4 6.4 %psum.7 = f32[1536]{0:T(1024)S(1)} all-reduce(f32[1536]{0:T(1024)S(1)} %multiply_reduce_fusion.1), channel_id=1, replica_groups=mesh['batch'=8,'proto'=4] {'proto'}, use_global_device_ids=true, to_apply=%region_11.12 | all-reduce | flops 1536 | bytes 12288 | tf_op jit(solution)/shard_map/psum | solution.py:111
  97.8 1.3 collective-permute-start.9
  99.1 2.4 %collective-permute-done.9 = f32[1536]{0:T(1024)S(1)} collective-permute-done((f32[1536]{0:T(1024)S(1)}, f32[1536]{0:T(1024)S(1)}, u32[]{:S(2)}, u32[]{:S(2)}) %collective-permute-start.9) | collective-permute-done | bytes 6176 | tf_op jit(solution)/shard_map/ppermute | solution.py:46
  101.5 0.8 collective-permute-start.10
  102.3 10.2 %all_gather.12 = bf16[192,1536]{1,0:T(8,128)(2,1)S(1)} all-gather(bf16[48,1536]{1,0:T(8,128)(2,1)S(1)} %copy-done.2), channel_id=1, replica_groups=mesh['batch'=8,'proto'=4] {'proto'}, dimensions={0}, use_global_device_ids=true | all-gather | bytes 737280 | tf_op jit(solution)/shard_map/all_gather | solution.py:68
  112.5 0.8 dynamic_slice.48
  113.2 0.0 collective-permute-start.11
  113.3 4.4 %fusion.33 = f32[192,2048]{1,0:T(8,128)} fusion(bf16[512,2048]{1,0:T(8,128)(2,1)S(1)} %copy-done, bf16[192,1536]{1,0:T(8,128)(2,1)S(1)} %all_gather.12, bf16[1536,512]{1,0:T(8,128)(2,1)} %param.11, f32[512]{0:T(512)S(1)} %dynamic_slice.48), kind=kOutput, calls=%fused_computation.67 | convolution fusion | flops 711131136 | bytes 5834752 | tf_op jit(solution)/shard_map/dot_general | solution.py:75
  117.7 0.1 collective-permute-done.11
  117.8 7.1 %multiply_reduce_fusion = f32[2048]{0:T(1024)S(1)} fusion(f32[1536]{0:T(1024)S(1)} %multiply_divide_fusion.1, f32[1536]{0:T(1024)S(1)} %reduce_max.29, f32[2048,1536]{1,0:T(8,128)} %get-tuple-element.24), kind=kLoop, calls=%fused_computation.5 | loop fusion | flops 12580864 | bytes 12603392 | tf_op jit(solution)/shard_map/reduce_sum | solution.py:114
  124.9 0.7 broadcast_in_dim.19
  125.6 5.3 %all-to-all-start.2 = ((f32[8,1,2048]{2,1,0:T(1,128)}), f32[8,1,2048]{2,1,0:T(1,128)S(1)}, u32[]{:S(2)}, u32[]{:S(2)}) async-start(f32[8,1,2048]{2,1,0:T(1,128)} %broadcast_in_dim.19), calls=%async_computation.2 | async-start | bytes 131072 | tf_op jit(solution)/shard_map/all_to_all | solution.py:39
  130.9 2.1 %constant_dynamic-slice_fusion.5 = (f32[48,2048]{1,0:T(8,128)S(1)}, f32[48,2048]{1,0:T(8,128)}, f32[48,2048]{1,0:T(8,128)S(1)}) fusion(f32[192,2048]{1,0:T(8,128)} %fusion.33, s32[]{:T(128)S(6)} %select_n.79, s32[]{:T(128)S(6)} %select_n.81, s32[]{:T(128)S(6)} %select_n.80), kind=kLoop, calls=%fused_computation.162 | loop fusion | bytes 2359308 | tf_op jit(solution)/shard_map/dynamic_slice | solution.py:31
  133.0 0.2 collective-permute-start.2
  133.2 1.2 collective-permute-start.1
  134.4 0.1 dynamic_slice.59
  134.5 3.3 %all-to-all-done.2 = f32[8,1,2048]{2,1,0:T(1,128)S(1)} async-done(((f32[8,1,2048]{2,1,0:T(1,128)}), f32[8,1,2048]{2,1,0:T(1,128)S(1)}, u32[]{:S(2)}, u32[]{:S(2)}) %all-to-all-start.2) | async-done | bytes 65568 | tf_op jit(solution)/shard_map/all_to_all | solution.py:39
  137.8 7.2 %fusion.153 = (f32[192]{0:T(256)S(1)}, bf16[192,16384]{1,0:T(8,128)(2,1)S(1)}) fusion(f32[16384]{0:T(1024)S(1)} %bitcast.17, f32[192]{0:T(256)S(1)} %dynamic_slice.59, bf16[192,256]{1,0:T(8,128)(2,1)S(1)} %fusion.35, bf16[16384,256]{1,0:T(8,128)(2,1)} %param.17), kind=kOutput, calls=%fused_computation.227 | convolution fusion | flops 1626341120 | bytes 14845440 | tf_op jit(solution)/shard_map/dot_general | solution.py:14
  145.1 5.3 %fusion.7 = f32[192,256]{1,0:T(8,128)S(1)} fusion(bf16[16384,256]{1,0:T(8,128)(2,1)} %param.17, bf16[192,16384]{1,0:T(8,128)(2,1)S(1)} %get-tuple-element.26), kind=kOutput, calls=%fused_computation.15 | convolution fusion | flops 1610612736 | bytes 14876672 | tf_op jit(solution)/shard_map/dot_general | solution.py:121
  150.4 0.1 broadcast_in_dim.20
  150.5 0.1 collective-permute-start.14
  150.6 0.9 collective-permute-start.13
  151.5 1.5 collective-permute-done.14
  152.9 0.7 collective-permute-start.12
  153.6 1.7 collective-permute-done.13
  155.3 1.5 collective-permute-done.12
  156.9 0.0 all-gather.2.cloned.1.call-done
  157.0 2.9 %multiply_reduce_fusion.6 = (f32[48]{0:T(128)S(1)}, f32[48,256]{1,0:T(8,128)S(1)}) fusion(f32[256]{0:T(256)} %param.16, bf16[2048,256]{1,0:T(8,128)(2,1)} %all-gather.2.cloned.1.call-done, f32[48,2048]{1,0:T(8,128)} %collective-permute-done.2, f32[48,2048]{1,0:T(8,128)} %collective-permute-done.1, f32[48,2048]{1,0:T(8,128)} %collective-permute-done, ...), kind=kOutput, calls=%fused_computation.130 | convolution fusion | flops 57151440 | bytes 2680004 | tf_op jit(solution)/shard_map/dot_general | solution.py:88
  159.8 0.1 fusion.151
  159.9 5.6 %all_gather.14 = bf16[192,256]{1,0:T(8,128)(2,1)S(1)} all-gather(bf16[48,256]{1,0:T(8,128)(2,1)S(1)} %fusion.151), channel_id=1, replica_groups=mesh['batch'=8,'proto'=4] {'proto'}, dimensions={0}, use_global_device_ids=true | all-gather | bytes 122880 | tf_op jit(solution)/shard_map/all_gather | solution.py:90
  165.5 6.3 %fusion.154 = (f32[192]{0:T(256)S(1)}, f32[192,16384]{1,0:T(8,128)S(1)}) fusion(bf16[192,256]{1,0:T(8,128)(2,1)S(1)} %all_gather.14, bf16[16384,256]{1,0:T(8,128)(2,1)} %param.17), kind=kOutput, calls=%fused_computation.228 | convolution fusion | flops 1616903936 | bytes 21070592 | tf_op jit(solution)/shard_map/dot_general | solution.py:14
  171.8 2.3 %fusion.3 = f32[192]{0:T(256)S(1)} fusion(f32[192,16384]{1,0:T(8,128)S(1)} %get-tuple-element.28, f32[192]{0:T(256)S(1)} %get-tuple-element.27), kind=kLoop, calls=%fused_computation.12 | loop fusion | flops 6291264 | bytes 12584448 | tf_op jit(solution)/shard_map/reduce_sum | solution.py:94
  174.1 5.5 %fusion.5 = f32[192,256]{1,0:T(8,128)S(1)} fusion(bf16[16384,256]{1,0:T(8,128)(2,1)} %param.17, f32[192,16384]{1,0:T(8,128)S(1)} %get-tuple-element.28, f32[192]{0:T(256)S(1)} %get-tuple-element.27), kind=kOutput, calls=%fused_computation.14 | convolution fusion | flops 1616904192 | bytes 21168896 | tf_op jit(solution)/shard_map/dot_general | solution.py:95
  179.7 0.1 broadcast_in_dim.15
  179.8 0.1 broadcast_in_dim.14
  179.9 0.4 collective-permute-start.5
  180.3 1.6 collective-permute-start.4
  182.0 0.1 slice_reduce_fusion
  182.1 1.3 collective-permute-done.5
  183.3 4.0 %collective-permute-done.4 = f32[48,512]{1,0:T(8,128)S(1)} collective-permute-done((f32[48,512]{1,0:T(8,128)S(1)}, f32[48,512]{1,0:T(8,128)S(1)}, u32[]{:S(2)}, u32[]{:S(2)}) %collective-permute-start.4) | collective-permute-done | bytes 98336 | tf_op jit(solution)/shard_map/ppermute | solution.py:32
  187.3 0.2 fusion.88
  187.5 0.2 multiply_reduce_fusion.5
  187.7 0.7 subtract_divide_fusion
  (33 shorter events, 0.3 us)
Async XLA Ops:
  6.5 106.7 %copy-start = (bf16[512,2048]{1,0:T(8,128)(2,1)S(1)}, bf16[512,2048]{1,0:T(8,128)(2,1)}, u32[]{:S(2)}) copy-start(bf16[512,2048]{1,0:T(8,128)(2,1)} %param.13) | copy-start | bytes 6291460
  6.5 150.4 %all-gather.2.cloned.1.call-start = ((), (), s32[]{:S(2)}) async-start(), calls=%async_computation.3 | async-start | bytes 1310720 | tf_op jit(solution)/shard_map/all_gather | solution.py:69
  8.7 4.8 %collective-permute-start.6 = (bf16[1,48,256]{2,1,0:T(8,128)(2,1)S(1)}, bf16[1,48,256]{2,1,0:T(8,128)(2,1)S(1)}, u32[]{:S(2)}, u32[]{:S(2)}) collective-permute-start(bf16[1,48,256]{2,1,0:T(8,128)(2,1)S(1)} %dynamic-slice_bitcast_fusion), channel_id=1, source_target_pairs={{0,4},{4,0},{8,12},{12,8},{16,20},{20,16},{24,28},{28,24},{1,5},{5... | collective-permute-start | bytes 73736 | tf_op jit(solution)/shard_map/ppermute | solution.py:46
  13.6 4.2 %collective-permute-start.7 = (bf16[2,48,256]{2,1,0:T(8,128)(2,1)S(1)}, bf16[2,48,256]{2,1,0:T(8,128)(2,1)S(1)}, u32[]{:S(2)}, u32[]{:S(2)}) collective-permute-start(bf16[2,48,256]{2,1,0:T(8,128)(2,1)S(1)} %maximum_select_fusion.2), channel_id=1, source_target_pairs={{0,8},{4,12},{8,0},{12,4},{16,24},{20,28},{24,16},{28,20},{1,9},{5... | collective-permute-start | bytes 147464 | tf_op jit(solution)/shard_map/ppermute | solution.py:46
  17.8 5.7 %collective-permute-start.8 = (bf16[4,48,256]{2,1,0:T(8,128)(2,1)S(1)}, bf16[4,48,256]{2,1,0:T(8,128)(2,1)S(1)}, u32[]{:S(2)}, u32[]{:S(2)}) collective-permute-start(bf16[4,48,256]{2,1,0:T(8,128)(2,1)S(1)} %maximum_select_fusion.1), channel_id=1, source_target_pairs={{0,16},{4,20},{8,24},{12,28},{16,0},{20,4},{24,8},{28,12},{1,17},{... | collective-permute-start | bytes 294920 | tf_op jit(solution)/shard_map/ppermute | solution.py:46
  54.9 8.2 %copy-start.1 = (f32[2048,1536]{1,0:T(8,128)S(1)}, f32[2048,1536]{1,0:T(8,128)}, u32[]{:S(2)}) copy-start(f32[2048,1536]{1,0:T(8,128)} %get-tuple-element.24) | copy-start | bytes 37748740
  77.8 24.4 %copy-start.2 = (bf16[48,1536]{1,0:T(8,128)(2,1)S(1)}, bf16[48,1536]{1,0:T(8,128)(2,1)}, u32[]{:S(2)}) copy-start(bf16[48,1536]{1,0:T(8,128)(2,1)} %param.9) | copy-start | bytes 442372
  97.8 3.7 %collective-permute-start.9 = (f32[1536]{0:T(1024)S(1)}, f32[1536]{0:T(1024)S(1)}, u32[]{:S(2)}, u32[]{:S(2)}) collective-permute-start(f32[1536]{0:T(1024)S(1)} %psum.7), channel_id=1, source_target_pairs={{0,4},{4,0},{8,12},{12,8},{16,20},{20,16},{24,28},{28,24},{1,5},{5... | collective-permute-start | bytes 18440 | tf_op jit(solution)/shard_map/ppermute | solution.py:46
  101.5 11.7 %collective-permute-start.10 = (f32[1536]{0:T(1024)S(1)}, f32[1536]{0:T(1024)S(1)}, u32[]{:S(2)}, u32[]{:S(2)}) collective-permute-start(f32[1536]{0:T(1024)S(1)} %add.183), channel_id=1, source_target_pairs={{0,8},{4,12},{8,0},{12,4},{16,24},{20,28},{24,16},{28,20},{1,9},{5... | collective-permute-start | bytes 18440 | tf_op jit(solution)/shard_map/ppermute | solution.py:46
  113.2 4.6 %collective-permute-start.11 = (f32[1536]{0:T(1024)S(1)}, f32[1536]{0:T(1024)S(1)}, u32[]{:S(2)}, u32[]{:S(2)}) collective-permute-start(f32[1536]{0:T(1024)S(1)} %add.184), channel_id=1, source_target_pairs={{0,16},{4,20},{8,24},{12,28},{16,0},{20,4},{24,8},{28,12},{1,17},{... | collective-permute-start | bytes 18440 | tf_op jit(solution)/shard_map/ppermute | solution.py:46
  125.6 12.2 %all-to-all-start.2 = ((f32[8,1,2048]{2,1,0:T(1,128)}), f32[8,1,2048]{2,1,0:T(1,128)S(1)}, u32[]{:S(2)}, u32[]{:S(2)}) async-start(f32[8,1,2048]{2,1,0:T(1,128)} %broadcast_in_dim.19), calls=%async_computation.2 | async-start | bytes 131072 | tf_op jit(solution)/shard_map/all_to_all | solution.py:39
  133.0 23.9 %collective-permute-start.2 = (f32[48,2048]{1,0:T(8,128)}, f32[48,2048]{1,0:T(8,128)}, u32[]{:S(2)}, u32[]{:S(2)}) collective-permute-start(f32[48,2048]{1,0:T(8,128)} %get-tuple-element.13), channel_id=1, source_target_pairs={{0,3},{1,0},{2,1},{3,2},{4,7},{5,4},{6,5},{7,6},{8,11},{9,8},{10,9... | collective-permute-start | bytes 1179656 | tf_op jit(solution)/shard_map/ppermute | solution.py:32
  133.2 23.7 %collective-permute-start.1 = (f32[48,2048]{1,0:T(8,128)S(1)}, f32[48,2048]{1,0:T(8,128)}, u32[]{:S(2)}, u32[]{:S(2)}) collective-permute-start(f32[48,2048]{1,0:T(8,128)S(1)} %get-tuple-element.14), channel_id=1, source_target_pairs={{0,2},{1,3},{2,0},{3,1},{4,6},{5,7},{6,4},{7,5},{8,10},{9,11},{10,... | collective-permute-start | bytes 1179656 | tf_op jit(solution)/shard_map/ppermute | solution.py:32
  134.4 22.5 %collective-permute-start = (f32[48,2048]{1,0:T(8,128)S(1)}, f32[48,2048]{1,0:T(8,128)}, u32[]{:S(2)}, u32[]{:S(2)}) collective-permute-start(f32[48,2048]{1,0:T(8,128)S(1)} %get-tuple-element.12), channel_id=1, source_target_pairs={{0,1},{1,2},{2,3},{3,0},{4,5},{5,6},{6,7},{7,4},{8,9},{9,10},{10,1... | collective-permute-start | bytes 1179656 | tf_op jit(solution)/shard_map/ppermute | solution.py:32
  145.1 11.9 %copy-start.3 = (f32[2048]{0:T(1024)S(1)}, f32[2048]{0:T(1024)}, u32[]{:S(2)}) copy-start(f32[2048]{0:T(1024)} %param.14) | copy-start | bytes 24580
  150.5 2.4 %collective-permute-start.14 = (f32[48,384]{1,0:T(8,128)S(1)}, f32[48,384]{1,0:T(8,128)S(1)}, u32[]{:S(2)}, u32[]{:S(2)}) collective-permute-start(f32[48,384]{1,0:T(8,128)S(1)} %get-tuple-element.20), channel_id=1, source_target_pairs={{0,3},{1,0},{2,1},{3,2},{4,7},{5,4},{6,5},{7,6},{8,11},{9,8},{10,9... | collective-permute-start | bytes 221192 | tf_op jit(solution)/shard_map/ppermute | solution.py:32
  150.6 4.8 %collective-permute-start.13 = (f32[48,384]{1,0:T(8,128)S(1)}, f32[48,384]{1,0:T(8,128)S(1)}, u32[]{:S(2)}, u32[]{:S(2)}) collective-permute-start(f32[48,384]{1,0:T(8,128)S(1)} %get-tuple-element.19), channel_id=1, source_target_pairs={{0,2},{1,3},{2,0},{3,1},{4,6},{5,7},{6,4},{7,5},{8,10},{9,11},{10,... | collective-permute-start | bytes 221192 | tf_op jit(solution)/shard_map/ppermute | solution.py:32
  152.9 3.9 %collective-permute-start.12 = (f32[48,384]{1,0:T(8,128)S(1)}, f32[48,384]{1,0:T(8,128)S(1)}, u32[]{:S(2)}, u32[]{:S(2)}) collective-permute-start(f32[48,384]{1,0:T(8,128)S(1)} %get-tuple-element.18), channel_id=1, source_target_pairs={{0,1},{1,2},{2,3},{3,0},{4,5},{5,6},{6,7},{7,4},{8,9},{9,10},{10,1... | collective-permute-start | bytes 221192 | tf_op jit(solution)/shard_map/ppermute | solution.py:32
  179.9 3.4 %collective-permute-start.5 = (f32[48,512]{1,0:T(8,128)S(1)}, f32[48,512]{1,0:T(8,128)S(1)}, u32[]{:S(2)}, u32[]{:S(2)}) collective-permute-start(f32[48,512]{1,0:T(8,128)S(1)} %get-tuple-element.16), channel_id=1, source_target_pairs={{0,3},{1,0},{2,1},{3,2},{4,7},{5,4},{6,5},{7,6},{8,11},{9,8},{10,9... | collective-permute-start | bytes 294920 | tf_op jit(solution)/shard_map/ppermute | solution.py:32
  180.3 7.0 %collective-permute-start.4 = (f32[48,512]{1,0:T(8,128)S(1)}, f32[48,512]{1,0:T(8,128)S(1)}, u32[]{:S(2)}, u32[]{:S(2)}) collective-permute-start(f32[48,512]{1,0:T(8,128)S(1)} %get-tuple-element.17), channel_id=1, source_target_pairs={{0,2},{1,3},{2,0},{3,1},{4,6},{5,7},{6,4},{7,5},{8,10},{9,11},{10,... | collective-permute-start | bytes 294920 | tf_op jit(solution)/shard_map/ppermute | solution.py:32
  181.9 5.3 %collective-permute-start.3 = (f32[48,512]{1,0:T(8,128)S(1)}, f32[48,512]{1,0:T(8,128)S(1)}, u32[]{:S(2)}, u32[]{:S(2)}) collective-permute-start(f32[48,512]{1,0:T(8,128)S(1)} %get-tuple-element.15), channel_id=1, source_target_pairs={{0,1},{1,2},{2,3},{3,0},{4,5},{5,6},{6,7},{7,4},{8,9},{9,10},{10,1... | collective-permute-start | bytes 294920 | tf_op jit(solution)/shard_map/ppermute | solution.py:32
Sparse Core Ops, SparseCore 0:
  99.2 16.3 all-gather.1

commit v3 on v1

v3 whole, which is shorter than its diff:
```python
import functools
import math

import jax
import jax.numpy as jnp
from jax import lax
from jax.experimental import pallas as pl
from jax.experimental.pallas import tpu as pltpu
from jax.sharding import PartitionSpec as P

ITERS = 3

student_temp = 0.1
teacher_temp = 0.07
norm_eps = 1e-06
teacher_rate = math.log2(math.e) / teacher_temp
student_rate = math.log2(math.e) / student_temp

VMEM_LIMIT = 48 * 1024 * 1024
BOTH = ("batch", "proto")


def scores(left_rows, right_rows):
    return lax.dot_general(
        left_rows, right_rows, (((1,), (1,)), ((), ())), preferred_element_type=jnp.float32
    )


def unit_rows(values):
    lengths = jnp.sqrt(jnp.sum(values * values, axis=1, keepdims=True) + norm_eps)
    return (values / lengths, lengths)


def whole(memory_space=pltpu.VMEM):
    return pl.BlockSpec(memory_space=memory_space)


def lane_fold(values, combine):
    folded = values[:, :128]
    for start in range(128, values.shape[1], 128):
        folded = combine(folded, values[:, start : start + 128])
    return folded


def params():
    return pltpu.CompilerParams(vmem_limit_bytes=VMEM_LIMIT)


def cost(flops, bytes_accessed, transcendentals=0):
    return pl.CostEstimate(
        flops=int(flops), bytes_accessed=int(bytes_accessed), transcendentals=int(transcendentals)
    )


def teacher_front_kernel(share, proto_ref, emb_ref, protos_ref, unit_ref, block_ref, top_ref):
    step = pl.program_id(0)
    rows = emb_ref.shape[0]

    @pl.when(step == 0)
    def _():
        unit_ref[...] = unit_rows(emb_ref[...].astype(jnp.float32))[0].astype(jnp.bfloat16)
        top_ref[...] = jnp.full(top_ref.shape, -jnp.inf, jnp.float32)

    products = scores(unit_ref[...], protos_ref[...])
    top_ref[:rows, :] = jnp.maximum(top_ref[:rows, :], lane_fold(products, jnp.maximum))

    @pl.when(step == pl.num_programs(0) - 1)
    def _():
        start = pl.multiple_of(proto_ref[0] * share, 16)
        block_ref[:share, :] = unit_ref[pl.ds(start, share), :]
        tops = jnp.max(jnp.transpose(top_ref[...]), axis=0, keepdims=True)
        lanes = lax.broadcasted_iota(jnp.int32, tops.shape, 1)
        tops = jnp.where(lanes < rows, tops, 0.0)
        high = tops.astype(jnp.bfloat16)
        rest = tops - high.astype(jnp.float32)
        middle = rest.astype(jnp.bfloat16)
        low = (rest - middle.astype(jnp.float32)).astype(jnp.bfloat16)
        block_ref[share:, :] = jnp.concatenate(
            [high, middle, low, jnp.zeros((13, tops.shape[1]), jnp.bfloat16)], axis=0
        )


def teacher_front(proto_index, teacher_emb, protos, share, steps):
    rows, width = teacher_emb.shape
    count = protos.shape[0]
    return pl.pallas_call(
        functools.partial(teacher_front_kernel, share),
        grid=(steps,),
        in_specs=[
            whole(pltpu.SMEM),
            whole(),
            pl.BlockSpec((count // steps, width), lambda i: (i, 0)),
        ],
        out_specs=[whole(), whole()],
        out_shape=[
            jax.ShapeDtypeStruct((rows, width), jnp.bfloat16),
            jax.ShapeDtypeStruct((share + 16, width), jnp.bfloat16),
        ],
        scratch_shapes=[pltpu.VMEM((256, 128), jnp.float32)],
        compiler_params=params(),
        cost_estimate=cost(2 * rows * width * count, 2 * width * count),
        name="teacher_front",
    )(proto_index, teacher_emb, protos)


def row_sums(values):
    return jnp.sum(lane_fold(values, jnp.add), axis=1, keepdims=True)


def first_sweep_kernel(chunk, protos_total, protos_ref, units_ref, top_ref, weights_ref, crop_sum_ref):
    crop_sum_ref[...] = jnp.zeros(crop_sum_ref.shape, jnp.float32)

    def sweep(index, carry):
        rows = pl.ds(pl.multiple_of(index * chunk, chunk), chunk)
        products = scores(protos_ref[rows, :], units_ref[...])
        weights = jnp.exp2((products - top_ref[...]) * teacher_rate)
        weights_ref[rows, :] = weights
        proto_scale = 1.0 / (protos_total * row_sums(weights))
        crop_sum_ref[...] += jnp.sum(weights * proto_scale, axis=0, keepdims=True)
        return carry

    lax.fori_loop(0, protos_ref.shape[0] // chunk, sweep, 0)


def first_sweep(thin_protos, units, top, protos_total):
    thin, width = thin_protos.shape
    crops_total = units.shape[0]
    chunk = min(thin, 128)
    return pl.pallas_call(
        functools.partial(first_sweep_kernel, chunk, protos_total),
        in_specs=[whole(), whole(), whole()],
        out_specs=[whole(), whole()],
        out_shape=[
            pltpu.VMEM((thin, crops_total), jnp.float32),
            jax.ShapeDtypeStruct((1, crops_total), jnp.float32),
        ],
        compiler_params=params(),
        cost_estimate=cost(2 * thin * width * crops_total, 2 * width * (thin + crops_total), thin * crops_total),
        name="first_sweep",
    )(thin_protos, units, top)


def crop_scales(parts_ref, crops_total):
    return 1.0 / (crops_total * jnp.sum(parts_ref[...], axis=0, keepdims=True))


def next_sweep_kernel(chunk, protos_total, weights_ref, parts_ref, crop_sum_ref, scale_ref):
    scale_ref[...] = crop_scales(parts_ref, weights_ref.shape[1])
    crop_sum_ref[...] = jnp.zeros(crop_sum_ref.shape, jnp.float32)

    def sweep(index, carry):
        weights = weights_ref[pl.ds(pl.multiple_of(index * chunk, chunk), chunk), :]
        proto_scale = 1.0 / (protos_total * row_sums(weights * scale_ref[...]))
        crop_sum_ref[...] += jnp.sum(weights * proto_scale, axis=0, keepdims=True)
        return carry

    lax.fori_loop(0, weights_ref.shape[0] // chunk, sweep, 0)


def next_sweep(weights, parts, protos_total):
    thin, crops_total = weights.shape
    chunk = min(thin, 64)
    return pl.pallas_call(
        functools.partial(next_sweep_kernel, chunk, protos_total),
        in_specs=[whole(), whole()],
        out_specs=whole(),
        out_shape=jax.ShapeDtypeStruct((1, crops_total), jnp.float32),
        scratch_shapes=[pltpu.VMEM((1, crops_total), jnp.float32)],
        compiler_params=params(),
        cost_estimate=cost(4 * thin * crops_total, 4 * thin * crops_total),
        name="next_sweep",
    )(pltpu.with_memory_space_constraint(weights, pltpu.VMEM), parts)


def last_scales_kernel(chunk, protos_total, weights_ref, parts_ref, proto_scale_ref, scale_ref):
    scale_ref[...] = crop_scales(parts_ref, weights_ref.shape[1])

    def sweep(index, carry):
        rows = pl.ds(pl.multiple_of(index * chunk, chunk), chunk)
        folded = lane_fold(weights_ref[rows, :] * scale_ref[...], jnp.add)
        sums = jnp.sum(jnp.transpose(folded), axis=0, keepdims=True)
        proto_scale_ref[:, rows] = 1.0 / (protos_total * sums)
        return carry

    lax.fori_loop(0, weights_ref.shape[0] // chunk, sweep, 0)


def last_scales(weights, parts, protos_total):
    thin, crops_total = weights.shape
    return pl.pallas_call(
        functools.partial(last_scales_kernel, 128, protos_total),
        in_specs=[whole(), whole()],
        out_specs=whole(),
        out_shape=jax.ShapeDtypeStruct((1, thin), jnp.float32),
        scratch_shapes=[pltpu.VMEM((1, crops_total), jnp.float32)],
        compiler_params=params(),
        cost_estimate=cost(2 * thin * crops_total, 4 * thin * crops_total),
        name="last_scales",
    )(pltpu.with_memory_space_constraint(weights, pltpu.VMEM), parts)


def wide_weights_kernel(unit_ref, protos_ref, top_ref, weights_ref, top_rows_ref):
    step = pl.program_id(0)
    rows = unit_ref.shape[0]
    block = protos_ref.shape[0]

    @pl.when(step == 0)
    def _():
        tops = jnp.transpose(jnp.broadcast_to(top_ref[...], (128, 256)))
        top_rows_ref[...] = tops[:rows, :]

    products = scores(unit_ref[...], protos_ref[...])
    tops = jnp.tile(top_rows_ref[...], (1, block // 128))
    weights_ref[:, pl.ds(pl.multiple_of(step * block, block), block)] = jnp.exp2(
        (products - tops) * teacher_rate
    )


def wide_weights(unit, protos, top, steps):
    rows, width = unit.shape
    count = protos.shape[0]
    return pl.pallas_call(
        wide_weights_kernel,
        grid=(steps,),
        in_specs=[whole(), pl.BlockSpec((count // steps, width), lambda i: (i, 0)), whole()],
        out_specs=whole(),
        out_shape=pltpu.VMEM((rows, count), jnp.float32),
        scratch_shapes=[pltpu.VMEM((rows, 128), jnp.float32)],
        compiler_params=params(),
        cost_estimate=cost(2 * rows * width * count, 2 * width * count, rows * count),
        name="wide_weights",
    )(unit, protos, top)


def repel_kernel(weights_ref, scale_ref, protos_ref, out_ref, sum_ref):
    step = pl.program_id(0)
    block, width = protos_ref.shape

    @pl.when(step == 0)
    def _():
        out_ref[...] = jnp.zeros(out_ref.shape, jnp.float32)
        sum_ref[...] = jnp.zeros(sum_ref.shape, jnp.float32)

    columns = pl.ds(pl.multiple_of(step * block, block), block)
    scaled = weights_ref[:, columns] * scale_ref[:, columns]
    rounded = scaled.astype(jnp.bfloat16)
    out_ref[:, :width] += jnp.dot(rounded, protos_ref[...], preferred_element_type=jnp.float32)
    sum_ref[...] += lane_fold(scaled, jnp.add)

    @pl.when(step == pl.num_programs(0) - 1)
    def _():
        total = jnp.sum(sum_ref[...], axis=1, keepdims=True)
        out_ref[:, width:] = jnp.broadcast_to(total, sum_ref.shape)


def repel(weights, scale, protos, steps):
    rows, count = weights.shape
    width = protos.shape[1]
    return pl.pallas_call(
        repel_kernel,
        grid=(steps,),
        in_specs=[whole(), whole(), pl.BlockSpec((count // steps, width), lambda i: (i, 0))],
        out_specs=whole(),
        out_shape=jax.ShapeDtypeStruct((rows, width + 128), jnp.float32),
        scratch_shapes=[pltpu.VMEM((rows, 128), jnp.float32)],
        compiler_params=params(),
        cost_estimate=cost(2 * rows * width * count, 2 * width * count),
        name="repel",
    )(pltpu.with_memory_space_constraint(weights, pltpu.VMEM), scale, protos)


def attract_kernel(emb_ref, protos_ref, out_ref, total_ref, top_ref):
    step = pl.program_id(0)
    block, width = protos_ref.shape

    @pl.when(step == 0)
    def _():
        out_ref[...] = jnp.zeros(out_ref.shape, jnp.float32)
        total_ref[...] = jnp.zeros(total_ref.shape, jnp.float32)
        top_ref[...] = jnp.full(top_ref.shape, -1e30, jnp.float32)

    products = scores(emb_ref[...], protos_ref[...])
    old_top = top_ref[...]
    block_top = jnp.max(lane_fold(products, jnp.maximum), axis=1, keepdims=True)
    new_top = jnp.maximum(old_top, block_top)
    fade = jnp.exp2((old_top - new_top) * student_rate)
    shifted = jnp.exp2((products - jnp.tile(new_top, (1, block // 128))) * student_rate)
    total_ref[...] = total_ref[...] * fade + lane_fold(shifted, jnp.add)
    top_ref[...] = new_top
    out_ref[:, :width] = out_ref[:, :width] * jnp.tile(fade, (1, width // 128)) + jnp.dot(
        shifted.astype(jnp.bfloat16), protos_ref[...], preferred_element_type=jnp.float32
    )

    @pl.when(step == pl.num_programs(0) - 1)
    def _():
        total = jnp.sum(total_ref[...], axis=1, keepdims=True)
        out_ref[:, width : width + 128] = jnp.broadcast_to(total, total_ref.shape)
        out_ref[:, width + 128 :] = new_top


def attract(emb, protos, steps):
    rows, width = emb.shape
    count = protos.shape[0]
    return pl.pallas_call(
        attract_kernel,
        grid=(steps,),
        in_specs=[whole(), pl.BlockSpec((count // steps, width), lambda i: (i, 0))],
        out_specs=whole(),
        out_shape=jax.ShapeDtypeStruct((rows, width + 256), jnp.float32),
        scratch_shapes=[pltpu.VMEM((rows, 128), jnp.float32), pltpu.VMEM((rows, 128), jnp.float32)],
        compiler_params=params(),
        cost_estimate=cost(4 * rows * width * count, 2 * width * count, rows * count),
        name="attract",
    )(emb, protos)


def exchange_rows(blocks, axis):
    count = lax.axis_size(axis)
    own = lax.axis_index(axis)
    rows = blocks.shape[0] // count
    parts = [lax.dynamic_slice_in_dim(blocks, own * rows, rows, 0)]
    for step in range(1, count):
        target = lax.rem(own + step, count)
        sent = lax.dynamic_slice_in_dim(blocks, target * rows, rows, 0)
        parts.append(lax.ppermute(sent, axis, [(i, (i + step) % count) for i in range(count)]))
    return parts


def spread(values, axes):
    count = lax.axis_size(axes)
    copies = jnp.broadcast_to(values[None], (count,) + values.shape)
    return lax.all_to_all(copies, axes, 0, 0, tiled=True)


def pairwise_gather(values, axis):
    count = lax.axis_size(axis)
    values = values[None, None]
    step = count // 2
    while step:
        other = lax.ppermute(values, axis, [(i, i ^ step) for i in range(count)])
        upper = (lax.axis_index(axis) // step) % 2
        both = jnp.where(
            upper == 0, jnp.concatenate([values, other], 1), jnp.concatenate([other, values], 1)
        )
        values = both.reshape((-1, 1) + values.shape[2:])
        step //= 2
    return values[:, 0]


def body(crops, teacher_emb, w_first, b_first, w_second, b_second, w_third, b_third, protos):
    batch_index = lax.axis_index("batch")
    proto_index = lax.axis_index("proto")
    batch_size = lax.axis_size("batch")
    proto_size = lax.axis_size("proto")
    share_rows = crops.shape[0]
    group_rows = teacher_emb.shape[0]
    crops_total = group_rows * batch_size
    protos_total = protos.shape[0] * proto_size
    thin = protos.shape[0] // batch_size
    hidden_share = w_first.shape[1]
    width = protos.shape[1]
    steps = 8

    own_unit, block = teacher_front(proto_index.reshape(1), teacher_emb, protos, share_rows, steps)
    blocks = pairwise_gather(block, "batch")
    blocks = lax.all_gather(blocks, "proto", axis=1)
    all_unit = blocks[:, :, :share_rows].reshape(crops_total, width)
    pieces = blocks[:, :, share_rows : share_rows + 3, :group_rows].astype(jnp.float32)
    tops = jnp.max(pieces[:, :, 0] + pieces[:, :, 1] + pieces[:, :, 2], axis=1)
    own_top = lax.dynamic_slice_in_dim(tops, batch_index, 1, 0)
    own_top = jnp.pad(own_top, ((0, 0), (0, 256 - group_rows)))
    thin_protos = lax.dynamic_slice_in_dim(protos, batch_index * thin, thin, 0)

    all_crops = lax.all_gather(crops, "proto", axis=0, tiled=True)
    w_third_all = lax.all_gather(w_third, "proto", axis=0, tiled=True)
    first_bias = lax.dynamic_slice_in_dim(b_first, proto_index * hidden_share, hidden_share)
    h_first = jax.nn.gelu(
        jnp.dot(all_crops, w_first, preferred_element_type=jnp.float32) + first_bias,
        approximate=False,
    ).astype(jnp.bfloat16)
    partial_value = jnp.dot(h_first, w_second, preferred_element_type=jnp.float32)
    pre_second = sum(exchange_rows(partial_value, "proto"))
    h_second = jax.nn.gelu(pre_second + b_second, approximate=False).astype(jnp.bfloat16)
    bottleneck = jnp.dot(h_second, w_third_all, preferred_element_type=jnp.float32) + b_third
    unit, lengths = unit_rows(bottleneck)
    student_emb = lax.all_gather(unit.astype(jnp.bfloat16), "proto", axis=0, tiled=True)
    attract_parts = exchange_rows(attract(student_emb, protos, steps), "proto")

    weights, crop_sum = first_sweep(thin_protos, all_unit, tops.reshape(1, crops_total), protos_total)
    for _ in range(ITERS - 2):
        crop_sum = next_sweep(weights, spread(crop_sum, BOTH).reshape(-1, crops_total), protos_total)
    scale = last_scales(weights, spread(crop_sum, BOTH).reshape(-1, crops_total), protos_total)
    all_scale = spread(scale, "batch").reshape(1, -1)

    own_weights = wide_weights(own_unit, protos, own_top, steps)
    repel_sum = sum(exchange_rows(repel(own_weights, all_scale, protos, steps), "proto"))

    tops_in = [part[:, width + 128 : width + 129] for part in attract_parts]
    row_top = functools.reduce(jnp.maximum, tops_in)
    fades = [jnp.exp2((top - row_top) * student_rate) for top in tops_in]
    attract_sum = sum(part[:, :width] * fade for part, fade in zip(attract_parts, fades))
    row_sum = sum(part[:, width : width + 1] * fade for part, fade in zip(attract_parts, fades))
    emb_grad = (
        attract_sum / row_sum - repel_sum[:, :width] / repel_sum[:, width : width + 1]
    ) / student_temp
    crop_grad = (emb_grad - unit * jnp.sum(unit * emb_grad, axis=1, keepdims=True)) / lengths
    return crop_grad


def solution(mesh):
    in_specs = (
        P(("batch", "proto"), None),
        P("batch", None),
        P(None, "proto"),
        P(),
        P("proto", None),
        P(),
        P("proto", None),
        P(),
        P("proto", None),
    )
    out_specs = P(("batch", "proto"), None)
    return jax.shard_map(body, mesh=mesh, in_specs=in_specs, out_specs=out_specs, check_vma=False)
```

time: 327 us -> 196 us (0.60)
  blocking collectives: 218 us -> 13.2 us
  Pallas kernels: 0 us -> 55.9 us
  local copies, waits for them, and re-layouts: 4.76 us -> 38.7 us
  matrix products: 39 us -> 7.24 us
  other arithmetic: 34.1 us -> 4.64 us
  waiting for transfers between devices: 7.72 us -> 32.5 us
  starting transfers between devices: 9.27 us -> 28.1 us
    all_gather x2 -> x0, blocking collectives: 85 us -> none  [the longest x1 54.3 us: body(): lax.all_gather(unit_share, ('batch', 'proto'), axis=0, tiled=True)]
    psum x2 -> x0, blocking collectives: 81.1 us -> none  [body(): lax.psum(jnp.sum(thin_weights * proto_scale[:, None], axis=0), ('batch',...]
    pallas_call x0 -> x7, Pallas kernels: none -> 55.9 us  [the longest x1 11.6 us: attract(): pl.pallas_call(attract_kernel, grid=(steps,), in_specs=[whole(), pl.Block...]
    pmax x1 -> x0, blocking collectives: 36.9 us -> none  [body(): teacher_top = lax.pmax(jnp.max(thin_logits, axis=0), ('batch', 'proto'))]
    reduce_sum x7 -> x0, other arithmetic: 32.7 us -> none  [the longest x2 14.2 us: body(): row_total = jnp.sum(thin_weights * crop_scale[None, :], axis=1)]
    dot_general x5 -> x0, matrix products: 31.7 us -> none  [the longest x3 21.1 us: scores(): lax.dot_general(left_rows, right_rows, (((1,), (1,)), ((), ())), preferre...]
    unnamed x10 -> x26, local copies, waits for them, and re-layouts: 1.33 us -> 26.3 us
    ppermute x9, waiting for transfers between devices: 6.99 us -> 24.5 us  [exchange_rows(): lax.ppermute(sent, axis, [(i, (i + step) % count) for i in range(count)])]
  transfers between devices with their start and end apart: 10 -> 17, of which waited for: 4 -> 8; matrix products, arithmetic and copies ran while one was open for 18% -> 8% of each run, Pallas kernels for 0% -> 20%
where the time goes in v3:
time: 196 us; the launch traced here: 194 us
  Pallas kernels  55.9 us (29%)
  local copies, waits for them, and re-layouts  38.7 us (20%)
  waiting for transfers between devices  32.5 us (17%)
  starting transfers between devices  28.1 us (14%)
  between operations  13.6 us (7%)
  blocking collectives  13.2 us (7%)
  matrix products  7.24 us (4%)
  other arithmetic  4.64 us (2%)
    unnamed x26, local copies, waits for them, and re-layouts  26.3 us
    ppermute x9, waiting for transfers between devices, exchange_rows(): lax.ppermute(sent, axis, [(i, (i + step) % count) for i in range(count)])  24.5 us
    all_to_all x3, starting transfers between devices, spread(): return lax.all_to_all(copies, axes, 0, 0, tiled=True)  12.3 us
    pallas_call x1, Pallas kernels, attract(): pl.pallas_call(attract_kernel, grid=(steps,), in_specs=[whole(), pl.Block...  11.6 us
    pallas_call x1, Pallas kernels, first_sweep(): pl.pallas_call(functools.partial(first_sweep_kernel, chunk, protos_total)...  10.5 us
    ppermute x9, starting transfers between devices, exchange_rows(): lax.ppermute(sent, axis, [(i, (i + step) % count) for i in range(count)])  8.34 us
    pallas_call x1, Pallas kernels, repel(): pl.pallas_call(repel_kernel, grid=(steps,), in_specs=[whole(), whole(), p...  8.02 us
    pallas_call x1, Pallas kernels, teacher_front(): pl.pallas_call(functools.partial(teacher_front_kernel, share), grid=(step...  7.97 us
  transfers between devices with their start and end apart: 17, of which 8 were waited for; matrix products, arithmetic and copies ran while one was open for 8% of the time, Pallas kernels for 20%

profile of v3, /device:TPU:0, one launch (start us, length us, event | category | flops | bytes accessed | tf_op | source)
XLA Modules:
  0.0 194.0 jit_solution(8777606437226765143)
XLA Ops:
  6.5 0.7 all-gather.3.cloned.1.call-update
  7.3 0.9 copy-done.6
  8.2 8.0 %teacher_front.1 = (bf16[192,256]{1,0:T(8,128)(2,1)S(1)}, bf16[64,256]{1,0:T(8,128)(2,1)S(1)}) custom-call(s32[1]{0:T(128)} %bitcast.proto_ref, bf16[192,256]{1,0:T(8,128)(2,1)S(1)} %copy-done.6, bf16[16384,256]{1,0:T(8,128)(2,1)} %protos_ref.7), custom_call_target="tpu_custom_call" | custom-call | flops 1610612736 | bytes 8388608 | tf_op jit(solution)/shard_map/teacher_front/pallas_call | solution.py:86
  16.2 0.6 copy-done.7
  16.8 4.0 %collective-permute-start.6 = (bf16[1,1,64,256]{3,2,1,0:T(8,128)(2,1)S(1)}, bf16[1,1,64,256]{3,2,1,0:T(8,128)(2,1)S(1)}, u32[]{:S(2)}, u32[]{:S(2)}) collective-permute-start(bf16[1,1,64,256]{3,2,1,0:T(8,128)(2,1)S(1)} %bitcast.17), channel_id=1, source_target_pairs={{0,16},{4,20},{8,24},{12,28},{16,0},{20,4},{24,8},{28,12},{1,17},{... | collective-permute-start | bytes 98312 | tf_op jit(solution)/shard_map/ppermute | solution.py:340
  20.9 2.2 %collective-permute-done.6 = bf16[1,1,64,256]{3,2,1,0:T(8,128)(2,1)S(1)} collective-permute-done((bf16[1,1,64,256]{3,2,1,0:T(8,128)(2,1)S(1)}, bf16[1,1,64,256]{3,2,1,0:T(8,128)(2,1)S(1)}, u32[]{:S(2)}, u32[]{:S(2)}) %collective-permute-start.6) | collective-permute-done | bytes 32800 | tf_op jit(solution)/shard_map/ppermute | solution.py:340
  23.1 1.6 collective-permute-start.7
  24.7 0.8 dynamic_slice.45
  25.5 1.9 %collective-permute-done.7 = bf16[2,1,64,256]{3,2,1,0:T(8,128)(2,1)S(1)} collective-permute-done((bf16[2,1,64,256]{3,2,1,0:T(8,128)(2,1)S(1)}, bf16[2,1,64,256]{3,2,1,0:T(8,128)(2,1)S(1)}, u32[]{:S(2)}, u32[]{:S(2)}) %collective-permute-start.7) | collective-permute-done | bytes 65568 | tf_op jit(solution)/shard_map/ppermute | solution.py:340
  27.5 1.8 collective-permute-start.8
  29.3 7.5 %all_gather.12 = bf16[192,1536]{1,0:T(8,128)(2,1)S(1)} all-gather(bf16[48,1536]{1,0:T(8,128)(2,1)S(1)} %copy-done.9), channel_id=1, replica_groups=mesh['batch'=8,'proto'=4] {'proto'}, dimensions={0}, use_global_device_ids=true | all-gather | bytes 737280 | tf_op jit(solution)/shard_map/all_gather | solution.py:374
  36.8 0.7 copy.12
  37.6 4.4 %fusion.20 = f32[192,2048]{1,0:T(8,128)} fusion(bf16[512,2048]{1,0:T(8,128)(2,1)S(1)} %copy-done, bf16[192,1536]{1,0:T(8,128)(2,1)S(1)} %all_gather.12, bf16[1536,512]{1,0:T(8,128)(2,1)} %param.11, f32[512]{0:T(512)S(1)} %dynamic_slice.45), kind=kOutput, calls=%fused_computation.41 | convolution fusion | flops 711131136 | bytes 5834752 | tf_op jit(solution)/shard_map/dot_general | solution.py:381
  42.0 1.3 constant_dynamic-slice_fusion.10
  43.3 0.4 collective-permute-start
  43.7 1.4 collective-permute-start.2
  45.1 0.6 collective-permute-start.1
  45.8 2.3 %constant_dynamic-slice_fusion.3.protos_ref = bf16[2048,256]{1,0:T(8,128)(2,1)} fusion(bf16[16384,256]{1,0:T(8,128)(2,1)} %protos_ref.7, s32[]{:T(128)S(6)} %select_n.124), kind=kLoop, calls=%fused_computation.119 | loop fusion | bytes 2097156 | tf_op jit(solution)/shard_map/dynamic_slice | solution.py:372
  48.0 12.1 %collective-permute-done = f32[48,2048]{1,0:T(8,128)} collective-permute-done((f32[48,2048]{1,0:T(8,128)S(1)}, f32[48,2048]{1,0:T(8,128)}, u32[]{:S(2)}, u32[]{:S(2)}) %collective-permute-start) | collective-permute-done | bytes 393248 | tf_op jit(solution)/shard_map/ppermute | solution.py:325
  60.1 8.9 %collective-permute-done.1 = f32[48,2048]{1,0:T(8,128)} collective-permute-done((f32[48,2048]{1,0:T(8,128)S(1)}, f32[48,2048]{1,0:T(8,128)}, u32[]{:S(2)}, u32[]{:S(2)}) %collective-permute-start.1) | collective-permute-done | bytes 393248 | tf_op jit(solution)/shard_map/ppermute | solution.py:325
  69.0 2.8 %multiply_reduce_fusion.1 = (f32[48]{0:T(128)S(1)}, f32[48,256]{1,0:T(8,128)S(1)}) fusion(f32[256]{0:T(256)S(1)} %copy-done.11, bf16[2048,256]{1,0:T(8,128)(2,1)} %all-gather.3.cloned.1.call-done, f32[48,2048]{1,0:T(8,128)} %collective-permute-done.2, f32[48,2048]{1,0:T(8,128)} %collective-permute-done.1, f32[48,2048]{1,0:T(8,128)} %collective-permute-done, ...), kind=kOutput, calls=%fused_computation.93 | convolution fusion | flops 57151440 | bytes 2680004 | tf_op jit(solution)/shard_map/dot_general | solution.py:384
  71.8 0.9 slice_convert_fusion
  72.8 0.1 fusion.59
  72.9 0.7 reshape.145.top_ref
  73.5 2.1 %slice.89 = bf16[8,4,48,256]{3,2,1,0:T(8,128)(2,1)} slice(bf16[8,4,64,256]{3,2,1,0:T(8,128)(2,1)} %all-gather.5.cloned.1.call-done), slice={[0:8], [0:4], [0:48], [0:256]} | slice | bytes 1572864 | tf_op jit(solution)/shard_map/slice | solution.py:367
  75.6 10.5 %first_sweep.1 = (f32[2048,1536]{1,0:T(8,128)S(1)}, f32[1,1536]{1,0:T(1,128)}) custom-call(bf16[2048,256]{1,0:T(8,128)(2,1)} %constant_dynamic-slice_fusion.3.protos_ref, bf16[1536,256]{1,0:T(8,128)(2,1)} %bitcast.20, f32[1,1536]{1,0:T(1,128)} %reshape.145.top_ref), custom_call_target="tpu_custom_call" | custom-call | flops 1610612736 | bytes 1835008 | tf_op jit(solution)/shard_map/first_sweep/pallas_call | solution.py:129
  86.1 4.5 %copy-done.1 = f32[2048,1536]{1,0:T(8,128)} copy-done((f32[2048,1536]{1,0:T(8,128)}, f32[2048,1536]{1,0:T(8,128)S(1)}, u32[]{:S(2)}) %copy-start.1) | copy-done | bytes 12582936
  90.6 0.7 reduce.6
  91.3 0.8 broadcast_in_dim.13
  92.1 4.0 %all-to-all-start = ((f32[32,1,1536]{2,1,0:T(1,128)}), f32[32,1,1536]{2,1,0:T(1,128)S(1)}, u32[]{:S(2)}, u32[]{:S(2)}) async-start(f32[32,1,1536]{2,1,0:T(1,128)} %broadcast_in_dim.13), calls=%async_computation | async-start | bytes 393216 | tf_op jit(solution)/shard_map/all_to_all | solution.py:332
  96.2 5.7 %all_gather.14.emb_ref = bf16[192,256]{1,0:T(8,128)(2,1)S(1)} all-gather(bf16[48,256]{1,0:T(8,128)(2,1)S(1)} %fusion.129), channel_id=1, replica_groups=mesh['batch'=8,'proto'=4] {'proto'}, dimensions={0}, use_global_device_ids=true | all-gather | bytes 122880 | tf_op jit(solution)/shard_map/all_gather | solution.py:386
  102.0 3.1 %all-to-all-done = f32[32,1,1536]{2,1,0:T(1,128)S(1)} async-done(((f32[32,1,1536]{2,1,0:T(1,128)}), f32[32,1,1536]{2,1,0:T(1,128)S(1)}, u32[]{:S(2)}, u32[]{:S(2)}) %all-to-all-start) | async-done | bytes 196640 | tf_op jit(solution)/shard_map/all_to_all | solution.py:332
  105.0 0.7 copy.18
  105.7 4.6 %copy-done.2 = f32[2048,1536]{1,0:T(8,128)S(1)} copy-done((f32[2048,1536]{1,0:T(8,128)S(1)}, f32[2048,1536]{1,0:T(8,128)}, u32[]{:S(2)}) %copy-start.2) | copy-done | bytes 12582936
  110.3 6.2 %next_sweep.1 = f32[1,1536]{1,0:T(1,128)} custom-call(f32[2048,1536]{1,0:T(8,128)S(1)} %copy-done.2, f32[32,1536]{1,0:T(8,128)} %bitcast.21), custom_call_target="tpu_custom_call" | custom-call | flops 12582912 | bytes 12582912 | tf_op jit(solution)/shard_map/next_sweep/pallas_call | solution.py:163
  116.5 0.7 reduce.7
  117.2 0.8 broadcast_in_dim.15
  118.0 2.7 %all-to-all-start.1 = ((f32[32,1,1536]{2,1,0:T(1,128)}), f32[32,1,1536]{2,1,0:T(1,128)S(1)}, u32[]{:S(2)}, u32[]{:S(2)}) async-start(f32[32,1,1536]{2,1,0:T(1,128)} %broadcast_in_dim.15), calls=%async_computation.1 | async-start | bytes 393216 | tf_op jit(solution)/shard_map/all_to_all | solution.py:332
  120.7 11.6 %attract.1 = f32[192,512]{1,0:T(8,128)S(1)} custom-call(bf16[192,256]{1,0:T(8,128)(2,1)S(1)} %all_gather.14.emb_ref, bf16[16384,256]{1,0:T(8,128)(2,1)} %protos_ref.7), custom_call_target="tpu_custom_call" | custom-call | flops 3221225472 | bytes 8388608 | tf_op jit(solution)/shard_map/attract/pallas_call | solution.py:304
  132.3 0.3 collective-permute-start.3
  132.6 1.5 collective-permute-start.5
  134.1 1.8 collective-permute-start.4
  135.9 0.6 pad.4.top_ref
  136.5 0.7 copy.17
  137.2 4.6 %copy-done.3 = f32[2048,1536]{1,0:T(8,128)S(1)} copy-done((f32[2048,1536]{1,0:T(8,128)S(1)}, f32[2048,1536]{1,0:T(8,128)}, u32[]{:S(2)}) %copy-start.3) | copy-done | bytes 12582936
  141.8 3.8 %last_scales.1 = f32[1,2048]{1,0:T(1,128)} custom-call(f32[2048,1536]{1,0:T(8,128)S(1)} %copy-done.3, f32[32,1536]{1,0:T(8,128)} %bitcast.22), custom_call_target="tpu_custom_call" | custom-call | flops 6291456 | bytes 12582912 | tf_op jit(solution)/shard_map/last_scales/pallas_call | solution.py:190
  145.6 1.3 broadcast_in_dim.17
  146.9 5.5 %all-to-all-start.2 = ((f32[8,1,2048]{2,1,0:T(1,128)}), f32[8,1,2048]{2,1,0:T(1,128)S(1)}, u32[]{:S(2)}, u32[]{:S(2)}) async-start(f32[8,1,2048]{2,1,0:T(1,128)} %broadcast_in_dim.17), calls=%async_computation.2 | async-start | bytes 131072 | tf_op jit(solution)/shard_map/all_to_all | solution.py:332
  152.4 7.9 %wide_weights.1.weights_ref = f32[192,16384]{1,0:T(8,128)S(1)} custom-call(bf16[192,256]{1,0:T(8,128)(2,1)} %copy-done.7, bf16[16384,256]{1,0:T(8,128)(2,1)} %protos_ref.7, f32[1,256]{1,0:T(1,128)} %pad.4.top_ref), custom_call_target="tpu_custom_call" | custom-call | flops 1610612736 | bytes 8388608 | tf_op jit(solution)/shard_map/wide_weights/pallas_call | solution.py:222
  160.3 4.5 %copy-done.4 = f32[192,16384]{1,0:T(8,128)} copy-done((f32[192,16384]{1,0:T(8,128)}, f32[192,16384]{1,0:T(8,128)S(1)}, u32[]{:S(2)}) %copy-start.4) | copy-done | bytes 12582936
  164.8 0.6 copy-done.8
  165.5 4.6 %copy-done.5 = f32[192,16384]{1,0:T(8,128)S(1)} copy-done((f32[192,16384]{1,0:T(8,128)S(1)}, f32[192,16384]{1,0:T(8,128)}, u32[]{:S(2)}) %copy-start.5) | copy-done | bytes 12582936
  170.0 8.0 %repel.1 = f32[192,384]{1,0:T(8,128)} custom-call(f32[192,16384]{1,0:T(8,128)S(1)} %copy-done.5, f32[1,16384]{1,0:T(1,128)} %bitcast.25, bf16[16384,256]{1,0:T(8,128)(2,1)} %protos_ref.7), custom_call_target="tpu_custom_call" | custom-call | flops 1610612736 | bytes 8388608 | tf_op jit(solution)/shard_map/repel/pallas_call | solution.py:259
  178.0 1.0 constant_dynamic-slice_fusion.2
  179.1 1.7 collective-permute-start.11
  180.8 0.6 collective-permute-start.10
  181.4 0.2 fusion.67
  181.6 1.3 collective-permute-done.9
  182.9 0.1 collective-permute-done.11
  182.9 2.3 %collective-permute-done.10 = f32[48,384]{1,0:T(8,128)S(1)} collective-permute-done((f32[48,384]{1,0:T(8,128)S(1)}, f32[48,384]{1,0:T(8,128)S(1)}, u32[]{:S(2)}, u32[]{:S(2)}) %collective-permute-start.10) | collective-permute-done | bytes 73760 | tf_op jit(solution)/shard_map/ppermute | solution.py:325
  185.2 0.9 add_add_fusion.1
  186.1 0.1 slice_reduce_fusion
  186.2 0.2 multiply_reduce_fusion
  186.5 0.7 subtract_divide_fusion
  (36 shorter events, 0.4 us)
Async XLA Ops:
  6.5 31.0 %copy-start = (bf16[512,2048]{1,0:T(8,128)(2,1)S(1)}, bf16[512,2048]{1,0:T(8,128)(2,1)}, u32[]{:S(2)}) copy-start(bf16[512,2048]{1,0:T(8,128)(2,1)} %param.13) | copy-start | bytes 6291460
  6.5 62.4 %all-gather.3.cloned.1.call-start = ((), (), s32[]{:S(2)}) async-start(), calls=%async_computation.3 | async-start | bytes 1310720 | tf_op jit(solution)/shard_map/all_gather | solution.py:375
  7.3 64.6 %all-gather.5.cloned.1.call-start = ((), (), s32[]{:S(2)}) async-start(), calls=%async_computation.4 | async-start | bytes 1310720 | tf_op jit(solution)/shard_map/all_gather | solution.py:366
  7.3 0.9 copy-start.6
  8.2 21.1 %copy-start.9 = (bf16[48,1536]{1,0:T(8,128)(2,1)S(1)}, bf16[48,1536]{1,0:T(8,128)(2,1)}, u32[]{:S(2)}) copy-start(bf16[48,1536]{1,0:T(8,128)(2,1)} %param.9) | copy-start | bytes 442372
  16.2 0.6 copy-start.7
  16.8 6.3 %collective-permute-start.6 = (bf16[1,1,64,256]{3,2,1,0:T(8,128)(2,1)S(1)}, bf16[1,1,64,256]{3,2,1,0:T(8,128)(2,1)S(1)}, u32[]{:S(2)}, u32[]{:S(2)}) collective-permute-start(bf16[1,1,64,256]{3,2,1,0:T(8,128)(2,1)S(1)} %bitcast.17), channel_id=1, source_target_pairs={{0,16},{4,20},{8,24},{12,28},{16,0},{20,4},{24,8},{28,12},{1,17},{... | collective-permute-start | bytes 98312 | tf_op jit(solution)/shard_map/ppermute | solution.py:340
  23.1 4.3 %collective-permute-start.7 = (bf16[2,1,64,256]{3,2,1,0:T(8,128)(2,1)S(1)}, bf16[2,1,64,256]{3,2,1,0:T(8,128)(2,1)S(1)}, u32[]{:S(2)}, u32[]{:S(2)}) collective-permute-start(bf16[2,1,64,256]{3,2,1,0:T(8,128)(2,1)S(1)} %maximum_select_fusion.2), channel_id=1, source_target_pairs={{0,8},{4,12},{8,0},{12,4},{16,24},{20,28},{24,16},{28,20},{1,9},{5... | collective-permute-start | bytes 196616 | tf_op jit(solution)/shard_map/ppermute | solution.py:340
  27.5 9.3 %collective-permute-start.8 = (bf16[4,1,64,256]{3,2,0,1:T(8,128)(2,1)S(1)}, bf16[4,1,64,256]{3,2,0,1:T(8,128)(2,1)S(1)}, u32[]{:S(2)}, u32[]{:S(2)}) collective-permute-start(bf16[4,1,64,256]{3,2,0,1:T(8,128)(2,1)S(1)} %bitcast.23), channel_id=1, source_target_pairs={{0,4},{4,0},{8,12},{12,8},{16,20},{20,16},{24,28},{28,24},{1,5},{5... | collective-permute-start | bytes 393224 | tf_op jit(solution)/shard_map/ppermute | solution.py:340
  43.3 25.6 %copy-start.10 = (f32[2048]{0:T(1024)S(1)}, f32[2048]{0:T(1024)}, u32[]{:S(2)}) copy-start(f32[2048]{0:T(1024)} %param.14) | copy-start | bytes 24580
  43.3 25.6 %copy-start.11 = (f32[256]{0:T(256)S(1)}, f32[256]{0:T(256)}, u32[]{:S(2)}) copy-start(f32[256]{0:T(256)} %param.16) | copy-start | bytes 3076
  43.3 16.8 %collective-permute-start = (f32[48,2048]{1,0:T(8,128)S(1)}, f32[48,2048]{1,0:T(8,128)}, u32[]{:S(2)}, u32[]{:S(2)}) collective-permute-start(f32[48,2048]{1,0:T(8,128)S(1)} %get-tuple-element.20), channel_id=1, source_target_pairs={{0,1},{1,2},{2,3},{3,0},{4,5},{5,6},{6,7},{7,4},{8,9},{9,10},{10,1... | collective-permute-start | bytes 1179656 | tf_op jit(solution)/shard_map/ppermute | solution.py:325
  43.7 16.4 %collective-permute-start.2 = (f32[48,2048]{1,0:T(8,128)S(1)}, f32[48,2048]{1,0:T(8,128)}, u32[]{:S(2)}, u32[]{:S(2)}) collective-permute-start(f32[48,2048]{1,0:T(8,128)S(1)} %get-tuple-element.21), channel_id=1, source_target_pairs={{0,3},{1,0},{2,1},{3,2},{4,7},{5,4},{6,5},{7,6},{8,11},{9,8},{10,9... | collective-permute-start | bytes 1179656 | tf_op jit(solution)/shard_map/ppermute | solution.py:325
  45.1 23.8 %collective-permute-start.1 = (f32[48,2048]{1,0:T(8,128)S(1)}, f32[48,2048]{1,0:T(8,128)}, u32[]{:S(2)}, u32[]{:S(2)}) collective-permute-start(f32[48,2048]{1,0:T(8,128)S(1)} %get-tuple-element.22), channel_id=1, source_target_pairs={{0,2},{1,3},{2,0},{3,1},{4,6},{5,7},{6,4},{7,5},{8,10},{9,11},{10,... | collective-permute-start | bytes 1179656 | tf_op jit(solution)/shard_map/ppermute | solution.py:325
  86.1 4.5 %copy-start.1 = (f32[2048,1536]{1,0:T(8,128)}, f32[2048,1536]{1,0:T(8,128)S(1)}, u32[]{:S(2)}) copy-start(f32[2048,1536]{1,0:T(8,128)S(1)} %get-tuple-element.11.weights_ref) | copy-start | bytes 37748740
  92.1 12.9 %all-to-all-start = ((f32[32,1,1536]{2,1,0:T(1,128)}), f32[32,1,1536]{2,1,0:T(1,128)S(1)}, u32[]{:S(2)}, u32[]{:S(2)}) async-start(f32[32,1,1536]{2,1,0:T(1,128)} %broadcast_in_dim.13), calls=%async_computation | async-start | bytes 393216 | tf_op jit(solution)/shard_map/all_to_all | solution.py:332
  105.7 4.6 %copy-start.2 = (f32[2048,1536]{1,0:T(8,128)S(1)}, f32[2048,1536]{1,0:T(8,128)}, u32[]{:S(2)}) copy-start(f32[2048,1536]{1,0:T(8,128)} %copy-done.1) | copy-start | bytes 37748740
  118.0 18.5 %all-to-all-start.1 = ((f32[32,1,1536]{2,1,0:T(1,128)}), f32[32,1,1536]{2,1,0:T(1,128)S(1)}, u32[]{:S(2)}, u32[]{:S(2)}) async-start(f32[32,1,1536]{2,1,0:T(1,128)} %broadcast_in_dim.15), calls=%async_computation.1 | async-start | bytes 393216 | tf_op jit(solution)/shard_map/all_to_all | solution.py:332
  132.3 48.5 %collective-permute-start.3 = (f32[48,512]{1,0:T(8,128)S(1)}, f32[48,512]{1,0:T(8,128)S(1)}, u32[]{:S(2)}, u32[]{:S(2)}) collective-permute-start(f32[48,512]{1,0:T(8,128)S(1)} %get-tuple-element.23), channel_id=1, source_target_pairs={{0,1},{1,2},{2,3},{3,0},{4,5},{5,6},{6,7},{7,4},{8,9},{9,10},{10,1... | collective-permute-start | bytes 294920 | tf_op jit(solution)/shard_map/ppermute | solution.py:325
  132.6 48.7 %collective-permute-start.5 = (f32[48,512]{1,0:T(8,128)S(1)}, f32[48,512]{1,0:T(8,128)S(1)}, u32[]{:S(2)}, u32[]{:S(2)}) collective-permute-start(f32[48,512]{1,0:T(8,128)S(1)} %get-tuple-element.24), channel_id=1, source_target_pairs={{0,3},{1,0},{2,1},{3,2},{4,7},{5,4},{6,5},{7,6},{8,11},{9,8},{10,9... | collective-permute-start | bytes 294920 | tf_op jit(solution)/shard_map/ppermute | solution.py:325
  134.1 47.2 %collective-permute-start.4 = (f32[48,512]{1,0:T(8,128)S(1)}, f32[48,512]{1,0:T(8,128)S(1)}, u32[]{:S(2)}, u32[]{:S(2)}) collective-permute-start(f32[48,512]{1,0:T(8,128)S(1)} %get-tuple-element.25), channel_id=1, source_target_pairs={{0,2},{1,3},{2,0},{3,1},{4,6},{5,7},{6,4},{7,5},{8,10},{9,11},{10,... | collective-permute-start | bytes 294920 | tf_op jit(solution)/shard_map/ppermute | solution.py:325
  137.2 4.6 %copy-start.3 = (f32[2048,1536]{1,0:T(8,128)S(1)}, f32[2048,1536]{1,0:T(8,128)}, u32[]{:S(2)}) copy-start(f32[2048,1536]{1,0:T(8,128)} %copy-done.1) | copy-start | bytes 37748740
  146.9 17.9 %all-to-all-start.2 = ((f32[8,1,2048]{2,1,0:T(1,128)}), f32[8,1,2048]{2,1,0:T(1,128)S(1)}, u32[]{:S(2)}, u32[]{:S(2)}) async-start(f32[8,1,2048]{2,1,0:T(1,128)} %broadcast_in_dim.17), calls=%async_computation.2 | async-start | bytes 131072 | tf_op jit(solution)/shard_map/all_to_all | solution.py:332
  160.3 4.5 %copy-start.4 = (f32[192,16384]{1,0:T(8,128)}, f32[192,16384]{1,0:T(8,128)S(1)}, u32[]{:S(2)}) copy-start(f32[192,16384]{1,0:T(8,128)S(1)} %wide_weights.1.weights_ref) | copy-start | bytes 37748740
  164.8 0.6 copy-start.8
  165.5 4.6 %copy-start.5 = (f32[192,16384]{1,0:T(8,128)S(1)}, f32[192,16384]{1,0:T(8,128)}, u32[]{:S(2)}) copy-start(f32[192,16384]{1,0:T(8,128)} %copy-done.4) | copy-start | bytes 37748740
  179.0 3.8 %collective-permute-start.9 = (f32[48,384]{1,0:T(8,128)S(1)}, f32[48,384]{1,0:T(8,128)S(1)}, u32[]{:S(2)}, u32[]{:S(2)}) collective-permute-start(f32[48,384]{1,0:T(8,128)S(1)} %get-tuple-element.26), channel_id=1, source_target_pairs={{0,1},{1,2},{2,3},{3,0},{4,5},{5,6},{6,7},{7,4},{8,9},{9,10},{10,1... | collective-permute-start | bytes 221192 | tf_op jit(solution)/shard_map/ppermute | solution.py:325
  179.1 3.9 %collective-permute-start.11 = (f32[48,384]{1,0:T(8,128)S(1)}, f32[48,384]{1,0:T(8,128)S(1)}, u32[]{:S(2)}, u32[]{:S(2)}) collective-permute-start(f32[48,384]{1,0:T(8,128)S(1)} %get-tuple-element.27), channel_id=1, source_target_pairs={{0,3},{1,0},{2,1},{3,2},{4,7},{5,4},{6,5},{7,6},{8,11},{9,8},{10,9... | collective-permute-start | bytes 221192 | tf_op jit(solution)/shard_map/ppermute | solution.py:325
  180.8 4.4 %collective-permute-start.10 = (f32[48,384]{1,0:T(8,128)S(1)}, f32[48,384]{1,0:T(8,128)S(1)}, u32[]{:S(2)}, u32[]{:S(2)}) collective-permute-start(f32[48,384]{1,0:T(8,128)S(1)} %get-tuple-element.28), channel_id=1, source_target_pairs={{0,2},{1,3},{2,0},{3,1},{4,6},{5,7},{6,4},{7,5},{8,10},{9,11},{10,... | collective-permute-start | bytes 221192 | tf_op jit(solution)/shard_map/ppermute | solution.py:325
Sparse Core Ops, SparseCore 0:
  8.9 19.4 all-gather.2
  37.7 21.7 all-gather.4

commit v4 on v0

v4 whole, which is shorter than its diff:
```python
import functools
import math

import jax
import jax.numpy as jnp
from jax import lax
from jax.experimental import pallas as pl
from jax.experimental.pallas import tpu as pltpu
from jax.sharding import PartitionSpec as P

ITERS = 3

student_temp = 0.1
teacher_temp = 0.07
norm_eps = 1e-06
teacher_rate = math.log2(math.e) / teacher_temp
student_rate = math.log2(math.e) / student_temp

MIB = 1024 * 1024
BOTH = ("batch", "proto")


def scores(left_rows, right_rows):
    return lax.dot_general(
        left_rows, right_rows, (((1,), (1,)), ((), ())), preferred_element_type=jnp.float32
    )


def unit_rows(values):
    lengths = jnp.sqrt(jnp.sum(values * values, axis=1, keepdims=True) + norm_eps)
    return (values / lengths, lengths)


def whole(memory_space=pltpu.VMEM):
    return pl.BlockSpec(memory_space=memory_space)


def resident(array):
    return pltpu.with_memory_space_constraint(array, pltpu.VMEM)


def lane_fold(values, combine):
    folded = values[:, :128]
    for start in range(128, values.shape[1], 128):
        folded = combine(folded, values[:, start : start + 128])
    return folded


def row_fold(values):
    return jnp.sum(values.reshape(-1, 8, values.shape[1]), axis=0)


def part(index, size):
    return pl.ds(pl.multiple_of(index * size, size), size)


def params(mib):
    return pltpu.CompilerParams(vmem_limit_bytes=mib * MIB)


def cost(flops, bytes_accessed, transcendentals=0):
    return pl.CostEstimate(
        flops=int(flops), bytes_accessed=int(bytes_accessed), transcendentals=int(transcendentals)
    )


def teacher_units_kernel(core_ref, emb_ref, unit_ref, half_ref):
    unit_ref[...] = unit_rows(emb_ref[...].astype(jnp.float32))[0].astype(jnp.bfloat16)
    half = half_ref.shape[0]
    half_ref[...] = unit_ref[part(core_ref[0], half), :]


def teacher_units(core, teacher_emb):
    rows, width = teacher_emb.shape
    return pl.pallas_call(
        teacher_units_kernel,
        in_specs=[whole(pltpu.SMEM), whole()],
        out_specs=[whole(), whole()],
        out_shape=[
            jax.ShapeDtypeStruct((rows, width), jnp.bfloat16),
            jax.ShapeDtypeStruct((rows // 2, width), jnp.bfloat16),
        ],
        compiler_params=params(4),
        cost_estimate=cost(4 * rows * width, 8 * rows * width),
        name="teacher_units",
    )(core, teacher_emb)


def wide_products_kernel(block, unit_ref, protos_ref, products_ref, tops_ref, top_ref):
    rows = unit_ref.shape[0]
    top_ref[...] = jnp.full(top_ref.shape, -jnp.inf, jnp.float32)

    def step(index, carry):
        products = scores(unit_ref[...], protos_ref[part(index, block), :])
        products_ref[:, part(index, block)] = products
        top_ref[:rows, :] = jnp.maximum(top_ref[:rows, :], lane_fold(products, jnp.maximum))
        return carry

    lax.fori_loop(0, protos_ref.shape[0] // block, step, 0, unroll=2)
    tops = jnp.max(jnp.transpose(top_ref[...]), axis=0, keepdims=True)
    tops_ref[...] = jnp.broadcast_to(tops[None], tops_ref.shape)


def wide_products(unit, protos, copies):
    rows, width = unit.shape
    count = protos.shape[0]
    return pl.pallas_call(
        functools.partial(wide_products_kernel, min(count, 1024)),
        in_specs=[whole(), whole()],
        out_specs=[whole(), whole()],
        out_shape=[
            pltpu.VMEM((rows, count), jnp.float32),
            jax.ShapeDtypeStruct((copies, 1, 256), jnp.float32),
        ],
        scratch_shapes=[pltpu.VMEM((256, 128), jnp.float32)],
        compiler_params=params(8),
        cost_estimate=cost(2 * rows * width * count, 2 * width * count + 4 * rows * count),
        name="wide_products",
    )(unit, protos)


def wide_weights_kernel(block, group, batch_ref, products_ref, tops_ref, weights_ref):
    rows = products_ref.shape[0]
    first = batch_ref[0] * group
    top = tops_ref[first]
    for other in range(1, group):
        top = jnp.maximum(top, tops_ref[first + other])
    tops = jnp.transpose(jnp.broadcast_to(top, (128, 256)))[:rows, :]

    def step(index, carry):
        columns = part(index, block)
        weights_ref[:, columns] = jnp.exp2(
            (products_ref[:, columns] - jnp.tile(tops, (1, block // 128))) * teacher_rate
        )
        return carry

    lax.fori_loop(0, products_ref.shape[1] // block, step, 0)


def wide_weights(batch_index, products, tops, proto_size):
    rows, count = products.shape
    return pl.pallas_call(
        functools.partial(wide_weights_kernel, min(count, 1024), proto_size),
        in_specs=[whole(pltpu.SMEM), whole(), whole()],
        out_specs=whole(),
        out_shape=pltpu.VMEM((rows, count), jnp.float32),
        input_output_aliases={1: 0},
        compiler_params=params(8),
        cost_estimate=cost(2 * rows * count, 8 * rows * count, rows * count),
        name="wide_weights",
    )(batch_index, resident(products), tops)


def repel_kernel(block, proto_ref, weights_ref, scale_ref, protos_ref, *rest):
    out_refs, (acc_ref, sum_ref) = rest[:-2], rest[-2:]
    width = protos_ref.shape[1]
    copies = scale_ref.shape[0]
    thin = scale_ref.shape[2]
    acc_ref[...] = jnp.zeros(acc_ref.shape, jnp.float32)
    sum_ref[...] = jnp.zeros(sum_ref.shape, jnp.float32)
    pieces = thin // block

    def step(index, carry):
        columns = part(index, block)
        scale = scale_ref[index // pieces, :, part(lax.rem(index, pieces), block)]
        scaled = weights_ref[:, columns] * scale
        sum_ref[...] += lane_fold(scaled, jnp.add)
        acc_ref[...] += jnp.dot(
            scaled.astype(jnp.bfloat16), protos_ref[columns, :], preferred_element_type=jnp.float32
        )
        return carry

    lax.fori_loop(0, copies * pieces, step, 0, unroll=2)
    total = jnp.sum(sum_ref[...], axis=1, keepdims=True)
    sum_ref[...] = jnp.broadcast_to(total, sum_ref.shape)
    share = out_refs[0].shape[0]
    for flip, out_ref in enumerate(out_refs):
        rows = part(proto_ref[0] ^ flip, share)
        out_ref[:, :width] = acc_ref[rows, :]
        out_ref[:, width:] = sum_ref[rows, :]


def repel(proto_index, weights, scale, protos, proto_size):
    rows, count = weights.shape
    width = protos.shape[1]
    block = min(scale.shape[2], 1024)
    return pl.pallas_call(
        functools.partial(repel_kernel, block),
        in_specs=[whole(pltpu.SMEM), whole(), whole(), whole()],
        out_specs=[whole()] * proto_size,
        out_shape=[jax.ShapeDtypeStruct((rows // proto_size, width + 128), jnp.float32)] * proto_size,
        scratch_shapes=[pltpu.VMEM((rows, width), jnp.float32), pltpu.VMEM((rows, 128), jnp.float32)],
        compiler_params=params(10),
        cost_estimate=cost(2 * rows * width * count, 2 * width * count + 4 * rows * count),
        name="repel",
    )(proto_index, resident(weights), scale, protos)


def attract_kernel(block, emb_ref, protos_ref, *rest):
    out_refs, (products_ref, acc_ref, sum_ref, top_ref) = rest[:-4], rest[-4:]
    width = protos_ref.shape[1]
    steps = protos_ref.shape[0] // block
    acc_ref[...] = jnp.zeros(acc_ref.shape, jnp.float32)
    sum_ref[...] = jnp.zeros(sum_ref.shape, jnp.float32)
    top_ref[...] = jnp.full(top_ref.shape, -jnp.inf, jnp.float32)

    def first(index, carry):
        products = scores(emb_ref[...], protos_ref[part(index, block), :])
        products_ref[:, part(index, block)] = products
        top_ref[...] = jnp.maximum(top_ref[...], lane_fold(products, jnp.maximum))
        return carry

    lax.fori_loop(0, steps, first, 0, unroll=2)
    top = jnp.max(top_ref[...], axis=1, keepdims=True)
    top_ref[...] = jnp.broadcast_to(top, top_ref.shape)

    def second(index, carry):
        columns = part(index, block)
        shifted = jnp.exp2(
            (products_ref[:, columns] - jnp.tile(top_ref[...], (1, block // 128))) * student_rate
        )
        sum_ref[...] += lane_fold(shifted, jnp.add)
        acc_ref[...] += jnp.dot(
            shifted.astype(jnp.bfloat16), protos_ref[columns, :], preferred_element_type=jnp.float32
        )
        return carry

    lax.fori_loop(0, steps, second, 0, unroll=2)
    total = jnp.sum(sum_ref[...], axis=1, keepdims=True)
    sum_ref[...] = jnp.broadcast_to(total, sum_ref.shape)
    share = out_refs[0].shape[0]
    for slot, out_ref in enumerate(out_refs):
        rows = pl.ds(slot * share, share)
        out_ref[:, :width] = acc_ref[rows, :]
        out_ref[:, width : width + 128] = sum_ref[rows, :]
        out_ref[:, width + 128 :] = top_ref[rows, :]


def attract(emb, protos, proto_size):
    rows, width = emb.shape
    count = protos.shape[0]
    return pl.pallas_call(
        functools.partial(attract_kernel, min(count, 1024)),
        in_specs=[whole(), whole()],
        out_specs=[whole()] * proto_size,
        out_shape=[jax.ShapeDtypeStruct((rows // proto_size, width + 256), jnp.float32)] * proto_size,
        scratch_shapes=[
            pltpu.VMEM((rows, count), jnp.float32),
            pltpu.VMEM((rows, width), jnp.float32),
            pltpu.VMEM((rows, 128), jnp.float32),
            pltpu.VMEM((rows, 128), jnp.float32),
        ],
        compiler_params=params(20),
        cost_estimate=cost(4 * rows * width * count, 2 * width * count, rows * count),
        name="attract",
    )(emb, protos)


def row_sums(values):
    return jnp.sum(lane_fold(values, jnp.add), axis=1, keepdims=True)


def give_copies(copies_ref, totals):
    copies_ref[...] = jnp.broadcast_to(totals[None], copies_ref.shape)


def first_sweep_kernel(
    chunk, lanes, protos_total, index_ref, protos_ref, mine_ref, other_ref, top_ref,
    weights_ref, copies_ref, units_ref, scale_ref,
):
    thin, crops_total = weights_ref.shape
    half = mine_ref.shape[0]
    core = index_ref[1]
    units_ref[part(core, half), :] = mine_ref[...]
    units_ref[part(1 - core, half), :] = other_ref[...]
    first_row = index_ref[0] * thin

    def weigh(index, carry):
        rows = part(index, chunk)
        protos = protos_ref[pl.ds(pl.multiple_of(first_row + index * chunk, chunk), chunk), :]
        folded = jnp.zeros((chunk, 128), jnp.float32)
        for start in range(0, crops_total, lanes):
            columns = pl.ds(start, lanes)
            products = scores(protos, units_ref[columns, :])
            weights = jnp.exp2((products - top_ref[:, columns]) * teacher_rate)
            weights_ref[rows, columns] = weights
            folded = folded + lane_fold(weights, jnp.add)
        sums = jnp.sum(folded, axis=1, keepdims=True)
        scale_ref[rows, :] = jnp.broadcast_to(1.0 / (protos_total * sums), (chunk, 128))
        return carry

    lax.fori_loop(0, thin // chunk, weigh, 0)
    small = min(thin, 64)

    def add_up(index, totals):
        rows = part(index, small)
        scaled = weights_ref[rows, :] * jnp.tile(scale_ref[rows, :], (1, crops_total // 128))
        return totals + row_fold(scaled)

    totals = lax.fori_loop(0, thin // small, add_up, jnp.zeros((8, crops_total), jnp.float32))
    give_copies(copies_ref, jnp.sum(totals, axis=0, keepdims=True))


def first_sweep(index, protos, mine, other, top, copies, thin, protos_total):
    width = protos.shape[1]
    crops_total = 2 * mine.shape[0]
    return pl.pallas_call(
        functools.partial(first_sweep_kernel, min(thin, 512), 256, protos_total),
        in_specs=[whole(pltpu.SMEM), whole(), whole(), whole(), whole()],
        out_specs=[whole(), whole()],
        out_shape=[
            pltpu.VMEM((thin, crops_total), jnp.float32),
            jax.ShapeDtypeStruct((copies, 1, crops_total), jnp.float32),
        ],
        scratch_shapes=[
            pltpu.VMEM((crops_total, width), jnp.bfloat16),
            pltpu.VMEM((thin, 128), jnp.float32),
        ],
        compiler_params=params(12 if crops_total <= 2048 else 40),
        cost_estimate=cost(2 * thin * width * crops_total, 4 * thin * crops_total, thin * crops_total),
        name="first_sweep",
    )(index, protos, mine, other, top)


def crop_scales(parts_ref, crops_total):
    return 1.0 / (crops_total * jnp.sum(parts_ref[...], axis=0))


def next_sweep_kernel(chunk, protos_total, weights_ref, parts_ref, copies_ref, scale_ref):
    thin, crops_total = weights_ref.shape
    crop_scale = crop_scales(parts_ref, crops_total)

    def weigh(index):
        sums = row_sums(weights_ref[part(index, chunk), :] * crop_scale)
        return jnp.broadcast_to(1.0 / (protos_total * sums), (chunk, 128))

    def add_up(index, totals):
        scaled = weights_ref[part(index, chunk), :] * jnp.tile(scale_ref[...], (1, crops_total // 128))
        return totals + row_fold(scaled)

    scale_ref[...] = weigh(0)

    def sweep(index, totals):
        totals = add_up(index - 1, totals)
        scale_ref[...] = weigh(index)
        return totals

    steps = thin // chunk
    totals = lax.fori_loop(1, steps, sweep, jnp.zeros((8, crops_total), jnp.float32))
    totals = add_up(steps - 1, totals)
    give_copies(copies_ref, jnp.sum(totals, axis=0, keepdims=True))


def next_sweep(weights, parts, protos_total):
    thin, crops_total = weights.shape
    copies = parts.shape[0]
    return pl.pallas_call(
        functools.partial(next_sweep_kernel, min(thin, 128), protos_total),
        in_specs=[whole(), whole()],
        out_specs=whole(),
        out_shape=jax.ShapeDtypeStruct((copies, 1, crops_total), jnp.float32),
        scratch_shapes=[pltpu.VMEM((min(thin, 128), 128), jnp.float32)],
        compiler_params=params(8 if crops_total <= 2048 else 40),
        cost_estimate=cost(4 * thin * crops_total, 4 * thin * crops_total),
        name="next_sweep",
    )(resident(weights), parts)


def last_scales_kernel(chunk, protos_total, weights_ref, parts_ref, copies_ref, scale_ref):
    thin, crops_total = weights_ref.shape
    crop_scale = crop_scales(parts_ref, crops_total)

    def weigh(index, carry):
        rows = part(index, chunk)
        folded = lane_fold(weights_ref[rows, :] * crop_scale, jnp.add)
        sums = jnp.sum(jnp.transpose(folded), axis=0, keepdims=True)
        scale_ref[:, rows] = 1.0 / (protos_total * sums)
        return carry

    lax.fori_loop(0, thin // chunk, weigh, 0, unroll=2)
    give_copies(copies_ref, scale_ref[...])


def last_scales(weights, parts, copies, protos_total):
    thin, crops_total = weights.shape
    return pl.pallas_call(
        functools.partial(last_scales_kernel, min(thin, 256), protos_total),
        in_specs=[whole(), whole()],
        out_specs=whole(),
        out_shape=jax.ShapeDtypeStruct((copies, 1, thin), jnp.float32),
        scratch_shapes=[pltpu.VMEM((1, thin), jnp.float32)],
        compiler_params=params(8 if crops_total <= 2048 else 40),
        cost_estimate=cost(2 * thin * crops_total, 4 * thin * crops_total),
        name="last_scales",
    )(resident(weights), parts)


def swap(values, axis, flip):
    return lax.ppermute(values, axis, [(i, i ^ flip) for i in range(lax.axis_size(axis))])


def ordered(values, other, axis, flip, dim):
    upper = (lax.axis_index(axis) // flip) % 2
    return jnp.where(
        upper == 0, jnp.concatenate([values, other], dim), jnp.concatenate([other, values], dim)
    )


def gather_batch(values):
    step = lax.axis_size("batch") // 2
    while step:
        values = ordered(values, swap(values, "batch", step), "batch", step, 0)
        step //= 2
    return values


def bit_reversed(values, count):
    bits = count.bit_length() - 1
    split = values.reshape((2,) * bits + values.shape[1:])
    turned = jnp.transpose(split, tuple(reversed(range(bits))) + tuple(range(bits, split.ndim)))
    return turned.reshape(values.shape)


def send_blocks(blocks):
    return [blocks[0]] + [swap(block, "proto", flip) for flip, block in enumerate(blocks) if flip]


def all_to_all(copies, axes):
    return lax.all_to_all(copies, axes, 0, 0, tiled=True)


def body(crops, teacher_emb, w_first, b_first, w_second, b_second, w_third, b_third, protos):
    batch_index = lax.axis_index("batch")
    proto_index = lax.axis_index("proto")
    batch_size = lax.axis_size("batch")
    proto_size = lax.axis_size("proto")
    devices = batch_size * proto_size
    share_rows = crops.shape[0]
    group_rows = teacher_emb.shape[0]
    crops_total = group_rows * batch_size
    protos_total = protos.shape[0] * proto_size
    thin = protos.shape[0] // batch_size
    hidden_share = w_first.shape[1]
    width = protos.shape[1]
    core = proto_index % 2
    protos = resident(protos)

    own_unit, half = teacher_units(core.reshape(1), teacher_emb)
    crops_pair = jnp.concatenate([crops, swap(crops, "proto", 2)])
    mine = gather_batch(half)
    other = swap(mine, "proto", 1)
    products, top_copies = wide_products(own_unit, protos, devices)
    all_tops = all_to_all(top_copies, BOTH)
    tops = jnp.max(all_tops.reshape(batch_size, proto_size, 256)[:, :, :group_rows], axis=1)
    tops = bit_reversed(tops, batch_size).reshape(batch_size, 2, group_rows // 2)
    tops = jnp.transpose(tops, (1, 0, 2)).reshape(1, crops_total)
    own_weights = wide_weights(batch_index.reshape(1), products, all_tops, proto_size)

    all_crops = jnp.concatenate([crops_pair, swap(crops_pair, "proto", 1)])
    w_third_x = ordered(w_third[None], swap(w_third[None], "proto", 2), "proto", 2, 0)
    w_third_all = ordered(w_third_x[:, None], swap(w_third_x[:, None], "proto", 1), "proto", 1, 1)
    w_third_all = w_third_all.reshape(-1, width)
    first_bias = lax.dynamic_slice_in_dim(b_first, proto_index * hidden_share, hidden_share)
    h_first = jax.nn.gelu(
        jnp.dot(all_crops, w_first, preferred_element_type=jnp.float32) + first_bias,
        approximate=False,
    ).astype(jnp.bfloat16)
    partial_value = jnp.dot(h_first, w_second, preferred_element_type=jnp.float32)
    chip_sum = partial_value[: 2 * share_rows] + swap(partial_value[2 * share_rows :], "proto", 1)
    pre_second = chip_sum[:share_rows] + swap(chip_sum[share_rows:], "proto", 2)
    h_second = jax.nn.gelu(pre_second + b_second, approximate=False).astype(jnp.bfloat16)
    bottleneck = jnp.dot(h_second, w_third_all, preferred_element_type=jnp.float32) + b_third
    unit, lengths = unit_rows(bottleneck)
    rounded = unit.astype(jnp.bfloat16)
    emb_pair = jnp.concatenate([rounded, swap(rounded, "proto", 2)])
    student_emb = jnp.concatenate([emb_pair, swap(emb_pair, "proto", 1)])
    slots = attract(student_emb, protos, proto_size)
    attract_parts = send_blocks([slots[0], slots[2], slots[1], slots[3]])

    index = jnp.stack([batch_index, core])
    weights, copies = first_sweep(index, protos, mine, other, tops, devices, thin, protos_total)
    for _ in range(ITERS - 2):
        copies = next_sweep(weights, all_to_all(copies, BOTH), protos_total)
    scale_copies = last_scales(weights, all_to_all(copies, BOTH), batch_size, protos_total)
    all_scale = all_to_all(scale_copies, "batch")
    repel_parts = send_blocks(repel(proto_index.reshape(1), own_weights, all_scale, protos, proto_size))
    repel_sum = sum(repel_parts)

    tops_in = [block[:, width + 128 : width + 129] for block in attract_parts]
    row_top = functools.reduce(jnp.maximum, tops_in)
    fades = [jnp.exp2((top - row_top) * student_rate) for top in tops_in]
    attract_sum = sum(block[:, :width] * fade for block, fade in zip(attract_parts, fades))
    row_sum = sum(block[:, width : width + 1] * fade for block, fade in zip(attract_parts, fades))
    emb_grad = (
        attract_sum / row_sum - repel_sum[:, :width] / repel_sum[:, width : width + 1]
    ) / student_temp
    crop_grad = (emb_grad - unit * jnp.sum(unit * emb_grad, axis=1, keepdims=True)) / lengths
    return crop_grad


def solution(mesh):
    in_specs = (
        P(("batch", "proto"), None),
        P("batch", None),
        P(None, "proto"),
        P(),
        P("proto", None),
        P(),
        P("proto", None),
        P(),
        P("proto", None),
    )
    out_specs = P(("batch", "proto"), None)
    return jax.shard_map(body, mesh=mesh, in_specs=in_specs, out_specs=out_specs, check_vma=False)
```

time: 442 us -> 157 us (0.36)
  waiting for transfers between devices: 268 us -> 27.8 us
  matrix products: 104 us -> 7.08 us
  local copies, waits for them, and re-layouts: 1.62 us -> 50.4 us
  starting transfers between devices: 0.87 us -> 33.3 us
  blocking collectives: 32 us -> 0 us
  Pallas kernels: 0 us -> 29.2 us
  between operations: 13.5 us -> 0.31 us
  other arithmetic: 20.9 us -> 7.76 us
    psum x4 -> x0, waiting for transfers between devices: 220 us -> none  [the longest x3 199 us: proto_scales(): row_total = lax.psum(local_rows, 'batch')]
    dot_general x9 -> x1, matrix products: 99.6 us -> 2.46 us  [body(): jnp.dot(h_second, w_third_all, preferred_element_type=jnp.float32) + b_third]
    reduce_scatter x2 -> x0, waiting for transfers between devices: 48.3 us -> none  [the longest x1 28.3 us: body(): lax.psum_scatter(partial_value, 'proto', scatter_dimension=1, tiled=True)]
    unnamed x8 -> x36, local copies, waits for them, and re-layouts: 0.02 us -> 46.4 us
    pallas_call x0 -> x8, Pallas kernels: none -> 29.2 us  [the longest x1 7.74 us: attract(): pl.pallas_call(functools.partial(attract_kernel, min(count, 1024)), in_sp...]
    ppermute x0 -> x18, starting transfers between devices: none -> 17.7 us  [swap(): lax.ppermute(values, axis, [(i, i ^ flip) for i in range(lax.axis_size(ax...]
    psum x3 -> x0, blocking collectives: 17 us -> none  [body(): lax.psum(jnp.dot(weights_e, proto_scale, precision=lax.Precision.HIGHEST)...]
    all_to_all x0 -> x4, starting transfers between devices: none -> 15.6 us  [all_to_all(): return lax.all_to_all(copies, axes, 0, 0, tiled=True)]
  transfers between devices with their start and end apart: 6 -> 22, of which waited for: 6 -> 10; matrix products, arithmetic and copies ran while one was open for 4% -> 11% of each run, Pallas kernels for 0% -> 14%
where the time goes in v4:
time: 157 us; the launch traced here: 156 us
  local copies, waits for them, and re-layouts  50.4 us (32%)
  starting transfers between devices  33.3 us (21%)
  Pallas kernels  29.2 us (19%)
  waiting for transfers between devices  27.8 us (18%)
  other arithmetic  7.76 us (5%)
  matrix products  7.08 us (5%)
    unnamed x36, local copies, waits for them, and re-layouts  46.4 us
    ppermute x18, starting transfers between devices, swap(): lax.ppermute(values, axis, [(i, i ^ flip) for i in range(lax.axis_size(ax...  17.7 us
    all_to_all x4, starting transfers between devices, all_to_all(): return lax.all_to_all(copies, axes, 0, 0, tiled=True)  15.6 us
    all_to_all x4, waiting for transfers between devices, all_to_all(): return lax.all_to_all(copies, axes, 0, 0, tiled=True)  14.7 us
    ppermute x18, waiting for transfers between devices, swap(): lax.ppermute(values, axis, [(i, i ^ flip) for i in range(lax.axis_size(ax...  13.2 us
    pallas_call x1, Pallas kernels, attract(): pl.pallas_call(functools.partial(attract_kernel, min(count, 1024)), in_sp...  7.74 us
    pallas_call x1, Pallas kernels, first_sweep(): pl.pallas_call(functools.partial(first_sweep_kernel, min(thin, 512), 256,...  5.3 us
    pallas_call x1, Pallas kernels, wide_products(): pl.pallas_call(functools.partial(wide_products_kernel, min(count, 1024)),...  4.78 us
  transfers between devices with their start and end apart: 22, of which 10 were waited for; matrix products, arithmetic and copies ran while one was open for 11% of the time, Pallas kernels for 14%

profile of v4, /device:TPU:0, one launch (start us, length us, event | category | flops | bytes accessed | tf_op | source)
XLA Modules:
  0.0 155.9 jit_solution(13481324762632908608)
XLA Ops:
  0.0 2.9 %collective-permute-start = (bf16[48,1536]{1,0:T(8,128)(2,1)}, bf16[48,1536]{1,0:T(8,128)(2,1)S(1)}, u32[]{:S(2)}, u32[]{:S(2)}) collective-permute-start(bf16[48,1536]{1,0:T(8,128)(2,1)} %param.9), channel_id=1, source_target_pairs={{0,2},{1,3},{2,0},{3,1},{4,6},{5,7},{6,4},{7,5},{8,10},{9,11},{10,... | collective-permute-start | bytes 442376 | tf_op jit(solution)/shard_map/ppermute | solution.py:399
  2.9 0.9 copy-done.12
  3.8 0.1 teacher_units.1
  4.0 2.7 %collective-permute-start.11 = (bf16[96,256]{1,0:T(8,128)(2,1)S(1)}, bf16[96,256]{1,0:T(8,128)(2,1)S(1)}, u32[]{:S(2)}, u32[]{:S(2)}) collective-permute-start(bf16[96,256]{1,0:T(8,128)(2,1)S(1)} %get-tuple-element.26), channel_id=1, source_target_pairs={{0,16},{4,20},{8,24},{12,28},{16,0},{20,4},{24,8},{28,12},{1,17},{... | collective-permute-start | bytes 147464 | tf_op jit(solution)/shard_map/ppermute | solution.py:399
  6.6 0.4 collective-permute-done
  7.0 0.9 pad_maximum_fusion
  8.0 1.1 collective-permute-done.11
  9.2 1.5 collective-permute-start.12
  10.7 0.8 dynamic_slice.3
  11.5 2.4 %collective-permute-done.12 = bf16[192,256]{1,0:T(8,128)(2,1)S(1)} collective-permute-done((bf16[192,256]{1,0:T(8,128)(2,1)S(1)}, bf16[192,256]{1,0:T(8,128)(2,1)S(1)}, u32[]{:S(2)}, u32[]{:S(2)}) %collective-permute-start.12) | collective-permute-done | bytes 98336 | tf_op jit(solution)/shard_map/ppermute | solution.py:399
  13.9 1.6 %collective-permute-start.13 = (bf16[384,256]{1,0:T(8,128)(2,1)S(1)}, bf16[384,256]{1,0:T(8,128)(2,1)S(1)}, u32[]{:S(2)}, u32[]{:S(2)}) collective-permute-start(bf16[384,256]{1,0:T(8,128)(2,1)S(1)} %maximum_select_fusion.3), channel_id=1, source_target_pairs={{0,4},{4,0},{8,12},{12,8},{16,20},{20,16},{24,28},{28,24},{1,5},{5... | collective-permute-start | bytes 589832 | tf_op jit(solution)/shard_map/ppermute | solution.py:399
  15.5 4.6 %fusion.29 = f32[192,2048]{1,0:T(8,128)} fusion(bf16[512,2048]{1,0:T(8,128)(2,1)S(1)} %copy-done, bf16[1536,512]{1,0:T(8,128)(2,1)} %param.11, bf16[96,1536]{1,0:T(8,128)(2,1)} %collective-permute-done.1, bf16[48,1536]{1,0:T(8,128)(2,1)S(1)} %collective-permute-done, bf16[48,1536]{1,0:T(8,128)(2,1)} %param.9, f32[512]{0:T(512)S(1)} %dynamic_slice.3), kind=kOutput, calls=%fused_computation.51 | convolution fusion | flops 712900608 | bytes 5834752 | tf_op jit(solution)/shard_map/dot_general | solution.py:468
  20.1 2.1 %slice.77 = f32[96,2048]{1,0:T(8,128)} slice(f32[192,2048]{1,0:T(8,128)} %fusion.29), slice={[96:192], [0:2048]} | slice | bytes 1572864 | tf_op jit(solution)/shard_map/slice | solution.py:469
  22.3 1.2 collective-permute-start.4
  23.4 0.2 maximum_select_fusion.2.mine_ref
  23.6 0.3 collective-permute-start.14
  23.9 3.4 %copy-done.1 = bf16[16384,256]{1,0:T(8,128)(2,1)S(1)} copy-done((bf16[16384,256]{1,0:T(8,128)(2,1)S(1)}, bf16[16384,256]{1,0:T(8,128)(2,1)}, u32[]{:S(2)}) %copy-start.1) | copy-done | bytes 8388632
  27.3 4.8 %wide_products.1 = (f32[192,16384]{1,0:T(8,128)S(1)}, f32[32,1,256]{2,1,0:T(1,128)}) custom-call(bf16[192,256]{1,0:T(8,128)(2,1)S(1)} %get-tuple-element.23.unit_ref, bf16[16384,256]{1,0:T(8,128)(2,1)S(1)} %copy-done.1), custom_call_target="tpu_custom_call" | custom-call | flops 1610612736 | bytes 20971520 | tf_op jit(solution)/shard_map/wide_products/pallas_call | solution.py:107
  32.1 4.5 %copy-done.8 = f32[192,16384]{1,0:T(8,128)} copy-done((f32[192,16384]{1,0:T(8,128)}, f32[192,16384]{1,0:T(8,128)S(1)}, u32[]{:S(2)}) %copy-start.8) | copy-done | bytes 12582936
  36.6 4.5 %all-to-all-start = ((f32[32,1,256]{2,1,0:T(1,128)}), f32[32,1,256]{2,1,0:T(1,128)S(1)}, u32[]{:S(2)}, u32[]{:S(2)}) async-start(f32[32,1,256]{2,1,0:T(1,128)} %get-tuple-element.25), calls=%async_computation | async-start | bytes 65536 | tf_op jit(solution)/shard_map/all_to_all | solution.py:429
  41.2 7.1 %all-to-all-done.tops_ref = f32[32,1,256]{2,1,0:T(1,128)S(1)} async-done(((f32[32,1,256]{2,1,0:T(1,128)}), f32[32,1,256]{2,1,0:T(1,128)S(1)}, u32[]{:S(2)}, u32[]{:S(2)}) %all-to-all-start) | async-done | bytes 32800 | tf_op jit(solution)/shard_map/all_to_all | solution.py:429
  48.7 1.3 maximum_select_fusion.1
  50.0 0.2 collective-permute-start.5
  50.2 3.4 %copy-done.2 = bf16[16384,256]{1,0:T(8,128)(2,1)S(1)} copy-done((bf16[16384,256]{1,0:T(8,128)(2,1)S(1)}, bf16[16384,256]{1,0:T(8,128)(2,1)}, u32[]{:S(2)}) %copy-start.2) | copy-done | bytes 8388632
  53.6 5.3 %first_sweep.1 = (f32[2048,1536]{1,0:T(8,128)S(1)}, f32[32,1,1536]{2,1,0:T(1,128)}) custom-call(s32[2]{0:T(128)S(1)} %pad_add_fusion.index_ref, bf16[16384,256]{1,0:T(8,128)(2,1)S(1)} %copy-done.2, bf16[768,256]{1,0:T(8,128)(2,1)S(1)} %maximum_select_fusion.2.mine_ref, bf16[768,256]{1,0:T(8,128)(2,1)S(1)} %collective-permute-done.14.other_ref, ...), custom_call_target="tpu_custom_call" | custom-call | flops 1610612736 | bytes 12582912 | tf_op jit(solution)/shard_map/first_sweep/pallas_call | solution.py:307
  58.9 4.5 %copy-done.5 = f32[2048,1536]{1,0:T(8,128)} copy-done((f32[2048,1536]{1,0:T(8,128)}, f32[2048,1536]{1,0:T(8,128)S(1)}, u32[]{:S(2)}) %copy-start.5) | copy-done | bytes 12582936
  63.4 2.6 %all-to-all-start.1 = ((f32[32,1,1536]{2,1,0:T(1,128)}), f32[32,1,1536]{2,1,0:T(1,128)S(1)}, u32[]{:S(2)}, u32[]{:S(2)}) async-start(f32[32,1,1536]{2,1,0:T(1,128)} %get-tuple-element.28), calls=%async_computation.1 | async-start | bytes 393216 | tf_op jit(solution)/shard_map/all_to_all | solution.py:429
  66.0 1.5 slice_add_fusion
  67.5 0.8 slice.79
  68.3 0.2 copy-done.13
  68.4 1.6 %collective-permute-start.3 = (f32[48,2048]{1,0:T(8,128)}, f32[48,2048]{1,0:T(8,128)}, u32[]{:S(2)}, u32[]{:S(2)}) collective-permute-start(f32[48,2048]{1,0:T(8,128)} %slice.79), channel_id=1, source_target_pairs={{0,2},{1,3},{2,0},{3,1},{4,6},{5,7},{6,4},{7,5},{8,10},{9,11},{10,... | collective-permute-start | bytes 1179656 | tf_op jit(solution)/shard_map/ppermute | solution.py:399
  70.1 4.8 %all-to-all-done.1.parts_ref = f32[32,1,1536]{2,1,0:T(1,128)S(1)} async-done(((f32[32,1,1536]{2,1,0:T(1,128)}), f32[32,1,1536]{2,1,0:T(1,128)S(1)}, u32[]{:S(2)}, u32[]{:S(2)}) %all-to-all-start.1) | async-done | bytes 196640 | tf_op jit(solution)/shard_map/all_to_all | solution.py:429
  74.9 4.6 %copy-done.6 = f32[2048,1536]{1,0:T(8,128)S(1)} copy-done((f32[2048,1536]{1,0:T(8,128)S(1)}, f32[2048,1536]{1,0:T(8,128)}, u32[]{:S(2)}) %copy-start.6) | copy-done | bytes 12582936
  79.4 3.2 %next_sweep.1 = f32[32,1,1536]{2,1,0:T(1,128)} custom-call(f32[2048,1536]{1,0:T(8,128)S(1)} %copy-done.6, f32[32,1,1536]{2,1,0:T(1,128)S(1)} %all-to-all-done.1.parts_ref), custom_call_target="tpu_custom_call" | custom-call | flops 12582912 | bytes 12582912 | tf_op jit(solution)/shard_map/next_sweep/pallas_call | solution.py:357
  82.6 2.6 %all-to-all-start.2 = ((f32[32,1,1536]{2,1,0:T(1,128)}), f32[32,1,1536]{2,1,0:T(1,128)S(1)}, u32[]{:S(2)}, u32[]{:S(2)}) async-start(f32[32,1,1536]{2,1,0:T(1,128)} %next_sweep.1), calls=%async_computation.2 | async-start | bytes 393216 | tf_op jit(solution)/shard_map/all_to_all | solution.py:429
  85.2 4.6 %copy-done.9 = f32[192,16384]{1,0:T(8,128)S(1)} copy-done((f32[192,16384]{1,0:T(8,128)S(1)}, f32[192,16384]{1,0:T(8,128)}, u32[]{:S(2)}) %copy-start.9) | copy-done | bytes 12582936
  89.8 2.5 %wide_weights.1.weights_ref = f32[192,16384]{1,0:T(8,128)S(1)} custom-call(s32[1]{0:T(128)} %bitcast.5.batch_ref, f32[192,16384]{1,0:T(8,128)S(1)} %copy-done.9, f32[32,1,256]{2,1,0:T(1,128)S(1)} %all-to-all-done.tops_ref), custom_call_target="tpu_custom_call", output_to_operand_aliasing={{}: (1, {})} | custom-call | flops 6291456 | bytes 25165824 | tf_op jit(solution)/shard_map/wide_weights/pallas_call | solution.py:142
  92.3 4.5 %copy-done.10 = f32[192,16384]{1,0:T(8,128)} copy-done((f32[192,16384]{1,0:T(8,128)}, f32[192,16384]{1,0:T(8,128)S(1)}, u32[]{:S(2)}) %copy-start.10) | copy-done | bytes 12582936
  96.8 2.4 %maximum_select_fusion = bf16[2,2,512,256]{3,2,1,0:T(8,128)(2,1)} fusion(bf16[2,1,512,256]{3,2,1,0:T(8,128)(2,1)} %collective-permute-done.5, bf16[2,1,512,256]{3,2,1,0:T(8,128)(2,1)S(1)} %maximum_select_fusion.1, pred[]{:T(512)S(6)} %eq.22), kind=kLoop, calls=%fused_computation.2 | loop fusion | flops 1572864 | bytes 2097153 | tf_op jit(solution)/shard_map/jit(_where)/select_n | solution.py:404
  99.2 4.6 %copy-done.7 = f32[2048,1536]{1,0:T(8,128)S(1)} copy-done((f32[2048,1536]{1,0:T(8,128)S(1)}, f32[2048,1536]{1,0:T(8,128)}, u32[]{:S(2)}) %copy-start.7) | copy-done | bytes 12582936
  103.8 1.9 %last_scales.1 = f32[8,1,2048]{2,1,0:T(1,128)} custom-call(f32[2048,1536]{1,0:T(8,128)S(1)} %copy-done.7, f32[32,1,1536]{2,1,0:T(1,128)S(1)} %all-to-all-done.2.parts_ref), custom_call_target="tpu_custom_call" | custom-call | flops 6291456 | bytes 12582912 | tf_op jit(solution)/shard_map/last_scales/pallas_call | solution.py:386
  105.8 5.8 %all-to-all-start.3 = ((f32[8,1,2048]{2,1,0:T(1,128)}), f32[8,1,2048]{2,1,0:T(1,128)S(1)}, u32[]{:S(2)}, u32[]{:S(2)}) async-start(f32[8,1,2048]{2,1,0:T(1,128)} %last_scales.1), calls=%async_computation.3 | async-start | bytes 131072 | tf_op jit(solution)/shard_map/all_to_all | solution.py:429
  111.6 2.5 %multiply_reduce_fusion.1 = (f32[48]{0:T(128)S(1)}, f32[48,256]{1,0:T(8,128)S(1)}) fusion(f32[256]{0:T(256)S(1)} %copy-done.17, bf16[2048,256]{1,0:T(8,128)(2,1)} %bitcast.12, f32[48,2048]{1,0:T(8,128)} %collective-permute-done.3, f32[96,2048]{1,0:T(8,128)S(1)} %copy-done.14, f32[2048]{0:T(1024)S(1)} %copy-done.16), kind=kOutput, calls=%fused_computation.132 | convolution fusion | flops 56954832 | bytes 1893568 | tf_op jit(solution)/shard_map/dot_general | solution.py:472
  114.2 1.5 collective-permute-start.6
  115.7 2.7 %all-to-all-done.3.scale_ref = f32[8,1,2048]{2,1,0:T(1,128)S(1)} async-done(((f32[8,1,2048]{2,1,0:T(1,128)}), f32[8,1,2048]{2,1,0:T(1,128)S(1)}, u32[]{:S(2)}, u32[]{:S(2)}) %all-to-all-start.3) | async-done | bytes 65568 | tf_op jit(solution)/shard_map/all_to_all | solution.py:429
  118.5 3.4 %copy-done.3 = bf16[16384,256]{1,0:T(8,128)(2,1)S(1)} copy-done((bf16[16384,256]{1,0:T(8,128)(2,1)S(1)}, bf16[16384,256]{1,0:T(8,128)(2,1)}, u32[]{:S(2)}) %copy-start.3) | copy-done | bytes 8388632
  121.9 4.6 %copy-done.11 = f32[192,16384]{1,0:T(8,128)S(1)} copy-done((f32[192,16384]{1,0:T(8,128)S(1)}, f32[192,16384]{1,0:T(8,128)}, u32[]{:S(2)}) %copy-start.11) | copy-done | bytes 12582936
  126.4 3.6 %repel.1 = (f32[48,384]{1,0:T(8,128)S(1)}, f32[48,384]{1,0:T(8,128)S(1)}, f32[48,384]{1,0:T(8,128)S(1)}, f32[48,384]{1,0:T(8,128)S(1)}) custom-call(s32[1]{0:T(128)} %bitcast.4.proto_ref, f32[192,16384]{1,0:T(8,128)S(1)} %copy-done.11, f32[8,1,2048]{2,1,0:T(1,128)S(1)} %all-to-all-done.3.scale_ref, bf16[16384,256]{1,0:T(8,128)(2,1)S(1)} %copy-done.3), custom_call_target="tpu_custom_call" | custom-call | flops 1610612736 | bytes 20971520 | tf_op jit(solution)/shard_map/repel/pallas_call | solution.py:187
  130.1 1.5 collective-permute-start.16
  131.7 0.3 collective-permute-start.15
  132.0 0.3 collective-permute-start.7
  132.3 2.4 %collective-permute-done.17 = f32[48,384]{1,0:T(8,128)S(1)} collective-permute-done((f32[48,384]{1,0:T(8,128)S(1)}, f32[48,384]{1,0:T(8,128)S(1)}, u32[]{:S(2)}, u32[]{:S(2)}) %collective-permute-start.17) | collective-permute-done | bytes 73760 | tf_op jit(solution)/shard_map/ppermute | solution.py:399
  134.7 1.6 %collective-permute-done.16 = f32[48,384]{1,0:T(8,128)S(1)} collective-permute-done((f32[48,384]{1,0:T(8,128)S(1)}, f32[48,384]{1,0:T(8,128)S(1)}, u32[]{:S(2)}, u32[]{:S(2)}) %collective-permute-start.16) | collective-permute-done | bytes 73760 | tf_op jit(solution)/shard_map/ppermute | solution.py:399
  136.3 3.4 %copy-done.4 = bf16[16384,256]{1,0:T(8,128)(2,1)S(1)} copy-done((bf16[16384,256]{1,0:T(8,128)(2,1)S(1)}, bf16[16384,256]{1,0:T(8,128)(2,1)}, u32[]{:S(2)}) %copy-start.4) | copy-done | bytes 8388632
  139.7 7.7 %attract.1 = (f32[48,512]{1,0:T(8,128)S(1)}, f32[48,512]{1,0:T(8,128)S(1)}, f32[48,512]{1,0:T(8,128)S(1)}, f32[48,512]{1,0:T(8,128)S(1)}) custom-call(bf16[192,256]{1,0:T(8,128)(2,1)S(1)} %pad_maximum_fusion.1.emb_ref, bf16[16384,256]{1,0:T(8,128)(2,1)S(1)} %copy-done.4), custom_call_target="tpu_custom_call" | custom-call | flops 3221225472 | bytes 8388608 | tf_op jit(solution)/shard_map/attract/pallas_call | solution.py:242
  147.5 0.3 collective-permute-start.10
  147.7 1.5 collective-permute-start.9
  149.2 0.2 collective-permute-start.8
  149.4 0.1 slice_reduce_fusion.1
  149.5 2.8 %collective-permute-done.10 = f32[48,512]{1,0:T(8,128)S(1)} collective-permute-done((f32[48,512]{1,0:T(8,128)S(1)}, f32[48,512]{1,0:T(8,128)S(1)}, u32[]{:S(2)}, u32[]{:S(2)}) %collective-permute-start.10) | collective-permute-done | bytes 98336 | tf_op jit(solution)/shard_map/ppermute | solution.py:399
  152.4 2.4 %collective-permute-done.9 = f32[48,512]{1,0:T(8,128)S(1)} collective-permute-done((f32[48,512]{1,0:T(8,128)S(1)}, f32[48,512]{1,0:T(8,128)S(1)}, u32[]{:S(2)}, u32[]{:S(2)}) %collective-permute-start.9) | collective-permute-done | bytes 98336 | tf_op jit(solution)/shard_map/ppermute | solution.py:399
  154.7 0.2 fusion.104
  154.9 0.2 multiply_reduce_fusion
  155.2 0.7 subtract_divide_fusion
  (54 shorter events, 0.8 us)
Async XLA Ops:
  0.0 15.5 %copy-start = (bf16[512,2048]{1,0:T(8,128)(2,1)S(1)}, bf16[512,2048]{1,0:T(8,128)(2,1)}, u32[]{:S(2)}) copy-start(bf16[512,2048]{1,0:T(8,128)(2,1)} %param.13) | copy-start | bytes 6291460
  0.0 7.0 %collective-permute-start = (bf16[48,1536]{1,0:T(8,128)(2,1)}, bf16[48,1536]{1,0:T(8,128)(2,1)S(1)}, u32[]{:S(2)}, u32[]{:S(2)}) collective-permute-start(bf16[48,1536]{1,0:T(8,128)(2,1)} %param.9), channel_id=1, source_target_pairs={{0,2},{1,3},{2,0},{3,1},{4,6},{5,7},{6,4},{7,5},{8,10},{9,11},{10,... | collective-permute-start | bytes 442376 | tf_op jit(solution)/shard_map/ppermute | solution.py:399
  2.9 0.9 copy-start.12
  4.0 5.2 %collective-permute-start.11 = (bf16[96,256]{1,0:T(8,128)(2,1)S(1)}, bf16[96,256]{1,0:T(8,128)(2,1)S(1)}, u32[]{:S(2)}, u32[]{:S(2)}) collective-permute-start(bf16[96,256]{1,0:T(8,128)(2,1)S(1)} %get-tuple-element.26), channel_id=1, source_target_pairs={{0,16},{4,20},{8,24},{12,28},{16,0},{20,4},{24,8},{28,12},{1,17},{... | collective-permute-start | bytes 147464 | tf_op jit(solution)/shard_map/ppermute | solution.py:399
  7.9 7.6 %collective-permute-start.1 = (bf16[96,1536]{1,0:T(8,128)(2,1)S(1)}, bf16[96,1536]{1,0:T(8,128)(2,1)}, u32[]{:S(2)}, u32[]{:S(2)}) collective-permute-start(bf16[96,1536]{1,0:T(8,128)(2,1)S(1)} %pad_maximum_fusion), channel_id=1, source_target_pairs={{0,1},{1,0},{2,3},{3,2},{4,5},{5,4},{6,7},{7,6},{8,9},{9,8},{10,11... | collective-permute-start | bytes 884744 | tf_op jit(solution)/shard_map/ppermute | solution.py:399
  9.2 4.7 %collective-permute-start.12 = (bf16[192,256]{1,0:T(8,128)(2,1)S(1)}, bf16[192,256]{1,0:T(8,128)(2,1)S(1)}, u32[]{:S(2)}, u32[]{:S(2)}) collective-permute-start(bf16[192,256]{1,0:T(8,128)(2,1)S(1)} %maximum_select_fusion.4), channel_id=1, source_target_pairs={{0,8},{4,12},{8,0},{12,4},{16,24},{20,28},{24,16},{28,20},{1,9},{5... | collective-permute-start | bytes 294920 | tf_op jit(solution)/shard_map/ppermute | solution.py:399
  13.9 9.5 %collective-permute-start.13 = (bf16[384,256]{1,0:T(8,128)(2,1)S(1)}, bf16[384,256]{1,0:T(8,128)(2,1)S(1)}, u32[]{:S(2)}, u32[]{:S(2)}) collective-permute-start(bf16[384,256]{1,0:T(8,128)(2,1)S(1)} %maximum_select_fusion.3), channel_id=1, source_target_pairs={{0,4},{4,0},{8,12},{12,8},{16,20},{20,16},{24,28},{28,24},{1,5},{5... | collective-permute-start | bytes 589832 | tf_op jit(solution)/shard_map/ppermute | solution.py:399
  20.1 2.1 %copy-start.15 = (bf16[512,256]{1,0:T(8,128)(2,1)S(1)}, bf16[512,256]{1,0:T(8,128)(2,1)}, u32[]{:S(2)}) copy-start(bf16[512,256]{1,0:T(8,128)(2,1)} %param.15) | copy-start | bytes 786436
  22.2 43.7 %collective-permute-start.2 = (f32[96,2048]{1,0:T(8,128)}, f32[96,2048]{1,0:T(8,128)}, u32[]{:S(2)}, u32[]{:S(2)}) collective-permute-start(f32[96,2048]{1,0:T(8,128)} %slice.77), channel_id=1, source_target_pairs={{0,1},{1,0},{2,3},{3,2},{4,5},{5,4},{6,7},{7,6},{8,9},{9,8},{10,11... | collective-permute-start | bytes 2359304 | tf_op jit(solution)/shard_map/ppermute | solution.py:399
  22.3 26.4 %collective-permute-start.4 = (bf16[1,512,256]{2,1,0:T(8,128)(2,1)S(1)}, bf16[1,512,256]{2,1,0:T(8,128)(2,1)}, u32[]{:S(2)}, u32[]{:S(2)}) collective-permute-start(bf16[1,512,256]{2,1,0:T(8,128)(2,1)S(1)} %bitcast.14), channel_id=1, source_target_pairs={{0,2},{1,3},{2,0},{3,1},{4,6},{5,7},{6,4},{7,5},{8,10},{9,11},{10,... | collective-permute-start | bytes 786440 | tf_op jit(solution)/shard_map/ppermute | solution.py:399
  23.6 26.6 %collective-permute-start.14 = (bf16[768,256]{1,0:T(8,128)(2,1)S(1)}, bf16[768,256]{1,0:T(8,128)(2,1)S(1)}, u32[]{:S(2)}, u32[]{:S(2)}) collective-permute-start(bf16[768,256]{1,0:T(8,128)(2,1)S(1)} %maximum_select_fusion.2.mine_ref), channel_id=1, source_target_pairs={{0,1},{1,0},{2,3},{3,2},{4,5},{5,4},{6,7},{7,6},{8,9},{9,8},{10,11... | collective-permute-start | bytes 1179656 | tf_op jit(solution)/shard_map/ppermute | solution.py:399
  23.9 3.4 %copy-start.1 = (bf16[16384,256]{1,0:T(8,128)(2,1)S(1)}, bf16[16384,256]{1,0:T(8,128)(2,1)}, u32[]{:S(2)}) copy-start(bf16[16384,256]{1,0:T(8,128)(2,1)} %protos_ref.7) | copy-start | bytes 25165828
  32.1 4.5 %copy-start.8 = (f32[192,16384]{1,0:T(8,128)}, f32[192,16384]{1,0:T(8,128)S(1)}, u32[]{:S(2)}) copy-start(f32[192,16384]{1,0:T(8,128)S(1)} %get-tuple-element.24.products_ref) | copy-start | bytes 37748740
  36.6 11.8 %all-to-all-start = ((f32[32,1,256]{2,1,0:T(1,128)}), f32[32,1,256]{2,1,0:T(1,128)S(1)}, u32[]{:S(2)}, u32[]{:S(2)}) async-start(f32[32,1,256]{2,1,0:T(1,128)} %get-tuple-element.25), calls=%async_computation | async-start | bytes 65536 | tf_op jit(solution)/shard_map/all_to_all | solution.py:429
  50.0 46.8 %collective-permute-start.5 = (bf16[2,1,512,256]{3,2,1,0:T(8,128)(2,1)S(1)}, bf16[2,1,512,256]{3,2,1,0:T(8,128)(2,1)}, u32[]{:S(2)}, u32[]{:S(2)}) collective-permute-start(bf16[2,1,512,256]{3,2,1,0:T(8,128)(2,1)S(1)} %maximum_select_fusion.1), channel_id=1, source_target_pairs={{0,1},{1,0},{2,3},{3,2},{4,5},{5,4},{6,7},{7,6},{8,9},{9,8},{10,11... | collective-permute-start | bytes 1572872 | tf_op jit(solution)/shard_map/ppermute | solution.py:399
  50.2 3.4 %copy-start.2 = (bf16[16384,256]{1,0:T(8,128)(2,1)S(1)}, bf16[16384,256]{1,0:T(8,128)(2,1)}, u32[]{:S(2)}) copy-start(bf16[16384,256]{1,0:T(8,128)(2,1)} %protos_ref.7) | copy-start | bytes 25165828
  58.9 4.5 %copy-start.5 = (f32[2048,1536]{1,0:T(8,128)}, f32[2048,1536]{1,0:T(8,128)S(1)}, u32[]{:S(2)}) copy-start(f32[2048,1536]{1,0:T(8,128)S(1)} %get-tuple-element.27.weights_ref) | copy-start | bytes 37748740
  63.4 11.5 %all-to-all-start.1 = ((f32[32,1,1536]{2,1,0:T(1,128)}), f32[32,1,1536]{2,1,0:T(1,128)S(1)}, u32[]{:S(2)}, u32[]{:S(2)}) async-start(f32[32,1,1536]{2,1,0:T(1,128)} %get-tuple-element.28), calls=%async_computation.1 | async-start | bytes 393216 | tf_op jit(solution)/shard_map/all_to_all | solution.py:429
  67.4 1.0 copy-start.13
  68.4 43.1 %collective-permute-start.3 = (f32[48,2048]{1,0:T(8,128)}, f32[48,2048]{1,0:T(8,128)}, u32[]{:S(2)}, u32[]{:S(2)}) collective-permute-start(f32[48,2048]{1,0:T(8,128)} %slice.79), channel_id=1, source_target_pairs={{0,2},{1,3},{2,0},{3,1},{4,6},{5,7},{6,4},{7,5},{8,10},{9,11},{10,... | collective-permute-start | bytes 1179656 | tf_op jit(solution)/shard_map/ppermute | solution.py:399
  74.9 4.6 %copy-start.6 = (f32[2048,1536]{1,0:T(8,128)S(1)}, f32[2048,1536]{1,0:T(8,128)}, u32[]{:S(2)}) copy-start(f32[2048,1536]{1,0:T(8,128)} %copy-done.5) | copy-start | bytes 37748740
  82.6 16.6 %all-to-all-start.2 = ((f32[32,1,1536]{2,1,0:T(1,128)}), f32[32,1,1536]{2,1,0:T(1,128)S(1)}, u32[]{:S(2)}, u32[]{:S(2)}) async-start(f32[32,1,1536]{2,1,0:T(1,128)} %next_sweep.1), calls=%async_computation.2 | async-start | bytes 393216 | tf_op jit(solution)/shard_map/all_to_all | solution.py:429
  85.2 4.6 %copy-start.9 = (f32[192,16384]{1,0:T(8,128)S(1)}, f32[192,16384]{1,0:T(8,128)}, u32[]{:S(2)}) copy-start(f32[192,16384]{1,0:T(8,128)} %copy-done.8) | copy-start | bytes 37748740
  92.3 4.5 %copy-start.10 = (f32[192,16384]{1,0:T(8,128)}, f32[192,16384]{1,0:T(8,128)S(1)}, u32[]{:S(2)}) copy-start(f32[192,16384]{1,0:T(8,128)S(1)} %wide_weights.1.weights_ref) | copy-start | bytes 37748740
  99.2 4.6 %copy-start.7 = (f32[2048,1536]{1,0:T(8,128)S(1)}, f32[2048,1536]{1,0:T(8,128)}, u32[]{:S(2)}) copy-start(f32[2048,1536]{1,0:T(8,128)} %copy-done.5) | copy-start | bytes 37748740
  103.8 7.8 %copy-start.14 = (f32[96,2048]{1,0:T(8,128)S(1)}, f32[96,2048]{1,0:T(8,128)}, u32[]{:S(2)}) copy-start(f32[96,2048]{1,0:T(8,128)} %copy-done.13) | copy-start | bytes 2359300
  103.8 7.8 %copy-start.16 = (f32[2048]{0:T(1024)S(1)}, f32[2048]{0:T(1024)}, u32[]{:S(2)}) copy-start(f32[2048]{0:T(1024)} %param.14) | copy-start | bytes 24580
  103.8 7.8 %copy-start.17 = (f32[256]{0:T(256)S(1)}, f32[256]{0:T(256)}, u32[]{:S(2)}) copy-start(f32[256]{0:T(256)} %param.16) | copy-start | bytes 3076
  105.8 12.7 %all-to-all-start.3 = ((f32[8,1,2048]{2,1,0:T(1,128)}), f32[8,1,2048]{2,1,0:T(1,128)S(1)}, u32[]{:S(2)}, u32[]{:S(2)}) async-start(f32[8,1,2048]{2,1,0:T(1,128)} %last_scales.1), calls=%async_computation.3 | async-start | bytes 131072 | tf_op jit(solution)/shard_map/all_to_all | solution.py:429
  114.2 17.8 %collective-permute-start.6 = (bf16[48,256]{1,0:T(8,128)(2,1)S(1)}, bf16[48,256]{1,0:T(8,128)(2,1)S(1)}, u32[]{:S(2)}, u32[]{:S(2)}) collective-permute-start(bf16[48,256]{1,0:T(8,128)(2,1)S(1)} %fusion.170), channel_id=1, source_target_pairs={{0,2},{1,3},{2,0},{3,1},{4,6},{5,7},{6,4},{7,5},{8,10},{9,11},{10,... | collective-permute-start | bytes 73736 | tf_op jit(solution)/shard_map/ppermute | solution.py:399
  118.5 3.4 %copy-start.3 = (bf16[16384,256]{1,0:T(8,128)(2,1)S(1)}, bf16[16384,256]{1,0:T(8,128)(2,1)}, u32[]{:S(2)}) copy-start(bf16[16384,256]{1,0:T(8,128)(2,1)} %protos_ref.7) | copy-start | bytes 25165828
  121.9 4.6 %copy-start.11 = (f32[192,16384]{1,0:T(8,128)S(1)}, f32[192,16384]{1,0:T(8,128)}, u32[]{:S(2)}) copy-start(f32[192,16384]{1,0:T(8,128)} %copy-done.10) | copy-start | bytes 37748740
  130.1 4.6 %collective-permute-start.17 = (f32[48,384]{1,0:T(8,128)S(1)}, f32[48,384]{1,0:T(8,128)S(1)}, u32[]{:S(2)}, u32[]{:S(2)}) collective-permute-start(f32[48,384]{1,0:T(8,128)S(1)} %get-tuple-element.32), channel_id=1, source_target_pairs={{0,3},{1,2},{2,1},{3,0},{4,7},{5,6},{6,5},{7,4},{8,11},{9,10},{10,... | collective-permute-start | bytes 221192 | tf_op jit(solution)/shard_map/ppermute | solution.py:399
  130.1 6.1 %collective-permute-start.16 = (f32[48,384]{1,0:T(8,128)S(1)}, f32[48,384]{1,0:T(8,128)S(1)}, u32[]{:S(2)}, u32[]{:S(2)}) collective-permute-start(f32[48,384]{1,0:T(8,128)S(1)} %get-tuple-element.31), channel_id=1, source_target_pairs={{0,2},{1,3},{2,0},{3,1},{4,6},{5,7},{6,4},{7,5},{8,10},{9,11},{10,... | collective-permute-start | bytes 221192 | tf_op jit(solution)/shard_map/ppermute | solution.py:399
  131.7 4.6 %collective-permute-start.15 = (f32[48,384]{1,0:T(8,128)S(1)}, f32[48,384]{1,0:T(8,128)S(1)}, u32[]{:S(2)}, u32[]{:S(2)}) collective-permute-start(f32[48,384]{1,0:T(8,128)S(1)} %get-tuple-element.30), channel_id=1, source_target_pairs={{0,1},{1,0},{2,3},{3,2},{4,5},{5,4},{6,7},{7,6},{8,9},{9,8},{10,11... | collective-permute-start | bytes 221192 | tf_op jit(solution)/shard_map/ppermute | solution.py:399
  132.0 4.3 %collective-permute-start.7 = (bf16[96,256]{1,0:T(8,128)(2,1)S(1)}, bf16[96,256]{1,0:T(8,128)(2,1)S(1)}, u32[]{:S(2)}, u32[]{:S(2)}) collective-permute-start(bf16[96,256]{1,0:T(8,128)(2,1)S(1)} %pad_maximum_fusion.2), channel_id=1, source_target_pairs={{0,1},{1,0},{2,3},{3,2},{4,5},{5,4},{6,7},{7,6},{8,9},{9,8},{10,11... | collective-permute-start | bytes 147464 | tf_op jit(solution)/shard_map/ppermute | solution.py:399
  136.3 3.4 %copy-start.4 = (bf16[16384,256]{1,0:T(8,128)(2,1)S(1)}, bf16[16384,256]{1,0:T(8,128)(2,1)}, u32[]{:S(2)}) copy-start(bf16[16384,256]{1,0:T(8,128)(2,1)} %protos_ref.7) | copy-start | bytes 25165828
  147.5 4.9 %collective-permute-start.10 = (f32[48,512]{1,0:T(8,128)S(1)}, f32[48,512]{1,0:T(8,128)S(1)}, u32[]{:S(2)}, u32[]{:S(2)}) collective-permute-start(f32[48,512]{1,0:T(8,128)S(1)} %get-tuple-element.22), channel_id=1, source_target_pairs={{0,3},{1,2},{2,1},{3,0},{4,7},{5,6},{6,5},{7,4},{8,11},{9,10},{10,... | collective-permute-start | bytes 294920 | tf_op jit(solution)/shard_map/ppermute | solution.py:399
  147.7 7.0 %collective-permute-start.9 = (f32[48,512]{1,0:T(8,128)S(1)}, f32[48,512]{1,0:T(8,128)S(1)}, u32[]{:S(2)}, u32[]{:S(2)}) collective-permute-start(f32[48,512]{1,0:T(8,128)S(1)} %get-tuple-element.21), channel_id=1, source_target_pairs={{0,2},{1,3},{2,0},{3,1},{4,6},{5,7},{6,4},{7,5},{8,10},{9,11},{10,... | collective-permute-start | bytes 294920 | tf_op jit(solution)/shard_map/ppermute | solution.py:399
  149.2 5.5 %collective-permute-start.8 = (f32[48,512]{1,0:T(8,128)S(1)}, f32[48,512]{1,0:T(8,128)S(1)}, u32[]{:S(2)}, u32[]{:S(2)}) collective-permute-start(f32[48,512]{1,0:T(8,128)S(1)} %get-tuple-element.20), channel_id=1, source_target_pairs={{0,1},{1,0},{2,3},{3,2},{4,5},{5,4},{6,7},{7,6},{8,9},{9,8},{10,11... | collective-permute-start | bytes 294920 | tf_op jit(solution)/shard_map/ppermute | solution.py:399

commit v5 on v0

v5 whole, which is shorter than its diff:
```python
import functools
import math

import jax
import jax.numpy as jnp
from jax import lax
from jax.experimental import pallas as pl
from jax.experimental.pallas import tpu as pltpu
from jax.sharding import PartitionSpec as P

ITERS = 3

student_temp = 0.1
teacher_temp = 0.07
norm_eps = 1e-06
teacher_rate = math.log2(math.e) / teacher_temp
student_rate = math.log2(math.e) / student_temp

MIB = 1024 * 1024
BOTH = ("batch", "proto")
TILE = 256


def scores(left_rows, right_rows):
    return lax.dot_general(
        left_rows, right_rows, (((1,), (1,)), ((), ())), preferred_element_type=jnp.float32
    )


def unit_rows(values):
    lengths = jnp.sqrt(jnp.sum(values * values, axis=1, keepdims=True) + norm_eps)
    return (values / lengths, lengths)


def gelu(values):
    return 0.5 * values * (1.0 + lax.erf(values * math.sqrt(0.5)))


def whole(memory_space=pltpu.VMEM):
    return pl.BlockSpec(memory_space=memory_space)


def part(index, size):
    return pl.ds(pl.multiple_of(index * size, size), size)


def lane_fold(values, combine):
    folded = values[:, :128]
    for start in range(128, values.shape[1], 128):
        folded = combine(folded, values[:, start : start + 128])
    return folded


def params(mib):
    return pltpu.CompilerParams(vmem_limit_bytes=mib * MIB)


def cost(flops, bytes_accessed, transcendentals=0):
    return pl.CostEstimate(
        flops=int(flops), bytes_accessed=int(bytes_accessed), transcendentals=int(transcendentals)
    )


def fetch(source, target, sems, first_row=0):
    count, rows = target.shape[:2]

    def chunk_copy(index):
        start = pl.multiple_of(first_row + index * rows, rows)
        return pltpu.make_async_copy(source.at[pl.ds(start, rows), :], target.at[index], sems.at[index])

    for index in range(count):
        chunk_copy(index).start()
    return lambda index: chunk_copy(index).wait()


def teacher_units_kernel(core_ref, emb_ref, unit_ref, half_ref):
    unit_ref[...] = unit_rows(emb_ref[...].astype(jnp.float32))[0].astype(jnp.bfloat16)
    half = half_ref.shape[0]
    half_ref[...] = unit_ref[part(core_ref[0], half), :]


def teacher_units(core, teacher_emb):
    rows, width = teacher_emb.shape
    return pl.pallas_call(
        teacher_units_kernel,
        in_specs=[whole(pltpu.SMEM), whole()],
        out_specs=[whole(), whole()],
        out_shape=[
            jax.ShapeDtypeStruct((rows, width), jnp.bfloat16),
            jax.ShapeDtypeStruct((rows // 2, width), jnp.bfloat16),
        ],
        compiler_params=params(4),
        cost_estimate=cost(4 * rows * width, 8 * rows * width),
        name="teacher_units",
    )(core, teacher_emb)


def wide_tops_kernel(unit_ref, protos_hbm, tops_ref, protos_ref, sems, top_ref):
    rows = unit_ref.shape[0]
    steps, block = protos_ref.shape[:2]
    arrived = fetch(protos_hbm, protos_ref, sems)
    top_ref[...] = jnp.full(top_ref.shape, -jnp.inf, jnp.float32)

    def step(index, carry):
        arrived(index)
        top = top_ref[:rows, :]
        for start in range(0, block, TILE):
            products = scores(unit_ref[...], protos_ref[index, start : start + TILE, :])
            top = jnp.maximum(top, lane_fold(products, jnp.maximum))
        top_ref[:rows, :] = top
        return carry

    lax.fori_loop(0, steps, step, 0)
    tops = jnp.max(jnp.transpose(top_ref[...]), axis=0, keepdims=True)
    tops_ref[...] = jnp.broadcast_to(tops[None], tops_ref.shape)


def wide_tops(unit, protos, copies, steps):
    rows, width = unit.shape
    count = protos.shape[0]
    return pl.pallas_call(
        wide_tops_kernel,
        in_specs=[whole(), whole(pl.ANY)],
        out_specs=whole(),
        out_shape=jax.ShapeDtypeStruct((copies, 1, 256), jnp.float32),
        scratch_shapes=[
            pltpu.VMEM((steps, count // steps, width), jnp.bfloat16),
            pltpu.SemaphoreType.DMA((steps,)),
            pltpu.VMEM((256, 128), jnp.float32),
        ],
        compiler_params=params(16),
        cost_estimate=cost(2 * rows * width * count, 2 * width * count),
        name="wide_tops",
    )(unit, protos)


def repel_kernel(group, index_ref, unit_ref, tops_ref, scale_ref, protos_hbm, order_ref, *rest):
    out_refs, (protos_ref, sems, scaled_ref, acc_ref, sum_ref, bias_ref) = rest[:-6], rest[-6:]
    rows, width = unit_ref.shape
    steps, block = protos_ref.shape[:2]
    arrived = fetch(protos_hbm, protos_ref, sems)
    first = index_ref[0] * group
    top = tops_ref[first]
    for other in range(1, group):
        top = jnp.maximum(top, tops_ref[first + other])
    bias_ref[...] = jnp.transpose(jnp.broadcast_to(top, (128, 256)))[:rows, :] * -teacher_rate
    acc_ref[...] = jnp.zeros(acc_ref.shape, jnp.float32)
    sum_ref[...] = jnp.zeros(sum_ref.shape, jnp.float32)

    def step(index, carry):
        arrived(index)
        bias = bias_ref[...]
        total = sum_ref[...]
        for start in range(0, block, TILE):
            products = scores(unit_ref[...], protos_ref[index, start : start + TILE, :])
            for lane in range(0, TILE, 128):
                columns = slice(start + lane, start + lane + 128)
                scaled = jnp.exp2(products[:, lane : lane + 128] * teacher_rate + bias)
                scaled = scaled * scale_ref[index, :, columns]
                total = total + scaled
                scaled_ref[:, columns] = scaled.astype(jnp.bfloat16)
        sum_ref[...] = total
        acc_ref[...] += jnp.dot(scaled_ref[...], protos_ref[index], preferred_element_type=jnp.float32)
        return carry

    lax.fori_loop(0, steps, step, 0)
    total = jnp.sum(sum_ref[...], axis=1, keepdims=True)
    sum_ref[...] = jnp.broadcast_to(total, sum_ref.shape)
    share = out_refs[0].shape[0]
    for flip, out_ref in enumerate(out_refs):
        span = part(index_ref[1] ^ flip, share)
        out_ref[:, :width] = acc_ref[span, :]
        out_ref[:, width:] = sum_ref[span, :]


def repel(index, unit, tops, scale, protos, order, proto_size):
    rows, width = unit.shape
    count = protos.shape[0]
    steps, _, block = scale.shape
    return pl.pallas_call(
        functools.partial(repel_kernel, proto_size),
        in_specs=[whole(pltpu.SMEM), whole(), whole(), whole(), whole(pl.ANY), whole(pl.ANY)],
        out_specs=[whole()] * proto_size,
        out_shape=[jax.ShapeDtypeStruct((rows // proto_size, width + 128), jnp.float32)] * proto_size,
        scratch_shapes=[
            pltpu.VMEM((steps, block, width), jnp.bfloat16),
            pltpu.SemaphoreType.DMA((steps,)),
            pltpu.VMEM((rows, block), jnp.bfloat16),
            pltpu.VMEM((rows, width), jnp.float32),
            pltpu.VMEM((rows, 128), jnp.float32),
            pltpu.VMEM((rows, 128), jnp.float32),
        ],
        compiler_params=params(16),
        cost_estimate=cost(4 * rows * width * count, 2 * width * count, rows * count),
        name="repel",
    )(index, unit, tops, scale, protos, order)


def attract_kernel(first_row, last, emb_ref, state_ref, protos_hbm, *rest):
    out_refs, scratch = rest[:-6], rest[-6:]
    protos_ref, sems, products_ref, acc_ref, sum_ref, top_ref = scratch
    width = emb_ref.shape[1]
    steps, block = protos_ref.shape[:2]
    arrived = fetch(protos_hbm, protos_ref, sems, first_row)
    old_top = state_ref[:, width + 128 :]
    top_ref[...] = old_top

    def first(index, carry):
        arrived(index)
        top = top_ref[...]
        for start in range(0, block, TILE):
            products = scores(emb_ref[...], protos_ref[index, start : start + TILE, :])
            products_ref[index, :, start : start + TILE] = products
            top = jnp.maximum(top, lane_fold(products, jnp.maximum))
        top_ref[...] = top
        return carry

    lax.fori_loop(0, steps, first, 0)
    top = jnp.broadcast_to(jnp.max(top_ref[...], axis=1, keepdims=True), top_ref.shape)
    fade = jnp.exp2((old_top - top) * student_rate)
    top_ref[...] = top
    sum_ref[...] = state_ref[:, width : width + 128] * fade
    acc_ref[...] = state_ref[:, :width] * jnp.tile(fade, (1, width // 128))

    def second(index, carry):
        top = top_ref[...]
        total = sum_ref[...]
        acc = acc_ref[...]
        for start in range(0, block, TILE):
            pieces = []
            for lane in range(start, start + TILE, 128):
                shifted = jnp.exp2((products_ref[index, :, lane : lane + 128] - top) * student_rate)
                total = total + shifted
                pieces.append(shifted.astype(jnp.bfloat16))
            acc = acc + jnp.dot(
                jnp.concatenate(pieces, axis=1),
                protos_ref[index, start : start + TILE, :],
                preferred_element_type=jnp.float32,
            )
        sum_ref[...] = total
        acc_ref[...] = acc
        return carry

    lax.fori_loop(0, steps, second, 0)
    if last:
        total = jnp.sum(sum_ref[...], axis=1, keepdims=True)
        sum_ref[...] = jnp.broadcast_to(total, sum_ref.shape)
    share = out_refs[0].shape[0]
    for slot, out_ref in enumerate(out_refs):
        rows = pl.ds(slot * share, share)
        out_ref[:, :width] = acc_ref[rows, :]
        out_ref[:, width : width + 128] = sum_ref[rows, :]
        out_ref[:, width + 128 :] = top_ref[rows, :]


def attract(emb, state, protos, first_row, count, steps, outputs):
    rows, width = emb.shape
    block = count // steps
    return pl.pallas_call(
        functools.partial(attract_kernel, first_row, outputs > 1),
        in_specs=[whole(), whole(), whole(pl.ANY)],
        out_specs=[whole()] * outputs,
        out_shape=[jax.ShapeDtypeStruct((rows // outputs, width + 256), jnp.float32)] * outputs,
        scratch_shapes=[
            pltpu.VMEM((steps, block, width), jnp.bfloat16),
            pltpu.SemaphoreType.DMA((steps,)),
            pltpu.VMEM((steps, rows, block), jnp.float32),
            pltpu.VMEM((rows, width), jnp.float32),
            pltpu.VMEM((rows, 128), jnp.float32),
            pltpu.VMEM((rows, 128), jnp.float32),
        ],
        compiler_params=params(24),
        cost_estimate=cost(4 * rows * width * count, 2 * width * count, rows * count),
        name="attract",
    )(emb, state, protos)


def local_lanes(core, values, half):
    return jnp.where(
        core == 0, values, jnp.concatenate([values[:, half:], values[:, :half]], axis=1)
    )


def weigh_chunk(protos, mine_ref, other_ref, bias_ref, weights_ref, slot):
    half = mine_ref.shape[0]
    rows = protos.shape[0]
    folds = [None] * (rows // 64)
    for side, units_ref in enumerate((mine_ref, other_ref)):
        for start in range(0, half, TILE):
            products = scores(protos, units_ref[start : start + TILE, :])
            for tile in range(rows // 64):
                for lane in range(0, TILE, 128):
                    column = side * half + start + lane
                    weights = jnp.exp2(
                        products[tile * 64 : tile * 64 + 64, lane : lane + 128] * teacher_rate
                        + bias_ref[:, column : column + 128]
                    )
                    weights_ref[slot, tile * 64 : tile * 64 + 64, column : column + 128] = weights
                    folds[tile] = weights if folds[tile] is None else folds[tile] + weights
    return folds


def sweep_kernel(
    chunk, protos_total, index_ref, protos_hbm, mine_ref, other_ref, base_ref, parts_ref, order_ref,
    copies_ref, protos_ref, sems, bias_ref, weights_ref, scale_ref, totals_ref,
):
    half = mine_ref.shape[0]
    crops_total = 2 * half
    steps = protos_ref.shape[0]
    core = index_ref[1]
    arrived = fetch(protos_hbm, protos_ref, sems, index_ref[0] * steps * chunk)
    inverse = None
    bias = base_ref[...]
    if parts_ref is not None:
        inverse = crops_total * jnp.sum(parts_ref[...], axis=0)
        bias = bias - jnp.log2(inverse)
        inverse = local_lanes(core, inverse, half)
    bias_ref[...] = jnp.broadcast_to(local_lanes(core, bias, half), bias_ref.shape)
    totals_ref[...] = jnp.zeros(totals_ref.shape, jnp.float32)

    def weigh(index, slot):
        arrived(index)
        folds = weigh_chunk(protos_ref[index], mine_ref, other_ref, bias_ref, weights_ref, slot)
        for tile, fold in enumerate(folds):
            sums = jnp.sum(fold, axis=1, keepdims=True)
            scale_ref[slot, tile * 64 : tile * 64 + 64, :] = jnp.broadcast_to(
                1.0 / (protos_total * sums), (64, 128)
            )

    def add_up(slot):
        for lane in range(0, crops_total, 128):
            total = totals_ref[:, lane : lane + 128]
            for row in range(0, chunk, 8):
                total = total + (
                    weights_ref[slot, row : row + 8, lane : lane + 128]
                    * scale_ref[slot, row : row + 8, :]
                )
            totals_ref[:, lane : lane + 128] = total

    weigh(0, 0)

    def sweep(index, carry):
        slot = lax.rem(index, 2)
        weigh(index, slot)
        add_up(1 - slot)
        return carry

    lax.fori_loop(1, steps, sweep, 0)
    add_up((steps - 1) % 2)
    totals = jnp.sum(totals_ref[...], axis=0, keepdims=True)
    if inverse is not None:
        totals = totals * inverse
    totals = local_lanes(core, totals, half)
    copies_ref[...] = jnp.broadcast_to(totals[None], copies_ref.shape)


def first_sweep_kernel(chunk, protos_total, index_ref, protos_hbm, mine_ref, other_ref, base_ref, order_ref, *rest):
    sweep_kernel(chunk, protos_total, index_ref, protos_hbm, mine_ref, other_ref, base_ref, None, order_ref, *rest)


def sweep(index, protos, mine, other, base, parts, order, copies, thin, protos_total):
    width = protos.shape[1]
    half = mine.shape[0]
    crops_total = 2 * half
    chunk = max(thin // 8, 128)
    steps = thin // chunk
    kernel = first_sweep_kernel if parts is None else sweep_kernel
    extra = [] if parts is None else [parts]
    return pl.pallas_call(
        functools.partial(kernel, chunk, protos_total),
        in_specs=[whole(pltpu.SMEM), whole(pl.ANY), whole(), whole(), whole()]
        + [whole()] * len(extra) + [whole(pl.ANY)],
        out_specs=whole(),
        out_shape=jax.ShapeDtypeStruct((copies, 1, crops_total), jnp.float32),
        scratch_shapes=[
            pltpu.VMEM((steps, chunk, width), jnp.bfloat16),
            pltpu.SemaphoreType.DMA((steps,)),
            pltpu.VMEM((64, crops_total), jnp.float32),
            pltpu.VMEM((2, chunk, crops_total), jnp.float32),
            pltpu.VMEM((2, chunk, 128), jnp.float32),
            pltpu.VMEM((8, crops_total), jnp.float32),
        ],
        compiler_params=params(16 if crops_total <= 2048 else 56),
        cost_estimate=cost(2 * thin * width * crops_total, 2 * width * (thin + crops_total), thin * crops_total),
        name="first_sweep" if parts is None else "next_sweep",
    )(index, protos, mine, other, base, *extra, order)


def last_scales_kernel(
    chunk, protos_total, index_ref, protos_hbm, mine_ref, other_ref, base_ref, parts_ref, order_ref,
    copies_ref, protos_ref, sems, bias_ref, scale_ref,
):
    half = mine_ref.shape[0]
    crops_total = 2 * half
    steps = protos_ref.shape[0]
    core = index_ref[1]
    arrived = fetch(protos_hbm, protos_ref, sems, index_ref[0] * steps * chunk)
    bias = base_ref[...] - jnp.log2(crops_total * jnp.sum(parts_ref[...], axis=0))
    bias_ref[...] = jnp.broadcast_to(local_lanes(core, bias, half), bias_ref.shape)

    def step(index, carry):
        arrived(index)
        folds = [None] * (chunk // 64)
        for side, units_ref in enumerate((mine_ref, other_ref)):
            for start in range(0, half, TILE):
                products = scores(protos_ref[index], units_ref[start : start + TILE, :])
                for tile in range(chunk // 64):
                    for lane in range(0, TILE, 128):
                        column = side * half + start + lane
                        weights = jnp.exp2(
                            products[tile * 64 : tile * 64 + 64, lane : lane + 128] * teacher_rate
                            + bias_ref[:, column : column + 128]
                        )
                        folds[tile] = weights if folds[tile] is None else folds[tile] + weights
        folded = jnp.concatenate(folds, axis=0)
        sums = jnp.sum(jnp.transpose(folded), axis=0, keepdims=True)
        scale_ref[:, part(index, chunk)] = 1.0 / (protos_total * sums)
        return carry

    lax.fori_loop(0, steps, step, 0)
    copies_ref[...] = jnp.broadcast_to(scale_ref[...][None], copies_ref.shape)


def last_scales(index, protos, mine, other, base, parts, order, copies, thin, protos_total):
    width = protos.shape[1]
    crops_total = 2 * mine.shape[0]
    chunk = max(thin // 8, 128)
    steps = thin // chunk
    return pl.pallas_call(
        functools.partial(last_scales_kernel, chunk, protos_total),
        in_specs=[whole(pltpu.SMEM), whole(pl.ANY), whole(), whole(), whole(), whole(), whole(pl.ANY)],
        out_specs=whole(),
        out_shape=jax.ShapeDtypeStruct((copies, 1, thin), jnp.float32),
        scratch_shapes=[
            pltpu.VMEM((steps, chunk, width), jnp.bfloat16),
            pltpu.SemaphoreType.DMA((steps,)),
            pltpu.VMEM((64, crops_total), jnp.float32),
            pltpu.VMEM((1, thin), jnp.float32),
        ],
        compiler_params=params(12 if crops_total <= 2048 else 56),
        cost_estimate=cost(2 * thin * width * crops_total, 2 * width * (thin + crops_total), thin * crops_total),
        name="last_scales",
    )(index, protos, mine, other, base, parts, order)


def student_front_kernel(
    index_ref, own_ref, x_ref, pair_ref, bias_ref, first_hbm, second_hbm, keep_ref, give_ref,
    first_ref, second_ref, sems, rows_ref,
):
    first_copy = pltpu.make_async_copy(first_hbm, first_ref, sems.at[0])
    second_copy = pltpu.make_async_copy(second_hbm, second_ref, sems.at[1])
    first_copy.start()
    second_copy.start()
    share = own_ref.shape[0]
    rows_ref[:share, :] = own_ref[...]
    rows_ref[share : 2 * share, :] = x_ref[...]
    rows_ref[2 * share :, :] = pair_ref[...]
    hidden = first_ref.shape[1]
    bias = bias_ref[:, part(index_ref[0], hidden)]
    first_copy.wait()
    h_first = gelu(
        jnp.dot(rows_ref[...], first_ref[...], preferred_element_type=jnp.float32) + bias
    ).astype(jnp.bfloat16)
    second_copy.wait()
    for start in range(0, second_ref.shape[1], 512):
        columns = slice(start, start + 512)
        product = jnp.dot(h_first, second_ref[:, columns], preferred_element_type=jnp.float32)
        keep_ref[:, columns] = product[: 2 * share]
        give_ref[:, columns] = product[2 * share :]


def student_front(index, own, x_rows, pair, bias, first, second):
    share = own.shape[0]
    hidden, units = second.shape
    return pl.pallas_call(
        student_front_kernel,
        in_specs=[whole(pltpu.SMEM), whole(), whole(), whole(), whole(), whole(pl.ANY), whole(pl.ANY)],
        out_specs=[whole(), whole()],
        out_shape=[jax.ShapeDtypeStruct((2 * share, units), jnp.float32)] * 2,
        scratch_shapes=[
            pltpu.VMEM(first.shape, jnp.bfloat16),
            pltpu.VMEM(second.shape, jnp.bfloat16),
            pltpu.SemaphoreType.DMA((2,)),
            pltpu.VMEM((4 * share, own.shape[1]), jnp.bfloat16),
        ],
        compiler_params=params(16),
        cost_estimate=cost(8 * share * hidden * (own.shape[1] + units), 2 * hidden * (own.shape[1] + units)),
        name="student_front",
    )(index, own, x_rows, pair, bias.reshape(1, -1), first, second)


def student_middle_kernel(
    index_ref, keep_ref, core_ref, x_ref, bias_ref, own_ref, partner_ref, pair_ref, last_bias_ref,
    unit_ref, emb_ref, lengths_ref, hidden_ref,
):
    share = x_ref.shape[0]
    block = own_ref.shape[0]
    sums = keep_ref[:share, :] + core_ref[:share, :] + x_ref[...]
    hidden_ref[...] = gelu(sums + bias_ref[...]).astype(jnp.bfloat16)
    index = index_ref[0]
    weights = ((0, own_ref[...]), (2, partner_ref[...]), (1, pair_ref[:block, :]), (3, pair_ref[block:, :]))
    bottleneck = jnp.broadcast_to(last_bias_ref[...], unit_ref.shape)
    for flip, weight in weights:
        bottleneck = bottleneck + jnp.dot(
            hidden_ref[:, part(index ^ flip, block)], weight, preferred_element_type=jnp.float32
        )
    unit, lengths = unit_rows(bottleneck)
    unit_ref[...] = unit
    emb_ref[...] = unit.astype(jnp.bfloat16)
    lengths_ref[...] = jnp.broadcast_to(lengths, lengths_ref.shape)


def student_middle(index, keep, core_rows, x_rows, bias, own, partner, pair, last_bias):
    share, units = x_rows.shape
    width = own.shape[1]
    return pl.pallas_call(
        student_middle_kernel,
        in_specs=[whole(pltpu.SMEM)] + [whole()] * 8,
        out_specs=[whole()] * 3,
        out_shape=[
            jax.ShapeDtypeStruct((share, width), jnp.float32),
            jax.ShapeDtypeStruct((share, width), jnp.bfloat16),
            jax.ShapeDtypeStruct((share, 128), jnp.float32),
        ],
        scratch_shapes=[pltpu.VMEM((share, units), jnp.bfloat16)],
        compiler_params=params(12),
        cost_estimate=cost(2 * share * units * width, 2 * units * width + 16 * share * units),
        name="student_middle",
    )(index, keep, core_rows, x_rows, bias.reshape(1, -1), own, partner, pair, last_bias.reshape(1, -1))


def finish_kernel(unit_ref, lengths_ref, *rest):
    out_ref, blocks = rest[-1], rest[:-1]
    attracts, repels = blocks[: len(blocks) // 2], blocks[len(blocks) // 2 :]
    width = unit_ref.shape[1]
    row_top = functools.reduce(jnp.maximum, [ref[:, width + 128 :] for ref in attracts])
    attract_sum = repel_sum = 0.0
    row_sum = column_sum = 0.0
    for ref in attracts:
        fade = jnp.exp2((ref[:, width + 128 :] - row_top) * student_rate)
        row_sum = row_sum + ref[:, width : width + 128] * fade
        attract_sum = attract_sum + ref[:, :width] * jnp.tile(fade, (1, width // 128))
    for ref in repels:
        column_sum = column_sum + ref[:, width:]
        repel_sum = repel_sum + ref[:, :width]
    emb_grad = (
        attract_sum / jnp.tile(row_sum, (1, width // 128))
        - repel_sum / jnp.tile(column_sum, (1, width // 128))
    ) / student_temp
    unit = unit_ref[...]
    along = jnp.sum(unit * emb_grad, axis=1, keepdims=True)
    out_ref[...] = (emb_grad - unit * along) / jnp.tile(lengths_ref[...], (1, width // 128))


def finish(unit, lengths, attracts, repels):
    return pl.pallas_call(
        finish_kernel,
        in_specs=[whole()] * (2 + len(attracts) + len(repels)),
        out_specs=whole(),
        out_shape=jax.ShapeDtypeStruct(unit.shape, jnp.float32),
        compiler_params=params(8),
        cost_estimate=cost(40 * unit.size, 40 * unit.size),
        name="finish",
    )(unit, lengths, *attracts, *repels)


def swap(values, axis, flip):
    return lax.ppermute(values, axis, [(i, i ^ flip) for i in range(lax.axis_size(axis))])


def gather_batch(values):
    step = lax.axis_size("batch") // 2
    while step:
        other = swap(values, "batch", step)
        upper = (lax.axis_index("batch") // step) % 2
        values = jnp.where(
            upper == 0, jnp.concatenate([values, other]), jnp.concatenate([other, values])
        )
        step //= 2
    return values


def bit_reversed(values, count):
    bits = count.bit_length() - 1
    split = values.reshape((2,) * bits + values.shape[1:])
    turned = jnp.transpose(split, tuple(reversed(range(bits))) + tuple(range(bits, split.ndim)))
    return turned.reshape(values.shape)


def send_blocks(blocks):
    return [blocks[0]] + [swap(block, "proto", flip) for flip, block in enumerate(blocks) if flip]


def all_to_all(copies, axes):
    return lax.all_to_all(copies, axes, 0, 0, tiled=True)


def body(crops, teacher_emb, w_first, b_first, w_second, b_second, w_third, b_third, protos):
    batch_index = lax.axis_index("batch")
    proto_index = lax.axis_index("proto")
    batch_size = lax.axis_size("batch")
    proto_size = lax.axis_size("proto")
    devices = batch_size * proto_size
    share_rows = crops.shape[0]
    group_rows = teacher_emb.shape[0]
    crops_total = group_rows * batch_size
    protos_total = protos.shape[0] * proto_size
    count, width = protos.shape
    thin = count // batch_size
    core = proto_index % 2
    proto_ref = proto_index.reshape(1)
    thin_ref = jnp.stack([batch_index, core])
    wide_ref = jnp.stack([batch_index, proto_index])

    own_unit, half = teacher_units(core.reshape(1), teacher_emb)
    crops_x = swap(crops, "proto", 2)
    mine = gather_batch(half)
    other = swap(mine, "proto", 1)
    all_tops = all_to_all(wide_tops(own_unit, protos, devices, 8), BOTH)
    tops = jnp.max(all_tops.reshape(batch_size, proto_size, 256)[:, :, :group_rows], axis=1)
    tops = bit_reversed(tops, batch_size).reshape(batch_size, 2, group_rows // 2)
    base = jnp.transpose(tops, (1, 0, 2)).reshape(1, crops_total) * -teacher_rate

    crops_pair = swap(jnp.concatenate([crops, crops_x]), "proto", 1)
    keep, give = student_front(proto_ref, crops, crops_x, crops_pair, b_first, w_first, w_second)
    core_rows = swap(give, "proto", 1)
    x_sent = keep[share_rows:] + core_rows[share_rows:]
    x_rows = swap(x_sent, "proto", 2)
    w_third_x = swap(w_third, "proto", 2)
    w_third_pair = swap(jnp.concatenate([w_third, w_third_x]), "proto", 1)
    unit, rounded, lengths = student_middle(
        proto_ref, keep, core_rows, x_rows, b_second, w_third, w_third_x, w_third_pair, b_third
    )
    emb_pair = jnp.concatenate([rounded, swap(rounded, "proto", 2)])
    student_emb = jnp.concatenate([emb_pair, swap(emb_pair, "proto", 1)])
    empty = jnp.concatenate(
        [jnp.zeros((group_rows, width + 128), jnp.float32), jnp.full((group_rows, 128), -1e30, jnp.float32)], axis=1
    )
    (state,) = attract(student_emb, empty, protos, 0, count // 2, 4, 1)
    slots = attract(student_emb, state, protos, count // 2, count // 2, 4, proto_size)
    attract_parts = send_blocks([slots[0], slots[2], slots[1], slots[3]])

    copies = sweep(thin_ref, protos, mine, other, base, None, x_sent, devices, thin, protos_total)
    for _ in range(ITERS - 2):
        copies = sweep(
            thin_ref, protos, mine, other, base, all_to_all(copies, BOTH), rounded, devices, thin, protos_total
        )
    scale_copies = last_scales(
        thin_ref, protos, mine, other, base, all_to_all(copies, BOTH), state, batch_size, thin, protos_total
    )
    all_scale = all_to_all(scale_copies, "batch")
    repels = repel(wide_ref, own_unit, all_tops, all_scale, protos, slots[0], proto_size)
    return finish(unit, lengths, attract_parts, send_blocks(repels))


def solution(mesh):
    in_specs = (
        P(("batch", "proto"), None),
        P("batch", None),
        P(None, "proto"),
        P(),
        P("proto", None),
        P(),
        P("proto", None),
        P(),
        P("proto", None),
    )
    out_specs = P(("batch", "proto"), None)
    return jax.shard_map(body, mesh=mesh, in_specs=in_specs, out_specs=out_specs, check_vma=False)
```

time: 442 us -> 144 us (0.33)
  waiting for transfers between devices: 268 us -> 21.6 us
  matrix products: 104 us -> 0 us
  Pallas kernels: 0 us -> 49.8 us
  starting transfers between devices: 0.87 us -> 35.7 us
  blocking collectives: 32 us -> 0 us
  local copies, waits for them, and re-layouts: 1.62 us -> 30.9 us
  other arithmetic: 20.9 us -> 4.52 us
  between operations: 13.5 us -> 0.36 us
    psum x4 -> x0, waiting for transfers between devices: 220 us -> none  [the longest x3 199 us: proto_scales(): row_total = lax.psum(local_rows, 'batch')]
    dot_general x10 -> x0, matrix products: 104 us -> none  [the longest x3 40.2 us: body(): jnp.dot(weights_e, proto_scale, precision=lax.Precision.HIGHEST)]
    pallas_call x0 -> x11, Pallas kernels: none -> 49.8 us  [the longest x2 14.4 us: sweep(): pl.pallas_call(functools.partial(kernel, chunk, protos_total), in_specs=[...]
    reduce_scatter x2 -> x0, waiting for transfers between devices: 48.3 us -> none  [the longest x1 28.3 us: body(): lax.psum_scatter(partial_value, 'proto', scatter_dimension=1, tiled=True)]
    unnamed x8 -> x48, local copies, waits for them, and re-layouts: 0.02 us -> 30.6 us
    ppermute x0 -> x18, starting transfers between devices: none -> 18.2 us  [swap(): lax.ppermute(values, axis, [(i, i ^ flip) for i in range(lax.axis_size(ax...]
    all_to_all x0 -> x4, starting transfers between devices: none -> 17.5 us  [all_to_all(): return lax.all_to_all(copies, axes, 0, 0, tiled=True)]
    psum x3 -> x0, blocking collectives: 17 us -> none  [body(): lax.psum(jnp.dot(weights_e, proto_scale, precision=lax.Precision.HIGHEST)...]
  transfers between devices with their start and end apart: 6 -> 22, of which waited for: 6 -> 8; matrix products, arithmetic and copies ran while one was open for 4% -> 3% of each run, Pallas kernels for 0% -> 30%
where the time goes in v5:
time: 144 us; the launch traced here: 143 us
  Pallas kernels  49.8 us (35%)
  starting transfers between devices  35.7 us (25%)
  local copies, waits for them, and re-layouts  30.9 us (21%)
  waiting for transfers between devices  21.6 us (15%)
  other arithmetic  4.52 us (3%)
    unnamed x48, local copies, waits for them, and re-layouts  30.6 us
    ppermute x18, starting transfers between devices, swap(): lax.ppermute(values, axis, [(i, i ^ flip) for i in range(lax.axis_size(ax...  18.2 us
    all_to_all x4, starting transfers between devices, all_to_all(): return lax.all_to_all(copies, axes, 0, 0, tiled=True)  17.5 us
    ppermute x18, waiting for transfers between devices, swap(): lax.ppermute(values, axis, [(i, i ^ flip) for i in range(lax.axis_size(ax...  16.4 us
    pallas_call x2, Pallas kernels, sweep(): pl.pallas_call(functools.partial(kernel, chunk, protos_total), in_specs=[...  14.4 us
    pallas_call x1, Pallas kernels, repel(): pl.pallas_call(functools.partial(repel_kernel, proto_size), in_specs=[who...  9.37 us
    pallas_call x2, Pallas kernels, attract(): pl.pallas_call(functools.partial(attract_kernel, first_row, outputs > 1),...  8.29 us
    pallas_call x1, Pallas kernels, last_scales(): pl.pallas_call(functools.partial(last_scales_kernel, chunk, protos_total)...  6.78 us
  transfers between devices with their start and end apart: 22, of which 8 were waited for; matrix products, arithmetic and copies ran while one was open for 3% of the time, Pallas kernels for 30%

profile of v5, /device:TPU:0, one launch (start us, length us, event | category | flops | bytes accessed | tf_op | source)
XLA Modules:
  0.0 142.8 jit_solution(12400622409905317263)
XLA Ops:
  0.0 2.9 %collective-permute-start = (bf16[48,1536]{1,0:T(8,128)(2,1)}, bf16[48,1536]{1,0:T(8,128)(2,1)S(1)}, u32[]{:S(2)}, u32[]{:S(2)}) collective-permute-start(bf16[48,1536]{1,0:T(8,128)(2,1)} %own_ref.2), channel_id=1, source_target_pairs={{0,2},{1,3},{2,0},{3,1},{4,6},{5,7},{6,4},{7,5},{8,10},{9,11},{10,... | collective-permute-start | bytes 442376 | tf_op jit(solution)/shard_map/ppermute | solution.py:568
  2.9 4.1 %collective-permute-done.x_ref = bf16[48,1536]{1,0:T(8,128)(2,1)S(1)} collective-permute-done((bf16[48,1536]{1,0:T(8,128)(2,1)}, bf16[48,1536]{1,0:T(8,128)(2,1)S(1)}, u32[]{:S(2)}, u32[]{:S(2)}) %collective-permute-start) | collective-permute-done | bytes 147488 | tf_op jit(solution)/shard_map/ppermute | solution.py:568
  7.0 1.0 pad_maximum_fusion.1
  8.0 0.1 collective-permute-start.1
  8.1 1.8 %collective-permute-start.4 = (bf16[512,256]{1,0:T(8,128)(2,1)}, bf16[512,256]{1,0:T(8,128)(2,1)S(1)}, u32[]{:S(2)}, u32[]{:S(2)}) collective-permute-start(bf16[512,256]{1,0:T(8,128)(2,1)} %own_ref.3), channel_id=1, source_target_pairs={{0,2},{1,3},{2,0},{3,1},{4,6},{5,7},{6,4},{7,5},{8,10},{9,11},{10,... | collective-permute-start | bytes 786440 | tf_op jit(solution)/shard_map/ppermute | solution.py:568
  9.9 0.9 copy-done.18
  10.8 0.8 teacher_units.1
  11.5 3.4 %copy-done = bf16[16384,256]{1,0:T(8,128)(2,1)S(1)} copy-done((bf16[16384,256]{1,0:T(8,128)(2,1)S(1)}, bf16[16384,256]{1,0:T(8,128)(2,1)}, u32[]{:S(2)}) %copy-start) | copy-done | bytes 8388632
  14.9 5.4 %wide_tops.1 = f32[32,1,256]{2,1,0:T(1,128)} custom-call(bf16[192,256]{1,0:T(8,128)(2,1)S(1)} %get-tuple-element.29.unit_ref, bf16[16384,256]{1,0:T(8,128)(2,1)S(1)} %copy-done), custom_call_target="tpu_custom_call" | custom-call | flops 1610612736 | bytes 8388608 | tf_op jit(solution)/shard_map/wide_tops/pallas_call | solution.py:121
  20.3 0.6 copy-done.16
  21.0 5.1 %all-to-all-start = ((f32[32,1,256]{2,1,0:T(1,128)}), f32[32,1,256]{2,1,0:T(1,128)}, u32[]{:S(2)}, u32[]{:S(2)}) async-start(f32[32,1,256]{2,1,0:T(1,128)} %wide_tops.1), calls=%async_computation | async-start | bytes 65536 | tf_op jit(solution)/shard_map/all_to_all | solution.py:595
  26.0 2.7 %collective-permute-start.11 = (bf16[96,256]{1,0:T(8,128)(2,1)}, bf16[96,256]{1,0:T(8,128)(2,1)}, u32[]{:S(2)}, u32[]{:S(2)}) collective-permute-start(bf16[96,256]{1,0:T(8,128)(2,1)} %get-tuple-element.30), channel_id=1, source_target_pairs={{0,16},{4,20},{8,24},{12,28},{16,0},{20,4},{24,8},{28,12},{1,17},{... | collective-permute-start | bytes 147464 | tf_op jit(solution)/shard_map/ppermute | solution.py:568
  28.7 0.6 pad_add_fusion.1.index_ref
  29.3 0.7 copy-done.14
  30.0 1.4 copy-done.8
  31.4 0.9 copy-done.13
  32.3 1.0 copy-done.15
  33.3 0.7 copy-done.19
  34.0 2.3 %student_front.1 = (f32[96,2048]{1,0:T(8,128)S(1)}, f32[96,2048]{1,0:T(8,128)}) custom-call(s32[1]{0:T(128)} %bitcast.index_ref, bf16[48,1536]{1,0:T(8,128)(2,1)S(1)} %copy-done.11, bf16[48,1536]{1,0:T(8,128)(2,1)S(1)} %copy-done.13, bf16[96,1536]{1,0:T(8,128)(2,1)S(1)} %copy-done.15, f32[1,2048]{1,0:T(1,128)S(1)} %bitcast.8, ...), custom_call_target="tpu_custom_call" | custom-call | flops 704643072 | bytes 3670016 | tf_op jit(solution)/shard_map/student_front/pallas_call | solution.py:475
  36.3 0.1 collective-permute-start.2
  36.4 0.9 maximum_select_fusion.2
  37.3 1.6 %collective-permute-start.12 = (bf16[192,256]{1,0:T(8,128)(2,1)S(1)}, bf16[192,256]{1,0:T(8,128)(2,1)S(1)}, u32[]{:S(2)}, u32[]{:S(2)}) collective-permute-start(bf16[192,256]{1,0:T(8,128)(2,1)S(1)} %maximum_select_fusion.2), channel_id=1, source_target_pairs={{0,8},{4,12},{8,0},{12,4},{16,24},{20,28},{24,16},{28,20},{1,9},{5... | collective-permute-start | bytes 294920 | tf_op jit(solution)/shard_map/ppermute | solution.py:568
  38.9 0.8 reduce
  39.8 2.8 %collective-permute-done.12 = bf16[192,256]{1,0:T(8,128)(2,1)S(1)} collective-permute-done((bf16[192,256]{1,0:T(8,128)(2,1)S(1)}, bf16[192,256]{1,0:T(8,128)(2,1)S(1)}, u32[]{:S(2)}, u32[]{:S(2)}) %collective-permute-start.12) | collective-permute-done | bytes 98336 | tf_op jit(solution)/shard_map/ppermute | solution.py:568
  42.6 0.1 maximum_select_fusion.1
  42.6 1.5 %collective-permute-start.13 = (bf16[384,256]{1,0:T(8,128)(2,1)S(1)}, bf16[384,256]{1,0:T(8,128)(2,1)S(1)}, u32[]{:S(2)}, u32[]{:S(2)}) collective-permute-start(bf16[384,256]{1,0:T(8,128)(2,1)S(1)} %maximum_select_fusion.1), channel_id=1, source_target_pairs={{0,4},{4,0},{8,12},{12,8},{16,20},{20,16},{24,28},{28,24},{1,5},{5... | collective-permute-start | bytes 589832 | tf_op jit(solution)/shard_map/ppermute | solution.py:568
  44.2 0.1 mul.17
  44.3 0.1 mul.19.base_ref
  44.4 0.8 pad_maximum_fusion
  45.2 4.0 %collective-permute-done.13 = bf16[384,256]{1,0:T(8,128)(2,1)S(1)} collective-permute-done((bf16[384,256]{1,0:T(8,128)(2,1)S(1)}, bf16[384,256]{1,0:T(8,128)(2,1)S(1)}, u32[]{:S(2)}, u32[]{:S(2)}) %collective-permute-start.13) | collective-permute-done | bytes 196640 | tf_op jit(solution)/shard_map/ppermute | solution.py:568
  49.2 0.2 maximum_select_fusion.mine_ref
  49.4 0.1 collective-permute-start.14
  49.5 1.5 %collective-permute-start.3 = (f32[48,2048]{1,0:T(8,128)S(1)}, f32[48,2048]{1,0:T(8,128)}, u32[]{:S(2)}, u32[]{:S(2)}) collective-permute-start(f32[48,2048]{1,0:T(8,128)S(1)} %slice_add_fusion.order_ref), channel_id=1, source_target_pairs={{0,2},{1,3},{2,0},{3,1},{4,6},{5,7},{6,4},{7,5},{8,10},{9,11},{10,... | collective-permute-start | bytes 1179656 | tf_op jit(solution)/shard_map/ppermute | solution.py:568
  51.1 0.1 collective-permute-done.14.other_ref
  51.2 3.4 %copy-done.1 = bf16[16384,256]{1,0:T(8,128)(2,1)S(1)} copy-done((bf16[16384,256]{1,0:T(8,128)(2,1)S(1)}, bf16[16384,256]{1,0:T(8,128)(2,1)}, u32[]{:S(2)}) %copy-start.1) | copy-done | bytes 8388632
  54.5 6.6 %first_sweep.1 = f32[32,1,1536]{2,1,0:T(1,128)S(1)} custom-call(s32[2]{0:T(128)S(1)} %copy-done.21, bf16[16384,256]{1,0:T(8,128)(2,1)S(1)} %copy-done.1, bf16[768,256]{1,0:T(8,128)(2,1)S(1)} %maximum_select_fusion.mine_ref, bf16[768,256]{1,0:T(8,128)(2,1)S(1)} %collective-permute-done.14.other_ref, f32[1,1536]{1,0:T(1,128)S(1)} %mul.19.base_ref, ...), custom_call_target="tpu_custom_call" | custom-call | flops 1610612736 | bytes 1835008 | tf_op jit(solution)/shard_map/first_sweep/pallas_call | solution.py:369
  61.2 0.7 copy-done.10
  61.9 3.8 %all-to-all-start.1 = ((f32[32,1,1536]{2,1,0:T(1,128)}), f32[32,1,1536]{2,1,0:T(1,128)}, u32[]{:S(2)}, u32[]{:S(2)}) async-start(f32[32,1,1536]{2,1,0:T(1,128)} %copy-done.10), calls=%async_computation.1 | async-start | bytes 393216 | tf_op jit(solution)/shard_map/all_to_all | solution.py:595
  65.7 0.1 pad_add_fusion.index_ref
  65.8 1.7 %student_middle.1 = (f32[48,256]{1,0:T(8,128)S(1)}, bf16[48,256]{1,0:T(8,128)(2,1)S(1)}, f32[48,128]{1,0:T(8,128)S(1)}) custom-call(s32[1]{0:T(128)} %bitcast.index_ref, f32[96,2048]{1,0:T(8,128)S(1)} %get-tuple-element.20.keep_ref, f32[96,2048]{1,0:T(8,128)S(1)} %collective-permute-done.2.core_ref, f32[48,2048]{1,0:T(8,128)} %collective-permute-done.3.x_ref, ...), custom_call_target="tpu_custom_call" | custom-call | flops 50331648 | bytes 2621440 | tf_op jit(solution)/shard_map/student_middle/pallas_call | solution.py:516
  67.6 1.8 %collective-permute-start.6 = (bf16[48,256]{1,0:T(8,128)(2,1)S(1)}, bf16[48,256]{1,0:T(8,128)(2,1)S(1)}, u32[]{:S(2)}, u32[]{:S(2)}) collective-permute-start(bf16[48,256]{1,0:T(8,128)(2,1)S(1)} %get-tuple-element.24.order_ref), channel_id=1, source_target_pairs={{0,2},{1,3},{2,0},{3,1},{4,6},{5,7},{6,4},{7,5},{8,10},{9,11},{10,... | collective-permute-start | bytes 73736 | tf_op jit(solution)/shard_map/ppermute | solution.py:568
  69.3 5.3 %all-to-all-done.1.parts_ref = f32[32,1,1536]{2,1,0:T(1,128)} async-done(((f32[32,1,1536]{2,1,0:T(1,128)}), f32[32,1,1536]{2,1,0:T(1,128)}, u32[]{:S(2)}, u32[]{:S(2)}) %all-to-all-start.1) | async-done | bytes 196640 | tf_op jit(solution)/shard_map/all_to_all | solution.py:595
  74.6 3.4 %copy-done.2 = bf16[16384,256]{1,0:T(8,128)(2,1)S(1)} copy-done((bf16[16384,256]{1,0:T(8,128)(2,1)S(1)}, bf16[16384,256]{1,0:T(8,128)(2,1)}, u32[]{:S(2)}) %copy-start.2) | copy-done | bytes 8388632
  78.0 7.8 %next_sweep.1 = f32[32,1,1536]{2,1,0:T(1,128)} custom-call(s32[2]{0:T(128)S(1)} %copy-done.21, bf16[16384,256]{1,0:T(8,128)(2,1)S(1)} %copy-done.2, bf16[768,256]{1,0:T(8,128)(2,1)S(1)} %maximum_select_fusion.mine_ref, bf16[768,256]{1,0:T(8,128)(2,1)S(1)} %collective-permute-done.14.other_ref, f32[1,1536]{1,0:T(1,128)S(1)} %mul.19.base_ref, ...), custom_call_target="tpu_custom_call" | custom-call | flops 1610612736 | bytes 1835008 | tf_op jit(solution)/shard_map/next_sweep/pallas_call | solution.py:369
  85.8 2.7 %all-to-all-start.2 = ((f32[32,1,1536]{2,1,0:T(1,128)}), f32[32,1,1536]{2,1,0:T(1,128)S(1)}, u32[]{:S(2)}, u32[]{:S(2)}) async-start(f32[32,1,1536]{2,1,0:T(1,128)} %next_sweep.1), calls=%async_computation.2 | async-start | bytes 393216 | tf_op jit(solution)/shard_map/all_to_all | solution.py:595
  88.5 0.3 collective-permute-start.7
  88.9 1.0 collective-permute-done.7
  89.9 3.4 %copy-done.3 = bf16[16384,256]{1,0:T(8,128)(2,1)S(1)} copy-done((bf16[16384,256]{1,0:T(8,128)(2,1)S(1)}, bf16[16384,256]{1,0:T(8,128)(2,1)}, u32[]{:S(2)}) %copy-start.3) | copy-done | bytes 8388632
  93.3 4.1 %attract.2.state_ref.order_ref = f32[192,512]{1,0:T(8,128)S(1)} custom-call(bf16[192,256]{1,0:T(8,128)(2,1)S(1)} %constant_dynamic-update-slice_fusion.emb_ref, f32[192,512]{1,0:T(8,128)S(1)} %concatenate.41.state_ref, bf16[16384,256]{1,0:T(8,128)(2,1)S(1)} %copy-done.3), custom_call_target="tpu_custom_call" | custom-call | flops 1610612736 | bytes 4194304 | tf_op jit(solution)/shard_map/attract/pallas_call | solution.py:259
  97.4 3.4 %copy-done.4 = bf16[16384,256]{1,0:T(8,128)(2,1)S(1)} copy-done((bf16[16384,256]{1,0:T(8,128)(2,1)S(1)}, bf16[16384,256]{1,0:T(8,128)(2,1)}, u32[]{:S(2)}) %copy-start.4) | copy-done | bytes 8388632
  100.8 6.8 %last_scales.1 = f32[8,1,2048]{2,1,0:T(1,128)} custom-call(s32[2]{0:T(128)S(1)} %copy-done.21, bf16[16384,256]{1,0:T(8,128)(2,1)S(1)} %copy-done.4, bf16[768,256]{1,0:T(8,128)(2,1)S(1)} %maximum_select_fusion.mine_ref, bf16[768,256]{1,0:T(8,128)(2,1)S(1)} %collective-permute-done.14.other_ref, f32[1,1536]{1,0:T(1,128)S(1)} %mul.19.base_ref, ...), custom_call_target="tpu_custom_call" | custom-call | flops 1610612736 | bytes 1835008 | tf_op jit(solution)/shard_map/last_scales/pallas_call | solution.py:429
  107.6 5.8 %all-to-all-start.3 = ((f32[8,1,2048]{2,1,0:T(1,128)}), f32[8,1,2048]{2,1,0:T(1,128)S(1)}, u32[]{:S(2)}, u32[]{:S(2)}) async-start(f32[8,1,2048]{2,1,0:T(1,128)} %last_scales.1), calls=%async_computation.3 | async-start | bytes 131072 | tf_op jit(solution)/shard_map/all_to_all | solution.py:595
  113.4 3.4 %copy-done.5 = bf16[16384,256]{1,0:T(8,128)(2,1)S(1)} copy-done((bf16[16384,256]{1,0:T(8,128)(2,1)S(1)}, bf16[16384,256]{1,0:T(8,128)(2,1)}, u32[]{:S(2)}) %copy-start.5) | copy-done | bytes 8388632
  116.8 4.2 %attract.3 = (f32[48,512]{1,0:T(8,128)S(1)}, f32[48,512]{1,0:T(8,128)S(1)}, f32[48,512]{1,0:T(8,128)S(1)}, f32[48,512]{1,0:T(8,128)S(1)}) custom-call(bf16[192,256]{1,0:T(8,128)(2,1)S(1)} %constant_dynamic-update-slice_fusion.emb_ref, f32[192,512]{1,0:T(8,128)S(1)} %attract.2.state_ref.order_ref, bf16[16384,256]{1,0:T(8,128)(2,1)S(1)} %copy-done.5), custom_call_target="tpu_custom_call" | custom-call | flops 1610612736 | bytes 4194304 | tf_op jit(solution)/shard_map/attract/pallas_call | solution.py:259
  121.0 0.1 collective-permute-start.8
  121.1 1.5 %collective-permute-start.9 = (f32[48,512]{1,0:T(8,128)S(1)}, f32[48,512]{1,0:T(8,128)S(1)}, u32[]{:S(2)}, u32[]{:S(2)}) collective-permute-start(f32[48,512]{1,0:T(8,128)S(1)} %get-tuple-element.27), channel_id=1, source_target_pairs={{0,2},{1,3},{2,0},{3,1},{4,6},{5,7},{6,4},{7,5},{8,10},{9,11},{10,... | collective-permute-start | bytes 294920 | tf_op jit(solution)/shard_map/ppermute | solution.py:568
  122.6 0.3 collective-permute-start.10
  122.9 3.4 %copy-done.6 = bf16[16384,256]{1,0:T(8,128)(2,1)S(1)} copy-done((bf16[16384,256]{1,0:T(8,128)(2,1)S(1)}, bf16[16384,256]{1,0:T(8,128)(2,1)}, u32[]{:S(2)}) %copy-start.6) | copy-done | bytes 8388632
  126.3 9.4 %repel.1 = (f32[48,384]{1,0:T(8,128)S(1)}, f32[48,384]{1,0:T(8,128)S(1)}, f32[48,384]{1,0:T(8,128)S(1)}, f32[48,384]{1,0:T(8,128)S(1)}) custom-call(s32[2]{0:T(128)S(1)} %pad_add_fusion.index_ref, bf16[192,256]{1,0:T(8,128)(2,1)S(1)} %copy-done.17, f32[32,1,256]{2,1,0:T(1,128)} %all-to-all-done.tops_ref, f32[8,1,2048]{2,1,0:T(1,128)S(1)} %all-to-all-done.3.scale_ref, ...), custom_call_target="tpu_custom_call" | custom-call | flops 3221225472 | bytes 8388608 | tf_op jit(solution)/shard_map/repel/pallas_call | solution.py:180
  135.7 0.4 collective-permute-start.15
  136.1 1.5 %collective-permute-start.16 = (f32[48,384]{1,0:T(8,128)S(1)}, f32[48,384]{1,0:T(8,128)S(1)}, u32[]{:S(2)}, u32[]{:S(2)}) collective-permute-start(f32[48,384]{1,0:T(8,128)S(1)} %get-tuple-element.33), channel_id=1, source_target_pairs={{0,2},{1,3},{2,0},{3,1},{4,6},{5,7},{6,4},{7,5},{8,10},{9,11},{10,... | collective-permute-start | bytes 221192 | tf_op jit(solution)/shard_map/ppermute | solution.py:568
  137.6 2.8 %collective-permute-done.16.rest_6_ = f32[48,384]{1,0:T(8,128)S(1)} collective-permute-done((f32[48,384]{1,0:T(8,128)S(1)}, f32[48,384]{1,0:T(8,128)S(1)}, u32[]{:S(2)}, u32[]{:S(2)}) %collective-permute-start.16) | collective-permute-done | bytes 73760 | tf_op jit(solution)/shard_map/ppermute | solution.py:568
  140.4 1.6 %collective-permute-done.17.rest_7_ = f32[48,384]{1,0:T(8,128)S(1)} collective-permute-done((f32[48,384]{1,0:T(8,128)S(1)}, f32[48,384]{1,0:T(8,128)S(1)}, u32[]{:S(2)}, u32[]{:S(2)}) %collective-permute-start.17) | collective-permute-done | bytes 73760 | tf_op jit(solution)/shard_map/ppermute | solution.py:568
  142.1 0.8 finish.1
  (61 shorter events, 0.3 us)
Async XLA Ops:
  0.0 7.0 %collective-permute-start = (bf16[48,1536]{1,0:T(8,128)(2,1)}, bf16[48,1536]{1,0:T(8,128)(2,1)S(1)}, u32[]{:S(2)}, u32[]{:S(2)}) collective-permute-start(bf16[48,1536]{1,0:T(8,128)(2,1)} %own_ref.2), channel_id=1, source_target_pairs={{0,2},{1,3},{2,0},{3,1},{4,6},{5,7},{6,4},{7,5},{8,10},{9,11},{10,... | collective-permute-start | bytes 442376 | tf_op jit(solution)/shard_map/ppermute | solution.py:568
  7.0 1.0 copy-start.12
  8.0 21.3 %collective-permute-start.1 = (bf16[96,1536]{1,0:T(8,128)(2,1)S(1)}, bf16[96,1536]{1,0:T(8,128)(2,1)S(1)}, u32[]{:S(2)}, u32[]{:S(2)}) collective-permute-start(bf16[96,1536]{1,0:T(8,128)(2,1)S(1)} %pad_maximum_fusion.1), channel_id=1, source_target_pairs={{0,1},{1,0},{2,3},{3,2},{4,5},{5,4},{6,7},{7,6},{8,9},{9,8},{10,11... | collective-permute-start | bytes 884744 | tf_op jit(solution)/shard_map/ppermute | solution.py:568
  8.1 36.3 %collective-permute-start.4 = (bf16[512,256]{1,0:T(8,128)(2,1)}, bf16[512,256]{1,0:T(8,128)(2,1)S(1)}, u32[]{:S(2)}, u32[]{:S(2)}) collective-permute-start(bf16[512,256]{1,0:T(8,128)(2,1)} %own_ref.3), channel_id=1, source_target_pairs={{0,2},{1,3},{2,0},{3,1},{4,6},{5,7},{6,4},{7,5},{8,10},{9,11},{10,... | collective-permute-start | bytes 786440 | tf_op jit(solution)/shard_map/ppermute | solution.py:568
  9.9 0.9 copy-start.18
  11.5 3.4 %copy-start = (bf16[16384,256]{1,0:T(8,128)(2,1)S(1)}, bf16[16384,256]{1,0:T(8,128)(2,1)}, u32[]{:S(2)}) copy-start(bf16[16384,256]{1,0:T(8,128)(2,1)} %protos_hbm.13) | copy-start | bytes 25165828
  14.9 15.1 %copy-start.7 = (bf16[512,2048]{1,0:T(8,128)(2,1)S(1)}, bf16[512,2048]{1,0:T(8,128)(2,1)}, u32[]{:S(2)}) copy-start(bf16[512,2048]{1,0:T(8,128)(2,1)} %second_hbm.1) | copy-start | bytes 6291460
  14.9 15.1 %copy-start.11 = (bf16[48,1536]{1,0:T(8,128)(2,1)S(1)}, bf16[48,1536]{1,0:T(8,128)(2,1)}, u32[]{:S(2)}) copy-start(bf16[48,1536]{1,0:T(8,128)(2,1)} %own_ref.2) | copy-start | bytes 442372
  20.3 0.6 copy-start.16
  21.0 17.9 %all-to-all-start = ((f32[32,1,256]{2,1,0:T(1,128)}), f32[32,1,256]{2,1,0:T(1,128)}, u32[]{:S(2)}, u32[]{:S(2)}) async-start(f32[32,1,256]{2,1,0:T(1,128)} %wide_tops.1), calls=%async_computation | async-start | bytes 65536 | tf_op jit(solution)/shard_map/all_to_all | solution.py:595
  26.0 10.4 %collective-permute-start.11 = (bf16[96,256]{1,0:T(8,128)(2,1)}, bf16[96,256]{1,0:T(8,128)(2,1)}, u32[]{:S(2)}, u32[]{:S(2)}) collective-permute-start(bf16[96,256]{1,0:T(8,128)(2,1)} %get-tuple-element.30), channel_id=1, source_target_pairs={{0,16},{4,20},{8,24},{12,28},{16,0},{20,4},{24,8},{28,12},{1,17},{... | collective-permute-start | bytes 147464 | tf_op jit(solution)/shard_map/ppermute | solution.py:568
  29.3 0.7 copy-start.14
  30.0 1.4 copy-start.8
  31.4 0.9 copy-start.13
  32.3 1.0 copy-start.15
  33.3 0.7 copy-start.19
  34.0 10.4 %copy-start.9 = (bf16[512,256]{1,0:T(8,128)(2,1)S(1)}, bf16[512,256]{1,0:T(8,128)(2,1)}, u32[]{:S(2)}) copy-start(bf16[512,256]{1,0:T(8,128)(2,1)} %own_ref.3) | copy-start | bytes 786436
  36.3 14.9 %copy-start.21 = (s32[2]{0:T(128)S(1)}, s32[2]{0:T(128)}, u32[]{:S(2)}) copy-start(s32[2]{0:T(128)} %pad_add_fusion.1.index_ref) | copy-start | bytes 28
  36.3 13.1 %collective-permute-start.2 = (f32[96,2048]{1,0:T(8,128)}, f32[96,2048]{1,0:T(8,128)S(1)}, u32[]{:S(2)}, u32[]{:S(2)}) collective-permute-start(f32[96,2048]{1,0:T(8,128)} %get-tuple-element.21), channel_id=1, source_target_pairs={{0,1},{1,0},{2,3},{3,2},{4,5},{5,4},{6,7},{7,6},{8,9},{9,8},{10,11... | collective-permute-start | bytes 2359304 | tf_op jit(solution)/shard_map/ppermute | solution.py:568
  37.3 5.3 %collective-permute-start.12 = (bf16[192,256]{1,0:T(8,128)(2,1)S(1)}, bf16[192,256]{1,0:T(8,128)(2,1)S(1)}, u32[]{:S(2)}, u32[]{:S(2)}) collective-permute-start(bf16[192,256]{1,0:T(8,128)(2,1)S(1)} %maximum_select_fusion.2), channel_id=1, source_target_pairs={{0,8},{4,12},{8,0},{12,4},{16,24},{20,28},{24,16},{28,20},{1,9},{5... | collective-permute-start | bytes 294920 | tf_op jit(solution)/shard_map/ppermute | solution.py:568
  42.6 6.6 %collective-permute-start.13 = (bf16[384,256]{1,0:T(8,128)(2,1)S(1)}, bf16[384,256]{1,0:T(8,128)(2,1)S(1)}, u32[]{:S(2)}, u32[]{:S(2)}) collective-permute-start(bf16[384,256]{1,0:T(8,128)(2,1)S(1)} %maximum_select_fusion.1), channel_id=1, source_target_pairs={{0,4},{4,0},{8,12},{12,8},{16,20},{20,16},{24,28},{28,24},{1,5},{5... | collective-permute-start | bytes 589832 | tf_op jit(solution)/shard_map/ppermute | solution.py:568
  45.2 20.6 %collective-permute-start.5 = (bf16[1024,256]{1,0:T(8,128)(2,1)}, bf16[1024,256]{1,0:T(8,128)(2,1)}, u32[]{:S(2)}, u32[]{:S(2)}) collective-permute-start(bf16[1024,256]{1,0:T(8,128)(2,1)} %pad_maximum_fusion), channel_id=1, source_target_pairs={{0,1},{1,0},{2,3},{3,2},{4,5},{5,4},{6,7},{7,6},{8,9},{9,8},{10,11... | collective-permute-start | bytes 1572872 | tf_op jit(solution)/shard_map/ppermute | solution.py:568
  49.4 1.8 %collective-permute-start.14 = (bf16[768,256]{1,0:T(8,128)(2,1)S(1)}, bf16[768,256]{1,0:T(8,128)(2,1)S(1)}, u32[]{:S(2)}, u32[]{:S(2)}) collective-permute-start(bf16[768,256]{1,0:T(8,128)(2,1)S(1)} %maximum_select_fusion.mine_ref), channel_id=1, source_target_pairs={{0,1},{1,0},{2,3},{3,2},{4,5},{5,4},{6,7},{7,6},{8,9},{9,8},{10,11... | collective-permute-start | bytes 1179656 | tf_op jit(solution)/shard_map/ppermute | solution.py:568
  49.5 16.4 %copy-start.20 = (f32[2048]{0:T(1024)S(1)}, f32[2048]{0:T(1024)}, u32[]{:S(2)}) copy-start(f32[2048]{0:T(1024)} %param.14) | copy-start | bytes 24580
  49.5 16.4 %copy-start.22 = (f32[256]{0:T(256)S(1)}, f32[256]{0:T(256)}, u32[]{:S(2)}) copy-start(f32[256]{0:T(256)} %param.16) | copy-start | bytes 3076
  49.5 16.3 %collective-permute-start.3 = (f32[48,2048]{1,0:T(8,128)S(1)}, f32[48,2048]{1,0:T(8,128)}, u32[]{:S(2)}, u32[]{:S(2)}) collective-permute-start(f32[48,2048]{1,0:T(8,128)S(1)} %slice_add_fusion.order_ref), channel_id=1, source_target_pairs={{0,2},{1,3},{2,0},{3,1},{4,6},{5,7},{6,4},{7,5},{8,10},{9,11},{10,... | collective-permute-start | bytes 1179656 | tf_op jit(solution)/shard_map/ppermute | solution.py:568
  51.2 3.4 %copy-start.1 = (bf16[16384,256]{1,0:T(8,128)(2,1)S(1)}, bf16[16384,256]{1,0:T(8,128)(2,1)}, u32[]{:S(2)}) copy-start(bf16[16384,256]{1,0:T(8,128)(2,1)} %protos_hbm.13) | copy-start | bytes 25165828
  61.2 0.7 copy-start.10
  61.9 12.7 %all-to-all-start.1 = ((f32[32,1,1536]{2,1,0:T(1,128)}), f32[32,1,1536]{2,1,0:T(1,128)}, u32[]{:S(2)}, u32[]{:S(2)}) async-start(f32[32,1,1536]{2,1,0:T(1,128)} %copy-done.10), calls=%async_computation.1 | async-start | bytes 393216 | tf_op jit(solution)/shard_map/all_to_all | solution.py:595
  67.6 21.0 %collective-permute-start.6 = (bf16[48,256]{1,0:T(8,128)(2,1)S(1)}, bf16[48,256]{1,0:T(8,128)(2,1)S(1)}, u32[]{:S(2)}, u32[]{:S(2)}) collective-permute-start(bf16[48,256]{1,0:T(8,128)(2,1)S(1)} %get-tuple-element.24.order_ref), channel_id=1, source_target_pairs={{0,2},{1,3},{2,0},{3,1},{4,6},{5,7},{6,4},{7,5},{8,10},{9,11},{10,... | collective-permute-start | bytes 73736 | tf_op jit(solution)/shard_map/ppermute | solution.py:568
  74.6 3.4 %copy-start.2 = (bf16[16384,256]{1,0:T(8,128)(2,1)S(1)}, bf16[16384,256]{1,0:T(8,128)(2,1)}, u32[]{:S(2)}) copy-start(bf16[16384,256]{1,0:T(8,128)(2,1)} %protos_hbm.13) | copy-start | bytes 25165828
  85.8 11.6 %all-to-all-start.2 = ((f32[32,1,1536]{2,1,0:T(1,128)}), f32[32,1,1536]{2,1,0:T(1,128)S(1)}, u32[]{:S(2)}, u32[]{:S(2)}) async-start(f32[32,1,1536]{2,1,0:T(1,128)} %next_sweep.1), calls=%async_computation.2 | async-start | bytes 393216 | tf_op jit(solution)/shard_map/all_to_all | solution.py:595
  88.5 1.3 collective-permute-start.7
  89.9 3.4 %copy-start.3 = (bf16[16384,256]{1,0:T(8,128)(2,1)S(1)}, bf16[16384,256]{1,0:T(8,128)(2,1)}, u32[]{:S(2)}) copy-start(bf16[16384,256]{1,0:T(8,128)(2,1)} %protos_hbm.13) | copy-start | bytes 25165828
  97.4 3.4 %copy-start.4 = (bf16[16384,256]{1,0:T(8,128)(2,1)S(1)}, bf16[16384,256]{1,0:T(8,128)(2,1)}, u32[]{:S(2)}) copy-start(bf16[16384,256]{1,0:T(8,128)(2,1)} %protos_hbm.13) | copy-start | bytes 25165828
  107.6 15.4 %all-to-all-start.3 = ((f32[8,1,2048]{2,1,0:T(1,128)}), f32[8,1,2048]{2,1,0:T(1,128)S(1)}, u32[]{:S(2)}, u32[]{:S(2)}) async-start(f32[8,1,2048]{2,1,0:T(1,128)} %last_scales.1), calls=%async_computation.3 | async-start | bytes 131072 | tf_op jit(solution)/shard_map/all_to_all | solution.py:595
  113.4 3.4 %copy-start.5 = (bf16[16384,256]{1,0:T(8,128)(2,1)S(1)}, bf16[16384,256]{1,0:T(8,128)(2,1)}, u32[]{:S(2)}) copy-start(bf16[16384,256]{1,0:T(8,128)(2,1)} %protos_hbm.13) | copy-start | bytes 25165828
  116.8 6.1 %copy-start.17 = (bf16[192,256]{1,0:T(8,128)(2,1)S(1)}, bf16[192,256]{1,0:T(8,128)(2,1)}, u32[]{:S(2)}) copy-start(bf16[192,256]{1,0:T(8,128)(2,1)} %copy-done.16) | copy-start | bytes 294916
  121.0 16.6 %collective-permute-start.8 = (f32[48,512]{1,0:T(8,128)S(1)}, f32[48,512]{1,0:T(8,128)S(1)}, u32[]{:S(2)}, u32[]{:S(2)}) collective-permute-start(f32[48,512]{1,0:T(8,128)S(1)} %get-tuple-element.26), channel_id=1, source_target_pairs={{0,1},{1,0},{2,3},{3,2},{4,5},{5,4},{6,7},{7,6},{8,9},{9,8},{10,11... | collective-permute-start | bytes 294920 | tf_op jit(solution)/shard_map/ppermute | solution.py:568
  121.1 16.6 %collective-permute-start.9 = (f32[48,512]{1,0:T(8,128)S(1)}, f32[48,512]{1,0:T(8,128)S(1)}, u32[]{:S(2)}, u32[]{:S(2)}) collective-permute-start(f32[48,512]{1,0:T(8,128)S(1)} %get-tuple-element.27), channel_id=1, source_target_pairs={{0,2},{1,3},{2,0},{3,1},{4,6},{5,7},{6,4},{7,5},{8,10},{9,11},{10,... | collective-permute-start | bytes 294920 | tf_op jit(solution)/shard_map/ppermute | solution.py:568
  122.6 15.0 %collective-permute-start.10 = (f32[48,512]{1,0:T(8,128)S(1)}, f32[48,512]{1,0:T(8,128)S(1)}, u32[]{:S(2)}, u32[]{:S(2)}) collective-permute-start(f32[48,512]{1,0:T(8,128)S(1)} %get-tuple-element.28), channel_id=1, source_target_pairs={{0,3},{1,2},{2,1},{3,0},{4,7},{5,6},{6,5},{7,4},{8,11},{9,10},{10,... | collective-permute-start | bytes 294920 | tf_op jit(solution)/shard_map/ppermute | solution.py:568
  122.9 3.4 %copy-start.6 = (bf16[16384,256]{1,0:T(8,128)(2,1)S(1)}, bf16[16384,256]{1,0:T(8,128)(2,1)}, u32[]{:S(2)}) copy-start(bf16[16384,256]{1,0:T(8,128)(2,1)} %protos_hbm.13) | copy-start | bytes 25165828
  135.7 2.0 %collective-permute-start.15 = (f32[48,384]{1,0:T(8,128)S(1)}, f32[48,384]{1,0:T(8,128)S(1)}, u32[]{:S(2)}, u32[]{:S(2)}) collective-permute-start(f32[48,384]{1,0:T(8,128)S(1)} %get-tuple-element.32), channel_id=1, source_target_pairs={{0,1},{1,0},{2,3},{3,2},{4,5},{5,4},{6,7},{7,6},{8,9},{9,8},{10,11... | collective-permute-start | bytes 221192 | tf_op jit(solution)/shard_map/ppermute | solution.py:568
  136.1 4.4 %collective-permute-start.16 = (f32[48,384]{1,0:T(8,128)S(1)}, f32[48,384]{1,0:T(8,128)S(1)}, u32[]{:S(2)}, u32[]{:S(2)}) collective-permute-start(f32[48,384]{1,0:T(8,128)S(1)} %get-tuple-element.33), channel_id=1, source_target_pairs={{0,2},{1,3},{2,0},{3,1},{4,6},{5,7},{6,4},{7,5},{8,10},{9,11},{10,... | collective-permute-start | bytes 221192 | tf_op jit(solution)/shard_map/ppermute | solution.py:568
  137.6 4.5 %collective-permute-start.17 = (f32[48,384]{1,0:T(8,128)S(1)}, f32[48,384]{1,0:T(8,128)S(1)}, u32[]{:S(2)}, u32[]{:S(2)}) collective-permute-start(f32[48,384]{1,0:T(8,128)S(1)} %get-tuple-element.34), channel_id=1, source_target_pairs={{0,3},{1,2},{2,1},{3,0},{4,7},{5,6},{6,5},{7,4},{8,11},{9,10},{10,... | collective-permute-start | bytes 221192 | tf_op jit(solution)/shard_map/ppermute | solution.py:568

commit v6 on v5

v6 whole, which is shorter than its diff:
```python
import functools
import math

import jax
import jax.numpy as jnp
from jax import lax
from jax.experimental import pallas as pl
from jax.experimental.pallas import tpu as pltpu
from jax.sharding import PartitionSpec as P

ITERS = 3

student_temp = 0.1
teacher_temp = 0.07
norm_eps = 1e-06
teacher_rate = math.log2(math.e) / teacher_temp
student_rate = math.log2(math.e) / student_temp

MIB = 1024 * 1024
BOTH = ("batch", "proto")
TILE = 256


def scores(left_rows, right_rows):
    return lax.dot_general(
        left_rows, right_rows, (((1,), (1,)), ((), ())), preferred_element_type=jnp.float32
    )


def unit_rows(values):
    lengths = jnp.sqrt(jnp.sum(values * values, axis=1, keepdims=True) + norm_eps)
    return (values / lengths, lengths)


def gelu(values):
    return 0.5 * values * (1.0 + lax.erf(values * math.sqrt(0.5)))


def whole(memory_space=pltpu.VMEM):
    return pl.BlockSpec(memory_space=memory_space)


def part(index, size):
    return pl.ds(pl.multiple_of(index * size, size), size)


def lane_fold(values, combine):
    folded = values[:, :128]
    for start in range(128, values.shape[1], 128):
        folded = combine(folded, values[:, start : start + 128])
    return folded


def params(mib):
    return pltpu.CompilerParams(vmem_limit_bytes=mib * MIB)


def cost(flops, bytes_accessed, transcendentals=0):
    return pl.CostEstimate(
        flops=int(flops), bytes_accessed=int(bytes_accessed), transcendentals=int(transcendentals)
    )


def fetch(source, target, sems, first_row=0):
    count, rows = target.shape[:2]

    def chunk_copy(index):
        start = pl.multiple_of(first_row + index * rows, rows)
        return pltpu.make_async_copy(source.at[pl.ds(start, rows), :], target.at[index], sems.at[index])

    for index in range(count):
        chunk_copy(index).start()
    return lambda index: chunk_copy(index).wait()


def teacher_units_kernel(core_ref, emb_ref, unit_ref, half_ref):
    unit_ref[...] = unit_rows(emb_ref[...].astype(jnp.float32))[0].astype(jnp.bfloat16)
    half = half_ref.shape[1]
    for copy in range(half_ref.shape[0]):
        half_ref[copy] = unit_ref[part(core_ref[0], half), :]


def teacher_units(core, teacher_emb, copies):
    rows, width = teacher_emb.shape
    return pl.pallas_call(
        teacher_units_kernel,
        in_specs=[whole(pltpu.SMEM), whole()],
        out_specs=[whole(), whole()],
        out_shape=[
            jax.ShapeDtypeStruct((rows, width), jnp.bfloat16),
            jax.ShapeDtypeStruct((copies, rows // 2, width), jnp.bfloat16),
        ],
        compiler_params=params(4),
        cost_estimate=cost(4 * rows * width, 8 * rows * width),
        name="teacher_units",
    )(core, teacher_emb)


def wide_tops_kernel(unit_ref, protos_hbm, order_ref, tops_ref, protos_ref, sems, top_ref):
    rows = unit_ref.shape[0]
    steps, block = protos_ref.shape[:2]
    arrived = fetch(protos_hbm, protos_ref, sems)
    top_ref[...] = jnp.full(top_ref.shape, -jnp.inf, jnp.float32)

    def step(index, carry):
        arrived(index)
        top = top_ref[:rows, :]
        for start in range(0, block, TILE):
            products = scores(unit_ref[...], protos_ref[index, start : start + TILE, :])
            top = jnp.maximum(top, lane_fold(products, jnp.maximum))
        top_ref[:rows, :] = top
        return carry

    lax.fori_loop(0, steps, step, 0)
    tops = jnp.max(jnp.transpose(top_ref[...]), axis=0, keepdims=True)
    tops_ref[...] = jnp.broadcast_to(tops[None], tops_ref.shape)


def wide_tops(unit, protos, order, copies, steps):
    rows, width = unit.shape
    count = protos.shape[0]
    return pl.pallas_call(
        wide_tops_kernel,
        in_specs=[whole(), whole(pltpu.HBM), whole(pltpu.HBM)],
        out_specs=whole(),
        out_shape=jax.ShapeDtypeStruct((copies, 1, 256), jnp.float32),
        scratch_shapes=[
            pltpu.VMEM((steps, count // steps, width), jnp.bfloat16),
            pltpu.SemaphoreType.DMA((steps,)),
            pltpu.VMEM((256, 128), jnp.float32),
        ],
        compiler_params=params(16),
        cost_estimate=cost(2 * rows * width * count, 2 * width * count),
        name="wide_tops",
    )(unit, protos, order)


def repel_kernel(group, index_ref, unit_ref, tops_ref, scale_ref, protos_hbm, order_ref, *rest):
    out_refs, (protos_ref, sems, scaled_ref, acc_ref, sum_ref, bias_ref) = rest[:-6], rest[-6:]
    rows, width = unit_ref.shape
    steps, block = protos_ref.shape[:2]
    arrived = fetch(protos_hbm, protos_ref, sems)
    first = index_ref[0] * group
    top = tops_ref[first]
    for other in range(1, group):
        top = jnp.maximum(top, tops_ref[first + other])
    bias_ref[...] = jnp.transpose(jnp.broadcast_to(top, (128, 256)))[:rows, :] * -teacher_rate
    acc_ref[...] = jnp.zeros(acc_ref.shape, jnp.float32)
    sum_ref[...] = jnp.zeros(sum_ref.shape, jnp.float32)

    def step(index, carry):
        arrived(index)
        bias = bias_ref[...]
        total = sum_ref[...]
        for start in range(0, block, TILE):
            products = scores(unit_ref[...], protos_ref[index, start : start + TILE, :])
            for lane in range(0, TILE, 128):
                columns = slice(start + lane, start + lane + 128)
                scaled = jnp.exp2(products[:, lane : lane + 128] * teacher_rate + bias)
                scaled = scaled * scale_ref[index, :, columns]
                total = total + scaled
                scaled_ref[:, columns] = scaled.astype(jnp.bfloat16)
        sum_ref[...] = total
        acc_ref[...] += jnp.dot(scaled_ref[...], protos_ref[index], preferred_element_type=jnp.float32)
        return carry

    lax.fori_loop(0, steps, step, 0)
    total = jnp.sum(sum_ref[...], axis=1, keepdims=True)
    sum_ref[...] = jnp.broadcast_to(total, sum_ref.shape)
    share = out_refs[0].shape[0]
    for flip, out_ref in enumerate(out_refs):
        span = part(index_ref[1] ^ flip, share)
        out_ref[:, :width] = acc_ref[span, :]
        out_ref[:, width:] = sum_ref[span, :]


def repel(index, unit, tops, scale, protos, order, proto_size):
    rows, width = unit.shape
    count = protos.shape[0]
    steps, _, block = scale.shape
    return pl.pallas_call(
        functools.partial(repel_kernel, proto_size),
        in_specs=[whole(pltpu.SMEM), whole(), whole(), whole(), whole(pltpu.HBM), whole(pltpu.HBM)],
        out_specs=[whole()] * proto_size,
        out_shape=[jax.ShapeDtypeStruct((rows // proto_size, width + 128), jnp.float32)] * proto_size,
        scratch_shapes=[
            pltpu.VMEM((steps, block, width), jnp.bfloat16),
            pltpu.SemaphoreType.DMA((steps,)),
            pltpu.VMEM((rows, block), jnp.bfloat16),
            pltpu.VMEM((rows, width), jnp.float32),
            pltpu.VMEM((rows, 128), jnp.float32),
            pltpu.VMEM((rows, 128), jnp.float32),
        ],
        compiler_params=params(16),
        cost_estimate=cost(4 * rows * width * count, 2 * width * count, rows * count),
        name="repel",
    )(index, unit, tops, scale, protos, order)


def attract_kernel(first_row, last, emb_ref, state_ref, protos_hbm, *rest):
    out_refs, scratch = rest[:-6], rest[-6:]
    protos_ref, sems, products_ref, acc_ref, sum_ref, top_ref = scratch
    width = emb_ref.shape[1]
    steps, block = protos_ref.shape[:2]
    arrived = fetch(protos_hbm, protos_ref, sems, first_row)
    old_top = state_ref[:, width + 128 :]
    top_ref[...] = old_top

    def first(index, carry):
        arrived(index)
        top = top_ref[...]
        for start in range(0, block, TILE):
            products = scores(emb_ref[...], protos_ref[index, start : start + TILE, :])
            products_ref[index, :, start : start + TILE] = products
            top = jnp.maximum(top, lane_fold(products, jnp.maximum))
        top_ref[...] = top
        return carry

    lax.fori_loop(0, steps, first, 0)
    top = jnp.broadcast_to(jnp.max(top_ref[...], axis=1, keepdims=True), top_ref.shape)
    fade = jnp.exp2((old_top - top) * student_rate)
    top_ref[...] = top
    sum_ref[...] = state_ref[:, width : width + 128] * fade
    acc_ref[...] = state_ref[:, :width] * jnp.tile(fade, (1, width // 128))

    def second(index, carry):
        top = top_ref[...]
        total = sum_ref[...]
        acc = acc_ref[...]
        for start in range(0, block, TILE):
            pieces = []
            for lane in range(start, start + TILE, 128):
                shifted = jnp.exp2((products_ref[index, :, lane : lane + 128] - top) * student_rate)
                total = total + shifted
                pieces.append(shifted.astype(jnp.bfloat16))
            acc = acc + jnp.dot(
                jnp.concatenate(pieces, axis=1),
                protos_ref[index, start : start + TILE, :],
                preferred_element_type=jnp.float32,
            )
        sum_ref[...] = total
        acc_ref[...] = acc
        return carry

    lax.fori_loop(0, steps, second, 0)
    if last:
        total = jnp.sum(sum_ref[...], axis=1, keepdims=True)
        sum_ref[...] = jnp.broadcast_to(total, sum_ref.shape)
    share = out_refs[0].shape[0]
    for slot, out_ref in enumerate(out_refs):
        rows = pl.ds(slot * share, share)
        out_ref[:, :width] = acc_ref[rows, :]
        out_ref[:, width : width + 128] = sum_ref[rows, :]
        out_ref[:, width + 128 :] = top_ref[rows, :]


def attract(emb, state, protos, first_row, count, steps, outputs):
    rows, width = emb.shape
    block = count // steps
    return pl.pallas_call(
        functools.partial(attract_kernel, first_row, outputs > 1),
        in_specs=[whole(), whole(), whole(pltpu.HBM)],
        out_specs=[whole()] * outputs,
        out_shape=[jax.ShapeDtypeStruct((rows // outputs, width + 256), jnp.float32)] * outputs,
        scratch_shapes=[
            pltpu.VMEM((steps, block, width), jnp.bfloat16),
            pltpu.SemaphoreType.DMA((steps,)),
            pltpu.VMEM((steps, rows, block), jnp.float32),
            pltpu.VMEM((rows, width), jnp.float32),
            pltpu.VMEM((rows, 128), jnp.float32),
            pltpu.VMEM((rows, 128), jnp.float32),
        ],
        compiler_params=params(24),
        cost_estimate=cost(4 * rows * width * count, 2 * width * count, rows * count),
        name="attract",
    )(emb, state, protos)


def three_pieces(values):
    high = values.astype(jnp.bfloat16)
    rest = values - high.astype(jnp.float32)
    middle = rest.astype(jnp.bfloat16)
    low = (rest - middle.astype(jnp.float32)).astype(jnp.bfloat16)
    return jnp.concatenate([high, middle, low, jnp.zeros((13, values.shape[1]), jnp.bfloat16)], axis=0)


def lane_scales(folded, protos_total):
    sums = [
        jnp.sum(jnp.transpose(folded[start : start + 128, :]), axis=0, keepdims=True)
        for start in range(0, folded.shape[0], 128)
    ]
    return 1.0 / (protos_total * jnp.concatenate(sums, axis=1))


def give_copies(copies_ref, totals):
    copies_ref[...] = jnp.broadcast_to(totals[None], copies_ref.shape)


def first_sweep_kernel(
    protos_total, index_ref, protos_hbm, mine_hbm, other_hbm, bias_ref, order_ref,
    copies_ref, weights_hbm, protos_ref, units_ref, weights_ref, fold_ref, totals_ref, sems, out_sems,
):
    tiles, thin, lanes = weights_ref.shape
    half = mine_hbm.shape[0]
    core = index_ref[1]
    copies = (
        pltpu.make_async_copy(protos_hbm.at[part(index_ref[0], thin), :], protos_ref, sems.at[0]),
        pltpu.make_async_copy(mine_hbm, units_ref.at[part(core, half), :], sems.at[1]),
        pltpu.make_async_copy(other_hbm, units_ref.at[part(1 - core, half), :], sems.at[2]),
    )
    for copy in copies:
        copy.start()
    fold_ref[...] = jnp.zeros(fold_ref.shape, jnp.float32)
    for copy in copies:
        copy.wait()

    def tile_out(tile):
        return pltpu.make_async_copy(weights_ref.at[tile], weights_hbm.at[tile], out_sems.at[tile])

    def weigh(tile, carry):
        products = scores(protos_ref[...], units_ref[part(tile, lanes), :])
        bias = bias_ref[:, part(tile, lanes)]
        for row in range(0, thin, 64):
            weights = jnp.exp2(products[row : row + 64, :] * teacher_rate + bias)
            weights_ref[tile, row : row + 64, :] = weights.astype(jnp.bfloat16)
            fold_ref[row : row + 64, :] += lane_fold(weights, jnp.add)
        tile_out(tile).start()
        return carry

    lax.fori_loop(0, tiles, weigh, 0)
    pieces = three_pieces(lane_scales(fold_ref[...], protos_total))

    def add_up(tile, carry):
        sums = jnp.dot(pieces, weights_ref[tile], preferred_element_type=jnp.float32)
        totals_ref[:, part(tile, lanes)] = jnp.sum(sums, axis=0, keepdims=True)
        return carry

    lax.fori_loop(0, tiles, add_up, 0)
    give_copies(copies_ref, totals_ref[...])
    for tile in range(tiles):
        tile_out(tile).wait()


def first_sweep(index, protos, mine, other, base, order, copies, thin, protos_total):
    width = protos.shape[1]
    crops_total = 2 * mine.shape[0]
    tiles = crops_total // TILE
    return pl.pallas_call(
        functools.partial(first_sweep_kernel, protos_total),
        in_specs=[whole(pltpu.SMEM), whole(pltpu.HBM), whole(pltpu.HBM), whole(pltpu.HBM), whole(), whole(pltpu.HBM)],
        out_specs=[whole(), whole(pltpu.HBM)],
        out_shape=[
            jax.ShapeDtypeStruct((copies, 1, crops_total), jnp.float32),
            jax.ShapeDtypeStruct((tiles, thin, TILE), jnp.bfloat16),
        ],
        scratch_shapes=[
            pltpu.VMEM((thin, width), jnp.bfloat16),
            pltpu.VMEM((crops_total, width), jnp.bfloat16),
            pltpu.VMEM((tiles, thin, TILE), jnp.bfloat16),
            pltpu.VMEM((thin, 128), jnp.float32),
            pltpu.VMEM((1, crops_total), jnp.float32),
            pltpu.SemaphoreType.DMA((3,)),
            pltpu.SemaphoreType.DMA((tiles,)),
        ],
        compiler_params=params(24 if crops_total <= 2048 else 50),
        cost_estimate=cost(2 * thin * width * crops_total, 2 * thin * crops_total, thin * crops_total),
        name="first_sweep",
    )(index, protos, mine, other, base, order)


def fetch_rows(weights_hbm, weights_ref, sems):
    steps, _, chunk, _ = weights_ref.shape

    def rows_copy(index):
        return pltpu.make_async_copy(
            weights_hbm.at[:, part(index, chunk), :], weights_ref.at[index], sems.at[index]
        )

    for index in range(steps):
        rows_copy(index).start()
    return lambda index: rows_copy(index).wait()


def scaled_fold(weights_ref, index, scale_ref):
    _, tiles, chunk, lanes = weights_ref.shape
    folds = []
    for row in range(0, chunk, 64):
        fold = None
        for tile in range(tiles):
            weights = weights_ref[index, tile, row : row + 64, :].astype(jnp.float32)
            scaled = lane_fold(weights * scale_ref[:, tile * lanes : (tile + 1) * lanes], jnp.add)
            fold = scaled if fold is None else fold + scaled
        folds.append(fold)
    return jnp.concatenate(folds, axis=0)


def next_sweep_kernel(
    protos_total, weights_hbm, parts_ref, order_ref, copies_ref, weights_ref, scale_ref, pieces_ref, totals_ref, sems,
):
    steps, tiles, chunk, lanes = weights_ref.shape
    arrived = fetch_rows(weights_hbm, weights_ref, sems)
    scale_ref[...] = 1.0 / (tiles * lanes * jnp.sum(parts_ref[...], axis=0))
    totals_ref[...] = jnp.zeros(totals_ref.shape, jnp.float32)

    def weigh(index):
        arrived(index)
        return three_pieces(lane_scales(scaled_fold(weights_ref, index, scale_ref), protos_total))

    def add_up(index):
        pieces = pieces_ref[...]
        for tile in range(tiles):
            columns = slice(tile * lanes, (tile + 1) * lanes)
            totals_ref[:, columns] += jnp.dot(
                pieces, weights_ref[index, tile], preferred_element_type=jnp.float32
            )

    pieces_ref[...] = weigh(0)

    def sweep(index, carry):
        add_up(index - 1)
        pieces_ref[...] = weigh(index)
        return carry

    lax.fori_loop(1, steps, sweep, 0)
    add_up(steps - 1)
    give_copies(copies_ref, jnp.sum(totals_ref[...], axis=0, keepdims=True))


def next_sweep(weights, parts, order, protos_total):
    tiles, thin, lanes = weights.shape
    copies, _, crops_total = parts.shape
    chunk = min(thin, 256)
    return pl.pallas_call(
        functools.partial(next_sweep_kernel, protos_total),
        in_specs=[whole(pltpu.HBM), whole(), whole(pltpu.HBM)],
        out_specs=whole(),
        out_shape=jax.ShapeDtypeStruct((copies, 1, crops_total), jnp.float32),
        scratch_shapes=[
            pltpu.VMEM((thin // chunk, tiles, chunk, lanes), jnp.bfloat16),
            pltpu.VMEM((1, crops_total), jnp.float32),
            pltpu.VMEM((16, chunk), jnp.bfloat16),
            pltpu.VMEM((16, crops_total), jnp.float32),
            pltpu.SemaphoreType.DMA((thin // chunk,)),
        ],
        compiler_params=params(16 if crops_total <= 2048 else 50),
        cost_estimate=cost(8 * thin * crops_total, 2 * thin * crops_total),
        name="next_sweep",
    )(weights, parts, order)


def last_scales_kernel(
    protos_total, weights_hbm, parts_ref, order_ref, copies_ref, weights_ref, scale_ref, out_ref, sems,
):
    steps, tiles, chunk, lanes = weights_ref.shape
    arrived = fetch_rows(weights_hbm, weights_ref, sems)
    scale_ref[...] = 1.0 / (tiles * lanes * jnp.sum(parts_ref[...], axis=0))

    def weigh(index, carry):
        arrived(index)
        out_ref[:, part(index, chunk)] = lane_scales(
            scaled_fold(weights_ref, index, scale_ref), protos_total
        )
        return carry

    lax.fori_loop(0, steps, weigh, 0)
    give_copies(copies_ref, out_ref[...])


def last_scales(weights, parts, order, copies, protos_total):
    tiles, thin, lanes = weights.shape
    crops_total = parts.shape[2]
    chunk = min(thin, 256)
    return pl.pallas_call(
        functools.partial(last_scales_kernel, protos_total),
        in_specs=[whole(pltpu.HBM), whole(), whole(pltpu.HBM)],
        out_specs=whole(),
        out_shape=jax.ShapeDtypeStruct((copies, 1, thin), jnp.float32),
        scratch_shapes=[
            pltpu.VMEM((thin // chunk, tiles, chunk, lanes), jnp.bfloat16),
            pltpu.VMEM((1, crops_total), jnp.float32),
            pltpu.VMEM((1, thin), jnp.float32),
            pltpu.SemaphoreType.DMA((thin // chunk,)),
        ],
        compiler_params=params(16 if crops_total <= 2048 else 50),
        cost_estimate=cost(4 * thin * crops_total, 2 * thin * crops_total),
        name="last_scales",
    )(weights, parts, order)


def student_front_kernel(
    index_ref, bias_ref, own_hbm, x_hbm, core_hbm, last_hbm, first_hbm, second_hbm, keep_ref, give_ref,
    first_ref, second_ref, rows_ref, sems,
):
    share = own_hbm.shape[0]
    copies = [
        pltpu.make_async_copy(source, rows_ref.at[slot * share : (slot + 1) * share, :], sems.at[slot])
        for slot, source in enumerate((own_hbm, x_hbm, core_hbm, last_hbm))
    ]
    copies.append(pltpu.make_async_copy(first_hbm, first_ref, sems.at[4]))
    second_copy = pltpu.make_async_copy(second_hbm, second_ref, sems.at[5])
    for copy in copies:
        copy.start()
    second_copy.start()
    hidden = first_ref.shape[1]
    bias = bias_ref[:, part(index_ref[0], hidden)]
    for copy in copies:
        copy.wait()
    h_first = gelu(
        jnp.dot(rows_ref[...], first_ref[...], preferred_element_type=jnp.float32) + bias
    ).astype(jnp.bfloat16)
    second_copy.wait()
    for start in range(0, second_ref.shape[1], 512):
        columns = slice(start, start + 512)
        product = jnp.dot(h_first, second_ref[:, columns], preferred_element_type=jnp.float32)
        keep_ref[:, columns] = product[: 2 * share]
        give_ref[:, columns] = product[2 * share :]


def student_front(index, bias, rows, first, second):
    share, features = rows[0].shape
    hidden, units = second.shape
    return pl.pallas_call(
        student_front_kernel,
        in_specs=[whole(pltpu.SMEM), whole()] + [whole(pltpu.HBM)] * 6,
        out_specs=[whole(), whole()],
        out_shape=[jax.ShapeDtypeStruct((2 * share, units), jnp.float32)] * 2,
        scratch_shapes=[
            pltpu.VMEM(first.shape, jnp.bfloat16),
            pltpu.VMEM(second.shape, jnp.bfloat16),
            pltpu.VMEM((4 * share, features), jnp.bfloat16),
            pltpu.SemaphoreType.DMA((6,)),
        ],
        compiler_params=params(16),
        cost_estimate=cost(8 * share * hidden * (features + units), 2 * hidden * (features + units)),
        name="student_front",
    )(index, bias.reshape(1, -1), *rows, first, second)


def student_middle_kernel(
    index_ref, keep_ref, core_ref, x_ref, bias_ref, own_ref, partner_ref, other_ref, last_ref, last_bias_ref,
    unit_ref, emb_ref, lengths_ref, hidden_ref,
):
    share = x_ref.shape[0]
    block = own_ref.shape[0]
    sums = keep_ref[:share, :] + core_ref[:share, :] + x_ref[...]
    hidden_ref[...] = gelu(sums + bias_ref[...]).astype(jnp.bfloat16)
    index = index_ref[0]
    weights = ((0, own_ref[...]), (2, partner_ref[...]), (1, other_ref[...]), (3, last_ref[...]))
    bottleneck = jnp.broadcast_to(last_bias_ref[...], unit_ref.shape)
    for flip, weight in weights:
        bottleneck = bottleneck + jnp.dot(
            hidden_ref[:, part(index ^ flip, block)], weight, preferred_element_type=jnp.float32
        )
    unit, lengths = unit_rows(bottleneck)
    unit_ref[...] = unit
    emb_ref[...] = unit.astype(jnp.bfloat16)
    lengths_ref[...] = jnp.broadcast_to(lengths, lengths_ref.shape)


def student_middle(index, keep, core_rows, x_rows, bias, weights, last_bias):
    share, units = x_rows.shape
    width = weights[0].shape[1]
    return pl.pallas_call(
        student_middle_kernel,
        in_specs=[whole(pltpu.SMEM)] + [whole()] * 9,
        out_specs=[whole()] * 3,
        out_shape=[
            jax.ShapeDtypeStruct((share, width), jnp.float32),
            jax.ShapeDtypeStruct((share, width), jnp.bfloat16),
            jax.ShapeDtypeStruct((share, 128), jnp.float32),
        ],
        scratch_shapes=[pltpu.VMEM((share, units), jnp.bfloat16)],
        compiler_params=params(12),
        cost_estimate=cost(2 * share * units * width, 2 * units * width + 16 * share * units),
        name="student_middle",
    )(index, keep, core_rows, x_rows, bias.reshape(1, -1), *weights, last_bias.reshape(1, -1))


def finish_kernel(unit_ref, lengths_ref, *rest):
    out_ref, blocks = rest[-1], rest[:-1]
    attracts, repels = blocks[: len(blocks) // 2], blocks[len(blocks) // 2 :]
    width = unit_ref.shape[1]
    row_top = functools.reduce(jnp.maximum, [ref[:, width + 128 :] for ref in attracts])
    attract_sum = repel_sum = 0.0
    row_sum = column_sum = 0.0
    for ref in attracts:
        fade = jnp.exp2((ref[:, width + 128 :] - row_top) * student_rate)
        row_sum = row_sum + ref[:, width : width + 128] * fade
        attract_sum = attract_sum + ref[:, :width] * jnp.tile(fade, (1, width // 128))
    for ref in repels:
        column_sum = column_sum + ref[:, width:]
        repel_sum = repel_sum + ref[:, :width]
    emb_grad = (
        attract_sum / jnp.tile(row_sum, (1, width // 128))
        - repel_sum / jnp.tile(column_sum, (1, width // 128))
    ) / student_temp
    unit = unit_ref[...]
    along = jnp.sum(unit * emb_grad, axis=1, keepdims=True)
    out_ref[...] = (emb_grad - unit * along) / jnp.tile(lengths_ref[...], (1, width // 128))


def finish(unit, lengths, attracts, repels):
    return pl.pallas_call(
        finish_kernel,
        in_specs=[whole()] * (2 + len(attracts) + len(repels)),
        out_specs=whole(),
        out_shape=jax.ShapeDtypeStruct(unit.shape, jnp.float32),
        compiler_params=params(8),
        cost_estimate=cost(40 * unit.size, 40 * unit.size),
        name="finish",
    )(unit, lengths, *attracts, *repels)


def swap(values, axis, flip):
    return lax.ppermute(values, axis, [(i, i ^ flip) for i in range(lax.axis_size(axis))])


def send_blocks(blocks):
    return [blocks[0]] + [swap(block, "proto", flip) for flip, block in enumerate(blocks) if flip]


def all_to_all(copies, axes):
    return lax.all_to_all(copies, axes, 0, 0, tiled=True)


def body(crops, teacher_emb, w_first, b_first, w_second, b_second, w_third, b_third, protos):
    batch_index = lax.axis_index("batch")
    proto_index = lax.axis_index("proto")
    batch_size = lax.axis_size("batch")
    proto_size = lax.axis_size("proto")
    devices = batch_size * proto_size
    share_rows = crops.shape[0]
    group_rows = teacher_emb.shape[0]
    crops_total = group_rows * batch_size
    protos_total = protos.shape[0] * proto_size
    count, width = protos.shape
    thin = count // batch_size
    core = proto_index % 2
    proto_ref = proto_index.reshape(1)
    thin_ref = jnp.stack([batch_index, core])
    wide_ref = jnp.stack([batch_index, proto_index])

    crops_x = swap(crops, "proto", 2)
    own_unit, halves = teacher_units(core.reshape(1), teacher_emb, batch_size)
    mine = all_to_all(halves, "batch").reshape(crops_total // 2, width)
    other = swap(mine, "proto", 1)
    all_tops = all_to_all(wide_tops(own_unit, protos, crops_x, devices, 8), BOTH)
    tops = jnp.max(all_tops.reshape(batch_size, proto_size, 256)[:, :, :group_rows], axis=1)
    tops = jnp.transpose(tops.reshape(batch_size, 2, group_rows // 2), (1, 0, 2))
    base = tops.reshape(1, crops_total) * -teacher_rate

    rows = [crops, crops_x, swap(crops, "proto", 1), swap(crops_x, "proto", 1)]
    keep, give = student_front(proto_ref, b_first, rows, w_first, w_second)
    core_rows = swap(give, "proto", 1)
    x_sent = keep[share_rows:] + core_rows[share_rows:]
    x_rows = swap(x_sent, "proto", 2)
    third_x = swap(w_third, "proto", 2)
    thirds = [w_third, third_x, swap(w_third, "proto", 1), swap(third_x, "proto", 1)]
    unit, rounded, lengths = student_middle(
        proto_ref, keep, core_rows, x_rows, b_second, thirds, b_third
    )
    emb_pair = jnp.concatenate([rounded, swap(rounded, "proto", 2)])
    student_emb = jnp.concatenate([emb_pair, swap(emb_pair, "proto", 1)])
    empty = jnp.concatenate(
        [jnp.zeros((group_rows, width + 128), jnp.float32), jnp.full((group_rows, 128), -1e30, jnp.float32)], axis=1
    )
    (state,) = attract(student_emb, empty, protos, 0, count // 2, 4, 1)
    slots = attract(student_emb, state, protos, count // 2, count // 2, 4, proto_size)
    attract_parts = send_blocks([slots[0], slots[2], slots[1], slots[3]])

    copies, weights = first_sweep(thin_ref, protos, mine, other, base, x_sent, devices, thin, protos_total)
    for _ in range(ITERS - 2):
        copies = next_sweep(weights, all_to_all(copies, BOTH), rounded, protos_total)
    scale_copies = last_scales(weights, all_to_all(copies, BOTH), state, batch_size, protos_total)
    all_scale = all_to_all(scale_copies, "batch")
    repels = repel(wide_ref, own_unit, all_tops, all_scale, protos, slots[0], proto_size)
    return finish(unit, lengths, attract_parts, send_blocks(repels))


def solution(mesh):
    in_specs = (
        P(("batch", "proto"), None),
        P("batch", None),
        P(None, "proto"),
        P(),
        P("proto", None),
        P(),
        P("proto", None),
        P(),
        P("proto", None),
    )
    out_specs = P(("batch", "proto"), None)
    return jax.shard_map(body, mesh=mesh, in_specs=in_specs, out_specs=out_specs, check_vma=False)
```

time: 144 us -> 142 us (0.986)
  blocking collectives: 0 us -> 13.2 us
  starting transfers between devices: 35.7 us -> 26 us
  Pallas kernels: 49.8 us -> 42.6 us
  waiting for transfers between devices: 21.6 us -> 27.6 us
  other arithmetic: 4.52 us -> 0.3 us
    all_to_all x0 -> x1, blocking collectives: none -> 13.2 us  [all_to_all(): return lax.all_to_all(copies, axes, 0, 0, tiled=True)]
    all_to_all x4, waiting for transfers between devices: 5.27 us -> 15.7 us  [all_to_all(): return lax.all_to_all(copies, axes, 0, 0, tiled=True)]
    ppermute x18 -> x17, starting transfers between devices: 18.2 us -> 11.2 us  [swap(): lax.ppermute(values, axis, [(i, i ^ flip) for i in range(lax.axis_size(ax...]
    pallas_call x4, Pallas kernels: 26.6 us -> 20.8 us  [the longest x1 7.35 us: first_sweep(): pl.pallas_call(functools.partial(first_sweep_kernel, protos_total), in_sp...]
    ppermute x18 -> x17, waiting for transfers between devices: 16.4 us -> 11.9 us  [swap(): lax.ppermute(values, axis, [(i, i ^ flip) for i in range(lax.axis_size(ax...]
    all_to_all x4, starting transfers between devices: 17.5 us -> 14.7 us  [all_to_all(): return lax.all_to_all(copies, axes, 0, 0, tiled=True)]
    concatenate x2 -> x0, other arithmetic: 1.82 us -> none  [the longest x1 0.98 us: body(): crops_pair = swap(jnp.concatenate([crops, crops_x]), 'proto', 1)]
    unnamed x48 -> x34, local copies, waits for them, and re-layouts: 30.6 us -> 30.6 us
  transfers between devices with their start and end apart: 22 -> 21, of which waited for: 8 -> 9; matrix products, arithmetic and copies ran while one was open for 3% -> 0% of each run, Pallas kernels for 30% -> 26%
where the time goes in v6:
time: 142 us; the launch traced here: 141 us
  Pallas kernels  42.6 us (30%)
  local copies, waits for them, and re-layouts  30.8 us (22%)
  waiting for transfers between devices  27.6 us (19%)
  starting transfers between devices  26 us (18%)
  blocking collectives  13.2 us (9%)
    unnamed x34, local copies, waits for them, and re-layouts  30.6 us
    all_to_all x4, waiting for transfers between devices, all_to_all(): return lax.all_to_all(copies, axes, 0, 0, tiled=True)  15.7 us
    all_to_all x4, starting transfers between devices, all_to_all(): return lax.all_to_all(copies, axes, 0, 0, tiled=True)  14.7 us
    all_to_all x1, blocking collectives, all_to_all(): return lax.all_to_all(copies, axes, 0, 0, tiled=True)  13.2 us
    ppermute x17, waiting for transfers between devices, swap(): lax.ppermute(values, axis, [(i, i ^ flip) for i in range(lax.axis_size(ax...  11.9 us
    ppermute x17, starting transfers between devices, swap(): lax.ppermute(values, axis, [(i, i ^ flip) for i in range(lax.axis_size(ax...  11.2 us
    pallas_call x1, Pallas kernels, repel(): pl.pallas_call(functools.partial(repel_kernel, proto_size), in_specs=[who...  9.14 us
    pallas_call x2, Pallas kernels, attract(): pl.pallas_call(functools.partial(attract_kernel, first_row, outputs > 1),...  8.29 us
  transfers between devices with their start and end apart: 21, of which 9 were waited for; matrix products, arithmetic and copies ran while one was open for 0% of the time, Pallas kernels for 26%

profile of v6, /device:TPU:0, one launch (start us, length us, event | category | flops | bytes accessed | tf_op | source)
XLA Modules:
  0.0 140.8 jit_solution(3310362897331736874)
XLA Ops:
  0.0 2.9 %collective-permute-start = (bf16[48,1536]{1,0:T(8,128)(2,1)}, bf16[48,1536]{1,0:T(8,128)(2,1)S(1)}, u32[]{:S(2)}, u32[]{:S(2)}) collective-permute-start(bf16[48,1536]{1,0:T(8,128)(2,1)} %own_hbm.1), channel_id=1, source_target_pairs={{0,2},{1,3},{2,0},{3,1},{4,6},{5,7},{6,4},{7,5},{8,10},{9,11},{10,... | collective-permute-start | bytes 442376 | tf_op jit(solution)/shard_map/ppermute | solution.py:615
  2.9 4.1 %collective-permute-done.x_hbm.order_ref = bf16[48,1536]{1,0:T(8,128)(2,1)S(1)} collective-permute-done((bf16[48,1536]{1,0:T(8,128)(2,1)}, bf16[48,1536]{1,0:T(8,128)(2,1)S(1)}, u32[]{:S(2)}, u32[]{:S(2)}) %collective-permute-start) | collective-permute-done | bytes 147488 | tf_op jit(solution)/shard_map/ppermute | solution.py:615
  7.0 0.9 copy-done.12
  7.9 0.9 teacher_units.1
  8.8 1.6 %copy-done.8 = bf16[512,2048]{1,0:T(8,128)(2,1)S(1)} copy-done((bf16[512,2048]{1,0:T(8,128)(2,1)S(1)}, bf16[512,2048]{1,0:T(8,128)(2,1)}, u32[]{:S(2)}) %copy-start.8) | copy-done | bytes 2097176
  10.4 1.4 copy-done.9
  11.8 0.9 copy-done.11
  12.7 0.7 copy-done.13
  13.4 2.1 %student_front.1 = (f32[96,2048]{1,0:T(8,128)S(1)}, f32[96,2048]{1,0:T(8,128)S(1)}) custom-call(s32[1]{0:T(128)} %bitcast.index_ref, f32[1,2048]{1,0:T(1,128)S(1)} %bitcast.10, bf16[48,1536]{1,0:T(8,128)(2,1)S(1)} %copy-done.11, bf16[48,1536]{1,0:T(8,128)(2,1)S(1)} %collective-permute-done.x_hbm.order_ref, ...), custom_call_target="tpu_custom_call" | custom-call | flops 704643072 | bytes 3670016 | tf_op jit(solution)/shard_map/student_front/pallas_call | solution.py:522
  15.6 0.6 collective-permute-start.3
  16.1 3.4 %copy-done = bf16[16384,256]{1,0:T(8,128)(2,1)S(1)} copy-done((bf16[16384,256]{1,0:T(8,128)(2,1)S(1)}, bf16[16384,256]{1,0:T(8,128)(2,1)}, u32[]{:S(2)}) %copy-start) | copy-done | bytes 8388632
  19.5 4.8 %wide_tops.1 = f32[32,1,256]{2,1,0:T(1,128)S(1)} custom-call(bf16[192,256]{1,0:T(8,128)(2,1)S(1)} %get-tuple-element.31.unit_ref, bf16[16384,256]{1,0:T(8,128)(2,1)S(1)} %copy-done, bf16[48,1536]{1,0:T(8,128)(2,1)S(1)} %collective-permute-done.x_hbm.order_ref), custom_call_target="tpu_custom_call" | custom-call | flops 1610612736 | bytes 8388608 | tf_op jit(solution)/shard_map/wide_tops/pallas_call | solution.py:122
  24.3 0.0 copy-start.14
  24.3 0.0 copy-start.15
  24.3 13.2 %all_to_all.25.tops_ref = f32[32,1,256]{2,1,0:T(1,128)S(1)} all-to-all(f32[32,1,256]{2,1,0:T(1,128)S(1)} %wide_tops.1), channel_id=1, replica_groups=mesh['batch'=8,'proto'=4] {'batch','proto'}, dimensions={0} | all-to-all | bytes 65536 | tf_op jit(solution)/shard_map/all_to_all | solution.py:623
  37.5 3.5 %all-to-all-start.1 = ((bf16[8,96,256]{2,1,0:T(8,128)(2,1)}), bf16[8,96,256]{2,1,0:T(8,128)(2,1)S(1)}, u32[]{:S(2)}, u32[]{:S(2)}) async-start(bf16[8,96,256]{2,1,0:T(8,128)(2,1)} %get-tuple-element.32), calls=%async_computation.1 | async-start | bytes 786432 | tf_op jit(solution)/shard_map/all_to_all | solution.py:623
  41.0 0.6 collective-permute-start.5
  41.5 0.1 pad_add_fusion.1.index_ref
  41.6 0.1 reduce
  41.8 0.1 mul.14
  41.8 0.1 mul.16.bias_ref
  41.9 11.2 %all-to-all-done.1 = bf16[8,96,256]{2,1,0:T(8,128)(2,1)S(1)} async-done(((bf16[8,96,256]{2,1,0:T(8,128)(2,1)}), bf16[8,96,256]{2,1,0:T(8,128)(2,1)S(1)}, u32[]{:S(2)}, u32[]{:S(2)}) %all-to-all-start.1) | async-done | bytes 393248 | tf_op jit(solution)/shard_map/all_to_all | solution.py:623
  53.1 0.0 collective-permute-start.13
  53.1 0.0 collective-permute-done.3.core_ref
  53.2 0.6 collective-permute-start.4
  53.7 1.1 collective-permute-done.13.other_hbm
  54.9 3.4 %copy-done.1 = bf16[16384,256]{1,0:T(8,128)(2,1)S(1)} copy-done((bf16[16384,256]{1,0:T(8,128)(2,1)S(1)}, bf16[16384,256]{1,0:T(8,128)(2,1)}, u32[]{:S(2)}) %copy-start.1) | copy-done | bytes 8388632
  58.2 7.3 %first_sweep.1 = (f32[32,1,1536]{2,1,0:T(1,128)}, bf16[6,2048,256]{2,1,0:T(8,128)(2,1)S(1)}) custom-call(s32[2]{0:T(128)S(1)} %pad_add_fusion.1.index_ref, bf16[16384,256]{1,0:T(8,128)(2,1)S(1)} %copy-done.1, bf16[768,256]{1,0:T(8,128)(2,1)S(1)} %bitcast.9, bf16[768,256]{1,0:T(8,128)(2,1)S(1)} %collective-permute-done.13.other_hbm, ...), custom_call_target="tpu_custom_call" | custom-call | flops 1610612736 | bytes 6291456 | tf_op jit(solution)/shard_map/first_sweep/pallas_call | solution.py:348
  65.6 2.6 %copy-done.5 = bf16[6,2048,256]{2,1,0:T(8,128)(2,1)} copy-done((bf16[6,2048,256]{2,1,0:T(8,128)(2,1)}, bf16[6,2048,256]{2,1,0:T(8,128)(2,1)S(1)}, u32[]{:S(2)}) %copy-start.5) | copy-done | bytes 6291480
  68.2 2.7 %all-to-all-start.2 = ((f32[32,1,1536]{2,1,0:T(1,128)}), f32[32,1,1536]{2,1,0:T(1,128)S(1)}, u32[]{:S(2)}, u32[]{:S(2)}) async-start(f32[32,1,1536]{2,1,0:T(1,128)} %get-tuple-element.34), calls=%async_computation.2 | async-start | bytes 393216 | tf_op jit(solution)/shard_map/all_to_all | solution.py:623
  70.9 0.3 collective-permute-start.6
  71.3 0.3 collective-permute-start.7
  71.5 0.1 pad_add_fusion.index_ref
  71.6 0.9 collective-permute-done.6.other_ref
  72.5 0.4 collective-permute-done.7.last_ref
  72.9 0.0 collective-permute-done.4.x_ref
  72.9 0.6 student_middle.1
  73.5 1.8 %collective-permute-start.8 = (bf16[48,256]{1,0:T(8,128)(2,1)S(1)}, bf16[48,256]{1,0:T(8,128)(2,1)S(1)}, u32[]{:S(2)}, u32[]{:S(2)}) collective-permute-start(bf16[48,256]{1,0:T(8,128)(2,1)S(1)} %get-tuple-element.26.order_ref), channel_id=1, source_target_pairs={{0,2},{1,3},{2,0},{3,1},{4,6},{5,7},{6,4},{7,5},{8,10},{9,11},{10,... | collective-permute-start | bytes 73736 | tf_op jit(solution)/shard_map/ppermute | solution.py:615
  75.3 4.5 %all-to-all-done.2.parts_ref = f32[32,1,1536]{2,1,0:T(1,128)S(1)} async-done(((f32[32,1,1536]{2,1,0:T(1,128)}), f32[32,1,1536]{2,1,0:T(1,128)S(1)}, u32[]{:S(2)}, u32[]{:S(2)}) %all-to-all-start.2) | async-done | bytes 196640 | tf_op jit(solution)/shard_map/all_to_all | solution.py:623
  79.8 2.8 %copy-done.6 = bf16[6,2048,256]{2,1,0:T(8,128)(2,1)S(1)} copy-done((bf16[6,2048,256]{2,1,0:T(8,128)(2,1)S(1)}, bf16[6,2048,256]{2,1,0:T(8,128)(2,1)}, u32[]{:S(2)}) %copy-start.6) | copy-done | bytes 6291480
  82.6 5.3 %next_sweep.1 = f32[32,1,1536]{2,1,0:T(1,128)} custom-call(bf16[6,2048,256]{2,1,0:T(8,128)(2,1)S(1)} %copy-done.6, f32[32,1,1536]{2,1,0:T(1,128)S(1)} %all-to-all-done.2.parts_ref, bf16[48,256]{1,0:T(8,128)(2,1)S(1)} %get-tuple-element.26.order_ref), custom_call_target="tpu_custom_call" | custom-call | flops 25165824 | bytes 6291456 | tf_op jit(solution)/shard_map/next_sweep/pallas_call | solution.py:433
  87.9 2.7 %all-to-all-start.3 = ((f32[32,1,1536]{2,1,0:T(1,128)}), f32[32,1,1536]{2,1,0:T(1,128)S(1)}, u32[]{:S(2)}, u32[]{:S(2)}) async-start(f32[32,1,1536]{2,1,0:T(1,128)} %next_sweep.1), calls=%async_computation.3 | async-start | bytes 393216 | tf_op jit(solution)/shard_map/all_to_all | solution.py:623
  90.7 0.3 collective-permute-start.9
  91.0 1.0 collective-permute-done.9
  92.0 0.0 copy-start.2
  92.0 3.4 %copy-done.2 = bf16[16384,256]{1,0:T(8,128)(2,1)S(1)} copy-done((bf16[16384,256]{1,0:T(8,128)(2,1)S(1)}, bf16[16384,256]{1,0:T(8,128)(2,1)}, u32[]{:S(2)}) %copy-start.2) | copy-done | bytes 8388632
  95.4 4.1 %attract.2.state_ref.order_ref = f32[192,512]{1,0:T(8,128)S(1)} custom-call(bf16[192,256]{1,0:T(8,128)(2,1)S(1)} %constant_dynamic-update-slice_fusion.emb_ref, f32[192,512]{1,0:T(8,128)S(1)} %concatenate.15.state_ref, bf16[16384,256]{1,0:T(8,128)(2,1)S(1)} %copy-done.2), custom_call_target="tpu_custom_call" | custom-call | flops 1610612736 | bytes 4194304 | tf_op jit(solution)/shard_map/attract/pallas_call | solution.py:260
  99.5 0.0 all-to-all-done.3.parts_ref
  99.5 2.8 %copy-done.7 = bf16[6,2048,256]{2,1,0:T(8,128)(2,1)S(1)} copy-done((bf16[6,2048,256]{2,1,0:T(8,128)(2,1)S(1)}, bf16[6,2048,256]{2,1,0:T(8,128)(2,1)}, u32[]{:S(2)}) %copy-start.7) | copy-done | bytes 6291480
  102.3 3.4 %last_scales.1 = f32[8,1,2048]{2,1,0:T(1,128)} custom-call(bf16[6,2048,256]{2,1,0:T(8,128)(2,1)S(1)} %copy-done.7, f32[32,1,1536]{2,1,0:T(1,128)S(1)} %all-to-all-done.3.parts_ref, f32[192,512]{1,0:T(8,128)S(1)} %attract.2.state_ref.order_ref), custom_call_target="tpu_custom_call" | custom-call | flops 12582912 | bytes 6291456 | tf_op jit(solution)/shard_map/last_scales/pallas_call | solution.py:473
  105.7 5.8 %all-to-all-start.4 = ((f32[8,1,2048]{2,1,0:T(1,128)}), f32[8,1,2048]{2,1,0:T(1,128)S(1)}, u32[]{:S(2)}, u32[]{:S(2)}) async-start(f32[8,1,2048]{2,1,0:T(1,128)} %last_scales.1), calls=%async_computation.4 | async-start | bytes 131072 | tf_op jit(solution)/shard_map/all_to_all | solution.py:623
  111.6 3.4 %copy-done.3 = bf16[16384,256]{1,0:T(8,128)(2,1)S(1)} copy-done((bf16[16384,256]{1,0:T(8,128)(2,1)S(1)}, bf16[16384,256]{1,0:T(8,128)(2,1)}, u32[]{:S(2)}) %copy-start.3) | copy-done | bytes 8388632
  114.9 4.2 %attract.3 = (f32[48,512]{1,0:T(8,128)S(1)}, f32[48,512]{1,0:T(8,128)S(1)}, f32[48,512]{1,0:T(8,128)S(1)}, f32[48,512]{1,0:T(8,128)S(1)}) custom-call(bf16[192,256]{1,0:T(8,128)(2,1)S(1)} %constant_dynamic-update-slice_fusion.emb_ref, f32[192,512]{1,0:T(8,128)S(1)} %attract.2.state_ref.order_ref, bf16[16384,256]{1,0:T(8,128)(2,1)S(1)} %copy-done.3), custom_call_target="tpu_custom_call" | custom-call | flops 1610612736 | bytes 4194304 | tf_op jit(solution)/shard_map/attract/pallas_call | solution.py:260
  119.1 0.1 collective-permute-start.10
  119.2 1.5 %collective-permute-start.11 = (f32[48,512]{1,0:T(8,128)S(1)}, f32[48,512]{1,0:T(8,128)S(1)}, u32[]{:S(2)}, u32[]{:S(2)}) collective-permute-start(f32[48,512]{1,0:T(8,128)S(1)} %get-tuple-element.29), channel_id=1, source_target_pairs={{0,2},{1,3},{2,0},{3,1},{4,6},{5,7},{6,4},{7,5},{8,10},{9,11},{10,... | collective-permute-start | bytes 294920 | tf_op jit(solution)/shard_map/ppermute | solution.py:615
  120.7 0.3 collective-permute-start.12
  121.1 3.4 %copy-done.4 = bf16[16384,256]{1,0:T(8,128)(2,1)S(1)} copy-done((bf16[16384,256]{1,0:T(8,128)(2,1)S(1)}, bf16[16384,256]{1,0:T(8,128)(2,1)}, u32[]{:S(2)}) %copy-start.4) | copy-done | bytes 8388632
  124.5 9.1 %repel.1 = (f32[48,384]{1,0:T(8,128)S(1)}, f32[48,384]{1,0:T(8,128)S(1)}, f32[48,384]{1,0:T(8,128)S(1)}, f32[48,384]{1,0:T(8,128)S(1)}) custom-call(s32[2]{0:T(128)S(1)} %pad_add_fusion.index_ref, bf16[192,256]{1,0:T(8,128)(2,1)S(1)} %get-tuple-element.31.unit_ref, f32[32,1,256]{2,1,0:T(1,128)S(1)} %all_to_all.25.tops_ref, ...), custom_call_target="tpu_custom_call" | custom-call | flops 3221225472 | bytes 8388608 | tf_op jit(solution)/shard_map/repel/pallas_call | solution.py:181
  133.6 0.4 collective-permute-start.14
  134.0 1.5 %collective-permute-start.15 = (f32[48,384]{1,0:T(8,128)S(1)}, f32[48,384]{1,0:T(8,128)S(1)}, u32[]{:S(2)}, u32[]{:S(2)}) collective-permute-start(f32[48,384]{1,0:T(8,128)S(1)} %get-tuple-element.37), channel_id=1, source_target_pairs={{0,2},{1,3},{2,0},{3,1},{4,6},{5,7},{6,4},{7,5},{8,10},{9,11},{10,... | collective-permute-start | bytes 221192 | tf_op jit(solution)/shard_map/ppermute | solution.py:615
  135.5 0.0 collective-permute-start.16
  135.5 2.8 %collective-permute-done.15.rest_6_ = f32[48,384]{1,0:T(8,128)S(1)} collective-permute-done((f32[48,384]{1,0:T(8,128)S(1)}, f32[48,384]{1,0:T(8,128)S(1)}, u32[]{:S(2)}, u32[]{:S(2)}) %collective-permute-start.15) | collective-permute-done | bytes 73760 | tf_op jit(solution)/shard_map/ppermute | solution.py:615
  138.4 1.6 %collective-permute-done.16.rest_7_ = f32[48,384]{1,0:T(8,128)S(1)} collective-permute-done((f32[48,384]{1,0:T(8,128)S(1)}, f32[48,384]{1,0:T(8,128)S(1)}, u32[]{:S(2)}, u32[]{:S(2)}) %collective-permute-start.16) | collective-permute-done | bytes 73760 | tf_op jit(solution)/shard_map/ppermute | solution.py:615
  140.0 0.8 finish.1
  (39 shorter events, 0.2 us)
Async XLA Ops:
  0.0 7.0 %collective-permute-start = (bf16[48,1536]{1,0:T(8,128)(2,1)}, bf16[48,1536]{1,0:T(8,128)(2,1)S(1)}, u32[]{:S(2)}, u32[]{:S(2)}) collective-permute-start(bf16[48,1536]{1,0:T(8,128)(2,1)} %own_hbm.1), channel_id=1, source_target_pairs={{0,2},{1,3},{2,0},{3,1},{4,6},{5,7},{6,4},{7,5},{8,10},{9,11},{10,... | collective-permute-start | bytes 442376 | tf_op jit(solution)/shard_map/ppermute | solution.py:615
  2.9 5.9 %collective-permute-start.1 = (bf16[48,1536]{1,0:T(8,128)(2,1)}, bf16[48,1536]{1,0:T(8,128)(2,1)S(1)}, u32[]{:S(2)}, u32[]{:S(2)}) collective-permute-start(bf16[48,1536]{1,0:T(8,128)(2,1)} %own_hbm.1), channel_id=1, source_target_pairs={{0,1},{1,0},{2,3},{3,2},{4,5},{5,4},{6,7},{7,6},{8,9},{9,8},{10,11... | collective-permute-start | bytes 442376 | tf_op jit(solution)/shard_map/ppermute | solution.py:615
  7.0 1.8 %collective-permute-start.2 = (bf16[48,1536]{1,0:T(8,128)(2,1)S(1)}, bf16[48,1536]{1,0:T(8,128)(2,1)S(1)}, u32[]{:S(2)}, u32[]{:S(2)}) collective-permute-start(bf16[48,1536]{1,0:T(8,128)(2,1)S(1)} %collective-permute-done.x_hbm.order_ref), channel_id=1, source_target_pairs={{0,1},{1,0},{2,3},{3,2},{4,5},{5,4},{6,7},{7,6},{8,9},{9,8},{10,11... | collective-permute-start | bytes 442376 | tf_op jit(solution)/shard_map/ppermute | solution.py:615
  7.0 0.9 copy-start.12
  8.8 1.6 %copy-start.8 = (bf16[512,2048]{1,0:T(8,128)(2,1)S(1)}, bf16[512,2048]{1,0:T(8,128)(2,1)}, u32[]{:S(2)}) copy-start(bf16[512,2048]{1,0:T(8,128)(2,1)} %second_hbm.1) | copy-start | bytes 6291460
  10.4 1.4 %copy-start.9 = (bf16[1536,512]{1,0:T(8,128)(2,1)S(1)}, bf16[1536,512]{1,0:T(8,128)(2,1)}, u32[]{:S(2)}) copy-start(bf16[1536,512]{1,0:T(8,128)(2,1)} %first_hbm.1) | copy-start | bytes 4718596
  11.8 0.9 copy-start.11
  12.7 0.7 copy-start.13
  13.4 27.6 %copy-start.10 = (bf16[512,256]{1,0:T(8,128)(2,1)S(1)}, bf16[512,256]{1,0:T(8,128)(2,1)}, u32[]{:S(2)}) copy-start(bf16[512,256]{1,0:T(8,128)(2,1)} %own_ref.1) | copy-start | bytes 786436
  15.6 37.6 %collective-permute-start.3 = (f32[96,2048]{1,0:T(8,128)S(1)}, f32[96,2048]{1,0:T(8,128)S(1)}, u32[]{:S(2)}, u32[]{:S(2)}) collective-permute-start(f32[96,2048]{1,0:T(8,128)S(1)} %get-tuple-element.23), channel_id=1, source_target_pairs={{0,1},{1,0},{2,3},{3,2},{4,5},{5,4},{6,7},{7,6},{8,9},{9,8},{10,11... | collective-permute-start | bytes 2359304 | tf_op jit(solution)/shard_map/ppermute | solution.py:615
  16.1 3.4 %copy-start = (bf16[16384,256]{1,0:T(8,128)(2,1)S(1)}, bf16[16384,256]{1,0:T(8,128)(2,1)}, u32[]{:S(2)}) copy-start(bf16[16384,256]{1,0:T(8,128)(2,1)} %protos_hbm.9) | copy-start | bytes 25165828
  24.3 48.6 %copy-start.14 = (f32[2048]{0:T(1024)S(1)}, f32[2048]{0:T(1024)}, u32[]{:S(2)}) copy-start(f32[2048]{0:T(1024)} %param.14) | copy-start | bytes 24580
  24.3 48.6 %copy-start.15 = (f32[256]{0:T(256)S(1)}, f32[256]{0:T(256)}, u32[]{:S(2)}) copy-start(f32[256]{0:T(256)} %param.16) | copy-start | bytes 3076
  37.5 15.6 %all-to-all-start.1 = ((bf16[8,96,256]{2,1,0:T(8,128)(2,1)}), bf16[8,96,256]{2,1,0:T(8,128)(2,1)S(1)}, u32[]{:S(2)}, u32[]{:S(2)}) async-start(bf16[8,96,256]{2,1,0:T(8,128)(2,1)} %get-tuple-element.32), calls=%async_computation.1 | async-start | bytes 786432 | tf_op jit(solution)/shard_map/all_to_all | solution.py:623
  41.0 30.3 %collective-permute-start.5 = (bf16[512,256]{1,0:T(8,128)(2,1)S(1)}, bf16[512,256]{1,0:T(8,128)(2,1)S(1)}, u32[]{:S(2)}, u32[]{:S(2)}) collective-permute-start(bf16[512,256]{1,0:T(8,128)(2,1)S(1)} %copy-done.10), channel_id=1, source_target_pairs={{0,2},{1,3},{2,0},{3,1},{4,6},{5,7},{6,4},{7,5},{8,10},{9,11},{10,... | collective-permute-start | bytes 786440 | tf_op jit(solution)/shard_map/ppermute | solution.py:615
  53.1 1.7 %collective-permute-start.13 = (bf16[768,256]{1,0:T(8,128)(2,1)S(1)}, bf16[768,256]{1,0:T(8,128)(2,1)S(1)}, u32[]{:S(2)}, u32[]{:S(2)}) collective-permute-start(bf16[768,256]{1,0:T(8,128)(2,1)S(1)} %bitcast.8), channel_id=1, source_target_pairs={{0,1},{1,0},{2,3},{3,2},{4,5},{5,4},{6,7},{7,6},{8,9},{9,8},{10,11... | collective-permute-start | bytes 1179656 | tf_op jit(solution)/shard_map/ppermute | solution.py:615
  53.2 19.7 %collective-permute-start.4 = (f32[48,2048]{1,0:T(8,128)S(1)}, f32[48,2048]{1,0:T(8,128)S(1)}, u32[]{:S(2)}, u32[]{:S(2)}) collective-permute-start(f32[48,2048]{1,0:T(8,128)S(1)} %slice_add_fusion.order_ref), channel_id=1, source_target_pairs={{0,2},{1,3},{2,0},{3,1},{4,6},{5,7},{6,4},{7,5},{8,10},{9,11},{10,... | collective-permute-start | bytes 1179656 | tf_op jit(solution)/shard_map/ppermute | solution.py:615
  54.8 3.4 %copy-start.1 = (bf16[16384,256]{1,0:T(8,128)(2,1)S(1)}, bf16[16384,256]{1,0:T(8,128)(2,1)}, u32[]{:S(2)}) copy-start(bf16[16384,256]{1,0:T(8,128)(2,1)} %protos_hbm.9) | copy-start | bytes 25165828
  65.6 2.6 %copy-start.5 = (bf16[6,2048,256]{2,1,0:T(8,128)(2,1)}, bf16[6,2048,256]{2,1,0:T(8,128)(2,1)S(1)}, u32[]{:S(2)}) copy-start(bf16[6,2048,256]{2,1,0:T(8,128)(2,1)S(1)} %get-tuple-element.33.weights_hbm) | copy-start | bytes 18874372
  68.2 11.6 %all-to-all-start.2 = ((f32[32,1,1536]{2,1,0:T(1,128)}), f32[32,1,1536]{2,1,0:T(1,128)S(1)}, u32[]{:S(2)}, u32[]{:S(2)}) async-start(f32[32,1,1536]{2,1,0:T(1,128)} %get-tuple-element.34), calls=%async_computation.2 | async-start | bytes 393216 | tf_op jit(solution)/shard_map/all_to_all | solution.py:623
  70.9 1.6 %collective-permute-start.6 = (bf16[512,256]{1,0:T(8,128)(2,1)S(1)}, bf16[512,256]{1,0:T(8,128)(2,1)S(1)}, u32[]{:S(2)}, u32[]{:S(2)}) collective-permute-start(bf16[512,256]{1,0:T(8,128)(2,1)S(1)} %copy-done.10), channel_id=1, source_target_pairs={{0,1},{1,0},{2,3},{3,2},{4,5},{5,4},{6,7},{7,6},{8,9},{9,8},{10,11... | collective-permute-start | bytes 786440 | tf_op jit(solution)/shard_map/ppermute | solution.py:615
  71.3 1.7 %collective-permute-start.7 = (bf16[512,256]{1,0:T(8,128)(2,1)S(1)}, bf16[512,256]{1,0:T(8,128)(2,1)S(1)}, u32[]{:S(2)}, u32[]{:S(2)}) collective-permute-start(bf16[512,256]{1,0:T(8,128)(2,1)S(1)} %collective-permute-done.5.partner_ref), channel_id=1, source_target_pairs={{0,1},{1,0},{2,3},{3,2},{4,5},{5,4},{6,7},{7,6},{8,9},{9,8},{10,11... | collective-permute-start | bytes 786440 | tf_op jit(solution)/shard_map/ppermute | solution.py:615
  73.5 17.1 %collective-permute-start.8 = (bf16[48,256]{1,0:T(8,128)(2,1)S(1)}, bf16[48,256]{1,0:T(8,128)(2,1)S(1)}, u32[]{:S(2)}, u32[]{:S(2)}) collective-permute-start(bf16[48,256]{1,0:T(8,128)(2,1)S(1)} %get-tuple-element.26.order_ref), channel_id=1, source_target_pairs={{0,2},{1,3},{2,0},{3,1},{4,6},{5,7},{6,4},{7,5},{8,10},{9,11},{10,... | collective-permute-start | bytes 73736 | tf_op jit(solution)/shard_map/ppermute | solution.py:615
  79.8 2.8 %copy-start.6 = (bf16[6,2048,256]{2,1,0:T(8,128)(2,1)S(1)}, bf16[6,2048,256]{2,1,0:T(8,128)(2,1)}, u32[]{:S(2)}) copy-start(bf16[6,2048,256]{2,1,0:T(8,128)(2,1)} %copy-done.5) | copy-start | bytes 18874372
  87.9 11.6 %all-to-all-start.3 = ((f32[32,1,1536]{2,1,0:T(1,128)}), f32[32,1,1536]{2,1,0:T(1,128)S(1)}, u32[]{:S(2)}, u32[]{:S(2)}) async-start(f32[32,1,1536]{2,1,0:T(1,128)} %next_sweep.1), calls=%async_computation.3 | async-start | bytes 393216 | tf_op jit(solution)/shard_map/all_to_all | solution.py:623
  90.7 1.3 collective-permute-start.9
  92.0 3.4 %copy-start.2 = (bf16[16384,256]{1,0:T(8,128)(2,1)S(1)}, bf16[16384,256]{1,0:T(8,128)(2,1)}, u32[]{:S(2)}) copy-start(bf16[16384,256]{1,0:T(8,128)(2,1)} %protos_hbm.9) | copy-start | bytes 25165828
  99.5 2.8 %copy-start.7 = (bf16[6,2048,256]{2,1,0:T(8,128)(2,1)S(1)}, bf16[6,2048,256]{2,1,0:T(8,128)(2,1)}, u32[]{:S(2)}) copy-start(bf16[6,2048,256]{2,1,0:T(8,128)(2,1)} %copy-done.5) | copy-start | bytes 18874372
  105.7 15.4 %all-to-all-start.4 = ((f32[8,1,2048]{2,1,0:T(1,128)}), f32[8,1,2048]{2,1,0:T(1,128)S(1)}, u32[]{:S(2)}, u32[]{:S(2)}) async-start(f32[8,1,2048]{2,1,0:T(1,128)} %last_scales.1), calls=%async_computation.4 | async-start | bytes 131072 | tf_op jit(solution)/shard_map/all_to_all | solution.py:623
  111.6 3.4 %copy-start.3 = (bf16[16384,256]{1,0:T(8,128)(2,1)S(1)}, bf16[16384,256]{1,0:T(8,128)(2,1)}, u32[]{:S(2)}) copy-start(bf16[16384,256]{1,0:T(8,128)(2,1)} %protos_hbm.9) | copy-start | bytes 25165828
  119.1 16.4 %collective-permute-start.10 = (f32[48,512]{1,0:T(8,128)S(1)}, f32[48,512]{1,0:T(8,128)S(1)}, u32[]{:S(2)}, u32[]{:S(2)}) collective-permute-start(f32[48,512]{1,0:T(8,128)S(1)} %get-tuple-element.28), channel_id=1, source_target_pairs={{0,1},{1,0},{2,3},{3,2},{4,5},{5,4},{6,7},{7,6},{8,9},{9,8},{10,11... | collective-permute-start | bytes 294920 | tf_op jit(solution)/shard_map/ppermute | solution.py:615
  119.2 16.3 %collective-permute-start.11 = (f32[48,512]{1,0:T(8,128)S(1)}, f32[48,512]{1,0:T(8,128)S(1)}, u32[]{:S(2)}, u32[]{:S(2)}) collective-permute-start(f32[48,512]{1,0:T(8,128)S(1)} %get-tuple-element.29), channel_id=1, source_target_pairs={{0,2},{1,3},{2,0},{3,1},{4,6},{5,7},{6,4},{7,5},{8,10},{9,11},{10,... | collective-permute-start | bytes 294920 | tf_op jit(solution)/shard_map/ppermute | solution.py:615
  120.7 14.8 %collective-permute-start.12 = (f32[48,512]{1,0:T(8,128)S(1)}, f32[48,512]{1,0:T(8,128)S(1)}, u32[]{:S(2)}, u32[]{:S(2)}) collective-permute-start(f32[48,512]{1,0:T(8,128)S(1)} %get-tuple-element.30), channel_id=1, source_target_pairs={{0,3},{1,2},{2,1},{3,0},{4,7},{5,6},{6,5},{7,4},{8,11},{9,10},{10,... | collective-permute-start | bytes 294920 | tf_op jit(solution)/shard_map/ppermute | solution.py:615
  121.1 3.4 %copy-start.4 = (bf16[16384,256]{1,0:T(8,128)(2,1)S(1)}, bf16[16384,256]{1,0:T(8,128)(2,1)}, u32[]{:S(2)}) copy-start(bf16[16384,256]{1,0:T(8,128)(2,1)} %protos_hbm.9) | copy-start | bytes 25165828
  133.6 1.9 %collective-permute-start.14 = (f32[48,384]{1,0:T(8,128)S(1)}, f32[48,384]{1,0:T(8,128)S(1)}, u32[]{:S(2)}, u32[]{:S(2)}) collective-permute-start(f32[48,384]{1,0:T(8,128)S(1)} %get-tuple-element.36), channel_id=1, source_target_pairs={{0,1},{1,0},{2,3},{3,2},{4,5},{5,4},{6,7},{7,6},{8,9},{9,8},{10,11... | collective-permute-start | bytes 221192 | tf_op jit(solution)/shard_map/ppermute | solution.py:615
  134.0 4.4 %collective-permute-start.15 = (f32[48,384]{1,0:T(8,128)S(1)}, f32[48,384]{1,0:T(8,128)S(1)}, u32[]{:S(2)}, u32[]{:S(2)}) collective-permute-start(f32[48,384]{1,0:T(8,128)S(1)} %get-tuple-element.37), channel_id=1, source_target_pairs={{0,2},{1,3},{2,0},{3,1},{4,6},{5,7},{6,4},{7,5},{8,10},{9,11},{10,... | collective-permute-start | bytes 221192 | tf_op jit(solution)/shard_map/ppermute | solution.py:615
  135.5 4.5 %collective-permute-start.16 = (f32[48,384]{1,0:T(8,128)S(1)}, f32[48,384]{1,0:T(8,128)S(1)}, u32[]{:S(2)}, u32[]{:S(2)}) collective-permute-start(f32[48,384]{1,0:T(8,128)S(1)} %get-tuple-element.38), channel_id=1, source_target_pairs={{0,3},{1,2},{2,1},{3,0},{4,7},{5,6},{6,5},{7,4},{8,11},{9,10},{10,... | collective-permute-start | bytes 221192 | tf_op jit(solution)/shard_map/ppermute | solution.py:615

commit v7 on v6

--- a/solution.py
+++ b/solution.py
@@ -40,6 +40,10 @@
     return pl.BlockSpec(memory_space=memory_space)
 
 
+def in_hbm(array):
+    return pltpu.with_memory_space_constraint(array, pltpu.HBM)
+
+
 def part(index, size):
     return pl.ds(pl.multiple_of(index * size, size), size)
 
@@ -75,12 +79,11 @@
 
 def teacher_units_kernel(core_ref, emb_ref, unit_ref, half_ref):
     unit_ref[...] = unit_rows(emb_ref[...].astype(jnp.float32))[0].astype(jnp.bfloat16)
-    half = half_ref.shape[1]
-    for copy in range(half_ref.shape[0]):
-        half_ref[copy] = unit_ref[part(core_ref[0], half), :]
-
-
-def teacher_units(core, teacher_emb, copies):
+    half = half_ref.shape[0]
+    half_ref[...] = unit_ref[part(core_ref[0], half), :]
+
+
+def teacher_units(core, teacher_emb):
     rows, width = teacher_emb.shape
     return pl.pallas_call(
         teacher_units_kernel,
@@ -88,19 +91,19 @@
         out_specs=[whole(), whole()],
         out_shape=[
             jax.ShapeDtypeStruct((rows, width), jnp.bfloat16),
-            jax.ShapeDtypeStruct((copies, rows // 2, width), jnp.bfloat16),
+            jax.ShapeDtypeStruct((rows // 2, width), jnp.bfloat16),
         ],
         compiler_params=params(4),
         cost_estimate=cost(4 * rows * width, 8 * rows * width),
         name="teacher_units",
-    )(core, teacher_emb)
-
-
-def wide_tops_kernel(unit_ref, protos_hbm, order_ref, tops_ref, protos_ref, sems, top_ref):
+    )(core, in_hbm(teacher_emb))
+
+
+def wide_tops_kernel(first_row, last, unit_ref, protos_hbm, before_ref, order_ref, out_ref, protos_ref, sems, top_ref):
     rows = unit_ref.shape[0]
     steps, block = protos_ref.shape[:2]
-    arrived = fetch(protos_hbm, protos_ref, sems)
-    top_ref[...] = jnp.full(top_ref.shape, -jnp.inf, jnp.float32)
+    arrived = fetch(protos_hbm, protos_ref, sems, first_row)
+    top_ref[...] = before_ref[...]
 
     def step(index, carry):
         arrived(index)
@@ -112,18 +115,21 @@
         return carry
 
     lax.fori_loop(0, steps, step, 0)
-    tops = jnp.max(jnp.transpose(top_ref[...]), axis=0, keepdims=True)
-    tops_ref[...] = jnp.broadcast_to(tops[None], tops_ref.shape)
-
-
-def wide_tops(unit, protos, order, copies, steps):
+    if last:
+        tops = jnp.max(jnp.transpose(top_ref[...]), axis=0, keepdims=True)
+        out_ref[...] = jnp.broadcast_to(tops[None], out_ref.shape)
+    else:
+        out_ref[...] = top_ref[...]
+
+
+def wide_tops(unit, protos, before, order, copies, first_row, count, steps):
     rows, width = unit.shape
-    count = protos.shape[0]
-    return pl.pallas_call(
-        wide_tops_kernel,
-        in_specs=[whole(), whole(pltpu.HBM), whole(pltpu.HBM)],
+    shape = (copies, 1, 256) if copies else before.shape
+    return pl.pallas_call(
+        functools.partial(wide_tops_kernel, first_row, copies > 0),
+        in_specs=[whole(), whole(pl.ANY), whole(), whole(pl.ANY)],
         out_specs=whole(),
-        out_shape=jax.ShapeDtypeStruct((copies, 1, 256), jnp.float32),
+        out_shape=jax.ShapeDtypeStruct(shape, jnp.float32),
         scratch_shapes=[
             pltpu.VMEM((steps, count // steps, width), jnp.bfloat16),
             pltpu.SemaphoreType.DMA((steps,)),
@@ -132,11 +138,11 @@
         compiler_params=params(16),
         cost_estimate=cost(2 * rows * width * count, 2 * width * count),
         name="wide_tops",
-    )(unit, protos, order)
+    )(unit, in_hbm(protos), before, order)
 
 
 def repel_kernel(group, index_ref, unit_ref, tops_ref, scale_ref, protos_hbm, order_ref, *rest):
-    out_refs, (protos_ref, sems, scaled_ref, acc_ref, sum_ref, bias_ref) = rest[:-6], rest[-6:]
+    out_refs, (protos_ref, sems, acc_ref, sum_ref, bias_ref) = rest[:-5], rest[-5:]
     rows, width = unit_ref.shape
     steps, block = protos_ref.shape[:2]
     arrived = fetch(protos_hbm, protos_ref, sems)
@@ -152,16 +158,21 @@
         arrived(index)
         bias = bias_ref[...]
         total = sum_ref[...]
+        acc = acc_ref[...]
         for start in range(0, block, TILE):
-            products = scores(unit_ref[...], protos_ref[index, start : start + TILE, :])
+            protos = protos_ref[index, start : start + TILE, :]
+            products = scores(unit_ref[...], protos)
+            pieces = []
             for lane in range(0, TILE, 128):
-                columns = slice(start + lane, start + lane + 128)
                 scaled = jnp.exp2(products[:, lane : lane + 128] * teacher_rate + bias)
-                scaled = scaled * scale_ref[index, :, columns]
+                scaled = scaled * scale_ref[index, :, start + lane : start + lane + 128]
                 total = total + scaled
-                scaled_ref[:, columns] = scaled.astype(jnp.bfloat16)
+                pieces.append(scaled.astype(jnp.bfloat16))
+            acc = acc + jnp.dot(
+                jnp.concatenate(pieces, axis=1), protos, preferred_element_type=jnp.float32
+            )
         sum_ref[...] = total
-        acc_ref[...] += jnp.dot(scaled_ref[...], protos_ref[index], preferred_element_type=jnp.float32)
+        acc_ref[...] = acc
         return carry
 
     lax.fori_loop(0, steps, step, 0)
@@ -180,13 +191,12 @@
     steps, _, block = scale.shape
     return pl.pallas_call(
         functools.partial(repel_kernel, proto_size),
-        in_specs=[whole(pltpu.SMEM), whole(), whole(), whole(), whole(pltpu.HBM), whole(pltpu.HBM)],
+        in_specs=[whole(pltpu.SMEM), whole(), whole(), whole(), whole(pl.ANY), whole(pl.ANY)],
         out_specs=[whole()] * proto_size,
         out_shape=[jax.ShapeDtypeStruct((rows // proto_size, width + 128), jnp.float32)] * proto_size,
         scratch_shapes=[
             pltpu.VMEM((steps, block, width), jnp.bfloat16),
             pltpu.SemaphoreType.DMA((steps,)),
-            pltpu.VMEM((rows, block), jnp.bfloat16),
             pltpu.VMEM((rows, width), jnp.float32),
             pltpu.VMEM((rows, 128), jnp.float32),
             pltpu.VMEM((rows, 128), jnp.float32),
@@ -194,7 +204,7 @@
         compiler_params=params(16),
         cost_estimate=cost(4 * rows * width * count, 2 * width * count, rows * count),
         name="repel",
-    )(index, unit, tops, scale, protos, order)
+    )(index, unit, tops, scale, in_hbm(protos), order)
 
 
 def attract_kernel(first_row, last, emb_ref, state_ref, protos_hbm, *rest):
@@ -259,7 +269,7 @@
     block = count // steps
     return pl.pallas_call(
         functools.partial(attract_kernel, first_row, outputs > 1),
-        in_specs=[whole(), whole(), whole(pltpu.HBM)],
+        in_specs=[whole(), whole(), whole(pl.ANY)],
         out_specs=[whole()] * outputs,
         out_shape=[jax.ShapeDtypeStruct((rows // outputs, width + 256), jnp.float32)] * outputs,
         scratch_shapes=[
@@ -273,7 +283,7 @@
         compiler_params=params(24),
         cost_estimate=cost(4 * rows * width * count, 2 * width * count, rows * count),
         name="attract",
-    )(emb, state, protos)
+    )(emb, state, in_hbm(protos))
 
 
 def three_pieces(values):
@@ -297,10 +307,10 @@
 
 
 def first_sweep_kernel(
-    protos_total, index_ref, protos_hbm, mine_hbm, other_hbm, bias_ref, order_ref,
-    copies_ref, weights_hbm, protos_ref, units_ref, weights_ref, fold_ref, totals_ref, sems, out_sems,
+    chunk, protos_total, index_ref, protos_hbm, mine_hbm, other_hbm, bias_ref, order_ref,
+    copies_ref, weights_hbm, protos_ref, units_ref, weights_ref, rounded_ref, scale_ref, sems, out_sems,
 ):
-    tiles, thin, lanes = weights_ref.shape
+    thin, crops_total = weights_ref.shape
     half = mine_hbm.shape[0]
     core = index_ref[1]
     copies = (
@@ -310,70 +320,77 @@
     )
     for copy in copies:
         copy.start()
-    fold_ref[...] = jnp.zeros(fold_ref.shape, jnp.float32)
     for copy in copies:
         copy.wait()
 
-    def tile_out(tile):
-        return pltpu.make_async_copy(weights_ref.at[tile], weights_hbm.at[tile], out_sems.at[tile])
-
-    def weigh(tile, carry):
-        products = scores(protos_ref[...], units_ref[part(tile, lanes), :])
-        bias = bias_ref[:, part(tile, lanes)]
-        for row in range(0, thin, 64):
-            weights = jnp.exp2(products[row : row + 64, :] * teacher_rate + bias)
-            weights_ref[tile, row : row + 64, :] = weights.astype(jnp.bfloat16)
-            fold_ref[row : row + 64, :] += lane_fold(weights, jnp.add)
-        tile_out(tile).start()
+    def chunk_out(index):
+        return pltpu.make_async_copy(
+            rounded_ref.at[index], weights_hbm.at[part(index, chunk), :], out_sems.at[index]
+        )
+
+    def weigh(index, carry):
+        rows = part(index, chunk)
+        protos = protos_ref[rows, :]
+        folded = jnp.zeros((chunk, 128), jnp.float32)
+        for start in range(0, crops_total, TILE):
+            columns = slice(start, start + TILE)
+            products = scores(protos, units_ref[columns, :])
+            weights = jnp.exp2(products * teacher_rate + bias_ref[:, columns])
+            weights_ref[rows, columns] = weights
+            rounded_ref[index, :, columns] = weights.astype(jnp.bfloat16)
+            folded = folded + lane_fold(weights, jnp.add)
+        sums = jnp.sum(folded, axis=1, keepdims=True)
+        scale_ref[rows, :] = jnp.broadcast_to(1.0 / (protos_total * sums), (chunk, 128))
+        chunk_out(index).start()
         return carry
 
-    lax.fori_loop(0, tiles, weigh, 0)
-    pieces = three_pieces(lane_scales(fold_ref[...], protos_total))
-
-    def add_up(tile, carry):
-        sums = jnp.dot(pieces, weights_ref[tile], preferred_element_type=jnp.float32)
-        totals_ref[:, part(tile, lanes)] = jnp.sum(sums, axis=0, keepdims=True)
-        return carry
-
-    lax.fori_loop(0, tiles, add_up, 0)
-    give_copies(copies_ref, totals_ref[...])
-    for tile in range(tiles):
-        tile_out(tile).wait()
+    lax.fori_loop(0, thin // chunk, weigh, 0)
+    small = min(thin, 64)
+
+    def add_up(index, totals):
+        rows = part(index, small)
+        scaled = weights_ref[rows, :] * jnp.tile(scale_ref[rows, :], (1, crops_total // 128))
+        return totals + jnp.sum(scaled.reshape(-1, 8, crops_total), axis=0)
+
+    totals = lax.fori_loop(0, thin // small, add_up, jnp.zeros((8, crops_total), jnp.float32))
+    give_copies(copies_ref, jnp.sum(totals, axis=0, keepdims=True))
+    for index in range(thin // chunk):
+        chunk_out(index).wait()
 
 
 def first_sweep(index, protos, mine, other, base, order, copies, thin, protos_total):
     width = protos.shape[1]
     crops_total = 2 * mine.shape[0]
-    tiles = crops_total // TILE
-    return pl.pallas_call(
-        functools.partial(first_sweep_kernel, protos_total),
-        in_specs=[whole(pltpu.SMEM), whole(pltpu.HBM), whole(pltpu.HBM), whole(pltpu.HBM), whole(), whole(pltpu.HBM)],
-        out_specs=[whole(), whole(pltpu.HBM)],
+    chunk = min(thin, 512)
+    return pl.pallas_call(
+        functools.partial(first_sweep_kernel, chunk, protos_total),
+        in_specs=[whole(pltpu.SMEM), whole(pl.ANY), whole(pl.ANY), whole(pl.ANY), whole(), whole(pl.ANY)],
+        out_specs=[whole(), whole(pl.ANY)],
         out_shape=[
             jax.ShapeDtypeStruct((copies, 1, crops_total), jnp.float32),
-            jax.ShapeDtypeStruct((tiles, thin, TILE), jnp.bfloat16),
+            pltpu.HBM((thin, crops_total), jnp.bfloat16),
         ],
         scratch_shapes=[
             pltpu.VMEM((thin, width), jnp.bfloat16),
             pltpu.VMEM((crops_total, width), jnp.bfloat16),
-            pltpu.VMEM((tiles, thin, TILE), jnp.bfloat16),
+            pltpu.VMEM((thin, crops_total), jnp.float32),
+            pltpu.VMEM((thin // chunk, chunk, crops_total), jnp.bfloat16),
             pltpu.VMEM((thin, 128), jnp.float32),
-            pltpu.VMEM((1, crops_total), jnp.float32),
             pltpu.SemaphoreType.DMA((3,)),
-            pltpu.SemaphoreType.DMA((tiles,)),
-        ],
-        compiler_params=params(24 if crops_total <= 2048 else 50),
+            pltpu.SemaphoreType.DMA((thin // chunk,)),
+        ],
+        compiler_params=params(32 if crops_total <= 2048 else 56),
         cost_estimate=cost(2 * thin * width * crops_total, 2 * thin * crops_total, thin * crops_total),
         name="first_sweep",
-    )(index, protos, mine, other, base, order)
+    )(index, in_hbm(protos), mine, other, base, order)
 
 
 def fetch_rows(weights_hbm, weights_ref, sems):
-    steps, _, chunk, _ = weights_ref.shape
+    steps, chunk, _ = weights_ref.shape
 
     def rows_copy(index):
         return pltpu.make_async_copy(
-            weights_hbm.at[:, part(index, chunk), :], weights_ref.at[index], sems.at[index]
+            weights_hbm.at[part(index, chunk), :], weights_ref.at[index], sems.at[index]
         )
 
     for index in range(steps):
@@ -382,13 +399,14 @@
 
 
 def scaled_fold(weights_ref, index, scale_ref):
-    _, tiles, chunk, lanes = weights_ref.shape
+    _, chunk, crops_total = weights_ref.shape
     folds = []
     for row in range(0, chunk, 64):
         fold = None
-        for tile in range(tiles):
-            weights = weights_ref[index, tile, row : row + 64, :].astype(jnp.float32)
-            scaled = lane_fold(weights * scale_ref[:, tile * lanes : (tile + 1) * lanes], jnp.add)
+        for start in range(0, crops_total, TILE):
+            columns = slice(start, start + TILE)
+            weights = weights_ref[index, row : row + 64, columns].astype(jnp.float32)
+            scaled = lane_fold(weights * scale_ref[:, columns], jnp.add)
             fold = scaled if fold is None else fold + scaled
         folds.append(fold)
     return jnp.concatenate(folds, axis=0)
@@ -397,46 +415,44 @@
 def next_sweep_kernel(
     protos_total, weights_hbm, parts_ref, order_ref, copies_ref, weights_ref, scale_ref, pieces_ref, totals_ref, sems,
 ):
-    steps, tiles, chunk, lanes = weights_ref.shape
+    steps, chunk, crops_total = weights_ref.shape
     arrived = fetch_rows(weights_hbm, weights_ref, sems)
-    scale_ref[...] = 1.0 / (tiles * lanes * jnp.sum(parts_ref[...], axis=0))
+    scale_ref[...] = 1.0 / (crops_total * jnp.sum(parts_ref[...], axis=0))
     totals_ref[...] = jnp.zeros(totals_ref.shape, jnp.float32)
 
     def weigh(index):
+        return three_pieces(lane_scales(scaled_fold(weights_ref, index, scale_ref), protos_total))
+
+    def add_up(index):
+        return jnp.dot(pieces_ref[...], weights_ref[index], preferred_element_type=jnp.float32)
+
+    arrived(0)
+    pieces_ref[...] = weigh(0)
+
+    def sweep(index, carry):
         arrived(index)
-        return three_pieces(lane_scales(scaled_fold(weights_ref, index, scale_ref), protos_total))
-
-    def add_up(index):
-        pieces = pieces_ref[...]
-        for tile in range(tiles):
-            columns = slice(tile * lanes, (tile + 1) * lanes)
-            totals_ref[:, columns] += jnp.dot(
-                pieces, weights_ref[index, tile], preferred_element_type=jnp.float32
-            )
-
-    pieces_ref[...] = weigh(0)
-
-    def sweep(index, carry):
-        add_up(index - 1)
-        pieces_ref[...] = weigh(index)
+        sums = add_up(index - 1)
+        pieces = weigh(index)
+        totals_ref[...] += sums
+        pieces_ref[...] = pieces
         return carry
 
     lax.fori_loop(1, steps, sweep, 0)
-    add_up(steps - 1)
-    give_copies(copies_ref, jnp.sum(totals_ref[...], axis=0, keepdims=True))
+    totals = totals_ref[...] + add_up(steps - 1)
+    give_copies(copies_ref, jnp.sum(totals, axis=0, keepdims=True))
 
 
 def next_sweep(weights, parts, order, protos_total):
-    tiles, thin, lanes = weights.shape
-    copies, _, crops_total = parts.shape
+    thin, crops_total = weights.shape
+    copies = parts.shape[0]
     chunk = min(thin, 256)
     return pl.pallas_call(
         functools.partial(next_sweep_kernel, protos_total),
-        in_specs=[whole(pltpu.HBM), whole(), whole(pltpu.HBM)],
+        in_specs=[whole(pl.ANY), whole(), whole(pl.ANY)],
         out_specs=whole(),
         out_shape=jax.ShapeDtypeStruct((copies, 1, crops_total), jnp.float32),
         scratch_shapes=[
-            pltpu.VMEM((thin // chunk, tiles, chunk, lanes), jnp.bfloat16),
+            pltpu.VMEM((thin // chunk, chunk, crops_total), jnp.bfloat16),
             pltpu.VMEM((1, crops_total), jnp.float32),
             pltpu.VMEM((16, chunk), jnp.bfloat16),
             pltpu.VMEM((16, crops_total), jnp.float32),
@@ -445,15 +461,15 @@
         compiler_params=params(16 if crops_total <= 2048 else 50),
         cost_estimate=cost(8 * thin * crops_total, 2 * thin * crops_total),
         name="next_sweep",
-    )(weights, parts, order)
+    )(in_hbm(weights), parts, order)
 
 
 def last_scales_kernel(
     protos_total, weights_hbm, parts_ref, order_ref, copies_ref, weights_ref, scale_ref, out_ref, sems,
 ):
-    steps, tiles, chunk, lanes = weights_ref.shape
+    steps, chunk, crops_total = weights_ref.shape
     arrived = fetch_rows(weights_hbm, weights_ref, sems)
-    scale_ref[...] = 1.0 / (tiles * lanes * jnp.sum(parts_ref[...], axis=0))
+    scale_ref[...] = 1.0 / (crops_total * jnp.sum(parts_ref[...], axis=0))
 
     def weigh(index, carry):
         arrived(index)
@@ -467,16 +483,15 @@
 
 
 def last_scales(weights, parts, order, copies, protos_total):
-    tiles, thin, lanes = weights.shape
-    crops_total = parts.shape[2]
+    thin, crops_total = weights.shape
     chunk = min(thin, 256)
     return pl.pallas_call(
         functools.partial(last_scales_kernel, protos_total),
-        in_specs=[whole(pltpu.HBM), whole(), whole(pltpu.HBM)],
+        in_specs=[whole(pl.ANY), whole(), whole(pl.ANY)],
         out_specs=whole(),
         out_shape=jax.ShapeDtypeStruct((copies, 1, thin), jnp.float32),
         scratch_shapes=[
-            pltpu.VMEM((thin // chunk, tiles, chunk, lanes), jnp.bfloat16),
+            pltpu.VMEM((thin // chunk, chunk, crops_total), jnp.bfloat16),
             pltpu.VMEM((1, crops_total), jnp.float32),
             pltpu.VMEM((1, thin), jnp.float32),
             pltpu.SemaphoreType.DMA((thin // chunk,)),
@@ -484,7 +499,7 @@
         compiler_params=params(16 if crops_total <= 2048 else 50),
         cost_estimate=cost(4 * thin * crops_total, 2 * thin * crops_total),
         name="last_scales",
-    )(weights, parts, order)
+    )(in_hbm(weights), parts, order)
 
 
 def student_front_kernel(
@@ -521,7 +536,7 @@
     hidden, units = second.shape
     return pl.pallas_call(
         student_front_kernel,
-        in_specs=[whole(pltpu.SMEM), whole()] + [whole(pltpu.HBM)] * 6,
+        in_specs=[whole(pltpu.SMEM), whole()] + [whole(pl.ANY)] * 6,
         out_specs=[whole(), whole()],
         out_shape=[jax.ShapeDtypeStruct((2 * share, units), jnp.float32)] * 2,
         scratch_shapes=[
@@ -533,7 +548,7 @@
         compiler_params=params(16),
         cost_estimate=cost(8 * share * hidden * (features + units), 2 * hidden * (features + units)),
         name="student_front",
-    )(index, bias.reshape(1, -1), *rows, first, second)
+    )(index, in_hbm(bias.reshape(1, -1)), in_hbm(rows[0]), *rows[1:], in_hbm(first), in_hbm(second))
 
 
 def student_middle_kernel(
@@ -573,7 +588,7 @@
         compiler_params=params(12),
         cost_estimate=cost(2 * share * units * width, 2 * units * width + 16 * share * units),
         name="student_middle",
-    )(index, keep, core_rows, x_rows, bias.reshape(1, -1), *weights, last_bias.reshape(1, -1))
+    )(index, keep, core_rows, x_rows, in_hbm(bias.reshape(1, -1)), in_hbm(weights[0]), *weights[1:], in_hbm(last_bias.reshape(1, -1)))
 
 
 def finish_kernel(unit_ref, lengths_ref, *rest):
@@ -615,6 +630,27 @@
     return lax.ppermute(values, axis, [(i, i ^ flip) for i in range(lax.axis_size(axis))])
 
 
+def bit_reversed(values, count):
+    bits = count.bit_length() - 1
+    split = values.reshape((2,) * bits + values.shape[1:])
+    turned = jnp.transpose(split, tuple(reversed(range(bits))) + tuple(range(bits, split.ndim)))
+    return turned.reshape(values.shape)
+
+
+def gather_batch(values):
+    step = lax.axis_size("batch") // 2
+    stages = [values]
+    while step:
+        other = swap(values, "batch", step)
+        upper = (lax.axis_index("batch") // step) % 2
+        values = jnp.where(
+            upper == 0, jnp.concatenate([values, other]), jnp.concatenate([other, values])
+        )
+        stages.append(values)
+        step //= 2
+    return stages
+
+
 def send_blocks(blocks):
     return [blocks[0]] + [swap(block, "proto", flip) for flip, block in enumerate(blocks) if flip]
 
@@ -640,22 +676,24 @@
     thin_ref = jnp.stack([batch_index, core])
     wide_ref = jnp.stack([batch_index, proto_index])
 
-    crops_x = swap(crops, "proto", 2)
-    own_unit, halves = teacher_units(core.reshape(1), teacher_emb, batch_size)
-    mine = all_to_all(halves, "batch").reshape(crops_total // 2, width)
+    own_unit, half = teacher_units(core.reshape(1), teacher_emb)
+    stages = gather_batch(half)
+    mine = stages[-1]
     other = swap(mine, "proto", 1)
-    all_tops = all_to_all(wide_tops(own_unit, protos, crops_x, devices, 8), BOTH)
+    top = jnp.full((256, 128), -jnp.inf, jnp.float32)
+    top = wide_tops(own_unit, protos, top, stages[1], 0, 0, count // 2, 4)
+    top_copies = wide_tops(own_unit, protos, top, stages[2], devices, count // 2, count // 2, 4)
+    all_tops = all_to_all(top_copies, BOTH)
     tops = jnp.max(all_tops.reshape(batch_size, proto_size, 256)[:, :, :group_rows], axis=1)
-    tops = jnp.transpose(tops.reshape(batch_size, 2, group_rows // 2), (1, 0, 2))
-    base = tops.reshape(1, crops_total) * -teacher_rate
-
-    rows = [crops, crops_x, swap(crops, "proto", 1), swap(crops_x, "proto", 1)]
+    tops = bit_reversed(tops, batch_size).reshape(batch_size, 2, group_rows // 2)
+    base = jnp.transpose(tops, (1, 0, 2)).reshape(1, crops_total) * -teacher_rate
+
+    rows = [crops, swap(crops, "proto", 2), swap(crops, "proto", 1), swap(crops, "proto", 3)]
     keep, give = student_front(proto_ref, b_first, rows, w_first, w_second)
     core_rows = swap(give, "proto", 1)
     x_sent = keep[share_rows:] + core_rows[share_rows:]
     x_rows = swap(x_sent, "proto", 2)
-    third_x = swap(w_third, "proto", 2)
-    thirds = [w_third, third_x, swap(w_third, "proto", 1), swap(third_x, "proto", 1)]
+    thirds = [w_third, swap(w_third, "proto", 2), swap(w_third, "proto", 1), swap(w_third, "proto", 3)]
     unit, rounded, lengths = student_middle(
         proto_ref, keep, core_rows, x_rows, b_second, thirds, b_third
     )

time: 142 us -> 120 us (0.85)
  local copies, waits for them, and re-layouts: 30.8 us -> 0.27 us
  blocking collectives: 13.2 us -> 0 us
  starting transfers between devices: 26 us -> 36.6 us
  Pallas kernels: 42.6 us -> 48.9 us
  waiting for transfers between devices: 27.6 us -> 32.6 us
    unnamed x34 -> x4, local copies, waits for them, and re-layouts: 30.6 us -> 0.01 us
    all_to_all x1 -> x0, blocking collectives: 13.2 us -> none  [all_to_all(): return lax.all_to_all(copies, axes, 0, 0, tiled=True)]
    ppermute x17 -> x20, waiting for transfers between devices: 11.9 us -> 24.7 us  [swap(): lax.ppermute(values, axis, [(i, i ^ flip) for i in range(lax.axis_size(ax...]
    ppermute x17 -> x20, starting transfers between devices: 11.2 us -> 19.2 us  [swap(): lax.ppermute(values, axis, [(i, i ^ flip) for i in range(lax.axis_size(ax...]
    all_to_all x4, waiting for transfers between devices: 15.7 us -> 7.87 us  [all_to_all(): return lax.all_to_all(copies, axes, 0, 0, tiled=True)]
    all_to_all x4, starting transfers between devices: 14.7 us -> 17.4 us  [all_to_all(): return lax.all_to_all(copies, axes, 0, 0, tiled=True)]
    pallas_call x2 -> x3, Pallas kernels: 12.1 us -> 14.1 us  [the longest x2 7.32 us: wide_tops(): pl.pallas_call(functools.partial(wide_tops_kernel, first_row, copies > 0)...]
    pallas_call x2, Pallas kernels: 8.29 us -> 10.1 us  [attract(): pl.pallas_call(functools.partial(attract_kernel, first_row, outputs > 1),...]
  transfers between devices with their start and end apart: 21 -> 24, of which waited for: 9 -> 11; matrix products, arithmetic and copies ran while one was open for 0% -> 1% of each run, Pallas kernels for 26% -> 36%
where the time goes in v7:
time: 120 us; the launch traced here: 119 us
  Pallas kernels  48.9 us (41%)
  starting transfers between devices  36.6 us (30%)
  waiting for transfers between devices  32.6 us (27%)
    ppermute x20, waiting for transfers between devices, swap(): lax.ppermute(values, axis, [(i, i ^ flip) for i in range(lax.axis_size(ax...  24.7 us
    ppermute x20, starting transfers between devices, swap(): lax.ppermute(values, axis, [(i, i ^ flip) for i in range(lax.axis_size(ax...  19.2 us
    all_to_all x4, starting transfers between devices, all_to_all(): return lax.all_to_all(copies, axes, 0, 0, tiled=True)  17.4 us
    pallas_call x2, Pallas kernels, attract(): pl.pallas_call(functools.partial(attract_kernel, first_row, outputs > 1),...  10.1 us
    pallas_call x1, Pallas kernels, repel(): pl.pallas_call(functools.partial(repel_kernel, proto_size), in_specs=[who...  9.31 us
    all_to_all x4, waiting for transfers between devices, all_to_all(): return lax.all_to_all(copies, axes, 0, 0, tiled=True)  7.87 us
    pallas_call x2, Pallas kernels, wide_tops(): pl.pallas_call(functools.partial(wide_tops_kernel, first_row, copies > 0)...  7.32 us
    pallas_call x1, Pallas kernels, first_sweep(): pl.pallas_call(functools.partial(first_sweep_kernel, chunk, protos_total)...  6.74 us
  transfers between devices with their start and end apart: 24, of which 11 were waited for; matrix products, arithmetic and copies ran while one was open for 1% of the time, Pallas kernels for 36%

profile of v7, /device:TPU:0, one launch (start us, length us, event | category | flops | bytes accessed | tf_op | source)
XLA Modules:
  0.0 119.2 jit_solution(2904228133732784885)
XLA Ops:
  0.0 1.0 teacher_units.1
  1.0 4.1 %collective-permute-start.13 = (bf16[96,256]{1,0:T(8,128)(2,1)S(1)}, bf16[96,256]{1,0:T(8,128)(2,1)S(1)}, u32[]{:S(2)}, u32[]{:S(2)}) collective-permute-start(bf16[96,256]{1,0:T(8,128)(2,1)S(1)} %get-tuple-element.32), channel_id=1, source_target_pairs={{0,16},{4,20},{8,24},{12,28},{16,0},{20,4},{24,8},{28,12},{1,17},{... | collective-permute-start | bytes 147464 | tf_op jit(solution)/shard_map/ppermute | solution.py:630
  5.1 0.0 collective-permute-start.1
  5.1 1.5 %collective-permute-start = (bf16[48,1536]{1,0:T(8,128)(2,1)}, bf16[48,1536]{1,0:T(8,128)(2,1)S(1)}, u32[]{:S(2)}, u32[]{:S(2)}) collective-permute-start(bf16[48,1536]{1,0:T(8,128)(2,1)} %own_hbm.1), channel_id=1, source_target_pairs={{0,2},{1,3},{2,0},{3,1},{4,6},{5,7},{6,4},{7,5},{8,10},{9,11},{10,... | collective-permute-start | bytes 442376 | tf_op jit(solution)/shard_map/ppermute | solution.py:630
  6.6 0.4 collective-permute-start.2
  7.0 0.7 collective-permute-done.13
  7.8 1.4 %collective-permute-start.14 = (bf16[192,256]{1,0:T(8,128)(2,1)S(1)}, bf16[192,256]{1,0:T(8,128)(2,1)S(1)}, u32[]{:S(2)}, u32[]{:S(2)}) collective-permute-start(bf16[192,256]{1,0:T(8,128)(2,1)S(1)} %maximum_select_fusion.2.order_ref), channel_id=1, source_target_pairs={{0,8},{4,12},{8,0},{12,4},{16,24},{20,28},{24,16},{28,20},{1,9},{5... | collective-permute-start | bytes 294920 | tf_op jit(solution)/shard_map/ppermute | solution.py:630
  9.2 0.0 collective-permute-done.1.core_hbm
  9.2 2.8 %collective-permute-done.x_hbm = bf16[48,1536]{1,0:T(8,128)(2,1)S(1)} collective-permute-done((bf16[48,1536]{1,0:T(8,128)(2,1)}, bf16[48,1536]{1,0:T(8,128)(2,1)S(1)}, u32[]{:S(2)}, u32[]{:S(2)}) %collective-permute-start) | collective-permute-done | bytes 147488 | tf_op jit(solution)/shard_map/ppermute | solution.py:630
  12.0 2.4 %collective-permute-done.2.last_hbm = bf16[48,1536]{1,0:T(8,128)(2,1)S(1)} collective-permute-done((bf16[48,1536]{1,0:T(8,128)(2,1)}, bf16[48,1536]{1,0:T(8,128)(2,1)S(1)}, u32[]{:S(2)}, u32[]{:S(2)}) %collective-permute-start.2) | collective-permute-done | bytes 147488 | tf_op jit(solution)/shard_map/ppermute | solution.py:630
  14.4 3.9 %student_front.1 = (f32[96,2048]{1,0:T(8,128)S(1)}, f32[96,2048]{1,0:T(8,128)S(1)}) custom-call(s32[1]{0:T(128)} %bitcast.index_ref, f32[1,2048]{1,0:T(1,128)} %bitcast.10, bf16[48,1536]{1,0:T(8,128)(2,1)} %own_hbm.1, bf16[48,1536]{1,0:T(8,128)(2,1)S(1)} %collective-permute-done.x_hbm, bf16[48,1536]{1,0:T(8,128)(2,1)S(1)} %collective-permute-done.1.core_hbm, ...), custom_call_target="tpu_custom_call" | custom-call | flops 704643072 | bytes 3670016 | tf_op jit(solution)/shard_map/student_front/pallas_call | solution.py:537
  18.3 0.3 collective-permute-start.3
  18.6 3.3 %wide_tops.2.before_ref = f32[256,128]{1,0:T(8,128)S(1)} custom-call(bf16[192,256]{1,0:T(8,128)(2,1)S(1)} %get-tuple-element.31.unit_ref, bf16[16384,256]{1,0:T(8,128)(2,1)} %protos_hbm.11, f32[256,128]{1,0:T(8,128)S(1)} %broadcast_in_dim.8.before_ref, bf16[192,256]{1,0:T(8,128)(2,1)S(1)} %maximum_select_fusion.2.order_ref), custom_call_target="tpu_custom_call" | custom-call | flops 805306368 | bytes 4194304 | tf_op jit(solution)/shard_map/wide_tops/pallas_call | solution.py:128
  21.9 0.0 collective-permute-done.14
  21.9 0.1 maximum_select_fusion.1.order_ref
  22.0 4.0 %wide_tops.3 = f32[32,1,256]{2,1,0:T(1,128)} custom-call(bf16[192,256]{1,0:T(8,128)(2,1)S(1)} %get-tuple-element.31.unit_ref, bf16[16384,256]{1,0:T(8,128)(2,1)} %protos_hbm.11, f32[256,128]{1,0:T(8,128)S(1)} %wide_tops.2.before_ref, bf16[384,256]{1,0:T(8,128)(2,1)S(1)} %maximum_select_fusion.1.order_ref), custom_call_target="tpu_custom_call" | custom-call | flops 805306368 | bytes 4194304 | tf_op jit(solution)/shard_map/wide_tops/pallas_call | solution.py:128
  26.0 0.0 copy-start
  26.0 3.9 %all-to-all-start = ((f32[32,1,256]{2,1,0:T(1,128)}), f32[32,1,256]{2,1,0:T(1,128)S(1)}, u32[]{:S(2)}, u32[]{:S(2)}) async-start(f32[32,1,256]{2,1,0:T(1,128)} %wide_tops.3), calls=%async_computation | async-start | bytes 65536 | tf_op jit(solution)/shard_map/all_to_all | solution.py:659
  30.0 0.1 pad_add_fusion.1.index_ref
  30.0 1.8 %collective-permute-start.15 = (bf16[384,256]{1,0:T(8,128)(2,1)S(1)}, bf16[384,256]{1,0:T(8,128)(2,1)S(1)}, u32[]{:S(2)}, u32[]{:S(2)}) collective-permute-start(bf16[384,256]{1,0:T(8,128)(2,1)S(1)} %maximum_select_fusion.1.order_ref), channel_id=1, source_target_pairs={{0,4},{4,0},{8,12},{12,8},{16,20},{20,16},{24,28},{28,24},{1,5},{5... | collective-permute-start | bytes 589832 | tf_op jit(solution)/shard_map/ppermute | solution.py:630
  31.8 5.4 %all-to-all-done.tops_ref = f32[32,1,256]{2,1,0:T(1,128)S(1)} async-done(((f32[32,1,256]{2,1,0:T(1,128)}), f32[32,1,256]{2,1,0:T(1,128)S(1)}, u32[]{:S(2)}, u32[]{:S(2)}) %all-to-all-start) | async-done | bytes 32800 | tf_op jit(solution)/shard_map/all_to_all | solution.py:659
  37.2 0.1 reduce
  37.4 0.1 mul.17
  37.5 0.1 mul.19.bias_ref
  37.6 0.0 collective-permute-done.15
  37.6 0.2 maximum_select_fusion.mine_hbm
  37.7 0.2 collective-permute-start.16
  37.9 0.0 collective-permute-done.3.core_ref
  37.9 1.5 %collective-permute-start.4 = (f32[48,2048]{1,0:T(8,128)S(1)}, f32[48,2048]{1,0:T(8,128)S(1)}, u32[]{:S(2)}, u32[]{:S(2)}) collective-permute-start(f32[48,2048]{1,0:T(8,128)S(1)} %slice_add_fusion.order_ref), channel_id=1, source_target_pairs={{0,2},{1,3},{2,0},{3,1},{4,6},{5,7},{6,4},{7,5},{8,10},{9,11},{10,... | collective-permute-start | bytes 1179656 | tf_op jit(solution)/shard_map/ppermute | solution.py:630
  39.4 0.1 collective-permute-done.16.other_hbm
  39.5 6.7 %first_sweep.1 = (f32[32,1,1536]{2,1,0:T(1,128)}, bf16[2048,1536]{1,0:T(8,128)(2,1)}) custom-call(s32[2]{0:T(128)S(1)} %pad_add_fusion.1.index_ref, bf16[16384,256]{1,0:T(8,128)(2,1)} %protos_hbm.11, bf16[768,256]{1,0:T(8,128)(2,1)S(1)} %maximum_select_fusion.mine_hbm, bf16[768,256]{1,0:T(8,128)(2,1)S(1)} %collective-permute-done.16.other_hbm, ...), custom_call_target="tpu_custom_call" | custom-call | flops 1610612736 | bytes 6291456 | tf_op jit(solution)/shard_map/first_sweep/pallas_call | solution.py:365
  46.3 5.3 %all-to-all-start.1 = ((f32[32,1,1536]{2,1,0:T(1,128)}), f32[32,1,1536]{2,1,0:T(1,128)S(1)}, u32[]{:S(2)}, u32[]{:S(2)}) async-start(f32[32,1,1536]{2,1,0:T(1,128)} %get-tuple-element.34), calls=%async_computation.1 | async-start | bytes 393216 | tf_op jit(solution)/shard_map/all_to_all | solution.py:659
  51.5 0.3 collective-permute-start.6
  51.9 1.7 %collective-permute-start.5 = (bf16[512,256]{1,0:T(8,128)(2,1)S(1)}, bf16[512,256]{1,0:T(8,128)(2,1)S(1)}, u32[]{:S(2)}, u32[]{:S(2)}) collective-permute-start(bf16[512,256]{1,0:T(8,128)(2,1)S(1)} %copy-done), channel_id=1, source_target_pairs={{0,2},{1,3},{2,0},{3,1},{4,6},{5,7},{6,4},{7,5},{8,10},{9,11},{10,... | collective-permute-start | bytes 786440 | tf_op jit(solution)/shard_map/ppermute | solution.py:630
  53.5 0.0 collective-permute-start.7
  53.6 0.1 pad_add_fusion.index_ref
  53.6 0.0 collective-permute-done.6.other_ref
  53.6 9.0 %collective-permute-done.5.partner_ref = bf16[512,256]{1,0:T(8,128)(2,1)S(1)} collective-permute-done((bf16[512,256]{1,0:T(8,128)(2,1)S(1)}, bf16[512,256]{1,0:T(8,128)(2,1)S(1)}, u32[]{:S(2)}, u32[]{:S(2)}) %collective-permute-start.5) | collective-permute-done | bytes 262176 | tf_op jit(solution)/shard_map/ppermute | solution.py:630
  62.7 4.7 %collective-permute-done.7.last_ref = bf16[512,256]{1,0:T(8,128)(2,1)S(1)} collective-permute-done((bf16[512,256]{1,0:T(8,128)(2,1)S(1)}, bf16[512,256]{1,0:T(8,128)(2,1)S(1)}, u32[]{:S(2)}, u32[]{:S(2)}) %collective-permute-start.7) | collective-permute-done | bytes 262176 | tf_op jit(solution)/shard_map/ppermute | solution.py:630
  67.3 0.0 collective-permute-done.4.x_ref
  67.3 1.5 %student_middle.1 = (f32[48,256]{1,0:T(8,128)S(1)}, bf16[48,256]{1,0:T(8,128)(2,1)S(1)}, f32[48,128]{1,0:T(8,128)S(1)}) custom-call(s32[1]{0:T(128)} %bitcast.index_ref, f32[96,2048]{1,0:T(8,128)S(1)} %get-tuple-element.22.keep_ref, f32[96,2048]{1,0:T(8,128)S(1)} %collective-permute-done.3.core_ref, f32[48,2048]{1,0:T(8,128)S(1)} %collective-permute-done.4.x_ref, ...), custom_call_target="tpu_custom_call" | custom-call | flops 50331648 | bytes 2621440 | tf_op jit(solution)/shard_map/student_middle/pallas_call | solution.py:578
  68.9 1.5 %collective-permute-start.8 = (bf16[48,256]{1,0:T(8,128)(2,1)S(1)}, bf16[48,256]{1,0:T(8,128)(2,1)S(1)}, u32[]{:S(2)}, u32[]{:S(2)}) collective-permute-start(bf16[48,256]{1,0:T(8,128)(2,1)S(1)} %get-tuple-element.26.order_ref), channel_id=1, source_target_pairs={{0,2},{1,3},{2,0},{3,1},{4,6},{5,7},{6,4},{7,5},{8,10},{9,11},{10,... | collective-permute-start | bytes 73736 | tf_op jit(solution)/shard_map/ppermute | solution.py:630
  70.3 0.0 all-to-all-done.1.parts_ref
  70.3 4.4 %next_sweep.1 = f32[32,1,1536]{2,1,0:T(1,128)} custom-call(bf16[2048,1536]{1,0:T(8,128)(2,1)} %get-tuple-element.33.weights_hbm, f32[32,1,1536]{2,1,0:T(1,128)S(1)} %all-to-all-done.1.parts_ref, bf16[48,256]{1,0:T(8,128)(2,1)S(1)} %get-tuple-element.26.order_ref), custom_call_target="tpu_custom_call" | custom-call | flops 25165824 | bytes 6291456 | tf_op jit(solution)/shard_map/next_sweep/pallas_call | solution.py:449
  74.8 4.9 %all-to-all-start.2 = ((f32[32,1,1536]{2,1,0:T(1,128)}), f32[32,1,1536]{2,1,0:T(1,128)S(1)}, u32[]{:S(2)}, u32[]{:S(2)}) async-start(f32[32,1,1536]{2,1,0:T(1,128)} %next_sweep.1), calls=%async_computation.2 | async-start | bytes 393216 | tf_op jit(solution)/shard_map/all_to_all | solution.py:659
  79.6 0.0 collective-permute-done.8
  79.7 0.3 collective-permute-start.9
  80.0 1.0 collective-permute-done.9
  81.0 5.0 %attract.2.state_ref.order_ref = f32[192,512]{1,0:T(8,128)S(1)} custom-call(bf16[192,256]{1,0:T(8,128)(2,1)S(1)} %constant_dynamic-update-slice_fusion.emb_ref, f32[192,512]{1,0:T(8,128)S(1)} %concatenate.33.state_ref, bf16[16384,256]{1,0:T(8,128)(2,1)} %protos_hbm.11), custom_call_target="tpu_custom_call" | custom-call | flops 1610612736 | bytes 4194304 | tf_op jit(solution)/shard_map/attract/pallas_call | solution.py:270
  86.1 2.5 %all-to-all-done.2.parts_ref = f32[32,1,1536]{2,1,0:T(1,128)S(1)} async-done(((f32[32,1,1536]{2,1,0:T(1,128)}), f32[32,1,1536]{2,1,0:T(1,128)S(1)}, u32[]{:S(2)}, u32[]{:S(2)}) %all-to-all-start.2) | async-done | bytes 196640 | tf_op jit(solution)/shard_map/all_to_all | solution.py:659
  88.5 3.7 %last_scales.1 = f32[8,1,2048]{2,1,0:T(1,128)} custom-call(bf16[2048,1536]{1,0:T(8,128)(2,1)} %get-tuple-element.33.weights_hbm, f32[32,1,1536]{2,1,0:T(1,128)S(1)} %all-to-all-done.2.parts_ref, f32[192,512]{1,0:T(8,128)S(1)} %attract.2.state_ref.order_ref), custom_call_target="tpu_custom_call" | custom-call | flops 12582912 | bytes 6291456 | tf_op jit(solution)/shard_map/last_scales/pallas_call | solution.py:488
  92.3 3.4 %all-to-all-start.3 = ((f32[8,1,2048]{2,1,0:T(1,128)}), f32[8,1,2048]{2,1,0:T(1,128)S(1)}, u32[]{:S(2)}, u32[]{:S(2)}) async-start(f32[8,1,2048]{2,1,0:T(1,128)} %last_scales.1), calls=%async_computation.3 | async-start | bytes 131072 | tf_op jit(solution)/shard_map/all_to_all | solution.py:659
  95.7 5.1 %attract.3 = (f32[48,512]{1,0:T(8,128)S(1)}, f32[48,512]{1,0:T(8,128)S(1)}, f32[48,512]{1,0:T(8,128)S(1)}, f32[48,512]{1,0:T(8,128)S(1)}) custom-call(bf16[192,256]{1,0:T(8,128)(2,1)S(1)} %constant_dynamic-update-slice_fusion.emb_ref, f32[192,512]{1,0:T(8,128)S(1)} %attract.2.state_ref.order_ref, bf16[16384,256]{1,0:T(8,128)(2,1)} %protos_hbm.11), custom_call_target="tpu_custom_call" | custom-call | flops 1610612736 | bytes 4194304 | tf_op jit(solution)/shard_map/attract/pallas_call | solution.py:270
  100.8 0.6 collective-permute-start.10
  101.4 1.0 collective-permute-start.11
  102.4 0.5 collective-permute-start.12
  102.9 9.3 %repel.1 = (f32[48,384]{1,0:T(8,128)S(1)}, f32[48,384]{1,0:T(8,128)S(1)}, f32[48,384]{1,0:T(8,128)S(1)}, f32[48,384]{1,0:T(8,128)S(1)}) custom-call(s32[2]{0:T(128)S(1)} %pad_add_fusion.index_ref, bf16[192,256]{1,0:T(8,128)(2,1)S(1)} %get-tuple-element.31.unit_ref, f32[32,1,256]{2,1,0:T(1,128)S(1)} %all-to-all-done.tops_ref, ...), custom_call_target="tpu_custom_call" | custom-call | flops 3221225472 | bytes 8388608 | tf_op jit(solution)/shard_map/repel/pallas_call | solution.py:192
  112.2 0.8 collective-permute-start.17
  113.0 1.0 collective-permute-start.18
  114.0 0.0 collective-permute-done.10.rest_1_
  114.0 0.4 collective-permute-start.19
  114.4 3.4 %collective-permute-done.18.rest_6_ = f32[48,384]{1,0:T(8,128)S(1)} collective-permute-done((f32[48,384]{1,0:T(8,128)S(1)}, f32[48,384]{1,0:T(8,128)S(1)}, u32[]{:S(2)}, u32[]{:S(2)}) %collective-permute-start.18) | collective-permute-done | bytes 73760 | tf_op jit(solution)/shard_map/ppermute | solution.py:630
  117.8 0.7 collective-permute-done.19.rest_7_
  118.4 0.8 finish.1
  (21 shorter events, 0.2 us)
Async XLA Ops:
  1.0 6.7 %collective-permute-start.13 = (bf16[96,256]{1,0:T(8,128)(2,1)S(1)}, bf16[96,256]{1,0:T(8,128)(2,1)S(1)}, u32[]{:S(2)}, u32[]{:S(2)}) collective-permute-start(bf16[96,256]{1,0:T(8,128)(2,1)S(1)} %get-tuple-element.32), channel_id=1, source_target_pairs={{0,16},{4,20},{8,24},{12,28},{16,0},{20,4},{24,8},{28,12},{1,17},{... | collective-permute-start | bytes 147464 | tf_op jit(solution)/shard_map/ppermute | solution.py:630
  5.1 4.1 %collective-permute-start.1 = (bf16[48,1536]{1,0:T(8,128)(2,1)}, bf16[48,1536]{1,0:T(8,128)(2,1)S(1)}, u32[]{:S(2)}, u32[]{:S(2)}) collective-permute-start(bf16[48,1536]{1,0:T(8,128)(2,1)} %own_hbm.1), channel_id=1, source_target_pairs={{0,1},{1,0},{2,3},{3,2},{4,5},{5,4},{6,7},{7,6},{8,9},{9,8},{10,11... | collective-permute-start | bytes 442376 | tf_op jit(solution)/shard_map/ppermute | solution.py:630
  5.1 6.9 %collective-permute-start = (bf16[48,1536]{1,0:T(8,128)(2,1)}, bf16[48,1536]{1,0:T(8,128)(2,1)S(1)}, u32[]{:S(2)}, u32[]{:S(2)}) collective-permute-start(bf16[48,1536]{1,0:T(8,128)(2,1)} %own_hbm.1), channel_id=1, source_target_pairs={{0,2},{1,3},{2,0},{3,1},{4,6},{5,7},{6,4},{7,5},{8,10},{9,11},{10,... | collective-permute-start | bytes 442376 | tf_op jit(solution)/shard_map/ppermute | solution.py:630
  6.6 7.8 %collective-permute-start.2 = (bf16[48,1536]{1,0:T(8,128)(2,1)}, bf16[48,1536]{1,0:T(8,128)(2,1)S(1)}, u32[]{:S(2)}, u32[]{:S(2)}) collective-permute-start(bf16[48,1536]{1,0:T(8,128)(2,1)} %own_hbm.1), channel_id=1, source_target_pairs={{0,3},{1,2},{2,1},{3,0},{4,7},{5,6},{6,5},{7,4},{8,11},{9,10},{10,... | collective-permute-start | bytes 442376 | tf_op jit(solution)/shard_map/ppermute | solution.py:630
  7.8 14.2 %collective-permute-start.14 = (bf16[192,256]{1,0:T(8,128)(2,1)S(1)}, bf16[192,256]{1,0:T(8,128)(2,1)S(1)}, u32[]{:S(2)}, u32[]{:S(2)}) collective-permute-start(bf16[192,256]{1,0:T(8,128)(2,1)S(1)} %maximum_select_fusion.2.order_ref), channel_id=1, source_target_pairs={{0,8},{4,12},{8,0},{12,4},{16,24},{20,28},{24,16},{28,20},{1,9},{5... | collective-permute-start | bytes 294920 | tf_op jit(solution)/shard_map/ppermute | solution.py:630
  18.3 19.6 %collective-permute-start.3 = (f32[96,2048]{1,0:T(8,128)S(1)}, f32[96,2048]{1,0:T(8,128)S(1)}, u32[]{:S(2)}, u32[]{:S(2)}) collective-permute-start(f32[96,2048]{1,0:T(8,128)S(1)} %get-tuple-element.23), channel_id=1, source_target_pairs={{0,1},{1,0},{2,3},{3,2},{4,5},{5,4},{6,7},{7,6},{8,9},{9,8},{10,11... | collective-permute-start | bytes 2359304 | tf_op jit(solution)/shard_map/ppermute | solution.py:630
  26.0 25.5 %copy-start = (bf16[512,256]{1,0:T(8,128)(2,1)S(1)}, bf16[512,256]{1,0:T(8,128)(2,1)}, u32[]{:S(2)}) copy-start(bf16[512,256]{1,0:T(8,128)(2,1)} %own_ref.1) | copy-start | bytes 786436
  26.0 11.2 %all-to-all-start = ((f32[32,1,256]{2,1,0:T(1,128)}), f32[32,1,256]{2,1,0:T(1,128)S(1)}, u32[]{:S(2)}, u32[]{:S(2)}) async-start(f32[32,1,256]{2,1,0:T(1,128)} %wide_tops.3), calls=%async_computation | async-start | bytes 65536 | tf_op jit(solution)/shard_map/all_to_all | solution.py:659
  30.0 7.5 %collective-permute-start.15 = (bf16[384,256]{1,0:T(8,128)(2,1)S(1)}, bf16[384,256]{1,0:T(8,128)(2,1)S(1)}, u32[]{:S(2)}, u32[]{:S(2)}) collective-permute-start(bf16[384,256]{1,0:T(8,128)(2,1)S(1)} %maximum_select_fusion.1.order_ref), channel_id=1, source_target_pairs={{0,4},{4,0},{8,12},{12,8},{16,20},{20,16},{24,28},{28,24},{1,5},{5... | collective-permute-start | bytes 589832 | tf_op jit(solution)/shard_map/ppermute | solution.py:630
  37.7 1.8 %collective-permute-start.16 = (bf16[768,256]{1,0:T(8,128)(2,1)S(1)}, bf16[768,256]{1,0:T(8,128)(2,1)S(1)}, u32[]{:S(2)}, u32[]{:S(2)}) collective-permute-start(bf16[768,256]{1,0:T(8,128)(2,1)S(1)} %maximum_select_fusion.mine_hbm), channel_id=1, source_target_pairs={{0,1},{1,0},{2,3},{3,2},{4,5},{5,4},{6,7},{7,6},{8,9},{9,8},{10,11... | collective-permute-start | bytes 1179656 | tf_op jit(solution)/shard_map/ppermute | solution.py:630
  37.9 29.4 %collective-permute-start.4 = (f32[48,2048]{1,0:T(8,128)S(1)}, f32[48,2048]{1,0:T(8,128)S(1)}, u32[]{:S(2)}, u32[]{:S(2)}) collective-permute-start(f32[48,2048]{1,0:T(8,128)S(1)} %slice_add_fusion.order_ref), channel_id=1, source_target_pairs={{0,2},{1,3},{2,0},{3,1},{4,6},{5,7},{6,4},{7,5},{8,10},{9,11},{10,... | collective-permute-start | bytes 1179656 | tf_op jit(solution)/shard_map/ppermute | solution.py:630
  46.3 24.1 %all-to-all-start.1 = ((f32[32,1,1536]{2,1,0:T(1,128)}), f32[32,1,1536]{2,1,0:T(1,128)S(1)}, u32[]{:S(2)}, u32[]{:S(2)}) async-start(f32[32,1,1536]{2,1,0:T(1,128)} %get-tuple-element.34), calls=%async_computation.1 | async-start | bytes 393216 | tf_op jit(solution)/shard_map/all_to_all | solution.py:659
  51.5 2.1 %collective-permute-start.6 = (bf16[512,256]{1,0:T(8,128)(2,1)S(1)}, bf16[512,256]{1,0:T(8,128)(2,1)S(1)}, u32[]{:S(2)}, u32[]{:S(2)}) collective-permute-start(bf16[512,256]{1,0:T(8,128)(2,1)S(1)} %copy-done), channel_id=1, source_target_pairs={{0,1},{1,0},{2,3},{3,2},{4,5},{5,4},{6,7},{7,6},{8,9},{9,8},{10,11... | collective-permute-start | bytes 786440 | tf_op jit(solution)/shard_map/ppermute | solution.py:630
  51.9 10.8 %collective-permute-start.5 = (bf16[512,256]{1,0:T(8,128)(2,1)S(1)}, bf16[512,256]{1,0:T(8,128)(2,1)S(1)}, u32[]{:S(2)}, u32[]{:S(2)}) collective-permute-start(bf16[512,256]{1,0:T(8,128)(2,1)S(1)} %copy-done), channel_id=1, source_target_pairs={{0,2},{1,3},{2,0},{3,1},{4,6},{5,7},{6,4},{7,5},{8,10},{9,11},{10,... | collective-permute-start | bytes 786440 | tf_op jit(solution)/shard_map/ppermute | solution.py:630
  53.5 13.8 %collective-permute-start.7 = (bf16[512,256]{1,0:T(8,128)(2,1)S(1)}, bf16[512,256]{1,0:T(8,128)(2,1)S(1)}, u32[]{:S(2)}, u32[]{:S(2)}) collective-permute-start(bf16[512,256]{1,0:T(8,128)(2,1)S(1)} %copy-done), channel_id=1, source_target_pairs={{0,3},{1,2},{2,1},{3,0},{4,7},{5,6},{6,5},{7,4},{8,11},{9,10},{10,... | collective-permute-start | bytes 786440 | tf_op jit(solution)/shard_map/ppermute | solution.py:630
  68.9 10.8 %collective-permute-start.8 = (bf16[48,256]{1,0:T(8,128)(2,1)S(1)}, bf16[48,256]{1,0:T(8,128)(2,1)S(1)}, u32[]{:S(2)}, u32[]{:S(2)}) collective-permute-start(bf16[48,256]{1,0:T(8,128)(2,1)S(1)} %get-tuple-element.26.order_ref), channel_id=1, source_target_pairs={{0,2},{1,3},{2,0},{3,1},{4,6},{5,7},{6,4},{7,5},{8,10},{9,11},{10,... | collective-permute-start | bytes 73736 | tf_op jit(solution)/shard_map/ppermute | solution.py:630
  74.8 13.8 %all-to-all-start.2 = ((f32[32,1,1536]{2,1,0:T(1,128)}), f32[32,1,1536]{2,1,0:T(1,128)S(1)}, u32[]{:S(2)}, u32[]{:S(2)}) async-start(f32[32,1,1536]{2,1,0:T(1,128)} %next_sweep.1), calls=%async_computation.2 | async-start | bytes 393216 | tf_op jit(solution)/shard_map/all_to_all | solution.py:659
  79.7 1.3 %collective-permute-start.9 = (bf16[96,256]{1,0:T(8,128)(2,1)S(1)}, bf16[96,256]{1,0:T(8,128)(2,1)S(1)}, u32[]{:S(2)}, u32[]{:S(2)}) collective-permute-start(bf16[96,256]{1,0:T(8,128)(2,1)S(1)} %pad_maximum_fusion), channel_id=1, source_target_pairs={{0,1},{1,0},{2,3},{3,2},{4,5},{5,4},{6,7},{7,6},{8,9},{9,8},{10,11... | collective-permute-start | bytes 147464 | tf_op jit(solution)/shard_map/ppermute | solution.py:630
  92.3 10.6 %all-to-all-start.3 = ((f32[8,1,2048]{2,1,0:T(1,128)}), f32[8,1,2048]{2,1,0:T(1,128)S(1)}, u32[]{:S(2)}, u32[]{:S(2)}) async-start(f32[8,1,2048]{2,1,0:T(1,128)} %last_scales.1), calls=%async_computation.3 | async-start | bytes 131072 | tf_op jit(solution)/shard_map/all_to_all | solution.py:659
  100.8 13.2 %collective-permute-start.10 = (f32[48,512]{1,0:T(8,128)S(1)}, f32[48,512]{1,0:T(8,128)S(1)}, u32[]{:S(2)}, u32[]{:S(2)}) collective-permute-start(f32[48,512]{1,0:T(8,128)S(1)} %get-tuple-element.28), channel_id=1, source_target_pairs={{0,1},{1,0},{2,3},{3,2},{4,5},{5,4},{6,7},{7,6},{8,9},{9,8},{10,11... | collective-permute-start | bytes 294920 | tf_op jit(solution)/shard_map/ppermute | solution.py:630
  101.4 13.0 %collective-permute-start.11 = (f32[48,512]{1,0:T(8,128)S(1)}, f32[48,512]{1,0:T(8,128)S(1)}, u32[]{:S(2)}, u32[]{:S(2)}) collective-permute-start(f32[48,512]{1,0:T(8,128)S(1)} %get-tuple-element.29), channel_id=1, source_target_pairs={{0,2},{1,3},{2,0},{3,1},{4,6},{5,7},{6,4},{7,5},{8,10},{9,11},{10,... | collective-permute-start | bytes 294920 | tf_op jit(solution)/shard_map/ppermute | solution.py:630
  102.4 12.0 %collective-permute-start.12 = (f32[48,512]{1,0:T(8,128)S(1)}, f32[48,512]{1,0:T(8,128)S(1)}, u32[]{:S(2)}, u32[]{:S(2)}) collective-permute-start(f32[48,512]{1,0:T(8,128)S(1)} %get-tuple-element.30), channel_id=1, source_target_pairs={{0,3},{1,2},{2,1},{3,0},{4,7},{5,6},{6,5},{7,4},{8,11},{9,10},{10,... | collective-permute-start | bytes 294920 | tf_op jit(solution)/shard_map/ppermute | solution.py:630
  112.2 2.2 %collective-permute-start.17 = (f32[48,384]{1,0:T(8,128)S(1)}, f32[48,384]{1,0:T(8,128)S(1)}, u32[]{:S(2)}, u32[]{:S(2)}) collective-permute-start(f32[48,384]{1,0:T(8,128)S(1)} %get-tuple-element.36), channel_id=1, source_target_pairs={{0,1},{1,0},{2,3},{3,2},{4,5},{5,4},{6,7},{7,6},{8,9},{9,8},{10,11... | collective-permute-start | bytes 221192 | tf_op jit(solution)/shard_map/ppermute | solution.py:630
  113.0 4.8 %collective-permute-start.18 = (f32[48,384]{1,0:T(8,128)S(1)}, f32[48,384]{1,0:T(8,128)S(1)}, u32[]{:S(2)}, u32[]{:S(2)}) collective-permute-start(f32[48,384]{1,0:T(8,128)S(1)} %get-tuple-element.37), channel_id=1, source_target_pairs={{0,2},{1,3},{2,0},{3,1},{4,6},{5,7},{6,4},{7,5},{8,10},{9,11},{10,... | collective-permute-start | bytes 221192 | tf_op jit(solution)/shard_map/ppermute | solution.py:630
  114.0 4.5 %collective-permute-start.19 = (f32[48,384]{1,0:T(8,128)S(1)}, f32[48,384]{1,0:T(8,128)S(1)}, u32[]{:S(2)}, u32[]{:S(2)}) collective-permute-start(f32[48,384]{1,0:T(8,128)S(1)} %get-tuple-element.38), channel_id=1, source_target_pairs={{0,3},{1,2},{2,1},{3,0},{4,7},{5,6},{6,5},{7,4},{8,11},{9,10},{10,... | collective-permute-start | bytes 221192 | tf_op jit(solution)/shard_map/ppermute | solution.py:630

commit v8 on v7

--- a/solution.py
+++ b/solution.py
@@ -19,6 +19,7 @@
 MIB = 1024 * 1024
 BOTH = ("batch", "proto")
 TILE = 256
+WIDE = 512
 
 
 def scores(left_rows, right_rows):
@@ -42,6 +43,13 @@
 
 def in_hbm(array):
     return pltpu.with_memory_space_constraint(array, pltpu.HBM)
+
+
+def skipping(kernel, first, count):
+    def trimmed(*refs):
+        kernel(*refs[:first], *refs[first + count :])
+
+    return trimmed
 
 
 def part(index, size):
@@ -99,17 +107,18 @@
     )(core, in_hbm(teacher_emb))
 
 
-def wide_tops_kernel(first_row, last, unit_ref, protos_hbm, before_ref, order_ref, out_ref, protos_ref, sems, top_ref):
+def wide_tops_kernel(first_row, last, unit_ref, protos_hbm, before_ref, out_ref, protos_ref, sems, top_ref):
     rows = unit_ref.shape[0]
     steps, block = protos_ref.shape[:2]
+    wide = min(WIDE, block)
     arrived = fetch(protos_hbm, protos_ref, sems, first_row)
     top_ref[...] = before_ref[...]
 
     def step(index, carry):
         arrived(index)
         top = top_ref[:rows, :]
-        for start in range(0, block, TILE):
-            products = scores(unit_ref[...], protos_ref[index, start : start + TILE, :])
+        for start in range(0, block, wide):
+            products = scores(unit_ref[...], protos_ref[index, start : start + wide, :])
             top = jnp.maximum(top, lane_fold(products, jnp.maximum))
         top_ref[:rows, :] = top
         return carry
@@ -126,8 +135,8 @@
     rows, width = unit.shape
     shape = (copies, 1, 256) if copies else before.shape
     return pl.pallas_call(
-        functools.partial(wide_tops_kernel, first_row, copies > 0),
-        in_specs=[whole(), whole(pl.ANY), whole(), whole(pl.ANY)],
+        skipping(functools.partial(wide_tops_kernel, first_row, copies > 0), 3, len(order)),
+        in_specs=[whole(), whole(pl.ANY), whole()] + [whole(pl.ANY)] * len(order),
         out_specs=whole(),
         out_shape=jax.ShapeDtypeStruct(shape, jnp.float32),
         scratch_shapes=[
@@ -138,13 +147,14 @@
         compiler_params=params(16),
         cost_estimate=cost(2 * rows * width * count, 2 * width * count),
         name="wide_tops",
-    )(unit, in_hbm(protos), before, order)
-
-
-def repel_kernel(group, index_ref, unit_ref, tops_ref, scale_ref, protos_hbm, order_ref, *rest):
+    )(unit, in_hbm(protos), before, *order)
+
+
+def repel_kernel(group, index_ref, unit_ref, tops_ref, scale_ref, protos_hbm, *rest):
     out_refs, (protos_ref, sems, acc_ref, sum_ref, bias_ref) = rest[:-5], rest[-5:]
     rows, width = unit_ref.shape
     steps, block = protos_ref.shape[:2]
+    wide = min(WIDE, block)
     arrived = fetch(protos_hbm, protos_ref, sems)
     first = index_ref[0] * group
     top = tops_ref[first]
@@ -159,11 +169,11 @@
         bias = bias_ref[...]
         total = sum_ref[...]
         acc = acc_ref[...]
-        for start in range(0, block, TILE):
-            protos = protos_ref[index, start : start + TILE, :]
+        for start in range(0, block, wide):
+            protos = protos_ref[index, start : start + wide, :]
             products = scores(unit_ref[...], protos)
             pieces = []
-            for lane in range(0, TILE, 128):
+            for lane in range(0, wide, 128):
                 scaled = jnp.exp2(products[:, lane : lane + 128] * teacher_rate + bias)
                 scaled = scaled * scale_ref[index, :, start + lane : start + lane + 128]
                 total = total + scaled
@@ -190,8 +200,8 @@
     count = protos.shape[0]
     steps, _, block = scale.shape
     return pl.pallas_call(
-        functools.partial(repel_kernel, proto_size),
-        in_specs=[whole(pltpu.SMEM), whole(), whole(), whole(), whole(pl.ANY), whole(pl.ANY)],
+        skipping(functools.partial(repel_kernel, proto_size), 5, len(order)),
+        in_specs=[whole(pltpu.SMEM), whole(), whole(), whole(), whole(pl.ANY)] + [whole(pl.ANY)] * len(order),
         out_specs=[whole()] * proto_size,
         out_shape=[jax.ShapeDtypeStruct((rows // proto_size, width + 128), jnp.float32)] * proto_size,
         scratch_shapes=[
@@ -204,7 +214,7 @@
         compiler_params=params(16),
         cost_estimate=cost(4 * rows * width * count, 2 * width * count, rows * count),
         name="repel",
-    )(index, unit, tops, scale, in_hbm(protos), order)
+    )(index, unit, tops, scale, in_hbm(protos), *order)
 
 
 def attract_kernel(first_row, last, emb_ref, state_ref, protos_hbm, *rest):
@@ -307,8 +317,7 @@
 
 
 def first_sweep_kernel(
-    chunk, protos_total, index_ref, protos_hbm, mine_hbm, other_hbm, bias_ref, order_ref,
-    copies_ref, weights_hbm, protos_ref, units_ref, weights_ref, rounded_ref, scale_ref, sems, out_sems,
+    chunk, protos_total, index_ref, protos_hbm, mine_hbm, other_hbm, bias_ref, copies_ref, weights_hbm, protos_ref, units_ref, weights_ref, rounded_ref, scale_ref, sems, out_sems,
 ):
     thin, crops_total = weights_ref.shape
     half = mine_hbm.shape[0]
@@ -361,10 +370,11 @@
 def first_sweep(index, protos, mine, other, base, order, copies, thin, protos_total):
     width = protos.shape[1]
     crops_total = 2 * mine.shape[0]
-    chunk = min(thin, 512)
-    return pl.pallas_call(
-        functools.partial(first_sweep_kernel, chunk, protos_total),
-        in_specs=[whole(pltpu.SMEM), whole(pl.ANY), whole(pl.ANY), whole(pl.ANY), whole(), whole(pl.ANY)],
+    chunk = min(thin, 1024)
+    return pl.pallas_call(
+        skipping(functools.partial(first_sweep_kernel, chunk, protos_total), 5, len(order)),
+        in_specs=[whole(pltpu.SMEM), whole(pl.ANY), whole(pl.ANY), whole(pl.ANY), whole()]
+        + [whole(pl.ANY)] * len(order),
         out_specs=[whole(), whole(pl.ANY)],
         out_shape=[
             jax.ShapeDtypeStruct((copies, 1, crops_total), jnp.float32),
@@ -382,7 +392,7 @@
         compiler_params=params(32 if crops_total <= 2048 else 56),
         cost_estimate=cost(2 * thin * width * crops_total, 2 * thin * crops_total, thin * crops_total),
         name="first_sweep",
-    )(index, in_hbm(protos), mine, other, base, order)
+    )(index, in_hbm(protos), mine, other, base, *order)
 
 
 def fetch_rows(weights_hbm, weights_ref, sems):
@@ -413,7 +423,7 @@
 
 
 def next_sweep_kernel(
-    protos_total, weights_hbm, parts_ref, order_ref, copies_ref, weights_ref, scale_ref, pieces_ref, totals_ref, sems,
+    protos_total, weights_hbm, parts_ref, copies_ref, weights_ref, scale_ref, pieces_ref, totals_ref, sems,
 ):
     steps, chunk, crops_total = weights_ref.shape
     arrived = fetch_rows(weights_hbm, weights_ref, sems)
@@ -447,8 +457,8 @@
     copies = parts.shape[0]
     chunk = min(thin, 256)
     return pl.pallas_call(
-        functools.partial(next_sweep_kernel, protos_total),
-        in_specs=[whole(pl.ANY), whole(), whole(pl.ANY)],
+        skipping(functools.partial(next_sweep_kernel, protos_total), 2, len(order)),
+        in_specs=[whole(pl.ANY), whole()] + [whole(pl.ANY)] * len(order),
         out_specs=whole(),
         out_shape=jax.ShapeDtypeStruct((copies, 1, crops_total), jnp.float32),
         scratch_shapes=[
@@ -461,11 +471,11 @@
         compiler_params=params(16 if crops_total <= 2048 else 50),
         cost_estimate=cost(8 * thin * crops_total, 2 * thin * crops_total),
         name="next_sweep",
-    )(in_hbm(weights), parts, order)
+    )(in_hbm(weights), parts, *order)
 
 
 def last_scales_kernel(
-    protos_total, weights_hbm, parts_ref, order_ref, copies_ref, weights_ref, scale_ref, out_ref, sems,
+    protos_total, weights_hbm, parts_ref, copies_ref, weights_ref, scale_ref, out_ref, sems,
 ):
     steps, chunk, crops_total = weights_ref.shape
     arrived = fetch_rows(weights_hbm, weights_ref, sems)
@@ -486,8 +496,8 @@
     thin, crops_total = weights.shape
     chunk = min(thin, 256)
     return pl.pallas_call(
-        functools.partial(last_scales_kernel, protos_total),
-        in_specs=[whole(pl.ANY), whole(), whole(pl.ANY)],
+        skipping(functools.partial(last_scales_kernel, protos_total), 2, len(order)),
+        in_specs=[whole(pl.ANY), whole()] + [whole(pl.ANY)] * len(order),
         out_specs=whole(),
         out_shape=jax.ShapeDtypeStruct((copies, 1, thin), jnp.float32),
         scratch_shapes=[
@@ -499,7 +509,7 @@
         compiler_params=params(16 if crops_total <= 2048 else 50),
         cost_estimate=cost(4 * thin * crops_total, 2 * thin * crops_total),
         name="last_scales",
-    )(in_hbm(weights), parts, order)
+    )(in_hbm(weights), parts, *order)
 
 
 def student_front_kernel(
@@ -531,12 +541,12 @@
         give_ref[:, columns] = product[2 * share :]
 
 
-def student_front(index, bias, rows, first, second):
+def student_front(index, bias, rows, first, second, order):
     share, features = rows[0].shape
     hidden, units = second.shape
     return pl.pallas_call(
-        student_front_kernel,
-        in_specs=[whole(pltpu.SMEM), whole()] + [whole(pl.ANY)] * 6,
+        skipping(student_front_kernel, 8, len(order)),
+        in_specs=[whole(pltpu.SMEM), whole()] + [whole(pl.ANY)] * (6 + len(order)),
         out_specs=[whole(), whole()],
         out_shape=[jax.ShapeDtypeStruct((2 * share, units), jnp.float32)] * 2,
         scratch_shapes=[
@@ -548,7 +558,7 @@
         compiler_params=params(16),
         cost_estimate=cost(8 * share * hidden * (features + units), 2 * hidden * (features + units)),
         name="student_front",
-    )(index, in_hbm(bias.reshape(1, -1)), in_hbm(rows[0]), *rows[1:], in_hbm(first), in_hbm(second))
+    )(index, in_hbm(bias.reshape(1, -1)), in_hbm(rows[0]), *rows[1:], in_hbm(first), in_hbm(second), *order)
 
 
 def student_middle_kernel(
@@ -681,19 +691,21 @@
     mine = stages[-1]
     other = swap(mine, "proto", 1)
     top = jnp.full((256, 128), -jnp.inf, jnp.float32)
-    top = wide_tops(own_unit, protos, top, stages[1], 0, 0, count // 2, 4)
-    top_copies = wide_tops(own_unit, protos, top, stages[2], devices, count // 2, count // 2, 4)
+    top = wide_tops(own_unit, protos, top, (stages[1],), 0, 0, count // 2, 4)
+    top_copies = wide_tops(own_unit, protos, top, (stages[2],), devices, count // 2, count // 2, 4)
     all_tops = all_to_all(top_copies, BOTH)
     tops = jnp.max(all_tops.reshape(batch_size, proto_size, 256)[:, :, :group_rows], axis=1)
     tops = bit_reversed(tops, batch_size).reshape(batch_size, 2, group_rows // 2)
     base = jnp.transpose(tops, (1, 0, 2)).reshape(1, crops_total) * -teacher_rate
 
-    rows = [crops, swap(crops, "proto", 2), swap(crops, "proto", 1), swap(crops, "proto", 3)]
-    keep, give = student_front(proto_ref, b_first, rows, w_first, w_second)
+    crops_x = swap(crops, "proto", 2)
+    rows = [crops, crops_x, swap(crops, "proto", 1), swap(crops_x, "proto", 1)]
+    third_x = swap(w_third, "proto", 2)
+    thirds = [w_third, third_x, swap(w_third, "proto", 1), swap(third_x, "proto", 1)]
+    keep, give = student_front(proto_ref, b_first, rows, w_first, w_second, (top,))
     core_rows = swap(give, "proto", 1)
     x_sent = keep[share_rows:] + core_rows[share_rows:]
     x_rows = swap(x_sent, "proto", 2)
-    thirds = [w_third, swap(w_third, "proto", 2), swap(w_third, "proto", 1), swap(w_third, "proto", 3)]
     unit, rounded, lengths = student_middle(
         proto_ref, keep, core_rows, x_rows, b_second, thirds, b_third
     )
@@ -706,12 +718,12 @@
     slots = attract(student_emb, state, protos, count // 2, count // 2, 4, proto_size)
     attract_parts = send_blocks([slots[0], slots[2], slots[1], slots[3]])
 
-    copies, weights = first_sweep(thin_ref, protos, mine, other, base, x_sent, devices, thin, protos_total)
+    copies, weights = first_sweep(thin_ref, protos, mine, other, base, (x_sent, *thirds[2:]), devices, thin, protos_total)
     for _ in range(ITERS - 2):
-        copies = next_sweep(weights, all_to_all(copies, BOTH), rounded, protos_total)
-    scale_copies = last_scales(weights, all_to_all(copies, BOTH), state, batch_size, protos_total)
+        copies = next_sweep(weights, all_to_all(copies, BOTH), (rounded,), protos_total)
+    scale_copies = last_scales(weights, all_to_all(copies, BOTH), (state,), batch_size, protos_total)
     all_scale = all_to_all(scale_copies, "batch")
-    repels = repel(wide_ref, own_unit, all_tops, all_scale, protos, slots[0], proto_size)
+    repels = repel(wide_ref, own_unit, all_tops, all_scale, protos, (slots[0],), proto_size)
     return finish(unit, lengths, attract_parts, send_blocks(repels))
 
 

time: 120 us -> 107 us (0.89)
  waiting for transfers between devices: 32.6 us -> 21 us
  starting transfers between devices: 36.6 us -> 34.4 us
    ppermute x20, waiting for transfers between devices: 24.7 us -> 7.65 us  [swap(): lax.ppermute(values, axis, [(i, i ^ flip) for i in range(lax.axis_size(ax...]
    all_to_all x4, waiting for transfers between devices: 7.87 us -> 13.3 us  [all_to_all(): return lax.all_to_all(copies, axes, 0, 0, tiled=True)]
    ppermute x20, starting transfers between devices: 19.2 us -> 18 us  [swap(): lax.ppermute(values, axis, [(i, i ^ flip) for i in range(lax.axis_size(ax...]
  transfers between devices with their start and end apart: 24 -> 24, of which waited for: 11 -> 9; matrix products, arithmetic and copies ran while one was open for 1% -> 1% of each run, Pallas kernels for 36% -> 42%
where the time goes in v8:
time: 107 us; the launch traced here: 106 us
  Pallas kernels  49.2 us (46%)
  starting transfers between devices  34.4 us (32%)
  waiting for transfers between devices  21 us (20%)
    ppermute x20, starting transfers between devices, swap(): lax.ppermute(values, axis, [(i, i ^ flip) for i in range(lax.axis_size(ax...  18 us
    all_to_all x4, starting transfers between devices, all_to_all(): return lax.all_to_all(copies, axes, 0, 0, tiled=True)  16.4 us
    all_to_all x4, waiting for transfers between devices, all_to_all(): return lax.all_to_all(copies, axes, 0, 0, tiled=True)  13.3 us
    pallas_call x2, Pallas kernels, attract(): pl.pallas_call(functools.partial(attract_kernel, first_row, outputs > 1),...  10.1 us
    pallas_call x1, Pallas kernels, repel(): pl.pallas_call(skipping(functools.partial(repel_kernel, proto_size), 5, l...  9.47 us
    ppermute x20, waiting for transfers between devices, swap(): lax.ppermute(values, axis, [(i, i ^ flip) for i in range(lax.axis_size(ax...  7.65 us
    pallas_call x2, Pallas kernels, wide_tops(): pl.pallas_call(skipping(functools.partial(wide_tops_kernel, first_row, co...  7.32 us
    pallas_call x1, Pallas kernels, first_sweep(): pl.pallas_call(skipping(functools.partial(first_sweep_kernel, chunk, prot...  5.95 us
  transfers between devices with their start and end apart: 24, of which 9 were waited for; matrix products, arithmetic and copies ran while one was open for 1% of the time, Pallas kernels for 42%

profile of v8, /device:TPU:0, one launch (start us, length us, event | category | flops | bytes accessed | tf_op | source)
XLA Modules:
  0.0 106.2 jit_solution(16440268099981175631)
XLA Ops:
  0.0 2.9 %collective-permute-start = (bf16[48,1536]{1,0:T(8,128)(2,1)}, bf16[48,1536]{1,0:T(8,128)(2,1)S(1)}, u32[]{:S(2)}, u32[]{:S(2)}) collective-permute-start(bf16[48,1536]{1,0:T(8,128)(2,1)} %refs_2_.1), channel_id=1, source_target_pairs={{0,2},{1,3},{2,0},{3,1},{4,6},{5,7},{6,4},{7,5},{8,10},{9,11},{10,... | collective-permute-start | bytes 442376 | tf_op jit(solution)/shard_map/ppermute | solution.py:640
  2.9 1.0 teacher_units.1
  4.0 2.7 %collective-permute-start.3 = (bf16[96,256]{1,0:T(8,128)(2,1)S(1)}, bf16[96,256]{1,0:T(8,128)(2,1)S(1)}, u32[]{:S(2)}, u32[]{:S(2)}) collective-permute-start(bf16[96,256]{1,0:T(8,128)(2,1)S(1)} %get-tuple-element.23), channel_id=1, source_target_pairs={{0,16},{4,20},{8,24},{12,28},{16,0},{20,4},{24,8},{28,12},{1,17},{... | collective-permute-start | bytes 147464 | tf_op jit(solution)/shard_map/ppermute | solution.py:640
  6.6 0.0 collective-permute-start.1
  6.6 0.4 collective-permute-done.refs_3_
  7.0 0.1 collective-permute-start.2
  7.1 2.0 %collective-permute-done.3 = bf16[96,256]{1,0:T(8,128)(2,1)S(1)} collective-permute-done((bf16[96,256]{1,0:T(8,128)(2,1)S(1)}, bf16[96,256]{1,0:T(8,128)(2,1)S(1)}, u32[]{:S(2)}, u32[]{:S(2)}) %collective-permute-start.3) | collective-permute-done | bytes 49184 | tf_op jit(solution)/shard_map/ppermute | solution.py:640
  9.2 1.5 %collective-permute-start.14 = (bf16[192,256]{1,0:T(8,128)(2,1)S(1)}, bf16[192,256]{1,0:T(8,128)(2,1)S(1)}, u32[]{:S(2)}, u32[]{:S(2)}) collective-permute-start(bf16[192,256]{1,0:T(8,128)(2,1)S(1)} %maximum_select_fusion.2.refs_3_), channel_id=1, source_target_pairs={{0,8},{4,12},{8,0},{12,4},{16,24},{20,28},{24,16},{28,20},{1,9},{5... | collective-permute-start | bytes 294920 | tf_op jit(solution)/shard_map/ppermute | solution.py:640
  10.7 3.3 %wide_tops.2.refs_8_.refs_2_ = f32[256,128]{1,0:T(8,128)S(1)} custom-call(bf16[192,256]{1,0:T(8,128)(2,1)S(1)} %get-tuple-element.22.refs_0_.refs_1_, bf16[16384,256]{1,0:T(8,128)(2,1)} %refs_4_.1, f32[256,128]{1,0:T(8,128)S(1)} %broadcast_in_dim.7.refs_2_, bf16[192,256]{1,0:T(8,128)(2,1)S(1)} %maximum_select_fusion.2.refs_3_), custom_call_target="tpu_custom_call" | custom-call | flops 805306368 | bytes 4194304 | tf_op jit(solution)/shard_map/wide_tops/pallas_call | solution.py:137
  14.0 0.0 collective-permute-done.1.refs_4_
  14.0 0.0 collective-permute-done.2.refs_5_
  14.0 4.8 %student_front.1 = (f32[96,2048]{1,0:T(8,128)S(1)}, f32[96,2048]{1,0:T(8,128)}) custom-call(s32[1]{0:T(128)} %bitcast.refs_0_.index_ref, f32[1,2048]{1,0:T(1,128)} %bitcast.10, bf16[48,1536]{1,0:T(8,128)(2,1)} %refs_2_.1, bf16[48,1536]{1,0:T(8,128)(2,1)S(1)} %collective-permute-done.refs_3_, bf16[48,1536]{1,0:T(8,128)(2,1)S(1)} %collective-permute-done.1.refs_4_, ...), custom_call_target="tpu_custom_call" | custom-call | flops 704643072 | bytes 3670016 | tf_op jit(solution)/shard_map/student_front/pallas_call | solution.py:547
  18.9 0.1 collective-permute-start.4
  19.0 0.6 collective-permute-start.6
  19.6 0.2 collective-permute-start.7
  19.7 0.0 collective-permute-done.14
  19.7 0.1 maximum_select_fusion.1.refs_3_
  19.8 4.0 %wide_tops.3 = f32[32,1,256]{2,1,0:T(1,128)} custom-call(bf16[192,256]{1,0:T(8,128)(2,1)S(1)} %get-tuple-element.22.refs_0_.refs_1_, bf16[16384,256]{1,0:T(8,128)(2,1)} %refs_4_.1, f32[256,128]{1,0:T(8,128)S(1)} %wide_tops.2.refs_8_.refs_2_, bf16[384,256]{1,0:T(8,128)(2,1)S(1)} %maximum_select_fusion.1.refs_3_), custom_call_target="tpu_custom_call" | custom-call | flops 805306368 | bytes 4194304 | tf_op jit(solution)/shard_map/wide_tops/pallas_call | solution.py:137
  23.8 5.3 %all-to-all-start = ((f32[32,1,256]{2,1,0:T(1,128)}), f32[32,1,256]{2,1,0:T(1,128)S(1)}, u32[]{:S(2)}, u32[]{:S(2)}) async-start(f32[32,1,256]{2,1,0:T(1,128)} %wide_tops.3), calls=%async_computation | async-start | bytes 65536 | tf_op jit(solution)/shard_map/all_to_all | solution.py:669
  29.1 0.1 pad_add_fusion.1.refs_0_
  29.2 1.8 %collective-permute-start.15 = (bf16[384,256]{1,0:T(8,128)(2,1)S(1)}, bf16[384,256]{1,0:T(8,128)(2,1)S(1)}, u32[]{:S(2)}, u32[]{:S(2)}) collective-permute-start(bf16[384,256]{1,0:T(8,128)(2,1)S(1)} %maximum_select_fusion.1.refs_3_), channel_id=1, source_target_pairs={{0,4},{4,0},{8,12},{12,8},{16,20},{20,16},{24,28},{28,24},{1,5},{5... | collective-permute-start | bytes 589832 | tf_op jit(solution)/shard_map/ppermute | solution.py:640
  30.9 5.4 %all-to-all-done.refs_2_ = f32[32,1,256]{2,1,0:T(1,128)S(1)} async-done(((f32[32,1,256]{2,1,0:T(1,128)}), f32[32,1,256]{2,1,0:T(1,128)S(1)}, u32[]{:S(2)}, u32[]{:S(2)}) %all-to-all-start) | async-done | bytes 32800 | tf_op jit(solution)/shard_map/all_to_all | solution.py:669
  36.3 0.1 reduce
  36.5 0.1 mul.17
  36.6 0.1 mul.19.refs_4_
  36.7 0.2 collective-permute-start.8
  36.9 0.0 collective-permute-done.15
  36.9 0.2 maximum_select_fusion.refs_2_
  37.0 0.5 collective-permute-start.16
  37.5 1.0 collective-permute-start.5
  38.6 0.0 collective-permute-done.7.other_ref.refs_6_
  38.6 0.3 collective-permute-done.16.refs_3_
  38.9 5.9 %first_sweep.1 = (f32[32,1,1536]{2,1,0:T(1,128)S(1)}, bf16[2048,1536]{1,0:T(8,128)(2,1)}) custom-call(s32[2]{0:T(128)S(1)} %pad_add_fusion.1.refs_0_, bf16[16384,256]{1,0:T(8,128)(2,1)} %refs_4_.1, bf16[768,256]{1,0:T(8,128)(2,1)S(1)} %maximum_select_fusion.refs_2_, bf16[768,256]{1,0:T(8,128)(2,1)S(1)} %collective-permute-done.16.refs_3_, ...), custom_call_target="tpu_custom_call" | custom-call | flops 1610612736 | bytes 6291456 | tf_op jit(solution)/shard_map/first_sweep/pallas_call | solution.py:374
  44.8 0.7 copy-done
  45.5 5.0 %all-to-all-start.1 = ((f32[32,1,1536]{2,1,0:T(1,128)}), f32[32,1,1536]{2,1,0:T(1,128)S(1)}, u32[]{:S(2)}, u32[]{:S(2)}) async-start(f32[32,1,1536]{2,1,0:T(1,128)} %copy-done), calls=%async_computation.1 | async-start | bytes 393216 | tf_op jit(solution)/shard_map/all_to_all | solution.py:669
  50.6 0.1 pad_add_fusion.refs_0_
  50.6 0.0 collective-permute-done.5.x_ref
  50.6 1.5 %student_middle.1 = (f32[48,256]{1,0:T(8,128)S(1)}, bf16[48,256]{1,0:T(8,128)(2,1)S(1)}, f32[48,128]{1,0:T(8,128)S(1)}) custom-call(s32[1]{0:T(128)} %bitcast.refs_0_.index_ref, f32[96,2048]{1,0:T(8,128)S(1)} %get-tuple-element.24.keep_ref, f32[96,2048]{1,0:T(8,128)S(1)} %collective-permute-done.4.core_ref, f32[48,2048]{1,0:T(8,128)S(1)} %collective-permute-done.5.x_ref, ...), custom_call_target="tpu_custom_call" | custom-call | flops 50331648 | bytes 2621440 | tf_op jit(solution)/shard_map/student_middle/pallas_call | solution.py:588
  52.2 1.8 %collective-permute-start.9 = (bf16[48,256]{1,0:T(8,128)(2,1)S(1)}, bf16[48,256]{1,0:T(8,128)(2,1)S(1)}, u32[]{:S(2)}, u32[]{:S(2)}) collective-permute-start(bf16[48,256]{1,0:T(8,128)(2,1)S(1)} %get-tuple-element.28.refs_2_), channel_id=1, source_target_pairs={{0,2},{1,3},{2,0},{3,1},{4,6},{5,7},{6,4},{7,5},{8,10},{9,11},{10,... | collective-permute-start | bytes 73736 | tf_op jit(solution)/shard_map/ppermute | solution.py:640
  54.0 5.4 %all-to-all-done.1.refs_1_ = f32[32,1,1536]{2,1,0:T(1,128)S(1)} async-done(((f32[32,1,1536]{2,1,0:T(1,128)}), f32[32,1,1536]{2,1,0:T(1,128)S(1)}, u32[]{:S(2)}, u32[]{:S(2)}) %all-to-all-start.1) | async-done | bytes 196640 | tf_op jit(solution)/shard_map/all_to_all | solution.py:669
  59.4 4.4 %next_sweep.1 = f32[32,1,1536]{2,1,0:T(1,128)} custom-call(bf16[2048,1536]{1,0:T(8,128)(2,1)} %get-tuple-element.33.refs_0_, f32[32,1,1536]{2,1,0:T(1,128)S(1)} %all-to-all-done.1.refs_1_, bf16[48,256]{1,0:T(8,128)(2,1)S(1)} %get-tuple-element.28.refs_2_), custom_call_target="tpu_custom_call" | custom-call | flops 25165824 | bytes 6291456 | tf_op jit(solution)/shard_map/next_sweep/pallas_call | solution.py:459
  63.8 2.7 %all-to-all-start.2 = ((f32[32,1,1536]{2,1,0:T(1,128)}), f32[32,1,1536]{2,1,0:T(1,128)S(1)}, u32[]{:S(2)}, u32[]{:S(2)}) async-start(f32[32,1,1536]{2,1,0:T(1,128)} %next_sweep.1), calls=%async_computation.2 | async-start | bytes 393216 | tf_op jit(solution)/shard_map/all_to_all | solution.py:669
  66.6 0.0 collective-permute-done.9
  66.6 0.3 collective-permute-start.10
  66.9 1.0 collective-permute-done.10
  67.9 5.0 %attract.2.state_ref.refs_2_ = f32[192,512]{1,0:T(8,128)S(1)} custom-call(bf16[192,256]{1,0:T(8,128)(2,1)S(1)} %constant_dynamic-update-slice_fusion.emb_ref, f32[192,512]{1,0:T(8,128)S(1)} %concatenate.35.state_ref, bf16[16384,256]{1,0:T(8,128)(2,1)} %refs_4_.1), custom_call_target="tpu_custom_call" | custom-call | flops 1610612736 | bytes 4194304 | tf_op jit(solution)/shard_map/attract/pallas_call | solution.py:280
  73.0 2.5 %all-to-all-done.2.refs_1_ = f32[32,1,1536]{2,1,0:T(1,128)S(1)} async-done(((f32[32,1,1536]{2,1,0:T(1,128)}), f32[32,1,1536]{2,1,0:T(1,128)S(1)}, u32[]{:S(2)}, u32[]{:S(2)}) %all-to-all-start.2) | async-done | bytes 196640 | tf_op jit(solution)/shard_map/all_to_all | solution.py:669
  75.4 3.7 %last_scales.1 = f32[8,1,2048]{2,1,0:T(1,128)} custom-call(bf16[2048,1536]{1,0:T(8,128)(2,1)} %get-tuple-element.33.refs_0_, f32[32,1,1536]{2,1,0:T(1,128)S(1)} %all-to-all-done.2.refs_1_, f32[192,512]{1,0:T(8,128)S(1)} %attract.2.state_ref.refs_2_), custom_call_target="tpu_custom_call" | custom-call | flops 12582912 | bytes 6291456 | tf_op jit(solution)/shard_map/last_scales/pallas_call | solution.py:498
  79.2 3.4 %all-to-all-start.3 = ((f32[8,1,2048]{2,1,0:T(1,128)}), f32[8,1,2048]{2,1,0:T(1,128)S(1)}, u32[]{:S(2)}, u32[]{:S(2)}) async-start(f32[8,1,2048]{2,1,0:T(1,128)} %last_scales.1), calls=%async_computation.3 | async-start | bytes 131072 | tf_op jit(solution)/shard_map/all_to_all | solution.py:669
  82.6 5.1 %attract.3 = (f32[48,512]{1,0:T(8,128)S(1)}, f32[48,512]{1,0:T(8,128)S(1)}, f32[48,512]{1,0:T(8,128)S(1)}, f32[48,512]{1,0:T(8,128)S(1)}) custom-call(bf16[192,256]{1,0:T(8,128)(2,1)S(1)} %constant_dynamic-update-slice_fusion.emb_ref, f32[192,512]{1,0:T(8,128)S(1)} %attract.2.state_ref.refs_2_, bf16[16384,256]{1,0:T(8,128)(2,1)} %refs_4_.1), custom_call_target="tpu_custom_call" | custom-call | flops 1610612736 | bytes 4194304 | tf_op jit(solution)/shard_map/attract/pallas_call | solution.py:280
  87.7 0.7 collective-permute-start.11
  88.3 1.0 collective-permute-start.12
  89.3 0.5 collective-permute-start.13
  89.8 0.0 all-to-all-done.3.refs_3_
  89.8 9.5 %repel.1 = (f32[48,384]{1,0:T(8,128)S(1)}, f32[48,384]{1,0:T(8,128)S(1)}, f32[48,384]{1,0:T(8,128)S(1)}, f32[48,384]{1,0:T(8,128)S(1)}) custom-call(s32[2]{0:T(128)S(1)} %pad_add_fusion.refs_0_, bf16[192,256]{1,0:T(8,128)(2,1)S(1)} %get-tuple-element.22.refs_0_.refs_1_, f32[32,1,256]{2,1,0:T(1,128)S(1)} %all-to-all-done.refs_2_, ...), custom_call_target="tpu_custom_call" | custom-call | flops 3221225472 | bytes 8388608 | tf_op jit(solution)/shard_map/repel/pallas_call | solution.py:202
  99.3 0.8 collective-permute-start.17
  100.0 0.9 collective-permute-start.18
  101.0 0.0 collective-permute-done.11.rest_1_
  101.0 0.5 collective-permute-start.19
  101.5 0.0 collective-permute-done.13.rest_3_
  101.5 0.0 collective-permute-done.17.rest_5_
  101.5 3.4 %collective-permute-done.18.rest_6_ = f32[48,384]{1,0:T(8,128)S(1)} collective-permute-done((f32[48,384]{1,0:T(8,128)S(1)}, f32[48,384]{1,0:T(8,128)S(1)}, u32[]{:S(2)}, u32[]{:S(2)}) %collective-permute-start.18) | collective-permute-done | bytes 73760 | tf_op jit(solution)/shard_map/ppermute | solution.py:640
  104.9 0.6 collective-permute-done.19.rest_7_
  105.5 0.8 finish.1
  (21 shorter events, 0.2 us)
Async XLA Ops:
  0.0 7.0 %collective-permute-start = (bf16[48,1536]{1,0:T(8,128)(2,1)}, bf16[48,1536]{1,0:T(8,128)(2,1)S(1)}, u32[]{:S(2)}, u32[]{:S(2)}) collective-permute-start(bf16[48,1536]{1,0:T(8,128)(2,1)} %refs_2_.1), channel_id=1, source_target_pairs={{0,2},{1,3},{2,0},{3,1},{4,6},{5,7},{6,4},{7,5},{8,10},{9,11},{10,... | collective-permute-start | bytes 442376 | tf_op jit(solution)/shard_map/ppermute | solution.py:640
  4.0 5.2 %collective-permute-start.3 = (bf16[96,256]{1,0:T(8,128)(2,1)S(1)}, bf16[96,256]{1,0:T(8,128)(2,1)S(1)}, u32[]{:S(2)}, u32[]{:S(2)}) collective-permute-start(bf16[96,256]{1,0:T(8,128)(2,1)S(1)} %get-tuple-element.23), channel_id=1, source_target_pairs={{0,16},{4,20},{8,24},{12,28},{16,0},{20,4},{24,8},{28,12},{1,17},{... | collective-permute-start | bytes 147464 | tf_op jit(solution)/shard_map/ppermute | solution.py:640
  6.6 7.4 %collective-permute-start.1 = (bf16[48,1536]{1,0:T(8,128)(2,1)}, bf16[48,1536]{1,0:T(8,128)(2,1)S(1)}, u32[]{:S(2)}, u32[]{:S(2)}) collective-permute-start(bf16[48,1536]{1,0:T(8,128)(2,1)} %refs_2_.1), channel_id=1, source_target_pairs={{0,1},{1,0},{2,3},{3,2},{4,5},{5,4},{6,7},{7,6},{8,9},{9,8},{10,11... | collective-permute-start | bytes 442376 | tf_op jit(solution)/shard_map/ppermute | solution.py:640
  7.0 7.0 %collective-permute-start.2 = (bf16[48,1536]{1,0:T(8,128)(2,1)S(1)}, bf16[48,1536]{1,0:T(8,128)(2,1)S(1)}, u32[]{:S(2)}, u32[]{:S(2)}) collective-permute-start(bf16[48,1536]{1,0:T(8,128)(2,1)S(1)} %collective-permute-done.refs_3_), channel_id=1, source_target_pairs={{0,1},{1,0},{2,3},{3,2},{4,5},{5,4},{6,7},{7,6},{8,9},{9,8},{10,11... | collective-permute-start | bytes 442376 | tf_op jit(solution)/shard_map/ppermute | solution.py:640
  9.2 10.6 %collective-permute-start.14 = (bf16[192,256]{1,0:T(8,128)(2,1)S(1)}, bf16[192,256]{1,0:T(8,128)(2,1)S(1)}, u32[]{:S(2)}, u32[]{:S(2)}) collective-permute-start(bf16[192,256]{1,0:T(8,128)(2,1)S(1)} %maximum_select_fusion.2.refs_3_), channel_id=1, source_target_pairs={{0,8},{4,12},{8,0},{12,4},{16,24},{20,28},{24,16},{28,20},{1,9},{5... | collective-permute-start | bytes 294920 | tf_op jit(solution)/shard_map/ppermute | solution.py:640
  18.9 18.6 %collective-permute-start.4 = (f32[96,2048]{1,0:T(8,128)}, f32[96,2048]{1,0:T(8,128)S(1)}, u32[]{:S(2)}, u32[]{:S(2)}) collective-permute-start(f32[96,2048]{1,0:T(8,128)} %get-tuple-element.25), channel_id=1, source_target_pairs={{0,1},{1,0},{2,3},{3,2},{4,5},{5,4},{6,7},{7,6},{8,9},{9,8},{10,11... | collective-permute-start | bytes 2359304 | tf_op jit(solution)/shard_map/ppermute | solution.py:640
  19.0 17.7 %collective-permute-start.6 = (bf16[512,256]{1,0:T(8,128)(2,1)}, bf16[512,256]{1,0:T(8,128)(2,1)S(1)}, u32[]{:S(2)}, u32[]{:S(2)}) collective-permute-start(bf16[512,256]{1,0:T(8,128)(2,1)} %own_ref.1), channel_id=1, source_target_pairs={{0,2},{1,3},{2,0},{3,1},{4,6},{5,7},{6,4},{7,5},{8,10},{9,11},{10,... | collective-permute-start | bytes 786440 | tf_op jit(solution)/shard_map/ppermute | solution.py:640
  19.6 19.0 %collective-permute-start.7 = (bf16[512,256]{1,0:T(8,128)(2,1)}, bf16[512,256]{1,0:T(8,128)(2,1)S(1)}, u32[]{:S(2)}, u32[]{:S(2)}) collective-permute-start(bf16[512,256]{1,0:T(8,128)(2,1)} %own_ref.1), channel_id=1, source_target_pairs={{0,1},{1,0},{2,3},{3,2},{4,5},{5,4},{6,7},{7,6},{8,9},{9,8},{10,11... | collective-permute-start | bytes 786440 | tf_op jit(solution)/shard_map/ppermute | solution.py:640
  23.8 12.5 %all-to-all-start = ((f32[32,1,256]{2,1,0:T(1,128)}), f32[32,1,256]{2,1,0:T(1,128)S(1)}, u32[]{:S(2)}, u32[]{:S(2)}) async-start(f32[32,1,256]{2,1,0:T(1,128)} %wide_tops.3), calls=%async_computation | async-start | bytes 65536 | tf_op jit(solution)/shard_map/all_to_all | solution.py:669
  29.2 7.7 %collective-permute-start.15 = (bf16[384,256]{1,0:T(8,128)(2,1)S(1)}, bf16[384,256]{1,0:T(8,128)(2,1)S(1)}, u32[]{:S(2)}, u32[]{:S(2)}) collective-permute-start(bf16[384,256]{1,0:T(8,128)(2,1)S(1)} %maximum_select_fusion.1.refs_3_), channel_id=1, source_target_pairs={{0,4},{4,0},{8,12},{12,8},{16,20},{20,16},{24,28},{28,24},{1,5},{5... | collective-permute-start | bytes 589832 | tf_op jit(solution)/shard_map/ppermute | solution.py:640
  36.7 1.9 %collective-permute-start.8 = (bf16[512,256]{1,0:T(8,128)(2,1)S(1)}, bf16[512,256]{1,0:T(8,128)(2,1)S(1)}, u32[]{:S(2)}, u32[]{:S(2)}) collective-permute-start(bf16[512,256]{1,0:T(8,128)(2,1)S(1)} %collective-permute-done.6.partner_ref), channel_id=1, source_target_pairs={{0,1},{1,0},{2,3},{3,2},{4,5},{5,4},{6,7},{7,6},{8,9},{9,8},{10,11... | collective-permute-start | bytes 786440 | tf_op jit(solution)/shard_map/ppermute | solution.py:640
  37.0 1.8 %collective-permute-start.16 = (bf16[768,256]{1,0:T(8,128)(2,1)S(1)}, bf16[768,256]{1,0:T(8,128)(2,1)S(1)}, u32[]{:S(2)}, u32[]{:S(2)}) collective-permute-start(bf16[768,256]{1,0:T(8,128)(2,1)S(1)} %maximum_select_fusion.refs_2_), channel_id=1, source_target_pairs={{0,1},{1,0},{2,3},{3,2},{4,5},{5,4},{6,7},{7,6},{8,9},{9,8},{10,11... | collective-permute-start | bytes 1179656 | tf_op jit(solution)/shard_map/ppermute | solution.py:640
  37.5 13.1 %collective-permute-start.5 = (f32[48,2048]{1,0:T(8,128)S(1)}, f32[48,2048]{1,0:T(8,128)S(1)}, u32[]{:S(2)}, u32[]{:S(2)}) collective-permute-start(f32[48,2048]{1,0:T(8,128)S(1)} %slice_add_fusion.refs_5_), channel_id=1, source_target_pairs={{0,2},{1,3},{2,0},{3,1},{4,6},{5,7},{6,4},{7,5},{8,10},{9,11},{10,... | collective-permute-start | bytes 1179656 | tf_op jit(solution)/shard_map/ppermute | solution.py:640
  44.8 0.7 copy-start
  45.5 13.9 %all-to-all-start.1 = ((f32[32,1,1536]{2,1,0:T(1,128)}), f32[32,1,1536]{2,1,0:T(1,128)S(1)}, u32[]{:S(2)}, u32[]{:S(2)}) async-start(f32[32,1,1536]{2,1,0:T(1,128)} %copy-done), calls=%async_computation.1 | async-start | bytes 393216 | tf_op jit(solution)/shard_map/all_to_all | solution.py:669
  52.2 14.4 %collective-permute-start.9 = (bf16[48,256]{1,0:T(8,128)(2,1)S(1)}, bf16[48,256]{1,0:T(8,128)(2,1)S(1)}, u32[]{:S(2)}, u32[]{:S(2)}) collective-permute-start(bf16[48,256]{1,0:T(8,128)(2,1)S(1)} %get-tuple-element.28.refs_2_), channel_id=1, source_target_pairs={{0,2},{1,3},{2,0},{3,1},{4,6},{5,7},{6,4},{7,5},{8,10},{9,11},{10,... | collective-permute-start | bytes 73736 | tf_op jit(solution)/shard_map/ppermute | solution.py:640
  63.8 11.6 %all-to-all-start.2 = ((f32[32,1,1536]{2,1,0:T(1,128)}), f32[32,1,1536]{2,1,0:T(1,128)S(1)}, u32[]{:S(2)}, u32[]{:S(2)}) async-start(f32[32,1,1536]{2,1,0:T(1,128)} %next_sweep.1), calls=%async_computation.2 | async-start | bytes 393216 | tf_op jit(solution)/shard_map/all_to_all | solution.py:669
  66.6 1.3 %collective-permute-start.10 = (bf16[96,256]{1,0:T(8,128)(2,1)S(1)}, bf16[96,256]{1,0:T(8,128)(2,1)S(1)}, u32[]{:S(2)}, u32[]{:S(2)}) collective-permute-start(bf16[96,256]{1,0:T(8,128)(2,1)S(1)} %pad_maximum_fusion), channel_id=1, source_target_pairs={{0,1},{1,0},{2,3},{3,2},{4,5},{5,4},{6,7},{7,6},{8,9},{9,8},{10,11... | collective-permute-start | bytes 147464 | tf_op jit(solution)/shard_map/ppermute | solution.py:640
  79.2 10.6 %all-to-all-start.3 = ((f32[8,1,2048]{2,1,0:T(1,128)}), f32[8,1,2048]{2,1,0:T(1,128)S(1)}, u32[]{:S(2)}, u32[]{:S(2)}) async-start(f32[8,1,2048]{2,1,0:T(1,128)} %last_scales.1), calls=%async_computation.3 | async-start | bytes 131072 | tf_op jit(solution)/shard_map/all_to_all | solution.py:669
  87.7 13.3 %collective-permute-start.11 = (f32[48,512]{1,0:T(8,128)S(1)}, f32[48,512]{1,0:T(8,128)S(1)}, u32[]{:S(2)}, u32[]{:S(2)}) collective-permute-start(f32[48,512]{1,0:T(8,128)S(1)} %get-tuple-element.30), channel_id=1, source_target_pairs={{0,1},{1,0},{2,3},{3,2},{4,5},{5,4},{6,7},{7,6},{8,9},{9,8},{10,11... | collective-permute-start | bytes 294920 | tf_op jit(solution)/shard_map/ppermute | solution.py:640
  88.3 13.1 %collective-permute-start.12 = (f32[48,512]{1,0:T(8,128)S(1)}, f32[48,512]{1,0:T(8,128)S(1)}, u32[]{:S(2)}, u32[]{:S(2)}) collective-permute-start(f32[48,512]{1,0:T(8,128)S(1)} %get-tuple-element.31), channel_id=1, source_target_pairs={{0,2},{1,3},{2,0},{3,1},{4,6},{5,7},{6,4},{7,5},{8,10},{9,11},{10,... | collective-permute-start | bytes 294920 | tf_op jit(solution)/shard_map/ppermute | solution.py:640
  89.3 12.2 %collective-permute-start.13 = (f32[48,512]{1,0:T(8,128)S(1)}, f32[48,512]{1,0:T(8,128)S(1)}, u32[]{:S(2)}, u32[]{:S(2)}) collective-permute-start(f32[48,512]{1,0:T(8,128)S(1)} %get-tuple-element.32), channel_id=1, source_target_pairs={{0,3},{1,2},{2,1},{3,0},{4,7},{5,6},{6,5},{7,4},{8,11},{9,10},{10,... | collective-permute-start | bytes 294920 | tf_op jit(solution)/shard_map/ppermute | solution.py:640
  99.3 2.2 %collective-permute-start.17 = (f32[48,384]{1,0:T(8,128)S(1)}, f32[48,384]{1,0:T(8,128)S(1)}, u32[]{:S(2)}, u32[]{:S(2)}) collective-permute-start(f32[48,384]{1,0:T(8,128)S(1)} %get-tuple-element.36), channel_id=1, source_target_pairs={{0,1},{1,0},{2,3},{3,2},{4,5},{5,4},{6,7},{7,6},{8,9},{9,8},{10,11... | collective-permute-start | bytes 221192 | tf_op jit(solution)/shard_map/ppermute | solution.py:640
  100.0 4.9 %collective-permute-start.18 = (f32[48,384]{1,0:T(8,128)S(1)}, f32[48,384]{1,0:T(8,128)S(1)}, u32[]{:S(2)}, u32[]{:S(2)}) collective-permute-start(f32[48,384]{1,0:T(8,128)S(1)} %get-tuple-element.37), channel_id=1, source_target_pairs={{0,2},{1,3},{2,0},{3,1},{4,6},{5,7},{6,4},{7,5},{8,10},{9,11},{10,... | collective-permute-start | bytes 221192 | tf_op jit(solution)/shard_map/ppermute | solution.py:640
  101.0 4.5 %collective-permute-start.19 = (f32[48,384]{1,0:T(8,128)S(1)}, f32[48,384]{1,0:T(8,128)S(1)}, u32[]{:S(2)}, u32[]{:S(2)}) collective-permute-start(f32[48,384]{1,0:T(8,128)S(1)} %get-tuple-element.38), channel_id=1, source_target_pairs={{0,3},{1,2},{2,1},{3,0},{4,7},{5,6},{6,5},{7,4},{8,11},{9,10},{10,... | collective-permute-start | bytes 221192 | tf_op jit(solution)/shard_map/ppermute | solution.py:640

commit v9 on v8

--- a/solution.py
+++ b/solution.py
@@ -107,7 +107,7 @@
     )(core, in_hbm(teacher_emb))
 
 
-def wide_tops_kernel(first_row, last, unit_ref, protos_hbm, before_ref, out_ref, protos_ref, sems, top_ref):
+def wide_tops_kernel(first_row, unit_ref, protos_hbm, before_ref, out_ref, protos_ref, sems, top_ref):
     rows = unit_ref.shape[0]
     steps, block = protos_ref.shape[:2]
     wide = min(WIDE, block)
@@ -124,21 +124,16 @@
         return carry
 
     lax.fori_loop(0, steps, step, 0)
-    if last:
-        tops = jnp.max(jnp.transpose(top_ref[...]), axis=0, keepdims=True)
-        out_ref[...] = jnp.broadcast_to(tops[None], out_ref.shape)
-    else:
-        out_ref[...] = top_ref[...]
-
-
-def wide_tops(unit, protos, before, order, copies, first_row, count, steps):
+    out_ref[...] = top_ref[...]
+
+
+def wide_tops(unit, protos, before, order, first_row, count, steps):
     rows, width = unit.shape
-    shape = (copies, 1, 256) if copies else before.shape
-    return pl.pallas_call(
-        skipping(functools.partial(wide_tops_kernel, first_row, copies > 0), 3, len(order)),
+    return pl.pallas_call(
+        skipping(functools.partial(wide_tops_kernel, first_row), 3, len(order)),
         in_specs=[whole(), whole(pl.ANY), whole()] + [whole(pl.ANY)] * len(order),
         out_specs=whole(),
-        out_shape=jax.ShapeDtypeStruct(shape, jnp.float32),
+        out_shape=jax.ShapeDtypeStruct(before.shape, jnp.float32),
         scratch_shapes=[
             pltpu.VMEM((steps, count // steps, width), jnp.bfloat16),
             pltpu.SemaphoreType.DMA((steps,)),
@@ -148,6 +143,23 @@
         cost_estimate=cost(2 * rows * width * count, 2 * width * count),
         name="wide_tops",
     )(unit, in_hbm(protos), before, *order)
+
+
+def spread_tops_kernel(top_ref, out_ref):
+    tops = jnp.max(jnp.transpose(top_ref[...]), axis=0, keepdims=True)
+    out_ref[...] = jnp.broadcast_to(tops[None], out_ref.shape)
+
+
+def spread_tops(top, order, copies):
+    return pl.pallas_call(
+        skipping(spread_tops_kernel, 1, len(order)),
+        in_specs=[whole()] + [whole(pl.ANY)] * len(order),
+        out_specs=whole(),
+        out_shape=jax.ShapeDtypeStruct((copies, 1, 256), jnp.float32),
+        compiler_params=params(4),
+        cost_estimate=cost(top.size, 8 * top.size),
+        name="spread_tops",
+    )(top, *order)
 
 
 def repel_kernel(group, index_ref, unit_ref, tops_ref, scale_ref, protos_hbm, *rest):
@@ -312,8 +324,24 @@
     return 1.0 / (protos_total * jnp.concatenate(sums, axis=1))
 
 
-def give_copies(copies_ref, totals):
-    copies_ref[...] = jnp.broadcast_to(totals[None], copies_ref.shape)
+def give_sums(copies_ref, totals):
+    rows = [totals[:, start : start + 128] for start in range(0, totals.shape[1], 128)]
+    spare = copies_ref.shape[1] - len(rows)
+    if spare:
+        rows.append(jnp.zeros((spare, 128), jnp.float32))
+    packed = jnp.concatenate(rows, axis=0).astype(jnp.bfloat16)
+    copies_ref[...] = jnp.broadcast_to(packed[None], copies_ref.shape)
+
+
+def take_scales(parts_ref, scale_ref):
+    crops_total = scale_ref.shape[1]
+    sums = jnp.sum(parts_ref[...].astype(jnp.float32), axis=0)
+    for row in range(crops_total // 128):
+        scale_ref[:, row * 128 : row * 128 + 128] = 1.0 / (crops_total * sums[row : row + 1, :])
+
+
+def sums_shape(copies, crops_total):
+    return (copies, -(-crops_total // 2048) * 16, 128)
 
 
 def first_sweep_kernel(
@@ -362,7 +390,7 @@
         return totals + jnp.sum(scaled.reshape(-1, 8, crops_total), axis=0)
 
     totals = lax.fori_loop(0, thin // small, add_up, jnp.zeros((8, crops_total), jnp.float32))
-    give_copies(copies_ref, jnp.sum(totals, axis=0, keepdims=True))
+    give_sums(copies_ref, jnp.sum(totals, axis=0, keepdims=True))
     for index in range(thin // chunk):
         chunk_out(index).wait()
 
@@ -377,7 +405,7 @@
         + [whole(pl.ANY)] * len(order),
         out_specs=[whole(), whole(pl.ANY)],
         out_shape=[
-            jax.ShapeDtypeStruct((copies, 1, crops_total), jnp.float32),
+            jax.ShapeDtypeStruct(sums_shape(copies, crops_total), jnp.bfloat16),
             pltpu.HBM((thin, crops_total), jnp.bfloat16),
         ],
         scratch_shapes=[
@@ -427,7 +455,7 @@
 ):
     steps, chunk, crops_total = weights_ref.shape
     arrived = fetch_rows(weights_hbm, weights_ref, sems)
-    scale_ref[...] = 1.0 / (crops_total * jnp.sum(parts_ref[...], axis=0))
+    take_scales(parts_ref, scale_ref)
     totals_ref[...] = jnp.zeros(totals_ref.shape, jnp.float32)
 
     def weigh(index):
@@ -449,7 +477,7 @@
 
     lax.fori_loop(1, steps, sweep, 0)
     totals = totals_ref[...] + add_up(steps - 1)
-    give_copies(copies_ref, jnp.sum(totals, axis=0, keepdims=True))
+    give_sums(copies_ref, jnp.sum(totals, axis=0, keepdims=True))
 
 
 def next_sweep(weights, parts, order, protos_total):
@@ -460,7 +488,7 @@
         skipping(functools.partial(next_sweep_kernel, protos_total), 2, len(order)),
         in_specs=[whole(pl.ANY), whole()] + [whole(pl.ANY)] * len(order),
         out_specs=whole(),
-        out_shape=jax.ShapeDtypeStruct((copies, 1, crops_total), jnp.float32),
+        out_shape=jax.ShapeDtypeStruct(sums_shape(copies, crops_total), jnp.bfloat16),
         scratch_shapes=[
             pltpu.VMEM((thin // chunk, chunk, crops_total), jnp.bfloat16),
             pltpu.VMEM((1, crops_total), jnp.float32),
@@ -479,7 +507,7 @@
 ):
     steps, chunk, crops_total = weights_ref.shape
     arrived = fetch_rows(weights_hbm, weights_ref, sems)
-    scale_ref[...] = 1.0 / (crops_total * jnp.sum(parts_ref[...], axis=0))
+    take_scales(parts_ref, scale_ref)
 
     def weigh(index, carry):
         arrived(index)
@@ -489,7 +517,7 @@
         return carry
 
     lax.fori_loop(0, steps, weigh, 0)
-    give_copies(copies_ref, out_ref[...])
+    copies_ref[...] = jnp.broadcast_to(out_ref[...][None], copies_ref.shape)
 
 
 def last_scales(weights, parts, order, copies, protos_total):
@@ -691,18 +719,19 @@
     mine = stages[-1]
     other = swap(mine, "proto", 1)
     top = jnp.full((256, 128), -jnp.inf, jnp.float32)
-    top = wide_tops(own_unit, protos, top, (stages[1],), 0, 0, count // 2, 4)
-    top_copies = wide_tops(own_unit, protos, top, (stages[2],), devices, count // 2, count // 2, 4)
-    all_tops = all_to_all(top_copies, BOTH)
-    tops = jnp.max(all_tops.reshape(batch_size, proto_size, 256)[:, :, :group_rows], axis=1)
-    tops = bit_reversed(tops, batch_size).reshape(batch_size, 2, group_rows // 2)
-    base = jnp.transpose(tops, (1, 0, 2)).reshape(1, crops_total) * -teacher_rate
+    top = wide_tops(own_unit, protos, top, (), 0, count // 2, 4)
 
     crops_x = swap(crops, "proto", 2)
     rows = [crops, crops_x, swap(crops, "proto", 1), swap(crops_x, "proto", 1)]
     third_x = swap(w_third, "proto", 2)
     thirds = [w_third, third_x, swap(w_third, "proto", 1), swap(third_x, "proto", 1)]
-    keep, give = student_front(proto_ref, b_first, rows, w_first, w_second, (top,))
+    keep, give = student_front(proto_ref, b_first, rows, w_first, w_second, (top, stages[1]))
+    top = wide_tops(own_unit, protos, top, (stages[2], give), count // 2, count // 2, 4)
+    all_tops = all_to_all(spread_tops(top, (mine,), devices), BOTH)
+    tops = jnp.max(all_tops.reshape(batch_size, proto_size, 256)[:, :, :group_rows], axis=1)
+    tops = bit_reversed(tops, batch_size).reshape(batch_size, 2, group_rows // 2)
+    base = jnp.transpose(tops, (1, 0, 2)).reshape(1, crops_total) * -teacher_rate
+
     core_rows = swap(give, "proto", 1)
     x_sent = keep[share_rows:] + core_rows[share_rows:]
     x_rows = swap(x_sent, "proto", 2)

time: 107 us -> 107 us (level)
  starting transfers between devices: 34.4 us -> 32 us
  waiting for transfers between devices: 21 us -> 23.3 us
    ppermute x20, waiting for transfers between devices: 7.65 us -> 10 us  [swap(): lax.ppermute(values, axis, [(i, i ^ flip) for i in range(lax.axis_size(ax...]
    all_to_all x4, starting transfers between devices: 16.4 us -> 14.9 us  [all_to_all(): return lax.all_to_all(copies, axes, 0, 0, tiled=True)]
    pallas_call x2 -> x3, Pallas kernels: 7.32 us -> 7.33 us  [the longest x2 6.59 us: wide_tops(): pl.pallas_call(skipping(functools.partial(wide_tops_kernel, first_row), 3...]
  transfers between devices with their start and end apart: 24 -> 24, of which waited for: 9 -> 9; matrix products, arithmetic and copies ran while one was open for 1% -> 1% of each run, Pallas kernels for 42% -> 38%
where the time goes in v9:
time: 107 us; the launch traced here: 106 us
  Pallas kernels  50 us (47%)
  starting transfers between devices  32 us (30%)
  waiting for transfers between devices  23.3 us (22%)
    ppermute x20, starting transfers between devices, swap(): lax.ppermute(values, axis, [(i, i ^ flip) for i in range(lax.axis_size(ax...  17.1 us
    all_to_all x4, starting transfers between devices, all_to_all(): return lax.all_to_all(copies, axes, 0, 0, tiled=True)  14.9 us
    all_to_all x4, waiting for transfers between devices, all_to_all(): return lax.all_to_all(copies, axes, 0, 0, tiled=True)  13.3 us
    pallas_call x2, Pallas kernels, attract(): pl.pallas_call(functools.partial(attract_kernel, first_row, outputs > 1),...  10.2 us
    ppermute x20, waiting for transfers between devices, swap(): lax.ppermute(values, axis, [(i, i ^ flip) for i in range(lax.axis_size(ax...  10 us
    pallas_call x1, Pallas kernels, repel(): pl.pallas_call(skipping(functools.partial(repel_kernel, proto_size), 5, l...  9.44 us
    pallas_call x1, Pallas kernels, first_sweep(): pl.pallas_call(skipping(functools.partial(first_sweep_kernel, chunk, prot...  6.71 us
    pallas_call x2, Pallas kernels, wide_tops(): pl.pallas_call(skipping(functools.partial(wide_tops_kernel, first_row), 3...  6.59 us
  transfers between devices with their start and end apart: 24, of which 9 were waited for; matrix products, arithmetic and copies ran while one was open for 1% of the time, Pallas kernels for 38%

profile of v9, /device:TPU:0, one launch (start us, length us, event | category | flops | bytes accessed | tf_op | source)
XLA Modules:
  0.0 106.4 jit_solution(17420582382648592275)
XLA Ops:
  0.0 2.9 %collective-permute-start = (bf16[48,1536]{1,0:T(8,128)(2,1)}, bf16[48,1536]{1,0:T(8,128)(2,1)S(1)}, u32[]{:S(2)}, u32[]{:S(2)}) collective-permute-start(bf16[48,1536]{1,0:T(8,128)(2,1)} %refs_2_.1), channel_id=1, source_target_pairs={{0,2},{1,3},{2,0},{3,1},{4,6},{5,7},{6,4},{7,5},{8,10},{9,11},{10,... | collective-permute-start | bytes 442376 | tf_op jit(solution)/shard_map/ppermute | solution.py:668
  2.9 0.0 collective-permute-start.1
  2.9 1.0 teacher_units.1
  4.0 2.7 %collective-permute-start.3 = (bf16[96,256]{1,0:T(8,128)(2,1)S(1)}, bf16[96,256]{1,0:T(8,128)(2,1)S(1)}, u32[]{:S(2)}, u32[]{:S(2)}) collective-permute-start(bf16[96,256]{1,0:T(8,128)(2,1)S(1)} %get-tuple-element.23), channel_id=1, source_target_pairs={{0,16},{4,20},{8,24},{12,28},{16,0},{20,4},{24,8},{28,12},{1,17},{... | collective-permute-start | bytes 147464 | tf_op jit(solution)/shard_map/ppermute | solution.py:668
  6.6 0.4 collective-permute-done.refs_3_
  7.0 0.0 collective-permute-start.2
  7.0 3.3 %wide_tops.2.refs_8_.refs_2_ = f32[256,128]{1,0:T(8,128)S(1)} custom-call(bf16[192,256]{1,0:T(8,128)(2,1)S(1)} %get-tuple-element.22.refs_0_.refs_1_, bf16[16384,256]{1,0:T(8,128)(2,1)} %refs_4_.1, f32[256,128]{1,0:T(8,128)S(1)} %broadcast_in_dim.7.refs_2_), custom_call_target="tpu_custom_call" | custom-call | flops 805306368 | bytes 4194304 | tf_op jit(solution)/shard_map/wide_tops/pallas_call | solution.py:132
  10.4 0.0 collective-permute-done.3
  10.4 0.0 collective-permute-done.1.refs_4_
  10.4 0.0 collective-permute-done.2.refs_5_
  10.4 4.8 %student_front.1 = (f32[96,2048]{1,0:T(8,128)S(1)}, f32[96,2048]{1,0:T(8,128)}) custom-call(s32[1]{0:T(128)} %bitcast.refs_0_.index_ref, f32[1,2048]{1,0:T(1,128)} %bitcast.10, bf16[48,1536]{1,0:T(8,128)(2,1)} %refs_2_.1, bf16[48,1536]{1,0:T(8,128)(2,1)S(1)} %collective-permute-done.refs_3_, bf16[48,1536]{1,0:T(8,128)(2,1)S(1)} %collective-permute-done.1.refs_4_, ...), custom_call_target="tpu_custom_call" | custom-call | flops 704643072 | bytes 3670016 | tf_op jit(solution)/shard_map/student_front/pallas_call | solution.py:575
  15.3 0.6 collective-permute-start.4
  15.8 1.8 %collective-permute-start.14 = (bf16[192,256]{1,0:T(8,128)(2,1)S(1)}, bf16[192,256]{1,0:T(8,128)(2,1)S(1)}, u32[]{:S(2)}, u32[]{:S(2)}) collective-permute-start(bf16[192,256]{1,0:T(8,128)(2,1)S(1)} %maximum_select_fusion.2.refs_9_), channel_id=1, source_target_pairs={{0,8},{4,12},{8,0},{12,4},{16,24},{20,28},{24,16},{28,20},{1,9},{5... | collective-permute-start | bytes 294920 | tf_op jit(solution)/shard_map/ppermute | solution.py:668
  17.7 3.0 %collective-permute-done.14 = bf16[192,256]{1,0:T(8,128)(2,1)S(1)} collective-permute-done((bf16[192,256]{1,0:T(8,128)(2,1)S(1)}, bf16[192,256]{1,0:T(8,128)(2,1)S(1)}, u32[]{:S(2)}, u32[]{:S(2)}) %collective-permute-start.14) | collective-permute-done | bytes 98336 | tf_op jit(solution)/shard_map/ppermute | solution.py:668
  20.7 0.1 maximum_select_fusion.1.refs_3_
  20.8 1.7 %collective-permute-start.15 = (bf16[384,256]{1,0:T(8,128)(2,1)S(1)}, bf16[384,256]{1,0:T(8,128)(2,1)S(1)}, u32[]{:S(2)}, u32[]{:S(2)}) collective-permute-start(bf16[384,256]{1,0:T(8,128)(2,1)S(1)} %maximum_select_fusion.1.refs_3_), channel_id=1, source_target_pairs={{0,4},{4,0},{8,12},{12,8},{16,20},{20,16},{24,28},{28,24},{1,5},{5... | collective-permute-start | bytes 589832 | tf_op jit(solution)/shard_map/ppermute | solution.py:668
  22.5 1.5 %collective-permute-start.6 = (bf16[512,256]{1,0:T(8,128)(2,1)}, bf16[512,256]{1,0:T(8,128)(2,1)}, u32[]{:S(2)}, u32[]{:S(2)}) collective-permute-start(bf16[512,256]{1,0:T(8,128)(2,1)} %own_ref.1), channel_id=1, source_target_pairs={{0,2},{1,3},{2,0},{3,1},{4,6},{5,7},{6,4},{7,5},{8,10},{9,11},{10,... | collective-permute-start | bytes 786440 | tf_op jit(solution)/shard_map/ppermute | solution.py:668
  24.0 3.3 %wide_tops.3.refs_0_ = f32[256,128]{1,0:T(8,128)S(1)} custom-call(bf16[192,256]{1,0:T(8,128)(2,1)S(1)} %get-tuple-element.22.refs_0_.refs_1_, bf16[16384,256]{1,0:T(8,128)(2,1)} %refs_4_.1, f32[256,128]{1,0:T(8,128)S(1)} %wide_tops.2.refs_8_.refs_2_, bf16[384,256]{1,0:T(8,128)(2,1)S(1)} %maximum_select_fusion.1.refs_3_, f32[96,2048]{1,0:T(8,128)} %get-tuple-element.25.refs_4_), custom_call_target="tpu_custom_call" | custom-call | flops 805306368 | bytes 4194304 | tf_op jit(solution)/shard_map/wide_tops/pallas_call | solution.py:132
  27.3 0.0 collective-permute-done.15
  27.3 0.2 maximum_select_fusion.refs_1_.refs_2_
  27.5 0.1 collective-permute-start.7
  27.6 0.7 spread_tops.1
  28.3 5.7 %all-to-all-start = ((f32[32,1,256]{2,1,0:T(1,128)}), f32[32,1,256]{2,1,0:T(1,128)S(1)}, u32[]{:S(2)}, u32[]{:S(2)}) async-start(f32[32,1,256]{2,1,0:T(1,128)} %spread_tops.1), calls=%async_computation | async-start | bytes 65536 | tf_op jit(solution)/shard_map/all_to_all | solution.py:697
  34.0 0.1 pad_add_fusion.1.refs_0_
  34.1 0.0 collective-permute-done.6.partner_ref
  34.1 0.3 collective-permute-start.8
  34.3 0.3 collective-permute-start.16
  34.6 6.6 %all-to-all-done.refs_2_ = f32[32,1,256]{2,1,0:T(1,128)S(1)} async-done(((f32[32,1,256]{2,1,0:T(1,128)}), f32[32,1,256]{2,1,0:T(1,128)S(1)}, u32[]{:S(2)}, u32[]{:S(2)}) %all-to-all-start) | async-done | bytes 32800 | tf_op jit(solution)/shard_map/all_to_all | solution.py:697
  41.2 0.1 reduce
  41.4 0.0 collective-permute-done.4.core_ref
  41.4 0.6 collective-permute-start.5
  42.0 0.1 mul.17
  42.1 0.1 mul.19.refs_4_
  42.2 0.0 collective-permute-done.8.last_ref.refs_7_
  42.2 6.7 %first_sweep.1 = (bf16[32,16,128]{2,1,0:T(8,128)(2,1)}, bf16[2048,1536]{1,0:T(8,128)(2,1)}) custom-call(s32[2]{0:T(128)S(1)} %pad_add_fusion.1.refs_0_, bf16[16384,256]{1,0:T(8,128)(2,1)} %refs_4_.1, bf16[768,256]{1,0:T(8,128)(2,1)S(1)} %maximum_select_fusion.refs_1_.refs_2_, bf16[768,256]{1,0:T(8,128)(2,1)} %collective-permute-done.16.refs_3_, ...), custom_call_target="tpu_custom_call" | custom-call | flops 1610612736 | bytes 6291456 | tf_op jit(solution)/shard_map/first_sweep/pallas_call | solution.py:402
  48.9 2.6 %all-to-all-start.1 = ((bf16[32,16,128]{2,1,0:T(8,128)(2,1)}), bf16[32,16,128]{2,1,0:T(8,128)(2,1)S(1)}, u32[]{:S(2)}, u32[]{:S(2)}) async-start(bf16[32,16,128]{2,1,0:T(8,128)(2,1)} %get-tuple-element.34), calls=%async_computation.1 | async-start | bytes 262144 | tf_op jit(solution)/shard_map/all_to_all | solution.py:697
  51.5 0.1 pad_add_fusion.refs_0_
  51.6 1.0 collective-permute-done.5.x_ref
  52.6 1.6 %student_middle.1 = (f32[48,256]{1,0:T(8,128)S(1)}, bf16[48,256]{1,0:T(8,128)(2,1)S(1)}, f32[48,128]{1,0:T(8,128)S(1)}) custom-call(s32[1]{0:T(128)} %bitcast.refs_0_.index_ref, f32[96,2048]{1,0:T(8,128)S(1)} %get-tuple-element.24.keep_ref, f32[96,2048]{1,0:T(8,128)S(1)} %collective-permute-done.4.core_ref, f32[48,2048]{1,0:T(8,128)S(1)} %collective-permute-done.5.x_ref, ...), custom_call_target="tpu_custom_call" | custom-call | flops 50331648 | bytes 2621440 | tf_op jit(solution)/shard_map/student_middle/pallas_call | solution.py:616
  54.2 0.7 collective-permute-start.9
  54.9 4.8 %all-to-all-done.1.refs_1_ = bf16[32,16,128]{2,1,0:T(8,128)(2,1)S(1)} async-done(((bf16[32,16,128]{2,1,0:T(8,128)(2,1)}), bf16[32,16,128]{2,1,0:T(8,128)(2,1)S(1)}, u32[]{:S(2)}, u32[]{:S(2)}) %all-to-all-start.1) | async-done | bytes 131104 | tf_op jit(solution)/shard_map/all_to_all | solution.py:697
  59.7 4.4 %next_sweep.1 = bf16[32,16,128]{2,1,0:T(8,128)(2,1)} custom-call(bf16[2048,1536]{1,0:T(8,128)(2,1)} %get-tuple-element.33.refs_0_, bf16[32,16,128]{2,1,0:T(8,128)(2,1)S(1)} %all-to-all-done.1.refs_1_, bf16[48,256]{1,0:T(8,128)(2,1)S(1)} %get-tuple-element.28.refs_2_), custom_call_target="tpu_custom_call" | custom-call | flops 25165824 | bytes 6291456 | tf_op jit(solution)/shard_map/next_sweep/pallas_call | solution.py:487
  64.1 2.6 %all-to-all-start.2 = ((bf16[32,16,128]{2,1,0:T(8,128)(2,1)}), bf16[32,16,128]{2,1,0:T(8,128)(2,1)S(1)}, u32[]{:S(2)}, u32[]{:S(2)}) async-start(bf16[32,16,128]{2,1,0:T(8,128)(2,1)} %next_sweep.1), calls=%async_computation.2 | async-start | bytes 262144 | tf_op jit(solution)/shard_map/all_to_all | solution.py:697
  66.7 0.0 collective-permute-done.9
  66.7 0.2 collective-permute-start.10
  66.9 1.1 %collective-permute-done.10 = bf16[96,256]{1,0:T(8,128)(2,1)S(1)} collective-permute-done((bf16[96,256]{1,0:T(8,128)(2,1)S(1)}, bf16[96,256]{1,0:T(8,128)(2,1)S(1)}, u32[]{:S(2)}, u32[]{:S(2)}) %collective-permute-start.10) | collective-permute-done | bytes 49184 | tf_op jit(solution)/shard_map/ppermute | solution.py:668
  68.1 5.0 %attract.2.state_ref.refs_2_ = f32[192,512]{1,0:T(8,128)S(1)} custom-call(bf16[192,256]{1,0:T(8,128)(2,1)S(1)} %constant_dynamic-update-slice_fusion.emb_ref, f32[192,512]{1,0:T(8,128)S(1)} %concatenate.35.state_ref, bf16[16384,256]{1,0:T(8,128)(2,1)} %refs_4_.1), custom_call_target="tpu_custom_call" | custom-call | flops 1610612736 | bytes 4194304 | tf_op jit(solution)/shard_map/attract/pallas_call | solution.py:292
  73.1 1.8 %all-to-all-done.2.refs_1_ = bf16[32,16,128]{2,1,0:T(8,128)(2,1)S(1)} async-done(((bf16[32,16,128]{2,1,0:T(8,128)(2,1)}), bf16[32,16,128]{2,1,0:T(8,128)(2,1)S(1)}, u32[]{:S(2)}, u32[]{:S(2)}) %all-to-all-start.2) | async-done | bytes 131104 | tf_op jit(solution)/shard_map/all_to_all | solution.py:697
  74.9 3.8 %last_scales.1 = f32[8,1,2048]{2,1,0:T(1,128)} custom-call(bf16[2048,1536]{1,0:T(8,128)(2,1)} %get-tuple-element.33.refs_0_, bf16[32,16,128]{2,1,0:T(8,128)(2,1)S(1)} %all-to-all-done.2.refs_1_, f32[192,512]{1,0:T(8,128)S(1)} %attract.2.state_ref.refs_2_), custom_call_target="tpu_custom_call" | custom-call | flops 12582912 | bytes 6291456 | tf_op jit(solution)/shard_map/last_scales/pallas_call | solution.py:526
  78.7 4.0 %all-to-all-start.3 = ((f32[8,1,2048]{2,1,0:T(1,128)}), f32[8,1,2048]{2,1,0:T(1,128)S(1)}, u32[]{:S(2)}, u32[]{:S(2)}) async-start(f32[8,1,2048]{2,1,0:T(1,128)} %last_scales.1), calls=%async_computation.3 | async-start | bytes 131072 | tf_op jit(solution)/shard_map/all_to_all | solution.py:697
  82.8 5.1 %attract.3 = (f32[48,512]{1,0:T(8,128)S(1)}, f32[48,512]{1,0:T(8,128)S(1)}, f32[48,512]{1,0:T(8,128)S(1)}, f32[48,512]{1,0:T(8,128)S(1)}) custom-call(bf16[192,256]{1,0:T(8,128)(2,1)S(1)} %constant_dynamic-update-slice_fusion.emb_ref, f32[192,512]{1,0:T(8,128)S(1)} %attract.2.state_ref.refs_2_, bf16[16384,256]{1,0:T(8,128)(2,1)} %refs_4_.1), custom_call_target="tpu_custom_call" | custom-call | flops 1610612736 | bytes 4194304 | tf_op jit(solution)/shard_map/attract/pallas_call | solution.py:292
  87.9 0.1 collective-permute-start.11
  87.9 1.5 %collective-permute-start.12 = (f32[48,512]{1,0:T(8,128)S(1)}, f32[48,512]{1,0:T(8,128)S(1)}, u32[]{:S(2)}, u32[]{:S(2)}) collective-permute-start(f32[48,512]{1,0:T(8,128)S(1)} %get-tuple-element.31), channel_id=1, source_target_pairs={{0,2},{1,3},{2,0},{3,1},{4,6},{5,7},{6,4},{7,5},{8,10},{9,11},{10,... | collective-permute-start | bytes 294920 | tf_op jit(solution)/shard_map/ppermute | solution.py:668
  89.5 0.3 collective-permute-start.13
  89.8 9.4 %repel.1 = (f32[48,384]{1,0:T(8,128)S(1)}, f32[48,384]{1,0:T(8,128)S(1)}, f32[48,384]{1,0:T(8,128)S(1)}, f32[48,384]{1,0:T(8,128)S(1)}) custom-call(s32[2]{0:T(128)S(1)} %pad_add_fusion.refs_0_, bf16[192,256]{1,0:T(8,128)(2,1)S(1)} %get-tuple-element.22.refs_0_.refs_1_, f32[32,1,256]{2,1,0:T(1,128)S(1)} %all-to-all-done.refs_2_, ...), custom_call_target="tpu_custom_call" | custom-call | flops 3221225472 | bytes 8388608 | tf_op jit(solution)/shard_map/repel/pallas_call | solution.py:214
  99.3 0.4 collective-permute-start.17
  99.7 1.5 %collective-permute-start.18 = (f32[48,384]{1,0:T(8,128)S(1)}, f32[48,384]{1,0:T(8,128)S(1)}, u32[]{:S(2)}, u32[]{:S(2)}) collective-permute-start(f32[48,384]{1,0:T(8,128)S(1)} %get-tuple-element.37), channel_id=1, source_target_pairs={{0,2},{1,3},{2,0},{3,1},{4,6},{5,7},{6,4},{7,5},{8,10},{9,11},{10,... | collective-permute-start | bytes 221192 | tf_op jit(solution)/shard_map/ppermute | solution.py:668
  101.1 0.0 collective-permute-start.19
  101.2 0.0 collective-permute-done.12.rest_2_
  101.2 0.0 collective-permute-done.13.rest_3_
  101.2 0.0 collective-permute-done.17.rest_5_
  101.2 2.8 %collective-permute-done.18.rest_6_ = f32[48,384]{1,0:T(8,128)S(1)} collective-permute-done((f32[48,384]{1,0:T(8,128)S(1)}, f32[48,384]{1,0:T(8,128)S(1)}, u32[]{:S(2)}, u32[]{:S(2)}) %collective-permute-start.18) | collective-permute-done | bytes 73760 | tf_op jit(solution)/shard_map/ppermute | solution.py:668
  104.0 1.6 %collective-permute-done.19.rest_7_ = f32[48,384]{1,0:T(8,128)S(1)} collective-permute-done((f32[48,384]{1,0:T(8,128)S(1)}, f32[48,384]{1,0:T(8,128)S(1)}, u32[]{:S(2)}, u32[]{:S(2)}) %collective-permute-start.19) | collective-permute-done | bytes 73760 | tf_op jit(solution)/shard_map/ppermute | solution.py:668
  105.6 0.8 finish.1
  (20 shorter events, 0.2 us)
Async XLA Ops:
  0.0 7.0 %collective-permute-start = (bf16[48,1536]{1,0:T(8,128)(2,1)}, bf16[48,1536]{1,0:T(8,128)(2,1)S(1)}, u32[]{:S(2)}, u32[]{:S(2)}) collective-permute-start(bf16[48,1536]{1,0:T(8,128)(2,1)} %refs_2_.1), channel_id=1, source_target_pairs={{0,2},{1,3},{2,0},{3,1},{4,6},{5,7},{6,4},{7,5},{8,10},{9,11},{10,... | collective-permute-start | bytes 442376 | tf_op jit(solution)/shard_map/ppermute | solution.py:668
  2.9 7.5 %collective-permute-start.1 = (bf16[48,1536]{1,0:T(8,128)(2,1)}, bf16[48,1536]{1,0:T(8,128)(2,1)S(1)}, u32[]{:S(2)}, u32[]{:S(2)}) collective-permute-start(bf16[48,1536]{1,0:T(8,128)(2,1)} %refs_2_.1), channel_id=1, source_target_pairs={{0,1},{1,0},{2,3},{3,2},{4,5},{5,4},{6,7},{7,6},{8,9},{9,8},{10,11... | collective-permute-start | bytes 442376 | tf_op jit(solution)/shard_map/ppermute | solution.py:668
  4.0 6.4 %collective-permute-start.3 = (bf16[96,256]{1,0:T(8,128)(2,1)S(1)}, bf16[96,256]{1,0:T(8,128)(2,1)S(1)}, u32[]{:S(2)}, u32[]{:S(2)}) collective-permute-start(bf16[96,256]{1,0:T(8,128)(2,1)S(1)} %get-tuple-element.23), channel_id=1, source_target_pairs={{0,16},{4,20},{8,24},{12,28},{16,0},{20,4},{24,8},{28,12},{1,17},{... | collective-permute-start | bytes 147464 | tf_op jit(solution)/shard_map/ppermute | solution.py:668
  7.0 3.4 %collective-permute-start.2 = (bf16[48,1536]{1,0:T(8,128)(2,1)S(1)}, bf16[48,1536]{1,0:T(8,128)(2,1)S(1)}, u32[]{:S(2)}, u32[]{:S(2)}) collective-permute-start(bf16[48,1536]{1,0:T(8,128)(2,1)S(1)} %collective-permute-done.refs_3_), channel_id=1, source_target_pairs={{0,1},{1,0},{2,3},{3,2},{4,5},{5,4},{6,7},{7,6},{8,9},{9,8},{10,11... | collective-permute-start | bytes 442376 | tf_op jit(solution)/shard_map/ppermute | solution.py:668
  15.3 26.1 %collective-permute-start.4 = (f32[96,2048]{1,0:T(8,128)}, f32[96,2048]{1,0:T(8,128)S(1)}, u32[]{:S(2)}, u32[]{:S(2)}) collective-permute-start(f32[96,2048]{1,0:T(8,128)} %get-tuple-element.25.refs_4_), channel_id=1, source_target_pairs={{0,1},{1,0},{2,3},{3,2},{4,5},{5,4},{6,7},{7,6},{8,9},{9,8},{10,11... | collective-permute-start | bytes 2359304 | tf_op jit(solution)/shard_map/ppermute | solution.py:668
  15.8 4.9 %collective-permute-start.14 = (bf16[192,256]{1,0:T(8,128)(2,1)S(1)}, bf16[192,256]{1,0:T(8,128)(2,1)S(1)}, u32[]{:S(2)}, u32[]{:S(2)}) collective-permute-start(bf16[192,256]{1,0:T(8,128)(2,1)S(1)} %maximum_select_fusion.2.refs_9_), channel_id=1, source_target_pairs={{0,8},{4,12},{8,0},{12,4},{16,24},{20,28},{24,16},{28,20},{1,9},{5... | collective-permute-start | bytes 294920 | tf_op jit(solution)/shard_map/ppermute | solution.py:668
  20.8 6.5 %collective-permute-start.15 = (bf16[384,256]{1,0:T(8,128)(2,1)S(1)}, bf16[384,256]{1,0:T(8,128)(2,1)S(1)}, u32[]{:S(2)}, u32[]{:S(2)}) collective-permute-start(bf16[384,256]{1,0:T(8,128)(2,1)S(1)} %maximum_select_fusion.1.refs_3_), channel_id=1, source_target_pairs={{0,4},{4,0},{8,12},{12,8},{16,20},{20,16},{24,28},{28,24},{1,5},{5... | collective-permute-start | bytes 589832 | tf_op jit(solution)/shard_map/ppermute | solution.py:668
  22.5 11.5 %collective-permute-start.6 = (bf16[512,256]{1,0:T(8,128)(2,1)}, bf16[512,256]{1,0:T(8,128)(2,1)}, u32[]{:S(2)}, u32[]{:S(2)}) collective-permute-start(bf16[512,256]{1,0:T(8,128)(2,1)} %own_ref.1), channel_id=1, source_target_pairs={{0,2},{1,3},{2,0},{3,1},{4,6},{5,7},{6,4},{7,5},{8,10},{9,11},{10,... | collective-permute-start | bytes 786440 | tf_op jit(solution)/shard_map/ppermute | solution.py:668
  27.5 14.7 %collective-permute-start.7 = (bf16[512,256]{1,0:T(8,128)(2,1)}, bf16[512,256]{1,0:T(8,128)(2,1)S(1)}, u32[]{:S(2)}, u32[]{:S(2)}) collective-permute-start(bf16[512,256]{1,0:T(8,128)(2,1)} %own_ref.1), channel_id=1, source_target_pairs={{0,1},{1,0},{2,3},{3,2},{4,5},{5,4},{6,7},{7,6},{8,9},{9,8},{10,11... | collective-permute-start | bytes 786440 | tf_op jit(solution)/shard_map/ppermute | solution.py:668
  28.3 12.9 %all-to-all-start = ((f32[32,1,256]{2,1,0:T(1,128)}), f32[32,1,256]{2,1,0:T(1,128)S(1)}, u32[]{:S(2)}, u32[]{:S(2)}) async-start(f32[32,1,256]{2,1,0:T(1,128)} %spread_tops.1), calls=%async_computation | async-start | bytes 65536 | tf_op jit(solution)/shard_map/all_to_all | solution.py:697
  34.1 8.1 %collective-permute-start.8 = (bf16[512,256]{1,0:T(8,128)(2,1)}, bf16[512,256]{1,0:T(8,128)(2,1)S(1)}, u32[]{:S(2)}, u32[]{:S(2)}) collective-permute-start(bf16[512,256]{1,0:T(8,128)(2,1)} %collective-permute-done.6.partner_ref), channel_id=1, source_target_pairs={{0,1},{1,0},{2,3},{3,2},{4,5},{5,4},{6,7},{7,6},{8,9},{9,8},{10,11... | collective-permute-start | bytes 786440 | tf_op jit(solution)/shard_map/ppermute | solution.py:668
  34.3 7.9 %collective-permute-start.16 = (bf16[768,256]{1,0:T(8,128)(2,1)S(1)}, bf16[768,256]{1,0:T(8,128)(2,1)}, u32[]{:S(2)}, u32[]{:S(2)}) collective-permute-start(bf16[768,256]{1,0:T(8,128)(2,1)S(1)} %maximum_select_fusion.refs_1_.refs_2_), channel_id=1, source_target_pairs={{0,1},{1,0},{2,3},{3,2},{4,5},{5,4},{6,7},{7,6},{8,9},{9,8},{10,11... | collective-permute-start | bytes 1179656 | tf_op jit(solution)/shard_map/ppermute | solution.py:668
  41.4 11.2 %collective-permute-start.5 = (f32[48,2048]{1,0:T(8,128)S(1)}, f32[48,2048]{1,0:T(8,128)S(1)}, u32[]{:S(2)}, u32[]{:S(2)}) collective-permute-start(f32[48,2048]{1,0:T(8,128)S(1)} %slice_add_fusion.refs_5_), channel_id=1, source_target_pairs={{0,2},{1,3},{2,0},{3,1},{4,6},{5,7},{6,4},{7,5},{8,10},{9,11},{10,... | collective-permute-start | bytes 1179656 | tf_op jit(solution)/shard_map/ppermute | solution.py:668
  48.9 10.8 %all-to-all-start.1 = ((bf16[32,16,128]{2,1,0:T(8,128)(2,1)}), bf16[32,16,128]{2,1,0:T(8,128)(2,1)S(1)}, u32[]{:S(2)}, u32[]{:S(2)}) async-start(bf16[32,16,128]{2,1,0:T(8,128)(2,1)} %get-tuple-element.34), calls=%async_computation.1 | async-start | bytes 262144 | tf_op jit(solution)/shard_map/all_to_all | solution.py:697
  54.2 12.5 %collective-permute-start.9 = (bf16[48,256]{1,0:T(8,128)(2,1)S(1)}, bf16[48,256]{1,0:T(8,128)(2,1)S(1)}, u32[]{:S(2)}, u32[]{:S(2)}) collective-permute-start(bf16[48,256]{1,0:T(8,128)(2,1)S(1)} %get-tuple-element.28.refs_2_), channel_id=1, source_target_pairs={{0,2},{1,3},{2,0},{3,1},{4,6},{5,7},{6,4},{7,5},{8,10},{9,11},{10,... | collective-permute-start | bytes 73736 | tf_op jit(solution)/shard_map/ppermute | solution.py:668
  64.1 10.8 %all-to-all-start.2 = ((bf16[32,16,128]{2,1,0:T(8,128)(2,1)}), bf16[32,16,128]{2,1,0:T(8,128)(2,1)S(1)}, u32[]{:S(2)}, u32[]{:S(2)}) async-start(bf16[32,16,128]{2,1,0:T(8,128)(2,1)} %next_sweep.1), calls=%async_computation.2 | async-start | bytes 262144 | tf_op jit(solution)/shard_map/all_to_all | solution.py:697
  66.7 1.3 %collective-permute-start.10 = (bf16[96,256]{1,0:T(8,128)(2,1)S(1)}, bf16[96,256]{1,0:T(8,128)(2,1)S(1)}, u32[]{:S(2)}, u32[]{:S(2)}) collective-permute-start(bf16[96,256]{1,0:T(8,128)(2,1)S(1)} %pad_maximum_fusion), channel_id=1, source_target_pairs={{0,1},{1,0},{2,3},{3,2},{4,5},{5,4},{6,7},{7,6},{8,9},{9,8},{10,11... | collective-permute-start | bytes 147464 | tf_op jit(solution)/shard_map/ppermute | solution.py:668
  78.7 11.1 %all-to-all-start.3 = ((f32[8,1,2048]{2,1,0:T(1,128)}), f32[8,1,2048]{2,1,0:T(1,128)S(1)}, u32[]{:S(2)}, u32[]{:S(2)}) async-start(f32[8,1,2048]{2,1,0:T(1,128)} %last_scales.1), calls=%async_computation.3 | async-start | bytes 131072 | tf_op jit(solution)/shard_map/all_to_all | solution.py:697
  87.9 13.3 %collective-permute-start.11 = (f32[48,512]{1,0:T(8,128)S(1)}, f32[48,512]{1,0:T(8,128)S(1)}, u32[]{:S(2)}, u32[]{:S(2)}) collective-permute-start(f32[48,512]{1,0:T(8,128)S(1)} %get-tuple-element.30), channel_id=1, source_target_pairs={{0,1},{1,0},{2,3},{3,2},{4,5},{5,4},{6,7},{7,6},{8,9},{9,8},{10,11... | collective-permute-start | bytes 294920 | tf_op jit(solution)/shard_map/ppermute | solution.py:668
  87.9 13.3 %collective-permute-start.12 = (f32[48,512]{1,0:T(8,128)S(1)}, f32[48,512]{1,0:T(8,128)S(1)}, u32[]{:S(2)}, u32[]{:S(2)}) collective-permute-start(f32[48,512]{1,0:T(8,128)S(1)} %get-tuple-element.31), channel_id=1, source_target_pairs={{0,2},{1,3},{2,0},{3,1},{4,6},{5,7},{6,4},{7,5},{8,10},{9,11},{10,... | collective-permute-start | bytes 294920 | tf_op jit(solution)/shard_map/ppermute | solution.py:668
  89.5 11.7 %collective-permute-start.13 = (f32[48,512]{1,0:T(8,128)S(1)}, f32[48,512]{1,0:T(8,128)S(1)}, u32[]{:S(2)}, u32[]{:S(2)}) collective-permute-start(f32[48,512]{1,0:T(8,128)S(1)} %get-tuple-element.32), channel_id=1, source_target_pairs={{0,3},{1,2},{2,1},{3,0},{4,7},{5,6},{6,5},{7,4},{8,11},{9,10},{10,... | collective-permute-start | bytes 294920 | tf_op jit(solution)/shard_map/ppermute | solution.py:668
  99.3 2.0 %collective-permute-start.17 = (f32[48,384]{1,0:T(8,128)S(1)}, f32[48,384]{1,0:T(8,128)S(1)}, u32[]{:S(2)}, u32[]{:S(2)}) collective-permute-start(f32[48,384]{1,0:T(8,128)S(1)} %get-tuple-element.36), channel_id=1, source_target_pairs={{0,1},{1,0},{2,3},{3,2},{4,5},{5,4},{6,7},{7,6},{8,9},{9,8},{10,11... | collective-permute-start | bytes 221192 | tf_op jit(solution)/shard_map/ppermute | solution.py:668
  99.7 4.4 %collective-permute-start.18 = (f32[48,384]{1,0:T(8,128)S(1)}, f32[48,384]{1,0:T(8,128)S(1)}, u32[]{:S(2)}, u32[]{:S(2)}) collective-permute-start(f32[48,384]{1,0:T(8,128)S(1)} %get-tuple-element.37), channel_id=1, source_target_pairs={{0,2},{1,3},{2,0},{3,1},{4,6},{5,7},{6,4},{7,5},{8,10},{9,11},{10,... | collective-permute-start | bytes 221192 | tf_op jit(solution)/shard_map/ppermute | solution.py:668
  101.1 4.5 %collective-permute-start.19 = (f32[48,384]{1,0:T(8,128)S(1)}, f32[48,384]{1,0:T(8,128)S(1)}, u32[]{:S(2)}, u32[]{:S(2)}) collective-permute-start(f32[48,384]{1,0:T(8,128)S(1)} %get-tuple-element.38), channel_id=1, source_target_pairs={{0,3},{1,2},{2,1},{3,0},{4,7},{5,6},{6,5},{7,4},{8,11},{9,10},{10,... | collective-permute-start | bytes 221192 | tf_op jit(solution)/shard_map/ppermute | solution.py:668

commit v10 on v9

--- a/solution.py
+++ b/solution.py
@@ -107,12 +107,24 @@
     )(core, in_hbm(teacher_emb))
 
 
-def wide_tops_kernel(first_row, unit_ref, protos_hbm, before_ref, out_ref, protos_ref, sems, top_ref):
+def front_kernel(
+    index_ref, unit_ref, bias_ref, own_hbm, x_hbm, core_hbm, last_hbm, first_hbm, second_hbm, protos_hbm,
+    tops_ref, keep_ref, give_ref, first_ref, second_ref, rows_ref, protos_ref, top_ref, sems, chunk_sems,
+):
     rows = unit_ref.shape[0]
     steps, block = protos_ref.shape[:2]
     wide = min(WIDE, block)
-    arrived = fetch(protos_hbm, protos_ref, sems, first_row)
-    top_ref[...] = before_ref[...]
+    share = own_hbm.shape[0]
+    arrived = fetch(protos_hbm, protos_ref, chunk_sems)
+    copies = [
+        pltpu.make_async_copy(source, rows_ref.at[slot * share : (slot + 1) * share, :], sems.at[slot])
+        for slot, source in enumerate((own_hbm, x_hbm, core_hbm, last_hbm))
+    ]
+    copies.append(pltpu.make_async_copy(first_hbm, first_ref, sems.at[4]))
+    copies.append(pltpu.make_async_copy(second_hbm, second_ref, sems.at[5]))
+    for copy in copies:
+        copy.start()
+    top_ref[...] = jnp.full(top_ref.shape, -jnp.inf, jnp.float32)
 
     def step(index, carry):
         arrived(index)
@@ -124,74 +136,137 @@
         return carry
 
     lax.fori_loop(0, steps, step, 0)
-    out_ref[...] = top_ref[...]
-
-
-def wide_tops(unit, protos, before, order, first_row, count, steps):
-    rows, width = unit.shape
-    return pl.pallas_call(
-        skipping(functools.partial(wide_tops_kernel, first_row), 3, len(order)),
-        in_specs=[whole(), whole(pl.ANY), whole()] + [whole(pl.ANY)] * len(order),
-        out_specs=whole(),
-        out_shape=jax.ShapeDtypeStruct(before.shape, jnp.float32),
+    tops = jnp.max(jnp.transpose(top_ref[...]), axis=0, keepdims=True)
+    tops_ref[...] = jnp.broadcast_to(tops[None], tops_ref.shape)
+    for copy in copies:
+        copy.wait()
+    hidden = first_ref.shape[1]
+    bias = bias_ref[:, part(index_ref[0], hidden)]
+    h_first = gelu(
+        jnp.dot(rows_ref[...], first_ref[...], preferred_element_type=jnp.float32) + bias
+    ).astype(jnp.bfloat16)
+    for start in range(0, second_ref.shape[1], 512):
+        columns = slice(start, start + 512)
+        product = jnp.dot(h_first, second_ref[:, columns], preferred_element_type=jnp.float32)
+        keep_ref[:, columns] = product[: 2 * share]
+        give_ref[:, columns] = product[2 * share :]
+
+
+def front(index, unit, bias, rows, first, second, protos, order, copies, steps):
+    share, features = rows[0].shape
+    hidden, units = second.shape
+    count, width = protos.shape
+    return pl.pallas_call(
+        skipping(front_kernel, 10, len(order)),
+        in_specs=[whole(pltpu.SMEM), whole(), whole()] + [whole(pl.ANY)] * (7 + len(order)),
+        out_specs=[whole()] * 3,
+        out_shape=[jax.ShapeDtypeStruct((copies, 1, 256), jnp.float32)]
+        + [jax.ShapeDtypeStruct((2 * share, units), jnp.float32)] * 2,
         scratch_shapes=[
+            pltpu.VMEM(first.shape, jnp.bfloat16),
+            pltpu.VMEM(second.shape, jnp.bfloat16),
+            pltpu.VMEM((4 * share, features), jnp.bfloat16),
             pltpu.VMEM((steps, count // steps, width), jnp.bfloat16),
+            pltpu.VMEM((256, 128), jnp.float32),
+            pltpu.SemaphoreType.DMA((6,)),
             pltpu.SemaphoreType.DMA((steps,)),
-            pltpu.VMEM((256, 128), jnp.float32),
-        ],
-        compiler_params=params(16),
-        cost_estimate=cost(2 * rows * width * count, 2 * width * count),
-        name="wide_tops",
-    )(unit, in_hbm(protos), before, *order)
-
-
-def spread_tops_kernel(top_ref, out_ref):
-    tops = jnp.max(jnp.transpose(top_ref[...]), axis=0, keepdims=True)
-    out_ref[...] = jnp.broadcast_to(tops[None], out_ref.shape)
-
-
-def spread_tops(top, order, copies):
-    return pl.pallas_call(
-        skipping(spread_tops_kernel, 1, len(order)),
-        in_specs=[whole()] + [whole(pl.ANY)] * len(order),
-        out_specs=whole(),
-        out_shape=jax.ShapeDtypeStruct((copies, 1, 256), jnp.float32),
-        compiler_params=params(4),
-        cost_estimate=cost(top.size, 8 * top.size),
-        name="spread_tops",
-    )(top, *order)
-
-
-def repel_kernel(group, index_ref, unit_ref, tops_ref, scale_ref, protos_hbm, *rest):
-    out_refs, (protos_ref, sems, acc_ref, sum_ref, bias_ref) = rest[:-5], rest[-5:]
-    rows, width = unit_ref.shape
+        ],
+        compiler_params=params(26),
+        cost_estimate=cost(
+            2 * unit.size * count + 8 * share * hidden * (features + units), 2 * width * count
+        ),
+        name="front",
+    )(
+        index, unit, in_hbm(bias.reshape(1, -1)), in_hbm(rows[0]), *rows[1:],
+        in_hbm(first), in_hbm(second), in_hbm(protos), *order,
+    )
+
+
+def wide_weights_kernel(group, index_ref, unit_ref, tops_ref, protos_hbm, weights_hbm, protos_ref, weights_ref, bias_ref, sems, out_sems):
+    rows = unit_ref.shape[0]
     steps, block = protos_ref.shape[:2]
-    wide = min(WIDE, block)
     arrived = fetch(protos_hbm, protos_ref, sems)
     first = index_ref[0] * group
     top = tops_ref[first]
     for other in range(1, group):
         top = jnp.maximum(top, tops_ref[first + other])
     bias_ref[...] = jnp.transpose(jnp.broadcast_to(top, (128, 256)))[:rows, :] * -teacher_rate
-    acc_ref[...] = jnp.zeros(acc_ref.shape, jnp.float32)
-    sum_ref[...] = jnp.zeros(sum_ref.shape, jnp.float32)
+
+    def chunk_out(index):
+        return pltpu.make_async_copy(weights_ref.at[index], weights_hbm.at[index], out_sems.at[index])
 
     def step(index, carry):
         arrived(index)
         bias = bias_ref[...]
+        for start in range(0, block, TILE):
+            products = scores(unit_ref[...], protos_ref[index, start : start + TILE, :])
+            for lane in range(0, TILE, 128):
+                weights = jnp.exp2(products[:, lane : lane + 128] * teacher_rate + bias)
+                weights_ref[index, :, start + lane : start + lane + 128] = weights.astype(jnp.bfloat16)
+        chunk_out(index).start()
+        return carry
+
+    lax.fori_loop(0, steps, step, 0)
+    for index in range(steps):
+        chunk_out(index).wait()
+
+
+def wide_weights(index, unit, tops, protos, order, proto_size, steps):
+    rows, width = unit.shape
+    count = protos.shape[0]
+    block = count // steps
+    return pl.pallas_call(
+        skipping(functools.partial(wide_weights_kernel, proto_size), 4, len(order)),
+        in_specs=[whole(pltpu.SMEM), whole(), whole(), whole(pl.ANY)] + [whole(pl.ANY)] * len(order),
+        out_specs=whole(pl.ANY),
+        out_shape=pltpu.HBM((steps, rows, block), jnp.bfloat16),
+        scratch_shapes=[
+            pltpu.VMEM((steps, block, width), jnp.bfloat16),
+            pltpu.VMEM((steps, rows, block), jnp.bfloat16),
+            pltpu.VMEM((rows, 128), jnp.float32),
+            pltpu.SemaphoreType.DMA((steps,)),
+            pltpu.SemaphoreType.DMA((steps,)),
+        ],
+        compiler_params=params(22),
+        cost_estimate=cost(2 * rows * width * count, 2 * (width + rows) * count, rows * count),
+        name="wide_weights",
+    )(index, unit, tops, in_hbm(protos), *order)
+
+
+def repel_kernel(index_ref, scale_ref, weights_hbm, protos_hbm, *rest):
+    out_refs, (protos_ref, weights_ref, acc_ref, sum_ref, sems, weight_sems) = rest[:-6], rest[-6:]
+    steps, block, width = protos_ref.shape
+
+    def weights_copy(index):
+        return pltpu.make_async_copy(weights_hbm.at[index], weights_ref.at[index], weight_sems.at[index])
+
+    def protos_copy(index):
+        return pltpu.make_async_copy(protos_hbm.at[part(index, block), :], protos_ref.at[index], sems.at[index])
+
+    for index in range(steps):
+        weights_copy(index).start()
+        protos_copy(index).start()
+    acc_ref[...] = jnp.zeros(acc_ref.shape, jnp.float32)
+    sum_ref[...] = jnp.zeros(sum_ref.shape, jnp.float32)
+    pieces = scale_ref.shape[2] // block
+
+    def step(index, carry):
+        weights_copy(index).wait()
+        protos_copy(index).wait()
         total = sum_ref[...]
         acc = acc_ref[...]
-        for start in range(0, block, wide):
-            protos = protos_ref[index, start : start + wide, :]
-            products = scores(unit_ref[...], protos)
-            pieces = []
-            for lane in range(0, wide, 128):
-                scaled = jnp.exp2(products[:, lane : lane + 128] * teacher_rate + bias)
-                scaled = scaled * scale_ref[index, :, start + lane : start + lane + 128]
+        scale = scale_ref[index // pieces, :, part(lax.rem(index, pieces), block)]
+        for start in range(0, block, TILE):
+            rounded = []
+            for lane in range(start, start + TILE, 128):
+                columns = slice(lane, lane + 128)
+                scaled = weights_ref[index, :, columns].astype(jnp.float32) * scale[:, columns]
                 total = total + scaled
-                pieces.append(scaled.astype(jnp.bfloat16))
+                rounded.append(scaled.astype(jnp.bfloat16))
             acc = acc + jnp.dot(
-                jnp.concatenate(pieces, axis=1), protos, preferred_element_type=jnp.float32
+                jnp.concatenate(rounded, axis=1),
+                protos_ref[index, start : start + TILE, :],
+                preferred_element_type=jnp.float32,
             )
         sum_ref[...] = total
         acc_ref[...] = acc
@@ -207,26 +282,26 @@
         out_ref[:, width:] = sum_ref[span, :]
 
 
-def repel(index, unit, tops, scale, protos, order, proto_size):
-    rows, width = unit.shape
-    count = protos.shape[0]
-    steps, _, block = scale.shape
-    return pl.pallas_call(
-        skipping(functools.partial(repel_kernel, proto_size), 5, len(order)),
-        in_specs=[whole(pltpu.SMEM), whole(), whole(), whole(), whole(pl.ANY)] + [whole(pl.ANY)] * len(order),
+def repel(index, scale, weights, protos, order, proto_size):
+    steps, rows, block = weights.shape
+    count, width = protos.shape
+    return pl.pallas_call(
+        skipping(repel_kernel, 4, len(order)),
+        in_specs=[whole(pltpu.SMEM), whole(), whole(pl.ANY), whole(pl.ANY)] + [whole(pl.ANY)] * len(order),
         out_specs=[whole()] * proto_size,
         out_shape=[jax.ShapeDtypeStruct((rows // proto_size, width + 128), jnp.float32)] * proto_size,
         scratch_shapes=[
             pltpu.VMEM((steps, block, width), jnp.bfloat16),
-            pltpu.SemaphoreType.DMA((steps,)),
+            pltpu.VMEM((steps, rows, block), jnp.bfloat16),
             pltpu.VMEM((rows, width), jnp.float32),
             pltpu.VMEM((rows, 128), jnp.float32),
-            pltpu.VMEM((rows, 128), jnp.float32),
-        ],
-        compiler_params=params(16),
-        cost_estimate=cost(4 * rows * width * count, 2 * width * count, rows * count),
+            pltpu.SemaphoreType.DMA((steps,)),
+            pltpu.SemaphoreType.DMA((steps,)),
+        ],
+        compiler_params=params(24),
+        cost_estimate=cost(2 * rows * width * count, 2 * (width + rows) * count),
         name="repel",
-    )(index, unit, tops, scale, in_hbm(protos), *order)
+    )(index, scale, in_hbm(weights), in_hbm(protos), *order)
 
 
 def attract_kernel(first_row, last, emb_ref, state_ref, protos_hbm, *rest):
@@ -538,55 +613,6 @@
         cost_estimate=cost(4 * thin * crops_total, 2 * thin * crops_total),
         name="last_scales",
     )(in_hbm(weights), parts, *order)
-
-
-def student_front_kernel(
-    index_ref, bias_ref, own_hbm, x_hbm, core_hbm, last_hbm, first_hbm, second_hbm, keep_ref, give_ref,
-    first_ref, second_ref, rows_ref, sems,
-):
-    share = own_hbm.shape[0]
-    copies = [
-        pltpu.make_async_copy(source, rows_ref.at[slot * share : (slot + 1) * share, :], sems.at[slot])
-        for slot, source in enumerate((own_hbm, x_hbm, core_hbm, last_hbm))
-    ]
-    copies.append(pltpu.make_async_copy(first_hbm, first_ref, sems.at[4]))
-    second_copy = pltpu.make_async_copy(second_hbm, second_ref, sems.at[5])
-    for copy in copies:
-        copy.start()
-    second_copy.start()
-    hidden = first_ref.shape[1]
-    bias = bias_ref[:, part(index_ref[0], hidden)]
-    for copy in copies:
-        copy.wait()
-    h_first = gelu(
-        jnp.dot(rows_ref[...], first_ref[...], preferred_element_type=jnp.float32) + bias
-    ).astype(jnp.bfloat16)
-    second_copy.wait()
-    for start in range(0, second_ref.shape[1], 512):
-        columns = slice(start, start + 512)
-        product = jnp.dot(h_first, second_ref[:, columns], preferred_element_type=jnp.float32)
-        keep_ref[:, columns] = product[: 2 * share]
-        give_ref[:, columns] = product[2 * share :]
-
-
-def student_front(index, bias, rows, first, second, order):
-    share, features = rows[0].shape
-    hidden, units = second.shape
-    return pl.pallas_call(
-        skipping(student_front_kernel, 8, len(order)),
-        in_specs=[whole(pltpu.SMEM), whole()] + [whole(pl.ANY)] * (6 + len(order)),
-        out_specs=[whole(), whole()],
-        out_shape=[jax.ShapeDtypeStruct((2 * share, units), jnp.float32)] * 2,
-        scratch_shapes=[
-            pltpu.VMEM(first.shape, jnp.bfloat16),
-            pltpu.VMEM(second.shape, jnp.bfloat16),
-            pltpu.VMEM((4 * share, features), jnp.bfloat16),
-            pltpu.SemaphoreType.DMA((6,)),
-        ],
-        compiler_params=params(16),
-        cost_estimate=cost(8 * share * hidden * (features + units), 2 * hidden * (features + units)),
-        name="student_front",
-    )(index, in_hbm(bias.reshape(1, -1)), in_hbm(rows[0]), *rows[1:], in_hbm(first), in_hbm(second), *order)
 
 
 def student_middle_kernel(
@@ -718,16 +744,15 @@
     stages = gather_batch(half)
     mine = stages[-1]
     other = swap(mine, "proto", 1)
-    top = jnp.full((256, 128), -jnp.inf, jnp.float32)
-    top = wide_tops(own_unit, protos, top, (), 0, count // 2, 4)
 
     crops_x = swap(crops, "proto", 2)
     rows = [crops, crops_x, swap(crops, "proto", 1), swap(crops_x, "proto", 1)]
     third_x = swap(w_third, "proto", 2)
     thirds = [w_third, third_x, swap(w_third, "proto", 1), swap(third_x, "proto", 1)]
-    keep, give = student_front(proto_ref, b_first, rows, w_first, w_second, (top, stages[1]))
-    top = wide_tops(own_unit, protos, top, (stages[2], give), count // 2, count // 2, 4)
-    all_tops = all_to_all(spread_tops(top, (mine,), devices), BOTH)
+    top_copies, keep, give = front(
+        proto_ref, own_unit, b_first, rows, w_first, w_second, protos, (stages[2],), devices, 8
+    )
+    all_tops = all_to_all(top_copies, BOTH)
     tops = jnp.max(all_tops.reshape(batch_size, proto_size, 256)[:, :, :group_rows], axis=1)
     tops = bit_reversed(tops, batch_size).reshape(batch_size, 2, group_rows // 2)
     base = jnp.transpose(tops, (1, 0, 2)).reshape(1, crops_total) * -teacher_rate
@@ -748,11 +773,12 @@
     attract_parts = send_blocks([slots[0], slots[2], slots[1], slots[3]])
 
     copies, weights = first_sweep(thin_ref, protos, mine, other, base, (x_sent, *thirds[2:]), devices, thin, protos_total)
+    own_weights = wide_weights(wide_ref, own_unit, all_tops, protos, (rounded,), proto_size, max(8, batch_size))
     for _ in range(ITERS - 2):
-        copies = next_sweep(weights, all_to_all(copies, BOTH), (rounded,), protos_total)
+        copies = next_sweep(weights, all_to_all(copies, BOTH), (own_weights,), protos_total)
     scale_copies = last_scales(weights, all_to_all(copies, BOTH), (state,), batch_size, protos_total)
     all_scale = all_to_all(scale_copies, "batch")
-    repels = repel(wide_ref, own_unit, all_tops, all_scale, protos, (slots[0],), proto_size)
+    repels = repel(wide_ref, all_scale, own_weights, protos, (slots[0],), proto_size)
     return finish(unit, lengths, attract_parts, send_blocks(repels))
 
 

time: 107 us -> 113 us (1.056)
  local copies, waits for them, and re-layouts: 0.27 us -> 3.69 us
  starting transfers between devices: 32 us -> 33.7 us
  waiting for transfers between devices: 23.3 us -> 24.8 us
    ppermute x20, waiting for transfers between devices: 10 us -> 16.3 us  [swap(): lax.ppermute(values, axis, [(i, i ^ flip) for i in range(lax.axis_size(ax...]
    all_to_all x4, waiting for transfers between devices: 13.3 us -> 8.58 us  [all_to_all(): return lax.all_to_all(copies, axes, 0, 0, tiled=True)]
    unnamed x2 -> x6, local copies, waits for them, and re-layouts: 0.01 us -> 3.44 us
    all_to_all x4, starting transfers between devices: 14.9 us -> 17.6 us  [all_to_all(): return lax.all_to_all(copies, axes, 0, 0, tiled=True)]
    pallas_call x5 -> x3, Pallas kernels: 21.6 us -> 21.5 us  [the longest x1 8.15 us: front(): pl.pallas_call(skipping(front_kernel, 10, len(order)), in_specs=[whole(pl...]
  transfers between devices with their start and end apart: 24 -> 24, of which waited for: 9 -> 10; matrix products, arithmetic and copies ran while one was open for 1% -> 1% of each run, Pallas kernels for 38% -> 32%
where the time goes in v10:
time: 113 us; the launch traced here: 112 us
  Pallas kernels  49.3 us (44%)
  starting transfers between devices  33.7 us (30%)
  waiting for transfers between devices  24.8 us (22%)
  local copies, waits for them, and re-layouts  3.69 us (3%)
    all_to_all x4, starting transfers between devices, all_to_all(): return lax.all_to_all(copies, axes, 0, 0, tiled=True)  17.6 us
    ppermute x20, waiting for transfers between devices, swap(): lax.ppermute(values, axis, [(i, i ^ flip) for i in range(lax.axis_size(ax...  16.3 us
    ppermute x20, starting transfers between devices, swap(): lax.ppermute(values, axis, [(i, i ^ flip) for i in range(lax.axis_size(ax...  16.2 us
    pallas_call x2, Pallas kernels, attract(): pl.pallas_call(functools.partial(attract_kernel, first_row, outputs > 1),...  10.2 us
    all_to_all x4, waiting for transfers between devices, all_to_all(): return lax.all_to_all(copies, axes, 0, 0, tiled=True)  8.58 us
    pallas_call x1, Pallas kernels, front(): pl.pallas_call(skipping(front_kernel, 10, len(order)), in_specs=[whole(pl...  8.15 us
    pallas_call x1, Pallas kernels, wide_weights(): pl.pallas_call(skipping(functools.partial(wide_weights_kernel, proto_size...  6.99 us
    pallas_call x1, Pallas kernels, repel(): pl.pallas_call(skipping(repel_kernel, 4, len(order)), in_specs=[whole(plt...  6.38 us
  transfers between devices with their start and end apart: 24, of which 10 were waited for; matrix products, arithmetic and copies ran while one was open for 1% of the time, Pallas kernels for 32%

profile of v10, /device:TPU:0, one launch (start us, length us, event | category | flops | bytes accessed | tf_op | source)
XLA Modules:
  0.0 112.5 jit_solution(11696799018918630777)
XLA Ops:
  0.0 1.0 teacher_units.1
  1.0 4.1 %collective-permute-start.3 = (bf16[96,256]{1,0:T(8,128)(2,1)S(1)}, bf16[96,256]{1,0:T(8,128)(2,1)S(1)}, u32[]{:S(2)}, u32[]{:S(2)}) collective-permute-start(bf16[96,256]{1,0:T(8,128)(2,1)S(1)} %get-tuple-element.24), channel_id=1, source_target_pairs={{0,16},{4,20},{8,24},{12,28},{16,0},{20,4},{24,8},{28,12},{1,17},{... | collective-permute-start | bytes 147464 | tf_op jit(solution)/shard_map/ppermute | solution.py:694
  5.1 1.5 %collective-permute-start = (bf16[48,1536]{1,0:T(8,128)(2,1)}, bf16[48,1536]{1,0:T(8,128)(2,1)S(1)}, u32[]{:S(2)}, u32[]{:S(2)}) collective-permute-start(bf16[48,1536]{1,0:T(8,128)(2,1)} %refs_3_.3), channel_id=1, source_target_pairs={{0,2},{1,3},{2,0},{3,1},{4,6},{5,7},{6,4},{7,5},{8,10},{9,11},{10,... | collective-permute-start | bytes 442376 | tf_op jit(solution)/shard_map/ppermute | solution.py:694
  6.6 1.1 collective-permute-done.3
  7.8 1.4 %collective-permute-start.4 = (bf16[192,256]{1,0:T(8,128)(2,1)S(1)}, bf16[192,256]{1,0:T(8,128)(2,1)S(1)}, u32[]{:S(2)}, u32[]{:S(2)}) collective-permute-start(bf16[192,256]{1,0:T(8,128)(2,1)S(1)} %maximum_select_fusion.2), channel_id=1, source_target_pairs={{0,8},{4,12},{8,0},{12,4},{16,24},{20,28},{24,16},{28,20},{1,9},{5... | collective-permute-start | bytes 294920 | tf_op jit(solution)/shard_map/ppermute | solution.py:694
  9.2 0.0 collective-permute-start.1
  9.2 1.5 %collective-permute-done.refs_4_ = bf16[48,1536]{1,0:T(8,128)(2,1)S(1)} collective-permute-done((bf16[48,1536]{1,0:T(8,128)(2,1)}, bf16[48,1536]{1,0:T(8,128)(2,1)S(1)}, u32[]{:S(2)}, u32[]{:S(2)}) %collective-permute-start) | collective-permute-done | bytes 147488 | tf_op jit(solution)/shard_map/ppermute | solution.py:694
  10.7 0.0 collective-permute-start.2
  10.7 1.8 %collective-permute-done.4 = bf16[192,256]{1,0:T(8,128)(2,1)S(1)} collective-permute-done((bf16[192,256]{1,0:T(8,128)(2,1)S(1)}, bf16[192,256]{1,0:T(8,128)(2,1)S(1)}, u32[]{:S(2)}, u32[]{:S(2)}) %collective-permute-start.4) | collective-permute-done | bytes 98336 | tf_op jit(solution)/shard_map/ppermute | solution.py:694
  12.4 0.1 maximum_select_fusion.1.refs_10_
  12.5 0.0 collective-permute-done.1.refs_5_
  12.5 0.0 collective-permute-done.2.refs_6_
  12.5 8.2 %front.1 = (f32[32,1,256]{2,1,0:T(1,128)}, f32[96,2048]{1,0:T(8,128)S(1)}, f32[96,2048]{1,0:T(8,128)}) custom-call(s32[1]{0:T(128)} %bitcast.refs_0_.index_ref, bf16[192,256]{1,0:T(8,128)(2,1)S(1)} %get-tuple-element.23.refs_1_, f32[1,2048]{1,0:T(1,128)} %bitcast.11, bf16[48,1536]{1,0:T(8,128)(2,1)} %refs_3_.3, ...), custom_call_target="tpu_custom_call" | custom-call | flops 2315255808 | bytes 8388608 | tf_op jit(solution)/shard_map/front/pallas_call | solution.py:159
  20.7 0.1 collective-permute-start.5
  20.8 1.8 %collective-permute-start.7 = (bf16[512,256]{1,0:T(8,128)(2,1)}, bf16[512,256]{1,0:T(8,128)(2,1)S(1)}, u32[]{:S(2)}, u32[]{:S(2)}) collective-permute-start(bf16[512,256]{1,0:T(8,128)(2,1)} %own_ref.1), channel_id=1, source_target_pairs={{0,2},{1,3},{2,0},{3,1},{4,6},{5,7},{6,4},{7,5},{8,10},{9,11},{10,... | collective-permute-start | bytes 786440 | tf_op jit(solution)/shard_map/ppermute | solution.py:694
  22.5 0.2 collective-permute-start.8
  22.7 1.5 %collective-permute-start.15 = (bf16[384,256]{1,0:T(8,128)(2,1)S(1)}, bf16[384,256]{1,0:T(8,128)(2,1)S(1)}, u32[]{:S(2)}, u32[]{:S(2)}) collective-permute-start(bf16[384,256]{1,0:T(8,128)(2,1)S(1)} %maximum_select_fusion.1.refs_10_), channel_id=1, source_target_pairs={{0,4},{4,0},{8,12},{12,8},{16,20},{20,16},{24,28},{28,24},{1,5},{5... | collective-permute-start | bytes 589832 | tf_op jit(solution)/shard_map/ppermute | solution.py:694
  24.2 0.1 pad_add_fusion.1.refs_0_
  24.3 0.1 pad_add_fusion.refs_0_
  24.4 5.3 %collective-permute-done.7.partner_ref = bf16[512,256]{1,0:T(8,128)(2,1)S(1)} collective-permute-done((bf16[512,256]{1,0:T(8,128)(2,1)}, bf16[512,256]{1,0:T(8,128)(2,1)S(1)}, u32[]{:S(2)}, u32[]{:S(2)}) %collective-permute-start.7) | collective-permute-done | bytes 262176 | tf_op jit(solution)/shard_map/ppermute | solution.py:694
  29.7 0.0 collective-permute-start.9
  29.7 6.2 %all-to-all-start = ((f32[32,1,256]{2,1,0:T(1,128)}), f32[32,1,256]{2,1,0:T(1,128)S(1)}, u32[]{:S(2)}, u32[]{:S(2)}) async-start(f32[32,1,256]{2,1,0:T(1,128)} %get-tuple-element.34), calls=%async_computation | async-start | bytes 65536 | tf_op jit(solution)/shard_map/all_to_all | solution.py:723
  35.9 0.0 collective-permute-done.15
  35.9 0.2 maximum_select_fusion.refs_2_
  36.1 0.3 collective-permute-start.16
  36.4 6.8 %all-to-all-done.refs_2_ = f32[32,1,256]{2,1,0:T(1,128)S(1)} async-done(((f32[32,1,256]{2,1,0:T(1,128)}), f32[32,1,256]{2,1,0:T(1,128)S(1)}, u32[]{:S(2)}, u32[]{:S(2)}) %all-to-all-start) | async-done | bytes 32800 | tf_op jit(solution)/shard_map/all_to_all | solution.py:723
  43.1 0.1 reduce
  43.2 0.0 collective-permute-done.5.core_ref
  43.3 0.6 collective-permute-start.6
  43.9 0.1 mul.17
  44.0 0.1 mul.19.refs_4_
  44.1 0.0 collective-permute-done.8.other_ref.refs_6_
  44.1 0.0 collective-permute-done.16.refs_3_
  44.1 6.1 %first_sweep.1 = (bf16[32,16,128]{2,1,0:T(8,128)(2,1)S(1)}, bf16[2048,1536]{1,0:T(8,128)(2,1)}) custom-call(s32[2]{0:T(128)S(1)} %pad_add_fusion.1.refs_0_, bf16[16384,256]{1,0:T(8,128)(2,1)} %refs_3_.5, bf16[768,256]{1,0:T(8,128)(2,1)S(1)} %maximum_select_fusion.refs_2_, bf16[768,256]{1,0:T(8,128)(2,1)} %collective-permute-done.16.refs_3_, ...), custom_call_target="tpu_custom_call" | custom-call | flops 1610612736 | bytes 6291456 | tf_op jit(solution)/shard_map/first_sweep/pallas_call | solution.py:477
  50.2 0.7 copy-done.1
  50.9 2.6 %all-to-all-start.1 = ((bf16[32,16,128]{2,1,0:T(8,128)(2,1)}), bf16[32,16,128]{2,1,0:T(8,128)(2,1)S(1)}, u32[]{:S(2)}, u32[]{:S(2)}) async-start(bf16[32,16,128]{2,1,0:T(8,128)(2,1)} %copy-done.1), calls=%async_computation.1 | async-start | bytes 262144 | tf_op jit(solution)/shard_map/all_to_all | solution.py:723
  53.4 1.2 %collective-permute-done.6.x_ref = f32[48,2048]{1,0:T(8,128)} collective-permute-done((f32[48,2048]{1,0:T(8,128)S(1)}, f32[48,2048]{1,0:T(8,128)}, u32[]{:S(2)}, u32[]{:S(2)}) %collective-permute-start.6) | collective-permute-done | bytes 393248 | tf_op jit(solution)/shard_map/ppermute | solution.py:694
  54.6 1.6 %student_middle.1 = (f32[48,256]{1,0:T(8,128)S(1)}, bf16[48,256]{1,0:T(8,128)(2,1)S(1)}, f32[48,128]{1,0:T(8,128)S(1)}) custom-call(s32[1]{0:T(128)} %bitcast.refs_0_.index_ref, f32[96,2048]{1,0:T(8,128)S(1)} %get-tuple-element.25.keep_ref, f32[96,2048]{1,0:T(8,128)S(1)} %collective-permute-done.5.core_ref, f32[48,2048]{1,0:T(8,128)} %collective-permute-done.6.x_ref, ...), custom_call_target="tpu_custom_call" | custom-call | flops 50331648 | bytes 2621440 | tf_op jit(solution)/shard_map/student_middle/pallas_call | solution.py:642
  56.3 0.6 collective-permute-start.10
  56.8 7.0 %wide_weights.1.refs_2_ = bf16[8,192,2048]{2,1,0:T(8,128)(2,1)} custom-call(s32[2]{0:T(128)S(1)} %pad_add_fusion.refs_0_, bf16[192,256]{1,0:T(8,128)(2,1)S(1)} %get-tuple-element.23.refs_1_, f32[32,1,256]{2,1,0:T(1,128)S(1)} %all-to-all-done.refs_2_, bf16[16384,256]{1,0:T(8,128)(2,1)} %refs_3_.5, bf16[48,256]{1,0:T(8,128)(2,1)S(1)} %get-tuple-element.29.refs_4_), custom_call_target="tpu_custom_call" | custom-call | flops 1610612736 | bytes 14680064 | tf_op jit(solution)/shard_map/wide_weights/pallas_call | solution.py:218
  63.9 2.8 %copy-done = bf16[8,192,2048]{2,1,0:T(8,128)(2,1)S(1)} copy-done((bf16[8,192,2048]{2,1,0:T(8,128)(2,1)S(1)}, bf16[8,192,2048]{2,1,0:T(8,128)(2,1)}, u32[]{:S(2)}) %copy-start) | copy-done | bytes 6291480
  66.6 4.4 %next_sweep.1 = bf16[32,16,128]{2,1,0:T(8,128)(2,1)} custom-call(bf16[2048,1536]{1,0:T(8,128)(2,1)} %get-tuple-element.35.refs_0_, bf16[32,16,128]{2,1,0:T(8,128)(2,1)S(1)} %all-to-all-done.1.refs_1_, bf16[8,192,2048]{2,1,0:T(8,128)(2,1)S(1)} %copy-done), custom_call_target="tpu_custom_call" | custom-call | flops 25165824 | bytes 6291456 | tf_op jit(solution)/shard_map/next_sweep/pallas_call | solution.py:562
  71.0 4.8 %all-to-all-start.2 = ((bf16[32,16,128]{2,1,0:T(8,128)(2,1)}), bf16[32,16,128]{2,1,0:T(8,128)(2,1)S(1)}, u32[]{:S(2)}, u32[]{:S(2)}) async-start(bf16[32,16,128]{2,1,0:T(8,128)(2,1)} %next_sweep.1), calls=%async_computation.2 | async-start | bytes 262144 | tf_op jit(solution)/shard_map/all_to_all | solution.py:723
  75.8 0.3 collective-permute-start.11
  76.1 1.0 collective-permute-done.11
  77.2 5.0 %attract.2.state_ref.refs_2_ = f32[192,512]{1,0:T(8,128)S(1)} custom-call(bf16[192,256]{1,0:T(8,128)(2,1)S(1)} %constant_dynamic-update-slice_fusion.emb_ref, f32[192,512]{1,0:T(8,128)S(1)} %concatenate.37.state_ref, bf16[16384,256]{1,0:T(8,128)(2,1)} %refs_3_.5), custom_call_target="tpu_custom_call" | custom-call | flops 1610612736 | bytes 4194304 | tf_op jit(solution)/shard_map/attract/pallas_call | solution.py:367
  82.2 1.8 %all-to-all-done.2.refs_1_ = bf16[32,16,128]{2,1,0:T(8,128)(2,1)S(1)} async-done(((bf16[32,16,128]{2,1,0:T(8,128)(2,1)}), bf16[32,16,128]{2,1,0:T(8,128)(2,1)S(1)}, u32[]{:S(2)}, u32[]{:S(2)}) %all-to-all-start.2) | async-done | bytes 131104 | tf_op jit(solution)/shard_map/all_to_all | solution.py:723
  84.0 3.8 %last_scales.1 = f32[8,1,2048]{2,1,0:T(1,128)} custom-call(bf16[2048,1536]{1,0:T(8,128)(2,1)} %get-tuple-element.35.refs_0_, bf16[32,16,128]{2,1,0:T(8,128)(2,1)S(1)} %all-to-all-done.2.refs_1_, f32[192,512]{1,0:T(8,128)S(1)} %attract.2.state_ref.refs_2_), custom_call_target="tpu_custom_call" | custom-call | flops 12582912 | bytes 6291456 | tf_op jit(solution)/shard_map/last_scales/pallas_call | solution.py:601
  87.8 4.0 %all-to-all-start.3 = ((f32[8,1,2048]{2,1,0:T(1,128)}), f32[8,1,2048]{2,1,0:T(1,128)S(1)}, u32[]{:S(2)}, u32[]{:S(2)}) async-start(f32[8,1,2048]{2,1,0:T(1,128)} %last_scales.1), calls=%async_computation.3 | async-start | bytes 131072 | tf_op jit(solution)/shard_map/all_to_all | solution.py:723
  91.8 5.1 %attract.3 = (f32[48,512]{1,0:T(8,128)S(1)}, f32[48,512]{1,0:T(8,128)S(1)}, f32[48,512]{1,0:T(8,128)S(1)}, f32[48,512]{1,0:T(8,128)S(1)}) custom-call(bf16[192,256]{1,0:T(8,128)(2,1)S(1)} %constant_dynamic-update-slice_fusion.emb_ref, f32[192,512]{1,0:T(8,128)S(1)} %attract.2.state_ref.refs_2_, bf16[16384,256]{1,0:T(8,128)(2,1)} %refs_3_.5), custom_call_target="tpu_custom_call" | custom-call | flops 1610612736 | bytes 4194304 | tf_op jit(solution)/shard_map/attract/pallas_call | solution.py:367
  96.9 0.1 collective-permute-start.12
  97.0 1.5 %collective-permute-start.13 = (f32[48,512]{1,0:T(8,128)S(1)}, f32[48,512]{1,0:T(8,128)S(1)}, u32[]{:S(2)}, u32[]{:S(2)}) collective-permute-start(f32[48,512]{1,0:T(8,128)S(1)} %get-tuple-element.32), channel_id=1, source_target_pairs={{0,2},{1,3},{2,0},{3,1},{4,6},{5,7},{6,4},{7,5},{8,10},{9,11},{10,... | collective-permute-start | bytes 294920 | tf_op jit(solution)/shard_map/ppermute | solution.py:694
  98.6 0.3 collective-permute-start.14
  98.9 6.4 %repel.1 = (f32[48,384]{1,0:T(8,128)S(1)}, f32[48,384]{1,0:T(8,128)S(1)}, f32[48,384]{1,0:T(8,128)S(1)}, f32[48,384]{1,0:T(8,128)S(1)}) custom-call(s32[2]{0:T(128)S(1)} %pad_add_fusion.refs_0_, f32[8,1,2048]{2,1,0:T(1,128)S(1)} %all-to-all-done.3.refs_1_, bf16[8,192,2048]{2,1,0:T(8,128)(2,1)} %wide_weights.1.refs_2_, bf16[16384,256]{1,0:T(8,128)(2,1)} %refs_3_.5, ...), custom_call_target="tpu_custom_call" | custom-call | flops 1610612736 | bytes 14680064 | tf_op jit(solution)/shard_map/repel/pallas_call | solution.py:288
  105.3 0.4 collective-permute-start.17
  105.7 1.5 %collective-permute-start.18 = (f32[48,384]{1,0:T(8,128)S(1)}, f32[48,384]{1,0:T(8,128)S(1)}, u32[]{:S(2)}, u32[]{:S(2)}) collective-permute-start(f32[48,384]{1,0:T(8,128)S(1)} %get-tuple-element.39), channel_id=1, source_target_pairs={{0,2},{1,3},{2,0},{3,1},{4,6},{5,7},{6,4},{7,5},{8,10},{9,11},{10,... | collective-permute-start | bytes 221192 | tf_op jit(solution)/shard_map/ppermute | solution.py:694
  107.2 0.0 collective-permute-done.12.rest_1_
  107.2 0.0 collective-permute-start.19
  107.2 0.0 collective-permute-done.13.rest_2_
  107.2 0.0 collective-permute-done.14.rest_3_
  107.2 0.0 collective-permute-done.17.rest_5_
  107.2 2.8 %collective-permute-done.18.rest_6_ = f32[48,384]{1,0:T(8,128)S(1)} collective-permute-done((f32[48,384]{1,0:T(8,128)S(1)}, f32[48,384]{1,0:T(8,128)S(1)}, u32[]{:S(2)}, u32[]{:S(2)}) %collective-permute-start.18) | collective-permute-done | bytes 73760 | tf_op jit(solution)/shard_map/ppermute | solution.py:694
  110.1 1.6 %collective-permute-done.19.rest_7_ = f32[48,384]{1,0:T(8,128)S(1)} collective-permute-done((f32[48,384]{1,0:T(8,128)S(1)}, f32[48,384]{1,0:T(8,128)S(1)}, u32[]{:S(2)}, u32[]{:S(2)}) %collective-permute-start.19) | collective-permute-done | bytes 73760 | tf_op jit(solution)/shard_map/ppermute | solution.py:694
  111.7 0.8 finish.1
  (21 shorter events, 0.2 us)
Async XLA Ops:
  1.0 6.7 %collective-permute-start.3 = (bf16[96,256]{1,0:T(8,128)(2,1)S(1)}, bf16[96,256]{1,0:T(8,128)(2,1)S(1)}, u32[]{:S(2)}, u32[]{:S(2)}) collective-permute-start(bf16[96,256]{1,0:T(8,128)(2,1)S(1)} %get-tuple-element.24), channel_id=1, source_target_pairs={{0,16},{4,20},{8,24},{12,28},{16,0},{20,4},{24,8},{28,12},{1,17},{... | collective-permute-start | bytes 147464 | tf_op jit(solution)/shard_map/ppermute | solution.py:694
  5.1 5.5 %collective-permute-start = (bf16[48,1536]{1,0:T(8,128)(2,1)}, bf16[48,1536]{1,0:T(8,128)(2,1)S(1)}, u32[]{:S(2)}, u32[]{:S(2)}) collective-permute-start(bf16[48,1536]{1,0:T(8,128)(2,1)} %refs_3_.3), channel_id=1, source_target_pairs={{0,2},{1,3},{2,0},{3,1},{4,6},{5,7},{6,4},{7,5},{8,10},{9,11},{10,... | collective-permute-start | bytes 442376 | tf_op jit(solution)/shard_map/ppermute | solution.py:694
  7.8 4.7 %collective-permute-start.4 = (bf16[192,256]{1,0:T(8,128)(2,1)S(1)}, bf16[192,256]{1,0:T(8,128)(2,1)S(1)}, u32[]{:S(2)}, u32[]{:S(2)}) collective-permute-start(bf16[192,256]{1,0:T(8,128)(2,1)S(1)} %maximum_select_fusion.2), channel_id=1, source_target_pairs={{0,8},{4,12},{8,0},{12,4},{16,24},{20,28},{24,16},{28,20},{1,9},{5... | collective-permute-start | bytes 294920 | tf_op jit(solution)/shard_map/ppermute | solution.py:694
  9.2 3.3 %collective-permute-start.1 = (bf16[48,1536]{1,0:T(8,128)(2,1)}, bf16[48,1536]{1,0:T(8,128)(2,1)S(1)}, u32[]{:S(2)}, u32[]{:S(2)}) collective-permute-start(bf16[48,1536]{1,0:T(8,128)(2,1)} %refs_3_.3), channel_id=1, source_target_pairs={{0,1},{1,0},{2,3},{3,2},{4,5},{5,4},{6,7},{7,6},{8,9},{9,8},{10,11... | collective-permute-start | bytes 442376 | tf_op jit(solution)/shard_map/ppermute | solution.py:694
  10.7 1.9 %collective-permute-start.2 = (bf16[48,1536]{1,0:T(8,128)(2,1)S(1)}, bf16[48,1536]{1,0:T(8,128)(2,1)S(1)}, u32[]{:S(2)}, u32[]{:S(2)}) collective-permute-start(bf16[48,1536]{1,0:T(8,128)(2,1)S(1)} %collective-permute-done.refs_4_), channel_id=1, source_target_pairs={{0,1},{1,0},{2,3},{3,2},{4,5},{5,4},{6,7},{7,6},{8,9},{9,8},{10,11... | collective-permute-start | bytes 442376 | tf_op jit(solution)/shard_map/ppermute | solution.py:694
  20.7 22.6 %collective-permute-start.5 = (f32[96,2048]{1,0:T(8,128)}, f32[96,2048]{1,0:T(8,128)S(1)}, u32[]{:S(2)}, u32[]{:S(2)}) collective-permute-start(f32[96,2048]{1,0:T(8,128)} %get-tuple-element.26), channel_id=1, source_target_pairs={{0,1},{1,0},{2,3},{3,2},{4,5},{5,4},{6,7},{7,6},{8,9},{9,8},{10,11... | collective-permute-start | bytes 2359304 | tf_op jit(solution)/shard_map/ppermute | solution.py:694
  20.8 8.9 %collective-permute-start.7 = (bf16[512,256]{1,0:T(8,128)(2,1)}, bf16[512,256]{1,0:T(8,128)(2,1)S(1)}, u32[]{:S(2)}, u32[]{:S(2)}) collective-permute-start(bf16[512,256]{1,0:T(8,128)(2,1)} %own_ref.1), channel_id=1, source_target_pairs={{0,2},{1,3},{2,0},{3,1},{4,6},{5,7},{6,4},{7,5},{8,10},{9,11},{10,... | collective-permute-start | bytes 786440 | tf_op jit(solution)/shard_map/ppermute | solution.py:694
  22.5 21.6 %collective-permute-start.8 = (bf16[512,256]{1,0:T(8,128)(2,1)}, bf16[512,256]{1,0:T(8,128)(2,1)S(1)}, u32[]{:S(2)}, u32[]{:S(2)}) collective-permute-start(bf16[512,256]{1,0:T(8,128)(2,1)} %own_ref.1), channel_id=1, source_target_pairs={{0,1},{1,0},{2,3},{3,2},{4,5},{5,4},{6,7},{7,6},{8,9},{9,8},{10,11... | collective-permute-start | bytes 786440 | tf_op jit(solution)/shard_map/ppermute | solution.py:694
  22.7 13.2 %collective-permute-start.15 = (bf16[384,256]{1,0:T(8,128)(2,1)S(1)}, bf16[384,256]{1,0:T(8,128)(2,1)S(1)}, u32[]{:S(2)}, u32[]{:S(2)}) collective-permute-start(bf16[384,256]{1,0:T(8,128)(2,1)S(1)} %maximum_select_fusion.1.refs_10_), channel_id=1, source_target_pairs={{0,4},{4,0},{8,12},{12,8},{16,20},{20,16},{24,28},{28,24},{1,5},{5... | collective-permute-start | bytes 589832 | tf_op jit(solution)/shard_map/ppermute | solution.py:694
  29.7 14.4 %collective-permute-start.9 = (bf16[512,256]{1,0:T(8,128)(2,1)S(1)}, bf16[512,256]{1,0:T(8,128)(2,1)S(1)}, u32[]{:S(2)}, u32[]{:S(2)}) collective-permute-start(bf16[512,256]{1,0:T(8,128)(2,1)S(1)} %collective-permute-done.7.partner_ref), channel_id=1, source_target_pairs={{0,1},{1,0},{2,3},{3,2},{4,5},{5,4},{6,7},{7,6},{8,9},{9,8},{10,11... | collective-permute-start | bytes 786440 | tf_op jit(solution)/shard_map/ppermute | solution.py:694
  29.7 13.4 %all-to-all-start = ((f32[32,1,256]{2,1,0:T(1,128)}), f32[32,1,256]{2,1,0:T(1,128)S(1)}, u32[]{:S(2)}, u32[]{:S(2)}) async-start(f32[32,1,256]{2,1,0:T(1,128)} %get-tuple-element.34), calls=%async_computation | async-start | bytes 65536 | tf_op jit(solution)/shard_map/all_to_all | solution.py:723
  36.1 8.1 %collective-permute-start.16 = (bf16[768,256]{1,0:T(8,128)(2,1)S(1)}, bf16[768,256]{1,0:T(8,128)(2,1)}, u32[]{:S(2)}, u32[]{:S(2)}) collective-permute-start(bf16[768,256]{1,0:T(8,128)(2,1)S(1)} %maximum_select_fusion.refs_2_), channel_id=1, source_target_pairs={{0,1},{1,0},{2,3},{3,2},{4,5},{5,4},{6,7},{7,6},{8,9},{9,8},{10,11... | collective-permute-start | bytes 1179656 | tf_op jit(solution)/shard_map/ppermute | solution.py:694
  43.3 11.3 %collective-permute-start.6 = (f32[48,2048]{1,0:T(8,128)S(1)}, f32[48,2048]{1,0:T(8,128)}, u32[]{:S(2)}, u32[]{:S(2)}) collective-permute-start(f32[48,2048]{1,0:T(8,128)S(1)} %slice_add_fusion.refs_5_), channel_id=1, source_target_pairs={{0,2},{1,3},{2,0},{3,1},{4,6},{5,7},{6,4},{7,5},{8,10},{9,11},{10,... | collective-permute-start | bytes 1179656 | tf_op jit(solution)/shard_map/ppermute | solution.py:694
  50.2 0.7 copy-start.1
  50.9 13.0 %all-to-all-start.1 = ((bf16[32,16,128]{2,1,0:T(8,128)(2,1)}), bf16[32,16,128]{2,1,0:T(8,128)(2,1)S(1)}, u32[]{:S(2)}, u32[]{:S(2)}) async-start(bf16[32,16,128]{2,1,0:T(8,128)(2,1)} %copy-done.1), calls=%async_computation.1 | async-start | bytes 262144 | tf_op jit(solution)/shard_map/all_to_all | solution.py:723
  56.3 19.5 %collective-permute-start.10 = (bf16[48,256]{1,0:T(8,128)(2,1)S(1)}, bf16[48,256]{1,0:T(8,128)(2,1)S(1)}, u32[]{:S(2)}, u32[]{:S(2)}) collective-permute-start(bf16[48,256]{1,0:T(8,128)(2,1)S(1)} %get-tuple-element.29.refs_4_), channel_id=1, source_target_pairs={{0,2},{1,3},{2,0},{3,1},{4,6},{5,7},{6,4},{7,5},{8,10},{9,11},{10,... | collective-permute-start | bytes 73736 | tf_op jit(solution)/shard_map/ppermute | solution.py:694
  63.8 2.8 %copy-start = (bf16[8,192,2048]{2,1,0:T(8,128)(2,1)S(1)}, bf16[8,192,2048]{2,1,0:T(8,128)(2,1)}, u32[]{:S(2)}) copy-start(bf16[8,192,2048]{2,1,0:T(8,128)(2,1)} %wide_weights.1.refs_2_) | copy-start | bytes 18874372
  71.0 13.0 %all-to-all-start.2 = ((bf16[32,16,128]{2,1,0:T(8,128)(2,1)}), bf16[32,16,128]{2,1,0:T(8,128)(2,1)S(1)}, u32[]{:S(2)}, u32[]{:S(2)}) async-start(bf16[32,16,128]{2,1,0:T(8,128)(2,1)} %next_sweep.1), calls=%async_computation.2 | async-start | bytes 262144 | tf_op jit(solution)/shard_map/all_to_all | solution.py:723
  75.8 1.3 %collective-permute-start.11 = (bf16[96,256]{1,0:T(8,128)(2,1)S(1)}, bf16[96,256]{1,0:T(8,128)(2,1)S(1)}, u32[]{:S(2)}, u32[]{:S(2)}) collective-permute-start(bf16[96,256]{1,0:T(8,128)(2,1)S(1)} %pad_maximum_fusion), channel_id=1, source_target_pairs={{0,1},{1,0},{2,3},{3,2},{4,5},{5,4},{6,7},{7,6},{8,9},{9,8},{10,11... | collective-permute-start | bytes 147464 | tf_op jit(solution)/shard_map/ppermute | solution.py:694
  87.8 11.1 %all-to-all-start.3 = ((f32[8,1,2048]{2,1,0:T(1,128)}), f32[8,1,2048]{2,1,0:T(1,128)S(1)}, u32[]{:S(2)}, u32[]{:S(2)}) async-start(f32[8,1,2048]{2,1,0:T(1,128)} %last_scales.1), calls=%async_computation.3 | async-start | bytes 131072 | tf_op jit(solution)/shard_map/all_to_all | solution.py:723
  96.9 10.2 %collective-permute-start.12 = (f32[48,512]{1,0:T(8,128)S(1)}, f32[48,512]{1,0:T(8,128)S(1)}, u32[]{:S(2)}, u32[]{:S(2)}) collective-permute-start(f32[48,512]{1,0:T(8,128)S(1)} %get-tuple-element.31), channel_id=1, source_target_pairs={{0,1},{1,0},{2,3},{3,2},{4,5},{5,4},{6,7},{7,6},{8,9},{9,8},{10,11... | collective-permute-start | bytes 294920 | tf_op jit(solution)/shard_map/ppermute | solution.py:694
  97.0 10.2 %collective-permute-start.13 = (f32[48,512]{1,0:T(8,128)S(1)}, f32[48,512]{1,0:T(8,128)S(1)}, u32[]{:S(2)}, u32[]{:S(2)}) collective-permute-start(f32[48,512]{1,0:T(8,128)S(1)} %get-tuple-element.32), channel_id=1, source_target_pairs={{0,2},{1,3},{2,0},{3,1},{4,6},{5,7},{6,4},{7,5},{8,10},{9,11},{10,... | collective-permute-start | bytes 294920 | tf_op jit(solution)/shard_map/ppermute | solution.py:694
  98.6 8.7 %collective-permute-start.14 = (f32[48,512]{1,0:T(8,128)S(1)}, f32[48,512]{1,0:T(8,128)S(1)}, u32[]{:S(2)}, u32[]{:S(2)}) collective-permute-start(f32[48,512]{1,0:T(8,128)S(1)} %get-tuple-element.33), channel_id=1, source_target_pairs={{0,3},{1,2},{2,1},{3,0},{4,7},{5,6},{6,5},{7,4},{8,11},{9,10},{10,... | collective-permute-start | bytes 294920 | tf_op jit(solution)/shard_map/ppermute | solution.py:694
  105.3 2.0 %collective-permute-start.17 = (f32[48,384]{1,0:T(8,128)S(1)}, f32[48,384]{1,0:T(8,128)S(1)}, u32[]{:S(2)}, u32[]{:S(2)}) collective-permute-start(f32[48,384]{1,0:T(8,128)S(1)} %get-tuple-element.38), channel_id=1, source_target_pairs={{0,1},{1,0},{2,3},{3,2},{4,5},{5,4},{6,7},{7,6},{8,9},{9,8},{10,11... | collective-permute-start | bytes 221192 | tf_op jit(solution)/shard_map/ppermute | solution.py:694
  105.7 4.4 %collective-permute-start.18 = (f32[48,384]{1,0:T(8,128)S(1)}, f32[48,384]{1,0:T(8,128)S(1)}, u32[]{:S(2)}, u32[]{:S(2)}) collective-permute-start(f32[48,384]{1,0:T(8,128)S(1)} %get-tuple-element.39), channel_id=1, source_target_pairs={{0,2},{1,3},{2,0},{3,1},{4,6},{5,7},{6,4},{7,5},{8,10},{9,11},{10,... | collective-permute-start | bytes 221192 | tf_op jit(solution)/shard_map/ppermute | solution.py:694
  107.2 4.5 %collective-permute-start.19 = (f32[48,384]{1,0:T(8,128)S(1)}, f32[48,384]{1,0:T(8,128)S(1)}, u32[]{:S(2)}, u32[]{:S(2)}) collective-permute-start(f32[48,384]{1,0:T(8,128)S(1)} %get-tuple-element.40), channel_id=1, source_target_pairs={{0,3},{1,2},{2,1},{3,0},{4,7},{5,6},{6,5},{7,4},{8,11},{9,10},{10,... | collective-permute-start | bytes 221192 | tf_op jit(solution)/shard_map/ppermute | solution.py:694

commit v11 on v10

--- a/solution.py
+++ b/solution.py
@@ -182,91 +182,36 @@
     )
 
 
-def wide_weights_kernel(group, index_ref, unit_ref, tops_ref, protos_hbm, weights_hbm, protos_ref, weights_ref, bias_ref, sems, out_sems):
-    rows = unit_ref.shape[0]
+def repel_kernel(group, index_ref, unit_ref, tops_ref, scale_ref, protos_hbm, *rest):
+    out_refs, (protos_ref, sems, acc_ref, sum_ref, bias_ref) = rest[:-5], rest[-5:]
+    rows, width = unit_ref.shape
     steps, block = protos_ref.shape[:2]
+    wide = min(WIDE, block)
     arrived = fetch(protos_hbm, protos_ref, sems)
     first = index_ref[0] * group
     top = tops_ref[first]
     for other in range(1, group):
         top = jnp.maximum(top, tops_ref[first + other])
     bias_ref[...] = jnp.transpose(jnp.broadcast_to(top, (128, 256)))[:rows, :] * -teacher_rate
-
-    def chunk_out(index):
-        return pltpu.make_async_copy(weights_ref.at[index], weights_hbm.at[index], out_sems.at[index])
+    acc_ref[...] = jnp.zeros(acc_ref.shape, jnp.float32)
+    sum_ref[...] = jnp.zeros(sum_ref.shape, jnp.float32)
 
     def step(index, carry):
         arrived(index)
         bias = bias_ref[...]
-        for start in range(0, block, TILE):
-            products = scores(unit_ref[...], protos_ref[index, start : start + TILE, :])
-            for lane in range(0, TILE, 128):
-                weights = jnp.exp2(products[:, lane : lane + 128] * teacher_rate + bias)
-                weights_ref[index, :, start + lane : start + lane + 128] = weights.astype(jnp.bfloat16)
-        chunk_out(index).start()
-        return carry
-
-    lax.fori_loop(0, steps, step, 0)
-    for index in range(steps):
-        chunk_out(index).wait()
-
-
-def wide_weights(index, unit, tops, protos, order, proto_size, steps):
-    rows, width = unit.shape
-    count = protos.shape[0]
-    block = count // steps
-    return pl.pallas_call(
-        skipping(functools.partial(wide_weights_kernel, proto_size), 4, len(order)),
-        in_specs=[whole(pltpu.SMEM), whole(), whole(), whole(pl.ANY)] + [whole(pl.ANY)] * len(order),
-        out_specs=whole(pl.ANY),
-        out_shape=pltpu.HBM((steps, rows, block), jnp.bfloat16),
-        scratch_shapes=[
-            pltpu.VMEM((steps, block, width), jnp.bfloat16),
-            pltpu.VMEM((steps, rows, block), jnp.bfloat16),
-            pltpu.VMEM((rows, 128), jnp.float32),
-            pltpu.SemaphoreType.DMA((steps,)),
-            pltpu.SemaphoreType.DMA((steps,)),
-        ],
-        compiler_params=params(22),
-        cost_estimate=cost(2 * rows * width * count, 2 * (width + rows) * count, rows * count),
-        name="wide_weights",
-    )(index, unit, tops, in_hbm(protos), *order)
-
-
-def repel_kernel(index_ref, scale_ref, weights_hbm, protos_hbm, *rest):
-    out_refs, (protos_ref, weights_ref, acc_ref, sum_ref, sems, weight_sems) = rest[:-6], rest[-6:]
-    steps, block, width = protos_ref.shape
-
-    def weights_copy(index):
-        return pltpu.make_async_copy(weights_hbm.at[index], weights_ref.at[index], weight_sems.at[index])
-
-    def protos_copy(index):
-        return pltpu.make_async_copy(protos_hbm.at[part(index, block), :], protos_ref.at[index], sems.at[index])
-
-    for index in range(steps):
-        weights_copy(index).start()
-        protos_copy(index).start()
-    acc_ref[...] = jnp.zeros(acc_ref.shape, jnp.float32)
-    sum_ref[...] = jnp.zeros(sum_ref.shape, jnp.float32)
-    pieces = scale_ref.shape[2] // block
-
-    def step(index, carry):
-        weights_copy(index).wait()
-        protos_copy(index).wait()
         total = sum_ref[...]
         acc = acc_ref[...]
-        scale = scale_ref[index // pieces, :, part(lax.rem(index, pieces), block)]
-        for start in range(0, block, TILE):
-            rounded = []
-            for lane in range(start, start + TILE, 128):
-                columns = slice(lane, lane + 128)
-                scaled = weights_ref[index, :, columns].astype(jnp.float32) * scale[:, columns]
+        for start in range(0, block, wide):
+            protos = protos_ref[index, start : start + wide, :]
+            products = scores(unit_ref[...], protos)
+            pieces = []
+            for lane in range(0, wide, 128):
+                scaled = jnp.exp2(products[:, lane : lane + 128] * teacher_rate + bias)
+                scaled = scaled * scale_ref[index, :, start + lane : start + lane + 128]
                 total = total + scaled
-                rounded.append(scaled.astype(jnp.bfloat16))
+                pieces.append(scaled.astype(jnp.bfloat16))
             acc = acc + jnp.dot(
-                jnp.concatenate(rounded, axis=1),
-                protos_ref[index, start : start + TILE, :],
-                preferred_element_type=jnp.float32,
+                jnp.concatenate(pieces, axis=1), protos, preferred_element_type=jnp.float32
             )
         sum_ref[...] = total
         acc_ref[...] = acc
@@ -282,26 +227,26 @@
         out_ref[:, width:] = sum_ref[span, :]
 
 
-def repel(index, scale, weights, protos, order, proto_size):
-    steps, rows, block = weights.shape
-    count, width = protos.shape
-    return pl.pallas_call(
-        skipping(repel_kernel, 4, len(order)),
-        in_specs=[whole(pltpu.SMEM), whole(), whole(pl.ANY), whole(pl.ANY)] + [whole(pl.ANY)] * len(order),
+def repel(index, unit, tops, scale, protos, order, proto_size):
+    rows, width = unit.shape
+    count = protos.shape[0]
+    steps, _, block = scale.shape
+    return pl.pallas_call(
+        skipping(functools.partial(repel_kernel, proto_size), 5, len(order)),
+        in_specs=[whole(pltpu.SMEM), whole(), whole(), whole(), whole(pl.ANY)] + [whole(pl.ANY)] * len(order),
         out_specs=[whole()] * proto_size,
         out_shape=[jax.ShapeDtypeStruct((rows // proto_size, width + 128), jnp.float32)] * proto_size,
         scratch_shapes=[
             pltpu.VMEM((steps, block, width), jnp.bfloat16),
-            pltpu.VMEM((steps, rows, block), jnp.bfloat16),
+            pltpu.SemaphoreType.DMA((steps,)),
             pltpu.VMEM((rows, width), jnp.float32),
             pltpu.VMEM((rows, 128), jnp.float32),
-            pltpu.SemaphoreType.DMA((steps,)),
-            pltpu.SemaphoreType.DMA((steps,)),
-        ],
-        compiler_params=params(24),
-        cost_estimate=cost(2 * rows * width * count, 2 * (width + rows) * count),
+            pltpu.VMEM((rows, 128), jnp.float32),
+        ],
+        compiler_params=params(16),
+        cost_estimate=cost(4 * rows * width * count, 2 * width * count, rows * count),
         name="repel",
-    )(index, scale, in_hbm(weights), in_hbm(protos), *order)
+    )(index, unit, tops, scale, in_hbm(protos), *order)
 
 
 def attract_kernel(first_row, last, emb_ref, state_ref, protos_hbm, *rest):
@@ -420,18 +365,21 @@
 
 
 def first_sweep_kernel(
-    chunk, protos_total, index_ref, protos_hbm, mine_hbm, other_hbm, bias_ref, copies_ref, weights_hbm, protos_ref, units_ref, weights_ref, rounded_ref, scale_ref, sems, out_sems,
+    protos_total, index_ref, protos_hbm, mine_hbm, other_hbm, bias_ref, copies_ref, weights_hbm,
+    protos_ref, units_ref, weights_ref, rounded_ref, scale_ref, totals_ref, sems, out_sems,
 ):
-    thin, crops_total = weights_ref.shape
+    steps, chunk, crops_total = rounded_ref.shape
+    thin = steps * chunk
     half = mine_hbm.shape[0]
     core = index_ref[1]
     copies = (
-        pltpu.make_async_copy(protos_hbm.at[part(index_ref[0], thin), :], protos_ref, sems.at[0]),
         pltpu.make_async_copy(mine_hbm, units_ref.at[part(core, half), :], sems.at[1]),
         pltpu.make_async_copy(other_hbm, units_ref.at[part(1 - core, half), :], sems.at[2]),
+        pltpu.make_async_copy(protos_hbm.at[part(index_ref[0], thin), :], protos_ref, sems.at[0]),
     )
     for copy in copies:
         copy.start()
+    totals_ref[...] = jnp.zeros(totals_ref.shape, jnp.float32)
     for copy in copies:
         copy.wait()
 
@@ -440,42 +388,50 @@
             rounded_ref.at[index], weights_hbm.at[part(index, chunk), :], out_sems.at[index]
         )
 
-    def weigh(index, carry):
-        rows = part(index, chunk)
-        protos = protos_ref[rows, :]
+    def weigh(index, slot):
+        protos = protos_ref[part(index, chunk), :]
         folded = jnp.zeros((chunk, 128), jnp.float32)
         for start in range(0, crops_total, TILE):
             columns = slice(start, start + TILE)
             products = scores(protos, units_ref[columns, :])
             weights = jnp.exp2(products * teacher_rate + bias_ref[:, columns])
-            weights_ref[rows, columns] = weights
+            weights_ref[slot, :, columns] = weights
             rounded_ref[index, :, columns] = weights.astype(jnp.bfloat16)
             folded = folded + lane_fold(weights, jnp.add)
         sums = jnp.sum(folded, axis=1, keepdims=True)
-        scale_ref[rows, :] = jnp.broadcast_to(1.0 / (protos_total * sums), (chunk, 128))
+        scale_ref[slot] = jnp.broadcast_to(1.0 / (protos_total * sums), (chunk, 128))
         chunk_out(index).start()
+
+    def add_up(slot):
+        for lane in range(0, crops_total, 128):
+            total = totals_ref[:, lane : lane + 128]
+            for row in range(0, chunk, 64):
+                scaled = weights_ref[slot, row : row + 64, lane : lane + 128] * scale_ref[slot, row : row + 64, :]
+                total = total + jnp.sum(scaled.reshape(-1, 8, 128), axis=0)
+            totals_ref[:, lane : lane + 128] = total
+
+    weigh(0, 0)
+
+    def sweep(index, carry):
+        slot = lax.rem(index, 2)
+        weigh(index, slot)
+        add_up(1 - slot)
         return carry
 
-    lax.fori_loop(0, thin // chunk, weigh, 0)
-    small = min(thin, 64)
-
-    def add_up(index, totals):
-        rows = part(index, small)
-        scaled = weights_ref[rows, :] * jnp.tile(scale_ref[rows, :], (1, crops_total // 128))
-        return totals + jnp.sum(scaled.reshape(-1, 8, crops_total), axis=0)
-
-    totals = lax.fori_loop(0, thin // small, add_up, jnp.zeros((8, crops_total), jnp.float32))
-    give_sums(copies_ref, jnp.sum(totals, axis=0, keepdims=True))
-    for index in range(thin // chunk):
+    lax.fori_loop(1, steps, sweep, 0)
+    add_up((steps - 1) % 2)
+    give_sums(copies_ref, jnp.sum(totals_ref[...], axis=0, keepdims=True))
+    for index in range(steps):
         chunk_out(index).wait()
 
 
 def first_sweep(index, protos, mine, other, base, order, copies, thin, protos_total):
     width = protos.shape[1]
     crops_total = 2 * mine.shape[0]
-    chunk = min(thin, 1024)
-    return pl.pallas_call(
-        skipping(functools.partial(first_sweep_kernel, chunk, protos_total), 5, len(order)),
+    chunk = min(thin, 512) if crops_total <= 2048 else 128
+    steps = thin // chunk
+    return pl.pallas_call(
+        skipping(functools.partial(first_sweep_kernel, protos_total), 5, len(order)),
         in_specs=[whole(pltpu.SMEM), whole(pl.ANY), whole(pl.ANY), whole(pl.ANY), whole()]
         + [whole(pl.ANY)] * len(order),
         out_specs=[whole(), whole(pl.ANY)],
@@ -486,11 +442,12 @@
         scratch_shapes=[
             pltpu.VMEM((thin, width), jnp.bfloat16),
             pltpu.VMEM((crops_total, width), jnp.bfloat16),
-            pltpu.VMEM((thin, crops_total), jnp.float32),
-            pltpu.VMEM((thin // chunk, chunk, crops_total), jnp.bfloat16),
-            pltpu.VMEM((thin, 128), jnp.float32),
+            pltpu.VMEM((2, chunk, crops_total), jnp.float32),
+            pltpu.VMEM((steps, chunk, crops_total), jnp.bfloat16),
+            pltpu.VMEM((2, chunk, 128), jnp.float32),
+            pltpu.VMEM((8, crops_total), jnp.float32),
             pltpu.SemaphoreType.DMA((3,)),
-            pltpu.SemaphoreType.DMA((thin // chunk,)),
+            pltpu.SemaphoreType.DMA((steps,)),
         ],
         compiler_params=params(32 if crops_total <= 2048 else 56),
         cost_estimate=cost(2 * thin * width * crops_total, 2 * thin * crops_total, thin * crops_total),
@@ -747,8 +704,7 @@
 
     crops_x = swap(crops, "proto", 2)
     rows = [crops, crops_x, swap(crops, "proto", 1), swap(crops_x, "proto", 1)]
-    third_x = swap(w_third, "proto", 2)
-    thirds = [w_third, third_x, swap(w_third, "proto", 1), swap(third_x, "proto", 1)]
+    thirds = [w_third, swap(w_third, "proto", 2), swap(w_third, "proto", 1), swap(w_third, "proto", 3)]
     top_copies, keep, give = front(
         proto_ref, own_unit, b_first, rows, w_first, w_second, protos, (stages[2],), devices, 8
     )
@@ -772,13 +728,12 @@
     slots = attract(student_emb, state, protos, count // 2, count // 2, 4, proto_size)
     attract_parts = send_blocks([slots[0], slots[2], slots[1], slots[3]])
 
-    copies, weights = first_sweep(thin_ref, protos, mine, other, base, (x_sent, *thirds[2:]), devices, thin, protos_total)
-    own_weights = wide_weights(wide_ref, own_unit, all_tops, protos, (rounded,), proto_size, max(8, batch_size))
+    copies, weights = first_sweep(thin_ref, protos, mine, other, base, (x_sent, *thirds[1:]), devices, thin, protos_total)
     for _ in range(ITERS - 2):
-        copies = next_sweep(weights, all_to_all(copies, BOTH), (own_weights,), protos_total)
+        copies = next_sweep(weights, all_to_all(copies, BOTH), (rounded,), protos_total)
     scale_copies = last_scales(weights, all_to_all(copies, BOTH), (state,), batch_size, protos_total)
     all_scale = all_to_all(scale_copies, "batch")
-    repels = repel(wide_ref, all_scale, own_weights, protos, (slots[0],), proto_size)
+    repels = repel(wide_ref, own_unit, all_tops, all_scale, protos, (slots[0],), proto_size)
     return finish(unit, lengths, attract_parts, send_blocks(repels))
 
 

time: 113 us -> 107 us (0.947)
  local copies, waits for them, and re-layouts: 3.69 us -> 0.26 us
  Pallas kernels: 49.3 us -> 46.9 us
  starting transfers between devices: 33.7 us -> 35 us
    ppermute x20, waiting for transfers between devices: 16.3 us -> 9.92 us  [swap(): lax.ppermute(values, axis, [(i, i ^ flip) for i in range(lax.axis_size(ax...]
    all_to_all x4, waiting for transfers between devices: 8.58 us -> 13.9 us  [all_to_all(): return lax.all_to_all(copies, axes, 0, 0, tiled=True)]
    unnamed x6 -> x2, local copies, waits for them, and re-layouts: 3.44 us -> 0.01 us
    pallas_call x3 -> x2, Pallas kernels: 19.4 us -> 17 us  [the longest x1 9.44 us: repel(): pl.pallas_call(skipping(functools.partial(repel_kernel, proto_size), 5, l...]
    ppermute x20, starting transfers between devices: 16.2 us -> 18.5 us  [swap(): lax.ppermute(values, axis, [(i, i ^ flip) for i in range(lax.axis_size(ax...]
  transfers between devices with their start and end apart: 24 -> 24, of which waited for: 10 -> 9; matrix products, arithmetic and copies ran while one was open for 1% -> 1% of each run, Pallas kernels for 32% -> 31%
where the time goes in v11:
time: 107 us
  Pallas kernels  46.9 us (44%)
  starting transfers between devices  35 us (33%)
  waiting for transfers between devices  23.8 us (22%)
    ppermute x20, starting transfers between devices, swap(): lax.ppermute(values, axis, [(i, i ^ flip) for i in range(lax.axis_size(ax...  18.5 us
    all_to_all x4, starting transfers between devices, all_to_all(): return lax.all_to_all(copies, axes, 0, 0, tiled=True)  16.4 us
    all_to_all x4, waiting for transfers between devices, all_to_all(): return lax.all_to_all(copies, axes, 0, 0, tiled=True)  13.9 us
    pallas_call x2, Pallas kernels, attract(): pl.pallas_call(functools.partial(attract_kernel, first_row, outputs > 1),...  10.1 us
    ppermute x20, waiting for transfers between devices, swap(): lax.ppermute(values, axis, [(i, i ^ flip) for i in range(lax.axis_size(ax...  9.92 us
    pallas_call x1, Pallas kernels, repel(): pl.pallas_call(skipping(functools.partial(repel_kernel, proto_size), 5, l...  9.44 us
    pallas_call x1, Pallas kernels, front(): pl.pallas_call(skipping(front_kernel, 10, len(order)), in_specs=[whole(pl...  8.14 us
    pallas_call x1, Pallas kernels, first_sweep(): pl.pallas_call(skipping(functools.partial(first_sweep_kernel, protos_tota...  7.58 us
  transfers between devices with their start and end apart: 24, of which 9 were waited for; matrix products, arithmetic and copies ran while one was open for 1% of the time, Pallas kernels for 31%

profile of v11, /device:TPU:0, one launch (start us, length us, event | category | flops | bytes accessed | tf_op | source)
XLA Modules:
  0.0 106.8 jit_solution(11922723749219126143)
XLA Ops:
  0.0 1.0 teacher_units.1
  1.0 4.1 %collective-permute-start.3 = (bf16[96,256]{1,0:T(8,128)(2,1)S(1)}, bf16[96,256]{1,0:T(8,128)(2,1)S(1)}, u32[]{:S(2)}, u32[]{:S(2)}) collective-permute-start(bf16[96,256]{1,0:T(8,128)(2,1)S(1)} %get-tuple-element.24), channel_id=1, source_target_pairs={{0,16},{4,20},{8,24},{12,28},{16,0},{20,4},{24,8},{28,12},{1,17},{... | collective-permute-start | bytes 147464 | tf_op jit(solution)/shard_map/ppermute | solution.py:651
  5.1 1.5 %collective-permute-start = (bf16[48,1536]{1,0:T(8,128)(2,1)}, bf16[48,1536]{1,0:T(8,128)(2,1)S(1)}, u32[]{:S(2)}, u32[]{:S(2)}) collective-permute-start(bf16[48,1536]{1,0:T(8,128)(2,1)} %refs_3_.1), channel_id=1, source_target_pairs={{0,2},{1,3},{2,0},{3,1},{4,6},{5,7},{6,4},{7,5},{8,10},{9,11},{10,... | collective-permute-start | bytes 442376 | tf_op jit(solution)/shard_map/ppermute | solution.py:651
  6.6 1.1 %collective-permute-done.3 = bf16[96,256]{1,0:T(8,128)(2,1)S(1)} collective-permute-done((bf16[96,256]{1,0:T(8,128)(2,1)S(1)}, bf16[96,256]{1,0:T(8,128)(2,1)S(1)}, u32[]{:S(2)}, u32[]{:S(2)}) %collective-permute-start.3) | collective-permute-done | bytes 49184 | tf_op jit(solution)/shard_map/ppermute | solution.py:651
  7.8 1.4 %collective-permute-start.4 = (bf16[192,256]{1,0:T(8,128)(2,1)S(1)}, bf16[192,256]{1,0:T(8,128)(2,1)S(1)}, u32[]{:S(2)}, u32[]{:S(2)}) collective-permute-start(bf16[192,256]{1,0:T(8,128)(2,1)S(1)} %maximum_select_fusion.2), channel_id=1, source_target_pairs={{0,8},{4,12},{8,0},{12,4},{16,24},{20,28},{24,16},{28,20},{1,9},{5... | collective-permute-start | bytes 294920 | tf_op jit(solution)/shard_map/ppermute | solution.py:651
  9.2 0.0 collective-permute-start.1
  9.2 1.5 %collective-permute-done.refs_4_ = bf16[48,1536]{1,0:T(8,128)(2,1)S(1)} collective-permute-done((bf16[48,1536]{1,0:T(8,128)(2,1)}, bf16[48,1536]{1,0:T(8,128)(2,1)S(1)}, u32[]{:S(2)}, u32[]{:S(2)}) %collective-permute-start) | collective-permute-done | bytes 147488 | tf_op jit(solution)/shard_map/ppermute | solution.py:651
  10.7 0.0 collective-permute-start.2
  10.7 1.8 %collective-permute-done.4 = bf16[192,256]{1,0:T(8,128)(2,1)S(1)} collective-permute-done((bf16[192,256]{1,0:T(8,128)(2,1)S(1)}, bf16[192,256]{1,0:T(8,128)(2,1)S(1)}, u32[]{:S(2)}, u32[]{:S(2)}) %collective-permute-start.4) | collective-permute-done | bytes 98336 | tf_op jit(solution)/shard_map/ppermute | solution.py:651
  12.4 0.1 maximum_select_fusion.1.refs_10_
  12.5 0.0 collective-permute-done.1.refs_5_
  12.5 0.0 collective-permute-done.2.refs_6_
  12.5 8.1 %front.1 = (f32[32,1,256]{2,1,0:T(1,128)}, f32[96,2048]{1,0:T(8,128)S(1)}, f32[96,2048]{1,0:T(8,128)}) custom-call(s32[1]{0:T(128)} %bitcast.refs_0_.index_ref, bf16[192,256]{1,0:T(8,128)(2,1)S(1)} %get-tuple-element.23.refs_1_, f32[1,2048]{1,0:T(1,128)} %bitcast.11, bf16[48,1536]{1,0:T(8,128)(2,1)} %refs_3_.1, ...), custom_call_target="tpu_custom_call" | custom-call | flops 2315255808 | bytes 8388608 | tf_op jit(solution)/shard_map/front/pallas_call | solution.py:159
  20.7 0.1 collective-permute-start.5
  20.8 1.8 %collective-permute-start.15 = (bf16[384,256]{1,0:T(8,128)(2,1)S(1)}, bf16[384,256]{1,0:T(8,128)(2,1)S(1)}, u32[]{:S(2)}, u32[]{:S(2)}) collective-permute-start(bf16[384,256]{1,0:T(8,128)(2,1)S(1)} %maximum_select_fusion.1.refs_10_), channel_id=1, source_target_pairs={{0,4},{4,0},{8,12},{12,8},{16,20},{20,16},{24,28},{28,24},{1,5},{5... | collective-permute-start | bytes 589832 | tf_op jit(solution)/shard_map/ppermute | solution.py:651
  22.5 0.2 collective-permute-start.8
  22.7 1.5 %collective-permute-start.7 = (bf16[512,256]{1,0:T(8,128)(2,1)}, bf16[512,256]{1,0:T(8,128)(2,1)S(1)}, u32[]{:S(2)}, u32[]{:S(2)}) collective-permute-start(bf16[512,256]{1,0:T(8,128)(2,1)} %own_ref.1), channel_id=1, source_target_pairs={{0,2},{1,3},{2,0},{3,1},{4,6},{5,7},{6,4},{7,5},{8,10},{9,11},{10,... | collective-permute-start | bytes 786440 | tf_op jit(solution)/shard_map/ppermute | solution.py:651
  24.2 0.2 collective-permute-start.9
  24.4 0.1 pad_add_fusion.1.refs_0_
  24.5 5.0 %all-to-all-start = ((f32[32,1,256]{2,1,0:T(1,128)}), f32[32,1,256]{2,1,0:T(1,128)S(1)}, u32[]{:S(2)}, u32[]{:S(2)}) async-start(f32[32,1,256]{2,1,0:T(1,128)} %get-tuple-element.34), calls=%async_computation | async-start | bytes 65536 | tf_op jit(solution)/shard_map/all_to_all | solution.py:680
  29.4 0.0 collective-permute-done.15
  29.5 0.2 maximum_select_fusion.refs_2_
  29.6 0.3 collective-permute-start.16
  29.9 7.5 %all-to-all-done.refs_2_ = f32[32,1,256]{2,1,0:T(1,128)S(1)} async-done(((f32[32,1,256]{2,1,0:T(1,128)}), f32[32,1,256]{2,1,0:T(1,128)S(1)}, u32[]{:S(2)}, u32[]{:S(2)}) %all-to-all-start) | async-done | bytes 32800 | tf_op jit(solution)/shard_map/all_to_all | solution.py:680
  37.4 0.1 reduce
  37.5 0.0 collective-permute-done.5.core_ref
  37.6 1.6 %collective-permute-start.6 = (f32[48,2048]{1,0:T(8,128)S(1)}, f32[48,2048]{1,0:T(8,128)}, u32[]{:S(2)}, u32[]{:S(2)}) collective-permute-start(f32[48,2048]{1,0:T(8,128)S(1)} %slice_add_fusion.refs_5_), channel_id=1, source_target_pairs={{0,2},{1,3},{2,0},{3,1},{4,6},{5,7},{6,4},{7,5},{8,10},{9,11},{10,... | collective-permute-start | bytes 1179656 | tf_op jit(solution)/shard_map/ppermute | solution.py:651
  39.2 0.1 mul.17
  39.3 0.1 mul.19.refs_4_
  39.4 0.0 collective-permute-done.8.other_ref.refs_7_
  39.4 0.0 collective-permute-done.7.partner_ref.refs_6_
  39.4 0.0 collective-permute-done.9.last_ref.refs_8_
  39.4 0.0 collective-permute-done.16.refs_3_
  39.4 7.6 %first_sweep.1 = (bf16[32,16,128]{2,1,0:T(8,128)(2,1)}, bf16[2048,1536]{1,0:T(8,128)(2,1)}) custom-call(s32[2]{0:T(128)S(1)} %pad_add_fusion.1.refs_0_, bf16[16384,256]{1,0:T(8,128)(2,1)} %refs_4_.1, bf16[768,256]{1,0:T(8,128)(2,1)S(1)} %maximum_select_fusion.refs_2_, bf16[768,256]{1,0:T(8,128)(2,1)} %collective-permute-done.16.refs_3_, ...), custom_call_target="tpu_custom_call" | custom-call | flops 1610612736 | bytes 6291456 | tf_op jit(solution)/shard_map/first_sweep/pallas_call | solution.py:433
  47.0 4.9 %all-to-all-start.1 = ((bf16[32,16,128]{2,1,0:T(8,128)(2,1)}), bf16[32,16,128]{2,1,0:T(8,128)(2,1)S(1)}, u32[]{:S(2)}, u32[]{:S(2)}) async-start(bf16[32,16,128]{2,1,0:T(8,128)(2,1)} %get-tuple-element.36), calls=%async_computation.1 | async-start | bytes 262144 | tf_op jit(solution)/shard_map/all_to_all | solution.py:680
  51.9 0.1 pad_add_fusion.refs_0_
  52.0 0.0 collective-permute-done.6.x_ref
  52.0 1.6 %student_middle.1 = (f32[48,256]{1,0:T(8,128)S(1)}, bf16[48,256]{1,0:T(8,128)(2,1)S(1)}, f32[48,128]{1,0:T(8,128)S(1)}) custom-call(s32[1]{0:T(128)} %bitcast.refs_0_.index_ref, f32[96,2048]{1,0:T(8,128)S(1)} %get-tuple-element.25.keep_ref, f32[96,2048]{1,0:T(8,128)S(1)} %collective-permute-done.5.core_ref, f32[48,2048]{1,0:T(8,128)} %collective-permute-done.6.x_ref, ...), custom_call_target="tpu_custom_call" | custom-call | flops 50331648 | bytes 2621440 | tf_op jit(solution)/shard_map/student_middle/pallas_call | solution.py:599
  53.6 1.8 %collective-permute-start.10 = (bf16[48,256]{1,0:T(8,128)(2,1)S(1)}, bf16[48,256]{1,0:T(8,128)(2,1)S(1)}, u32[]{:S(2)}, u32[]{:S(2)}) collective-permute-start(bf16[48,256]{1,0:T(8,128)(2,1)S(1)} %get-tuple-element.29.refs_2_), channel_id=1, source_target_pairs={{0,2},{1,3},{2,0},{3,1},{4,6},{5,7},{6,4},{7,5},{8,10},{9,11},{10,... | collective-permute-start | bytes 73736 | tf_op jit(solution)/shard_map/ppermute | solution.py:651
  55.5 4.6 %all-to-all-done.1.refs_1_ = bf16[32,16,128]{2,1,0:T(8,128)(2,1)S(1)} async-done(((bf16[32,16,128]{2,1,0:T(8,128)(2,1)}), bf16[32,16,128]{2,1,0:T(8,128)(2,1)S(1)}, u32[]{:S(2)}, u32[]{:S(2)}) %all-to-all-start.1) | async-done | bytes 131104 | tf_op jit(solution)/shard_map/all_to_all | solution.py:680
  60.1 4.4 %next_sweep.1 = bf16[32,16,128]{2,1,0:T(8,128)(2,1)} custom-call(bf16[2048,1536]{1,0:T(8,128)(2,1)} %get-tuple-element.35.refs_0_, bf16[32,16,128]{2,1,0:T(8,128)(2,1)S(1)} %all-to-all-done.1.refs_1_, bf16[48,256]{1,0:T(8,128)(2,1)S(1)} %get-tuple-element.29.refs_2_), custom_call_target="tpu_custom_call" | custom-call | flops 25165824 | bytes 6291456 | tf_op jit(solution)/shard_map/next_sweep/pallas_call | solution.py:519
  64.5 2.6 %all-to-all-start.2 = ((bf16[32,16,128]{2,1,0:T(8,128)(2,1)}), bf16[32,16,128]{2,1,0:T(8,128)(2,1)S(1)}, u32[]{:S(2)}, u32[]{:S(2)}) async-start(bf16[32,16,128]{2,1,0:T(8,128)(2,1)} %next_sweep.1), calls=%async_computation.2 | async-start | bytes 262144 | tf_op jit(solution)/shard_map/all_to_all | solution.py:680
  67.1 0.0 collective-permute-done.10
  67.1 0.2 collective-permute-start.11
  67.3 1.1 %collective-permute-done.11 = bf16[96,256]{1,0:T(8,128)(2,1)S(1)} collective-permute-done((bf16[96,256]{1,0:T(8,128)(2,1)S(1)}, bf16[96,256]{1,0:T(8,128)(2,1)S(1)}, u32[]{:S(2)}, u32[]{:S(2)}) %collective-permute-start.11) | collective-permute-done | bytes 49184 | tf_op jit(solution)/shard_map/ppermute | solution.py:651
  68.4 5.0 %attract.2.state_ref.refs_2_ = f32[192,512]{1,0:T(8,128)S(1)} custom-call(bf16[192,256]{1,0:T(8,128)(2,1)S(1)} %constant_dynamic-update-slice_fusion.emb_ref, f32[192,512]{1,0:T(8,128)S(1)} %concatenate.37.state_ref, bf16[16384,256]{1,0:T(8,128)(2,1)} %refs_4_.1), custom_call_target="tpu_custom_call" | custom-call | flops 1610612736 | bytes 4194304 | tf_op jit(solution)/shard_map/attract/pallas_call | solution.py:312
  73.5 1.8 %all-to-all-done.2.refs_1_ = bf16[32,16,128]{2,1,0:T(8,128)(2,1)S(1)} async-done(((bf16[32,16,128]{2,1,0:T(8,128)(2,1)}), bf16[32,16,128]{2,1,0:T(8,128)(2,1)S(1)}, u32[]{:S(2)}, u32[]{:S(2)}) %all-to-all-start.2) | async-done | bytes 131104 | tf_op jit(solution)/shard_map/all_to_all | solution.py:680
  75.3 3.8 %last_scales.1 = f32[8,1,2048]{2,1,0:T(1,128)} custom-call(bf16[2048,1536]{1,0:T(8,128)(2,1)} %get-tuple-element.35.refs_0_, bf16[32,16,128]{2,1,0:T(8,128)(2,1)S(1)} %all-to-all-done.2.refs_1_, f32[192,512]{1,0:T(8,128)S(1)} %attract.2.state_ref.refs_2_), custom_call_target="tpu_custom_call" | custom-call | flops 12582912 | bytes 6291456 | tf_op jit(solution)/shard_map/last_scales/pallas_call | solution.py:558
  79.1 4.0 %all-to-all-start.3 = ((f32[8,1,2048]{2,1,0:T(1,128)}), f32[8,1,2048]{2,1,0:T(1,128)S(1)}, u32[]{:S(2)}, u32[]{:S(2)}) async-start(f32[8,1,2048]{2,1,0:T(1,128)} %last_scales.1), calls=%async_computation.3 | async-start | bytes 131072 | tf_op jit(solution)/shard_map/all_to_all | solution.py:680
  83.1 5.1 %attract.3 = (f32[48,512]{1,0:T(8,128)S(1)}, f32[48,512]{1,0:T(8,128)S(1)}, f32[48,512]{1,0:T(8,128)S(1)}, f32[48,512]{1,0:T(8,128)S(1)}) custom-call(bf16[192,256]{1,0:T(8,128)(2,1)S(1)} %constant_dynamic-update-slice_fusion.emb_ref, f32[192,512]{1,0:T(8,128)S(1)} %attract.2.state_ref.refs_2_, bf16[16384,256]{1,0:T(8,128)(2,1)} %refs_4_.1), custom_call_target="tpu_custom_call" | custom-call | flops 1610612736 | bytes 4194304 | tf_op jit(solution)/shard_map/attract/pallas_call | solution.py:312
  88.2 0.1 collective-permute-start.12
  88.3 1.5 %collective-permute-start.13 = (f32[48,512]{1,0:T(8,128)S(1)}, f32[48,512]{1,0:T(8,128)S(1)}, u32[]{:S(2)}, u32[]{:S(2)}) collective-permute-start(f32[48,512]{1,0:T(8,128)S(1)} %get-tuple-element.32), channel_id=1, source_target_pairs={{0,2},{1,3},{2,0},{3,1},{4,6},{5,7},{6,4},{7,5},{8,10},{9,11},{10,... | collective-permute-start | bytes 294920 | tf_op jit(solution)/shard_map/ppermute | solution.py:651
  89.9 0.3 collective-permute-start.14
  90.2 0.0 all-to-all-done.3.refs_3_
  90.2 9.4 %repel.1 = (f32[48,384]{1,0:T(8,128)S(1)}, f32[48,384]{1,0:T(8,128)S(1)}, f32[48,384]{1,0:T(8,128)S(1)}, f32[48,384]{1,0:T(8,128)S(1)}) custom-call(s32[2]{0:T(128)S(1)} %pad_add_fusion.refs_0_, bf16[192,256]{1,0:T(8,128)(2,1)S(1)} %get-tuple-element.23.refs_1_, f32[32,1,256]{2,1,0:T(1,128)S(1)} %all-to-all-done.refs_2_, ...), custom_call_target="tpu_custom_call" | custom-call | flops 3221225472 | bytes 8388608 | tf_op jit(solution)/shard_map/repel/pallas_call | solution.py:234
  99.6 0.4 collective-permute-start.17
  100.0 1.5 %collective-permute-start.18 = (f32[48,384]{1,0:T(8,128)S(1)}, f32[48,384]{1,0:T(8,128)S(1)}, u32[]{:S(2)}, u32[]{:S(2)}) collective-permute-start(f32[48,384]{1,0:T(8,128)S(1)} %get-tuple-element.39), channel_id=1, source_target_pairs={{0,2},{1,3},{2,0},{3,1},{4,6},{5,7},{6,4},{7,5},{8,10},{9,11},{10,... | collective-permute-start | bytes 221192 | tf_op jit(solution)/shard_map/ppermute | solution.py:651
  101.5 0.0 collective-permute-done.12.rest_1_
  101.5 0.0 collective-permute-start.19
  101.6 0.0 collective-permute-done.13.rest_2_
  101.6 0.0 collective-permute-done.14.rest_3_
  101.6 2.8 %collective-permute-done.18.rest_6_ = f32[48,384]{1,0:T(8,128)S(1)} collective-permute-done((f32[48,384]{1,0:T(8,128)S(1)}, f32[48,384]{1,0:T(8,128)S(1)}, u32[]{:S(2)}, u32[]{:S(2)}) %collective-permute-start.18) | collective-permute-done | bytes 73760 | tf_op jit(solution)/shard_map/ppermute | solution.py:651
  104.4 1.6 %collective-permute-done.19.rest_7_ = f32[48,384]{1,0:T(8,128)S(1)} collective-permute-done((f32[48,384]{1,0:T(8,128)S(1)}, f32[48,384]{1,0:T(8,128)S(1)}, u32[]{:S(2)}, u32[]{:S(2)}) %collective-permute-start.19) | collective-permute-done | bytes 73760 | tf_op jit(solution)/shard_map/ppermute | solution.py:651
  106.0 0.8 finish.1
  (16 shorter events, 0.2 us)
Async XLA Ops:
  1.0 6.7 %collective-permute-start.3 = (bf16[96,256]{1,0:T(8,128)(2,1)S(1)}, bf16[96,256]{1,0:T(8,128)(2,1)S(1)}, u32[]{:S(2)}, u32[]{:S(2)}) collective-permute-start(bf16[96,256]{1,0:T(8,128)(2,1)S(1)} %get-tuple-element.24), channel_id=1, source_target_pairs={{0,16},{4,20},{8,24},{12,28},{16,0},{20,4},{24,8},{28,12},{1,17},{... | collective-permute-start | bytes 147464 | tf_op jit(solution)/shard_map/ppermute | solution.py:651
  5.1 5.5 %collective-permute-start = (bf16[48,1536]{1,0:T(8,128)(2,1)}, bf16[48,1536]{1,0:T(8,128)(2,1)S(1)}, u32[]{:S(2)}, u32[]{:S(2)}) collective-permute-start(bf16[48,1536]{1,0:T(8,128)(2,1)} %refs_3_.1), channel_id=1, source_target_pairs={{0,2},{1,3},{2,0},{3,1},{4,6},{5,7},{6,4},{7,5},{8,10},{9,11},{10,... | collective-permute-start | bytes 442376 | tf_op jit(solution)/shard_map/ppermute | solution.py:651
  7.8 4.7 %collective-permute-start.4 = (bf16[192,256]{1,0:T(8,128)(2,1)S(1)}, bf16[192,256]{1,0:T(8,128)(2,1)S(1)}, u32[]{:S(2)}, u32[]{:S(2)}) collective-permute-start(bf16[192,256]{1,0:T(8,128)(2,1)S(1)} %maximum_select_fusion.2), channel_id=1, source_target_pairs={{0,8},{4,12},{8,0},{12,4},{16,24},{20,28},{24,16},{28,20},{1,9},{5... | collective-permute-start | bytes 294920 | tf_op jit(solution)/shard_map/ppermute | solution.py:651
  9.2 3.3 %collective-permute-start.1 = (bf16[48,1536]{1,0:T(8,128)(2,1)}, bf16[48,1536]{1,0:T(8,128)(2,1)S(1)}, u32[]{:S(2)}, u32[]{:S(2)}) collective-permute-start(bf16[48,1536]{1,0:T(8,128)(2,1)} %refs_3_.1), channel_id=1, source_target_pairs={{0,1},{1,0},{2,3},{3,2},{4,5},{5,4},{6,7},{7,6},{8,9},{9,8},{10,11... | collective-permute-start | bytes 442376 | tf_op jit(solution)/shard_map/ppermute | solution.py:651
  10.7 1.9 %collective-permute-start.2 = (bf16[48,1536]{1,0:T(8,128)(2,1)S(1)}, bf16[48,1536]{1,0:T(8,128)(2,1)S(1)}, u32[]{:S(2)}, u32[]{:S(2)}) collective-permute-start(bf16[48,1536]{1,0:T(8,128)(2,1)S(1)} %collective-permute-done.refs_4_), channel_id=1, source_target_pairs={{0,1},{1,0},{2,3},{3,2},{4,5},{5,4},{6,7},{7,6},{8,9},{9,8},{10,11... | collective-permute-start | bytes 442376 | tf_op jit(solution)/shard_map/ppermute | solution.py:651
  20.7 16.9 %collective-permute-start.5 = (f32[96,2048]{1,0:T(8,128)}, f32[96,2048]{1,0:T(8,128)S(1)}, u32[]{:S(2)}, u32[]{:S(2)}) collective-permute-start(f32[96,2048]{1,0:T(8,128)} %get-tuple-element.26), channel_id=1, source_target_pairs={{0,1},{1,0},{2,3},{3,2},{4,5},{5,4},{6,7},{7,6},{8,9},{9,8},{10,11... | collective-permute-start | bytes 2359304 | tf_op jit(solution)/shard_map/ppermute | solution.py:651
  20.8 8.7 %collective-permute-start.15 = (bf16[384,256]{1,0:T(8,128)(2,1)S(1)}, bf16[384,256]{1,0:T(8,128)(2,1)S(1)}, u32[]{:S(2)}, u32[]{:S(2)}) collective-permute-start(bf16[384,256]{1,0:T(8,128)(2,1)S(1)} %maximum_select_fusion.1.refs_10_), channel_id=1, source_target_pairs={{0,4},{4,0},{8,12},{12,8},{16,20},{20,16},{24,28},{28,24},{1,5},{5... | collective-permute-start | bytes 589832 | tf_op jit(solution)/shard_map/ppermute | solution.py:651
  22.5 16.8 %collective-permute-start.8 = (bf16[512,256]{1,0:T(8,128)(2,1)}, bf16[512,256]{1,0:T(8,128)(2,1)S(1)}, u32[]{:S(2)}, u32[]{:S(2)}) collective-permute-start(bf16[512,256]{1,0:T(8,128)(2,1)} %own_ref.1), channel_id=1, source_target_pairs={{0,1},{1,0},{2,3},{3,2},{4,5},{5,4},{6,7},{7,6},{8,9},{9,8},{10,11... | collective-permute-start | bytes 786440 | tf_op jit(solution)/shard_map/ppermute | solution.py:651
  22.7 16.7 %collective-permute-start.7 = (bf16[512,256]{1,0:T(8,128)(2,1)}, bf16[512,256]{1,0:T(8,128)(2,1)S(1)}, u32[]{:S(2)}, u32[]{:S(2)}) collective-permute-start(bf16[512,256]{1,0:T(8,128)(2,1)} %own_ref.1), channel_id=1, source_target_pairs={{0,2},{1,3},{2,0},{3,1},{4,6},{5,7},{6,4},{7,5},{8,10},{9,11},{10,... | collective-permute-start | bytes 786440 | tf_op jit(solution)/shard_map/ppermute | solution.py:651
  24.2 15.2 %collective-permute-start.9 = (bf16[512,256]{1,0:T(8,128)(2,1)}, bf16[512,256]{1,0:T(8,128)(2,1)S(1)}, u32[]{:S(2)}, u32[]{:S(2)}) collective-permute-start(bf16[512,256]{1,0:T(8,128)(2,1)} %own_ref.1), channel_id=1, source_target_pairs={{0,3},{1,2},{2,1},{3,0},{4,7},{5,6},{6,5},{7,4},{8,11},{9,10},{10,... | collective-permute-start | bytes 786440 | tf_op jit(solution)/shard_map/ppermute | solution.py:651
  24.5 12.9 %all-to-all-start = ((f32[32,1,256]{2,1,0:T(1,128)}), f32[32,1,256]{2,1,0:T(1,128)S(1)}, u32[]{:S(2)}, u32[]{:S(2)}) async-start(f32[32,1,256]{2,1,0:T(1,128)} %get-tuple-element.34), calls=%async_computation | async-start | bytes 65536 | tf_op jit(solution)/shard_map/all_to_all | solution.py:680
  29.6 9.8 %collective-permute-start.16 = (bf16[768,256]{1,0:T(8,128)(2,1)S(1)}, bf16[768,256]{1,0:T(8,128)(2,1)}, u32[]{:S(2)}, u32[]{:S(2)}) collective-permute-start(bf16[768,256]{1,0:T(8,128)(2,1)S(1)} %maximum_select_fusion.refs_2_), channel_id=1, source_target_pairs={{0,1},{1,0},{2,3},{3,2},{4,5},{5,4},{6,7},{7,6},{8,9},{9,8},{10,11... | collective-permute-start | bytes 1179656 | tf_op jit(solution)/shard_map/ppermute | solution.py:651
  37.6 14.4 %collective-permute-start.6 = (f32[48,2048]{1,0:T(8,128)S(1)}, f32[48,2048]{1,0:T(8,128)}, u32[]{:S(2)}, u32[]{:S(2)}) collective-permute-start(f32[48,2048]{1,0:T(8,128)S(1)} %slice_add_fusion.refs_5_), channel_id=1, source_target_pairs={{0,2},{1,3},{2,0},{3,1},{4,6},{5,7},{6,4},{7,5},{8,10},{9,11},{10,... | collective-permute-start | bytes 1179656 | tf_op jit(solution)/shard_map/ppermute | solution.py:651
  47.0 13.1 %all-to-all-start.1 = ((bf16[32,16,128]{2,1,0:T(8,128)(2,1)}), bf16[32,16,128]{2,1,0:T(8,128)(2,1)S(1)}, u32[]{:S(2)}, u32[]{:S(2)}) async-start(bf16[32,16,128]{2,1,0:T(8,128)(2,1)} %get-tuple-element.36), calls=%async_computation.1 | async-start | bytes 262144 | tf_op jit(solution)/shard_map/all_to_all | solution.py:680
  53.6 13.4 %collective-permute-start.10 = (bf16[48,256]{1,0:T(8,128)(2,1)S(1)}, bf16[48,256]{1,0:T(8,128)(2,1)S(1)}, u32[]{:S(2)}, u32[]{:S(2)}) collective-permute-start(bf16[48,256]{1,0:T(8,128)(2,1)S(1)} %get-tuple-element.29.refs_2_), channel_id=1, source_target_pairs={{0,2},{1,3},{2,0},{3,1},{4,6},{5,7},{6,4},{7,5},{8,10},{9,11},{10,... | collective-permute-start | bytes 73736 | tf_op jit(solution)/shard_map/ppermute | solution.py:651
  64.5 10.8 %all-to-all-start.2 = ((bf16[32,16,128]{2,1,0:T(8,128)(2,1)}), bf16[32,16,128]{2,1,0:T(8,128)(2,1)S(1)}, u32[]{:S(2)}, u32[]{:S(2)}) async-start(bf16[32,16,128]{2,1,0:T(8,128)(2,1)} %next_sweep.1), calls=%async_computation.2 | async-start | bytes 262144 | tf_op jit(solution)/shard_map/all_to_all | solution.py:680
  67.1 1.3 %collective-permute-start.11 = (bf16[96,256]{1,0:T(8,128)(2,1)S(1)}, bf16[96,256]{1,0:T(8,128)(2,1)S(1)}, u32[]{:S(2)}, u32[]{:S(2)}) collective-permute-start(bf16[96,256]{1,0:T(8,128)(2,1)S(1)} %pad_maximum_fusion), channel_id=1, source_target_pairs={{0,1},{1,0},{2,3},{3,2},{4,5},{5,4},{6,7},{7,6},{8,9},{9,8},{10,11... | collective-permute-start | bytes 147464 | tf_op jit(solution)/shard_map/ppermute | solution.py:651
  79.1 11.1 %all-to-all-start.3 = ((f32[8,1,2048]{2,1,0:T(1,128)}), f32[8,1,2048]{2,1,0:T(1,128)S(1)}, u32[]{:S(2)}, u32[]{:S(2)}) async-start(f32[8,1,2048]{2,1,0:T(1,128)} %last_scales.1), calls=%async_computation.3 | async-start | bytes 131072 | tf_op jit(solution)/shard_map/all_to_all | solution.py:680
  88.2 13.3 %collective-permute-start.12 = (f32[48,512]{1,0:T(8,128)S(1)}, f32[48,512]{1,0:T(8,128)S(1)}, u32[]{:S(2)}, u32[]{:S(2)}) collective-permute-start(f32[48,512]{1,0:T(8,128)S(1)} %get-tuple-element.31), channel_id=1, source_target_pairs={{0,1},{1,0},{2,3},{3,2},{4,5},{5,4},{6,7},{7,6},{8,9},{9,8},{10,11... | collective-permute-start | bytes 294920 | tf_op jit(solution)/shard_map/ppermute | solution.py:651
  88.3 13.3 %collective-permute-start.13 = (f32[48,512]{1,0:T(8,128)S(1)}, f32[48,512]{1,0:T(8,128)S(1)}, u32[]{:S(2)}, u32[]{:S(2)}) collective-permute-start(f32[48,512]{1,0:T(8,128)S(1)} %get-tuple-element.32), channel_id=1, source_target_pairs={{0,2},{1,3},{2,0},{3,1},{4,6},{5,7},{6,4},{7,5},{8,10},{9,11},{10,... | collective-permute-start | bytes 294920 | tf_op jit(solution)/shard_map/ppermute | solution.py:651
  89.9 11.7 %collective-permute-start.14 = (f32[48,512]{1,0:T(8,128)S(1)}, f32[48,512]{1,0:T(8,128)S(1)}, u32[]{:S(2)}, u32[]{:S(2)}) collective-permute-start(f32[48,512]{1,0:T(8,128)S(1)} %get-tuple-element.33), channel_id=1, source_target_pairs={{0,3},{1,2},{2,1},{3,0},{4,7},{5,6},{6,5},{7,4},{8,11},{9,10},{10,... | collective-permute-start | bytes 294920 | tf_op jit(solution)/shard_map/ppermute | solution.py:651
  99.6 2.0 %collective-permute-start.17 = (f32[48,384]{1,0:T(8,128)S(1)}, f32[48,384]{1,0:T(8,128)S(1)}, u32[]{:S(2)}, u32[]{:S(2)}) collective-permute-start(f32[48,384]{1,0:T(8,128)S(1)} %get-tuple-element.38), channel_id=1, source_target_pairs={{0,1},{1,0},{2,3},{3,2},{4,5},{5,4},{6,7},{7,6},{8,9},{9,8},{10,11... | collective-permute-start | bytes 221192 | tf_op jit(solution)/shard_map/ppermute | solution.py:651
  100.0 4.4 %collective-permute-start.18 = (f32[48,384]{1,0:T(8,128)S(1)}, f32[48,384]{1,0:T(8,128)S(1)}, u32[]{:S(2)}, u32[]{:S(2)}) collective-permute-start(f32[48,384]{1,0:T(8,128)S(1)} %get-tuple-element.39), channel_id=1, source_target_pairs={{0,2},{1,3},{2,0},{3,1},{4,6},{5,7},{6,4},{7,5},{8,10},{9,11},{10,... | collective-permute-start | bytes 221192 | tf_op jit(solution)/shard_map/ppermute | solution.py:651
  101.5 4.5 %collective-permute-start.19 = (f32[48,384]{1,0:T(8,128)S(1)}, f32[48,384]{1,0:T(8,128)S(1)}, u32[]{:S(2)}, u32[]{:S(2)}) collective-permute-start(f32[48,384]{1,0:T(8,128)S(1)} %get-tuple-element.40), channel_id=1, source_target_pairs={{0,3},{1,2},{2,1},{3,0},{4,7},{5,6},{6,5},{7,4},{8,11},{9,10},{10,... | collective-permute-start | bytes 221192 | tf_op jit(solution)/shard_map/ppermute | solution.py:651

commit v12 on v11

--- a/solution.py
+++ b/solution.py
@@ -219,12 +219,21 @@
 
     lax.fori_loop(0, steps, step, 0)
     total = jnp.sum(sum_ref[...], axis=1, keepdims=True)
+    lanes = lax.broadcasted_iota(jnp.int32, sum_ref.shape, 1)
     sum_ref[...] = jnp.broadcast_to(total, sum_ref.shape)
     share = out_refs[0].shape[0]
+    lanes = lanes[:share, :]
     for flip, out_ref in enumerate(out_refs):
         span = part(index_ref[1] ^ flip, share)
-        out_ref[:, :width] = acc_ref[span, :]
-        out_ref[:, width:] = sum_ref[span, :]
+        total = sum_ref[span, :]
+        out_ref[:, :width] = acc_ref[span, :].astype(out_ref.dtype)
+        if flip == 0:
+            out_ref[:, width:] = jnp.where(lanes == 0, total, 0.0)
+        else:
+            high = total.astype(jnp.bfloat16).astype(jnp.float32)
+            middle = (total - high).astype(jnp.bfloat16).astype(jnp.float32)
+            pieces = jnp.where(lanes == 0, high, jnp.where(lanes == 1, middle, total - high - middle))
+            out_ref[:, width:] = jnp.where(lanes < 3, pieces, 0.0).astype(jnp.bfloat16)
 
 
 def repel(index, unit, tops, scale, protos, order, proto_size):
@@ -235,7 +244,10 @@
         skipping(functools.partial(repel_kernel, proto_size), 5, len(order)),
         in_specs=[whole(pltpu.SMEM), whole(), whole(), whole(), whole(pl.ANY)] + [whole(pl.ANY)] * len(order),
         out_specs=[whole()] * proto_size,
-        out_shape=[jax.ShapeDtypeStruct((rows // proto_size, width + 128), jnp.float32)] * proto_size,
+        out_shape=[
+            jax.ShapeDtypeStruct((rows // proto_size, width + 128), jnp.bfloat16 if flip else jnp.float32)
+            for flip in range(proto_size)
+        ],
         scratch_shapes=[
             pltpu.VMEM((steps, block, width), jnp.bfloat16),
             pltpu.SemaphoreType.DMA((steps,)),
@@ -365,21 +377,18 @@
 
 
 def first_sweep_kernel(
-    protos_total, index_ref, protos_hbm, mine_hbm, other_hbm, bias_ref, copies_ref, weights_hbm,
-    protos_ref, units_ref, weights_ref, rounded_ref, scale_ref, totals_ref, sems, out_sems,
+    chunk, protos_total, index_ref, protos_hbm, mine_hbm, other_hbm, bias_ref, copies_ref, weights_hbm, protos_ref, units_ref, weights_ref, rounded_ref, scale_ref, sems, out_sems,
 ):
-    steps, chunk, crops_total = rounded_ref.shape
-    thin = steps * chunk
+    thin, crops_total = weights_ref.shape
     half = mine_hbm.shape[0]
     core = index_ref[1]
     copies = (
+        pltpu.make_async_copy(protos_hbm.at[part(index_ref[0], thin), :], protos_ref, sems.at[0]),
         pltpu.make_async_copy(mine_hbm, units_ref.at[part(core, half), :], sems.at[1]),
         pltpu.make_async_copy(other_hbm, units_ref.at[part(1 - core, half), :], sems.at[2]),
-        pltpu.make_async_copy(protos_hbm.at[part(index_ref[0], thin), :], protos_ref, sems.at[0]),
     )
     for copy in copies:
         copy.start()
-    totals_ref[...] = jnp.zeros(totals_ref.shape, jnp.float32)
     for copy in copies:
         copy.wait()
 
@@ -388,50 +397,42 @@
             rounded_ref.at[index], weights_hbm.at[part(index, chunk), :], out_sems.at[index]
         )
 
-    def weigh(index, slot):
-        protos = protos_ref[part(index, chunk), :]
+    def weigh(index, carry):
+        rows = part(index, chunk)
+        protos = protos_ref[rows, :]
         folded = jnp.zeros((chunk, 128), jnp.float32)
         for start in range(0, crops_total, TILE):
             columns = slice(start, start + TILE)
             products = scores(protos, units_ref[columns, :])
             weights = jnp.exp2(products * teacher_rate + bias_ref[:, columns])
-            weights_ref[slot, :, columns] = weights
+            weights_ref[rows, columns] = weights
             rounded_ref[index, :, columns] = weights.astype(jnp.bfloat16)
             folded = folded + lane_fold(weights, jnp.add)
         sums = jnp.sum(folded, axis=1, keepdims=True)
-        scale_ref[slot] = jnp.broadcast_to(1.0 / (protos_total * sums), (chunk, 128))
+        scale_ref[rows, :] = jnp.broadcast_to(1.0 / (protos_total * sums), (chunk, 128))
         chunk_out(index).start()
-
-    def add_up(slot):
-        for lane in range(0, crops_total, 128):
-            total = totals_ref[:, lane : lane + 128]
-            for row in range(0, chunk, 64):
-                scaled = weights_ref[slot, row : row + 64, lane : lane + 128] * scale_ref[slot, row : row + 64, :]
-                total = total + jnp.sum(scaled.reshape(-1, 8, 128), axis=0)
-            totals_ref[:, lane : lane + 128] = total
-
-    weigh(0, 0)
-
-    def sweep(index, carry):
-        slot = lax.rem(index, 2)
-        weigh(index, slot)
-        add_up(1 - slot)
         return carry
 
-    lax.fori_loop(1, steps, sweep, 0)
-    add_up((steps - 1) % 2)
-    give_sums(copies_ref, jnp.sum(totals_ref[...], axis=0, keepdims=True))
-    for index in range(steps):
+    lax.fori_loop(0, thin // chunk, weigh, 0)
+    small = min(thin, 64)
+
+    def add_up(index, totals):
+        rows = part(index, small)
+        scaled = weights_ref[rows, :] * jnp.tile(scale_ref[rows, :], (1, crops_total // 128))
+        return totals + jnp.sum(scaled.reshape(-1, 8, crops_total), axis=0)
+
+    totals = lax.fori_loop(0, thin // small, add_up, jnp.zeros((8, crops_total), jnp.float32))
+    give_sums(copies_ref, jnp.sum(totals, axis=0, keepdims=True))
+    for index in range(thin // chunk):
         chunk_out(index).wait()
 
 
 def first_sweep(index, protos, mine, other, base, order, copies, thin, protos_total):
     width = protos.shape[1]
     crops_total = 2 * mine.shape[0]
-    chunk = min(thin, 512) if crops_total <= 2048 else 128
-    steps = thin // chunk
-    return pl.pallas_call(
-        skipping(functools.partial(first_sweep_kernel, protos_total), 5, len(order)),
+    chunk = min(thin, 1024)
+    return pl.pallas_call(
+        skipping(functools.partial(first_sweep_kernel, chunk, protos_total), 5, len(order)),
         in_specs=[whole(pltpu.SMEM), whole(pl.ANY), whole(pl.ANY), whole(pl.ANY), whole()]
         + [whole(pl.ANY)] * len(order),
         out_specs=[whole(), whole(pl.ANY)],
@@ -442,12 +443,11 @@
         scratch_shapes=[
             pltpu.VMEM((thin, width), jnp.bfloat16),
             pltpu.VMEM((crops_total, width), jnp.bfloat16),
-            pltpu.VMEM((2, chunk, crops_total), jnp.float32),
-            pltpu.VMEM((steps, chunk, crops_total), jnp.bfloat16),
-            pltpu.VMEM((2, chunk, 128), jnp.float32),
-            pltpu.VMEM((8, crops_total), jnp.float32),
+            pltpu.VMEM((thin, crops_total), jnp.float32),
+            pltpu.VMEM((thin // chunk, chunk, crops_total), jnp.bfloat16),
+            pltpu.VMEM((thin, 128), jnp.float32),
             pltpu.SemaphoreType.DMA((3,)),
-            pltpu.SemaphoreType.DMA((steps,)),
+            pltpu.SemaphoreType.DMA((thin // chunk,)),
         ],
         compiler_params=params(32 if crops_total <= 2048 else 56),
         cost_estimate=cost(2 * thin * width * crops_total, 2 * thin * crops_total, thin * crops_total),
@@ -624,11 +624,11 @@
         row_sum = row_sum + ref[:, width : width + 128] * fade
         attract_sum = attract_sum + ref[:, :width] * jnp.tile(fade, (1, width // 128))
     for ref in repels:
-        column_sum = column_sum + ref[:, width:]
-        repel_sum = repel_sum + ref[:, :width]
+        column_sum = column_sum + jnp.sum(ref[:, width:].astype(jnp.float32), axis=1, keepdims=True)
+        repel_sum = repel_sum + ref[:, :width].astype(jnp.float32)
     emb_grad = (
         attract_sum / jnp.tile(row_sum, (1, width // 128))
-        - repel_sum / jnp.tile(column_sum, (1, width // 128))
+        - repel_sum / column_sum
     ) / student_temp
     unit = unit_ref[...]
     along = jnp.sum(unit * emb_grad, axis=1, keepdims=True)
@@ -704,9 +704,10 @@
 
     crops_x = swap(crops, "proto", 2)
     rows = [crops, crops_x, swap(crops, "proto", 1), swap(crops_x, "proto", 1)]
-    thirds = [w_third, swap(w_third, "proto", 2), swap(w_third, "proto", 1), swap(w_third, "proto", 3)]
+    third_x = swap(w_third, "proto", 2)
+    thirds = [w_third, third_x, swap(w_third, "proto", 1), swap(third_x, "proto", 1)]
     top_copies, keep, give = front(
-        proto_ref, own_unit, b_first, rows, w_first, w_second, protos, (stages[2],), devices, 8
+        proto_ref, own_unit, b_first, rows, w_first, w_second, protos, (stages[2], third_x), devices, 8
     )
     all_tops = all_to_all(top_copies, BOTH)
     tops = jnp.max(all_tops.reshape(batch_size, proto_size, 256)[:, :, :group_rows], axis=1)
@@ -719,16 +720,15 @@
     unit, rounded, lengths = student_middle(
         proto_ref, keep, core_rows, x_rows, b_second, thirds, b_third
     )
-    emb_pair = jnp.concatenate([rounded, swap(rounded, "proto", 2)])
-    student_emb = jnp.concatenate([emb_pair, swap(emb_pair, "proto", 1)])
+    student_emb = jnp.concatenate([rounded] + [swap(rounded, "proto", flip) for flip in range(1, proto_size)])
     empty = jnp.concatenate(
         [jnp.zeros((group_rows, width + 128), jnp.float32), jnp.full((group_rows, 128), -1e30, jnp.float32)], axis=1
     )
     (state,) = attract(student_emb, empty, protos, 0, count // 2, 4, 1)
     slots = attract(student_emb, state, protos, count // 2, count // 2, 4, proto_size)
-    attract_parts = send_blocks([slots[0], slots[2], slots[1], slots[3]])
-
-    copies, weights = first_sweep(thin_ref, protos, mine, other, base, (x_sent, *thirds[1:]), devices, thin, protos_total)
+    attract_parts = send_blocks(slots)
+
+    copies, weights = first_sweep(thin_ref, protos, mine, other, base, (x_sent, *thirds[2:]), devices, thin, protos_total)
     for _ in range(ITERS - 2):
         copies = next_sweep(weights, all_to_all(copies, BOTH), (rounded,), protos_total)
     scale_copies = last_scales(weights, all_to_all(copies, BOTH), (state,), batch_size, protos_total)

time: 107 us -> 101 us (0.944)
  starting transfers between devices: 35 us -> 27.6 us
  waiting for transfers between devices: 23.8 us -> 25.3 us
    all_to_all x4, starting transfers between devices: 16.4 us -> 11.4 us  [all_to_all(): return lax.all_to_all(copies, axes, 0, 0, tiled=True)]
    ppermute x20 -> x21, waiting for transfers between devices: 9.92 us -> 14 us  [swap(): lax.ppermute(values, axis, [(i, i ^ flip) for i in range(lax.axis_size(ax...]
    all_to_all x4, waiting for transfers between devices: 13.9 us -> 11.3 us  [all_to_all(): return lax.all_to_all(copies, axes, 0, 0, tiled=True)]
    ppermute x20 -> x21, starting transfers between devices: 18.5 us -> 16.2 us  [swap(): lax.ppermute(values, axis, [(i, i ^ flip) for i in range(lax.axis_size(ax...]
  transfers between devices with their start and end apart: 24 -> 25, of which waited for: 9 -> 11; matrix products, arithmetic and copies ran while one was open for 1% -> 1% of each run, Pallas kernels for 31% -> 32%
where the time goes in v12:
time: 101 us; the launch traced here: 100 us
  Pallas kernels  46.1 us (46%)
  starting transfers between devices  27.6 us (27%)
  waiting for transfers between devices  25.3 us (25%)
    ppermute x21, starting transfers between devices, swap(): lax.ppermute(values, axis, [(i, i ^ flip) for i in range(lax.axis_size(ax...  16.2 us
    ppermute x21, waiting for transfers between devices, swap(): lax.ppermute(values, axis, [(i, i ^ flip) for i in range(lax.axis_size(ax...  14 us
    all_to_all x4, starting transfers between devices, all_to_all(): return lax.all_to_all(copies, axes, 0, 0, tiled=True)  11.4 us
    all_to_all x4, waiting for transfers between devices, all_to_all(): return lax.all_to_all(copies, axes, 0, 0, tiled=True)  11.3 us
    pallas_call x2, Pallas kernels, attract(): pl.pallas_call(functools.partial(attract_kernel, first_row, outputs > 1),...  10.2 us
    pallas_call x1, Pallas kernels, repel(): pl.pallas_call(skipping(functools.partial(repel_kernel, proto_size), 5, l...  9.48 us
    pallas_call x1, Pallas kernels, front(): pl.pallas_call(skipping(front_kernel, 10, len(order)), in_specs=[whole(pl...  8.13 us
    pallas_call x1, Pallas kernels, first_sweep(): pl.pallas_call(skipping(functools.partial(first_sweep_kernel, chunk, prot...  6.72 us
  transfers between devices with their start and end apart: 25, of which 11 were waited for; matrix products, arithmetic and copies ran while one was open for 1% of the time, Pallas kernels for 32%

profile of v12, /device:TPU:0, one launch (start us, length us, event | category | flops | bytes accessed | tf_op | source)
XLA Modules:
  0.0 100.1 jit_solution(17683277782570560009)
XLA Ops:
  0.0 1.0 %teacher_units.1 = (bf16[192,256]{1,0:T(8,128)(2,1)S(1)}, bf16[96,256]{1,0:T(8,128)(2,1)S(1)}) custom-call(s32[1]{0:T(128)} %bitcast.1.core_ref, bf16[192,256]{1,0:T(8,128)(2,1)} %emb_ref.1), custom_call_target="tpu_custom_call" | custom-call | flops 196608 | bytes 393216 | tf_op jit(solution)/shard_map/teacher_units/pallas_call | solution.py:96
  1.0 4.1 %collective-permute-start.3 = (bf16[96,256]{1,0:T(8,128)(2,1)S(1)}, bf16[96,256]{1,0:T(8,128)(2,1)S(1)}, u32[]{:S(2)}, u32[]{:S(2)}) collective-permute-start(bf16[96,256]{1,0:T(8,128)(2,1)S(1)} %get-tuple-element.24), channel_id=1, source_target_pairs={{0,16},{4,20},{8,24},{12,28},{16,0},{20,4},{24,8},{28,12},{1,17},{... | collective-permute-start | bytes 147464 | tf_op jit(solution)/shard_map/ppermute | solution.py:651
  5.1 1.5 %collective-permute-start = (bf16[48,1536]{1,0:T(8,128)(2,1)}, bf16[48,1536]{1,0:T(8,128)(2,1)S(1)}, u32[]{:S(2)}, u32[]{:S(2)}) collective-permute-start(bf16[48,1536]{1,0:T(8,128)(2,1)} %refs_3_.1), channel_id=1, source_target_pairs={{0,2},{1,3},{2,0},{3,1},{4,6},{5,7},{6,4},{7,5},{8,10},{9,11},{10,... | collective-permute-start | bytes 442376 | tf_op jit(solution)/shard_map/ppermute | solution.py:651
  6.6 0.5 collective-permute-start.5
  7.2 0.6 collective-permute-done.3
  7.8 1.4 %collective-permute-start.4 = (bf16[192,256]{1,0:T(8,128)(2,1)S(1)}, bf16[192,256]{1,0:T(8,128)(2,1)S(1)}, u32[]{:S(2)}, u32[]{:S(2)}) collective-permute-start(bf16[192,256]{1,0:T(8,128)(2,1)S(1)} %maximum_select_fusion.2), channel_id=1, source_target_pairs={{0,8},{4,12},{8,0},{12,4},{16,24},{20,28},{24,16},{28,20},{1,9},{5... | collective-permute-start | bytes 294920 | tf_op jit(solution)/shard_map/ppermute | solution.py:651
  9.2 0.0 collective-permute-start.1
  9.2 2.9 %collective-permute-done.refs_4_ = bf16[48,1536]{1,0:T(8,128)(2,1)S(1)} collective-permute-done((bf16[48,1536]{1,0:T(8,128)(2,1)}, bf16[48,1536]{1,0:T(8,128)(2,1)S(1)}, u32[]{:S(2)}, u32[]{:S(2)}) %collective-permute-start) | collective-permute-done | bytes 147488 | tf_op jit(solution)/shard_map/ppermute | solution.py:651
  12.1 0.0 collective-permute-start.2
  12.1 0.3 collective-permute-done.4
  12.4 0.1 maximum_select_fusion.1.refs_10_
  12.5 0.0 collective-permute-done.1.refs_5_
  12.5 3.8 %collective-permute-done.5.refs_11_.partner_ref = bf16[512,256]{1,0:T(8,128)(2,1)S(1)} collective-permute-done((bf16[512,256]{1,0:T(8,128)(2,1)}, bf16[512,256]{1,0:T(8,128)(2,1)S(1)}, u32[]{:S(2)}, u32[]{:S(2)}) %collective-permute-start.5) | collective-permute-done | bytes 262176 | tf_op jit(solution)/shard_map/ppermute | solution.py:651
  16.3 0.0 collective-permute-done.2.refs_6_
  16.3 8.1 %front.1 = (f32[32,1,256]{2,1,0:T(1,128)}, f32[96,2048]{1,0:T(8,128)S(1)}, f32[96,2048]{1,0:T(8,128)}) custom-call(s32[1]{0:T(128)} %bitcast.refs_0_.index_ref, bf16[192,256]{1,0:T(8,128)(2,1)S(1)} %get-tuple-element.23.refs_1_, f32[1,2048]{1,0:T(1,128)} %bitcast.11, bf16[48,1536]{1,0:T(8,128)(2,1)} %refs_3_.1, ...), custom_call_target="tpu_custom_call" | custom-call | flops 2315255808 | bytes 8388608 | tf_op jit(solution)/shard_map/front/pallas_call | solution.py:159
  24.4 0.1 collective-permute-start.6
  24.5 1.6 %collective-permute-start.16 = (bf16[384,256]{1,0:T(8,128)(2,1)S(1)}, bf16[384,256]{1,0:T(8,128)(2,1)S(1)}, u32[]{:S(2)}, u32[]{:S(2)}) collective-permute-start(bf16[384,256]{1,0:T(8,128)(2,1)S(1)} %maximum_select_fusion.1.refs_10_), channel_id=1, source_target_pairs={{0,4},{4,0},{8,12},{12,8},{16,20},{20,16},{24,28},{28,24},{1,5},{5... | collective-permute-start | bytes 589832 | tf_op jit(solution)/shard_map/ppermute | solution.py:651
  26.1 0.2 collective-permute-start.8
  26.2 0.1 pad_add_fusion.1.refs_0_
  26.3 0.3 collective-permute-start.9
  26.7 2.9 %all-to-all-start = ((f32[32,1,256]{2,1,0:T(1,128)}), f32[32,1,256]{2,1,0:T(1,128)S(1)}, u32[]{:S(2)}, u32[]{:S(2)}) async-start(f32[32,1,256]{2,1,0:T(1,128)} %get-tuple-element.34), calls=%async_computation | async-start | bytes 65536 | tf_op jit(solution)/shard_map/all_to_all | solution.py:680
  29.5 2.3 %collective-permute-done.16 = bf16[384,256]{1,0:T(8,128)(2,1)S(1)} collective-permute-done((bf16[384,256]{1,0:T(8,128)(2,1)S(1)}, bf16[384,256]{1,0:T(8,128)(2,1)S(1)}, u32[]{:S(2)}, u32[]{:S(2)}) %collective-permute-start.16) | collective-permute-done | bytes 196640 | tf_op jit(solution)/shard_map/ppermute | solution.py:651
  31.8 0.2 maximum_select_fusion.refs_2_
  32.0 0.1 collective-permute-start.17
  32.0 4.7 %all-to-all-done.refs_2_ = f32[32,1,256]{2,1,0:T(1,128)S(1)} async-done(((f32[32,1,256]{2,1,0:T(1,128)}), f32[32,1,256]{2,1,0:T(1,128)S(1)}, u32[]{:S(2)}, u32[]{:S(2)}) %all-to-all-start) | async-done | bytes 32800 | tf_op jit(solution)/shard_map/all_to_all | solution.py:680
  36.8 0.1 reduce
  37.0 0.6 collective-permute-start.7
  37.6 0.1 mul.17
  37.7 0.1 mul.19.refs_4_
  37.8 0.0 collective-permute-done.8.other_ref.refs_6_
  37.8 0.0 collective-permute-done.9.last_ref.refs_7_
  37.8 0.0 collective-permute-done.17.refs_3_
  37.8 6.7 %first_sweep.1 = (bf16[32,16,128]{2,1,0:T(8,128)(2,1)}, bf16[2048,1536]{1,0:T(8,128)(2,1)}) custom-call(s32[2]{0:T(128)S(1)} %pad_add_fusion.1.refs_0_, bf16[16384,256]{1,0:T(8,128)(2,1)} %refs_4_.1, bf16[768,256]{1,0:T(8,128)(2,1)S(1)} %maximum_select_fusion.refs_2_, bf16[768,256]{1,0:T(8,128)(2,1)} %collective-permute-done.17.refs_3_, ...), custom_call_target="tpu_custom_call" | custom-call | flops 1610612736 | bytes 6291456 | tf_op jit(solution)/shard_map/first_sweep/pallas_call | solution.py:434
  44.5 2.6 %all-to-all-start.1 = ((bf16[32,16,128]{2,1,0:T(8,128)(2,1)}), bf16[32,16,128]{2,1,0:T(8,128)(2,1)S(1)}, u32[]{:S(2)}, u32[]{:S(2)}) async-start(bf16[32,16,128]{2,1,0:T(8,128)(2,1)} %get-tuple-element.36), calls=%async_computation.1 | async-start | bytes 262144 | tf_op jit(solution)/shard_map/all_to_all | solution.py:680
  47.1 0.1 pad_add_fusion.refs_0_
  47.2 1.1 %collective-permute-done.7.x_ref = f32[48,2048]{1,0:T(8,128)} collective-permute-done((f32[48,2048]{1,0:T(8,128)S(1)}, f32[48,2048]{1,0:T(8,128)}, u32[]{:S(2)}, u32[]{:S(2)}) %collective-permute-start.7) | collective-permute-done | bytes 393248 | tf_op jit(solution)/shard_map/ppermute | solution.py:651
  48.3 1.6 %student_middle.1 = (f32[48,256]{1,0:T(8,128)S(1)}, bf16[48,256]{1,0:T(8,128)(2,1)S(1)}, f32[48,128]{1,0:T(8,128)S(1)}) custom-call(s32[1]{0:T(128)} %bitcast.refs_0_.index_ref, f32[96,2048]{1,0:T(8,128)S(1)} %get-tuple-element.25.keep_ref, f32[96,2048]{1,0:T(8,128)S(1)} %collective-permute-done.6.core_ref, f32[48,2048]{1,0:T(8,128)} %collective-permute-done.7.x_ref, ...), custom_call_target="tpu_custom_call" | custom-call | flops 50331648 | bytes 2621440 | tf_op jit(solution)/shard_map/student_middle/pallas_call | solution.py:599
  49.9 0.4 collective-permute-start.12
  50.3 0.6 collective-permute-start.11
  50.9 0.9 collective-permute-start.10
  51.9 3.5 %all-to-all-done.1.refs_1_ = bf16[32,16,128]{2,1,0:T(8,128)(2,1)S(1)} async-done(((bf16[32,16,128]{2,1,0:T(8,128)(2,1)}), bf16[32,16,128]{2,1,0:T(8,128)(2,1)S(1)}, u32[]{:S(2)}, u32[]{:S(2)}) %all-to-all-start.1) | async-done | bytes 131104 | tf_op jit(solution)/shard_map/all_to_all | solution.py:680
  55.3 4.4 %next_sweep.1 = bf16[32,16,128]{2,1,0:T(8,128)(2,1)} custom-call(bf16[2048,1536]{1,0:T(8,128)(2,1)} %get-tuple-element.35.refs_0_, bf16[32,16,128]{2,1,0:T(8,128)(2,1)S(1)} %all-to-all-done.1.refs_1_, bf16[48,256]{1,0:T(8,128)(2,1)S(1)} %get-tuple-element.29.refs_2_), custom_call_target="tpu_custom_call" | custom-call | flops 25165824 | bytes 6291456 | tf_op jit(solution)/shard_map/next_sweep/pallas_call | solution.py:519
  59.7 2.6 %all-to-all-start.2 = ((bf16[32,16,128]{2,1,0:T(8,128)(2,1)}), bf16[32,16,128]{2,1,0:T(8,128)(2,1)S(1)}, u32[]{:S(2)}, u32[]{:S(2)}) async-start(bf16[32,16,128]{2,1,0:T(8,128)(2,1)} %next_sweep.1), calls=%async_computation.2 | async-start | bytes 262144 | tf_op jit(solution)/shard_map/all_to_all | solution.py:680
  62.3 0.0 collective-permute-done.10
  62.4 0.0 collective-permute-done.12
  62.4 5.1 %attract.2.state_ref.refs_2_ = f32[192,512]{1,0:T(8,128)S(1)} custom-call(bf16[192,256]{1,0:T(8,128)(2,1)S(1)} %constant_dynamic-update-slice_fusion.emb_ref, f32[192,512]{1,0:T(8,128)S(1)} %concatenate.32.state_ref, bf16[16384,256]{1,0:T(8,128)(2,1)} %refs_4_.1), custom_call_target="tpu_custom_call" | custom-call | flops 1610612736 | bytes 4194304 | tf_op jit(solution)/shard_map/attract/pallas_call | solution.py:324
  67.5 3.1 %all-to-all-done.2.refs_1_ = bf16[32,16,128]{2,1,0:T(8,128)(2,1)S(1)} async-done(((bf16[32,16,128]{2,1,0:T(8,128)(2,1)}), bf16[32,16,128]{2,1,0:T(8,128)(2,1)S(1)}, u32[]{:S(2)}, u32[]{:S(2)}) %all-to-all-start.2) | async-done | bytes 131104 | tf_op jit(solution)/shard_map/all_to_all | solution.py:680
  70.5 3.7 %last_scales.1 = f32[8,1,2048]{2,1,0:T(1,128)} custom-call(bf16[2048,1536]{1,0:T(8,128)(2,1)} %get-tuple-element.35.refs_0_, bf16[32,16,128]{2,1,0:T(8,128)(2,1)S(1)} %all-to-all-done.2.refs_1_, f32[192,512]{1,0:T(8,128)S(1)} %attract.2.state_ref.refs_2_), custom_call_target="tpu_custom_call" | custom-call | flops 12582912 | bytes 6291456 | tf_op jit(solution)/shard_map/last_scales/pallas_call | solution.py:558
  74.3 3.4 %all-to-all-start.3 = ((f32[8,1,2048]{2,1,0:T(1,128)}), f32[8,1,2048]{2,1,0:T(1,128)S(1)}, u32[]{:S(2)}, u32[]{:S(2)}) async-start(f32[8,1,2048]{2,1,0:T(1,128)} %last_scales.1), calls=%async_computation.3 | async-start | bytes 131072 | tf_op jit(solution)/shard_map/all_to_all | solution.py:680
  77.7 5.1 %attract.3 = (f32[48,512]{1,0:T(8,128)S(1)}, f32[48,512]{1,0:T(8,128)S(1)}, f32[48,512]{1,0:T(8,128)S(1)}, f32[48,512]{1,0:T(8,128)S(1)}) custom-call(bf16[192,256]{1,0:T(8,128)(2,1)S(1)} %constant_dynamic-update-slice_fusion.emb_ref, f32[192,512]{1,0:T(8,128)S(1)} %attract.2.state_ref.refs_2_, bf16[16384,256]{1,0:T(8,128)(2,1)} %refs_4_.1), custom_call_target="tpu_custom_call" | custom-call | flops 1610612736 | bytes 4194304 | tf_op jit(solution)/shard_map/attract/pallas_call | solution.py:324
  82.8 0.3 collective-permute-start.13
  83.1 0.8 collective-permute-start.14
  83.8 0.9 collective-permute-start.15
  84.7 0.0 all-to-all-done.3.refs_3_
  84.7 9.5 %repel.1 = (f32[48,384]{1,0:T(8,128)S(1)}, bf16[48,384]{1,0:T(8,128)(2,1)S(1)}, bf16[48,384]{1,0:T(8,128)(2,1)S(1)}, bf16[48,384]{1,0:T(8,128)(2,1)S(1)}) custom-call(s32[2]{0:T(128)S(1)} %pad_add_fusion.refs_0_, bf16[192,256]{1,0:T(8,128)(2,1)S(1)} %get-tuple-element.23.refs_1_, f32[32,1,256]{2,1,0:T(1,128)S(1)} %all-to-all-done.refs_2_, ...), custom_call_target="tpu_custom_call" | custom-call | flops 3221225472 | bytes 8388608 | tf_op jit(solution)/shard_map/repel/pallas_call | solution.py:243
  94.2 0.5 collective-permute-start.18
  94.7 0.8 collective-permute-start.19
  95.5 0.0 collective-permute-done.13.rest_1_
  95.5 0.7 collective-permute-start.20
  96.2 0.0 collective-permute-done.15.rest_3_
  96.2 0.0 collective-permute-done.18.rest_5_
  96.2 2.7 %collective-permute-done.19.rest_6_ = bf16[48,384]{1,0:T(8,128)(2,1)S(1)} collective-permute-done((bf16[48,384]{1,0:T(8,128)(2,1)S(1)}, bf16[48,384]{1,0:T(8,128)(2,1)S(1)}, u32[]{:S(2)}, u32[]{:S(2)}) %collective-permute-start.19) | collective-permute-done | bytes 36896 | tf_op jit(solution)/shard_map/ppermute | solution.py:651
  98.9 0.4 collective-permute-done.20.rest_7_
  99.3 0.8 finish.1
  (18 shorter events, 0.2 us)
Async XLA Ops:
  1.0 6.7 %collective-permute-start.3 = (bf16[96,256]{1,0:T(8,128)(2,1)S(1)}, bf16[96,256]{1,0:T(8,128)(2,1)S(1)}, u32[]{:S(2)}, u32[]{:S(2)}) collective-permute-start(bf16[96,256]{1,0:T(8,128)(2,1)S(1)} %get-tuple-element.24), channel_id=1, source_target_pairs={{0,16},{4,20},{8,24},{12,28},{16,0},{20,4},{24,8},{28,12},{1,17},{... | collective-permute-start | bytes 147464 | tf_op jit(solution)/shard_map/ppermute | solution.py:651
  5.1 7.0 %collective-permute-start = (bf16[48,1536]{1,0:T(8,128)(2,1)}, bf16[48,1536]{1,0:T(8,128)(2,1)S(1)}, u32[]{:S(2)}, u32[]{:S(2)}) collective-permute-start(bf16[48,1536]{1,0:T(8,128)(2,1)} %refs_3_.1), channel_id=1, source_target_pairs={{0,2},{1,3},{2,0},{3,1},{4,6},{5,7},{6,4},{7,5},{8,10},{9,11},{10,... | collective-permute-start | bytes 442376 | tf_op jit(solution)/shard_map/ppermute | solution.py:651
  6.6 9.6 %collective-permute-start.5 = (bf16[512,256]{1,0:T(8,128)(2,1)}, bf16[512,256]{1,0:T(8,128)(2,1)S(1)}, u32[]{:S(2)}, u32[]{:S(2)}) collective-permute-start(bf16[512,256]{1,0:T(8,128)(2,1)} %own_ref.1), channel_id=1, source_target_pairs={{0,2},{1,3},{2,0},{3,1},{4,6},{5,7},{6,4},{7,5},{8,10},{9,11},{10,... | collective-permute-start | bytes 786440 | tf_op jit(solution)/shard_map/ppermute | solution.py:651
  7.8 4.7 %collective-permute-start.4 = (bf16[192,256]{1,0:T(8,128)(2,1)S(1)}, bf16[192,256]{1,0:T(8,128)(2,1)S(1)}, u32[]{:S(2)}, u32[]{:S(2)}) collective-permute-start(bf16[192,256]{1,0:T(8,128)(2,1)S(1)} %maximum_select_fusion.2), channel_id=1, source_target_pairs={{0,8},{4,12},{8,0},{12,4},{16,24},{20,28},{24,16},{28,20},{1,9},{5... | collective-permute-start | bytes 294920 | tf_op jit(solution)/shard_map/ppermute | solution.py:651
  9.2 3.3 %collective-permute-start.1 = (bf16[48,1536]{1,0:T(8,128)(2,1)}, bf16[48,1536]{1,0:T(8,128)(2,1)S(1)}, u32[]{:S(2)}, u32[]{:S(2)}) collective-permute-start(bf16[48,1536]{1,0:T(8,128)(2,1)} %refs_3_.1), channel_id=1, source_target_pairs={{0,1},{1,0},{2,3},{3,2},{4,5},{5,4},{6,7},{7,6},{8,9},{9,8},{10,11... | collective-permute-start | bytes 442376 | tf_op jit(solution)/shard_map/ppermute | solution.py:651
  12.1 4.2 %collective-permute-start.2 = (bf16[48,1536]{1,0:T(8,128)(2,1)S(1)}, bf16[48,1536]{1,0:T(8,128)(2,1)S(1)}, u32[]{:S(2)}, u32[]{:S(2)}) collective-permute-start(bf16[48,1536]{1,0:T(8,128)(2,1)S(1)} %collective-permute-done.refs_4_), channel_id=1, source_target_pairs={{0,1},{1,0},{2,3},{3,2},{4,5},{5,4},{6,7},{7,6},{8,9},{9,8},{10,11... | collective-permute-start | bytes 442376 | tf_op jit(solution)/shard_map/ppermute | solution.py:651
  24.4 12.5 %collective-permute-start.6 = (f32[96,2048]{1,0:T(8,128)}, f32[96,2048]{1,0:T(8,128)S(1)}, u32[]{:S(2)}, u32[]{:S(2)}) collective-permute-start(f32[96,2048]{1,0:T(8,128)} %get-tuple-element.26), channel_id=1, source_target_pairs={{0,1},{1,0},{2,3},{3,2},{4,5},{5,4},{6,7},{7,6},{8,9},{9,8},{10,11... | collective-permute-start | bytes 2359304 | tf_op jit(solution)/shard_map/ppermute | solution.py:651
  24.5 7.3 %collective-permute-start.16 = (bf16[384,256]{1,0:T(8,128)(2,1)S(1)}, bf16[384,256]{1,0:T(8,128)(2,1)S(1)}, u32[]{:S(2)}, u32[]{:S(2)}) collective-permute-start(bf16[384,256]{1,0:T(8,128)(2,1)S(1)} %maximum_select_fusion.1.refs_10_), channel_id=1, source_target_pairs={{0,4},{4,0},{8,12},{12,8},{16,20},{20,16},{24,28},{28,24},{1,5},{5... | collective-permute-start | bytes 589832 | tf_op jit(solution)/shard_map/ppermute | solution.py:651
  26.1 11.7 %collective-permute-start.8 = (bf16[512,256]{1,0:T(8,128)(2,1)}, bf16[512,256]{1,0:T(8,128)(2,1)S(1)}, u32[]{:S(2)}, u32[]{:S(2)}) collective-permute-start(bf16[512,256]{1,0:T(8,128)(2,1)} %own_ref.1), channel_id=1, source_target_pairs={{0,1},{1,0},{2,3},{3,2},{4,5},{5,4},{6,7},{7,6},{8,9},{9,8},{10,11... | collective-permute-start | bytes 786440 | tf_op jit(solution)/shard_map/ppermute | solution.py:651
  26.3 11.4 %collective-permute-start.9 = (bf16[512,256]{1,0:T(8,128)(2,1)S(1)}, bf16[512,256]{1,0:T(8,128)(2,1)S(1)}, u32[]{:S(2)}, u32[]{:S(2)}) collective-permute-start(bf16[512,256]{1,0:T(8,128)(2,1)S(1)} %collective-permute-done.5.refs_11_.partner_ref), channel_id=1, source_target_pairs={{0,1},{1,0},{2,3},{3,2},{4,5},{5,4},{6,7},{7,6},{8,9},{9,8},{10,11... | collective-permute-start | bytes 786440 | tf_op jit(solution)/shard_map/ppermute | solution.py:651
  26.7 10.1 %all-to-all-start = ((f32[32,1,256]{2,1,0:T(1,128)}), f32[32,1,256]{2,1,0:T(1,128)S(1)}, u32[]{:S(2)}, u32[]{:S(2)}) async-start(f32[32,1,256]{2,1,0:T(1,128)} %get-tuple-element.34), calls=%async_computation | async-start | bytes 65536 | tf_op jit(solution)/shard_map/all_to_all | solution.py:680
  32.0 5.8 %collective-permute-start.17 = (bf16[768,256]{1,0:T(8,128)(2,1)S(1)}, bf16[768,256]{1,0:T(8,128)(2,1)}, u32[]{:S(2)}, u32[]{:S(2)}) collective-permute-start(bf16[768,256]{1,0:T(8,128)(2,1)S(1)} %maximum_select_fusion.refs_2_), channel_id=1, source_target_pairs={{0,1},{1,0},{2,3},{3,2},{4,5},{5,4},{6,7},{7,6},{8,9},{9,8},{10,11... | collective-permute-start | bytes 1179656 | tf_op jit(solution)/shard_map/ppermute | solution.py:651
  37.0 11.3 %collective-permute-start.7 = (f32[48,2048]{1,0:T(8,128)S(1)}, f32[48,2048]{1,0:T(8,128)}, u32[]{:S(2)}, u32[]{:S(2)}) collective-permute-start(f32[48,2048]{1,0:T(8,128)S(1)} %slice_add_fusion.refs_5_), channel_id=1, source_target_pairs={{0,2},{1,3},{2,0},{3,1},{4,6},{5,7},{6,4},{7,5},{8,10},{9,11},{10,... | collective-permute-start | bytes 1179656 | tf_op jit(solution)/shard_map/ppermute | solution.py:651
  44.5 10.8 %all-to-all-start.1 = ((bf16[32,16,128]{2,1,0:T(8,128)(2,1)}), bf16[32,16,128]{2,1,0:T(8,128)(2,1)S(1)}, u32[]{:S(2)}, u32[]{:S(2)}) async-start(bf16[32,16,128]{2,1,0:T(8,128)(2,1)} %get-tuple-element.36), calls=%async_computation.1 | async-start | bytes 262144 | tf_op jit(solution)/shard_map/all_to_all | solution.py:680
  49.9 12.4 %collective-permute-start.12 = (bf16[48,256]{1,0:T(8,128)(2,1)S(1)}, bf16[48,256]{1,0:T(8,128)(2,1)S(1)}, u32[]{:S(2)}, u32[]{:S(2)}) collective-permute-start(bf16[48,256]{1,0:T(8,128)(2,1)S(1)} %get-tuple-element.29.refs_2_), channel_id=1, source_target_pairs={{0,3},{1,2},{2,1},{3,0},{4,7},{5,6},{6,5},{7,4},{8,11},{9,10},{10,... | collective-permute-start | bytes 73736 | tf_op jit(solution)/shard_map/ppermute | solution.py:651
  50.3 12.0 %collective-permute-start.11 = (bf16[48,256]{1,0:T(8,128)(2,1)S(1)}, bf16[48,256]{1,0:T(8,128)(2,1)S(1)}, u32[]{:S(2)}, u32[]{:S(2)}) collective-permute-start(bf16[48,256]{1,0:T(8,128)(2,1)S(1)} %get-tuple-element.29.refs_2_), channel_id=1, source_target_pairs={{0,2},{1,3},{2,0},{3,1},{4,6},{5,7},{6,4},{7,5},{8,10},{9,11},{10,... | collective-permute-start | bytes 73736 | tf_op jit(solution)/shard_map/ppermute | solution.py:651
  50.9 11.4 %collective-permute-start.10 = (bf16[48,256]{1,0:T(8,128)(2,1)S(1)}, bf16[48,256]{1,0:T(8,128)(2,1)S(1)}, u32[]{:S(2)}, u32[]{:S(2)}) collective-permute-start(bf16[48,256]{1,0:T(8,128)(2,1)S(1)} %get-tuple-element.29.refs_2_), channel_id=1, source_target_pairs={{0,1},{1,0},{2,3},{3,2},{4,5},{5,4},{6,7},{7,6},{8,9},{9,8},{10,11... | collective-permute-start | bytes 73736 | tf_op jit(solution)/shard_map/ppermute | solution.py:651
  59.7 10.8 %all-to-all-start.2 = ((bf16[32,16,128]{2,1,0:T(8,128)(2,1)}), bf16[32,16,128]{2,1,0:T(8,128)(2,1)S(1)}, u32[]{:S(2)}, u32[]{:S(2)}) async-start(bf16[32,16,128]{2,1,0:T(8,128)(2,1)} %next_sweep.1), calls=%async_computation.2 | async-start | bytes 262144 | tf_op jit(solution)/shard_map/all_to_all | solution.py:680
  74.3 10.4 %all-to-all-start.3 = ((f32[8,1,2048]{2,1,0:T(1,128)}), f32[8,1,2048]{2,1,0:T(1,128)S(1)}, u32[]{:S(2)}, u32[]{:S(2)}) async-start(f32[8,1,2048]{2,1,0:T(1,128)} %last_scales.1), calls=%async_computation.3 | async-start | bytes 131072 | tf_op jit(solution)/shard_map/all_to_all | solution.py:680
  82.8 12.7 %collective-permute-start.13 = (f32[48,512]{1,0:T(8,128)S(1)}, f32[48,512]{1,0:T(8,128)S(1)}, u32[]{:S(2)}, u32[]{:S(2)}) collective-permute-start(f32[48,512]{1,0:T(8,128)S(1)} %get-tuple-element.31), channel_id=1, source_target_pairs={{0,1},{1,0},{2,3},{3,2},{4,5},{5,4},{6,7},{7,6},{8,9},{9,8},{10,11... | collective-permute-start | bytes 294920 | tf_op jit(solution)/shard_map/ppermute | solution.py:651
  83.1 13.1 %collective-permute-start.14 = (f32[48,512]{1,0:T(8,128)S(1)}, f32[48,512]{1,0:T(8,128)S(1)}, u32[]{:S(2)}, u32[]{:S(2)}) collective-permute-start(f32[48,512]{1,0:T(8,128)S(1)} %get-tuple-element.32), channel_id=1, source_target_pairs={{0,2},{1,3},{2,0},{3,1},{4,6},{5,7},{6,4},{7,5},{8,10},{9,11},{10,... | collective-permute-start | bytes 294920 | tf_op jit(solution)/shard_map/ppermute | solution.py:651
  83.8 12.4 %collective-permute-start.15 = (f32[48,512]{1,0:T(8,128)S(1)}, f32[48,512]{1,0:T(8,128)S(1)}, u32[]{:S(2)}, u32[]{:S(2)}) collective-permute-start(f32[48,512]{1,0:T(8,128)S(1)} %get-tuple-element.33), channel_id=1, source_target_pairs={{0,3},{1,2},{2,1},{3,0},{4,7},{5,6},{6,5},{7,4},{8,11},{9,10},{10,... | collective-permute-start | bytes 294920 | tf_op jit(solution)/shard_map/ppermute | solution.py:651
  94.2 2.0 %collective-permute-start.18 = (bf16[48,384]{1,0:T(8,128)(2,1)S(1)}, bf16[48,384]{1,0:T(8,128)(2,1)S(1)}, u32[]{:S(2)}, u32[]{:S(2)}) collective-permute-start(bf16[48,384]{1,0:T(8,128)(2,1)S(1)} %get-tuple-element.38), channel_id=1, source_target_pairs={{0,1},{1,0},{2,3},{3,2},{4,5},{5,4},{6,7},{7,6},{8,9},{9,8},{10,11... | collective-permute-start | bytes 110600 | tf_op jit(solution)/shard_map/ppermute | solution.py:651
  94.7 4.2 %collective-permute-start.19 = (bf16[48,384]{1,0:T(8,128)(2,1)S(1)}, bf16[48,384]{1,0:T(8,128)(2,1)S(1)}, u32[]{:S(2)}, u32[]{:S(2)}) collective-permute-start(bf16[48,384]{1,0:T(8,128)(2,1)S(1)} %get-tuple-element.39), channel_id=1, source_target_pairs={{0,2},{1,3},{2,0},{3,1},{4,6},{5,7},{6,4},{7,5},{8,10},{9,11},{10,... | collective-permute-start | bytes 110600 | tf_op jit(solution)/shard_map/ppermute | solution.py:651
  95.5 3.8 %collective-permute-start.20 = (bf16[48,384]{1,0:T(8,128)(2,1)S(1)}, bf16[48,384]{1,0:T(8,128)(2,1)S(1)}, u32[]{:S(2)}, u32[]{:S(2)}) collective-permute-start(bf16[48,384]{1,0:T(8,128)(2,1)S(1)} %get-tuple-element.40), channel_id=1, source_target_pairs={{0,3},{1,2},{2,1},{3,0},{4,7},{5,6},{6,5},{7,4},{8,11},{9,10},{10,... | collective-permute-start | bytes 110600 | tf_op jit(solution)/shard_map/ppermute | solution.py:651

commit v13 on v9

--- a/solution.py
+++ b/solution.py
@@ -107,12 +107,12 @@
     )(core, in_hbm(teacher_emb))
 
 
-def wide_tops_kernel(first_row, unit_ref, protos_hbm, before_ref, out_ref, protos_ref, sems, top_ref):
+def wide_tops_kernel(unit_ref, protos_hbm, tops_ref, protos_ref, sems, top_ref):
     rows = unit_ref.shape[0]
     steps, block = protos_ref.shape[:2]
     wide = min(WIDE, block)
-    arrived = fetch(protos_hbm, protos_ref, sems, first_row)
-    top_ref[...] = before_ref[...]
+    arrived = fetch(protos_hbm, protos_ref, sems)
+    top_ref[...] = jnp.full(top_ref.shape, -jnp.inf, jnp.float32)
 
     def step(index, carry):
         arrived(index)
@@ -124,16 +124,18 @@
         return carry
 
     lax.fori_loop(0, steps, step, 0)
-    out_ref[...] = top_ref[...]
-
-
-def wide_tops(unit, protos, before, order, first_row, count, steps):
+    tops = jnp.max(jnp.transpose(top_ref[...]), axis=0, keepdims=True)
+    tops_ref[...] = jnp.broadcast_to(tops[None], tops_ref.shape)
+
+
+def wide_tops(unit, protos, order, copies, steps):
     rows, width = unit.shape
-    return pl.pallas_call(
-        skipping(functools.partial(wide_tops_kernel, first_row), 3, len(order)),
-        in_specs=[whole(), whole(pl.ANY), whole()] + [whole(pl.ANY)] * len(order),
+    count = protos.shape[0]
+    return pl.pallas_call(
+        skipping(wide_tops_kernel, 2, len(order)),
+        in_specs=[whole(), whole(pl.ANY)] + [whole(pl.ANY)] * len(order),
         out_specs=whole(),
-        out_shape=jax.ShapeDtypeStruct(before.shape, jnp.float32),
+        out_shape=jax.ShapeDtypeStruct((copies, 1, 256), jnp.float32),
         scratch_shapes=[
             pltpu.VMEM((steps, count // steps, width), jnp.bfloat16),
             pltpu.SemaphoreType.DMA((steps,)),
@@ -142,24 +144,7 @@
         compiler_params=params(16),
         cost_estimate=cost(2 * rows * width * count, 2 * width * count),
         name="wide_tops",
-    )(unit, in_hbm(protos), before, *order)
-
-
-def spread_tops_kernel(top_ref, out_ref):
-    tops = jnp.max(jnp.transpose(top_ref[...]), axis=0, keepdims=True)
-    out_ref[...] = jnp.broadcast_to(tops[None], out_ref.shape)
-
-
-def spread_tops(top, order, copies):
-    return pl.pallas_call(
-        skipping(spread_tops_kernel, 1, len(order)),
-        in_specs=[whole()] + [whole(pl.ANY)] * len(order),
-        out_specs=whole(),
-        out_shape=jax.ShapeDtypeStruct((copies, 1, 256), jnp.float32),
-        compiler_params=params(4),
-        cost_estimate=cost(top.size, 8 * top.size),
-        name="spread_tops",
-    )(top, *order)
+    )(unit, in_hbm(protos), *order)
 
 
 def repel_kernel(group, index_ref, unit_ref, tops_ref, scale_ref, protos_hbm, *rest):
@@ -199,12 +184,21 @@
 
     lax.fori_loop(0, steps, step, 0)
     total = jnp.sum(sum_ref[...], axis=1, keepdims=True)
+    lanes = lax.broadcasted_iota(jnp.int32, sum_ref.shape, 1)
     sum_ref[...] = jnp.broadcast_to(total, sum_ref.shape)
     share = out_refs[0].shape[0]
+    lanes = lanes[:share, :]
     for flip, out_ref in enumerate(out_refs):
         span = part(index_ref[1] ^ flip, share)
-        out_ref[:, :width] = acc_ref[span, :]
-        out_ref[:, width:] = sum_ref[span, :]
+        total = sum_ref[span, :]
+        out_ref[:, :width] = acc_ref[span, :].astype(out_ref.dtype)
+        if flip == 0:
+            out_ref[:, width:] = jnp.where(lanes == 0, total, 0.0)
+        else:
+            high = total.astype(jnp.bfloat16).astype(jnp.float32)
+            middle = (total - high).astype(jnp.bfloat16).astype(jnp.float32)
+            pieces = jnp.where(lanes == 0, high, jnp.where(lanes == 1, middle, total - high - middle))
+            out_ref[:, width:] = jnp.where(lanes < 3, pieces, 0.0).astype(jnp.bfloat16)
 
 
 def repel(index, unit, tops, scale, protos, order, proto_size):
@@ -215,7 +209,10 @@
         skipping(functools.partial(repel_kernel, proto_size), 5, len(order)),
         in_specs=[whole(pltpu.SMEM), whole(), whole(), whole(), whole(pl.ANY)] + [whole(pl.ANY)] * len(order),
         out_specs=[whole()] * proto_size,
-        out_shape=[jax.ShapeDtypeStruct((rows // proto_size, width + 128), jnp.float32)] * proto_size,
+        out_shape=[
+            jax.ShapeDtypeStruct((rows // proto_size, width + 128), jnp.bfloat16 if flip else jnp.float32)
+            for flip in range(proto_size)
+        ],
         scratch_shapes=[
             pltpu.VMEM((steps, block, width), jnp.bfloat16),
             pltpu.SemaphoreType.DMA((steps,)),
@@ -641,11 +638,11 @@
         row_sum = row_sum + ref[:, width : width + 128] * fade
         attract_sum = attract_sum + ref[:, :width] * jnp.tile(fade, (1, width // 128))
     for ref in repels:
-        column_sum = column_sum + ref[:, width:]
-        repel_sum = repel_sum + ref[:, :width]
+        column_sum = column_sum + jnp.sum(ref[:, width:].astype(jnp.float32), axis=1, keepdims=True)
+        repel_sum = repel_sum + ref[:, :width].astype(jnp.float32)
     emb_grad = (
         attract_sum / jnp.tile(row_sum, (1, width // 128))
-        - repel_sum / jnp.tile(column_sum, (1, width // 128))
+        - repel_sum / column_sum
     ) / student_temp
     unit = unit_ref[...]
     along = jnp.sum(unit * emb_grad, axis=1, keepdims=True)
@@ -718,16 +715,14 @@
     stages = gather_batch(half)
     mine = stages[-1]
     other = swap(mine, "proto", 1)
-    top = jnp.full((256, 128), -jnp.inf, jnp.float32)
-    top = wide_tops(own_unit, protos, top, (), 0, count // 2, 4)
 
     crops_x = swap(crops, "proto", 2)
     rows = [crops, crops_x, swap(crops, "proto", 1), swap(crops_x, "proto", 1)]
     third_x = swap(w_third, "proto", 2)
     thirds = [w_third, third_x, swap(w_third, "proto", 1), swap(third_x, "proto", 1)]
-    keep, give = student_front(proto_ref, b_first, rows, w_first, w_second, (top, stages[1]))
-    top = wide_tops(own_unit, protos, top, (stages[2], give), count // 2, count // 2, 4)
-    all_tops = all_to_all(spread_tops(top, (mine,), devices), BOTH)
+    top_copies = wide_tops(own_unit, protos, (stages[1],), devices, 8)
+    keep, give = student_front(proto_ref, b_first, rows, w_first, w_second, (stages[2], third_x))
+    all_tops = all_to_all(top_copies, BOTH)
     tops = jnp.max(all_tops.reshape(batch_size, proto_size, 256)[:, :, :group_rows], axis=1)
     tops = bit_reversed(tops, batch_size).reshape(batch_size, 2, group_rows // 2)
     base = jnp.transpose(tops, (1, 0, 2)).reshape(1, crops_total) * -teacher_rate
@@ -738,14 +733,13 @@
     unit, rounded, lengths = student_middle(
         proto_ref, keep, core_rows, x_rows, b_second, thirds, b_third
     )
-    emb_pair = jnp.concatenate([rounded, swap(rounded, "proto", 2)])
-    student_emb = jnp.concatenate([emb_pair, swap(emb_pair, "proto", 1)])
+    student_emb = jnp.concatenate([rounded] + [swap(rounded, "proto", flip) for flip in range(1, proto_size)])
     empty = jnp.concatenate(
         [jnp.zeros((group_rows, width + 128), jnp.float32), jnp.full((group_rows, 128), -1e30, jnp.float32)], axis=1
     )
     (state,) = attract(student_emb, empty, protos, 0, count // 2, 4, 1)
     slots = attract(student_emb, state, protos, count // 2, count // 2, 4, proto_size)
-    attract_parts = send_blocks([slots[0], slots[2], slots[1], slots[3]])
+    attract_parts = send_blocks(slots)
 
     copies, weights = first_sweep(thin_ref, protos, mine, other, base, (x_sent, *thirds[2:]), devices, thin, protos_total)
     for _ in range(ITERS - 2):

time: 107 us -> 107 us (level)
  Pallas kernels: 50 us -> 48.9 us
    pallas_call x3 -> x1, Pallas kernels: 7.33 us -> 6.07 us  [wide_tops(): pl.pallas_call(skipping(wide_tops_kernel, 2, len(order)), in_specs=[whole...]
    ppermute x20 -> x21, waiting for transfers between devices: 10 us -> 10.7 us  [swap(): lax.ppermute(values, axis, [(i, i ^ flip) for i in range(lax.axis_size(ax...]
    ppermute x20 -> x21, starting transfers between devices: 17.1 us -> 17.7 us  [swap(): lax.ppermute(values, axis, [(i, i ^ flip) for i in range(lax.axis_size(ax...]
  transfers between devices with their start and end apart: 24 -> 25, of which waited for: 9 -> 9; matrix products, arithmetic and copies ran while one was open for 1% -> 1% of each run, Pallas kernels for 38% -> 36%
where the time goes in v13:
time: 107 us; the launch traced here: 106 us
  Pallas kernels  48.9 us (46%)
  starting transfers between devices  32.7 us (31%)
  waiting for transfers between devices  23.6 us (22%)
    ppermute x21, starting transfers between devices, swap(): lax.ppermute(values, axis, [(i, i ^ flip) for i in range(lax.axis_size(ax...  17.7 us
    all_to_all x4, starting transfers between devices, all_to_all(): return lax.all_to_all(copies, axes, 0, 0, tiled=True)  15 us
    all_to_all x4, waiting for transfers between devices, all_to_all(): return lax.all_to_all(copies, axes, 0, 0, tiled=True)  12.9 us
    ppermute x21, waiting for transfers between devices, swap(): lax.ppermute(values, axis, [(i, i ^ flip) for i in range(lax.axis_size(ax...  10.7 us
    pallas_call x2, Pallas kernels, attract(): pl.pallas_call(functools.partial(attract_kernel, first_row, outputs > 1),...  10.2 us
    pallas_call x1, Pallas kernels, repel(): pl.pallas_call(skipping(functools.partial(repel_kernel, proto_size), 5, l...  9.48 us
    pallas_call x1, Pallas kernels, first_sweep(): pl.pallas_call(skipping(functools.partial(first_sweep_kernel, chunk, prot...  6.72 us
    pallas_call x1, Pallas kernels, wide_tops(): pl.pallas_call(skipping(wide_tops_kernel, 2, len(order)), in_specs=[whole...  6.07 us
  transfers between devices with their start and end apart: 25, of which 9 were waited for; matrix products, arithmetic and copies ran while one was open for 1% of the time, Pallas kernels for 36%

profile of v13, /device:TPU:0, one launch (start us, length us, event | category | flops | bytes accessed | tf_op | source)
XLA Modules:
  0.0 106.3 jit_solution(8831131322827722067)
XLA Ops:
  0.0 1.0 teacher_units.1
  1.0 4.1 %collective-permute-start.3 = (bf16[96,256]{1,0:T(8,128)(2,1)S(1)}, bf16[96,256]{1,0:T(8,128)(2,1)S(1)}, u32[]{:S(2)}, u32[]{:S(2)}) collective-permute-start(bf16[96,256]{1,0:T(8,128)(2,1)S(1)} %get-tuple-element.22), channel_id=1, source_target_pairs={{0,16},{4,20},{8,24},{12,28},{16,0},{20,4},{24,8},{28,12},{1,17},{... | collective-permute-start | bytes 147464 | tf_op jit(solution)/shard_map/ppermute | solution.py:665
  5.1 1.5 %collective-permute-start = (bf16[48,1536]{1,0:T(8,128)(2,1)}, bf16[48,1536]{1,0:T(8,128)(2,1)S(1)}, u32[]{:S(2)}, u32[]{:S(2)}) collective-permute-start(bf16[48,1536]{1,0:T(8,128)(2,1)} %refs_2_.1), channel_id=1, source_target_pairs={{0,2},{1,3},{2,0},{3,1},{4,6},{5,7},{6,4},{7,5},{8,10},{9,11},{10,... | collective-permute-start | bytes 442376 | tf_op jit(solution)/shard_map/ppermute | solution.py:665
  6.6 0.5 collective-permute-start.5
  7.2 0.6 collective-permute-done.3
  7.8 1.4 %collective-permute-start.4 = (bf16[192,256]{1,0:T(8,128)(2,1)S(1)}, bf16[192,256]{1,0:T(8,128)(2,1)S(1)}, u32[]{:S(2)}, u32[]{:S(2)}) collective-permute-start(bf16[192,256]{1,0:T(8,128)(2,1)S(1)} %maximum_select_fusion.2.refs_2_), channel_id=1, source_target_pairs={{0,8},{4,12},{8,0},{12,4},{16,24},{20,28},{24,16},{28,20},{1,9},{5... | collective-permute-start | bytes 294920 | tf_op jit(solution)/shard_map/ppermute | solution.py:665
  9.2 0.0 collective-permute-start.1
  9.2 2.9 %collective-permute-done.refs_3_ = bf16[48,1536]{1,0:T(8,128)(2,1)S(1)} collective-permute-done((bf16[48,1536]{1,0:T(8,128)(2,1)}, bf16[48,1536]{1,0:T(8,128)(2,1)S(1)}, u32[]{:S(2)}, u32[]{:S(2)}) %collective-permute-start) | collective-permute-done | bytes 147488 | tf_op jit(solution)/shard_map/ppermute | solution.py:665
  12.1 0.0 collective-permute-start.2
  12.1 0.3 collective-permute-done.4
  12.4 0.1 maximum_select_fusion.1.refs_8_
  12.5 0.0 collective-permute-done.1.refs_4_
  12.5 3.8 %collective-permute-done.5.refs_9_.partner_ref = bf16[512,256]{1,0:T(8,128)(2,1)S(1)} collective-permute-done((bf16[512,256]{1,0:T(8,128)(2,1)}, bf16[512,256]{1,0:T(8,128)(2,1)S(1)}, u32[]{:S(2)}, u32[]{:S(2)}) %collective-permute-start.5) | collective-permute-done | bytes 262176 | tf_op jit(solution)/shard_map/ppermute | solution.py:665
  16.3 0.0 collective-permute-done.2.refs_5_
  16.3 4.8 %student_front.1 = (f32[96,2048]{1,0:T(8,128)S(1)}, f32[96,2048]{1,0:T(8,128)}) custom-call(s32[1]{0:T(128)} %bitcast.refs_0_.index_ref, f32[1,2048]{1,0:T(1,128)} %bitcast.10, bf16[48,1536]{1,0:T(8,128)(2,1)} %refs_2_.1, bf16[48,1536]{1,0:T(8,128)(2,1)S(1)} %collective-permute-done.refs_3_, bf16[48,1536]{1,0:T(8,128)(2,1)S(1)} %collective-permute-done.1.refs_4_, ...), custom_call_target="tpu_custom_call" | custom-call | flops 704643072 | bytes 3670016 | tf_op jit(solution)/shard_map/student_front/pallas_call | solution.py:572
  21.1 0.1 collective-permute-start.6
  21.2 0.5 collective-permute-start.8
  21.7 6.1 %wide_tops.1 = f32[32,1,256]{2,1,0:T(1,128)} custom-call(bf16[192,256]{1,0:T(8,128)(2,1)S(1)} %get-tuple-element.32.refs_0_.refs_1_, bf16[16384,256]{1,0:T(8,128)(2,1)} %refs_4_.1, bf16[192,256]{1,0:T(8,128)(2,1)S(1)} %maximum_select_fusion.2.refs_2_), custom_call_target="tpu_custom_call" | custom-call | flops 1610612736 | bytes 8388608 | tf_op jit(solution)/shard_map/wide_tops/pallas_call | solution.py:134
  27.8 3.8 %all-to-all-start = ((f32[32,1,256]{2,1,0:T(1,128)}), f32[32,1,256]{2,1,0:T(1,128)S(1)}, u32[]{:S(2)}, u32[]{:S(2)}) async-start(f32[32,1,256]{2,1,0:T(1,128)} %wide_tops.1), calls=%async_computation | async-start | bytes 65536 | tf_op jit(solution)/shard_map/all_to_all | solution.py:694
  31.6 1.8 %collective-permute-start.16 = (bf16[384,256]{1,0:T(8,128)(2,1)S(1)}, bf16[384,256]{1,0:T(8,128)(2,1)S(1)}, u32[]{:S(2)}, u32[]{:S(2)}) collective-permute-start(bf16[384,256]{1,0:T(8,128)(2,1)S(1)} %maximum_select_fusion.1.refs_8_), channel_id=1, source_target_pairs={{0,4},{4,0},{8,12},{12,8},{16,20},{20,16},{24,28},{28,24},{1,5},{5... | collective-permute-start | bytes 589832 | tf_op jit(solution)/shard_map/ppermute | solution.py:665
  33.4 0.1 pad_add_fusion.1.refs_0_
  33.5 5.3 %all-to-all-done.refs_2_ = f32[32,1,256]{2,1,0:T(1,128)S(1)} async-done(((f32[32,1,256]{2,1,0:T(1,128)}), f32[32,1,256]{2,1,0:T(1,128)S(1)}, u32[]{:S(2)}, u32[]{:S(2)}) %all-to-all-start) | async-done | bytes 32800 | tf_op jit(solution)/shard_map/all_to_all | solution.py:694
  38.9 0.1 reduce
  39.0 0.2 collective-permute-start.9
  39.2 0.0 collective-permute-done.16
  39.2 0.2 maximum_select_fusion.refs_2_
  39.3 0.5 collective-permute-start.17
  39.8 0.0 collective-permute-done.6.core_ref
  39.9 1.2 %collective-permute-start.7 = (f32[48,2048]{1,0:T(8,128)S(1)}, f32[48,2048]{1,0:T(8,128)}, u32[]{:S(2)}, u32[]{:S(2)}) collective-permute-start(f32[48,2048]{1,0:T(8,128)S(1)} %slice_add_fusion.refs_5_), channel_id=1, source_target_pairs={{0,2},{1,3},{2,0},{3,1},{4,6},{5,7},{6,4},{7,5},{8,10},{9,11},{10,... | collective-permute-start | bytes 1179656 | tf_op jit(solution)/shard_map/ppermute | solution.py:665
  41.1 0.1 mul.17
  41.2 0.1 mul.19.refs_4_
  41.3 0.0 collective-permute-done.8.other_ref.refs_6_
  41.3 0.0 collective-permute-done.9.last_ref.refs_7_
  41.3 6.7 %first_sweep.1 = (bf16[32,16,128]{2,1,0:T(8,128)(2,1)}, bf16[2048,1536]{1,0:T(8,128)(2,1)}) custom-call(s32[2]{0:T(128)S(1)} %pad_add_fusion.1.refs_0_, bf16[16384,256]{1,0:T(8,128)(2,1)} %refs_4_.1, bf16[768,256]{1,0:T(8,128)(2,1)S(1)} %maximum_select_fusion.refs_2_, bf16[768,256]{1,0:T(8,128)(2,1)} %collective-permute-done.17.refs_3_, ...), custom_call_target="tpu_custom_call" | custom-call | flops 1610612736 | bytes 6291456 | tf_op jit(solution)/shard_map/first_sweep/pallas_call | solution.py:399
  48.0 5.2 %all-to-all-start.1 = ((bf16[32,16,128]{2,1,0:T(8,128)(2,1)}), bf16[32,16,128]{2,1,0:T(8,128)(2,1)S(1)}, u32[]{:S(2)}, u32[]{:S(2)}) async-start(bf16[32,16,128]{2,1,0:T(8,128)(2,1)} %get-tuple-element.34), calls=%async_computation.1 | async-start | bytes 262144 | tf_op jit(solution)/shard_map/all_to_all | solution.py:694
  53.3 0.1 pad_add_fusion.refs_0_
  53.4 0.0 collective-permute-done.7.x_ref
  53.4 1.6 %student_middle.1 = (f32[48,256]{1,0:T(8,128)S(1)}, bf16[48,256]{1,0:T(8,128)(2,1)S(1)}, f32[48,128]{1,0:T(8,128)S(1)}) custom-call(s32[1]{0:T(128)} %bitcast.refs_0_.index_ref, f32[96,2048]{1,0:T(8,128)S(1)} %get-tuple-element.23.keep_ref, f32[96,2048]{1,0:T(8,128)S(1)} %collective-permute-done.6.core_ref, f32[48,2048]{1,0:T(8,128)} %collective-permute-done.7.x_ref, ...), custom_call_target="tpu_custom_call" | custom-call | flops 50331648 | bytes 2621440 | tf_op jit(solution)/shard_map/student_middle/pallas_call | solution.py:613
  55.0 1.6 %collective-permute-start.12 = (bf16[48,256]{1,0:T(8,128)(2,1)S(1)}, bf16[48,256]{1,0:T(8,128)(2,1)S(1)}, u32[]{:S(2)}, u32[]{:S(2)}) collective-permute-start(bf16[48,256]{1,0:T(8,128)(2,1)S(1)} %get-tuple-element.27.refs_2_), channel_id=1, source_target_pairs={{0,3},{1,2},{2,1},{3,0},{4,7},{5,6},{6,5},{7,4},{8,11},{9,10},{10,... | collective-permute-start | bytes 73736 | tf_op jit(solution)/shard_map/ppermute | solution.py:665
  56.6 0.4 collective-permute-start.11
  57.0 0.0 collective-permute-start.10
  57.0 4.5 %all-to-all-done.1.refs_1_ = bf16[32,16,128]{2,1,0:T(8,128)(2,1)S(1)} async-done(((bf16[32,16,128]{2,1,0:T(8,128)(2,1)}), bf16[32,16,128]{2,1,0:T(8,128)(2,1)S(1)}, u32[]{:S(2)}, u32[]{:S(2)}) %all-to-all-start.1) | async-done | bytes 131104 | tf_op jit(solution)/shard_map/all_to_all | solution.py:694
  61.5 4.4 %next_sweep.1 = bf16[32,16,128]{2,1,0:T(8,128)(2,1)} custom-call(bf16[2048,1536]{1,0:T(8,128)(2,1)} %get-tuple-element.33.refs_0_, bf16[32,16,128]{2,1,0:T(8,128)(2,1)S(1)} %all-to-all-done.1.refs_1_, bf16[48,256]{1,0:T(8,128)(2,1)S(1)} %get-tuple-element.27.refs_2_), custom_call_target="tpu_custom_call" | custom-call | flops 25165824 | bytes 6291456 | tf_op jit(solution)/shard_map/next_sweep/pallas_call | solution.py:484
  65.9 2.6 %all-to-all-start.2 = ((bf16[32,16,128]{2,1,0:T(8,128)(2,1)}), bf16[32,16,128]{2,1,0:T(8,128)(2,1)S(1)}, u32[]{:S(2)}, u32[]{:S(2)}) async-start(bf16[32,16,128]{2,1,0:T(8,128)(2,1)} %next_sweep.1), calls=%async_computation.2 | async-start | bytes 262144 | tf_op jit(solution)/shard_map/all_to_all | solution.py:694
  68.5 0.0 collective-permute-done.10
  68.5 0.0 collective-permute-done.11
  68.6 5.0 %attract.2.state_ref.refs_2_ = f32[192,512]{1,0:T(8,128)S(1)} custom-call(bf16[192,256]{1,0:T(8,128)(2,1)S(1)} %constant_dynamic-update-slice_fusion.emb_ref, f32[192,512]{1,0:T(8,128)S(1)} %concatenate.32.state_ref, bf16[16384,256]{1,0:T(8,128)(2,1)} %refs_4_.1), custom_call_target="tpu_custom_call" | custom-call | flops 1610612736 | bytes 4194304 | tf_op jit(solution)/shard_map/attract/pallas_call | solution.py:289
  73.7 3.1 %all-to-all-done.2.refs_1_ = bf16[32,16,128]{2,1,0:T(8,128)(2,1)S(1)} async-done(((bf16[32,16,128]{2,1,0:T(8,128)(2,1)}), bf16[32,16,128]{2,1,0:T(8,128)(2,1)S(1)}, u32[]{:S(2)}, u32[]{:S(2)}) %all-to-all-start.2) | async-done | bytes 131104 | tf_op jit(solution)/shard_map/all_to_all | solution.py:694
  76.7 3.7 %last_scales.1 = f32[8,1,2048]{2,1,0:T(1,128)} custom-call(bf16[2048,1536]{1,0:T(8,128)(2,1)} %get-tuple-element.33.refs_0_, bf16[32,16,128]{2,1,0:T(8,128)(2,1)S(1)} %all-to-all-done.2.refs_1_, f32[192,512]{1,0:T(8,128)S(1)} %attract.2.state_ref.refs_2_), custom_call_target="tpu_custom_call" | custom-call | flops 12582912 | bytes 6291456 | tf_op jit(solution)/shard_map/last_scales/pallas_call | solution.py:523
  80.5 3.4 %all-to-all-start.3 = ((f32[8,1,2048]{2,1,0:T(1,128)}), f32[8,1,2048]{2,1,0:T(1,128)S(1)}, u32[]{:S(2)}, u32[]{:S(2)}) async-start(f32[8,1,2048]{2,1,0:T(1,128)} %last_scales.1), calls=%async_computation.3 | async-start | bytes 131072 | tf_op jit(solution)/shard_map/all_to_all | solution.py:694
  83.8 5.1 %attract.3 = (f32[48,512]{1,0:T(8,128)S(1)}, f32[48,512]{1,0:T(8,128)S(1)}, f32[48,512]{1,0:T(8,128)S(1)}, f32[48,512]{1,0:T(8,128)S(1)}) custom-call(bf16[192,256]{1,0:T(8,128)(2,1)S(1)} %constant_dynamic-update-slice_fusion.emb_ref, f32[192,512]{1,0:T(8,128)S(1)} %attract.2.state_ref.refs_2_, bf16[16384,256]{1,0:T(8,128)(2,1)} %refs_4_.1), custom_call_target="tpu_custom_call" | custom-call | flops 1610612736 | bytes 4194304 | tf_op jit(solution)/shard_map/attract/pallas_call | solution.py:289
  89.0 0.3 collective-permute-start.13
  89.2 0.8 collective-permute-start.14
  90.0 0.9 collective-permute-start.15
  90.9 9.5 %repel.1 = (f32[48,384]{1,0:T(8,128)S(1)}, bf16[48,384]{1,0:T(8,128)(2,1)S(1)}, bf16[48,384]{1,0:T(8,128)(2,1)S(1)}, bf16[48,384]{1,0:T(8,128)(2,1)S(1)}) custom-call(s32[2]{0:T(128)S(1)} %pad_add_fusion.refs_0_, bf16[192,256]{1,0:T(8,128)(2,1)S(1)} %get-tuple-element.32.refs_0_.refs_1_, f32[32,1,256]{2,1,0:T(1,128)S(1)} %all-to-all-done.refs_2_, ...), custom_call_target="tpu_custom_call" | custom-call | flops 3221225472 | bytes 8388608 | tf_op jit(solution)/shard_map/repel/pallas_call | solution.py:208
  100.4 0.5 collective-permute-start.18
  100.9 0.8 collective-permute-start.19
  101.7 0.7 collective-permute-start.20
  102.4 0.0 collective-permute-done.14.rest_2_
  102.4 0.0 collective-permute-done.15.rest_3_
  102.4 0.0 collective-permute-done.18.rest_5_
  102.4 2.7 %collective-permute-done.19.rest_6_ = bf16[48,384]{1,0:T(8,128)(2,1)S(1)} collective-permute-done((bf16[48,384]{1,0:T(8,128)(2,1)S(1)}, bf16[48,384]{1,0:T(8,128)(2,1)S(1)}, u32[]{:S(2)}, u32[]{:S(2)}) %collective-permute-start.19) | collective-permute-done | bytes 36896 | tf_op jit(solution)/shard_map/ppermute | solution.py:665
  105.1 0.4 collective-permute-done.20.rest_7_
  105.5 0.8 finish.1
  (19 shorter events, 0.2 us)
Async XLA Ops:
  1.0 6.7 %collective-permute-start.3 = (bf16[96,256]{1,0:T(8,128)(2,1)S(1)}, bf16[96,256]{1,0:T(8,128)(2,1)S(1)}, u32[]{:S(2)}, u32[]{:S(2)}) collective-permute-start(bf16[96,256]{1,0:T(8,128)(2,1)S(1)} %get-tuple-element.22), channel_id=1, source_target_pairs={{0,16},{4,20},{8,24},{12,28},{16,0},{20,4},{24,8},{28,12},{1,17},{... | collective-permute-start | bytes 147464 | tf_op jit(solution)/shard_map/ppermute | solution.py:665
  5.1 7.0 %collective-permute-start = (bf16[48,1536]{1,0:T(8,128)(2,1)}, bf16[48,1536]{1,0:T(8,128)(2,1)S(1)}, u32[]{:S(2)}, u32[]{:S(2)}) collective-permute-start(bf16[48,1536]{1,0:T(8,128)(2,1)} %refs_2_.1), channel_id=1, source_target_pairs={{0,2},{1,3},{2,0},{3,1},{4,6},{5,7},{6,4},{7,5},{8,10},{9,11},{10,... | collective-permute-start | bytes 442376 | tf_op jit(solution)/shard_map/ppermute | solution.py:665
  6.6 9.6 %collective-permute-start.5 = (bf16[512,256]{1,0:T(8,128)(2,1)}, bf16[512,256]{1,0:T(8,128)(2,1)S(1)}, u32[]{:S(2)}, u32[]{:S(2)}) collective-permute-start(bf16[512,256]{1,0:T(8,128)(2,1)} %own_ref.1), channel_id=1, source_target_pairs={{0,2},{1,3},{2,0},{3,1},{4,6},{5,7},{6,4},{7,5},{8,10},{9,11},{10,... | collective-permute-start | bytes 786440 | tf_op jit(solution)/shard_map/ppermute | solution.py:665
  7.8 4.7 %collective-permute-start.4 = (bf16[192,256]{1,0:T(8,128)(2,1)S(1)}, bf16[192,256]{1,0:T(8,128)(2,1)S(1)}, u32[]{:S(2)}, u32[]{:S(2)}) collective-permute-start(bf16[192,256]{1,0:T(8,128)(2,1)S(1)} %maximum_select_fusion.2.refs_2_), channel_id=1, source_target_pairs={{0,8},{4,12},{8,0},{12,4},{16,24},{20,28},{24,16},{28,20},{1,9},{5... | collective-permute-start | bytes 294920 | tf_op jit(solution)/shard_map/ppermute | solution.py:665
  9.2 3.3 %collective-permute-start.1 = (bf16[48,1536]{1,0:T(8,128)(2,1)}, bf16[48,1536]{1,0:T(8,128)(2,1)S(1)}, u32[]{:S(2)}, u32[]{:S(2)}) collective-permute-start(bf16[48,1536]{1,0:T(8,128)(2,1)} %refs_2_.1), channel_id=1, source_target_pairs={{0,1},{1,0},{2,3},{3,2},{4,5},{5,4},{6,7},{7,6},{8,9},{9,8},{10,11... | collective-permute-start | bytes 442376 | tf_op jit(solution)/shard_map/ppermute | solution.py:665
  12.1 4.2 %collective-permute-start.2 = (bf16[48,1536]{1,0:T(8,128)(2,1)S(1)}, bf16[48,1536]{1,0:T(8,128)(2,1)S(1)}, u32[]{:S(2)}, u32[]{:S(2)}) collective-permute-start(bf16[48,1536]{1,0:T(8,128)(2,1)S(1)} %collective-permute-done.refs_3_), channel_id=1, source_target_pairs={{0,1},{1,0},{2,3},{3,2},{4,5},{5,4},{6,7},{7,6},{8,9},{9,8},{10,11... | collective-permute-start | bytes 442376 | tf_op jit(solution)/shard_map/ppermute | solution.py:665
  21.1 18.7 %collective-permute-start.6 = (f32[96,2048]{1,0:T(8,128)}, f32[96,2048]{1,0:T(8,128)S(1)}, u32[]{:S(2)}, u32[]{:S(2)}) collective-permute-start(f32[96,2048]{1,0:T(8,128)} %get-tuple-element.24), channel_id=1, source_target_pairs={{0,1},{1,0},{2,3},{3,2},{4,5},{5,4},{6,7},{7,6},{8,9},{9,8},{10,11... | collective-permute-start | bytes 2359304 | tf_op jit(solution)/shard_map/ppermute | solution.py:665
  21.2 20.1 %collective-permute-start.8 = (bf16[512,256]{1,0:T(8,128)(2,1)}, bf16[512,256]{1,0:T(8,128)(2,1)S(1)}, u32[]{:S(2)}, u32[]{:S(2)}) collective-permute-start(bf16[512,256]{1,0:T(8,128)(2,1)} %own_ref.1), channel_id=1, source_target_pairs={{0,1},{1,0},{2,3},{3,2},{4,5},{5,4},{6,7},{7,6},{8,9},{9,8},{10,11... | collective-permute-start | bytes 786440 | tf_op jit(solution)/shard_map/ppermute | solution.py:665
  27.8 11.1 %all-to-all-start = ((f32[32,1,256]{2,1,0:T(1,128)}), f32[32,1,256]{2,1,0:T(1,128)S(1)}, u32[]{:S(2)}, u32[]{:S(2)}) async-start(f32[32,1,256]{2,1,0:T(1,128)} %wide_tops.1), calls=%async_computation | async-start | bytes 65536 | tf_op jit(solution)/shard_map/all_to_all | solution.py:694
  31.6 7.6 %collective-permute-start.16 = (bf16[384,256]{1,0:T(8,128)(2,1)S(1)}, bf16[384,256]{1,0:T(8,128)(2,1)S(1)}, u32[]{:S(2)}, u32[]{:S(2)}) collective-permute-start(bf16[384,256]{1,0:T(8,128)(2,1)S(1)} %maximum_select_fusion.1.refs_8_), channel_id=1, source_target_pairs={{0,4},{4,0},{8,12},{12,8},{16,20},{20,16},{24,28},{28,24},{1,5},{5... | collective-permute-start | bytes 589832 | tf_op jit(solution)/shard_map/ppermute | solution.py:665
  39.0 2.3 %collective-permute-start.9 = (bf16[512,256]{1,0:T(8,128)(2,1)S(1)}, bf16[512,256]{1,0:T(8,128)(2,1)S(1)}, u32[]{:S(2)}, u32[]{:S(2)}) collective-permute-start(bf16[512,256]{1,0:T(8,128)(2,1)S(1)} %collective-permute-done.5.refs_9_.partner_ref), channel_id=1, source_target_pairs={{0,1},{1,0},{2,3},{3,2},{4,5},{5,4},{6,7},{7,6},{8,9},{9,8},{10,11... | collective-permute-start | bytes 786440 | tf_op jit(solution)/shard_map/ppermute | solution.py:665
  39.3 2.0 %collective-permute-start.17 = (bf16[768,256]{1,0:T(8,128)(2,1)S(1)}, bf16[768,256]{1,0:T(8,128)(2,1)}, u32[]{:S(2)}, u32[]{:S(2)}) collective-permute-start(bf16[768,256]{1,0:T(8,128)(2,1)S(1)} %maximum_select_fusion.refs_2_), channel_id=1, source_target_pairs={{0,1},{1,0},{2,3},{3,2},{4,5},{5,4},{6,7},{7,6},{8,9},{9,8},{10,11... | collective-permute-start | bytes 1179656 | tf_op jit(solution)/shard_map/ppermute | solution.py:665
  39.9 13.5 %collective-permute-start.7 = (f32[48,2048]{1,0:T(8,128)S(1)}, f32[48,2048]{1,0:T(8,128)}, u32[]{:S(2)}, u32[]{:S(2)}) collective-permute-start(f32[48,2048]{1,0:T(8,128)S(1)} %slice_add_fusion.refs_5_), channel_id=1, source_target_pairs={{0,2},{1,3},{2,0},{3,1},{4,6},{5,7},{6,4},{7,5},{8,10},{9,11},{10,... | collective-permute-start | bytes 1179656 | tf_op jit(solution)/shard_map/ppermute | solution.py:665
  48.0 13.5 %all-to-all-start.1 = ((bf16[32,16,128]{2,1,0:T(8,128)(2,1)}), bf16[32,16,128]{2,1,0:T(8,128)(2,1)S(1)}, u32[]{:S(2)}, u32[]{:S(2)}) async-start(bf16[32,16,128]{2,1,0:T(8,128)(2,1)} %get-tuple-element.34), calls=%async_computation.1 | async-start | bytes 262144 | tf_op jit(solution)/shard_map/all_to_all | solution.py:694
  55.0 13.5 %collective-permute-start.12 = (bf16[48,256]{1,0:T(8,128)(2,1)S(1)}, bf16[48,256]{1,0:T(8,128)(2,1)S(1)}, u32[]{:S(2)}, u32[]{:S(2)}) collective-permute-start(bf16[48,256]{1,0:T(8,128)(2,1)S(1)} %get-tuple-element.27.refs_2_), channel_id=1, source_target_pairs={{0,3},{1,2},{2,1},{3,0},{4,7},{5,6},{6,5},{7,4},{8,11},{9,10},{10,... | collective-permute-start | bytes 73736 | tf_op jit(solution)/shard_map/ppermute | solution.py:665
  56.6 11.9 %collective-permute-start.11 = (bf16[48,256]{1,0:T(8,128)(2,1)S(1)}, bf16[48,256]{1,0:T(8,128)(2,1)S(1)}, u32[]{:S(2)}, u32[]{:S(2)}) collective-permute-start(bf16[48,256]{1,0:T(8,128)(2,1)S(1)} %get-tuple-element.27.refs_2_), channel_id=1, source_target_pairs={{0,2},{1,3},{2,0},{3,1},{4,6},{5,7},{6,4},{7,5},{8,10},{9,11},{10,... | collective-permute-start | bytes 73736 | tf_op jit(solution)/shard_map/ppermute | solution.py:665
  57.0 11.5 %collective-permute-start.10 = (bf16[48,256]{1,0:T(8,128)(2,1)S(1)}, bf16[48,256]{1,0:T(8,128)(2,1)S(1)}, u32[]{:S(2)}, u32[]{:S(2)}) collective-permute-start(bf16[48,256]{1,0:T(8,128)(2,1)S(1)} %get-tuple-element.27.refs_2_), channel_id=1, source_target_pairs={{0,1},{1,0},{2,3},{3,2},{4,5},{5,4},{6,7},{7,6},{8,9},{9,8},{10,11... | collective-permute-start | bytes 73736 | tf_op jit(solution)/shard_map/ppermute | solution.py:665
  65.9 10.8 %all-to-all-start.2 = ((bf16[32,16,128]{2,1,0:T(8,128)(2,1)}), bf16[32,16,128]{2,1,0:T(8,128)(2,1)S(1)}, u32[]{:S(2)}, u32[]{:S(2)}) async-start(bf16[32,16,128]{2,1,0:T(8,128)(2,1)} %next_sweep.1), calls=%async_computation.2 | async-start | bytes 262144 | tf_op jit(solution)/shard_map/all_to_all | solution.py:694
  80.5 10.4 %all-to-all-start.3 = ((f32[8,1,2048]{2,1,0:T(1,128)}), f32[8,1,2048]{2,1,0:T(1,128)S(1)}, u32[]{:S(2)}, u32[]{:S(2)}) async-start(f32[8,1,2048]{2,1,0:T(1,128)} %last_scales.1), calls=%async_computation.3 | async-start | bytes 131072 | tf_op jit(solution)/shard_map/all_to_all | solution.py:694
  89.0 12.7 %collective-permute-start.13 = (f32[48,512]{1,0:T(8,128)S(1)}, f32[48,512]{1,0:T(8,128)S(1)}, u32[]{:S(2)}, u32[]{:S(2)}) collective-permute-start(f32[48,512]{1,0:T(8,128)S(1)} %get-tuple-element.29), channel_id=1, source_target_pairs={{0,1},{1,0},{2,3},{3,2},{4,5},{5,4},{6,7},{7,6},{8,9},{9,8},{10,11... | collective-permute-start | bytes 294920 | tf_op jit(solution)/shard_map/ppermute | solution.py:665
  89.2 13.1 %collective-permute-start.14 = (f32[48,512]{1,0:T(8,128)S(1)}, f32[48,512]{1,0:T(8,128)S(1)}, u32[]{:S(2)}, u32[]{:S(2)}) collective-permute-start(f32[48,512]{1,0:T(8,128)S(1)} %get-tuple-element.30), channel_id=1, source_target_pairs={{0,2},{1,3},{2,0},{3,1},{4,6},{5,7},{6,4},{7,5},{8,10},{9,11},{10,... | collective-permute-start | bytes 294920 | tf_op jit(solution)/shard_map/ppermute | solution.py:665
  90.0 12.4 %collective-permute-start.15 = (f32[48,512]{1,0:T(8,128)S(1)}, f32[48,512]{1,0:T(8,128)S(1)}, u32[]{:S(2)}, u32[]{:S(2)}) collective-permute-start(f32[48,512]{1,0:T(8,128)S(1)} %get-tuple-element.31), channel_id=1, source_target_pairs={{0,3},{1,2},{2,1},{3,0},{4,7},{5,6},{6,5},{7,4},{8,11},{9,10},{10,... | collective-permute-start | bytes 294920 | tf_op jit(solution)/shard_map/ppermute | solution.py:665
  100.4 2.0 %collective-permute-start.18 = (bf16[48,384]{1,0:T(8,128)(2,1)S(1)}, bf16[48,384]{1,0:T(8,128)(2,1)S(1)}, u32[]{:S(2)}, u32[]{:S(2)}) collective-permute-start(bf16[48,384]{1,0:T(8,128)(2,1)S(1)} %get-tuple-element.36), channel_id=1, source_target_pairs={{0,1},{1,0},{2,3},{3,2},{4,5},{5,4},{6,7},{7,6},{8,9},{9,8},{10,11... | collective-permute-start | bytes 110600 | tf_op jit(solution)/shard_map/ppermute | solution.py:665
  100.9 4.2 %collective-permute-start.19 = (bf16[48,384]{1,0:T(8,128)(2,1)S(1)}, bf16[48,384]{1,0:T(8,128)(2,1)S(1)}, u32[]{:S(2)}, u32[]{:S(2)}) collective-permute-start(bf16[48,384]{1,0:T(8,128)(2,1)S(1)} %get-tuple-element.37), channel_id=1, source_target_pairs={{0,2},{1,3},{2,0},{3,1},{4,6},{5,7},{6,4},{7,5},{8,10},{9,11},{10,... | collective-permute-start | bytes 110600 | tf_op jit(solution)/shard_map/ppermute | solution.py:665
  101.7 3.8 %collective-permute-start.20 = (bf16[48,384]{1,0:T(8,128)(2,1)S(1)}, bf16[48,384]{1,0:T(8,128)(2,1)S(1)}, u32[]{:S(2)}, u32[]{:S(2)}) collective-permute-start(bf16[48,384]{1,0:T(8,128)(2,1)S(1)} %get-tuple-element.38), channel_id=1, source_target_pairs={{0,3},{1,2},{2,1},{3,0},{4,7},{5,6},{6,5},{7,4},{8,11},{9,10},{10,... | collective-permute-start | bytes 110600 | tf_op jit(solution)/shard_map/ppermute | solution.py:665

commit v14 on v12

--- a/solution.py
+++ b/solution.py
@@ -109,7 +109,8 @@
 
 def front_kernel(
     index_ref, unit_ref, bias_ref, own_hbm, x_hbm, core_hbm, last_hbm, first_hbm, second_hbm, protos_hbm,
-    tops_ref, keep_ref, give_ref, first_ref, second_ref, rows_ref, protos_ref, top_ref, sems, chunk_sems,
+    top_ref, keep_ref, give_ref, turned_hbm, first_ref, second_ref, rows_ref, protos_ref, turned_ref, sems,
+    chunk_sems, out_sems,
 ):
     rows = unit_ref.shape[0]
     steps, block = protos_ref.shape[:2]
@@ -126,18 +127,22 @@
         copy.start()
     top_ref[...] = jnp.full(top_ref.shape, -jnp.inf, jnp.float32)
 
+    def chunk_out(index):
+        return pltpu.make_async_copy(turned_ref.at[index], turned_hbm.at[index], out_sems.at[index])
+
     def step(index, carry):
         arrived(index)
         top = top_ref[:rows, :]
         for start in range(0, block, wide):
-            products = scores(unit_ref[...], protos_ref[index, start : start + wide, :])
+            turned = jnp.transpose(protos_ref[index, start : start + wide, :])
+            turned_ref[index, :, start : start + wide] = turned
+            products = jnp.dot(unit_ref[...], turned, preferred_element_type=jnp.float32)
             top = jnp.maximum(top, lane_fold(products, jnp.maximum))
         top_ref[:rows, :] = top
+        chunk_out(index).start()
         return carry
 
     lax.fori_loop(0, steps, step, 0)
-    tops = jnp.max(jnp.transpose(top_ref[...]), axis=0, keepdims=True)
-    tops_ref[...] = jnp.broadcast_to(tops[None], tops_ref.shape)
     for copy in copies:
         copy.wait()
     hidden = first_ref.shape[1]
@@ -150,28 +155,32 @@
         product = jnp.dot(h_first, second_ref[:, columns], preferred_element_type=jnp.float32)
         keep_ref[:, columns] = product[: 2 * share]
         give_ref[:, columns] = product[2 * share :]
-
-
-def front(index, unit, bias, rows, first, second, protos, order, copies, steps):
+    for index in range(steps):
+        chunk_out(index).wait()
+
+
+def front(index, unit, bias, rows, first, second, protos, order, steps):
     share, features = rows[0].shape
     hidden, units = second.shape
     count, width = protos.shape
     return pl.pallas_call(
         skipping(front_kernel, 10, len(order)),
         in_specs=[whole(pltpu.SMEM), whole(), whole()] + [whole(pl.ANY)] * (7 + len(order)),
-        out_specs=[whole()] * 3,
-        out_shape=[jax.ShapeDtypeStruct((copies, 1, 256), jnp.float32)]
-        + [jax.ShapeDtypeStruct((2 * share, units), jnp.float32)] * 2,
+        out_specs=[whole()] * 3 + [whole(pl.ANY)],
+        out_shape=[jax.ShapeDtypeStruct((256, 128), jnp.float32)]
+        + [jax.ShapeDtypeStruct((2 * share, units), jnp.float32)] * 2
+        + [pltpu.HBM((steps, width, count // steps), jnp.bfloat16)],
         scratch_shapes=[
             pltpu.VMEM(first.shape, jnp.bfloat16),
             pltpu.VMEM(second.shape, jnp.bfloat16),
             pltpu.VMEM((4 * share, features), jnp.bfloat16),
             pltpu.VMEM((steps, count // steps, width), jnp.bfloat16),
-            pltpu.VMEM((256, 128), jnp.float32),
+            pltpu.VMEM((steps, width, count // steps), jnp.bfloat16),
             pltpu.SemaphoreType.DMA((6,)),
             pltpu.SemaphoreType.DMA((steps,)),
-        ],
-        compiler_params=params(26),
+            pltpu.SemaphoreType.DMA((steps,)),
+        ],
+        compiler_params=params(34),
         cost_estimate=cost(
             2 * unit.size * count + 8 * share * hidden * (features + units), 2 * width * count
         ),
@@ -182,11 +191,44 @@
     )
 
 
-def repel_kernel(group, index_ref, unit_ref, tops_ref, scale_ref, protos_hbm, *rest):
-    out_refs, (protos_ref, sems, acc_ref, sum_ref, bias_ref) = rest[:-5], rest[-5:]
+def fetch_turned(source, target, sems, first_block=0):
+    count, _, columns = target.shape
+    pieces = source.shape[2] // columns
+
+    def chunk_copy(index):
+        place = source.at[first_block + index // pieces]
+        if pieces > 1:
+            place = place.at[:, part(lax.rem(index, pieces), columns)]
+        return pltpu.make_async_copy(place, target.at[index], sems.at[index])
+
+    for index in range(count):
+        chunk_copy(index).start()
+    return lambda index: chunk_copy(index).wait()
+
+
+def spread_tops_kernel(top_ref, out_ref):
+    tops = jnp.max(jnp.transpose(top_ref[...]), axis=0, keepdims=True)
+    out_ref[...] = jnp.broadcast_to(tops[None], out_ref.shape)
+
+
+def spread_tops(top, order, copies):
+    return pl.pallas_call(
+        skipping(spread_tops_kernel, 1, len(order)),
+        in_specs=[whole()] + [whole(pl.ANY)] * len(order),
+        out_specs=whole(),
+        out_shape=jax.ShapeDtypeStruct((copies, 1, 256), jnp.float32),
+        compiler_params=params(4),
+        cost_estimate=cost(top.size, 8 * top.size),
+        name="spread_tops",
+    )(top, *order)
+
+
+def repel_kernel(group, index_ref, unit_ref, tops_ref, scale_ref, protos_hbm, turned_hbm, *rest):
+    out_refs, (protos_ref, turned_ref, sems, turned_sems, acc_ref, sum_ref, bias_ref) = rest[:-7], rest[-7:]
     rows, width = unit_ref.shape
     steps, block = protos_ref.shape[:2]
     wide = min(WIDE, block)
+    turned_arrived = fetch_turned(turned_hbm, turned_ref, turned_sems)
     arrived = fetch(protos_hbm, protos_ref, sems)
     first = index_ref[0] * group
     top = tops_ref[first]
@@ -197,13 +239,15 @@
     sum_ref[...] = jnp.zeros(sum_ref.shape, jnp.float32)
 
     def step(index, carry):
+        turned_arrived(index)
         arrived(index)
         bias = bias_ref[...]
         total = sum_ref[...]
         acc = acc_ref[...]
         for start in range(0, block, wide):
             protos = protos_ref[index, start : start + wide, :]
-            products = scores(unit_ref[...], protos)
+            turned = turned_ref[index, :, start : start + wide]
+            products = jnp.dot(unit_ref[...], turned, preferred_element_type=jnp.float32)
             pieces = []
             for lane in range(0, wide, 128):
                 scaled = jnp.exp2(products[:, lane : lane + 128] * teacher_rate + bias)
@@ -236,13 +280,13 @@
             out_ref[:, width:] = jnp.where(lanes < 3, pieces, 0.0).astype(jnp.bfloat16)
 
 
-def repel(index, unit, tops, scale, protos, order, proto_size):
+def repel(index, unit, tops, scale, protos, turned, order, proto_size):
     rows, width = unit.shape
     count = protos.shape[0]
     steps, _, block = scale.shape
     return pl.pallas_call(
-        skipping(functools.partial(repel_kernel, proto_size), 5, len(order)),
-        in_specs=[whole(pltpu.SMEM), whole(), whole(), whole(), whole(pl.ANY)] + [whole(pl.ANY)] * len(order),
+        skipping(functools.partial(repel_kernel, proto_size), 6, len(order)),
+        in_specs=[whole(pltpu.SMEM), whole(), whole(), whole(), whole(pl.ANY), whole(pl.ANY)] + [whole(pl.ANY)] * len(order),
         out_specs=[whole()] * proto_size,
         out_shape=[
             jax.ShapeDtypeStruct((rows // proto_size, width + 128), jnp.bfloat16 if flip else jnp.float32)
@@ -250,31 +294,35 @@
         ],
         scratch_shapes=[
             pltpu.VMEM((steps, block, width), jnp.bfloat16),
+            pltpu.VMEM((steps, width, block), jnp.bfloat16),
+            pltpu.SemaphoreType.DMA((steps,)),
             pltpu.SemaphoreType.DMA((steps,)),
             pltpu.VMEM((rows, width), jnp.float32),
             pltpu.VMEM((rows, 128), jnp.float32),
             pltpu.VMEM((rows, 128), jnp.float32),
         ],
-        compiler_params=params(16),
+        compiler_params=params(26),
         cost_estimate=cost(4 * rows * width * count, 2 * width * count, rows * count),
         name="repel",
-    )(index, unit, tops, scale, in_hbm(protos), *order)
-
-
-def attract_kernel(first_row, last, emb_ref, state_ref, protos_hbm, *rest):
-    out_refs, scratch = rest[:-6], rest[-6:]
-    protos_ref, sems, products_ref, acc_ref, sum_ref, top_ref = scratch
+    )(index, unit, tops, scale, in_hbm(protos), in_hbm(turned), *order)
+
+
+def attract_kernel(first_row, last, emb_ref, state_ref, protos_hbm, turned_hbm, *rest):
+    out_refs, scratch = rest[:-8], rest[-8:]
+    protos_ref, turned_ref, sems, turned_sems, products_ref, acc_ref, sum_ref, top_ref = scratch
     width = emb_ref.shape[1]
     steps, block = protos_ref.shape[:2]
+    turned_arrived = fetch_turned(turned_hbm, turned_ref, turned_sems, first_row // block)
     arrived = fetch(protos_hbm, protos_ref, sems, first_row)
     old_top = state_ref[:, width + 128 :]
     top_ref[...] = old_top
 
     def first(index, carry):
-        arrived(index)
+        turned_arrived(index)
         top = top_ref[...]
         for start in range(0, block, TILE):
-            products = scores(emb_ref[...], protos_ref[index, start : start + TILE, :])
+            turned = turned_ref[index, :, start : start + TILE]
+            products = jnp.dot(emb_ref[...], turned, preferred_element_type=jnp.float32)
             products_ref[index, :, start : start + TILE] = products
             top = jnp.maximum(top, lane_fold(products, jnp.maximum))
         top_ref[...] = top
@@ -288,6 +336,7 @@
     acc_ref[...] = state_ref[:, :width] * jnp.tile(fade, (1, width // 128))
 
     def second(index, carry):
+        arrived(index)
         top = top_ref[...]
         total = sum_ref[...]
         acc = acc_ref[...]
@@ -318,26 +367,28 @@
         out_ref[:, width + 128 :] = top_ref[rows, :]
 
 
-def attract(emb, state, protos, first_row, count, steps, outputs):
+def attract(emb, state, protos, turned, first_row, count, steps, outputs):
     rows, width = emb.shape
     block = count // steps
     return pl.pallas_call(
         functools.partial(attract_kernel, first_row, outputs > 1),
-        in_specs=[whole(), whole(), whole(pl.ANY)],
+        in_specs=[whole(), whole(), whole(pl.ANY), whole(pl.ANY)],
         out_specs=[whole()] * outputs,
         out_shape=[jax.ShapeDtypeStruct((rows // outputs, width + 256), jnp.float32)] * outputs,
         scratch_shapes=[
             pltpu.VMEM((steps, block, width), jnp.bfloat16),
+            pltpu.VMEM((steps, width, block), jnp.bfloat16),
+            pltpu.SemaphoreType.DMA((steps,)),
             pltpu.SemaphoreType.DMA((steps,)),
             pltpu.VMEM((steps, rows, block), jnp.float32),
             pltpu.VMEM((rows, width), jnp.float32),
             pltpu.VMEM((rows, 128), jnp.float32),
             pltpu.VMEM((rows, 128), jnp.float32),
         ],
-        compiler_params=params(24),
+        compiler_params=params(30),
         cost_estimate=cost(4 * rows * width * count, 2 * width * count, rows * count),
         name="attract",
-    )(emb, state, in_hbm(protos))
+    )(emb, state, in_hbm(protos), in_hbm(turned))
 
 
 def three_pieces(values):
@@ -377,18 +428,18 @@
 
 
 def first_sweep_kernel(
-    chunk, protos_total, index_ref, protos_hbm, mine_hbm, other_hbm, bias_ref, copies_ref, weights_hbm, protos_ref, units_ref, weights_ref, rounded_ref, scale_ref, sems, out_sems,
+    chunk, protos_total, index_ref, protos_hbm, mine_hbm, other_hbm, bias_ref, copies_ref, weights_hbm, protos_ref, units_ref, weights_ref, rounded_ref, scale_ref, sems, chunk_sems, out_sems,
 ):
     thin, crops_total = weights_ref.shape
     half = mine_hbm.shape[0]
     core = index_ref[1]
     copies = (
-        pltpu.make_async_copy(protos_hbm.at[part(index_ref[0], thin), :], protos_ref, sems.at[0]),
-        pltpu.make_async_copy(mine_hbm, units_ref.at[part(core, half), :], sems.at[1]),
-        pltpu.make_async_copy(other_hbm, units_ref.at[part(1 - core, half), :], sems.at[2]),
+        pltpu.make_async_copy(mine_hbm, units_ref.at[part(core, half), :], sems.at[0]),
+        pltpu.make_async_copy(other_hbm, units_ref.at[part(1 - core, half), :], sems.at[1]),
     )
     for copy in copies:
         copy.start()
+    arrived = fetch(protos_hbm, protos_ref, chunk_sems, index_ref[0] * thin)
     for copy in copies:
         copy.wait()
 
@@ -399,7 +450,8 @@
 
     def weigh(index, carry):
         rows = part(index, chunk)
-        protos = protos_ref[rows, :]
+        arrived(index)
+        protos = protos_ref[index]
         folded = jnp.zeros((chunk, 128), jnp.float32)
         for start in range(0, crops_total, TILE):
             columns = slice(start, start + TILE)
@@ -441,12 +493,13 @@
             pltpu.HBM((thin, crops_total), jnp.bfloat16),
         ],
         scratch_shapes=[
-            pltpu.VMEM((thin, width), jnp.bfloat16),
+            pltpu.VMEM((thin // chunk, chunk, width), jnp.bfloat16),
             pltpu.VMEM((crops_total, width), jnp.bfloat16),
             pltpu.VMEM((thin, crops_total), jnp.float32),
             pltpu.VMEM((thin // chunk, chunk, crops_total), jnp.bfloat16),
             pltpu.VMEM((thin, 128), jnp.float32),
-            pltpu.SemaphoreType.DMA((3,)),
+            pltpu.SemaphoreType.DMA((2,)),
+            pltpu.SemaphoreType.DMA((thin // chunk,)),
             pltpu.SemaphoreType.DMA((thin // chunk,)),
         ],
         compiler_params=params(32 if crops_total <= 2048 else 56),
@@ -706,10 +759,10 @@
     rows = [crops, crops_x, swap(crops, "proto", 1), swap(crops_x, "proto", 1)]
     third_x = swap(w_third, "proto", 2)
     thirds = [w_third, third_x, swap(w_third, "proto", 1), swap(third_x, "proto", 1)]
-    top_copies, keep, give = front(
-        proto_ref, own_unit, b_first, rows, w_first, w_second, protos, (stages[2], third_x), devices, 8
+    top, keep, give, turned = front(
+        proto_ref, own_unit, b_first, rows, w_first, w_second, protos, (stages[2],), 8
     )
-    all_tops = all_to_all(top_copies, BOTH)
+    all_tops = all_to_all(spread_tops(top, (third_x,), devices), BOTH)
     tops = jnp.max(all_tops.reshape(batch_size, proto_size, 256)[:, :, :group_rows], axis=1)
     tops = bit_reversed(tops, batch_size).reshape(batch_size, 2, group_rows // 2)
     base = jnp.transpose(tops, (1, 0, 2)).reshape(1, crops_total) * -teacher_rate
@@ -724,8 +777,8 @@
     empty = jnp.concatenate(
         [jnp.zeros((group_rows, width + 128), jnp.float32), jnp.full((group_rows, 128), -1e30, jnp.float32)], axis=1
     )
-    (state,) = attract(student_emb, empty, protos, 0, count // 2, 4, 1)
-    slots = attract(student_emb, state, protos, count // 2, count // 2, 4, proto_size)
+    (state,) = attract(student_emb, empty, protos, turned, 0, count // 2, 4, 1)
+    slots = attract(student_emb, state, protos, turned, count // 2, count // 2, 4, proto_size)
     attract_parts = send_blocks(slots)
 
     copies, weights = first_sweep(thin_ref, protos, mine, other, base, (x_sent, *thirds[2:]), devices, thin, protos_total)
@@ -733,7 +786,7 @@
         copies = next_sweep(weights, all_to_all(copies, BOTH), (rounded,), protos_total)
     scale_copies = last_scales(weights, all_to_all(copies, BOTH), (state,), batch_size, protos_total)
     all_scale = all_to_all(scale_copies, "batch")
-    repels = repel(wide_ref, own_unit, all_tops, all_scale, protos, (slots[0],), proto_size)
+    repels = repel(wide_ref, own_unit, all_tops, all_scale, protos, turned, (slots[0],), proto_size)
     return finish(unit, lengths, attract_parts, send_blocks(repels))
 
 

time: 101 us -> 109 us (1.079)
  starting transfers between devices: 27.6 us -> 31.8 us
  waiting for transfers between devices: 25.3 us -> 27.4 us
  Pallas kernels: 46.1 us -> 47.6 us
    all_to_all x4, starting transfers between devices: 11.4 us -> 14.7 us  [all_to_all(): return lax.all_to_all(copies, axes, 0, 0, tiled=True)]
    pallas_call x1, Pallas kernels: 8.13 us -> 10.6 us  [front(): pl.pallas_call(skipping(front_kernel, 10, len(order)), in_specs=[whole(pl...]
    all_to_all x4, waiting for transfers between devices: 11.3 us -> 13 us  [all_to_all(): return lax.all_to_all(copies, axes, 0, 0, tiled=True)]
    pallas_call x1 -> x2, Pallas kernels: 9.48 us -> 8.58 us  [the longest x1 7.85 us: repel(): pl.pallas_call(skipping(functools.partial(repel_kernel, proto_size), 6, l...]
  transfers between devices with their start and end apart: 25 -> 25, of which waited for: 11 -> 10; matrix products, arithmetic and copies ran while one was open for 1% -> 1% of each run, Pallas kernels for 32% -> 29%
where the time goes in v14:
time: 109 us
  Pallas kernels  47.6 us (44%)
  starting transfers between devices  31.8 us (29%)
  waiting for transfers between devices  27.4 us (25%)
    ppermute x21, starting transfers between devices, swap(): lax.ppermute(values, axis, [(i, i ^ flip) for i in range(lax.axis_size(ax...  17.1 us
    all_to_all x4, starting transfers between devices, all_to_all(): return lax.all_to_all(copies, axes, 0, 0, tiled=True)  14.7 us
    ppermute x21, waiting for transfers between devices, swap(): lax.ppermute(values, axis, [(i, i ^ flip) for i in range(lax.axis_size(ax...  14.3 us
    all_to_all x4, waiting for transfers between devices, all_to_all(): return lax.all_to_all(copies, axes, 0, 0, tiled=True)  13 us
    pallas_call x2, Pallas kernels, attract(): pl.pallas_call(functools.partial(attract_kernel, first_row, outputs > 1),...  10.7 us
    pallas_call x1, Pallas kernels, front(): pl.pallas_call(skipping(front_kernel, 10, len(order)), in_specs=[whole(pl...  10.6 us
    pallas_call x1, Pallas kernels, repel(): pl.pallas_call(skipping(functools.partial(repel_kernel, proto_size), 6, l...  7.85 us
    pallas_call x1, Pallas kernels, first_sweep(): pl.pallas_call(skipping(functools.partial(first_sweep_kernel, chunk, prot...  6.12 us
  transfers between devices with their start and end apart: 25, of which 10 were waited for; matrix products, arithmetic and copies ran while one was open for 1% of the time, Pallas kernels for 29%

profile of v14, /device:TPU:0, one launch (start us, length us, event | category | flops | bytes accessed | tf_op | source)
XLA Modules:
  0.0 108.5 jit_solution(17191107671387901946)
XLA Ops:
  0.0 1.0 teacher_units.1
  1.0 4.1 %collective-permute-start.3 = (bf16[96,256]{1,0:T(8,128)(2,1)S(1)}, bf16[96,256]{1,0:T(8,128)(2,1)S(1)}, u32[]{:S(2)}, u32[]{:S(2)}) collective-permute-start(bf16[96,256]{1,0:T(8,128)(2,1)S(1)} %get-tuple-element.25), channel_id=1, source_target_pairs={{0,16},{4,20},{8,24},{12,28},{16,0},{20,4},{24,8},{28,12},{1,17},{... | collective-permute-start | bytes 147464 | tf_op jit(solution)/shard_map/ppermute | solution.py:704
  5.1 1.5 %collective-permute-start = (bf16[48,1536]{1,0:T(8,128)(2,1)}, bf16[48,1536]{1,0:T(8,128)(2,1)S(1)}, u32[]{:S(2)}, u32[]{:S(2)}) collective-permute-start(bf16[48,1536]{1,0:T(8,128)(2,1)} %refs_3_.1), channel_id=1, source_target_pairs={{0,2},{1,3},{2,0},{3,1},{4,6},{5,7},{6,4},{7,5},{8,10},{9,11},{10,... | collective-permute-start | bytes 442376 | tf_op jit(solution)/shard_map/ppermute | solution.py:704
  6.6 1.1 %collective-permute-done.3 = bf16[96,256]{1,0:T(8,128)(2,1)S(1)} collective-permute-done((bf16[96,256]{1,0:T(8,128)(2,1)S(1)}, bf16[96,256]{1,0:T(8,128)(2,1)S(1)}, u32[]{:S(2)}, u32[]{:S(2)}) %collective-permute-start.3) | collective-permute-done | bytes 49184 | tf_op jit(solution)/shard_map/ppermute | solution.py:704
  7.8 1.4 %collective-permute-start.4 = (bf16[192,256]{1,0:T(8,128)(2,1)S(1)}, bf16[192,256]{1,0:T(8,128)(2,1)S(1)}, u32[]{:S(2)}, u32[]{:S(2)}) collective-permute-start(bf16[192,256]{1,0:T(8,128)(2,1)S(1)} %maximum_select_fusion.2), channel_id=1, source_target_pairs={{0,8},{4,12},{8,0},{12,4},{16,24},{20,28},{24,16},{28,20},{1,9},{5... | collective-permute-start | bytes 294920 | tf_op jit(solution)/shard_map/ppermute | solution.py:704
  9.2 0.0 collective-permute-start.1
  9.2 1.5 %collective-permute-done.refs_4_ = bf16[48,1536]{1,0:T(8,128)(2,1)S(1)} collective-permute-done((bf16[48,1536]{1,0:T(8,128)(2,1)}, bf16[48,1536]{1,0:T(8,128)(2,1)S(1)}, u32[]{:S(2)}, u32[]{:S(2)}) %collective-permute-start) | collective-permute-done | bytes 147488 | tf_op jit(solution)/shard_map/ppermute | solution.py:704
  10.7 0.0 collective-permute-start.2
  10.7 1.8 %collective-permute-done.4 = bf16[192,256]{1,0:T(8,128)(2,1)S(1)} collective-permute-done((bf16[192,256]{1,0:T(8,128)(2,1)S(1)}, bf16[192,256]{1,0:T(8,128)(2,1)S(1)}, u32[]{:S(2)}, u32[]{:S(2)}) %collective-permute-start.4) | collective-permute-done | bytes 98336 | tf_op jit(solution)/shard_map/ppermute | solution.py:704
  12.4 0.1 maximum_select_fusion.1.refs_10_
  12.5 0.0 collective-permute-done.1.refs_5_
  12.5 0.0 collective-permute-done.2.refs_6_
  12.5 10.6 %front.1 = (f32[256,128]{1,0:T(8,128)S(1)}, f32[96,2048]{1,0:T(8,128)S(1)}, f32[96,2048]{1,0:T(8,128)}, bf16[8,256,2048]{2,1,0:T(8,128)(2,1)}) custom-call(s32[1]{0:T(128)} %bitcast.refs_0_.index_ref, bf16[192,256]{1,0:T(8,128)(2,1)S(1)} %get-tuple-element.24.refs_1_, f32[1,2048]{1,0:T(1,128)} %bitcast.11, bf16[48,1536]{1,0:T(8,128)(2,1)} %refs_3_.1, ...), custom_call_target="tpu_custom_call" | custom-call | flops 2315255808 | bytes 8388608 | tf_op jit(solution)/shard_map/front/pallas_call | solution.py:166
  23.1 0.1 collective-permute-start.5
  23.2 1.8 %collective-permute-start.7 = (bf16[512,256]{1,0:T(8,128)(2,1)}, bf16[512,256]{1,0:T(8,128)(2,1)S(1)}, u32[]{:S(2)}, u32[]{:S(2)}) collective-permute-start(bf16[512,256]{1,0:T(8,128)(2,1)} %own_ref.1), channel_id=1, source_target_pairs={{0,2},{1,3},{2,0},{3,1},{4,6},{5,7},{6,4},{7,5},{8,10},{9,11},{10,... | collective-permute-start | bytes 786440 | tf_op jit(solution)/shard_map/ppermute | solution.py:704
  24.9 1.5 %collective-permute-start.16 = (bf16[384,256]{1,0:T(8,128)(2,1)S(1)}, bf16[384,256]{1,0:T(8,128)(2,1)S(1)}, u32[]{:S(2)}, u32[]{:S(2)}) collective-permute-start(bf16[384,256]{1,0:T(8,128)(2,1)S(1)} %maximum_select_fusion.1.refs_10_), channel_id=1, source_target_pairs={{0,4},{4,0},{8,12},{12,8},{16,20},{20,16},{24,28},{28,24},{1,5},{5... | collective-permute-start | bytes 589832 | tf_op jit(solution)/shard_map/ppermute | solution.py:704
  26.4 0.0 collective-permute-start.8
  26.4 0.1 pad_add_fusion.1.refs_0_
  26.5 5.6 %collective-permute-done.7.partner_ref.refs_1_ = bf16[512,256]{1,0:T(8,128)(2,1)S(1)} collective-permute-done((bf16[512,256]{1,0:T(8,128)(2,1)}, bf16[512,256]{1,0:T(8,128)(2,1)S(1)}, u32[]{:S(2)}, u32[]{:S(2)}) %collective-permute-start.7) | collective-permute-done | bytes 262176 | tf_op jit(solution)/shard_map/ppermute | solution.py:704
  32.1 0.0 collective-permute-start.9
  32.1 0.7 spread_tops.1
  32.8 6.2 %all-to-all-start = ((f32[32,1,256]{2,1,0:T(1,128)}), f32[32,1,256]{2,1,0:T(1,128)S(1)}, u32[]{:S(2)}, u32[]{:S(2)}) async-start(f32[32,1,256]{2,1,0:T(1,128)} %spread_tops.1), calls=%async_computation | async-start | bytes 65536 | tf_op jit(solution)/shard_map/all_to_all | solution.py:733
  39.0 0.0 collective-permute-done.16
  39.0 0.2 maximum_select_fusion.refs_2_
  39.2 0.3 collective-permute-start.17
  39.5 6.8 %all-to-all-done.refs_2_ = f32[32,1,256]{2,1,0:T(1,128)S(1)} async-done(((f32[32,1,256]{2,1,0:T(1,128)}), f32[32,1,256]{2,1,0:T(1,128)S(1)}, u32[]{:S(2)}, u32[]{:S(2)}) %all-to-all-start) | async-done | bytes 32800 | tf_op jit(solution)/shard_map/all_to_all | solution.py:733
  46.3 0.1 reduce
  46.4 0.0 collective-permute-done.5.core_ref
  46.5 0.6 collective-permute-start.6
  47.1 0.1 mul.17
  47.2 0.1 mul.19.refs_4_
  47.3 6.1 %first_sweep.1 = (bf16[32,16,128]{2,1,0:T(8,128)(2,1)S(1)}, bf16[2048,1536]{1,0:T(8,128)(2,1)}) custom-call(s32[2]{0:T(128)S(1)} %pad_add_fusion.1.refs_0_, bf16[16384,256]{1,0:T(8,128)(2,1)} %refs_4_.1, bf16[768,256]{1,0:T(8,128)(2,1)S(1)} %maximum_select_fusion.refs_2_, bf16[768,256]{1,0:T(8,128)(2,1)} %collective-permute-done.17.refs_3_, ...), custom_call_target="tpu_custom_call" | custom-call | flops 1610612736 | bytes 6291456 | tf_op jit(solution)/shard_map/first_sweep/pallas_call | solution.py:486
  53.4 0.7 copy-done
  54.1 2.6 %all-to-all-start.1 = ((bf16[32,16,128]{2,1,0:T(8,128)(2,1)}), bf16[32,16,128]{2,1,0:T(8,128)(2,1)S(1)}, u32[]{:S(2)}, u32[]{:S(2)}) async-start(bf16[32,16,128]{2,1,0:T(8,128)(2,1)} %copy-done), calls=%async_computation.1 | async-start | bytes 262144 | tf_op jit(solution)/shard_map/all_to_all | solution.py:733
  56.6 0.1 pad_add_fusion.refs_0_
  56.7 1.1 collective-permute-done.6.x_ref
  57.8 1.6 %student_middle.1 = (f32[48,256]{1,0:T(8,128)S(1)}, bf16[48,256]{1,0:T(8,128)(2,1)S(1)}, f32[48,128]{1,0:T(8,128)S(1)}) custom-call(s32[1]{0:T(128)} %bitcast.refs_0_.index_ref, f32[96,2048]{1,0:T(8,128)S(1)} %get-tuple-element.26.keep_ref, f32[96,2048]{1,0:T(8,128)S(1)} %collective-permute-done.5.core_ref, f32[48,2048]{1,0:T(8,128)} %collective-permute-done.6.x_ref, ...), custom_call_target="tpu_custom_call" | custom-call | flops 50331648 | bytes 2621440 | tf_op jit(solution)/shard_map/student_middle/pallas_call | solution.py:652
  59.4 0.4 collective-permute-start.12
  59.8 0.6 collective-permute-start.11
  60.4 0.9 collective-permute-start.10
  61.4 3.5 %all-to-all-done.1.refs_1_ = bf16[32,16,128]{2,1,0:T(8,128)(2,1)S(1)} async-done(((bf16[32,16,128]{2,1,0:T(8,128)(2,1)}), bf16[32,16,128]{2,1,0:T(8,128)(2,1)S(1)}, u32[]{:S(2)}, u32[]{:S(2)}) %all-to-all-start.1) | async-done | bytes 131104 | tf_op jit(solution)/shard_map/all_to_all | solution.py:733
  64.8 4.4 %next_sweep.1 = bf16[32,16,128]{2,1,0:T(8,128)(2,1)} custom-call(bf16[2048,1536]{1,0:T(8,128)(2,1)} %get-tuple-element.37.refs_0_, bf16[32,16,128]{2,1,0:T(8,128)(2,1)S(1)} %all-to-all-done.1.refs_1_, bf16[48,256]{1,0:T(8,128)(2,1)S(1)} %get-tuple-element.30.refs_2_), custom_call_target="tpu_custom_call" | custom-call | flops 25165824 | bytes 6291456 | tf_op jit(solution)/shard_map/next_sweep/pallas_call | solution.py:572
  69.2 2.6 %all-to-all-start.2 = ((bf16[32,16,128]{2,1,0:T(8,128)(2,1)}), bf16[32,16,128]{2,1,0:T(8,128)(2,1)S(1)}, u32[]{:S(2)}, u32[]{:S(2)}) async-start(bf16[32,16,128]{2,1,0:T(8,128)(2,1)} %next_sweep.1), calls=%async_computation.2 | async-start | bytes 262144 | tf_op jit(solution)/shard_map/all_to_all | solution.py:733
  71.8 0.0 collective-permute-done.10
  71.9 0.0 collective-permute-done.12
  71.9 5.3 %attract.2.state_ref.refs_2_ = f32[192,512]{1,0:T(8,128)S(1)} custom-call(bf16[192,256]{1,0:T(8,128)(2,1)S(1)} %constant_dynamic-update-slice_fusion.emb_ref, f32[192,512]{1,0:T(8,128)S(1)} %concatenate.32.state_ref, bf16[16384,256]{1,0:T(8,128)(2,1)} %refs_4_.1, bf16[8,256,2048]{2,1,0:T(8,128)(2,1)} %get-tuple-element.31.turned_hbm.refs_5_), custom_call_target="tpu_custom_call" | custom-call | flops 1610612736 | bytes 4194304 | tf_op jit(solution)/shard_map/attract/pallas_call | solution.py:373
  77.3 2.8 %all-to-all-done.2.refs_1_ = bf16[32,16,128]{2,1,0:T(8,128)(2,1)S(1)} async-done(((bf16[32,16,128]{2,1,0:T(8,128)(2,1)}), bf16[32,16,128]{2,1,0:T(8,128)(2,1)S(1)}, u32[]{:S(2)}, u32[]{:S(2)}) %all-to-all-start.2) | async-done | bytes 131104 | tf_op jit(solution)/shard_map/all_to_all | solution.py:733
  80.1 3.7 %last_scales.1 = f32[8,1,2048]{2,1,0:T(1,128)} custom-call(bf16[2048,1536]{1,0:T(8,128)(2,1)} %get-tuple-element.37.refs_0_, bf16[32,16,128]{2,1,0:T(8,128)(2,1)S(1)} %all-to-all-done.2.refs_1_, f32[192,512]{1,0:T(8,128)S(1)} %attract.2.state_ref.refs_2_), custom_call_target="tpu_custom_call" | custom-call | flops 12582912 | bytes 6291456 | tf_op jit(solution)/shard_map/last_scales/pallas_call | solution.py:611
  83.8 3.4 %all-to-all-start.3 = ((f32[8,1,2048]{2,1,0:T(1,128)}), f32[8,1,2048]{2,1,0:T(1,128)S(1)}, u32[]{:S(2)}, u32[]{:S(2)}) async-start(f32[8,1,2048]{2,1,0:T(1,128)} %last_scales.1), calls=%async_computation.3 | async-start | bytes 131072 | tf_op jit(solution)/shard_map/all_to_all | solution.py:733
  87.2 5.4 %attract.3 = (f32[48,512]{1,0:T(8,128)S(1)}, f32[48,512]{1,0:T(8,128)S(1)}, f32[48,512]{1,0:T(8,128)S(1)}, f32[48,512]{1,0:T(8,128)S(1)}) custom-call(bf16[192,256]{1,0:T(8,128)(2,1)S(1)} %constant_dynamic-update-slice_fusion.emb_ref, f32[192,512]{1,0:T(8,128)S(1)} %attract.2.state_ref.refs_2_, bf16[16384,256]{1,0:T(8,128)(2,1)} %refs_4_.1, ...), custom_call_target="tpu_custom_call" | custom-call | flops 1610612736 | bytes 4194304 | tf_op jit(solution)/shard_map/attract/pallas_call | solution.py:373
  92.6 0.3 collective-permute-start.13
  92.9 1.1 collective-permute-start.14
  93.9 0.6 collective-permute-start.15
  94.5 7.8 %repel.1 = (f32[48,384]{1,0:T(8,128)S(1)}, bf16[48,384]{1,0:T(8,128)(2,1)S(1)}, bf16[48,384]{1,0:T(8,128)(2,1)S(1)}, bf16[48,384]{1,0:T(8,128)(2,1)S(1)}) custom-call(s32[2]{0:T(128)S(1)} %pad_add_fusion.refs_0_, bf16[192,256]{1,0:T(8,128)(2,1)S(1)} %get-tuple-element.24.refs_1_, f32[32,1,256]{2,1,0:T(1,128)S(1)} %all-to-all-done.refs_2_, ...), custom_call_target="tpu_custom_call" | custom-call | flops 3221225472 | bytes 8388608 | tf_op jit(solution)/shard_map/repel/pallas_call | solution.py:287
  102.4 0.6 collective-permute-start.18
  102.9 1.1 collective-permute-start.19
  104.0 0.0 collective-permute-done.13.rest_1_
  104.0 0.4 collective-permute-start.20
  104.4 0.0 collective-permute-done.14.rest_2_
  104.4 0.0 collective-permute-done.15.rest_3_
  104.4 0.0 collective-permute-done.18.rest_5_
  104.4 2.5 %collective-permute-done.19.rest_6_ = bf16[48,384]{1,0:T(8,128)(2,1)S(1)} collective-permute-done((bf16[48,384]{1,0:T(8,128)(2,1)S(1)}, bf16[48,384]{1,0:T(8,128)(2,1)S(1)}, u32[]{:S(2)}, u32[]{:S(2)}) %collective-permute-start.19) | collective-permute-done | bytes 36896 | tf_op jit(solution)/shard_map/ppermute | solution.py:704
  106.9 0.8 collective-permute-done.20.rest_7_
  107.7 0.8 finish.1
  (21 shorter events, 0.2 us)
Async XLA Ops:
  1.0 6.7 %collective-permute-start.3 = (bf16[96,256]{1,0:T(8,128)(2,1)S(1)}, bf16[96,256]{1,0:T(8,128)(2,1)S(1)}, u32[]{:S(2)}, u32[]{:S(2)}) collective-permute-start(bf16[96,256]{1,0:T(8,128)(2,1)S(1)} %get-tuple-element.25), channel_id=1, source_target_pairs={{0,16},{4,20},{8,24},{12,28},{16,0},{20,4},{24,8},{28,12},{1,17},{... | collective-permute-start | bytes 147464 | tf_op jit(solution)/shard_map/ppermute | solution.py:704
  5.1 5.5 %collective-permute-start = (bf16[48,1536]{1,0:T(8,128)(2,1)}, bf16[48,1536]{1,0:T(8,128)(2,1)S(1)}, u32[]{:S(2)}, u32[]{:S(2)}) collective-permute-start(bf16[48,1536]{1,0:T(8,128)(2,1)} %refs_3_.1), channel_id=1, source_target_pairs={{0,2},{1,3},{2,0},{3,1},{4,6},{5,7},{6,4},{7,5},{8,10},{9,11},{10,... | collective-permute-start | bytes 442376 | tf_op jit(solution)/shard_map/ppermute | solution.py:704
  7.8 4.7 %collective-permute-start.4 = (bf16[192,256]{1,0:T(8,128)(2,1)S(1)}, bf16[192,256]{1,0:T(8,128)(2,1)S(1)}, u32[]{:S(2)}, u32[]{:S(2)}) collective-permute-start(bf16[192,256]{1,0:T(8,128)(2,1)S(1)} %maximum_select_fusion.2), channel_id=1, source_target_pairs={{0,8},{4,12},{8,0},{12,4},{16,24},{20,28},{24,16},{28,20},{1,9},{5... | collective-permute-start | bytes 294920 | tf_op jit(solution)/shard_map/ppermute | solution.py:704
  9.2 3.3 %collective-permute-start.1 = (bf16[48,1536]{1,0:T(8,128)(2,1)}, bf16[48,1536]{1,0:T(8,128)(2,1)S(1)}, u32[]{:S(2)}, u32[]{:S(2)}) collective-permute-start(bf16[48,1536]{1,0:T(8,128)(2,1)} %refs_3_.1), channel_id=1, source_target_pairs={{0,1},{1,0},{2,3},{3,2},{4,5},{5,4},{6,7},{7,6},{8,9},{9,8},{10,11... | collective-permute-start | bytes 442376 | tf_op jit(solution)/shard_map/ppermute | solution.py:704
  10.7 1.9 %collective-permute-start.2 = (bf16[48,1536]{1,0:T(8,128)(2,1)S(1)}, bf16[48,1536]{1,0:T(8,128)(2,1)S(1)}, u32[]{:S(2)}, u32[]{:S(2)}) collective-permute-start(bf16[48,1536]{1,0:T(8,128)(2,1)S(1)} %collective-permute-done.refs_4_), channel_id=1, source_target_pairs={{0,1},{1,0},{2,3},{3,2},{4,5},{5,4},{6,7},{7,6},{8,9},{9,8},{10,11... | collective-permute-start | bytes 442376 | tf_op jit(solution)/shard_map/ppermute | solution.py:704
  23.1 23.3 %collective-permute-start.5 = (f32[96,2048]{1,0:T(8,128)}, f32[96,2048]{1,0:T(8,128)S(1)}, u32[]{:S(2)}, u32[]{:S(2)}) collective-permute-start(f32[96,2048]{1,0:T(8,128)} %get-tuple-element.27), channel_id=1, source_target_pairs={{0,1},{1,0},{2,3},{3,2},{4,5},{5,4},{6,7},{7,6},{8,9},{9,8},{10,11... | collective-permute-start | bytes 2359304 | tf_op jit(solution)/shard_map/ppermute | solution.py:704
  23.2 8.9 %collective-permute-start.7 = (bf16[512,256]{1,0:T(8,128)(2,1)}, bf16[512,256]{1,0:T(8,128)(2,1)S(1)}, u32[]{:S(2)}, u32[]{:S(2)}) collective-permute-start(bf16[512,256]{1,0:T(8,128)(2,1)} %own_ref.1), channel_id=1, source_target_pairs={{0,2},{1,3},{2,0},{3,1},{4,6},{5,7},{6,4},{7,5},{8,10},{9,11},{10,... | collective-permute-start | bytes 786440 | tf_op jit(solution)/shard_map/ppermute | solution.py:704
  24.9 14.1 %collective-permute-start.16 = (bf16[384,256]{1,0:T(8,128)(2,1)S(1)}, bf16[384,256]{1,0:T(8,128)(2,1)S(1)}, u32[]{:S(2)}, u32[]{:S(2)}) collective-permute-start(bf16[384,256]{1,0:T(8,128)(2,1)S(1)} %maximum_select_fusion.1.refs_10_), channel_id=1, source_target_pairs={{0,4},{4,0},{8,12},{12,8},{16,20},{20,16},{24,28},{28,24},{1,5},{5... | collective-permute-start | bytes 589832 | tf_op jit(solution)/shard_map/ppermute | solution.py:704
  26.4 20.8 %collective-permute-start.8 = (bf16[512,256]{1,0:T(8,128)(2,1)}, bf16[512,256]{1,0:T(8,128)(2,1)S(1)}, u32[]{:S(2)}, u32[]{:S(2)}) collective-permute-start(bf16[512,256]{1,0:T(8,128)(2,1)} %own_ref.1), channel_id=1, source_target_pairs={{0,1},{1,0},{2,3},{3,2},{4,5},{5,4},{6,7},{7,6},{8,9},{9,8},{10,11... | collective-permute-start | bytes 786440 | tf_op jit(solution)/shard_map/ppermute | solution.py:704
  32.1 15.1 %collective-permute-start.9 = (bf16[512,256]{1,0:T(8,128)(2,1)S(1)}, bf16[512,256]{1,0:T(8,128)(2,1)S(1)}, u32[]{:S(2)}, u32[]{:S(2)}) collective-permute-start(bf16[512,256]{1,0:T(8,128)(2,1)S(1)} %collective-permute-done.7.partner_ref.refs_1_), channel_id=1, source_target_pairs={{0,1},{1,0},{2,3},{3,2},{4,5},{5,4},{6,7},{7,6},{8,9},{9,8},{10,11... | collective-permute-start | bytes 786440 | tf_op jit(solution)/shard_map/ppermute | solution.py:704
  32.8 13.4 %all-to-all-start = ((f32[32,1,256]{2,1,0:T(1,128)}), f32[32,1,256]{2,1,0:T(1,128)S(1)}, u32[]{:S(2)}, u32[]{:S(2)}) async-start(f32[32,1,256]{2,1,0:T(1,128)} %spread_tops.1), calls=%async_computation | async-start | bytes 65536 | tf_op jit(solution)/shard_map/all_to_all | solution.py:733
  39.2 8.1 %collective-permute-start.17 = (bf16[768,256]{1,0:T(8,128)(2,1)S(1)}, bf16[768,256]{1,0:T(8,128)(2,1)}, u32[]{:S(2)}, u32[]{:S(2)}) collective-permute-start(bf16[768,256]{1,0:T(8,128)(2,1)S(1)} %maximum_select_fusion.refs_2_), channel_id=1, source_target_pairs={{0,1},{1,0},{2,3},{3,2},{4,5},{5,4},{6,7},{7,6},{8,9},{9,8},{10,11... | collective-permute-start | bytes 1179656 | tf_op jit(solution)/shard_map/ppermute | solution.py:704
  46.5 11.3 %collective-permute-start.6 = (f32[48,2048]{1,0:T(8,128)S(1)}, f32[48,2048]{1,0:T(8,128)}, u32[]{:S(2)}, u32[]{:S(2)}) collective-permute-start(f32[48,2048]{1,0:T(8,128)S(1)} %slice_add_fusion.refs_5_), channel_id=1, source_target_pairs={{0,2},{1,3},{2,0},{3,1},{4,6},{5,7},{6,4},{7,5},{8,10},{9,11},{10,... | collective-permute-start | bytes 1179656 | tf_op jit(solution)/shard_map/ppermute | solution.py:704
  53.4 0.7 copy-start
  54.1 10.8 %all-to-all-start.1 = ((bf16[32,16,128]{2,1,0:T(8,128)(2,1)}), bf16[32,16,128]{2,1,0:T(8,128)(2,1)S(1)}, u32[]{:S(2)}, u32[]{:S(2)}) async-start(bf16[32,16,128]{2,1,0:T(8,128)(2,1)} %copy-done), calls=%async_computation.1 | async-start | bytes 262144 | tf_op jit(solution)/shard_map/all_to_all | solution.py:733
  59.4 12.4 %collective-permute-start.12 = (bf16[48,256]{1,0:T(8,128)(2,1)S(1)}, bf16[48,256]{1,0:T(8,128)(2,1)S(1)}, u32[]{:S(2)}, u32[]{:S(2)}) collective-permute-start(bf16[48,256]{1,0:T(8,128)(2,1)S(1)} %get-tuple-element.30.refs_2_), channel_id=1, source_target_pairs={{0,3},{1,2},{2,1},{3,0},{4,7},{5,6},{6,5},{7,4},{8,11},{9,10},{10,... | collective-permute-start | bytes 73736 | tf_op jit(solution)/shard_map/ppermute | solution.py:704
  59.8 12.0 %collective-permute-start.11 = (bf16[48,256]{1,0:T(8,128)(2,1)S(1)}, bf16[48,256]{1,0:T(8,128)(2,1)S(1)}, u32[]{:S(2)}, u32[]{:S(2)}) collective-permute-start(bf16[48,256]{1,0:T(8,128)(2,1)S(1)} %get-tuple-element.30.refs_2_), channel_id=1, source_target_pairs={{0,2},{1,3},{2,0},{3,1},{4,6},{5,7},{6,4},{7,5},{8,10},{9,11},{10,... | collective-permute-start | bytes 73736 | tf_op jit(solution)/shard_map/ppermute | solution.py:704
  60.4 11.4 %collective-permute-start.10 = (bf16[48,256]{1,0:T(8,128)(2,1)S(1)}, bf16[48,256]{1,0:T(8,128)(2,1)S(1)}, u32[]{:S(2)}, u32[]{:S(2)}) collective-permute-start(bf16[48,256]{1,0:T(8,128)(2,1)S(1)} %get-tuple-element.30.refs_2_), channel_id=1, source_target_pairs={{0,1},{1,0},{2,3},{3,2},{4,5},{5,4},{6,7},{7,6},{8,9},{9,8},{10,11... | collective-permute-start | bytes 73736 | tf_op jit(solution)/shard_map/ppermute | solution.py:704
  69.2 10.8 %all-to-all-start.2 = ((bf16[32,16,128]{2,1,0:T(8,128)(2,1)}), bf16[32,16,128]{2,1,0:T(8,128)(2,1)S(1)}, u32[]{:S(2)}, u32[]{:S(2)}) async-start(bf16[32,16,128]{2,1,0:T(8,128)(2,1)} %next_sweep.1), calls=%async_computation.2 | async-start | bytes 262144 | tf_op jit(solution)/shard_map/all_to_all | solution.py:733
  83.8 10.7 %all-to-all-start.3 = ((f32[8,1,2048]{2,1,0:T(1,128)}), f32[8,1,2048]{2,1,0:T(1,128)S(1)}, u32[]{:S(2)}, u32[]{:S(2)}) async-start(f32[8,1,2048]{2,1,0:T(1,128)} %last_scales.1), calls=%async_computation.3 | async-start | bytes 131072 | tf_op jit(solution)/shard_map/all_to_all | solution.py:733
  92.6 11.4 %collective-permute-start.13 = (f32[48,512]{1,0:T(8,128)S(1)}, f32[48,512]{1,0:T(8,128)S(1)}, u32[]{:S(2)}, u32[]{:S(2)}) collective-permute-start(f32[48,512]{1,0:T(8,128)S(1)} %get-tuple-element.33), channel_id=1, source_target_pairs={{0,1},{1,0},{2,3},{3,2},{4,5},{5,4},{6,7},{7,6},{8,9},{9,8},{10,11... | collective-permute-start | bytes 294920 | tf_op jit(solution)/shard_map/ppermute | solution.py:704
  92.9 11.5 %collective-permute-start.14 = (f32[48,512]{1,0:T(8,128)S(1)}, f32[48,512]{1,0:T(8,128)S(1)}, u32[]{:S(2)}, u32[]{:S(2)}) collective-permute-start(f32[48,512]{1,0:T(8,128)S(1)} %get-tuple-element.34), channel_id=1, source_target_pairs={{0,2},{1,3},{2,0},{3,1},{4,6},{5,7},{6,4},{7,5},{8,10},{9,11},{10,... | collective-permute-start | bytes 294920 | tf_op jit(solution)/shard_map/ppermute | solution.py:704
  93.9 10.4 %collective-permute-start.15 = (f32[48,512]{1,0:T(8,128)S(1)}, f32[48,512]{1,0:T(8,128)S(1)}, u32[]{:S(2)}, u32[]{:S(2)}) collective-permute-start(f32[48,512]{1,0:T(8,128)S(1)} %get-tuple-element.35), channel_id=1, source_target_pairs={{0,3},{1,2},{2,1},{3,0},{4,7},{5,6},{6,5},{7,4},{8,11},{9,10},{10,... | collective-permute-start | bytes 294920 | tf_op jit(solution)/shard_map/ppermute | solution.py:704
  102.4 2.0 %collective-permute-start.18 = (bf16[48,384]{1,0:T(8,128)(2,1)S(1)}, bf16[48,384]{1,0:T(8,128)(2,1)S(1)}, u32[]{:S(2)}, u32[]{:S(2)}) collective-permute-start(bf16[48,384]{1,0:T(8,128)(2,1)S(1)} %get-tuple-element.40), channel_id=1, source_target_pairs={{0,1},{1,0},{2,3},{3,2},{4,5},{5,4},{6,7},{7,6},{8,9},{9,8},{10,11... | collective-permute-start | bytes 110600 | tf_op jit(solution)/shard_map/ppermute | solution.py:704
  102.9 4.0 %collective-permute-start.19 = (bf16[48,384]{1,0:T(8,128)(2,1)S(1)}, bf16[48,384]{1,0:T(8,128)(2,1)S(1)}, u32[]{:S(2)}, u32[]{:S(2)}) collective-permute-start(bf16[48,384]{1,0:T(8,128)(2,1)S(1)} %get-tuple-element.41), channel_id=1, source_target_pairs={{0,2},{1,3},{2,0},{3,1},{4,6},{5,7},{6,4},{7,5},{8,10},{9,11},{10,... | collective-permute-start | bytes 110600 | tf_op jit(solution)/shard_map/ppermute | solution.py:704
  104.0 3.7 %collective-permute-start.20 = (bf16[48,384]{1,0:T(8,128)(2,1)S(1)}, bf16[48,384]{1,0:T(8,128)(2,1)S(1)}, u32[]{:S(2)}, u32[]{:S(2)}) collective-permute-start(bf16[48,384]{1,0:T(8,128)(2,1)S(1)} %get-tuple-element.42), channel_id=1, source_target_pairs={{0,3},{1,2},{2,1},{3,0},{4,7},{5,6},{6,5},{7,4},{8,11},{9,10},{10,... | collective-permute-start | bytes 110600 | tf_op jit(solution)/shard_map/ppermute | solution.py:704

commit v15 on v13

--- a/solution.py
+++ b/solution.py
@@ -721,7 +721,7 @@
     third_x = swap(w_third, "proto", 2)
     thirds = [w_third, third_x, swap(w_third, "proto", 1), swap(third_x, "proto", 1)]
     top_copies = wide_tops(own_unit, protos, (stages[1],), devices, 8)
-    keep, give = student_front(proto_ref, b_first, rows, w_first, w_second, (stages[2], third_x))
+    keep, give = student_front(proto_ref, b_first, rows, w_first, w_second, (stages[2], third_x, top_copies))
     all_tops = all_to_all(top_copies, BOTH)
     tops = jnp.max(all_tops.reshape(batch_size, proto_size, 256)[:, :, :group_rows], axis=1)
     tops = bit_reversed(tops, batch_size).reshape(batch_size, 2, group_rows // 2)

time: 107 us -> 103 us (0.963)
  waiting for transfers between devices: 23.6 us -> 18.8 us
    ppermute x21, waiting for transfers between devices: 10.7 us -> 5.87 us  [swap(): lax.ppermute(values, axis, [(i, i ^ flip) for i in range(lax.axis_size(ax...]
  transfers between devices with their start and end apart: 25 -> 25, of which waited for: 9 -> 7; matrix products, arithmetic and copies ran while one was open for 1% -> 1% of each run, Pallas kernels for 36% -> 38%
where the time goes in v15:
time: 103 us; the launch traced here: 102 us
  Pallas kernels  48.9 us (47%)
  starting transfers between devices  33.6 us (33%)
  waiting for transfers between devices  18.8 us (18%)
    ppermute x21, starting transfers between devices, swap(): lax.ppermute(values, axis, [(i, i ^ flip) for i in range(lax.axis_size(ax...  17.8 us
    all_to_all x4, starting transfers between devices, all_to_all(): return lax.all_to_all(copies, axes, 0, 0, tiled=True)  15.8 us
    all_to_all x4, waiting for transfers between devices, all_to_all(): return lax.all_to_all(copies, axes, 0, 0, tiled=True)  12.9 us
    pallas_call x2, Pallas kernels, attract(): pl.pallas_call(functools.partial(attract_kernel, first_row, outputs > 1),...  10.2 us
    pallas_call x1, Pallas kernels, repel(): pl.pallas_call(skipping(functools.partial(repel_kernel, proto_size), 5, l...  9.48 us
    pallas_call x1, Pallas kernels, first_sweep(): pl.pallas_call(skipping(functools.partial(first_sweep_kernel, chunk, prot...  6.72 us
    pallas_call x1, Pallas kernels, wide_tops(): pl.pallas_call(skipping(wide_tops_kernel, 2, len(order)), in_specs=[whole...  6.07 us
    ppermute x21, waiting for transfers between devices, swap(): lax.ppermute(values, axis, [(i, i ^ flip) for i in range(lax.axis_size(ax...  5.87 us
  transfers between devices with their start and end apart: 25, of which 7 were waited for; matrix products, arithmetic and copies ran while one was open for 1% of the time, Pallas kernels for 38%

profile of v15, /device:TPU:0, one launch (start us, length us, event | category | flops | bytes accessed | tf_op | source)
XLA Modules:
  0.0 102.4 jit_solution(13427438819595188071)
XLA Ops:
  0.0 1.0 teacher_units.1
  1.0 4.1 %collective-permute-start.3 = (bf16[96,256]{1,0:T(8,128)(2,1)S(1)}, bf16[96,256]{1,0:T(8,128)(2,1)S(1)}, u32[]{:S(2)}, u32[]{:S(2)}) collective-permute-start(bf16[96,256]{1,0:T(8,128)(2,1)S(1)} %get-tuple-element.22), channel_id=1, source_target_pairs={{0,16},{4,20},{8,24},{12,28},{16,0},{20,4},{24,8},{28,12},{1,17},{... | collective-permute-start | bytes 147464 | tf_op jit(solution)/shard_map/ppermute | solution.py:665
  5.1 1.5 %collective-permute-start = (bf16[48,1536]{1,0:T(8,128)(2,1)}, bf16[48,1536]{1,0:T(8,128)(2,1)S(1)}, u32[]{:S(2)}, u32[]{:S(2)}) collective-permute-start(bf16[48,1536]{1,0:T(8,128)(2,1)} %refs_2_.1), channel_id=1, source_target_pairs={{0,2},{1,3},{2,0},{3,1},{4,6},{5,7},{6,4},{7,5},{8,10},{9,11},{10,... | collective-permute-start | bytes 442376 | tf_op jit(solution)/shard_map/ppermute | solution.py:665
  6.6 0.0 collective-permute-start.1
  6.6 0.5 collective-permute-start.5
  7.2 0.6 collective-permute-done.3
  7.8 1.4 %collective-permute-start.4 = (bf16[192,256]{1,0:T(8,128)(2,1)S(1)}, bf16[192,256]{1,0:T(8,128)(2,1)S(1)}, u32[]{:S(2)}, u32[]{:S(2)}) collective-permute-start(bf16[192,256]{1,0:T(8,128)(2,1)S(1)} %maximum_select_fusion.2.refs_2_), channel_id=1, source_target_pairs={{0,8},{4,12},{8,0},{12,4},{16,24},{20,28},{24,16},{28,20},{1,9},{5... | collective-permute-start | bytes 294920 | tf_op jit(solution)/shard_map/ppermute | solution.py:665
  9.2 2.2 %collective-permute-done.refs_3_ = bf16[48,1536]{1,0:T(8,128)(2,1)S(1)} collective-permute-done((bf16[48,1536]{1,0:T(8,128)(2,1)}, bf16[48,1536]{1,0:T(8,128)(2,1)S(1)}, u32[]{:S(2)}, u32[]{:S(2)}) %collective-permute-start) | collective-permute-done | bytes 147488 | tf_op jit(solution)/shard_map/ppermute | solution.py:665
  11.4 0.0 collective-permute-start.2
  11.4 6.1 %wide_tops.1.refs_10_ = f32[32,1,256]{2,1,0:T(1,128)} custom-call(bf16[192,256]{1,0:T(8,128)(2,1)S(1)} %get-tuple-element.23.refs_0_.refs_1_, bf16[16384,256]{1,0:T(8,128)(2,1)} %refs_4_.1, bf16[192,256]{1,0:T(8,128)(2,1)S(1)} %maximum_select_fusion.2.refs_2_), custom_call_target="tpu_custom_call" | custom-call | flops 1610612736 | bytes 8388608 | tf_op jit(solution)/shard_map/wide_tops/pallas_call | solution.py:134
  17.4 0.0 collective-permute-done.4
  17.5 0.1 maximum_select_fusion.1.refs_8_
  17.5 0.0 collective-permute-done.1.refs_4_
  17.5 0.0 collective-permute-done.5.refs_9_.partner_ref
  17.5 0.0 collective-permute-done.2.refs_5_
  17.6 4.8 %student_front.1 = (f32[96,2048]{1,0:T(8,128)S(1)}, f32[96,2048]{1,0:T(8,128)}) custom-call(s32[1]{0:T(128)} %bitcast.refs_0_.index_ref, f32[1,2048]{1,0:T(1,128)} %bitcast.10, bf16[48,1536]{1,0:T(8,128)(2,1)} %refs_2_.1, bf16[48,1536]{1,0:T(8,128)(2,1)S(1)} %collective-permute-done.refs_3_, bf16[48,1536]{1,0:T(8,128)(2,1)S(1)} %collective-permute-done.1.refs_4_, ...), custom_call_target="tpu_custom_call" | custom-call | flops 704643072 | bytes 3670016 | tf_op jit(solution)/shard_map/student_front/pallas_call | solution.py:572
  22.4 0.6 collective-permute-start.6
  23.0 0.1 collective-permute-start.8
  23.1 4.6 %all-to-all-start = ((f32[32,1,256]{2,1,0:T(1,128)}), f32[32,1,256]{2,1,0:T(1,128)S(1)}, u32[]{:S(2)}, u32[]{:S(2)}) async-start(f32[32,1,256]{2,1,0:T(1,128)} %wide_tops.1.refs_10_), calls=%async_computation | async-start | bytes 65536 | tf_op jit(solution)/shard_map/all_to_all | solution.py:694
  27.7 1.8 %collective-permute-start.16 = (bf16[384,256]{1,0:T(8,128)(2,1)S(1)}, bf16[384,256]{1,0:T(8,128)(2,1)S(1)}, u32[]{:S(2)}, u32[]{:S(2)}) collective-permute-start(bf16[384,256]{1,0:T(8,128)(2,1)S(1)} %maximum_select_fusion.1.refs_8_), channel_id=1, source_target_pairs={{0,4},{4,0},{8,12},{12,8},{16,20},{20,16},{24,28},{28,24},{1,5},{5... | collective-permute-start | bytes 589832 | tf_op jit(solution)/shard_map/ppermute | solution.py:665
  29.5 0.1 pad_add_fusion.1.refs_0_
  29.6 5.3 %all-to-all-done.refs_2_ = f32[32,1,256]{2,1,0:T(1,128)S(1)} async-done(((f32[32,1,256]{2,1,0:T(1,128)}), f32[32,1,256]{2,1,0:T(1,128)S(1)}, u32[]{:S(2)}, u32[]{:S(2)}) %all-to-all-start) | async-done | bytes 32800 | tf_op jit(solution)/shard_map/all_to_all | solution.py:694
  34.9 0.1 reduce
  35.1 0.2 collective-permute-start.9
  35.3 0.0 collective-permute-done.16
  35.3 0.2 maximum_select_fusion.refs_2_
  35.4 0.5 collective-permute-start.17
  35.9 0.0 collective-permute-done.6.core_ref
  35.9 1.2 %collective-permute-start.7 = (f32[48,2048]{1,0:T(8,128)S(1)}, f32[48,2048]{1,0:T(8,128)}, u32[]{:S(2)}, u32[]{:S(2)}) collective-permute-start(f32[48,2048]{1,0:T(8,128)S(1)} %slice_add_fusion.refs_5_), channel_id=1, source_target_pairs={{0,2},{1,3},{2,0},{3,1},{4,6},{5,7},{6,4},{7,5},{8,10},{9,11},{10,... | collective-permute-start | bytes 1179656 | tf_op jit(solution)/shard_map/ppermute | solution.py:665
  37.2 0.1 mul.17
  37.3 0.1 mul.19.refs_4_
  37.4 0.0 collective-permute-done.8.other_ref.refs_6_
  37.4 0.0 collective-permute-done.9.last_ref.refs_7_
  37.4 0.0 collective-permute-done.17.refs_3_
  37.4 6.7 %first_sweep.1 = (bf16[32,16,128]{2,1,0:T(8,128)(2,1)}, bf16[2048,1536]{1,0:T(8,128)(2,1)}) custom-call(s32[2]{0:T(128)S(1)} %pad_add_fusion.1.refs_0_, bf16[16384,256]{1,0:T(8,128)(2,1)} %refs_4_.1, bf16[768,256]{1,0:T(8,128)(2,1)S(1)} %maximum_select_fusion.refs_2_, bf16[768,256]{1,0:T(8,128)(2,1)} %collective-permute-done.17.refs_3_, ...), custom_call_target="tpu_custom_call" | custom-call | flops 1610612736 | bytes 6291456 | tf_op jit(solution)/shard_map/first_sweep/pallas_call | solution.py:399
  44.1 5.2 %all-to-all-start.1 = ((bf16[32,16,128]{2,1,0:T(8,128)(2,1)}), bf16[32,16,128]{2,1,0:T(8,128)(2,1)S(1)}, u32[]{:S(2)}, u32[]{:S(2)}) async-start(bf16[32,16,128]{2,1,0:T(8,128)(2,1)} %get-tuple-element.34), calls=%async_computation.1 | async-start | bytes 262144 | tf_op jit(solution)/shard_map/all_to_all | solution.py:694
  49.4 0.1 pad_add_fusion.refs_0_
  49.5 1.6 %student_middle.1 = (f32[48,256]{1,0:T(8,128)S(1)}, bf16[48,256]{1,0:T(8,128)(2,1)S(1)}, f32[48,128]{1,0:T(8,128)S(1)}) custom-call(s32[1]{0:T(128)} %bitcast.refs_0_.index_ref, f32[96,2048]{1,0:T(8,128)S(1)} %get-tuple-element.24.keep_ref, f32[96,2048]{1,0:T(8,128)S(1)} %collective-permute-done.6.core_ref, f32[48,2048]{1,0:T(8,128)} %collective-permute-done.7.x_ref, ...), custom_call_target="tpu_custom_call" | custom-call | flops 50331648 | bytes 2621440 | tf_op jit(solution)/shard_map/student_middle/pallas_call | solution.py:613
  51.1 1.6 %collective-permute-start.12 = (bf16[48,256]{1,0:T(8,128)(2,1)S(1)}, bf16[48,256]{1,0:T(8,128)(2,1)S(1)}, u32[]{:S(2)}, u32[]{:S(2)}) collective-permute-start(bf16[48,256]{1,0:T(8,128)(2,1)S(1)} %get-tuple-element.28.refs_2_), channel_id=1, source_target_pairs={{0,3},{1,2},{2,1},{3,0},{4,7},{5,6},{6,5},{7,4},{8,11},{9,10},{10,... | collective-permute-start | bytes 73736 | tf_op jit(solution)/shard_map/ppermute | solution.py:665
  52.7 0.4 collective-permute-start.11
  53.1 0.0 collective-permute-start.10
  53.1 4.5 %all-to-all-done.1.refs_1_ = bf16[32,16,128]{2,1,0:T(8,128)(2,1)S(1)} async-done(((bf16[32,16,128]{2,1,0:T(8,128)(2,1)}), bf16[32,16,128]{2,1,0:T(8,128)(2,1)S(1)}, u32[]{:S(2)}, u32[]{:S(2)}) %all-to-all-start.1) | async-done | bytes 131104 | tf_op jit(solution)/shard_map/all_to_all | solution.py:694
  57.6 4.4 %next_sweep.1 = bf16[32,16,128]{2,1,0:T(8,128)(2,1)} custom-call(bf16[2048,1536]{1,0:T(8,128)(2,1)} %get-tuple-element.33.refs_0_, bf16[32,16,128]{2,1,0:T(8,128)(2,1)S(1)} %all-to-all-done.1.refs_1_, bf16[48,256]{1,0:T(8,128)(2,1)S(1)} %get-tuple-element.28.refs_2_), custom_call_target="tpu_custom_call" | custom-call | flops 25165824 | bytes 6291456 | tf_op jit(solution)/shard_map/next_sweep/pallas_call | solution.py:484
  62.0 2.6 %all-to-all-start.2 = ((bf16[32,16,128]{2,1,0:T(8,128)(2,1)}), bf16[32,16,128]{2,1,0:T(8,128)(2,1)S(1)}, u32[]{:S(2)}, u32[]{:S(2)}) async-start(bf16[32,16,128]{2,1,0:T(8,128)(2,1)} %next_sweep.1), calls=%async_computation.2 | async-start | bytes 262144 | tf_op jit(solution)/shard_map/all_to_all | solution.py:694
  64.6 0.0 collective-permute-done.11
  64.6 0.0 collective-permute-done.12
  64.7 5.0 %attract.2.state_ref.refs_2_ = f32[192,512]{1,0:T(8,128)S(1)} custom-call(bf16[192,256]{1,0:T(8,128)(2,1)S(1)} %constant_dynamic-update-slice_fusion.emb_ref, f32[192,512]{1,0:T(8,128)S(1)} %concatenate.32.state_ref, bf16[16384,256]{1,0:T(8,128)(2,1)} %refs_4_.1), custom_call_target="tpu_custom_call" | custom-call | flops 1610612736 | bytes 4194304 | tf_op jit(solution)/shard_map/attract/pallas_call | solution.py:289
  69.7 3.1 %all-to-all-done.2.refs_1_ = bf16[32,16,128]{2,1,0:T(8,128)(2,1)S(1)} async-done(((bf16[32,16,128]{2,1,0:T(8,128)(2,1)}), bf16[32,16,128]{2,1,0:T(8,128)(2,1)S(1)}, u32[]{:S(2)}, u32[]{:S(2)}) %all-to-all-start.2) | async-done | bytes 131104 | tf_op jit(solution)/shard_map/all_to_all | solution.py:694
  72.8 3.7 %last_scales.1 = f32[8,1,2048]{2,1,0:T(1,128)} custom-call(bf16[2048,1536]{1,0:T(8,128)(2,1)} %get-tuple-element.33.refs_0_, bf16[32,16,128]{2,1,0:T(8,128)(2,1)S(1)} %all-to-all-done.2.refs_1_, f32[192,512]{1,0:T(8,128)S(1)} %attract.2.state_ref.refs_2_), custom_call_target="tpu_custom_call" | custom-call | flops 12582912 | bytes 6291456 | tf_op jit(solution)/shard_map/last_scales/pallas_call | solution.py:523
  76.6 3.4 %all-to-all-start.3 = ((f32[8,1,2048]{2,1,0:T(1,128)}), f32[8,1,2048]{2,1,0:T(1,128)S(1)}, u32[]{:S(2)}, u32[]{:S(2)}) async-start(f32[8,1,2048]{2,1,0:T(1,128)} %last_scales.1), calls=%async_computation.3 | async-start | bytes 131072 | tf_op jit(solution)/shard_map/all_to_all | solution.py:694
  79.9 5.1 %attract.3 = (f32[48,512]{1,0:T(8,128)S(1)}, f32[48,512]{1,0:T(8,128)S(1)}, f32[48,512]{1,0:T(8,128)S(1)}, f32[48,512]{1,0:T(8,128)S(1)}) custom-call(bf16[192,256]{1,0:T(8,128)(2,1)S(1)} %constant_dynamic-update-slice_fusion.emb_ref, f32[192,512]{1,0:T(8,128)S(1)} %attract.2.state_ref.refs_2_, bf16[16384,256]{1,0:T(8,128)(2,1)} %refs_4_.1), custom_call_target="tpu_custom_call" | custom-call | flops 1610612736 | bytes 4194304 | tf_op jit(solution)/shard_map/attract/pallas_call | solution.py:289
  85.0 0.3 collective-permute-start.13
  85.3 0.8 collective-permute-start.14
  86.1 0.9 collective-permute-start.15
  87.0 0.0 all-to-all-done.3.refs_3_
  87.0 9.5 %repel.1 = (f32[48,384]{1,0:T(8,128)S(1)}, bf16[48,384]{1,0:T(8,128)(2,1)S(1)}, bf16[48,384]{1,0:T(8,128)(2,1)S(1)}, bf16[48,384]{1,0:T(8,128)(2,1)S(1)}) custom-call(s32[2]{0:T(128)S(1)} %pad_add_fusion.refs_0_, bf16[192,256]{1,0:T(8,128)(2,1)S(1)} %get-tuple-element.23.refs_0_.refs_1_, f32[32,1,256]{2,1,0:T(1,128)S(1)} %all-to-all-done.refs_2_, ...), custom_call_target="tpu_custom_call" | custom-call | flops 3221225472 | bytes 8388608 | tf_op jit(solution)/shard_map/repel/pallas_call | solution.py:208
  96.5 0.5 collective-permute-start.18
  97.0 0.8 collective-permute-start.19
  97.8 0.0 collective-permute-done.13.rest_1_
  97.8 0.7 collective-permute-start.20
  98.4 0.0 collective-permute-done.18.rest_5_
  98.4 2.7 %collective-permute-done.19.rest_6_ = bf16[48,384]{1,0:T(8,128)(2,1)S(1)} collective-permute-done((bf16[48,384]{1,0:T(8,128)(2,1)S(1)}, bf16[48,384]{1,0:T(8,128)(2,1)S(1)}, u32[]{:S(2)}, u32[]{:S(2)}) %collective-permute-start.19) | collective-permute-done | bytes 36896 | tf_op jit(solution)/shard_map/ppermute | solution.py:665
  101.2 0.4 collective-permute-done.20.rest_7_
  101.5 0.8 finish.1
  (19 shorter events, 0.2 us)
Async XLA Ops:
  1.0 6.7 %collective-permute-start.3 = (bf16[96,256]{1,0:T(8,128)(2,1)S(1)}, bf16[96,256]{1,0:T(8,128)(2,1)S(1)}, u32[]{:S(2)}, u32[]{:S(2)}) collective-permute-start(bf16[96,256]{1,0:T(8,128)(2,1)S(1)} %get-tuple-element.22), channel_id=1, source_target_pairs={{0,16},{4,20},{8,24},{12,28},{16,0},{20,4},{24,8},{28,12},{1,17},{... | collective-permute-start | bytes 147464 | tf_op jit(solution)/shard_map/ppermute | solution.py:665
  5.1 6.2 %collective-permute-start = (bf16[48,1536]{1,0:T(8,128)(2,1)}, bf16[48,1536]{1,0:T(8,128)(2,1)S(1)}, u32[]{:S(2)}, u32[]{:S(2)}) collective-permute-start(bf16[48,1536]{1,0:T(8,128)(2,1)} %refs_2_.1), channel_id=1, source_target_pairs={{0,2},{1,3},{2,0},{3,1},{4,6},{5,7},{6,4},{7,5},{8,10},{9,11},{10,... | collective-permute-start | bytes 442376 | tf_op jit(solution)/shard_map/ppermute | solution.py:665
  6.6 10.9 %collective-permute-start.1 = (bf16[48,1536]{1,0:T(8,128)(2,1)}, bf16[48,1536]{1,0:T(8,128)(2,1)S(1)}, u32[]{:S(2)}, u32[]{:S(2)}) collective-permute-start(bf16[48,1536]{1,0:T(8,128)(2,1)} %refs_2_.1), channel_id=1, source_target_pairs={{0,1},{1,0},{2,3},{3,2},{4,5},{5,4},{6,7},{7,6},{8,9},{9,8},{10,11... | collective-permute-start | bytes 442376 | tf_op jit(solution)/shard_map/ppermute | solution.py:665
  6.6 10.9 %collective-permute-start.5 = (bf16[512,256]{1,0:T(8,128)(2,1)}, bf16[512,256]{1,0:T(8,128)(2,1)S(1)}, u32[]{:S(2)}, u32[]{:S(2)}) collective-permute-start(bf16[512,256]{1,0:T(8,128)(2,1)} %own_ref.1), channel_id=1, source_target_pairs={{0,2},{1,3},{2,0},{3,1},{4,6},{5,7},{6,4},{7,5},{8,10},{9,11},{10,... | collective-permute-start | bytes 786440 | tf_op jit(solution)/shard_map/ppermute | solution.py:665
  7.8 9.7 %collective-permute-start.4 = (bf16[192,256]{1,0:T(8,128)(2,1)S(1)}, bf16[192,256]{1,0:T(8,128)(2,1)S(1)}, u32[]{:S(2)}, u32[]{:S(2)}) collective-permute-start(bf16[192,256]{1,0:T(8,128)(2,1)S(1)} %maximum_select_fusion.2.refs_2_), channel_id=1, source_target_pairs={{0,8},{4,12},{8,0},{12,4},{16,24},{20,28},{24,16},{28,20},{1,9},{5... | collective-permute-start | bytes 294920 | tf_op jit(solution)/shard_map/ppermute | solution.py:665
  11.4 6.2 %collective-permute-start.2 = (bf16[48,1536]{1,0:T(8,128)(2,1)S(1)}, bf16[48,1536]{1,0:T(8,128)(2,1)S(1)}, u32[]{:S(2)}, u32[]{:S(2)}) collective-permute-start(bf16[48,1536]{1,0:T(8,128)(2,1)S(1)} %collective-permute-done.refs_3_), channel_id=1, source_target_pairs={{0,1},{1,0},{2,3},{3,2},{4,5},{5,4},{6,7},{7,6},{8,9},{9,8},{10,11... | collective-permute-start | bytes 442376 | tf_op jit(solution)/shard_map/ppermute | solution.py:665
  22.4 13.5 %collective-permute-start.6 = (f32[96,2048]{1,0:T(8,128)}, f32[96,2048]{1,0:T(8,128)S(1)}, u32[]{:S(2)}, u32[]{:S(2)}) collective-permute-start(f32[96,2048]{1,0:T(8,128)} %get-tuple-element.25), channel_id=1, source_target_pairs={{0,1},{1,0},{2,3},{3,2},{4,5},{5,4},{6,7},{7,6},{8,9},{9,8},{10,11... | collective-permute-start | bytes 2359304 | tf_op jit(solution)/shard_map/ppermute | solution.py:665
  23.0 14.4 %collective-permute-start.8 = (bf16[512,256]{1,0:T(8,128)(2,1)}, bf16[512,256]{1,0:T(8,128)(2,1)S(1)}, u32[]{:S(2)}, u32[]{:S(2)}) collective-permute-start(bf16[512,256]{1,0:T(8,128)(2,1)} %own_ref.1), channel_id=1, source_target_pairs={{0,1},{1,0},{2,3},{3,2},{4,5},{5,4},{6,7},{7,6},{8,9},{9,8},{10,11... | collective-permute-start | bytes 786440 | tf_op jit(solution)/shard_map/ppermute | solution.py:665
  23.1 11.9 %all-to-all-start = ((f32[32,1,256]{2,1,0:T(1,128)}), f32[32,1,256]{2,1,0:T(1,128)S(1)}, u32[]{:S(2)}, u32[]{:S(2)}) async-start(f32[32,1,256]{2,1,0:T(1,128)} %wide_tops.1.refs_10_), calls=%async_computation | async-start | bytes 65536 | tf_op jit(solution)/shard_map/all_to_all | solution.py:694
  27.7 7.6 %collective-permute-start.16 = (bf16[384,256]{1,0:T(8,128)(2,1)S(1)}, bf16[384,256]{1,0:T(8,128)(2,1)S(1)}, u32[]{:S(2)}, u32[]{:S(2)}) collective-permute-start(bf16[384,256]{1,0:T(8,128)(2,1)S(1)} %maximum_select_fusion.1.refs_8_), channel_id=1, source_target_pairs={{0,4},{4,0},{8,12},{12,8},{16,20},{20,16},{24,28},{28,24},{1,5},{5... | collective-permute-start | bytes 589832 | tf_op jit(solution)/shard_map/ppermute | solution.py:665
  35.1 2.3 %collective-permute-start.9 = (bf16[512,256]{1,0:T(8,128)(2,1)S(1)}, bf16[512,256]{1,0:T(8,128)(2,1)S(1)}, u32[]{:S(2)}, u32[]{:S(2)}) collective-permute-start(bf16[512,256]{1,0:T(8,128)(2,1)S(1)} %collective-permute-done.5.refs_9_.partner_ref), channel_id=1, source_target_pairs={{0,1},{1,0},{2,3},{3,2},{4,5},{5,4},{6,7},{7,6},{8,9},{9,8},{10,11... | collective-permute-start | bytes 786440 | tf_op jit(solution)/shard_map/ppermute | solution.py:665
  35.4 2.0 %collective-permute-start.17 = (bf16[768,256]{1,0:T(8,128)(2,1)S(1)}, bf16[768,256]{1,0:T(8,128)(2,1)}, u32[]{:S(2)}, u32[]{:S(2)}) collective-permute-start(bf16[768,256]{1,0:T(8,128)(2,1)S(1)} %maximum_select_fusion.refs_2_), channel_id=1, source_target_pairs={{0,1},{1,0},{2,3},{3,2},{4,5},{5,4},{6,7},{7,6},{8,9},{9,8},{10,11... | collective-permute-start | bytes 1179656 | tf_op jit(solution)/shard_map/ppermute | solution.py:665
  35.9 13.5 %collective-permute-start.7 = (f32[48,2048]{1,0:T(8,128)S(1)}, f32[48,2048]{1,0:T(8,128)}, u32[]{:S(2)}, u32[]{:S(2)}) collective-permute-start(f32[48,2048]{1,0:T(8,128)S(1)} %slice_add_fusion.refs_5_), channel_id=1, source_target_pairs={{0,2},{1,3},{2,0},{3,1},{4,6},{5,7},{6,4},{7,5},{8,10},{9,11},{10,... | collective-permute-start | bytes 1179656 | tf_op jit(solution)/shard_map/ppermute | solution.py:665
  44.1 13.5 %all-to-all-start.1 = ((bf16[32,16,128]{2,1,0:T(8,128)(2,1)}), bf16[32,16,128]{2,1,0:T(8,128)(2,1)S(1)}, u32[]{:S(2)}, u32[]{:S(2)}) async-start(bf16[32,16,128]{2,1,0:T(8,128)(2,1)} %get-tuple-element.34), calls=%async_computation.1 | async-start | bytes 262144 | tf_op jit(solution)/shard_map/all_to_all | solution.py:694
  51.1 13.5 %collective-permute-start.12 = (bf16[48,256]{1,0:T(8,128)(2,1)S(1)}, bf16[48,256]{1,0:T(8,128)(2,1)S(1)}, u32[]{:S(2)}, u32[]{:S(2)}) collective-permute-start(bf16[48,256]{1,0:T(8,128)(2,1)S(1)} %get-tuple-element.28.refs_2_), channel_id=1, source_target_pairs={{0,3},{1,2},{2,1},{3,0},{4,7},{5,6},{6,5},{7,4},{8,11},{9,10},{10,... | collective-permute-start | bytes 73736 | tf_op jit(solution)/shard_map/ppermute | solution.py:665
  52.7 11.9 %collective-permute-start.11 = (bf16[48,256]{1,0:T(8,128)(2,1)S(1)}, bf16[48,256]{1,0:T(8,128)(2,1)S(1)}, u32[]{:S(2)}, u32[]{:S(2)}) collective-permute-start(bf16[48,256]{1,0:T(8,128)(2,1)S(1)} %get-tuple-element.28.refs_2_), channel_id=1, source_target_pairs={{0,2},{1,3},{2,0},{3,1},{4,6},{5,7},{6,4},{7,5},{8,10},{9,11},{10,... | collective-permute-start | bytes 73736 | tf_op jit(solution)/shard_map/ppermute | solution.py:665
  53.1 11.5 %collective-permute-start.10 = (bf16[48,256]{1,0:T(8,128)(2,1)S(1)}, bf16[48,256]{1,0:T(8,128)(2,1)S(1)}, u32[]{:S(2)}, u32[]{:S(2)}) collective-permute-start(bf16[48,256]{1,0:T(8,128)(2,1)S(1)} %get-tuple-element.28.refs_2_), channel_id=1, source_target_pairs={{0,1},{1,0},{2,3},{3,2},{4,5},{5,4},{6,7},{7,6},{8,9},{9,8},{10,11... | collective-permute-start | bytes 73736 | tf_op jit(solution)/shard_map/ppermute | solution.py:665
  62.0 10.8 %all-to-all-start.2 = ((bf16[32,16,128]{2,1,0:T(8,128)(2,1)}), bf16[32,16,128]{2,1,0:T(8,128)(2,1)S(1)}, u32[]{:S(2)}, u32[]{:S(2)}) async-start(bf16[32,16,128]{2,1,0:T(8,128)(2,1)} %next_sweep.1), calls=%async_computation.2 | async-start | bytes 262144 | tf_op jit(solution)/shard_map/all_to_all | solution.py:694
  76.6 10.4 %all-to-all-start.3 = ((f32[8,1,2048]{2,1,0:T(1,128)}), f32[8,1,2048]{2,1,0:T(1,128)S(1)}, u32[]{:S(2)}, u32[]{:S(2)}) async-start(f32[8,1,2048]{2,1,0:T(1,128)} %last_scales.1), calls=%async_computation.3 | async-start | bytes 131072 | tf_op jit(solution)/shard_map/all_to_all | solution.py:694
  85.0 12.7 %collective-permute-start.13 = (f32[48,512]{1,0:T(8,128)S(1)}, f32[48,512]{1,0:T(8,128)S(1)}, u32[]{:S(2)}, u32[]{:S(2)}) collective-permute-start(f32[48,512]{1,0:T(8,128)S(1)} %get-tuple-element.30), channel_id=1, source_target_pairs={{0,1},{1,0},{2,3},{3,2},{4,5},{5,4},{6,7},{7,6},{8,9},{9,8},{10,11... | collective-permute-start | bytes 294920 | tf_op jit(solution)/shard_map/ppermute | solution.py:665
  85.3 13.1 %collective-permute-start.14 = (f32[48,512]{1,0:T(8,128)S(1)}, f32[48,512]{1,0:T(8,128)S(1)}, u32[]{:S(2)}, u32[]{:S(2)}) collective-permute-start(f32[48,512]{1,0:T(8,128)S(1)} %get-tuple-element.31), channel_id=1, source_target_pairs={{0,2},{1,3},{2,0},{3,1},{4,6},{5,7},{6,4},{7,5},{8,10},{9,11},{10,... | collective-permute-start | bytes 294920 | tf_op jit(solution)/shard_map/ppermute | solution.py:665
  86.1 12.4 %collective-permute-start.15 = (f32[48,512]{1,0:T(8,128)S(1)}, f32[48,512]{1,0:T(8,128)S(1)}, u32[]{:S(2)}, u32[]{:S(2)}) collective-permute-start(f32[48,512]{1,0:T(8,128)S(1)} %get-tuple-element.32), channel_id=1, source_target_pairs={{0,3},{1,2},{2,1},{3,0},{4,7},{5,6},{6,5},{7,4},{8,11},{9,10},{10,... | collective-permute-start | bytes 294920 | tf_op jit(solution)/shard_map/ppermute | solution.py:665
  96.5 2.0 %collective-permute-start.18 = (bf16[48,384]{1,0:T(8,128)(2,1)S(1)}, bf16[48,384]{1,0:T(8,128)(2,1)S(1)}, u32[]{:S(2)}, u32[]{:S(2)}) collective-permute-start(bf16[48,384]{1,0:T(8,128)(2,1)S(1)} %get-tuple-element.36), channel_id=1, source_target_pairs={{0,1},{1,0},{2,3},{3,2},{4,5},{5,4},{6,7},{7,6},{8,9},{9,8},{10,11... | collective-permute-start | bytes 110600 | tf_op jit(solution)/shard_map/ppermute | solution.py:665
  97.0 4.2 %collective-permute-start.19 = (bf16[48,384]{1,0:T(8,128)(2,1)S(1)}, bf16[48,384]{1,0:T(8,128)(2,1)S(1)}, u32[]{:S(2)}, u32[]{:S(2)}) collective-permute-start(bf16[48,384]{1,0:T(8,128)(2,1)S(1)} %get-tuple-element.37), channel_id=1, source_target_pairs={{0,2},{1,3},{2,0},{3,1},{4,6},{5,7},{6,4},{7,5},{8,10},{9,11},{10,... | collective-permute-start | bytes 110600 | tf_op jit(solution)/shard_map/ppermute | solution.py:665
  97.8 3.8 %collective-permute-start.20 = (bf16[48,384]{1,0:T(8,128)(2,1)S(1)}, bf16[48,384]{1,0:T(8,128)(2,1)S(1)}, u32[]{:S(2)}, u32[]{:S(2)}) collective-permute-start(bf16[48,384]{1,0:T(8,128)(2,1)S(1)} %get-tuple-element.38), channel_id=1, source_target_pairs={{0,3},{1,2},{2,1},{3,0},{4,7},{5,6},{6,5},{7,4},{8,11},{9,10},{10,... | collective-permute-start | bytes 110600 | tf_op jit(solution)/shard_map/ppermute | solution.py:665

commit v16 on v15

--- a/solution.py
+++ b/solution.py
@@ -687,7 +687,8 @@
 
 
 def send_blocks(blocks):
-    return [blocks[0]] + [swap(block, "proto", flip) for flip, block in enumerate(blocks) if flip]
+    flips = list(range(len(blocks) - 1, 0, -1))
+    return [blocks[0]] + [swap(blocks[flip], "proto", flip) for flip in flips]
 
 
 def all_to_all(copies, axes):
@@ -720,8 +721,8 @@
     rows = [crops, crops_x, swap(crops, "proto", 1), swap(crops_x, "proto", 1)]
     third_x = swap(w_third, "proto", 2)
     thirds = [w_third, third_x, swap(w_third, "proto", 1), swap(third_x, "proto", 1)]
-    top_copies = wide_tops(own_unit, protos, (stages[1],), devices, 8)
-    keep, give = student_front(proto_ref, b_first, rows, w_first, w_second, (stages[2], third_x, top_copies))
+    top_copies = wide_tops(own_unit, protos, (stages[2],), devices, 8)
+    keep, give = student_front(proto_ref, b_first, rows, w_first, w_second, (mine, third_x, top_copies))
     all_tops = all_to_all(top_copies, BOTH)
     tops = jnp.max(all_tops.reshape(batch_size, proto_size, 256)[:, :, :group_rows], axis=1)
     tops = bit_reversed(tops, batch_size).reshape(batch_size, 2, group_rows // 2)
@@ -737,8 +738,9 @@
     empty = jnp.concatenate(
         [jnp.zeros((group_rows, width + 128), jnp.float32), jnp.full((group_rows, 128), -1e30, jnp.float32)], axis=1
     )
-    (state,) = attract(student_emb, empty, protos, 0, count // 2, 4, 1)
-    slots = attract(student_emb, state, protos, count // 2, count // 2, 4, proto_size)
+    eighth = count // 8
+    (state,) = attract(student_emb, empty, protos, 0, 5 * eighth, 5, 1)
+    slots = attract(student_emb, state, protos, 5 * eighth, 3 * eighth, 3, proto_size)
     attract_parts = send_blocks(slots)
 
     copies, weights = first_sweep(thin_ref, protos, mine, other, base, (x_sent, *thirds[2:]), devices, thin, protos_total)

time: 103 us -> 109 us (1.058)
  waiting for transfers between devices: 18.8 us -> 23 us
  local copies, waits for them, and re-layouts: 0.27 us -> 4.2 us
  starting transfers between devices: 33.6 us -> 31.9 us
    mul x5, local copies, waits for them, and re-layouts: 0.2 us -> 3.46 us  [body(): jnp.transpose(tops, (1, 0, 2)).reshape(1, crops_total) * -teacher_rate]
    ppermute x21, waiting for transfers between devices: 5.87 us -> 8.24 us  [swap(): lax.ppermute(values, axis, [(i, i ^ flip) for i in range(lax.axis_size(ax...]
    all_to_all x4, starting transfers between devices: 15.8 us -> 13.8 us  [all_to_all(): return lax.all_to_all(copies, axes, 0, 0, tiled=True)]
    all_to_all x4, waiting for transfers between devices: 12.9 us -> 14.7 us  [all_to_all(): return lax.all_to_all(copies, axes, 0, 0, tiled=True)]
  transfers between devices with their start and end apart: 25 -> 25, of which waited for: 7 -> 9; matrix products, arithmetic and copies ran while one was open for 1% -> 4% of each run, Pallas kernels for 38% -> 35%
where the time goes in v16:
time: 109 us
  Pallas kernels  48.1 us (44%)
  starting transfers between devices  31.9 us (29%)
  waiting for transfers between devices  23 us (21%)
  local copies, waits for them, and re-layouts  4.2 us (4%)
  other arithmetic  1.13 us (1%)
    ppermute x21, starting transfers between devices, swap(): lax.ppermute(values, axis, [(i, i ^ flip) for i in range(lax.axis_size(ax...  18.1 us
    all_to_all x4, waiting for transfers between devices, all_to_all(): return lax.all_to_all(copies, axes, 0, 0, tiled=True)  14.7 us
    all_to_all x4, starting transfers between devices, all_to_all(): return lax.all_to_all(copies, axes, 0, 0, tiled=True)  13.8 us
    pallas_call x2, Pallas kernels, attract(): pl.pallas_call(functools.partial(attract_kernel, first_row, outputs > 1),...  10.1 us
    pallas_call x1, Pallas kernels, repel(): pl.pallas_call(skipping(functools.partial(repel_kernel, proto_size), 5, l...  9.45 us
    ppermute x21, waiting for transfers between devices, swap(): lax.ppermute(values, axis, [(i, i ^ flip) for i in range(lax.axis_size(ax...  8.24 us
    pallas_call x1, Pallas kernels, first_sweep(): pl.pallas_call(skipping(functools.partial(first_sweep_kernel, chunk, prot...  6.08 us
    pallas_call x1, Pallas kernels, wide_tops(): pl.pallas_call(skipping(wide_tops_kernel, 2, len(order)), in_specs=[whole...  6.07 us
  transfers between devices with their start and end apart: 25, of which 9 were waited for; matrix products, arithmetic and copies ran while one was open for 4% of the time, Pallas kernels for 35%

profile of v16, /device:TPU:0, one launch (start us, length us, event | category | flops | bytes accessed | tf_op | source)
XLA Modules:
  0.0 108.6 jit_solution(13660510843243568457)
XLA Ops:
  0.0 1.0 teacher_units.1
  1.0 4.1 %collective-permute-start.3 = (bf16[96,256]{1,0:T(8,128)(2,1)S(1)}, bf16[96,256]{1,0:T(8,128)(2,1)S(1)}, u32[]{:S(2)}, u32[]{:S(2)}) collective-permute-start(bf16[96,256]{1,0:T(8,128)(2,1)S(1)} %get-tuple-element.22), channel_id=1, source_target_pairs={{0,16},{4,20},{8,24},{12,28},{16,0},{20,4},{24,8},{28,12},{1,17},{... | collective-permute-start | bytes 147464 | tf_op jit(solution)/shard_map/ppermute | solution.py:665
  5.1 2.6 %collective-permute-done.3 = bf16[96,256]{1,0:T(8,128)(2,1)S(1)} collective-permute-done((bf16[96,256]{1,0:T(8,128)(2,1)S(1)}, bf16[96,256]{1,0:T(8,128)(2,1)S(1)}, u32[]{:S(2)}, u32[]{:S(2)}) %collective-permute-start.3) | collective-permute-done | bytes 49184 | tf_op jit(solution)/shard_map/ppermute | solution.py:665
  7.8 1.4 %collective-permute-start.4 = (bf16[192,256]{1,0:T(8,128)(2,1)S(1)}, bf16[192,256]{1,0:T(8,128)(2,1)S(1)}, u32[]{:S(2)}, u32[]{:S(2)}) collective-permute-start(bf16[192,256]{1,0:T(8,128)(2,1)S(1)} %maximum_select_fusion.2), channel_id=1, source_target_pairs={{0,8},{4,12},{8,0},{12,4},{16,24},{20,28},{24,16},{28,20},{1,9},{5... | collective-permute-start | bytes 294920 | tf_op jit(solution)/shard_map/ppermute | solution.py:665
  9.2 1.5 %collective-permute-start = (bf16[48,1536]{1,0:T(8,128)(2,1)}, bf16[48,1536]{1,0:T(8,128)(2,1)S(1)}, u32[]{:S(2)}, u32[]{:S(2)}) collective-permute-start(bf16[48,1536]{1,0:T(8,128)(2,1)} %refs_2_.1), channel_id=1, source_target_pairs={{0,2},{1,3},{2,0},{3,1},{4,6},{5,7},{6,4},{7,5},{8,10},{9,11},{10,... | collective-permute-start | bytes 442376 | tf_op jit(solution)/shard_map/ppermute | solution.py:665
  10.7 1.7 %collective-permute-done.4 = bf16[192,256]{1,0:T(8,128)(2,1)S(1)} collective-permute-done((bf16[192,256]{1,0:T(8,128)(2,1)S(1)}, bf16[192,256]{1,0:T(8,128)(2,1)S(1)}, u32[]{:S(2)}, u32[]{:S(2)}) %collective-permute-start.4) | collective-permute-done | bytes 98336 | tf_op jit(solution)/shard_map/ppermute | solution.py:665
  12.4 0.1 maximum_select_fusion.1.refs_2_
  12.5 1.8 %collective-permute-start.5 = (bf16[384,256]{1,0:T(8,128)(2,1)S(1)}, bf16[384,256]{1,0:T(8,128)(2,1)S(1)}, u32[]{:S(2)}, u32[]{:S(2)}) collective-permute-start(bf16[384,256]{1,0:T(8,128)(2,1)S(1)} %maximum_select_fusion.1.refs_2_), channel_id=1, source_target_pairs={{0,4},{4,0},{8,12},{12,8},{16,20},{20,16},{24,28},{28,24},{1,5},{5... | collective-permute-start | bytes 589832 | tf_op jit(solution)/shard_map/ppermute | solution.py:665
  14.3 0.0 collective-permute-start.1
  14.3 1.5 %collective-permute-start.6 = (bf16[512,256]{1,0:T(8,128)(2,1)}, bf16[512,256]{1,0:T(8,128)(2,1)S(1)}, u32[]{:S(2)}, u32[]{:S(2)}) collective-permute-start(bf16[512,256]{1,0:T(8,128)(2,1)} %own_ref.1), channel_id=1, source_target_pairs={{0,2},{1,3},{2,0},{3,1},{4,6},{5,7},{6,4},{7,5},{8,10},{9,11},{10,... | collective-permute-start | bytes 786440 | tf_op jit(solution)/shard_map/ppermute | solution.py:665
  15.8 0.2 collective-permute-start.2
  16.0 6.1 %wide_tops.1.refs_10_ = f32[32,1,256]{2,1,0:T(1,128)} custom-call(bf16[192,256]{1,0:T(8,128)(2,1)S(1)} %get-tuple-element.23.refs_0_.refs_1_, bf16[16384,256]{1,0:T(8,128)(2,1)} %refs_4_.1, bf16[384,256]{1,0:T(8,128)(2,1)S(1)} %maximum_select_fusion.1.refs_2_), custom_call_target="tpu_custom_call" | custom-call | flops 1610612736 | bytes 8388608 | tf_op jit(solution)/shard_map/wide_tops/pallas_call | solution.py:134
  22.1 0.2 maximum_select_fusion.refs_8_.refs_2_
  22.3 0.0 collective-permute-done.1.refs_4_
  22.3 0.9 collective-permute-done.6.refs_9_.partner_ref
  23.2 4.9 %student_front.1 = (f32[96,2048]{1,0:T(8,128)S(1)}, f32[96,2048]{1,0:T(8,128)}) custom-call(s32[1]{0:T(128)} %bitcast.refs_0_.index_ref, f32[1,2048]{1,0:T(1,128)} %bitcast.10, bf16[48,1536]{1,0:T(8,128)(2,1)} %refs_2_.1, bf16[48,1536]{1,0:T(8,128)(2,1)S(1)} %collective-permute-done.refs_3_, bf16[48,1536]{1,0:T(8,128)(2,1)S(1)} %collective-permute-done.1.refs_4_, ...), custom_call_target="tpu_custom_call" | custom-call | flops 704643072 | bytes 3670016 | tf_op jit(solution)/shard_map/student_front/pallas_call | solution.py:572
  28.1 0.1 collective-permute-start.7
  28.2 0.5 collective-permute-start.9
  28.7 4.9 %all-to-all-start = ((f32[32,1,256]{2,1,0:T(1,128)}), f32[32,1,256]{2,1,0:T(1,128)S(1)}, u32[]{:S(2)}, u32[]{:S(2)}) async-start(f32[32,1,256]{2,1,0:T(1,128)} %wide_tops.1.refs_10_), calls=%async_computation | async-start | bytes 65536 | tf_op jit(solution)/shard_map/all_to_all | solution.py:695
  33.6 0.1 pad_add_fusion.1.refs_0_
  33.7 7.2 %all-to-all-done.refs_2_ = f32[32,1,256]{2,1,0:T(1,128)S(1)} async-done(((f32[32,1,256]{2,1,0:T(1,128)}), f32[32,1,256]{2,1,0:T(1,128)S(1)}, u32[]{:S(2)}, u32[]{:S(2)}) %all-to-all-start) | async-done | bytes 32800 | tf_op jit(solution)/shard_map/all_to_all | solution.py:695
  40.8 0.1 reduce
  41.0 0.2 collective-permute-start.10
  41.1 0.4 collective-permute-start.17
  41.5 0.0 collective-permute-done.7.core_ref
  41.6 0.6 collective-permute-start.8
  42.2 0.6 broadcast_multiply_fusion
  42.8 0.7 reshape.46
  43.5 0.6 copy.11
  44.1 0.8 mul.17
  44.8 0.6 copy.12
  45.4 0.8 mul.19.refs_4_
  46.2 0.0 collective-permute-done.10.last_ref.refs_7_
  46.2 6.1 %first_sweep.1 = (bf16[32,16,128]{2,1,0:T(8,128)(2,1)S(1)}, bf16[2048,1536]{1,0:T(8,128)(2,1)}) custom-call(s32[2]{0:T(128)S(1)} %pad_add_fusion.1.refs_0_, bf16[16384,256]{1,0:T(8,128)(2,1)} %refs_4_.1, bf16[768,256]{1,0:T(8,128)(2,1)S(1)} %maximum_select_fusion.refs_8_.refs_2_, bf16[768,256]{1,0:T(8,128)(2,1)} %collective-permute-done.17.refs_3_, ...), custom_call_target="tpu_custom_call" | custom-call | flops 1610612736 | bytes 6291456 | tf_op jit(solution)/shard_map/first_sweep/pallas_call | solution.py:399
  52.3 0.7 copy-done
  53.0 2.6 %all-to-all-start.1 = ((bf16[32,16,128]{2,1,0:T(8,128)(2,1)}), bf16[32,16,128]{2,1,0:T(8,128)(2,1)S(1)}, u32[]{:S(2)}, u32[]{:S(2)}) async-start(bf16[32,16,128]{2,1,0:T(8,128)(2,1)} %copy-done), calls=%async_computation.1 | async-start | bytes 262144 | tf_op jit(solution)/shard_map/all_to_all | solution.py:695
  55.6 0.0 collective-permute-done.8.x_ref
  55.6 1.5 %student_middle.1 = (f32[48,256]{1,0:T(8,128)S(1)}, bf16[48,256]{1,0:T(8,128)(2,1)S(1)}, f32[48,128]{1,0:T(8,128)S(1)}) custom-call(s32[1]{0:T(128)} %bitcast.refs_0_.index_ref, f32[96,2048]{1,0:T(8,128)S(1)} %get-tuple-element.24.keep_ref, f32[96,2048]{1,0:T(8,128)S(1)} %collective-permute-done.7.core_ref, f32[48,2048]{1,0:T(8,128)S(1)} %collective-permute-done.8.x_ref, ...), custom_call_target="tpu_custom_call" | custom-call | flops 50331648 | bytes 2621440 | tf_op jit(solution)/shard_map/student_middle/pallas_call | solution.py:613
  57.1 1.5 %collective-permute-start.13 = (bf16[48,256]{1,0:T(8,128)(2,1)S(1)}, bf16[48,256]{1,0:T(8,128)(2,1)S(1)}, u32[]{:S(2)}, u32[]{:S(2)}) collective-permute-start(bf16[48,256]{1,0:T(8,128)(2,1)S(1)} %get-tuple-element.28.refs_2_), channel_id=1, source_target_pairs={{0,3},{1,2},{2,1},{3,0},{4,7},{5,6},{6,5},{7,4},{8,11},{9,10},{10,... | collective-permute-start | bytes 73736 | tf_op jit(solution)/shard_map/ppermute | solution.py:665
  58.6 0.4 collective-permute-start.12
  58.9 0.1 collective-permute-start.11
  59.1 4.7 %all-to-all-done.1.refs_1_ = bf16[32,16,128]{2,1,0:T(8,128)(2,1)S(1)} async-done(((bf16[32,16,128]{2,1,0:T(8,128)(2,1)}), bf16[32,16,128]{2,1,0:T(8,128)(2,1)S(1)}, u32[]{:S(2)}, u32[]{:S(2)}) %all-to-all-start.1) | async-done | bytes 131104 | tf_op jit(solution)/shard_map/all_to_all | solution.py:695
  63.8 4.4 %next_sweep.1 = bf16[32,16,128]{2,1,0:T(8,128)(2,1)} custom-call(bf16[2048,1536]{1,0:T(8,128)(2,1)} %get-tuple-element.33.refs_0_, bf16[32,16,128]{2,1,0:T(8,128)(2,1)S(1)} %all-to-all-done.1.refs_1_, bf16[48,256]{1,0:T(8,128)(2,1)S(1)} %get-tuple-element.28.refs_2_), custom_call_target="tpu_custom_call" | custom-call | flops 25165824 | bytes 6291456 | tf_op jit(solution)/shard_map/next_sweep/pallas_call | solution.py:484
  68.2 2.6 %all-to-all-start.2 = ((bf16[32,16,128]{2,1,0:T(8,128)(2,1)}), bf16[32,16,128]{2,1,0:T(8,128)(2,1)S(1)}, u32[]{:S(2)}, u32[]{:S(2)}) async-start(bf16[32,16,128]{2,1,0:T(8,128)(2,1)} %next_sweep.1), calls=%async_computation.2 | async-start | bytes 262144 | tf_op jit(solution)/shard_map/all_to_all | solution.py:695
  70.8 0.0 collective-permute-done.12
  70.8 0.0 collective-permute-done.13
  70.9 6.0 %attract.2.state_ref.refs_2_ = f32[192,512]{1,0:T(8,128)S(1)} custom-call(bf16[192,256]{1,0:T(8,128)(2,1)S(1)} %constant_dynamic-update-slice_fusion.emb_ref, f32[192,512]{1,0:T(8,128)S(1)} %concatenate.34.state_ref, bf16[16384,256]{1,0:T(8,128)(2,1)} %refs_4_.1), custom_call_target="tpu_custom_call" | custom-call | flops 2013265920 | bytes 5242880 | tf_op jit(solution)/shard_map/attract/pallas_call | solution.py:289
  76.9 0.0 copy-start.2
  76.9 2.1 %all-to-all-done.2.refs_1_ = bf16[32,16,128]{2,1,0:T(8,128)(2,1)S(1)} async-done(((bf16[32,16,128]{2,1,0:T(8,128)(2,1)}), bf16[32,16,128]{2,1,0:T(8,128)(2,1)S(1)}, u32[]{:S(2)}, u32[]{:S(2)}) %all-to-all-start.2) | async-done | bytes 131104 | tf_op jit(solution)/shard_map/all_to_all | solution.py:695
  79.0 3.8 %last_scales.1 = f32[8,1,2048]{2,1,0:T(1,128)} custom-call(bf16[2048,1536]{1,0:T(8,128)(2,1)} %get-tuple-element.33.refs_0_, bf16[32,16,128]{2,1,0:T(8,128)(2,1)S(1)} %all-to-all-done.2.refs_1_, f32[192,512]{1,0:T(8,128)S(1)} %attract.2.state_ref.refs_2_), custom_call_target="tpu_custom_call" | custom-call | flops 12582912 | bytes 6291456 | tf_op jit(solution)/shard_map/last_scales/pallas_call | solution.py:523
  82.8 3.8 %all-to-all-start.3 = ((f32[8,1,2048]{2,1,0:T(1,128)}), f32[8,1,2048]{2,1,0:T(1,128)S(1)}, u32[]{:S(2)}, u32[]{:S(2)}) async-start(f32[8,1,2048]{2,1,0:T(1,128)} %last_scales.1), calls=%async_computation.3 | async-start | bytes 131072 | tf_op jit(solution)/shard_map/all_to_all | solution.py:695
  86.6 0.1 pad_add_fusion.refs_0_
  86.6 4.2 %attract.3 = (f32[48,512]{1,0:T(8,128)S(1)}, f32[48,512]{1,0:T(8,128)S(1)}, f32[48,512]{1,0:T(8,128)S(1)}, f32[48,512]{1,0:T(8,128)S(1)}) custom-call(bf16[192,256]{1,0:T(8,128)(2,1)S(1)} %constant_dynamic-update-slice_fusion.emb_ref, f32[192,512]{1,0:T(8,128)S(1)} %attract.2.state_ref.refs_2_, bf16[16384,256]{1,0:T(8,128)(2,1)} %refs_4_.1), custom_call_target="tpu_custom_call" | custom-call | flops 1207959552 | bytes 3145728 | tf_op jit(solution)/shard_map/attract/pallas_call | solution.py:289
  90.8 1.0 collective-permute-start.14
  91.8 0.6 collective-permute-start.15
  92.4 0.3 collective-permute-start.16
  92.7 0.7 all-to-all-done.3.refs_3_
  93.5 9.5 %repel.1 = (f32[48,384]{1,0:T(8,128)S(1)}, bf16[48,384]{1,0:T(8,128)(2,1)S(1)}, bf16[48,384]{1,0:T(8,128)(2,1)S(1)}, bf16[48,384]{1,0:T(8,128)(2,1)S(1)}) custom-call(s32[2]{0:T(128)S(1)} %pad_add_fusion.refs_0_, bf16[192,256]{1,0:T(8,128)(2,1)S(1)} %copy-done.4, f32[32,1,256]{2,1,0:T(1,128)S(1)} %copy-done.2, f32[8,1,2048]{2,1,0:T(1,128)S(1)} %all-to-all-done.3.refs_3_, ...), custom_call_target="tpu_custom_call" | custom-call | flops 3221225472 | bytes 8388608 | tf_op jit(solution)/shard_map/repel/pallas_call | solution.py:208
  102.9 0.6 collective-permute-start.18
  103.5 1.0 collective-permute-start.19
  104.5 0.3 collective-permute-start.20
  104.9 1.9 %collective-permute-done.18.rest_5_ = bf16[48,384]{1,0:T(8,128)(2,1)S(1)} collective-permute-done((bf16[48,384]{1,0:T(8,128)(2,1)S(1)}, bf16[48,384]{1,0:T(8,128)(2,1)S(1)}, u32[]{:S(2)}, u32[]{:S(2)}) %collective-permute-start.18) | collective-permute-done | bytes 36896 | tf_op jit(solution)/shard_map/ppermute | solution.py:665
  106.7 1.0 collective-permute-done.19.rest_6_
  107.8 0.8 finish.1
  (29 shorter events, 0.2 us)
Async XLA Ops:
  1.0 21.1 %copy-start.3 = (bf16[192,256]{1,0:T(8,128)(2,1)}, bf16[192,256]{1,0:T(8,128)(2,1)S(1)}, u32[]{:S(2)}) copy-start(bf16[192,256]{1,0:T(8,128)(2,1)S(1)} %get-tuple-element.23.refs_0_.refs_1_) | copy-start | bytes 294916
  1.0 6.7 %collective-permute-start.3 = (bf16[96,256]{1,0:T(8,128)(2,1)S(1)}, bf16[96,256]{1,0:T(8,128)(2,1)S(1)}, u32[]{:S(2)}, u32[]{:S(2)}) collective-permute-start(bf16[96,256]{1,0:T(8,128)(2,1)S(1)} %get-tuple-element.22), channel_id=1, source_target_pairs={{0,16},{4,20},{8,24},{12,28},{16,0},{20,4},{24,8},{28,12},{1,17},{... | collective-permute-start | bytes 147464 | tf_op jit(solution)/shard_map/ppermute | solution.py:665
  7.8 4.7 %collective-permute-start.4 = (bf16[192,256]{1,0:T(8,128)(2,1)S(1)}, bf16[192,256]{1,0:T(8,128)(2,1)S(1)}, u32[]{:S(2)}, u32[]{:S(2)}) collective-permute-start(bf16[192,256]{1,0:T(8,128)(2,1)S(1)} %maximum_select_fusion.2), channel_id=1, source_target_pairs={{0,8},{4,12},{8,0},{12,4},{16,24},{20,28},{24,16},{28,20},{1,9},{5... | collective-permute-start | bytes 294920 | tf_op jit(solution)/shard_map/ppermute | solution.py:665
  9.2 6.6 %collective-permute-start = (bf16[48,1536]{1,0:T(8,128)(2,1)}, bf16[48,1536]{1,0:T(8,128)(2,1)S(1)}, u32[]{:S(2)}, u32[]{:S(2)}) collective-permute-start(bf16[48,1536]{1,0:T(8,128)(2,1)} %refs_2_.1), channel_id=1, source_target_pairs={{0,2},{1,3},{2,0},{3,1},{4,6},{5,7},{6,4},{7,5},{8,10},{9,11},{10,... | collective-permute-start | bytes 442376 | tf_op jit(solution)/shard_map/ppermute | solution.py:665
  12.5 9.6 %collective-permute-start.5 = (bf16[384,256]{1,0:T(8,128)(2,1)S(1)}, bf16[384,256]{1,0:T(8,128)(2,1)S(1)}, u32[]{:S(2)}, u32[]{:S(2)}) collective-permute-start(bf16[384,256]{1,0:T(8,128)(2,1)S(1)} %maximum_select_fusion.1.refs_2_), channel_id=1, source_target_pairs={{0,4},{4,0},{8,12},{12,8},{16,20},{20,16},{24,28},{28,24},{1,5},{5... | collective-permute-start | bytes 589832 | tf_op jit(solution)/shard_map/ppermute | solution.py:665
  14.3 8.0 %collective-permute-start.1 = (bf16[48,1536]{1,0:T(8,128)(2,1)}, bf16[48,1536]{1,0:T(8,128)(2,1)S(1)}, u32[]{:S(2)}, u32[]{:S(2)}) collective-permute-start(bf16[48,1536]{1,0:T(8,128)(2,1)} %refs_2_.1), channel_id=1, source_target_pairs={{0,1},{1,0},{2,3},{3,2},{4,5},{5,4},{6,7},{7,6},{8,9},{9,8},{10,11... | collective-permute-start | bytes 442376 | tf_op jit(solution)/shard_map/ppermute | solution.py:665
  14.3 8.9 %collective-permute-start.6 = (bf16[512,256]{1,0:T(8,128)(2,1)}, bf16[512,256]{1,0:T(8,128)(2,1)S(1)}, u32[]{:S(2)}, u32[]{:S(2)}) collective-permute-start(bf16[512,256]{1,0:T(8,128)(2,1)} %own_ref.1), channel_id=1, source_target_pairs={{0,2},{1,3},{2,0},{3,1},{4,6},{5,7},{6,4},{7,5},{8,10},{9,11},{10,... | collective-permute-start | bytes 786440 | tf_op jit(solution)/shard_map/ppermute | solution.py:665
  15.8 7.4 %collective-permute-start.2 = (bf16[48,1536]{1,0:T(8,128)(2,1)S(1)}, bf16[48,1536]{1,0:T(8,128)(2,1)S(1)}, u32[]{:S(2)}, u32[]{:S(2)}) collective-permute-start(bf16[48,1536]{1,0:T(8,128)(2,1)S(1)} %collective-permute-done.refs_3_), channel_id=1, source_target_pairs={{0,1},{1,0},{2,3},{3,2},{4,5},{5,4},{6,7},{7,6},{8,9},{9,8},{10,11... | collective-permute-start | bytes 442376 | tf_op jit(solution)/shard_map/ppermute | solution.py:665
  28.1 13.4 %collective-permute-start.7 = (f32[96,2048]{1,0:T(8,128)}, f32[96,2048]{1,0:T(8,128)S(1)}, u32[]{:S(2)}, u32[]{:S(2)}) collective-permute-start(f32[96,2048]{1,0:T(8,128)} %get-tuple-element.25), channel_id=1, source_target_pairs={{0,1},{1,0},{2,3},{3,2},{4,5},{5,4},{6,7},{7,6},{8,9},{9,8},{10,11... | collective-permute-start | bytes 2359304 | tf_op jit(solution)/shard_map/ppermute | solution.py:665
  28.2 18.0 %collective-permute-start.9 = (bf16[512,256]{1,0:T(8,128)(2,1)}, bf16[512,256]{1,0:T(8,128)(2,1)S(1)}, u32[]{:S(2)}, u32[]{:S(2)}) collective-permute-start(bf16[512,256]{1,0:T(8,128)(2,1)} %own_ref.1), channel_id=1, source_target_pairs={{0,1},{1,0},{2,3},{3,2},{4,5},{5,4},{6,7},{7,6},{8,9},{9,8},{10,11... | collective-permute-start | bytes 786440 | tf_op jit(solution)/shard_map/ppermute | solution.py:665
  28.7 12.2 %all-to-all-start = ((f32[32,1,256]{2,1,0:T(1,128)}), f32[32,1,256]{2,1,0:T(1,128)S(1)}, u32[]{:S(2)}, u32[]{:S(2)}) async-start(f32[32,1,256]{2,1,0:T(1,128)} %wide_tops.1.refs_10_), calls=%async_computation | async-start | bytes 65536 | tf_op jit(solution)/shard_map/all_to_all | solution.py:695
  40.8 0.7 copy-start.1
  41.0 5.3 %collective-permute-start.10 = (bf16[512,256]{1,0:T(8,128)(2,1)S(1)}, bf16[512,256]{1,0:T(8,128)(2,1)S(1)}, u32[]{:S(2)}, u32[]{:S(2)}) collective-permute-start(bf16[512,256]{1,0:T(8,128)(2,1)S(1)} %collective-permute-done.6.refs_9_.partner_ref), channel_id=1, source_target_pairs={{0,1},{1,0},{2,3},{3,2},{4,5},{5,4},{6,7},{7,6},{8,9},{9,8},{10,11... | collective-permute-start | bytes 786440 | tf_op jit(solution)/shard_map/ppermute | solution.py:665
  41.1 5.1 %collective-permute-start.17 = (bf16[768,256]{1,0:T(8,128)(2,1)S(1)}, bf16[768,256]{1,0:T(8,128)(2,1)}, u32[]{:S(2)}, u32[]{:S(2)}) collective-permute-start(bf16[768,256]{1,0:T(8,128)(2,1)S(1)} %maximum_select_fusion.refs_8_.refs_2_), channel_id=1, source_target_pairs={{0,1},{1,0},{2,3},{3,2},{4,5},{5,4},{6,7},{7,6},{8,9},{9,8},{10,11... | collective-permute-start | bytes 1179656 | tf_op jit(solution)/shard_map/ppermute | solution.py:665
  41.6 14.0 %collective-permute-start.8 = (f32[48,2048]{1,0:T(8,128)S(1)}, f32[48,2048]{1,0:T(8,128)S(1)}, u32[]{:S(2)}, u32[]{:S(2)}) collective-permute-start(f32[48,2048]{1,0:T(8,128)S(1)} %slice_add_fusion.refs_5_), channel_id=1, source_target_pairs={{0,2},{1,3},{2,0},{3,1},{4,6},{5,7},{6,4},{7,5},{8,10},{9,11},{10,... | collective-permute-start | bytes 1179656 | tf_op jit(solution)/shard_map/ppermute | solution.py:665
  52.3 0.7 copy-start
  53.0 10.8 %all-to-all-start.1 = ((bf16[32,16,128]{2,1,0:T(8,128)(2,1)}), bf16[32,16,128]{2,1,0:T(8,128)(2,1)S(1)}, u32[]{:S(2)}, u32[]{:S(2)}) async-start(bf16[32,16,128]{2,1,0:T(8,128)(2,1)} %copy-done), calls=%async_computation.1 | async-start | bytes 262144 | tf_op jit(solution)/shard_map/all_to_all | solution.py:695
  57.1 13.7 %collective-permute-start.13 = (bf16[48,256]{1,0:T(8,128)(2,1)S(1)}, bf16[48,256]{1,0:T(8,128)(2,1)S(1)}, u32[]{:S(2)}, u32[]{:S(2)}) collective-permute-start(bf16[48,256]{1,0:T(8,128)(2,1)S(1)} %get-tuple-element.28.refs_2_), channel_id=1, source_target_pairs={{0,3},{1,2},{2,1},{3,0},{4,7},{5,6},{6,5},{7,4},{8,11},{9,10},{10,... | collective-permute-start | bytes 73736 | tf_op jit(solution)/shard_map/ppermute | solution.py:665
  58.6 12.2 %collective-permute-start.12 = (bf16[48,256]{1,0:T(8,128)(2,1)S(1)}, bf16[48,256]{1,0:T(8,128)(2,1)S(1)}, u32[]{:S(2)}, u32[]{:S(2)}) collective-permute-start(bf16[48,256]{1,0:T(8,128)(2,1)S(1)} %get-tuple-element.28.refs_2_), channel_id=1, source_target_pairs={{0,2},{1,3},{2,0},{3,1},{4,6},{5,7},{6,4},{7,5},{8,10},{9,11},{10,... | collective-permute-start | bytes 73736 | tf_op jit(solution)/shard_map/ppermute | solution.py:665
  58.9 11.9 %collective-permute-start.11 = (bf16[48,256]{1,0:T(8,128)(2,1)S(1)}, bf16[48,256]{1,0:T(8,128)(2,1)S(1)}, u32[]{:S(2)}, u32[]{:S(2)}) collective-permute-start(bf16[48,256]{1,0:T(8,128)(2,1)S(1)} %get-tuple-element.28.refs_2_), channel_id=1, source_target_pairs={{0,1},{1,0},{2,3},{3,2},{4,5},{5,4},{6,7},{7,6},{8,9},{9,8},{10,11... | collective-permute-start | bytes 73736 | tf_op jit(solution)/shard_map/ppermute | solution.py:665
  68.2 10.8 %all-to-all-start.2 = ((bf16[32,16,128]{2,1,0:T(8,128)(2,1)}), bf16[32,16,128]{2,1,0:T(8,128)(2,1)S(1)}, u32[]{:S(2)}, u32[]{:S(2)}) async-start(bf16[32,16,128]{2,1,0:T(8,128)(2,1)} %next_sweep.1), calls=%async_computation.2 | async-start | bytes 262144 | tf_op jit(solution)/shard_map/all_to_all | solution.py:695
  76.9 16.6 %copy-start.2 = (f32[32,1,256]{2,1,0:T(1,128)S(1)}, f32[32,1,256]{2,1,0:T(1,128)}, u32[]{:S(2)}) copy-start(f32[32,1,256]{2,1,0:T(1,128)} %copy-done.1) | copy-start | bytes 98308
  76.9 16.6 %copy-start.4 = (bf16[192,256]{1,0:T(8,128)(2,1)S(1)}, bf16[192,256]{1,0:T(8,128)(2,1)}, u32[]{:S(2)}) copy-start(bf16[192,256]{1,0:T(8,128)(2,1)} %copy-done.3) | copy-start | bytes 294916
  82.8 10.7 %all-to-all-start.3 = ((f32[8,1,2048]{2,1,0:T(1,128)}), f32[8,1,2048]{2,1,0:T(1,128)S(1)}, u32[]{:S(2)}, u32[]{:S(2)}) async-start(f32[8,1,2048]{2,1,0:T(1,128)} %last_scales.1), calls=%async_computation.3 | async-start | bytes 131072 | tf_op jit(solution)/shard_map/all_to_all | solution.py:695
  90.8 13.7 %collective-permute-start.14 = (f32[48,512]{1,0:T(8,128)S(1)}, f32[48,512]{1,0:T(8,128)S(1)}, u32[]{:S(2)}, u32[]{:S(2)}) collective-permute-start(f32[48,512]{1,0:T(8,128)S(1)} %get-tuple-element.30), channel_id=1, source_target_pairs={{0,3},{1,2},{2,1},{3,0},{4,7},{5,6},{6,5},{7,4},{8,11},{9,10},{10,... | collective-permute-start | bytes 294920 | tf_op jit(solution)/shard_map/ppermute | solution.py:665
  91.8 13.0 %collective-permute-start.15 = (f32[48,512]{1,0:T(8,128)S(1)}, f32[48,512]{1,0:T(8,128)S(1)}, u32[]{:S(2)}, u32[]{:S(2)}) collective-permute-start(f32[48,512]{1,0:T(8,128)S(1)} %get-tuple-element.31), channel_id=1, source_target_pairs={{0,2},{1,3},{2,0},{3,1},{4,6},{5,7},{6,4},{7,5},{8,10},{9,11},{10,... | collective-permute-start | bytes 294920 | tf_op jit(solution)/shard_map/ppermute | solution.py:665
  92.4 12.4 %collective-permute-start.16 = (f32[48,512]{1,0:T(8,128)S(1)}, f32[48,512]{1,0:T(8,128)S(1)}, u32[]{:S(2)}, u32[]{:S(2)}) collective-permute-start(f32[48,512]{1,0:T(8,128)S(1)} %get-tuple-element.32), channel_id=1, source_target_pairs={{0,1},{1,0},{2,3},{3,2},{4,5},{5,4},{6,7},{7,6},{8,9},{9,8},{10,11... | collective-permute-start | bytes 294920 | tf_op jit(solution)/shard_map/ppermute | solution.py:665
  102.9 3.8 %collective-permute-start.18 = (bf16[48,384]{1,0:T(8,128)(2,1)S(1)}, bf16[48,384]{1,0:T(8,128)(2,1)S(1)}, u32[]{:S(2)}, u32[]{:S(2)}) collective-permute-start(bf16[48,384]{1,0:T(8,128)(2,1)S(1)} %get-tuple-element.36), channel_id=1, source_target_pairs={{0,3},{1,2},{2,1},{3,0},{4,7},{5,6},{6,5},{7,4},{8,11},{9,10},{10,... | collective-permute-start | bytes 110600 | tf_op jit(solution)/shard_map/ppermute | solution.py:665
  103.5 4.3 %collective-permute-start.19 = (bf16[48,384]{1,0:T(8,128)(2,1)S(1)}, bf16[48,384]{1,0:T(8,128)(2,1)S(1)}, u32[]{:S(2)}, u32[]{:S(2)}) collective-permute-start(bf16[48,384]{1,0:T(8,128)(2,1)S(1)} %get-tuple-element.37), channel_id=1, source_target_pairs={{0,2},{1,3},{2,0},{3,1},{4,6},{5,7},{6,4},{7,5},{8,10},{9,11},{10,... | collective-permute-start | bytes 110600 | tf_op jit(solution)/shard_map/ppermute | solution.py:665
  104.5 3.2 %collective-permute-start.20 = (bf16[48,384]{1,0:T(8,128)(2,1)S(1)}, bf16[48,384]{1,0:T(8,128)(2,1)S(1)}, u32[]{:S(2)}, u32[]{:S(2)}) collective-permute-start(bf16[48,384]{1,0:T(8,128)(2,1)S(1)} %get-tuple-element.38), channel_id=1, source_target_pairs={{0,1},{1,0},{2,3},{3,2},{4,5},{5,4},{6,7},{7,6},{8,9},{9,8},{10,11... | collective-permute-start | bytes 110600 | tf_op jit(solution)/shard_map/ppermute | solution.py:665

commit v17 on v12

--- a/solution.py
+++ b/solution.py
@@ -376,8 +376,23 @@
     return (copies, -(-crops_total // 2048) * 16, 128)
 
 
+def lane_order(tops_ref, group, crops_total):
+    batches = tops_ref.shape[0] // group
+    rows = crops_total // batches
+    bits = batches.bit_length() - 1
+    tops = []
+    for batch in range(batches):
+        source = int(format(batch, "b").zfill(bits)[::-1], 2) if bits else 0
+        tops.append(
+            functools.reduce(jnp.maximum, [tops_ref[source * group + other] for other in range(group)])
+        )
+    halves = [top[:, core * rows // 2 : (core + 1) * rows // 2] for core in range(2) for top in tops]
+    return jnp.concatenate(halves, axis=1)
+
+
 def first_sweep_kernel(
-    chunk, protos_total, index_ref, protos_hbm, mine_hbm, other_hbm, bias_ref, copies_ref, weights_hbm, protos_ref, units_ref, weights_ref, rounded_ref, scale_ref, sems, out_sems,
+    chunk, protos_total, group, index_ref, protos_hbm, mine_hbm, other_hbm, tops_ref, copies_ref, weights_hbm,
+    protos_ref, units_ref, weights_ref, rounded_ref, scale_ref, bias_ref, sems, out_sems,
 ):
     thin, crops_total = weights_ref.shape
     half = mine_hbm.shape[0]
@@ -389,6 +404,7 @@
     )
     for copy in copies:
         copy.start()
+    bias_ref[...] = lane_order(tops_ref, group, crops_total) * -teacher_rate
     for copy in copies:
         copy.wait()
 
@@ -427,12 +443,12 @@
         chunk_out(index).wait()
 
 
-def first_sweep(index, protos, mine, other, base, order, copies, thin, protos_total):
+def first_sweep(index, protos, mine, other, tops, order, copies, thin, protos_total):
     width = protos.shape[1]
     crops_total = 2 * mine.shape[0]
     chunk = min(thin, 1024)
     return pl.pallas_call(
-        skipping(functools.partial(first_sweep_kernel, chunk, protos_total), 5, len(order)),
+        skipping(functools.partial(first_sweep_kernel, chunk, protos_total, protos_total // protos.shape[0]), 5, len(order)),
         in_specs=[whole(pltpu.SMEM), whole(pl.ANY), whole(pl.ANY), whole(pl.ANY), whole()]
         + [whole(pl.ANY)] * len(order),
         out_specs=[whole(), whole(pl.ANY)],
@@ -446,13 +462,14 @@
             pltpu.VMEM((thin, crops_total), jnp.float32),
             pltpu.VMEM((thin // chunk, chunk, crops_total), jnp.bfloat16),
             pltpu.VMEM((thin, 128), jnp.float32),
+            pltpu.VMEM((1, crops_total), jnp.float32),
             pltpu.SemaphoreType.DMA((3,)),
             pltpu.SemaphoreType.DMA((thin // chunk,)),
         ],
         compiler_params=params(32 if crops_total <= 2048 else 56),
         cost_estimate=cost(2 * thin * width * crops_total, 2 * thin * crops_total, thin * crops_total),
         name="first_sweep",
-    )(index, in_hbm(protos), mine, other, base, *order)
+    )(index, in_hbm(protos), mine, other, tops, *order)
 
 
 def fetch_rows(weights_hbm, weights_ref, sems):
@@ -673,7 +690,8 @@
 
 
 def send_blocks(blocks):
-    return [blocks[0]] + [swap(block, "proto", flip) for flip, block in enumerate(blocks) if flip]
+    flips = list(range(len(blocks) - 1, 0, -1))
+    return [blocks[0]] + [swap(blocks[flip], "proto", flip) for flip in flips]
 
 
 def all_to_all(copies, axes):
@@ -710,10 +728,6 @@
         proto_ref, own_unit, b_first, rows, w_first, w_second, protos, (stages[2], third_x), devices, 8
     )
     all_tops = all_to_all(top_copies, BOTH)
-    tops = jnp.max(all_tops.reshape(batch_size, proto_size, 256)[:, :, :group_rows], axis=1)
-    tops = bit_reversed(tops, batch_size).reshape(batch_size, 2, group_rows // 2)
-    base = jnp.transpose(tops, (1, 0, 2)).reshape(1, crops_total) * -teacher_rate
-
     core_rows = swap(give, "proto", 1)
     x_sent = keep[share_rows:] + core_rows[share_rows:]
     x_rows = swap(x_sent, "proto", 2)
@@ -724,11 +738,12 @@
     empty = jnp.concatenate(
         [jnp.zeros((group_rows, width + 128), jnp.float32), jnp.full((group_rows, 128), -1e30, jnp.float32)], axis=1
     )
-    (state,) = attract(student_emb, empty, protos, 0, count // 2, 4, 1)
-    slots = attract(student_emb, state, protos, count // 2, count // 2, 4, proto_size)
+    eighth = count // 8
+    (state,) = attract(student_emb, empty, protos, 0, 5 * eighth, 5, 1)
+    slots = attract(student_emb, state, protos, 5 * eighth, 3 * eighth, 3, proto_size)
     attract_parts = send_blocks(slots)
 
-    copies, weights = first_sweep(thin_ref, protos, mine, other, base, (x_sent, *thirds[2:]), devices, thin, protos_total)
+    copies, weights = first_sweep(thin_ref, protos, mine, other, all_tops, (x_sent, *thirds[2:]), devices, thin, protos_total)
     for _ in range(ITERS - 2):
         copies = next_sweep(weights, all_to_all(copies, BOTH), (rounded,), protos_total)
     scale_copies = last_scales(weights, all_to_all(copies, BOTH), (state,), batch_size, protos_total)

time: 101 us -> 99.6 us (0.986)
  waiting for transfers between devices: 25.3 us -> 23.3 us
  starting transfers between devices: 27.6 us -> 28.9 us
    ppermute x21, waiting for transfers between devices: 14 us -> 12.9 us  [swap(): lax.ppermute(values, axis, [(i, i ^ flip) for i in range(lax.axis_size(ax...]
  transfers between devices with their start and end apart: 25 -> 25, of which waited for: 11 -> 11; matrix products, arithmetic and copies ran while one was open for 1% -> 0% of each run, Pallas kernels for 32% -> 33%
where the time goes in v17:
time: 99.6 us; the launch traced here: 99.1 us
  Pallas kernels  46.2 us (46%)
  starting transfers between devices  28.9 us (29%)
  waiting for transfers between devices  23.3 us (23%)
    ppermute x21, starting transfers between devices, swap(): lax.ppermute(values, axis, [(i, i ^ flip) for i in range(lax.axis_size(ax...  17.2 us
    ppermute x21, waiting for transfers between devices, swap(): lax.ppermute(values, axis, [(i, i ^ flip) for i in range(lax.axis_size(ax...  12.9 us
    all_to_all x4, starting transfers between devices, all_to_all(): return lax.all_to_all(copies, axes, 0, 0, tiled=True)  11.7 us
    all_to_all x4, waiting for transfers between devices, all_to_all(): return lax.all_to_all(copies, axes, 0, 0, tiled=True)  10.4 us
    pallas_call x2, Pallas kernels, attract(): pl.pallas_call(functools.partial(attract_kernel, first_row, outputs > 1),...  10.2 us
    pallas_call x1, Pallas kernels, repel(): pl.pallas_call(skipping(functools.partial(repel_kernel, proto_size), 5, l...  9.45 us
    pallas_call x1, Pallas kernels, front(): pl.pallas_call(skipping(front_kernel, 10, len(order)), in_specs=[whole(pl...  8.14 us
    pallas_call x1, Pallas kernels, first_sweep(): pl.pallas_call(skipping(functools.partial(first_sweep_kernel, chunk, prot...  6.8 us
  transfers between devices with their start and end apart: 25, of which 11 were waited for; matrix products, arithmetic and copies ran while one was open for 0% of the time, Pallas kernels for 33%

profile of v17, /device:TPU:0, one launch (start us, length us, event | category | flops | bytes accessed | tf_op | source)
XLA Modules:
  0.0 99.1 jit_solution(4749747192631374502)
XLA Ops:
  0.0 1.0 %teacher_units.1 = (bf16[192,256]{1,0:T(8,128)(2,1)S(1)}, bf16[96,256]{1,0:T(8,128)(2,1)S(1)}) custom-call(s32[1]{0:T(128)} %bitcast.1.core_ref, bf16[192,256]{1,0:T(8,128)(2,1)} %emb_ref.1), custom_call_target="tpu_custom_call" | custom-call | flops 196608 | bytes 393216 | tf_op jit(solution)/shard_map/teacher_units/pallas_call | solution.py:96
  1.0 4.1 %collective-permute-start.3 = (bf16[96,256]{1,0:T(8,128)(2,1)S(1)}, bf16[96,256]{1,0:T(8,128)(2,1)S(1)}, u32[]{:S(2)}, u32[]{:S(2)}) collective-permute-start(bf16[96,256]{1,0:T(8,128)(2,1)S(1)} %get-tuple-element.24), channel_id=1, source_target_pairs={{0,16},{4,20},{8,24},{12,28},{16,0},{20,4},{24,8},{28,12},{1,17},{... | collective-permute-start | bytes 147464 | tf_op jit(solution)/shard_map/ppermute | solution.py:668
  5.1 1.5 %collective-permute-start = (bf16[48,1536]{1,0:T(8,128)(2,1)}, bf16[48,1536]{1,0:T(8,128)(2,1)S(1)}, u32[]{:S(2)}, u32[]{:S(2)}) collective-permute-start(bf16[48,1536]{1,0:T(8,128)(2,1)} %refs_3_.1), channel_id=1, source_target_pairs={{0,2},{1,3},{2,0},{3,1},{4,6},{5,7},{6,4},{7,5},{8,10},{9,11},{10,... | collective-permute-start | bytes 442376 | tf_op jit(solution)/shard_map/ppermute | solution.py:668
  6.6 0.5 collective-permute-start.5
  7.2 0.6 collective-permute-done.3
  7.8 1.4 %collective-permute-start.4 = (bf16[192,256]{1,0:T(8,128)(2,1)S(1)}, bf16[192,256]{1,0:T(8,128)(2,1)S(1)}, u32[]{:S(2)}, u32[]{:S(2)}) collective-permute-start(bf16[192,256]{1,0:T(8,128)(2,1)S(1)} %maximum_select_fusion.2), channel_id=1, source_target_pairs={{0,8},{4,12},{8,0},{12,4},{16,24},{20,28},{24,16},{28,20},{1,9},{5... | collective-permute-start | bytes 294920 | tf_op jit(solution)/shard_map/ppermute | solution.py:668
  9.2 0.0 collective-permute-start.1
  9.2 2.9 %collective-permute-done.refs_4_ = bf16[48,1536]{1,0:T(8,128)(2,1)S(1)} collective-permute-done((bf16[48,1536]{1,0:T(8,128)(2,1)}, bf16[48,1536]{1,0:T(8,128)(2,1)S(1)}, u32[]{:S(2)}, u32[]{:S(2)}) %collective-permute-start) | collective-permute-done | bytes 147488 | tf_op jit(solution)/shard_map/ppermute | solution.py:668
  12.1 0.0 collective-permute-start.2
  12.1 0.3 collective-permute-done.4
  12.4 0.1 maximum_select_fusion.1.refs_10_
  12.5 0.0 collective-permute-done.1.refs_5_
  12.5 3.8 %collective-permute-done.5.refs_11_.partner_ref = bf16[512,256]{1,0:T(8,128)(2,1)S(1)} collective-permute-done((bf16[512,256]{1,0:T(8,128)(2,1)}, bf16[512,256]{1,0:T(8,128)(2,1)S(1)}, u32[]{:S(2)}, u32[]{:S(2)}) %collective-permute-start.5) | collective-permute-done | bytes 262176 | tf_op jit(solution)/shard_map/ppermute | solution.py:668
  16.3 0.0 collective-permute-done.2.refs_6_
  16.3 8.1 %front.1 = (f32[32,1,256]{2,1,0:T(1,128)}, f32[96,2048]{1,0:T(8,128)S(1)}, f32[96,2048]{1,0:T(8,128)}) custom-call(s32[1]{0:T(128)} %bitcast.refs_0_.index_ref, bf16[192,256]{1,0:T(8,128)(2,1)S(1)} %get-tuple-element.23.refs_1_, f32[1,2048]{1,0:T(1,128)} %bitcast.7, bf16[48,1536]{1,0:T(8,128)(2,1)} %refs_3_.1, ...), custom_call_target="tpu_custom_call" | custom-call | flops 2315255808 | bytes 8388608 | tf_op jit(solution)/shard_map/front/pallas_call | solution.py:159
  24.4 0.1 collective-permute-start.6
  24.5 1.6 %collective-permute-start.16 = (bf16[384,256]{1,0:T(8,128)(2,1)S(1)}, bf16[384,256]{1,0:T(8,128)(2,1)S(1)}, u32[]{:S(2)}, u32[]{:S(2)}) collective-permute-start(bf16[384,256]{1,0:T(8,128)(2,1)S(1)} %maximum_select_fusion.1.refs_10_), channel_id=1, source_target_pairs={{0,4},{4,0},{8,12},{12,8},{16,20},{20,16},{24,28},{28,24},{1,5},{5... | collective-permute-start | bytes 589832 | tf_op jit(solution)/shard_map/ppermute | solution.py:668
  26.1 0.2 collective-permute-start.8
  26.3 0.3 collective-permute-start.9
  26.6 2.9 %all-to-all-start = ((f32[32,1,256]{2,1,0:T(1,128)}), f32[32,1,256]{2,1,0:T(1,128)S(1)}, u32[]{:S(2)}, u32[]{:S(2)}) async-start(f32[32,1,256]{2,1,0:T(1,128)} %get-tuple-element.34), calls=%async_computation | async-start | bytes 65536 | tf_op jit(solution)/shard_map/all_to_all | solution.py:698
  29.5 2.3 %collective-permute-done.16 = bf16[384,256]{1,0:T(8,128)(2,1)S(1)} collective-permute-done((bf16[384,256]{1,0:T(8,128)(2,1)S(1)}, bf16[384,256]{1,0:T(8,128)(2,1)S(1)}, u32[]{:S(2)}, u32[]{:S(2)}) %collective-permute-start.16) | collective-permute-done | bytes 196640 | tf_op jit(solution)/shard_map/ppermute | solution.py:668
  31.8 0.2 maximum_select_fusion.refs_2_
  32.0 0.1 collective-permute-start.17
  32.1 0.0 collective-permute-done.6.core_ref
  32.1 1.6 %collective-permute-start.7 = (f32[48,2048]{1,0:T(8,128)S(1)}, f32[48,2048]{1,0:T(8,128)}, u32[]{:S(2)}, u32[]{:S(2)}) collective-permute-start(f32[48,2048]{1,0:T(8,128)S(1)} %slice_add_fusion.refs_5_), channel_id=1, source_target_pairs={{0,2},{1,3},{2,0},{3,1},{4,6},{5,7},{6,4},{7,5},{8,10},{9,11},{10,... | collective-permute-start | bytes 1179656 | tf_op jit(solution)/shard_map/ppermute | solution.py:668
  33.7 0.1 pad_add_fusion.1.refs_0_
  33.8 0.0 collective-permute-done.8.other_ref.refs_6_
  33.8 3.0 %all-to-all-done.refs_4_.refs_2_ = f32[32,1,256]{2,1,0:T(1,128)S(1)} async-done(((f32[32,1,256]{2,1,0:T(1,128)}), f32[32,1,256]{2,1,0:T(1,128)S(1)}, u32[]{:S(2)}, u32[]{:S(2)}) %all-to-all-start) | async-done | bytes 32800 | tf_op jit(solution)/shard_map/all_to_all | solution.py:698
  36.7 0.0 collective-permute-done.9.last_ref.refs_7_
  36.7 0.0 collective-permute-done.17.refs_3_
  36.7 6.8 %first_sweep.1 = (bf16[32,16,128]{2,1,0:T(8,128)(2,1)}, bf16[2048,1536]{1,0:T(8,128)(2,1)}) custom-call(s32[2]{0:T(128)S(1)} %pad_add_fusion.1.refs_0_, bf16[16384,256]{1,0:T(8,128)(2,1)} %refs_4_.1, bf16[768,256]{1,0:T(8,128)(2,1)S(1)} %maximum_select_fusion.refs_2_, bf16[768,256]{1,0:T(8,128)(2,1)} %collective-permute-done.17.refs_3_, ...), custom_call_target="tpu_custom_call" | custom-call | flops 1610612736 | bytes 6291456 | tf_op jit(solution)/shard_map/first_sweep/pallas_call | solution.py:450
  43.5 2.6 %all-to-all-start.1 = ((bf16[32,16,128]{2,1,0:T(8,128)(2,1)}), bf16[32,16,128]{2,1,0:T(8,128)(2,1)S(1)}, u32[]{:S(2)}, u32[]{:S(2)}) async-start(bf16[32,16,128]{2,1,0:T(8,128)(2,1)} %get-tuple-element.36), calls=%async_computation.1 | async-start | bytes 262144 | tf_op jit(solution)/shard_map/all_to_all | solution.py:698
  46.1 0.0 collective-permute-done.7.x_ref
  46.2 1.7 %student_middle.1 = (f32[48,256]{1,0:T(8,128)S(1)}, bf16[48,256]{1,0:T(8,128)(2,1)S(1)}, f32[48,128]{1,0:T(8,128)S(1)}) custom-call(s32[1]{0:T(128)} %bitcast.refs_0_.index_ref, f32[96,2048]{1,0:T(8,128)S(1)} %get-tuple-element.25.keep_ref, f32[96,2048]{1,0:T(8,128)S(1)} %collective-permute-done.6.core_ref, f32[48,2048]{1,0:T(8,128)} %collective-permute-done.7.x_ref, ...), custom_call_target="tpu_custom_call" | custom-call | flops 50331648 | bytes 2621440 | tf_op jit(solution)/shard_map/student_middle/pallas_call | solution.py:616
  47.8 1.5 %collective-permute-start.12 = (bf16[48,256]{1,0:T(8,128)(2,1)S(1)}, bf16[48,256]{1,0:T(8,128)(2,1)S(1)}, u32[]{:S(2)}, u32[]{:S(2)}) collective-permute-start(bf16[48,256]{1,0:T(8,128)(2,1)S(1)} %get-tuple-element.29.refs_2_), channel_id=1, source_target_pairs={{0,3},{1,2},{2,1},{3,0},{4,7},{5,6},{6,5},{7,4},{8,11},{9,10},{10,... | collective-permute-start | bytes 73736 | tf_op jit(solution)/shard_map/ppermute | solution.py:668
  49.3 0.4 collective-permute-start.11
  49.6 0.1 collective-permute-start.10
  49.8 4.6 %all-to-all-done.1.refs_1_ = bf16[32,16,128]{2,1,0:T(8,128)(2,1)S(1)} async-done(((bf16[32,16,128]{2,1,0:T(8,128)(2,1)}), bf16[32,16,128]{2,1,0:T(8,128)(2,1)S(1)}, u32[]{:S(2)}, u32[]{:S(2)}) %all-to-all-start.1) | async-done | bytes 131104 | tf_op jit(solution)/shard_map/all_to_all | solution.py:698
  54.4 4.4 %next_sweep.1 = bf16[32,16,128]{2,1,0:T(8,128)(2,1)} custom-call(bf16[2048,1536]{1,0:T(8,128)(2,1)} %get-tuple-element.35.refs_0_, bf16[32,16,128]{2,1,0:T(8,128)(2,1)S(1)} %all-to-all-done.1.refs_1_, bf16[48,256]{1,0:T(8,128)(2,1)S(1)} %get-tuple-element.29.refs_2_), custom_call_target="tpu_custom_call" | custom-call | flops 25165824 | bytes 6291456 | tf_op jit(solution)/shard_map/next_sweep/pallas_call | solution.py:536
  58.8 2.6 %all-to-all-start.2 = ((bf16[32,16,128]{2,1,0:T(8,128)(2,1)}), bf16[32,16,128]{2,1,0:T(8,128)(2,1)S(1)}, u32[]{:S(2)}, u32[]{:S(2)}) async-start(bf16[32,16,128]{2,1,0:T(8,128)(2,1)} %next_sweep.1), calls=%async_computation.2 | async-start | bytes 262144 | tf_op jit(solution)/shard_map/all_to_all | solution.py:698
  61.3 0.0 collective-permute-done.10
  61.4 0.0 collective-permute-done.11
  61.4 0.0 collective-permute-done.12
  61.5 6.0 %attract.2.state_ref.refs_2_ = f32[192,512]{1,0:T(8,128)S(1)} custom-call(bf16[192,256]{1,0:T(8,128)(2,1)S(1)} %constant_dynamic-update-slice_fusion.emb_ref, f32[192,512]{1,0:T(8,128)S(1)} %concatenate.32.state_ref, bf16[16384,256]{1,0:T(8,128)(2,1)} %refs_4_.1), custom_call_target="tpu_custom_call" | custom-call | flops 2013265920 | bytes 5242880 | tf_op jit(solution)/shard_map/attract/pallas_call | solution.py:324
  67.4 2.1 %all-to-all-done.2.refs_1_ = bf16[32,16,128]{2,1,0:T(8,128)(2,1)S(1)} async-done(((bf16[32,16,128]{2,1,0:T(8,128)(2,1)}), bf16[32,16,128]{2,1,0:T(8,128)(2,1)S(1)}, u32[]{:S(2)}, u32[]{:S(2)}) %all-to-all-start.2) | async-done | bytes 131104 | tf_op jit(solution)/shard_map/all_to_all | solution.py:698
  69.6 3.8 %last_scales.1 = f32[8,1,2048]{2,1,0:T(1,128)} custom-call(bf16[2048,1536]{1,0:T(8,128)(2,1)} %get-tuple-element.35.refs_0_, bf16[32,16,128]{2,1,0:T(8,128)(2,1)S(1)} %all-to-all-done.2.refs_1_, f32[192,512]{1,0:T(8,128)S(1)} %attract.2.state_ref.refs_2_), custom_call_target="tpu_custom_call" | custom-call | flops 12582912 | bytes 6291456 | tf_op jit(solution)/shard_map/last_scales/pallas_call | solution.py:575
  73.3 3.7 %all-to-all-start.3 = ((f32[8,1,2048]{2,1,0:T(1,128)}), f32[8,1,2048]{2,1,0:T(1,128)S(1)}, u32[]{:S(2)}, u32[]{:S(2)}) async-start(f32[8,1,2048]{2,1,0:T(1,128)} %last_scales.1), calls=%async_computation.3 | async-start | bytes 131072 | tf_op jit(solution)/shard_map/all_to_all | solution.py:698
  77.1 0.1 pad_add_fusion.refs_0_
  77.1 4.2 %attract.3 = (f32[48,512]{1,0:T(8,128)S(1)}, f32[48,512]{1,0:T(8,128)S(1)}, f32[48,512]{1,0:T(8,128)S(1)}, f32[48,512]{1,0:T(8,128)S(1)}) custom-call(bf16[192,256]{1,0:T(8,128)(2,1)S(1)} %constant_dynamic-update-slice_fusion.emb_ref, f32[192,512]{1,0:T(8,128)S(1)} %attract.2.state_ref.refs_2_, bf16[16384,256]{1,0:T(8,128)(2,1)} %refs_4_.1), custom_call_target="tpu_custom_call" | custom-call | flops 1207959552 | bytes 3145728 | tf_op jit(solution)/shard_map/attract/pallas_call | solution.py:324
  81.3 1.0 %collective-permute-start.13 = (f32[48,512]{1,0:T(8,128)S(1)}, f32[48,512]{1,0:T(8,128)S(1)}, u32[]{:S(2)}, u32[]{:S(2)}) collective-permute-start(f32[48,512]{1,0:T(8,128)S(1)} %get-tuple-element.31), channel_id=1, source_target_pairs={{0,3},{1,2},{2,1},{3,0},{4,7},{5,6},{6,5},{7,4},{8,11},{9,10},{10,... | collective-permute-start | bytes 294920 | tf_op jit(solution)/shard_map/ppermute | solution.py:668
  82.3 0.6 collective-permute-start.14
  82.9 0.3 collective-permute-start.15
  83.2 0.7 all-to-all-done.3.refs_3_
  84.0 9.5 %repel.1 = (f32[48,384]{1,0:T(8,128)S(1)}, bf16[48,384]{1,0:T(8,128)(2,1)S(1)}, bf16[48,384]{1,0:T(8,128)(2,1)S(1)}, bf16[48,384]{1,0:T(8,128)(2,1)S(1)}) custom-call(s32[2]{0:T(128)S(1)} %pad_add_fusion.refs_0_, bf16[192,256]{1,0:T(8,128)(2,1)S(1)} %get-tuple-element.23.refs_1_, f32[32,1,256]{2,1,0:T(1,128)S(1)} %all-to-all-done.refs_4_.refs_2_, ...), custom_call_target="tpu_custom_call" | custom-call | flops 3221225472 | bytes 8388608 | tf_op jit(solution)/shard_map/repel/pallas_call | solution.py:243
  93.4 0.6 collective-permute-start.18
  94.0 1.0 %collective-permute-start.19 = (bf16[48,384]{1,0:T(8,128)(2,1)S(1)}, bf16[48,384]{1,0:T(8,128)(2,1)S(1)}, u32[]{:S(2)}, u32[]{:S(2)}) collective-permute-start(bf16[48,384]{1,0:T(8,128)(2,1)S(1)} %get-tuple-element.39), channel_id=1, source_target_pairs={{0,2},{1,3},{2,0},{3,1},{4,6},{5,7},{6,4},{7,5},{8,10},{9,11},{10,... | collective-permute-start | bytes 110600 | tf_op jit(solution)/shard_map/ppermute | solution.py:668
  95.0 0.0 collective-permute-done.13.rest_1_
  95.0 0.3 collective-permute-start.20
  95.3 0.0 collective-permute-done.14.rest_2_
  95.4 0.0 collective-permute-done.15.rest_3_
  95.4 1.9 %collective-permute-done.18.rest_5_ = bf16[48,384]{1,0:T(8,128)(2,1)S(1)} collective-permute-done((bf16[48,384]{1,0:T(8,128)(2,1)S(1)}, bf16[48,384]{1,0:T(8,128)(2,1)S(1)}, u32[]{:S(2)}, u32[]{:S(2)}) %collective-permute-start.18) | collective-permute-done | bytes 36896 | tf_op jit(solution)/shard_map/ppermute | solution.py:668
  97.2 1.1 %collective-permute-done.19.rest_6_ = bf16[48,384]{1,0:T(8,128)(2,1)S(1)} collective-permute-done((bf16[48,384]{1,0:T(8,128)(2,1)S(1)}, bf16[48,384]{1,0:T(8,128)(2,1)S(1)}, u32[]{:S(2)}, u32[]{:S(2)}) %collective-permute-start.19) | collective-permute-done | bytes 36896 | tf_op jit(solution)/shard_map/ppermute | solution.py:668
  98.3 0.0 collective-permute-done.20.rest_7_
  98.3 0.8 finish.1
  (9 shorter events, 0.1 us)
Async XLA Ops:
  1.0 6.7 %collective-permute-start.3 = (bf16[96,256]{1,0:T(8,128)(2,1)S(1)}, bf16[96,256]{1,0:T(8,128)(2,1)S(1)}, u32[]{:S(2)}, u32[]{:S(2)}) collective-permute-start(bf16[96,256]{1,0:T(8,128)(2,1)S(1)} %get-tuple-element.24), channel_id=1, source_target_pairs={{0,16},{4,20},{8,24},{12,28},{16,0},{20,4},{24,8},{28,12},{1,17},{... | collective-permute-start | bytes 147464 | tf_op jit(solution)/shard_map/ppermute | solution.py:668
  5.1 7.0 %collective-permute-start = (bf16[48,1536]{1,0:T(8,128)(2,1)}, bf16[48,1536]{1,0:T(8,128)(2,1)S(1)}, u32[]{:S(2)}, u32[]{:S(2)}) collective-permute-start(bf16[48,1536]{1,0:T(8,128)(2,1)} %refs_3_.1), channel_id=1, source_target_pairs={{0,2},{1,3},{2,0},{3,1},{4,6},{5,7},{6,4},{7,5},{8,10},{9,11},{10,... | collective-permute-start | bytes 442376 | tf_op jit(solution)/shard_map/ppermute | solution.py:668
  6.6 9.6 %collective-permute-start.5 = (bf16[512,256]{1,0:T(8,128)(2,1)}, bf16[512,256]{1,0:T(8,128)(2,1)S(1)}, u32[]{:S(2)}, u32[]{:S(2)}) collective-permute-start(bf16[512,256]{1,0:T(8,128)(2,1)} %own_ref.1), channel_id=1, source_target_pairs={{0,2},{1,3},{2,0},{3,1},{4,6},{5,7},{6,4},{7,5},{8,10},{9,11},{10,... | collective-permute-start | bytes 786440 | tf_op jit(solution)/shard_map/ppermute | solution.py:668
  7.8 4.7 %collective-permute-start.4 = (bf16[192,256]{1,0:T(8,128)(2,1)S(1)}, bf16[192,256]{1,0:T(8,128)(2,1)S(1)}, u32[]{:S(2)}, u32[]{:S(2)}) collective-permute-start(bf16[192,256]{1,0:T(8,128)(2,1)S(1)} %maximum_select_fusion.2), channel_id=1, source_target_pairs={{0,8},{4,12},{8,0},{12,4},{16,24},{20,28},{24,16},{28,20},{1,9},{5... | collective-permute-start | bytes 294920 | tf_op jit(solution)/shard_map/ppermute | solution.py:668
  9.2 3.3 %collective-permute-start.1 = (bf16[48,1536]{1,0:T(8,128)(2,1)}, bf16[48,1536]{1,0:T(8,128)(2,1)S(1)}, u32[]{:S(2)}, u32[]{:S(2)}) collective-permute-start(bf16[48,1536]{1,0:T(8,128)(2,1)} %refs_3_.1), channel_id=1, source_target_pairs={{0,1},{1,0},{2,3},{3,2},{4,5},{5,4},{6,7},{7,6},{8,9},{9,8},{10,11... | collective-permute-start | bytes 442376 | tf_op jit(solution)/shard_map/ppermute | solution.py:668
  12.1 4.2 %collective-permute-start.2 = (bf16[48,1536]{1,0:T(8,128)(2,1)S(1)}, bf16[48,1536]{1,0:T(8,128)(2,1)S(1)}, u32[]{:S(2)}, u32[]{:S(2)}) collective-permute-start(bf16[48,1536]{1,0:T(8,128)(2,1)S(1)} %collective-permute-done.refs_4_), channel_id=1, source_target_pairs={{0,1},{1,0},{2,3},{3,2},{4,5},{5,4},{6,7},{7,6},{8,9},{9,8},{10,11... | collective-permute-start | bytes 442376 | tf_op jit(solution)/shard_map/ppermute | solution.py:668
  24.4 7.6 %collective-permute-start.6 = (f32[96,2048]{1,0:T(8,128)}, f32[96,2048]{1,0:T(8,128)S(1)}, u32[]{:S(2)}, u32[]{:S(2)}) collective-permute-start(f32[96,2048]{1,0:T(8,128)} %get-tuple-element.26), channel_id=1, source_target_pairs={{0,1},{1,0},{2,3},{3,2},{4,5},{5,4},{6,7},{7,6},{8,9},{9,8},{10,11... | collective-permute-start | bytes 2359304 | tf_op jit(solution)/shard_map/ppermute | solution.py:668
  24.5 7.3 %collective-permute-start.16 = (bf16[384,256]{1,0:T(8,128)(2,1)S(1)}, bf16[384,256]{1,0:T(8,128)(2,1)S(1)}, u32[]{:S(2)}, u32[]{:S(2)}) collective-permute-start(bf16[384,256]{1,0:T(8,128)(2,1)S(1)} %maximum_select_fusion.1.refs_10_), channel_id=1, source_target_pairs={{0,4},{4,0},{8,12},{12,8},{16,20},{20,16},{24,28},{28,24},{1,5},{5... | collective-permute-start | bytes 589832 | tf_op jit(solution)/shard_map/ppermute | solution.py:668
  26.1 7.7 %collective-permute-start.8 = (bf16[512,256]{1,0:T(8,128)(2,1)}, bf16[512,256]{1,0:T(8,128)(2,1)S(1)}, u32[]{:S(2)}, u32[]{:S(2)}) collective-permute-start(bf16[512,256]{1,0:T(8,128)(2,1)} %own_ref.1), channel_id=1, source_target_pairs={{0,1},{1,0},{2,3},{3,2},{4,5},{5,4},{6,7},{7,6},{8,9},{9,8},{10,11... | collective-permute-start | bytes 786440 | tf_op jit(solution)/shard_map/ppermute | solution.py:668
  26.3 10.5 %collective-permute-start.9 = (bf16[512,256]{1,0:T(8,128)(2,1)S(1)}, bf16[512,256]{1,0:T(8,128)(2,1)S(1)}, u32[]{:S(2)}, u32[]{:S(2)}) collective-permute-start(bf16[512,256]{1,0:T(8,128)(2,1)S(1)} %collective-permute-done.5.refs_11_.partner_ref), channel_id=1, source_target_pairs={{0,1},{1,0},{2,3},{3,2},{4,5},{5,4},{6,7},{7,6},{8,9},{9,8},{10,11... | collective-permute-start | bytes 786440 | tf_op jit(solution)/shard_map/ppermute | solution.py:668
  26.6 10.1 %all-to-all-start = ((f32[32,1,256]{2,1,0:T(1,128)}), f32[32,1,256]{2,1,0:T(1,128)S(1)}, u32[]{:S(2)}, u32[]{:S(2)}) async-start(f32[32,1,256]{2,1,0:T(1,128)} %get-tuple-element.34), calls=%async_computation | async-start | bytes 65536 | tf_op jit(solution)/shard_map/all_to_all | solution.py:698
  32.0 4.8 %collective-permute-start.17 = (bf16[768,256]{1,0:T(8,128)(2,1)S(1)}, bf16[768,256]{1,0:T(8,128)(2,1)}, u32[]{:S(2)}, u32[]{:S(2)}) collective-permute-start(bf16[768,256]{1,0:T(8,128)(2,1)S(1)} %maximum_select_fusion.refs_2_), channel_id=1, source_target_pairs={{0,1},{1,0},{2,3},{3,2},{4,5},{5,4},{6,7},{7,6},{8,9},{9,8},{10,11... | collective-permute-start | bytes 1179656 | tf_op jit(solution)/shard_map/ppermute | solution.py:668
  32.1 14.0 %collective-permute-start.7 = (f32[48,2048]{1,0:T(8,128)S(1)}, f32[48,2048]{1,0:T(8,128)}, u32[]{:S(2)}, u32[]{:S(2)}) collective-permute-start(f32[48,2048]{1,0:T(8,128)S(1)} %slice_add_fusion.refs_5_), channel_id=1, source_target_pairs={{0,2},{1,3},{2,0},{3,1},{4,6},{5,7},{6,4},{7,5},{8,10},{9,11},{10,... | collective-permute-start | bytes 1179656 | tf_op jit(solution)/shard_map/ppermute | solution.py:668
  43.5 10.8 %all-to-all-start.1 = ((bf16[32,16,128]{2,1,0:T(8,128)(2,1)}), bf16[32,16,128]{2,1,0:T(8,128)(2,1)S(1)}, u32[]{:S(2)}, u32[]{:S(2)}) async-start(bf16[32,16,128]{2,1,0:T(8,128)(2,1)} %get-tuple-element.36), calls=%async_computation.1 | async-start | bytes 262144 | tf_op jit(solution)/shard_map/all_to_all | solution.py:698
  47.8 13.6 %collective-permute-start.12 = (bf16[48,256]{1,0:T(8,128)(2,1)S(1)}, bf16[48,256]{1,0:T(8,128)(2,1)S(1)}, u32[]{:S(2)}, u32[]{:S(2)}) collective-permute-start(bf16[48,256]{1,0:T(8,128)(2,1)S(1)} %get-tuple-element.29.refs_2_), channel_id=1, source_target_pairs={{0,3},{1,2},{2,1},{3,0},{4,7},{5,6},{6,5},{7,4},{8,11},{9,10},{10,... | collective-permute-start | bytes 73736 | tf_op jit(solution)/shard_map/ppermute | solution.py:668
  49.3 12.1 %collective-permute-start.11 = (bf16[48,256]{1,0:T(8,128)(2,1)S(1)}, bf16[48,256]{1,0:T(8,128)(2,1)S(1)}, u32[]{:S(2)}, u32[]{:S(2)}) collective-permute-start(bf16[48,256]{1,0:T(8,128)(2,1)S(1)} %get-tuple-element.29.refs_2_), channel_id=1, source_target_pairs={{0,2},{1,3},{2,0},{3,1},{4,6},{5,7},{6,4},{7,5},{8,10},{9,11},{10,... | collective-permute-start | bytes 73736 | tf_op jit(solution)/shard_map/ppermute | solution.py:668
  49.6 11.7 %collective-permute-start.10 = (bf16[48,256]{1,0:T(8,128)(2,1)S(1)}, bf16[48,256]{1,0:T(8,128)(2,1)S(1)}, u32[]{:S(2)}, u32[]{:S(2)}) collective-permute-start(bf16[48,256]{1,0:T(8,128)(2,1)S(1)} %get-tuple-element.29.refs_2_), channel_id=1, source_target_pairs={{0,1},{1,0},{2,3},{3,2},{4,5},{5,4},{6,7},{7,6},{8,9},{9,8},{10,11... | collective-permute-start | bytes 73736 | tf_op jit(solution)/shard_map/ppermute | solution.py:668
  58.8 10.8 %all-to-all-start.2 = ((bf16[32,16,128]{2,1,0:T(8,128)(2,1)}), bf16[32,16,128]{2,1,0:T(8,128)(2,1)S(1)}, u32[]{:S(2)}, u32[]{:S(2)}) async-start(bf16[32,16,128]{2,1,0:T(8,128)(2,1)} %next_sweep.1), calls=%async_computation.2 | async-start | bytes 262144 | tf_op jit(solution)/shard_map/all_to_all | solution.py:698
  73.3 10.6 %all-to-all-start.3 = ((f32[8,1,2048]{2,1,0:T(1,128)}), f32[8,1,2048]{2,1,0:T(1,128)S(1)}, u32[]{:S(2)}, u32[]{:S(2)}) async-start(f32[8,1,2048]{2,1,0:T(1,128)} %last_scales.1), calls=%async_computation.3 | async-start | bytes 131072 | tf_op jit(solution)/shard_map/all_to_all | solution.py:698
  81.3 13.7 %collective-permute-start.13 = (f32[48,512]{1,0:T(8,128)S(1)}, f32[48,512]{1,0:T(8,128)S(1)}, u32[]{:S(2)}, u32[]{:S(2)}) collective-permute-start(f32[48,512]{1,0:T(8,128)S(1)} %get-tuple-element.31), channel_id=1, source_target_pairs={{0,3},{1,2},{2,1},{3,0},{4,7},{5,6},{6,5},{7,4},{8,11},{9,10},{10,... | collective-permute-start | bytes 294920 | tf_op jit(solution)/shard_map/ppermute | solution.py:668
  82.3 13.0 %collective-permute-start.14 = (f32[48,512]{1,0:T(8,128)S(1)}, f32[48,512]{1,0:T(8,128)S(1)}, u32[]{:S(2)}, u32[]{:S(2)}) collective-permute-start(f32[48,512]{1,0:T(8,128)S(1)} %get-tuple-element.32), channel_id=1, source_target_pairs={{0,2},{1,3},{2,0},{3,1},{4,6},{5,7},{6,4},{7,5},{8,10},{9,11},{10,... | collective-permute-start | bytes 294920 | tf_op jit(solution)/shard_map/ppermute | solution.py:668
  82.9 12.4 %collective-permute-start.15 = (f32[48,512]{1,0:T(8,128)S(1)}, f32[48,512]{1,0:T(8,128)S(1)}, u32[]{:S(2)}, u32[]{:S(2)}) collective-permute-start(f32[48,512]{1,0:T(8,128)S(1)} %get-tuple-element.33), channel_id=1, source_target_pairs={{0,1},{1,0},{2,3},{3,2},{4,5},{5,4},{6,7},{7,6},{8,9},{9,8},{10,11... | collective-permute-start | bytes 294920 | tf_op jit(solution)/shard_map/ppermute | solution.py:668
  93.4 3.8 %collective-permute-start.18 = (bf16[48,384]{1,0:T(8,128)(2,1)S(1)}, bf16[48,384]{1,0:T(8,128)(2,1)S(1)}, u32[]{:S(2)}, u32[]{:S(2)}) collective-permute-start(bf16[48,384]{1,0:T(8,128)(2,1)S(1)} %get-tuple-element.38), channel_id=1, source_target_pairs={{0,3},{1,2},{2,1},{3,0},{4,7},{5,6},{6,5},{7,4},{8,11},{9,10},{10,... | collective-permute-start | bytes 110600 | tf_op jit(solution)/shard_map/ppermute | solution.py:668
  94.0 4.3 %collective-permute-start.19 = (bf16[48,384]{1,0:T(8,128)(2,1)S(1)}, bf16[48,384]{1,0:T(8,128)(2,1)S(1)}, u32[]{:S(2)}, u32[]{:S(2)}) collective-permute-start(bf16[48,384]{1,0:T(8,128)(2,1)S(1)} %get-tuple-element.39), channel_id=1, source_target_pairs={{0,2},{1,3},{2,0},{3,1},{4,6},{5,7},{6,4},{7,5},{8,10},{9,11},{10,... | collective-permute-start | bytes 110600 | tf_op jit(solution)/shard_map/ppermute | solution.py:668
  95.0 3.3 %collective-permute-start.20 = (bf16[48,384]{1,0:T(8,128)(2,1)S(1)}, bf16[48,384]{1,0:T(8,128)(2,1)S(1)}, u32[]{:S(2)}, u32[]{:S(2)}) collective-permute-start(bf16[48,384]{1,0:T(8,128)(2,1)S(1)} %get-tuple-element.40), channel_id=1, source_target_pairs={{0,1},{1,0},{2,3},{3,2},{4,5},{5,4},{6,7},{7,6},{8,9},{9,8},{10,11... | collective-permute-start | bytes 110600 | tf_op jit(solution)/shard_map/ppermute | solution.py:668

commit v18 on v17

--- a/solution.py
+++ b/solution.py
@@ -109,7 +109,7 @@
 
 def front_kernel(
     index_ref, unit_ref, bias_ref, own_hbm, x_hbm, core_hbm, last_hbm, first_hbm, second_hbm, protos_hbm,
-    tops_ref, keep_ref, give_ref, first_ref, second_ref, rows_ref, protos_ref, top_ref, sems, chunk_sems,
+    tops_ref, keep_ref, give_ref, first_ref, second_ref, rows_ref, protos_ref, padded_ref, top_ref, sems, chunk_sems,
 ):
     rows = unit_ref.shape[0]
     steps, block = protos_ref.shape[:2]
@@ -124,19 +124,21 @@
     copies.append(pltpu.make_async_copy(second_hbm, second_ref, sems.at[5]))
     for copy in copies:
         copy.start()
+    padded_ref[...] = jnp.zeros(padded_ref.shape, jnp.bfloat16)
+    padded_ref[:rows, :] = unit_ref[...]
     top_ref[...] = jnp.full(top_ref.shape, -jnp.inf, jnp.float32)
 
     def step(index, carry):
         arrived(index)
-        top = top_ref[:rows, :]
+        top = top_ref[...]
         for start in range(0, block, wide):
-            products = scores(unit_ref[...], protos_ref[index, start : start + wide, :])
-            top = jnp.maximum(top, lane_fold(products, jnp.maximum))
-        top_ref[:rows, :] = top
+            products = scores(protos_ref[index, start : start + wide, :], padded_ref[...])
+            top = jnp.maximum(top, jnp.max(products.reshape(-1, 8, products.shape[1]), axis=0))
+        top_ref[...] = top
         return carry
 
     lax.fori_loop(0, steps, step, 0)
-    tops = jnp.max(jnp.transpose(top_ref[...]), axis=0, keepdims=True)
+    tops = jnp.max(top_ref[...], axis=0, keepdims=True)
     tops_ref[...] = jnp.broadcast_to(tops[None], tops_ref.shape)
     for copy in copies:
         copy.wait()
@@ -167,7 +169,8 @@
             pltpu.VMEM(second.shape, jnp.bfloat16),
             pltpu.VMEM((4 * share, features), jnp.bfloat16),
             pltpu.VMEM((steps, count // steps, width), jnp.bfloat16),
-            pltpu.VMEM((256, 128), jnp.float32),
+            pltpu.VMEM((256, width), jnp.bfloat16),
+            pltpu.VMEM((8, 256), jnp.float32),
             pltpu.SemaphoreType.DMA((6,)),
             pltpu.SemaphoreType.DMA((steps,)),
         ],

time: 99.6 us -> 99.3 us (level)
  no operation moved by 1% of the time
where the time goes in v18:
time: 99.3 us; the launch traced here: 98.8 us
  Pallas kernels  45.9 us (46%)
  starting transfers between devices  29 us (29%)
  waiting for transfers between devices  23.3 us (23%)
    ppermute x21, starting transfers between devices, swap(): lax.ppermute(values, axis, [(i, i ^ flip) for i in range(lax.axis_size(ax...  17.2 us
    ppermute x21, waiting for transfers between devices, swap(): lax.ppermute(values, axis, [(i, i ^ flip) for i in range(lax.axis_size(ax...  12.9 us
    all_to_all x4, starting transfers between devices, all_to_all(): return lax.all_to_all(copies, axes, 0, 0, tiled=True)  11.8 us
    all_to_all x4, waiting for transfers between devices, all_to_all(): return lax.all_to_all(copies, axes, 0, 0, tiled=True)  10.4 us
    pallas_call x2, Pallas kernels, attract(): pl.pallas_call(functools.partial(attract_kernel, first_row, outputs > 1),...  10.2 us
    pallas_call x1, Pallas kernels, repel(): pl.pallas_call(skipping(functools.partial(repel_kernel, proto_size), 5, l...  9.45 us
    pallas_call x1, Pallas kernels, front(): pl.pallas_call(skipping(front_kernel, 10, len(order)), in_specs=[whole(pl...  7.82 us
    pallas_call x1, Pallas kernels, first_sweep(): pl.pallas_call(skipping(functools.partial(first_sweep_kernel, chunk, prot...  6.8 us
  transfers between devices with their start and end apart: 25, of which 11 were waited for; matrix products, arithmetic and copies ran while one was open for 0% of the time, Pallas kernels for 33%

profile of v18, /device:TPU:0, one launch (start us, length us, event | category | flops | bytes accessed | tf_op | source)
XLA Modules:
  0.0 98.8 jit_solution(18275168011088074259)
XLA Ops:
  0.0 1.0 %teacher_units.1 = (bf16[192,256]{1,0:T(8,128)(2,1)S(1)}, bf16[96,256]{1,0:T(8,128)(2,1)S(1)}) custom-call(s32[1]{0:T(128)} %bitcast.1.core_ref, bf16[192,256]{1,0:T(8,128)(2,1)} %emb_ref.1), custom_call_target="tpu_custom_call" | custom-call | flops 196608 | bytes 393216 | tf_op jit(solution)/shard_map/teacher_units/pallas_call | solution.py:96
  1.0 4.1 %collective-permute-start.3 = (bf16[96,256]{1,0:T(8,128)(2,1)S(1)}, bf16[96,256]{1,0:T(8,128)(2,1)S(1)}, u32[]{:S(2)}, u32[]{:S(2)}) collective-permute-start(bf16[96,256]{1,0:T(8,128)(2,1)S(1)} %get-tuple-element.24), channel_id=1, source_target_pairs={{0,16},{4,20},{8,24},{12,28},{16,0},{20,4},{24,8},{28,12},{1,17},{... | collective-permute-start | bytes 147464 | tf_op jit(solution)/shard_map/ppermute | solution.py:671
  5.1 1.5 %collective-permute-start = (bf16[48,1536]{1,0:T(8,128)(2,1)}, bf16[48,1536]{1,0:T(8,128)(2,1)S(1)}, u32[]{:S(2)}, u32[]{:S(2)}) collective-permute-start(bf16[48,1536]{1,0:T(8,128)(2,1)} %refs_3_.1), channel_id=1, source_target_pairs={{0,2},{1,3},{2,0},{3,1},{4,6},{5,7},{6,4},{7,5},{8,10},{9,11},{10,... | collective-permute-start | bytes 442376 | tf_op jit(solution)/shard_map/ppermute | solution.py:671
  6.6 0.5 collective-permute-start.5
  7.2 0.6 collective-permute-done.3
  7.8 1.4 %collective-permute-start.4 = (bf16[192,256]{1,0:T(8,128)(2,1)S(1)}, bf16[192,256]{1,0:T(8,128)(2,1)S(1)}, u32[]{:S(2)}, u32[]{:S(2)}) collective-permute-start(bf16[192,256]{1,0:T(8,128)(2,1)S(1)} %maximum_select_fusion.2), channel_id=1, source_target_pairs={{0,8},{4,12},{8,0},{12,4},{16,24},{20,28},{24,16},{28,20},{1,9},{5... | collective-permute-start | bytes 294920 | tf_op jit(solution)/shard_map/ppermute | solution.py:671
  9.2 0.0 collective-permute-start.1
  9.2 2.9 %collective-permute-done.refs_4_ = bf16[48,1536]{1,0:T(8,128)(2,1)S(1)} collective-permute-done((bf16[48,1536]{1,0:T(8,128)(2,1)}, bf16[48,1536]{1,0:T(8,128)(2,1)S(1)}, u32[]{:S(2)}, u32[]{:S(2)}) %collective-permute-start) | collective-permute-done | bytes 147488 | tf_op jit(solution)/shard_map/ppermute | solution.py:671
  12.1 0.0 collective-permute-start.2
  12.1 0.3 collective-permute-done.4
  12.4 0.1 maximum_select_fusion.1.refs_10_
  12.5 0.0 collective-permute-done.1.refs_5_
  12.5 3.8 %collective-permute-done.5.refs_11_.partner_ref = bf16[512,256]{1,0:T(8,128)(2,1)S(1)} collective-permute-done((bf16[512,256]{1,0:T(8,128)(2,1)}, bf16[512,256]{1,0:T(8,128)(2,1)S(1)}, u32[]{:S(2)}, u32[]{:S(2)}) %collective-permute-start.5) | collective-permute-done | bytes 262176 | tf_op jit(solution)/shard_map/ppermute | solution.py:671
  16.3 0.0 collective-permute-done.2.refs_6_
  16.3 7.8 %front.1 = (f32[32,1,256]{2,1,0:T(1,128)}, f32[96,2048]{1,0:T(8,128)S(1)}, f32[96,2048]{1,0:T(8,128)}) custom-call(s32[1]{0:T(128)} %bitcast.refs_0_.index_ref, bf16[192,256]{1,0:T(8,128)(2,1)S(1)} %get-tuple-element.23.refs_1_, f32[1,2048]{1,0:T(1,128)} %bitcast.7, bf16[48,1536]{1,0:T(8,128)(2,1)} %refs_3_.1, ...), custom_call_target="tpu_custom_call" | custom-call | flops 2315255808 | bytes 8388608 | tf_op jit(solution)/shard_map/front/pallas_call | solution.py:161
  24.1 0.1 collective-permute-start.6
  24.2 1.6 %collective-permute-start.16 = (bf16[384,256]{1,0:T(8,128)(2,1)S(1)}, bf16[384,256]{1,0:T(8,128)(2,1)S(1)}, u32[]{:S(2)}, u32[]{:S(2)}) collective-permute-start(bf16[384,256]{1,0:T(8,128)(2,1)S(1)} %maximum_select_fusion.1.refs_10_), channel_id=1, source_target_pairs={{0,4},{4,0},{8,12},{12,8},{16,20},{20,16},{24,28},{28,24},{1,5},{5... | collective-permute-start | bytes 589832 | tf_op jit(solution)/shard_map/ppermute | solution.py:671
  25.8 0.2 collective-permute-start.8
  25.9 0.3 collective-permute-start.9
  26.3 2.9 %all-to-all-start = ((f32[32,1,256]{2,1,0:T(1,128)}), f32[32,1,256]{2,1,0:T(1,128)S(1)}, u32[]{:S(2)}, u32[]{:S(2)}) async-start(f32[32,1,256]{2,1,0:T(1,128)} %get-tuple-element.34), calls=%async_computation | async-start | bytes 65536 | tf_op jit(solution)/shard_map/all_to_all | solution.py:701
  29.2 2.3 %collective-permute-done.16 = bf16[384,256]{1,0:T(8,128)(2,1)S(1)} collective-permute-done((bf16[384,256]{1,0:T(8,128)(2,1)S(1)}, bf16[384,256]{1,0:T(8,128)(2,1)S(1)}, u32[]{:S(2)}, u32[]{:S(2)}) %collective-permute-start.16) | collective-permute-done | bytes 196640 | tf_op jit(solution)/shard_map/ppermute | solution.py:671
  31.5 0.2 maximum_select_fusion.refs_2_
  31.7 0.1 collective-permute-start.17
  31.7 0.0 collective-permute-done.6.core_ref
  31.8 1.6 %collective-permute-start.7 = (f32[48,2048]{1,0:T(8,128)S(1)}, f32[48,2048]{1,0:T(8,128)}, u32[]{:S(2)}, u32[]{:S(2)}) collective-permute-start(f32[48,2048]{1,0:T(8,128)S(1)} %slice_add_fusion.refs_5_), channel_id=1, source_target_pairs={{0,2},{1,3},{2,0},{3,1},{4,6},{5,7},{6,4},{7,5},{8,10},{9,11},{10,... | collective-permute-start | bytes 1179656 | tf_op jit(solution)/shard_map/ppermute | solution.py:671
  33.4 0.1 pad_add_fusion.1.refs_0_
  33.5 0.0 collective-permute-done.8.other_ref.refs_6_
  33.5 3.0 %all-to-all-done.refs_4_.refs_2_ = f32[32,1,256]{2,1,0:T(1,128)S(1)} async-done(((f32[32,1,256]{2,1,0:T(1,128)}), f32[32,1,256]{2,1,0:T(1,128)S(1)}, u32[]{:S(2)}, u32[]{:S(2)}) %all-to-all-start) | async-done | bytes 32800 | tf_op jit(solution)/shard_map/all_to_all | solution.py:701
  36.4 0.0 collective-permute-done.9.last_ref.refs_7_
  36.4 0.0 collective-permute-done.17.refs_3_
  36.4 6.8 %first_sweep.1 = (bf16[32,16,128]{2,1,0:T(8,128)(2,1)}, bf16[2048,1536]{1,0:T(8,128)(2,1)}) custom-call(s32[2]{0:T(128)S(1)} %pad_add_fusion.1.refs_0_, bf16[16384,256]{1,0:T(8,128)(2,1)} %refs_4_.1, bf16[768,256]{1,0:T(8,128)(2,1)S(1)} %maximum_select_fusion.refs_2_, bf16[768,256]{1,0:T(8,128)(2,1)} %collective-permute-done.17.refs_3_, ...), custom_call_target="tpu_custom_call" | custom-call | flops 1610612736 | bytes 6291456 | tf_op jit(solution)/shard_map/first_sweep/pallas_call | solution.py:453
  43.2 2.6 %all-to-all-start.1 = ((bf16[32,16,128]{2,1,0:T(8,128)(2,1)}), bf16[32,16,128]{2,1,0:T(8,128)(2,1)S(1)}, u32[]{:S(2)}, u32[]{:S(2)}) async-start(bf16[32,16,128]{2,1,0:T(8,128)(2,1)} %get-tuple-element.36), calls=%async_computation.1 | async-start | bytes 262144 | tf_op jit(solution)/shard_map/all_to_all | solution.py:701
  45.8 0.0 collective-permute-done.7.x_ref
  45.9 1.7 %student_middle.1 = (f32[48,256]{1,0:T(8,128)S(1)}, bf16[48,256]{1,0:T(8,128)(2,1)S(1)}, f32[48,128]{1,0:T(8,128)S(1)}) custom-call(s32[1]{0:T(128)} %bitcast.refs_0_.index_ref, f32[96,2048]{1,0:T(8,128)S(1)} %get-tuple-element.25.keep_ref, f32[96,2048]{1,0:T(8,128)S(1)} %collective-permute-done.6.core_ref, f32[48,2048]{1,0:T(8,128)} %collective-permute-done.7.x_ref, ...), custom_call_target="tpu_custom_call" | custom-call | flops 50331648 | bytes 2621440 | tf_op jit(solution)/shard_map/student_middle/pallas_call | solution.py:619
  47.5 1.5 %collective-permute-start.12 = (bf16[48,256]{1,0:T(8,128)(2,1)S(1)}, bf16[48,256]{1,0:T(8,128)(2,1)S(1)}, u32[]{:S(2)}, u32[]{:S(2)}) collective-permute-start(bf16[48,256]{1,0:T(8,128)(2,1)S(1)} %get-tuple-element.29.refs_2_), channel_id=1, source_target_pairs={{0,3},{1,2},{2,1},{3,0},{4,7},{5,6},{6,5},{7,4},{8,11},{9,10},{10,... | collective-permute-start | bytes 73736 | tf_op jit(solution)/shard_map/ppermute | solution.py:671
  49.0 0.4 collective-permute-start.11
  49.3 0.1 collective-permute-start.10
  49.5 4.6 %all-to-all-done.1.refs_1_ = bf16[32,16,128]{2,1,0:T(8,128)(2,1)S(1)} async-done(((bf16[32,16,128]{2,1,0:T(8,128)(2,1)}), bf16[32,16,128]{2,1,0:T(8,128)(2,1)S(1)}, u32[]{:S(2)}, u32[]{:S(2)}) %all-to-all-start.1) | async-done | bytes 131104 | tf_op jit(solution)/shard_map/all_to_all | solution.py:701
  54.1 4.4 %next_sweep.1 = bf16[32,16,128]{2,1,0:T(8,128)(2,1)} custom-call(bf16[2048,1536]{1,0:T(8,128)(2,1)} %get-tuple-element.35.refs_0_, bf16[32,16,128]{2,1,0:T(8,128)(2,1)S(1)} %all-to-all-done.1.refs_1_, bf16[48,256]{1,0:T(8,128)(2,1)S(1)} %get-tuple-element.29.refs_2_), custom_call_target="tpu_custom_call" | custom-call | flops 25165824 | bytes 6291456 | tf_op jit(solution)/shard_map/next_sweep/pallas_call | solution.py:539
  58.5 2.6 %all-to-all-start.2 = ((bf16[32,16,128]{2,1,0:T(8,128)(2,1)}), bf16[32,16,128]{2,1,0:T(8,128)(2,1)S(1)}, u32[]{:S(2)}, u32[]{:S(2)}) async-start(bf16[32,16,128]{2,1,0:T(8,128)(2,1)} %next_sweep.1), calls=%async_computation.2 | async-start | bytes 262144 | tf_op jit(solution)/shard_map/all_to_all | solution.py:701
  61.0 0.0 collective-permute-done.10
  61.1 0.0 collective-permute-done.11
  61.1 0.0 collective-permute-done.12
  61.2 6.0 %attract.2.state_ref.refs_2_ = f32[192,512]{1,0:T(8,128)S(1)} custom-call(bf16[192,256]{1,0:T(8,128)(2,1)S(1)} %constant_dynamic-update-slice_fusion.emb_ref, f32[192,512]{1,0:T(8,128)S(1)} %concatenate.32.state_ref, bf16[16384,256]{1,0:T(8,128)(2,1)} %refs_4_.1), custom_call_target="tpu_custom_call" | custom-call | flops 2013265920 | bytes 5242880 | tf_op jit(solution)/shard_map/attract/pallas_call | solution.py:327
  67.1 2.1 %all-to-all-done.2.refs_1_ = bf16[32,16,128]{2,1,0:T(8,128)(2,1)S(1)} async-done(((bf16[32,16,128]{2,1,0:T(8,128)(2,1)}), bf16[32,16,128]{2,1,0:T(8,128)(2,1)S(1)}, u32[]{:S(2)}, u32[]{:S(2)}) %all-to-all-start.2) | async-done | bytes 131104 | tf_op jit(solution)/shard_map/all_to_all | solution.py:701
  69.3 3.8 %last_scales.1 = f32[8,1,2048]{2,1,0:T(1,128)} custom-call(bf16[2048,1536]{1,0:T(8,128)(2,1)} %get-tuple-element.35.refs_0_, bf16[32,16,128]{2,1,0:T(8,128)(2,1)S(1)} %all-to-all-done.2.refs_1_, f32[192,512]{1,0:T(8,128)S(1)} %attract.2.state_ref.refs_2_), custom_call_target="tpu_custom_call" | custom-call | flops 12582912 | bytes 6291456 | tf_op jit(solution)/shard_map/last_scales/pallas_call | solution.py:578
  73.0 3.7 %all-to-all-start.3 = ((f32[8,1,2048]{2,1,0:T(1,128)}), f32[8,1,2048]{2,1,0:T(1,128)S(1)}, u32[]{:S(2)}, u32[]{:S(2)}) async-start(f32[8,1,2048]{2,1,0:T(1,128)} %last_scales.1), calls=%async_computation.3 | async-start | bytes 131072 | tf_op jit(solution)/shard_map/all_to_all | solution.py:701
  76.7 0.1 pad_add_fusion.refs_0_
  76.8 4.2 %attract.3 = (f32[48,512]{1,0:T(8,128)S(1)}, f32[48,512]{1,0:T(8,128)S(1)}, f32[48,512]{1,0:T(8,128)S(1)}, f32[48,512]{1,0:T(8,128)S(1)}) custom-call(bf16[192,256]{1,0:T(8,128)(2,1)S(1)} %constant_dynamic-update-slice_fusion.emb_ref, f32[192,512]{1,0:T(8,128)S(1)} %attract.2.state_ref.refs_2_, bf16[16384,256]{1,0:T(8,128)(2,1)} %refs_4_.1), custom_call_target="tpu_custom_call" | custom-call | flops 1207959552 | bytes 3145728 | tf_op jit(solution)/shard_map/attract/pallas_call | solution.py:327
  81.0 1.0 %collective-permute-start.13 = (f32[48,512]{1,0:T(8,128)S(1)}, f32[48,512]{1,0:T(8,128)S(1)}, u32[]{:S(2)}, u32[]{:S(2)}) collective-permute-start(f32[48,512]{1,0:T(8,128)S(1)} %get-tuple-element.31), channel_id=1, source_target_pairs={{0,3},{1,2},{2,1},{3,0},{4,7},{5,6},{6,5},{7,4},{8,11},{9,10},{10,... | collective-permute-start | bytes 294920 | tf_op jit(solution)/shard_map/ppermute | solution.py:671
  82.0 0.6 collective-permute-start.14
  82.6 0.3 collective-permute-start.15
  82.9 0.7 all-to-all-done.3.refs_3_
  83.7 9.5 %repel.1 = (f32[48,384]{1,0:T(8,128)S(1)}, bf16[48,384]{1,0:T(8,128)(2,1)S(1)}, bf16[48,384]{1,0:T(8,128)(2,1)S(1)}, bf16[48,384]{1,0:T(8,128)(2,1)S(1)}) custom-call(s32[2]{0:T(128)S(1)} %pad_add_fusion.refs_0_, bf16[192,256]{1,0:T(8,128)(2,1)S(1)} %get-tuple-element.23.refs_1_, f32[32,1,256]{2,1,0:T(1,128)S(1)} %all-to-all-done.refs_4_.refs_2_, ...), custom_call_target="tpu_custom_call" | custom-call | flops 3221225472 | bytes 8388608 | tf_op jit(solution)/shard_map/repel/pallas_call | solution.py:246
  93.1 0.6 collective-permute-start.18
  93.7 1.0 %collective-permute-start.19 = (bf16[48,384]{1,0:T(8,128)(2,1)S(1)}, bf16[48,384]{1,0:T(8,128)(2,1)S(1)}, u32[]{:S(2)}, u32[]{:S(2)}) collective-permute-start(bf16[48,384]{1,0:T(8,128)(2,1)S(1)} %get-tuple-element.39), channel_id=1, source_target_pairs={{0,2},{1,3},{2,0},{3,1},{4,6},{5,7},{6,4},{7,5},{8,10},{9,11},{10,... | collective-permute-start | bytes 110600 | tf_op jit(solution)/shard_map/ppermute | solution.py:671
  94.7 0.0 collective-permute-done.13.rest_1_
  94.7 0.3 collective-permute-start.20
  95.0 0.0 collective-permute-done.14.rest_2_
  95.0 0.0 collective-permute-done.15.rest_3_
  95.1 1.9 %collective-permute-done.18.rest_5_ = bf16[48,384]{1,0:T(8,128)(2,1)S(1)} collective-permute-done((bf16[48,384]{1,0:T(8,128)(2,1)S(1)}, bf16[48,384]{1,0:T(8,128)(2,1)S(1)}, u32[]{:S(2)}, u32[]{:S(2)}) %collective-permute-start.18) | collective-permute-done | bytes 36896 | tf_op jit(solution)/shard_map/ppermute | solution.py:671
  96.9 1.1 %collective-permute-done.19.rest_6_ = bf16[48,384]{1,0:T(8,128)(2,1)S(1)} collective-permute-done((bf16[48,384]{1,0:T(8,128)(2,1)S(1)}, bf16[48,384]{1,0:T(8,128)(2,1)S(1)}, u32[]{:S(2)}, u32[]{:S(2)}) %collective-permute-start.19) | collective-permute-done | bytes 36896 | tf_op jit(solution)/shard_map/ppermute | solution.py:671
  98.0 0.0 collective-permute-done.20.rest_7_
  98.0 0.8 finish.1
  (9 shorter events, 0.1 us)
Async XLA Ops:
  1.0 6.7 %collective-permute-start.3 = (bf16[96,256]{1,0:T(8,128)(2,1)S(1)}, bf16[96,256]{1,0:T(8,128)(2,1)S(1)}, u32[]{:S(2)}, u32[]{:S(2)}) collective-permute-start(bf16[96,256]{1,0:T(8,128)(2,1)S(1)} %get-tuple-element.24), channel_id=1, source_target_pairs={{0,16},{4,20},{8,24},{12,28},{16,0},{20,4},{24,8},{28,12},{1,17},{... | collective-permute-start | bytes 147464 | tf_op jit(solution)/shard_map/ppermute | solution.py:671
  5.1 7.0 %collective-permute-start = (bf16[48,1536]{1,0:T(8,128)(2,1)}, bf16[48,1536]{1,0:T(8,128)(2,1)S(1)}, u32[]{:S(2)}, u32[]{:S(2)}) collective-permute-start(bf16[48,1536]{1,0:T(8,128)(2,1)} %refs_3_.1), channel_id=1, source_target_pairs={{0,2},{1,3},{2,0},{3,1},{4,6},{5,7},{6,4},{7,5},{8,10},{9,11},{10,... | collective-permute-start | bytes 442376 | tf_op jit(solution)/shard_map/ppermute | solution.py:671
  6.6 9.6 %collective-permute-start.5 = (bf16[512,256]{1,0:T(8,128)(2,1)}, bf16[512,256]{1,0:T(8,128)(2,1)S(1)}, u32[]{:S(2)}, u32[]{:S(2)}) collective-permute-start(bf16[512,256]{1,0:T(8,128)(2,1)} %own_ref.1), channel_id=1, source_target_pairs={{0,2},{1,3},{2,0},{3,1},{4,6},{5,7},{6,4},{7,5},{8,10},{9,11},{10,... | collective-permute-start | bytes 786440 | tf_op jit(solution)/shard_map/ppermute | solution.py:671
  7.8 4.7 %collective-permute-start.4 = (bf16[192,256]{1,0:T(8,128)(2,1)S(1)}, bf16[192,256]{1,0:T(8,128)(2,1)S(1)}, u32[]{:S(2)}, u32[]{:S(2)}) collective-permute-start(bf16[192,256]{1,0:T(8,128)(2,1)S(1)} %maximum_select_fusion.2), channel_id=1, source_target_pairs={{0,8},{4,12},{8,0},{12,4},{16,24},{20,28},{24,16},{28,20},{1,9},{5... | collective-permute-start | bytes 294920 | tf_op jit(solution)/shard_map/ppermute | solution.py:671
  9.2 3.3 %collective-permute-start.1 = (bf16[48,1536]{1,0:T(8,128)(2,1)}, bf16[48,1536]{1,0:T(8,128)(2,1)S(1)}, u32[]{:S(2)}, u32[]{:S(2)}) collective-permute-start(bf16[48,1536]{1,0:T(8,128)(2,1)} %refs_3_.1), channel_id=1, source_target_pairs={{0,1},{1,0},{2,3},{3,2},{4,5},{5,4},{6,7},{7,6},{8,9},{9,8},{10,11... | collective-permute-start | bytes 442376 | tf_op jit(solution)/shard_map/ppermute | solution.py:671
  12.1 4.2 %collective-permute-start.2 = (bf16[48,1536]{1,0:T(8,128)(2,1)S(1)}, bf16[48,1536]{1,0:T(8,128)(2,1)S(1)}, u32[]{:S(2)}, u32[]{:S(2)}) collective-permute-start(bf16[48,1536]{1,0:T(8,128)(2,1)S(1)} %collective-permute-done.refs_4_), channel_id=1, source_target_pairs={{0,1},{1,0},{2,3},{3,2},{4,5},{5,4},{6,7},{7,6},{8,9},{9,8},{10,11... | collective-permute-start | bytes 442376 | tf_op jit(solution)/shard_map/ppermute | solution.py:671
  24.1 7.6 %collective-permute-start.6 = (f32[96,2048]{1,0:T(8,128)}, f32[96,2048]{1,0:T(8,128)S(1)}, u32[]{:S(2)}, u32[]{:S(2)}) collective-permute-start(f32[96,2048]{1,0:T(8,128)} %get-tuple-element.26), channel_id=1, source_target_pairs={{0,1},{1,0},{2,3},{3,2},{4,5},{5,4},{6,7},{7,6},{8,9},{9,8},{10,11... | collective-permute-start | bytes 2359304 | tf_op jit(solution)/shard_map/ppermute | solution.py:671
  24.2 7.3 %collective-permute-start.16 = (bf16[384,256]{1,0:T(8,128)(2,1)S(1)}, bf16[384,256]{1,0:T(8,128)(2,1)S(1)}, u32[]{:S(2)}, u32[]{:S(2)}) collective-permute-start(bf16[384,256]{1,0:T(8,128)(2,1)S(1)} %maximum_select_fusion.1.refs_10_), channel_id=1, source_target_pairs={{0,4},{4,0},{8,12},{12,8},{16,20},{20,16},{24,28},{28,24},{1,5},{5... | collective-permute-start | bytes 589832 | tf_op jit(solution)/shard_map/ppermute | solution.py:671
  25.8 7.7 %collective-permute-start.8 = (bf16[512,256]{1,0:T(8,128)(2,1)}, bf16[512,256]{1,0:T(8,128)(2,1)S(1)}, u32[]{:S(2)}, u32[]{:S(2)}) collective-permute-start(bf16[512,256]{1,0:T(8,128)(2,1)} %own_ref.1), channel_id=1, source_target_pairs={{0,1},{1,0},{2,3},{3,2},{4,5},{5,4},{6,7},{7,6},{8,9},{9,8},{10,11... | collective-permute-start | bytes 786440 | tf_op jit(solution)/shard_map/ppermute | solution.py:671
  25.9 10.5 %collective-permute-start.9 = (bf16[512,256]{1,0:T(8,128)(2,1)S(1)}, bf16[512,256]{1,0:T(8,128)(2,1)S(1)}, u32[]{:S(2)}, u32[]{:S(2)}) collective-permute-start(bf16[512,256]{1,0:T(8,128)(2,1)S(1)} %collective-permute-done.5.refs_11_.partner_ref), channel_id=1, source_target_pairs={{0,1},{1,0},{2,3},{3,2},{4,5},{5,4},{6,7},{7,6},{8,9},{9,8},{10,11... | collective-permute-start | bytes 786440 | tf_op jit(solution)/shard_map/ppermute | solution.py:671
  26.3 10.1 %all-to-all-start = ((f32[32,1,256]{2,1,0:T(1,128)}), f32[32,1,256]{2,1,0:T(1,128)S(1)}, u32[]{:S(2)}, u32[]{:S(2)}) async-start(f32[32,1,256]{2,1,0:T(1,128)} %get-tuple-element.34), calls=%async_computation | async-start | bytes 65536 | tf_op jit(solution)/shard_map/all_to_all | solution.py:701
  31.7 4.8 %collective-permute-start.17 = (bf16[768,256]{1,0:T(8,128)(2,1)S(1)}, bf16[768,256]{1,0:T(8,128)(2,1)}, u32[]{:S(2)}, u32[]{:S(2)}) collective-permute-start(bf16[768,256]{1,0:T(8,128)(2,1)S(1)} %maximum_select_fusion.refs_2_), channel_id=1, source_target_pairs={{0,1},{1,0},{2,3},{3,2},{4,5},{5,4},{6,7},{7,6},{8,9},{9,8},{10,11... | collective-permute-start | bytes 1179656 | tf_op jit(solution)/shard_map/ppermute | solution.py:671
  31.8 14.1 %collective-permute-start.7 = (f32[48,2048]{1,0:T(8,128)S(1)}, f32[48,2048]{1,0:T(8,128)}, u32[]{:S(2)}, u32[]{:S(2)}) collective-permute-start(f32[48,2048]{1,0:T(8,128)S(1)} %slice_add_fusion.refs_5_), channel_id=1, source_target_pairs={{0,2},{1,3},{2,0},{3,1},{4,6},{5,7},{6,4},{7,5},{8,10},{9,11},{10,... | collective-permute-start | bytes 1179656 | tf_op jit(solution)/shard_map/ppermute | solution.py:671
  43.2 10.8 %all-to-all-start.1 = ((bf16[32,16,128]{2,1,0:T(8,128)(2,1)}), bf16[32,16,128]{2,1,0:T(8,128)(2,1)S(1)}, u32[]{:S(2)}, u32[]{:S(2)}) async-start(bf16[32,16,128]{2,1,0:T(8,128)(2,1)} %get-tuple-element.36), calls=%async_computation.1 | async-start | bytes 262144 | tf_op jit(solution)/shard_map/all_to_all | solution.py:701
  47.5 13.6 %collective-permute-start.12 = (bf16[48,256]{1,0:T(8,128)(2,1)S(1)}, bf16[48,256]{1,0:T(8,128)(2,1)S(1)}, u32[]{:S(2)}, u32[]{:S(2)}) collective-permute-start(bf16[48,256]{1,0:T(8,128)(2,1)S(1)} %get-tuple-element.29.refs_2_), channel_id=1, source_target_pairs={{0,3},{1,2},{2,1},{3,0},{4,7},{5,6},{6,5},{7,4},{8,11},{9,10},{10,... | collective-permute-start | bytes 73736 | tf_op jit(solution)/shard_map/ppermute | solution.py:671
  49.0 12.1 %collective-permute-start.11 = (bf16[48,256]{1,0:T(8,128)(2,1)S(1)}, bf16[48,256]{1,0:T(8,128)(2,1)S(1)}, u32[]{:S(2)}, u32[]{:S(2)}) collective-permute-start(bf16[48,256]{1,0:T(8,128)(2,1)S(1)} %get-tuple-element.29.refs_2_), channel_id=1, source_target_pairs={{0,2},{1,3},{2,0},{3,1},{4,6},{5,7},{6,4},{7,5},{8,10},{9,11},{10,... | collective-permute-start | bytes 73736 | tf_op jit(solution)/shard_map/ppermute | solution.py:671
  49.3 11.7 %collective-permute-start.10 = (bf16[48,256]{1,0:T(8,128)(2,1)S(1)}, bf16[48,256]{1,0:T(8,128)(2,1)S(1)}, u32[]{:S(2)}, u32[]{:S(2)}) collective-permute-start(bf16[48,256]{1,0:T(8,128)(2,1)S(1)} %get-tuple-element.29.refs_2_), channel_id=1, source_target_pairs={{0,1},{1,0},{2,3},{3,2},{4,5},{5,4},{6,7},{7,6},{8,9},{9,8},{10,11... | collective-permute-start | bytes 73736 | tf_op jit(solution)/shard_map/ppermute | solution.py:671
  58.5 10.8 %all-to-all-start.2 = ((bf16[32,16,128]{2,1,0:T(8,128)(2,1)}), bf16[32,16,128]{2,1,0:T(8,128)(2,1)S(1)}, u32[]{:S(2)}, u32[]{:S(2)}) async-start(bf16[32,16,128]{2,1,0:T(8,128)(2,1)} %next_sweep.1), calls=%async_computation.2 | async-start | bytes 262144 | tf_op jit(solution)/shard_map/all_to_all | solution.py:701
  73.0 10.6 %all-to-all-start.3 = ((f32[8,1,2048]{2,1,0:T(1,128)}), f32[8,1,2048]{2,1,0:T(1,128)S(1)}, u32[]{:S(2)}, u32[]{:S(2)}) async-start(f32[8,1,2048]{2,1,0:T(1,128)} %last_scales.1), calls=%async_computation.3 | async-start | bytes 131072 | tf_op jit(solution)/shard_map/all_to_all | solution.py:701
  81.0 13.7 %collective-permute-start.13 = (f32[48,512]{1,0:T(8,128)S(1)}, f32[48,512]{1,0:T(8,128)S(1)}, u32[]{:S(2)}, u32[]{:S(2)}) collective-permute-start(f32[48,512]{1,0:T(8,128)S(1)} %get-tuple-element.31), channel_id=1, source_target_pairs={{0,3},{1,2},{2,1},{3,0},{4,7},{5,6},{6,5},{7,4},{8,11},{9,10},{10,... | collective-permute-start | bytes 294920 | tf_op jit(solution)/shard_map/ppermute | solution.py:671
  82.0 13.0 %collective-permute-start.14 = (f32[48,512]{1,0:T(8,128)S(1)}, f32[48,512]{1,0:T(8,128)S(1)}, u32[]{:S(2)}, u32[]{:S(2)}) collective-permute-start(f32[48,512]{1,0:T(8,128)S(1)} %get-tuple-element.32), channel_id=1, source_target_pairs={{0,2},{1,3},{2,0},{3,1},{4,6},{5,7},{6,4},{7,5},{8,10},{9,11},{10,... | collective-permute-start | bytes 294920 | tf_op jit(solution)/shard_map/ppermute | solution.py:671
  82.6 12.4 %collective-permute-start.15 = (f32[48,512]{1,0:T(8,128)S(1)}, f32[48,512]{1,0:T(8,128)S(1)}, u32[]{:S(2)}, u32[]{:S(2)}) collective-permute-start(f32[48,512]{1,0:T(8,128)S(1)} %get-tuple-element.33), channel_id=1, source_target_pairs={{0,1},{1,0},{2,3},{3,2},{4,5},{5,4},{6,7},{7,6},{8,9},{9,8},{10,11... | collective-permute-start | bytes 294920 | tf_op jit(solution)/shard_map/ppermute | solution.py:671
  93.1 3.8 %collective-permute-start.18 = (bf16[48,384]{1,0:T(8,128)(2,1)S(1)}, bf16[48,384]{1,0:T(8,128)(2,1)S(1)}, u32[]{:S(2)}, u32[]{:S(2)}) collective-permute-start(bf16[48,384]{1,0:T(8,128)(2,1)S(1)} %get-tuple-element.38), channel_id=1, source_target_pairs={{0,3},{1,2},{2,1},{3,0},{4,7},{5,6},{6,5},{7,4},{8,11},{9,10},{10,... | collective-permute-start | bytes 110600 | tf_op jit(solution)/shard_map/ppermute | solution.py:671
  93.7 4.3 %collective-permute-start.19 = (bf16[48,384]{1,0:T(8,128)(2,1)S(1)}, bf16[48,384]{1,0:T(8,128)(2,1)S(1)}, u32[]{:S(2)}, u32[]{:S(2)}) collective-permute-start(bf16[48,384]{1,0:T(8,128)(2,1)S(1)} %get-tuple-element.39), channel_id=1, source_target_pairs={{0,2},{1,3},{2,0},{3,1},{4,6},{5,7},{6,4},{7,5},{8,10},{9,11},{10,... | collective-permute-start | bytes 110600 | tf_op jit(solution)/shard_map/ppermute | solution.py:671
  94.7 3.3 %collective-permute-start.20 = (bf16[48,384]{1,0:T(8,128)(2,1)S(1)}, bf16[48,384]{1,0:T(8,128)(2,1)S(1)}, u32[]{:S(2)}, u32[]{:S(2)}) collective-permute-start(bf16[48,384]{1,0:T(8,128)(2,1)S(1)} %get-tuple-element.40), channel_id=1, source_target_pairs={{0,1},{1,0},{2,3},{3,2},{4,5},{5,4},{6,7},{7,6},{8,9},{9,8},{10,11... | collective-permute-start | bytes 110600 | tf_op jit(solution)/shard_map/ppermute | solution.py:671

commit v19 on v18

--- a/solution.py
+++ b/solution.py
@@ -113,7 +113,7 @@
 ):
     rows = unit_ref.shape[0]
     steps, block = protos_ref.shape[:2]
-    wide = min(WIDE, block)
+    wide = min(2 * WIDE, block)
     share = own_hbm.shape[0]
     arrived = fetch(protos_hbm, protos_ref, chunk_sems)
     copies = [

time: 99.3 us -> 99.2 us (level)
  no operation moved by 1% of the time
where the time goes in v19:
time: 99.2 us; the launch traced here: 98.8 us
  Pallas kernels  45.8 us (46%)
  starting transfers between devices  28.9 us (29%)
  waiting for transfers between devices  23.3 us (23%)
    ppermute x21, starting transfers between devices, swap(): lax.ppermute(values, axis, [(i, i ^ flip) for i in range(lax.axis_size(ax...  17.2 us
    ppermute x21, waiting for transfers between devices, swap(): lax.ppermute(values, axis, [(i, i ^ flip) for i in range(lax.axis_size(ax...  12.9 us
    all_to_all x4, starting transfers between devices, all_to_all(): return lax.all_to_all(copies, axes, 0, 0, tiled=True)  11.7 us
    all_to_all x4, waiting for transfers between devices, all_to_all(): return lax.all_to_all(copies, axes, 0, 0, tiled=True)  10.4 us
    pallas_call x2, Pallas kernels, attract(): pl.pallas_call(functools.partial(attract_kernel, first_row, outputs > 1),...  10.2 us
    pallas_call x1, Pallas kernels, repel(): pl.pallas_call(skipping(functools.partial(repel_kernel, proto_size), 5, l...  9.45 us
    pallas_call x1, Pallas kernels, front(): pl.pallas_call(skipping(front_kernel, 10, len(order)), in_specs=[whole(pl...  7.78 us
    pallas_call x1, Pallas kernels, first_sweep(): pl.pallas_call(skipping(functools.partial(first_sweep_kernel, chunk, prot...  6.8 us
  transfers between devices with their start and end apart: 25, of which 11 were waited for; matrix products, arithmetic and copies ran while one was open for 0% of the time, Pallas kernels for 33%

profile of v19, /device:TPU:0, one launch (start us, length us, event | category | flops | bytes accessed | tf_op | source)
XLA Modules:
  0.0 98.8 jit_solution(8571588514209691554)
XLA Ops:
  0.0 1.0 %teacher_units.1 = (bf16[192,256]{1,0:T(8,128)(2,1)S(1)}, bf16[96,256]{1,0:T(8,128)(2,1)S(1)}) custom-call(s32[1]{0:T(128)} %bitcast.1.core_ref, bf16[192,256]{1,0:T(8,128)(2,1)} %emb_ref.1), custom_call_target="tpu_custom_call" | custom-call | flops 196608 | bytes 393216 | tf_op jit(solution)/shard_map/teacher_units/pallas_call | solution.py:96
  1.0 4.1 %collective-permute-start.3 = (bf16[96,256]{1,0:T(8,128)(2,1)S(1)}, bf16[96,256]{1,0:T(8,128)(2,1)S(1)}, u32[]{:S(2)}, u32[]{:S(2)}) collective-permute-start(bf16[96,256]{1,0:T(8,128)(2,1)S(1)} %get-tuple-element.24), channel_id=1, source_target_pairs={{0,16},{4,20},{8,24},{12,28},{16,0},{20,4},{24,8},{28,12},{1,17},{... | collective-permute-start | bytes 147464 | tf_op jit(solution)/shard_map/ppermute | solution.py:671
  5.1 1.5 %collective-permute-start = (bf16[48,1536]{1,0:T(8,128)(2,1)}, bf16[48,1536]{1,0:T(8,128)(2,1)S(1)}, u32[]{:S(2)}, u32[]{:S(2)}) collective-permute-start(bf16[48,1536]{1,0:T(8,128)(2,1)} %refs_3_.1), channel_id=1, source_target_pairs={{0,2},{1,3},{2,0},{3,1},{4,6},{5,7},{6,4},{7,5},{8,10},{9,11},{10,... | collective-permute-start | bytes 442376 | tf_op jit(solution)/shard_map/ppermute | solution.py:671
  6.6 0.5 collective-permute-start.5
  7.2 0.6 collective-permute-done.3
  7.8 1.4 %collective-permute-start.4 = (bf16[192,256]{1,0:T(8,128)(2,1)S(1)}, bf16[192,256]{1,0:T(8,128)(2,1)S(1)}, u32[]{:S(2)}, u32[]{:S(2)}) collective-permute-start(bf16[192,256]{1,0:T(8,128)(2,1)S(1)} %maximum_select_fusion.2), channel_id=1, source_target_pairs={{0,8},{4,12},{8,0},{12,4},{16,24},{20,28},{24,16},{28,20},{1,9},{5... | collective-permute-start | bytes 294920 | tf_op jit(solution)/shard_map/ppermute | solution.py:671
  9.2 0.0 collective-permute-start.1
  9.2 2.9 %collective-permute-done.refs_4_ = bf16[48,1536]{1,0:T(8,128)(2,1)S(1)} collective-permute-done((bf16[48,1536]{1,0:T(8,128)(2,1)}, bf16[48,1536]{1,0:T(8,128)(2,1)S(1)}, u32[]{:S(2)}, u32[]{:S(2)}) %collective-permute-start) | collective-permute-done | bytes 147488 | tf_op jit(solution)/shard_map/ppermute | solution.py:671
  12.1 0.0 collective-permute-start.2
  12.1 0.3 collective-permute-done.4
  12.4 0.1 maximum_select_fusion.1.refs_10_
  12.5 0.0 collective-permute-done.1.refs_5_
  12.5 3.8 %collective-permute-done.5.refs_11_.partner_ref = bf16[512,256]{1,0:T(8,128)(2,1)S(1)} collective-permute-done((bf16[512,256]{1,0:T(8,128)(2,1)}, bf16[512,256]{1,0:T(8,128)(2,1)S(1)}, u32[]{:S(2)}, u32[]{:S(2)}) %collective-permute-start.5) | collective-permute-done | bytes 262176 | tf_op jit(solution)/shard_map/ppermute | solution.py:671
  16.3 0.0 collective-permute-done.2.refs_6_
  16.3 7.8 %front.1 = (f32[32,1,256]{2,1,0:T(1,128)}, f32[96,2048]{1,0:T(8,128)S(1)}, f32[96,2048]{1,0:T(8,128)}) custom-call(s32[1]{0:T(128)} %bitcast.refs_0_.index_ref, bf16[192,256]{1,0:T(8,128)(2,1)S(1)} %get-tuple-element.23.refs_1_, f32[1,2048]{1,0:T(1,128)} %bitcast.7, bf16[48,1536]{1,0:T(8,128)(2,1)} %refs_3_.1, ...), custom_call_target="tpu_custom_call" | custom-call | flops 2315255808 | bytes 8388608 | tf_op jit(solution)/shard_map/front/pallas_call | solution.py:161
  24.1 0.1 collective-permute-start.6
  24.1 1.6 %collective-permute-start.16 = (bf16[384,256]{1,0:T(8,128)(2,1)S(1)}, bf16[384,256]{1,0:T(8,128)(2,1)S(1)}, u32[]{:S(2)}, u32[]{:S(2)}) collective-permute-start(bf16[384,256]{1,0:T(8,128)(2,1)S(1)} %maximum_select_fusion.1.refs_10_), channel_id=1, source_target_pairs={{0,4},{4,0},{8,12},{12,8},{16,20},{20,16},{24,28},{28,24},{1,5},{5... | collective-permute-start | bytes 589832 | tf_op jit(solution)/shard_map/ppermute | solution.py:671
  25.7 0.2 collective-permute-start.8
  25.9 0.3 collective-permute-start.9
  26.2 2.9 %all-to-all-start = ((f32[32,1,256]{2,1,0:T(1,128)}), f32[32,1,256]{2,1,0:T(1,128)S(1)}, u32[]{:S(2)}, u32[]{:S(2)}) async-start(f32[32,1,256]{2,1,0:T(1,128)} %get-tuple-element.34), calls=%async_computation | async-start | bytes 65536 | tf_op jit(solution)/shard_map/all_to_all | solution.py:701
  29.1 2.3 %collective-permute-done.16 = bf16[384,256]{1,0:T(8,128)(2,1)S(1)} collective-permute-done((bf16[384,256]{1,0:T(8,128)(2,1)S(1)}, bf16[384,256]{1,0:T(8,128)(2,1)S(1)}, u32[]{:S(2)}, u32[]{:S(2)}) %collective-permute-start.16) | collective-permute-done | bytes 196640 | tf_op jit(solution)/shard_map/ppermute | solution.py:671
  31.5 0.2 maximum_select_fusion.refs_2_
  31.6 0.1 collective-permute-start.17
  31.7 0.0 collective-permute-done.6.core_ref
  31.8 1.6 %collective-permute-start.7 = (f32[48,2048]{1,0:T(8,128)S(1)}, f32[48,2048]{1,0:T(8,128)}, u32[]{:S(2)}, u32[]{:S(2)}) collective-permute-start(f32[48,2048]{1,0:T(8,128)S(1)} %slice_add_fusion.refs_5_), channel_id=1, source_target_pairs={{0,2},{1,3},{2,0},{3,1},{4,6},{5,7},{6,4},{7,5},{8,10},{9,11},{10,... | collective-permute-start | bytes 1179656 | tf_op jit(solution)/shard_map/ppermute | solution.py:671
  33.3 0.1 pad_add_fusion.1.refs_0_
  33.4 0.0 collective-permute-done.8.other_ref.refs_6_
  33.4 3.0 %all-to-all-done.refs_4_.refs_2_ = f32[32,1,256]{2,1,0:T(1,128)S(1)} async-done(((f32[32,1,256]{2,1,0:T(1,128)}), f32[32,1,256]{2,1,0:T(1,128)S(1)}, u32[]{:S(2)}, u32[]{:S(2)}) %all-to-all-start) | async-done | bytes 32800 | tf_op jit(solution)/shard_map/all_to_all | solution.py:701
  36.4 0.0 collective-permute-done.9.last_ref.refs_7_
  36.4 0.0 collective-permute-done.17.refs_3_
  36.4 6.8 %first_sweep.1 = (bf16[32,16,128]{2,1,0:T(8,128)(2,1)}, bf16[2048,1536]{1,0:T(8,128)(2,1)}) custom-call(s32[2]{0:T(128)S(1)} %pad_add_fusion.1.refs_0_, bf16[16384,256]{1,0:T(8,128)(2,1)} %refs_4_.1, bf16[768,256]{1,0:T(8,128)(2,1)S(1)} %maximum_select_fusion.refs_2_, bf16[768,256]{1,0:T(8,128)(2,1)} %collective-permute-done.17.refs_3_, ...), custom_call_target="tpu_custom_call" | custom-call | flops 1610612736 | bytes 6291456 | tf_op jit(solution)/shard_map/first_sweep/pallas_call | solution.py:453
  43.2 2.6 %all-to-all-start.1 = ((bf16[32,16,128]{2,1,0:T(8,128)(2,1)}), bf16[32,16,128]{2,1,0:T(8,128)(2,1)S(1)}, u32[]{:S(2)}, u32[]{:S(2)}) async-start(bf16[32,16,128]{2,1,0:T(8,128)(2,1)} %get-tuple-element.36), calls=%async_computation.1 | async-start | bytes 262144 | tf_op jit(solution)/shard_map/all_to_all | solution.py:701
  45.8 0.0 collective-permute-done.7.x_ref
  45.8 1.7 %student_middle.1 = (f32[48,256]{1,0:T(8,128)S(1)}, bf16[48,256]{1,0:T(8,128)(2,1)S(1)}, f32[48,128]{1,0:T(8,128)S(1)}) custom-call(s32[1]{0:T(128)} %bitcast.refs_0_.index_ref, f32[96,2048]{1,0:T(8,128)S(1)} %get-tuple-element.25.keep_ref, f32[96,2048]{1,0:T(8,128)S(1)} %collective-permute-done.6.core_ref, f32[48,2048]{1,0:T(8,128)} %collective-permute-done.7.x_ref, ...), custom_call_target="tpu_custom_call" | custom-call | flops 50331648 | bytes 2621440 | tf_op jit(solution)/shard_map/student_middle/pallas_call | solution.py:619
  47.4 1.5 %collective-permute-start.12 = (bf16[48,256]{1,0:T(8,128)(2,1)S(1)}, bf16[48,256]{1,0:T(8,128)(2,1)S(1)}, u32[]{:S(2)}, u32[]{:S(2)}) collective-permute-start(bf16[48,256]{1,0:T(8,128)(2,1)S(1)} %get-tuple-element.29.refs_2_), channel_id=1, source_target_pairs={{0,3},{1,2},{2,1},{3,0},{4,7},{5,6},{6,5},{7,4},{8,11},{9,10},{10,... | collective-permute-start | bytes 73736 | tf_op jit(solution)/shard_map/ppermute | solution.py:671
  48.9 0.4 collective-permute-start.11
  49.3 0.1 collective-permute-start.10
  49.4 4.6 %all-to-all-done.1.refs_1_ = bf16[32,16,128]{2,1,0:T(8,128)(2,1)S(1)} async-done(((bf16[32,16,128]{2,1,0:T(8,128)(2,1)}), bf16[32,16,128]{2,1,0:T(8,128)(2,1)S(1)}, u32[]{:S(2)}, u32[]{:S(2)}) %all-to-all-start.1) | async-done | bytes 131104 | tf_op jit(solution)/shard_map/all_to_all | solution.py:701
  54.0 4.4 %next_sweep.1 = bf16[32,16,128]{2,1,0:T(8,128)(2,1)} custom-call(bf16[2048,1536]{1,0:T(8,128)(2,1)} %get-tuple-element.35.refs_0_, bf16[32,16,128]{2,1,0:T(8,128)(2,1)S(1)} %all-to-all-done.1.refs_1_, bf16[48,256]{1,0:T(8,128)(2,1)S(1)} %get-tuple-element.29.refs_2_), custom_call_target="tpu_custom_call" | custom-call | flops 25165824 | bytes 6291456 | tf_op jit(solution)/shard_map/next_sweep/pallas_call | solution.py:539
  58.4 2.6 %all-to-all-start.2 = ((bf16[32,16,128]{2,1,0:T(8,128)(2,1)}), bf16[32,16,128]{2,1,0:T(8,128)(2,1)S(1)}, u32[]{:S(2)}, u32[]{:S(2)}) async-start(bf16[32,16,128]{2,1,0:T(8,128)(2,1)} %next_sweep.1), calls=%async_computation.2 | async-start | bytes 262144 | tf_op jit(solution)/shard_map/all_to_all | solution.py:701
  61.0 0.0 collective-permute-done.10
  61.0 0.0 collective-permute-done.11
  61.0 0.0 collective-permute-done.12
  61.1 6.0 %attract.2.state_ref.refs_2_ = f32[192,512]{1,0:T(8,128)S(1)} custom-call(bf16[192,256]{1,0:T(8,128)(2,1)S(1)} %constant_dynamic-update-slice_fusion.emb_ref, f32[192,512]{1,0:T(8,128)S(1)} %concatenate.32.state_ref, bf16[16384,256]{1,0:T(8,128)(2,1)} %refs_4_.1), custom_call_target="tpu_custom_call" | custom-call | flops 2013265920 | bytes 5242880 | tf_op jit(solution)/shard_map/attract/pallas_call | solution.py:327
  67.1 2.1 %all-to-all-done.2.refs_1_ = bf16[32,16,128]{2,1,0:T(8,128)(2,1)S(1)} async-done(((bf16[32,16,128]{2,1,0:T(8,128)(2,1)}), bf16[32,16,128]{2,1,0:T(8,128)(2,1)S(1)}, u32[]{:S(2)}, u32[]{:S(2)}) %all-to-all-start.2) | async-done | bytes 131104 | tf_op jit(solution)/shard_map/all_to_all | solution.py:701
  69.2 3.8 %last_scales.1 = f32[8,1,2048]{2,1,0:T(1,128)} custom-call(bf16[2048,1536]{1,0:T(8,128)(2,1)} %get-tuple-element.35.refs_0_, bf16[32,16,128]{2,1,0:T(8,128)(2,1)S(1)} %all-to-all-done.2.refs_1_, f32[192,512]{1,0:T(8,128)S(1)} %attract.2.state_ref.refs_2_), custom_call_target="tpu_custom_call" | custom-call | flops 12582912 | bytes 6291456 | tf_op jit(solution)/shard_map/last_scales/pallas_call | solution.py:578
  73.0 3.7 %all-to-all-start.3 = ((f32[8,1,2048]{2,1,0:T(1,128)}), f32[8,1,2048]{2,1,0:T(1,128)S(1)}, u32[]{:S(2)}, u32[]{:S(2)}) async-start(f32[8,1,2048]{2,1,0:T(1,128)} %last_scales.1), calls=%async_computation.3 | async-start | bytes 131072 | tf_op jit(solution)/shard_map/all_to_all | solution.py:701
  76.7 0.1 pad_add_fusion.refs_0_
  76.8 4.2 %attract.3 = (f32[48,512]{1,0:T(8,128)S(1)}, f32[48,512]{1,0:T(8,128)S(1)}, f32[48,512]{1,0:T(8,128)S(1)}, f32[48,512]{1,0:T(8,128)S(1)}) custom-call(bf16[192,256]{1,0:T(8,128)(2,1)S(1)} %constant_dynamic-update-slice_fusion.emb_ref, f32[192,512]{1,0:T(8,128)S(1)} %attract.2.state_ref.refs_2_, bf16[16384,256]{1,0:T(8,128)(2,1)} %refs_4_.1), custom_call_target="tpu_custom_call" | custom-call | flops 1207959552 | bytes 3145728 | tf_op jit(solution)/shard_map/attract/pallas_call | solution.py:327
  80.9 1.0 %collective-permute-start.13 = (f32[48,512]{1,0:T(8,128)S(1)}, f32[48,512]{1,0:T(8,128)S(1)}, u32[]{:S(2)}, u32[]{:S(2)}) collective-permute-start(f32[48,512]{1,0:T(8,128)S(1)} %get-tuple-element.31), channel_id=1, source_target_pairs={{0,3},{1,2},{2,1},{3,0},{4,7},{5,6},{6,5},{7,4},{8,11},{9,10},{10,... | collective-permute-start | bytes 294920 | tf_op jit(solution)/shard_map/ppermute | solution.py:671
  82.0 0.6 collective-permute-start.14
  82.6 0.3 collective-permute-start.15
  82.9 0.7 all-to-all-done.3.refs_3_
  83.6 9.5 %repel.1 = (f32[48,384]{1,0:T(8,128)S(1)}, bf16[48,384]{1,0:T(8,128)(2,1)S(1)}, bf16[48,384]{1,0:T(8,128)(2,1)S(1)}, bf16[48,384]{1,0:T(8,128)(2,1)S(1)}) custom-call(s32[2]{0:T(128)S(1)} %pad_add_fusion.refs_0_, bf16[192,256]{1,0:T(8,128)(2,1)S(1)} %get-tuple-element.23.refs_1_, f32[32,1,256]{2,1,0:T(1,128)S(1)} %all-to-all-done.refs_4_.refs_2_, ...), custom_call_target="tpu_custom_call" | custom-call | flops 3221225472 | bytes 8388608 | tf_op jit(solution)/shard_map/repel/pallas_call | solution.py:246
  93.0 0.6 collective-permute-start.18
  93.7 1.0 %collective-permute-start.19 = (bf16[48,384]{1,0:T(8,128)(2,1)S(1)}, bf16[48,384]{1,0:T(8,128)(2,1)S(1)}, u32[]{:S(2)}, u32[]{:S(2)}) collective-permute-start(bf16[48,384]{1,0:T(8,128)(2,1)S(1)} %get-tuple-element.39), channel_id=1, source_target_pairs={{0,2},{1,3},{2,0},{3,1},{4,6},{5,7},{6,4},{7,5},{8,10},{9,11},{10,... | collective-permute-start | bytes 110600 | tf_op jit(solution)/shard_map/ppermute | solution.py:671
  94.7 0.0 collective-permute-done.13.rest_1_
  94.7 0.3 collective-permute-start.20
  95.0 0.0 collective-permute-done.14.rest_2_
  95.0 0.0 collective-permute-done.15.rest_3_
  95.0 1.9 %collective-permute-done.18.rest_5_ = bf16[48,384]{1,0:T(8,128)(2,1)S(1)} collective-permute-done((bf16[48,384]{1,0:T(8,128)(2,1)S(1)}, bf16[48,384]{1,0:T(8,128)(2,1)S(1)}, u32[]{:S(2)}, u32[]{:S(2)}) %collective-permute-start.18) | collective-permute-done | bytes 36896 | tf_op jit(solution)/shard_map/ppermute | solution.py:671
  96.9 1.1 %collective-permute-done.19.rest_6_ = bf16[48,384]{1,0:T(8,128)(2,1)S(1)} collective-permute-done((bf16[48,384]{1,0:T(8,128)(2,1)S(1)}, bf16[48,384]{1,0:T(8,128)(2,1)S(1)}, u32[]{:S(2)}, u32[]{:S(2)}) %collective-permute-start.19) | collective-permute-done | bytes 36896 | tf_op jit(solution)/shard_map/ppermute | solution.py:671
  97.9 0.0 collective-permute-done.20.rest_7_
  97.9 0.8 finish.1
  (9 shorter events, 0.1 us)
Async XLA Ops:
  1.0 6.7 %collective-permute-start.3 = (bf16[96,256]{1,0:T(8,128)(2,1)S(1)}, bf16[96,256]{1,0:T(8,128)(2,1)S(1)}, u32[]{:S(2)}, u32[]{:S(2)}) collective-permute-start(bf16[96,256]{1,0:T(8,128)(2,1)S(1)} %get-tuple-element.24), channel_id=1, source_target_pairs={{0,16},{4,20},{8,24},{12,28},{16,0},{20,4},{24,8},{28,12},{1,17},{... | collective-permute-start | bytes 147464 | tf_op jit(solution)/shard_map/ppermute | solution.py:671
  5.1 7.0 %collective-permute-start = (bf16[48,1536]{1,0:T(8,128)(2,1)}, bf16[48,1536]{1,0:T(8,128)(2,1)S(1)}, u32[]{:S(2)}, u32[]{:S(2)}) collective-permute-start(bf16[48,1536]{1,0:T(8,128)(2,1)} %refs_3_.1), channel_id=1, source_target_pairs={{0,2},{1,3},{2,0},{3,1},{4,6},{5,7},{6,4},{7,5},{8,10},{9,11},{10,... | collective-permute-start | bytes 442376 | tf_op jit(solution)/shard_map/ppermute | solution.py:671
  6.6 9.6 %collective-permute-start.5 = (bf16[512,256]{1,0:T(8,128)(2,1)}, bf16[512,256]{1,0:T(8,128)(2,1)S(1)}, u32[]{:S(2)}, u32[]{:S(2)}) collective-permute-start(bf16[512,256]{1,0:T(8,128)(2,1)} %own_ref.1), channel_id=1, source_target_pairs={{0,2},{1,3},{2,0},{3,1},{4,6},{5,7},{6,4},{7,5},{8,10},{9,11},{10,... | collective-permute-start | bytes 786440 | tf_op jit(solution)/shard_map/ppermute | solution.py:671
  7.8 4.7 %collective-permute-start.4 = (bf16[192,256]{1,0:T(8,128)(2,1)S(1)}, bf16[192,256]{1,0:T(8,128)(2,1)S(1)}, u32[]{:S(2)}, u32[]{:S(2)}) collective-permute-start(bf16[192,256]{1,0:T(8,128)(2,1)S(1)} %maximum_select_fusion.2), channel_id=1, source_target_pairs={{0,8},{4,12},{8,0},{12,4},{16,24},{20,28},{24,16},{28,20},{1,9},{5... | collective-permute-start | bytes 294920 | tf_op jit(solution)/shard_map/ppermute | solution.py:671
  9.2 3.3 %collective-permute-start.1 = (bf16[48,1536]{1,0:T(8,128)(2,1)}, bf16[48,1536]{1,0:T(8,128)(2,1)S(1)}, u32[]{:S(2)}, u32[]{:S(2)}) collective-permute-start(bf16[48,1536]{1,0:T(8,128)(2,1)} %refs_3_.1), channel_id=1, source_target_pairs={{0,1},{1,0},{2,3},{3,2},{4,5},{5,4},{6,7},{7,6},{8,9},{9,8},{10,11... | collective-permute-start | bytes 442376 | tf_op jit(solution)/shard_map/ppermute | solution.py:671
  12.1 4.2 %collective-permute-start.2 = (bf16[48,1536]{1,0:T(8,128)(2,1)S(1)}, bf16[48,1536]{1,0:T(8,128)(2,1)S(1)}, u32[]{:S(2)}, u32[]{:S(2)}) collective-permute-start(bf16[48,1536]{1,0:T(8,128)(2,1)S(1)} %collective-permute-done.refs_4_), channel_id=1, source_target_pairs={{0,1},{1,0},{2,3},{3,2},{4,5},{5,4},{6,7},{7,6},{8,9},{9,8},{10,11... | collective-permute-start | bytes 442376 | tf_op jit(solution)/shard_map/ppermute | solution.py:671
  24.1 7.6 %collective-permute-start.6 = (f32[96,2048]{1,0:T(8,128)}, f32[96,2048]{1,0:T(8,128)S(1)}, u32[]{:S(2)}, u32[]{:S(2)}) collective-permute-start(f32[96,2048]{1,0:T(8,128)} %get-tuple-element.26), channel_id=1, source_target_pairs={{0,1},{1,0},{2,3},{3,2},{4,5},{5,4},{6,7},{7,6},{8,9},{9,8},{10,11... | collective-permute-start | bytes 2359304 | tf_op jit(solution)/shard_map/ppermute | solution.py:671
  24.1 7.3 %collective-permute-start.16 = (bf16[384,256]{1,0:T(8,128)(2,1)S(1)}, bf16[384,256]{1,0:T(8,128)(2,1)S(1)}, u32[]{:S(2)}, u32[]{:S(2)}) collective-permute-start(bf16[384,256]{1,0:T(8,128)(2,1)S(1)} %maximum_select_fusion.1.refs_10_), channel_id=1, source_target_pairs={{0,4},{4,0},{8,12},{12,8},{16,20},{20,16},{24,28},{28,24},{1,5},{5... | collective-permute-start | bytes 589832 | tf_op jit(solution)/shard_map/ppermute | solution.py:671
  25.7 7.7 %collective-permute-start.8 = (bf16[512,256]{1,0:T(8,128)(2,1)}, bf16[512,256]{1,0:T(8,128)(2,1)S(1)}, u32[]{:S(2)}, u32[]{:S(2)}) collective-permute-start(bf16[512,256]{1,0:T(8,128)(2,1)} %own_ref.1), channel_id=1, source_target_pairs={{0,1},{1,0},{2,3},{3,2},{4,5},{5,4},{6,7},{7,6},{8,9},{9,8},{10,11... | collective-permute-start | bytes 786440 | tf_op jit(solution)/shard_map/ppermute | solution.py:671
  25.9 10.5 %collective-permute-start.9 = (bf16[512,256]{1,0:T(8,128)(2,1)S(1)}, bf16[512,256]{1,0:T(8,128)(2,1)S(1)}, u32[]{:S(2)}, u32[]{:S(2)}) collective-permute-start(bf16[512,256]{1,0:T(8,128)(2,1)S(1)} %collective-permute-done.5.refs_11_.partner_ref), channel_id=1, source_target_pairs={{0,1},{1,0},{2,3},{3,2},{4,5},{5,4},{6,7},{7,6},{8,9},{9,8},{10,11... | collective-permute-start | bytes 786440 | tf_op jit(solution)/shard_map/ppermute | solution.py:671
  26.2 10.1 %all-to-all-start = ((f32[32,1,256]{2,1,0:T(1,128)}), f32[32,1,256]{2,1,0:T(1,128)S(1)}, u32[]{:S(2)}, u32[]{:S(2)}) async-start(f32[32,1,256]{2,1,0:T(1,128)} %get-tuple-element.34), calls=%async_computation | async-start | bytes 65536 | tf_op jit(solution)/shard_map/all_to_all | solution.py:701
  31.6 4.8 %collective-permute-start.17 = (bf16[768,256]{1,0:T(8,128)(2,1)S(1)}, bf16[768,256]{1,0:T(8,128)(2,1)}, u32[]{:S(2)}, u32[]{:S(2)}) collective-permute-start(bf16[768,256]{1,0:T(8,128)(2,1)S(1)} %maximum_select_fusion.refs_2_), channel_id=1, source_target_pairs={{0,1},{1,0},{2,3},{3,2},{4,5},{5,4},{6,7},{7,6},{8,9},{9,8},{10,11... | collective-permute-start | bytes 1179656 | tf_op jit(solution)/shard_map/ppermute | solution.py:671
  31.8 14.0 %collective-permute-start.7 = (f32[48,2048]{1,0:T(8,128)S(1)}, f32[48,2048]{1,0:T(8,128)}, u32[]{:S(2)}, u32[]{:S(2)}) collective-permute-start(f32[48,2048]{1,0:T(8,128)S(1)} %slice_add_fusion.refs_5_), channel_id=1, source_target_pairs={{0,2},{1,3},{2,0},{3,1},{4,6},{5,7},{6,4},{7,5},{8,10},{9,11},{10,... | collective-permute-start | bytes 1179656 | tf_op jit(solution)/shard_map/ppermute | solution.py:671
  43.2 10.8 %all-to-all-start.1 = ((bf16[32,16,128]{2,1,0:T(8,128)(2,1)}), bf16[32,16,128]{2,1,0:T(8,128)(2,1)S(1)}, u32[]{:S(2)}, u32[]{:S(2)}) async-start(bf16[32,16,128]{2,1,0:T(8,128)(2,1)} %get-tuple-element.36), calls=%async_computation.1 | async-start | bytes 262144 | tf_op jit(solution)/shard_map/all_to_all | solution.py:701
  47.4 13.6 %collective-permute-start.12 = (bf16[48,256]{1,0:T(8,128)(2,1)S(1)}, bf16[48,256]{1,0:T(8,128)(2,1)S(1)}, u32[]{:S(2)}, u32[]{:S(2)}) collective-permute-start(bf16[48,256]{1,0:T(8,128)(2,1)S(1)} %get-tuple-element.29.refs_2_), channel_id=1, source_target_pairs={{0,3},{1,2},{2,1},{3,0},{4,7},{5,6},{6,5},{7,4},{8,11},{9,10},{10,... | collective-permute-start | bytes 73736 | tf_op jit(solution)/shard_map/ppermute | solution.py:671
  48.9 12.1 %collective-permute-start.11 = (bf16[48,256]{1,0:T(8,128)(2,1)S(1)}, bf16[48,256]{1,0:T(8,128)(2,1)S(1)}, u32[]{:S(2)}, u32[]{:S(2)}) collective-permute-start(bf16[48,256]{1,0:T(8,128)(2,1)S(1)} %get-tuple-element.29.refs_2_), channel_id=1, source_target_pairs={{0,2},{1,3},{2,0},{3,1},{4,6},{5,7},{6,4},{7,5},{8,10},{9,11},{10,... | collective-permute-start | bytes 73736 | tf_op jit(solution)/shard_map/ppermute | solution.py:671
  49.3 11.7 %collective-permute-start.10 = (bf16[48,256]{1,0:T(8,128)(2,1)S(1)}, bf16[48,256]{1,0:T(8,128)(2,1)S(1)}, u32[]{:S(2)}, u32[]{:S(2)}) collective-permute-start(bf16[48,256]{1,0:T(8,128)(2,1)S(1)} %get-tuple-element.29.refs_2_), channel_id=1, source_target_pairs={{0,1},{1,0},{2,3},{3,2},{4,5},{5,4},{6,7},{7,6},{8,9},{9,8},{10,11... | collective-permute-start | bytes 73736 | tf_op jit(solution)/shard_map/ppermute | solution.py:671
  58.4 10.8 %all-to-all-start.2 = ((bf16[32,16,128]{2,1,0:T(8,128)(2,1)}), bf16[32,16,128]{2,1,0:T(8,128)(2,1)S(1)}, u32[]{:S(2)}, u32[]{:S(2)}) async-start(bf16[32,16,128]{2,1,0:T(8,128)(2,1)} %next_sweep.1), calls=%async_computation.2 | async-start | bytes 262144 | tf_op jit(solution)/shard_map/all_to_all | solution.py:701
  73.0 10.6 %all-to-all-start.3 = ((f32[8,1,2048]{2,1,0:T(1,128)}), f32[8,1,2048]{2,1,0:T(1,128)S(1)}, u32[]{:S(2)}, u32[]{:S(2)}) async-start(f32[8,1,2048]{2,1,0:T(1,128)} %last_scales.1), calls=%async_computation.3 | async-start | bytes 131072 | tf_op jit(solution)/shard_map/all_to_all | solution.py:701
  80.9 13.7 %collective-permute-start.13 = (f32[48,512]{1,0:T(8,128)S(1)}, f32[48,512]{1,0:T(8,128)S(1)}, u32[]{:S(2)}, u32[]{:S(2)}) collective-permute-start(f32[48,512]{1,0:T(8,128)S(1)} %get-tuple-element.31), channel_id=1, source_target_pairs={{0,3},{1,2},{2,1},{3,0},{4,7},{5,6},{6,5},{7,4},{8,11},{9,10},{10,... | collective-permute-start | bytes 294920 | tf_op jit(solution)/shard_map/ppermute | solution.py:671
  82.0 13.0 %collective-permute-start.14 = (f32[48,512]{1,0:T(8,128)S(1)}, f32[48,512]{1,0:T(8,128)S(1)}, u32[]{:S(2)}, u32[]{:S(2)}) collective-permute-start(f32[48,512]{1,0:T(8,128)S(1)} %get-tuple-element.32), channel_id=1, source_target_pairs={{0,2},{1,3},{2,0},{3,1},{4,6},{5,7},{6,4},{7,5},{8,10},{9,11},{10,... | collective-permute-start | bytes 294920 | tf_op jit(solution)/shard_map/ppermute | solution.py:671
  82.6 12.4 %collective-permute-start.15 = (f32[48,512]{1,0:T(8,128)S(1)}, f32[48,512]{1,0:T(8,128)S(1)}, u32[]{:S(2)}, u32[]{:S(2)}) collective-permute-start(f32[48,512]{1,0:T(8,128)S(1)} %get-tuple-element.33), channel_id=1, source_target_pairs={{0,1},{1,0},{2,3},{3,2},{4,5},{5,4},{6,7},{7,6},{8,9},{9,8},{10,11... | collective-permute-start | bytes 294920 | tf_op jit(solution)/shard_map/ppermute | solution.py:671
  93.0 3.8 %collective-permute-start.18 = (bf16[48,384]{1,0:T(8,128)(2,1)S(1)}, bf16[48,384]{1,0:T(8,128)(2,1)S(1)}, u32[]{:S(2)}, u32[]{:S(2)}) collective-permute-start(bf16[48,384]{1,0:T(8,128)(2,1)S(1)} %get-tuple-element.38), channel_id=1, source_target_pairs={{0,3},{1,2},{2,1},{3,0},{4,7},{5,6},{6,5},{7,4},{8,11},{9,10},{10,... | collective-permute-start | bytes 110600 | tf_op jit(solution)/shard_map/ppermute | solution.py:671
  93.7 4.3 %collective-permute-start.19 = (bf16[48,384]{1,0:T(8,128)(2,1)S(1)}, bf16[48,384]{1,0:T(8,128)(2,1)S(1)}, u32[]{:S(2)}, u32[]{:S(2)}) collective-permute-start(bf16[48,384]{1,0:T(8,128)(2,1)S(1)} %get-tuple-element.39), channel_id=1, source_target_pairs={{0,2},{1,3},{2,0},{3,1},{4,6},{5,7},{6,4},{7,5},{8,10},{9,11},{10,... | collective-permute-start | bytes 110600 | tf_op jit(solution)/shard_map/ppermute | solution.py:671
  94.7 3.3 %collective-permute-start.20 = (bf16[48,384]{1,0:T(8,128)(2,1)S(1)}, bf16[48,384]{1,0:T(8,128)(2,1)S(1)}, u32[]{:S(2)}, u32[]{:S(2)}) collective-permute-start(bf16[48,384]{1,0:T(8,128)(2,1)S(1)} %get-tuple-element.40), channel_id=1, source_target_pairs={{0,1},{1,0},{2,3},{3,2},{4,5},{5,4},{6,7},{7,6},{8,9},{9,8},{10,11... | collective-permute-start | bytes 110600 | tf_op jit(solution)/shard_map/ppermute | solution.py:671

commit v20 on v19

--- a/solution.py
+++ b/solution.py
@@ -742,8 +742,8 @@
         [jnp.zeros((group_rows, width + 128), jnp.float32), jnp.full((group_rows, 128), -1e30, jnp.float32)], axis=1
     )
     eighth = count // 8
-    (state,) = attract(student_emb, empty, protos, 0, 5 * eighth, 5, 1)
-    slots = attract(student_emb, state, protos, 5 * eighth, 3 * eighth, 3, proto_size)
+    (state,) = attract(student_emb, empty, protos, 0, 6 * eighth, 6, 1)
+    slots = attract(student_emb, state, protos, 6 * eighth, 2 * eighth, 2, proto_size)
     attract_parts = send_blocks(slots)
 
     copies, weights = first_sweep(thin_ref, protos, mine, other, all_tops, (x_sent, *thirds[2:]), devices, thin, protos_total)

time: 99.2 us -> 99.5 us (level)
  no operation moved by 1% of the time
where the time goes in v20:
time: 99.5 us; the launch traced here: 99.1 us
  Pallas kernels  45.8 us (46%)
  starting transfers between devices  29.8 us (30%)
  waiting for transfers between devices  22.6 us (23%)
    ppermute x21, starting transfers between devices, swap(): lax.ppermute(values, axis, [(i, i ^ flip) for i in range(lax.axis_size(ax...  17.2 us
    all_to_all x4, starting transfers between devices, all_to_all(): return lax.all_to_all(copies, axes, 0, 0, tiled=True)  12.7 us
    ppermute x21, waiting for transfers between devices, swap(): lax.ppermute(values, axis, [(i, i ^ flip) for i in range(lax.axis_size(ax...  12.2 us
    all_to_all x4, waiting for transfers between devices, all_to_all(): return lax.all_to_all(copies, axes, 0, 0, tiled=True)  10.4 us
    pallas_call x2, Pallas kernels, attract(): pl.pallas_call(functools.partial(attract_kernel, first_row, outputs > 1),...  10.2 us
    pallas_call x1, Pallas kernels, repel(): pl.pallas_call(skipping(functools.partial(repel_kernel, proto_size), 5, l...  9.49 us
    pallas_call x1, Pallas kernels, front(): pl.pallas_call(skipping(front_kernel, 10, len(order)), in_specs=[whole(pl...  7.78 us
    pallas_call x1, Pallas kernels, first_sweep(): pl.pallas_call(skipping(functools.partial(first_sweep_kernel, chunk, prot...  6.8 us
  transfers between devices with their start and end apart: 25, of which 11 were waited for; matrix products, arithmetic and copies ran while one was open for 0% of the time, Pallas kernels for 33%

profile of v20, /device:TPU:0, one launch (start us, length us, event | category | flops | bytes accessed | tf_op | source)
XLA Modules:
  0.0 99.1 jit_solution(3439769220307228549)
XLA Ops:
  0.0 1.0 %teacher_units.1 = (bf16[192,256]{1,0:T(8,128)(2,1)S(1)}, bf16[96,256]{1,0:T(8,128)(2,1)S(1)}) custom-call(s32[1]{0:T(128)} %bitcast.1.core_ref, bf16[192,256]{1,0:T(8,128)(2,1)} %emb_ref.1), custom_call_target="tpu_custom_call" | custom-call | flops 196608 | bytes 393216 | tf_op jit(solution)/shard_map/teacher_units/pallas_call | solution.py:96
  1.0 4.1 %collective-permute-start.3 = (bf16[96,256]{1,0:T(8,128)(2,1)S(1)}, bf16[96,256]{1,0:T(8,128)(2,1)S(1)}, u32[]{:S(2)}, u32[]{:S(2)}) collective-permute-start(bf16[96,256]{1,0:T(8,128)(2,1)S(1)} %get-tuple-element.24), channel_id=1, source_target_pairs={{0,16},{4,20},{8,24},{12,28},{16,0},{20,4},{24,8},{28,12},{1,17},{... | collective-permute-start | bytes 147464 | tf_op jit(solution)/shard_map/ppermute | solution.py:671
  5.1 1.5 %collective-permute-start = (bf16[48,1536]{1,0:T(8,128)(2,1)}, bf16[48,1536]{1,0:T(8,128)(2,1)S(1)}, u32[]{:S(2)}, u32[]{:S(2)}) collective-permute-start(bf16[48,1536]{1,0:T(8,128)(2,1)} %refs_3_.1), channel_id=1, source_target_pairs={{0,2},{1,3},{2,0},{3,1},{4,6},{5,7},{6,4},{7,5},{8,10},{9,11},{10,... | collective-permute-start | bytes 442376 | tf_op jit(solution)/shard_map/ppermute | solution.py:671
  6.6 0.5 collective-permute-start.5
  7.2 0.6 collective-permute-done.3
  7.8 1.4 %collective-permute-start.4 = (bf16[192,256]{1,0:T(8,128)(2,1)S(1)}, bf16[192,256]{1,0:T(8,128)(2,1)S(1)}, u32[]{:S(2)}, u32[]{:S(2)}) collective-permute-start(bf16[192,256]{1,0:T(8,128)(2,1)S(1)} %maximum_select_fusion.2), channel_id=1, source_target_pairs={{0,8},{4,12},{8,0},{12,4},{16,24},{20,28},{24,16},{28,20},{1,9},{5... | collective-permute-start | bytes 294920 | tf_op jit(solution)/shard_map/ppermute | solution.py:671
  9.2 0.0 collective-permute-start.1
  9.2 2.9 %collective-permute-done.refs_4_ = bf16[48,1536]{1,0:T(8,128)(2,1)S(1)} collective-permute-done((bf16[48,1536]{1,0:T(8,128)(2,1)}, bf16[48,1536]{1,0:T(8,128)(2,1)S(1)}, u32[]{:S(2)}, u32[]{:S(2)}) %collective-permute-start) | collective-permute-done | bytes 147488 | tf_op jit(solution)/shard_map/ppermute | solution.py:671
  12.1 0.0 collective-permute-start.2
  12.1 0.3 collective-permute-done.4
  12.4 0.1 maximum_select_fusion.1.refs_10_
  12.5 0.0 collective-permute-done.1.refs_5_
  12.5 3.8 %collective-permute-done.5.refs_11_.partner_ref = bf16[512,256]{1,0:T(8,128)(2,1)S(1)} collective-permute-done((bf16[512,256]{1,0:T(8,128)(2,1)}, bf16[512,256]{1,0:T(8,128)(2,1)S(1)}, u32[]{:S(2)}, u32[]{:S(2)}) %collective-permute-start.5) | collective-permute-done | bytes 262176 | tf_op jit(solution)/shard_map/ppermute | solution.py:671
  16.3 0.0 collective-permute-done.2.refs_6_
  16.3 7.8 %front.1 = (f32[32,1,256]{2,1,0:T(1,128)}, f32[96,2048]{1,0:T(8,128)S(1)}, f32[96,2048]{1,0:T(8,128)}) custom-call(s32[1]{0:T(128)} %bitcast.refs_0_.index_ref, bf16[192,256]{1,0:T(8,128)(2,1)S(1)} %get-tuple-element.23.refs_1_, f32[1,2048]{1,0:T(1,128)} %bitcast.7, bf16[48,1536]{1,0:T(8,128)(2,1)} %refs_3_.1, ...), custom_call_target="tpu_custom_call" | custom-call | flops 2315255808 | bytes 8388608 | tf_op jit(solution)/shard_map/front/pallas_call | solution.py:161
  24.1 0.1 collective-permute-start.6
  24.1 1.6 %collective-permute-start.16 = (bf16[384,256]{1,0:T(8,128)(2,1)S(1)}, bf16[384,256]{1,0:T(8,128)(2,1)S(1)}, u32[]{:S(2)}, u32[]{:S(2)}) collective-permute-start(bf16[384,256]{1,0:T(8,128)(2,1)S(1)} %maximum_select_fusion.1.refs_10_), channel_id=1, source_target_pairs={{0,4},{4,0},{8,12},{12,8},{16,20},{20,16},{24,28},{28,24},{1,5},{5... | collective-permute-start | bytes 589832 | tf_op jit(solution)/shard_map/ppermute | solution.py:671
  25.7 0.2 collective-permute-start.8
  25.9 0.3 collective-permute-start.9
  26.2 2.9 %all-to-all-start = ((f32[32,1,256]{2,1,0:T(1,128)}), f32[32,1,256]{2,1,0:T(1,128)S(1)}, u32[]{:S(2)}, u32[]{:S(2)}) async-start(f32[32,1,256]{2,1,0:T(1,128)} %get-tuple-element.34), calls=%async_computation | async-start | bytes 65536 | tf_op jit(solution)/shard_map/all_to_all | solution.py:701
  29.1 2.3 %collective-permute-done.16 = bf16[384,256]{1,0:T(8,128)(2,1)S(1)} collective-permute-done((bf16[384,256]{1,0:T(8,128)(2,1)S(1)}, bf16[384,256]{1,0:T(8,128)(2,1)S(1)}, u32[]{:S(2)}, u32[]{:S(2)}) %collective-permute-start.16) | collective-permute-done | bytes 196640 | tf_op jit(solution)/shard_map/ppermute | solution.py:671
  31.5 0.2 maximum_select_fusion.refs_2_
  31.6 0.1 collective-permute-start.17
  31.7 0.0 collective-permute-done.6.core_ref
  31.8 1.6 %collective-permute-start.7 = (f32[48,2048]{1,0:T(8,128)S(1)}, f32[48,2048]{1,0:T(8,128)}, u32[]{:S(2)}, u32[]{:S(2)}) collective-permute-start(f32[48,2048]{1,0:T(8,128)S(1)} %slice_add_fusion.refs_5_), channel_id=1, source_target_pairs={{0,2},{1,3},{2,0},{3,1},{4,6},{5,7},{6,4},{7,5},{8,10},{9,11},{10,... | collective-permute-start | bytes 1179656 | tf_op jit(solution)/shard_map/ppermute | solution.py:671
  33.3 0.1 pad_add_fusion.1.refs_0_
  33.4 0.0 collective-permute-done.8.other_ref.refs_6_
  33.4 3.0 %all-to-all-done.refs_4_.refs_2_ = f32[32,1,256]{2,1,0:T(1,128)S(1)} async-done(((f32[32,1,256]{2,1,0:T(1,128)}), f32[32,1,256]{2,1,0:T(1,128)S(1)}, u32[]{:S(2)}, u32[]{:S(2)}) %all-to-all-start) | async-done | bytes 32800 | tf_op jit(solution)/shard_map/all_to_all | solution.py:701
  36.4 0.0 collective-permute-done.9.last_ref.refs_7_
  36.4 0.0 collective-permute-done.17.refs_3_
  36.4 6.8 %first_sweep.1 = (bf16[32,16,128]{2,1,0:T(8,128)(2,1)}, bf16[2048,1536]{1,0:T(8,128)(2,1)}) custom-call(s32[2]{0:T(128)S(1)} %pad_add_fusion.1.refs_0_, bf16[16384,256]{1,0:T(8,128)(2,1)} %refs_4_.1, bf16[768,256]{1,0:T(8,128)(2,1)S(1)} %maximum_select_fusion.refs_2_, bf16[768,256]{1,0:T(8,128)(2,1)} %collective-permute-done.17.refs_3_, ...), custom_call_target="tpu_custom_call" | custom-call | flops 1610612736 | bytes 6291456 | tf_op jit(solution)/shard_map/first_sweep/pallas_call | solution.py:453
  43.2 2.6 %all-to-all-start.1 = ((bf16[32,16,128]{2,1,0:T(8,128)(2,1)}), bf16[32,16,128]{2,1,0:T(8,128)(2,1)S(1)}, u32[]{:S(2)}, u32[]{:S(2)}) async-start(bf16[32,16,128]{2,1,0:T(8,128)(2,1)} %get-tuple-element.36), calls=%async_computation.1 | async-start | bytes 262144 | tf_op jit(solution)/shard_map/all_to_all | solution.py:701
  45.8 0.0 collective-permute-done.7.x_ref
  45.8 1.7 %student_middle.1 = (f32[48,256]{1,0:T(8,128)S(1)}, bf16[48,256]{1,0:T(8,128)(2,1)S(1)}, f32[48,128]{1,0:T(8,128)S(1)}) custom-call(s32[1]{0:T(128)} %bitcast.refs_0_.index_ref, f32[96,2048]{1,0:T(8,128)S(1)} %get-tuple-element.25.keep_ref, f32[96,2048]{1,0:T(8,128)S(1)} %collective-permute-done.6.core_ref, f32[48,2048]{1,0:T(8,128)} %collective-permute-done.7.x_ref, ...), custom_call_target="tpu_custom_call" | custom-call | flops 50331648 | bytes 2621440 | tf_op jit(solution)/shard_map/student_middle/pallas_call | solution.py:619
  47.4 1.5 %collective-permute-start.12 = (bf16[48,256]{1,0:T(8,128)(2,1)S(1)}, bf16[48,256]{1,0:T(8,128)(2,1)S(1)}, u32[]{:S(2)}, u32[]{:S(2)}) collective-permute-start(bf16[48,256]{1,0:T(8,128)(2,1)S(1)} %get-tuple-element.29.refs_2_), channel_id=1, source_target_pairs={{0,3},{1,2},{2,1},{3,0},{4,7},{5,6},{6,5},{7,4},{8,11},{9,10},{10,... | collective-permute-start | bytes 73736 | tf_op jit(solution)/shard_map/ppermute | solution.py:671
  48.9 0.4 collective-permute-start.11
  49.3 0.1 collective-permute-start.10
  49.4 4.6 %all-to-all-done.1.refs_1_ = bf16[32,16,128]{2,1,0:T(8,128)(2,1)S(1)} async-done(((bf16[32,16,128]{2,1,0:T(8,128)(2,1)}), bf16[32,16,128]{2,1,0:T(8,128)(2,1)S(1)}, u32[]{:S(2)}, u32[]{:S(2)}) %all-to-all-start.1) | async-done | bytes 131104 | tf_op jit(solution)/shard_map/all_to_all | solution.py:701
  54.0 4.4 %next_sweep.1 = bf16[32,16,128]{2,1,0:T(8,128)(2,1)} custom-call(bf16[2048,1536]{1,0:T(8,128)(2,1)} %get-tuple-element.35.refs_0_, bf16[32,16,128]{2,1,0:T(8,128)(2,1)S(1)} %all-to-all-done.1.refs_1_, bf16[48,256]{1,0:T(8,128)(2,1)S(1)} %get-tuple-element.29.refs_2_), custom_call_target="tpu_custom_call" | custom-call | flops 25165824 | bytes 6291456 | tf_op jit(solution)/shard_map/next_sweep/pallas_call | solution.py:539
  58.4 2.6 %all-to-all-start.2 = ((bf16[32,16,128]{2,1,0:T(8,128)(2,1)}), bf16[32,16,128]{2,1,0:T(8,128)(2,1)S(1)}, u32[]{:S(2)}, u32[]{:S(2)}) async-start(bf16[32,16,128]{2,1,0:T(8,128)(2,1)} %next_sweep.1), calls=%async_computation.2 | async-start | bytes 262144 | tf_op jit(solution)/shard_map/all_to_all | solution.py:701
  61.0 0.0 collective-permute-done.10
  61.0 0.0 collective-permute-done.11
  61.0 0.0 collective-permute-done.12
  61.1 6.9 %attract.2.state_ref.refs_2_ = f32[192,512]{1,0:T(8,128)S(1)} custom-call(bf16[192,256]{1,0:T(8,128)(2,1)S(1)} %constant_dynamic-update-slice_fusion.emb_ref, f32[192,512]{1,0:T(8,128)S(1)} %concatenate.32.state_ref, bf16[16384,256]{1,0:T(8,128)(2,1)} %refs_4_.1), custom_call_target="tpu_custom_call" | custom-call | flops 2415919104 | bytes 6291456 | tf_op jit(solution)/shard_map/attract/pallas_call | solution.py:327
  68.0 1.2 %all-to-all-done.2.refs_1_ = bf16[32,16,128]{2,1,0:T(8,128)(2,1)S(1)} async-done(((bf16[32,16,128]{2,1,0:T(8,128)(2,1)}), bf16[32,16,128]{2,1,0:T(8,128)(2,1)S(1)}, u32[]{:S(2)}, u32[]{:S(2)}) %all-to-all-start.2) | async-done | bytes 131104 | tf_op jit(solution)/shard_map/all_to_all | solution.py:701
  69.2 3.8 %last_scales.1 = f32[8,1,2048]{2,1,0:T(1,128)} custom-call(bf16[2048,1536]{1,0:T(8,128)(2,1)} %get-tuple-element.35.refs_0_, bf16[32,16,128]{2,1,0:T(8,128)(2,1)S(1)} %all-to-all-done.2.refs_1_, f32[192,512]{1,0:T(8,128)S(1)} %attract.2.state_ref.refs_2_), custom_call_target="tpu_custom_call" | custom-call | flops 12582912 | bytes 6291456 | tf_op jit(solution)/shard_map/last_scales/pallas_call | solution.py:578
  73.0 4.6 %all-to-all-start.3 = ((f32[8,1,2048]{2,1,0:T(1,128)}), f32[8,1,2048]{2,1,0:T(1,128)S(1)}, u32[]{:S(2)}, u32[]{:S(2)}) async-start(f32[8,1,2048]{2,1,0:T(1,128)} %last_scales.1), calls=%async_computation.3 | async-start | bytes 131072 | tf_op jit(solution)/shard_map/all_to_all | solution.py:701
  77.6 0.1 pad_add_fusion.refs_0_
  77.7 3.3 %attract.3 = (f32[48,512]{1,0:T(8,128)S(1)}, f32[48,512]{1,0:T(8,128)S(1)}, f32[48,512]{1,0:T(8,128)S(1)}, f32[48,512]{1,0:T(8,128)S(1)}) custom-call(bf16[192,256]{1,0:T(8,128)(2,1)S(1)} %constant_dynamic-update-slice_fusion.emb_ref, f32[192,512]{1,0:T(8,128)S(1)} %attract.2.state_ref.refs_2_, bf16[16384,256]{1,0:T(8,128)(2,1)} %refs_4_.1), custom_call_target="tpu_custom_call" | custom-call | flops 805306368 | bytes 2097152 | tf_op jit(solution)/shard_map/attract/pallas_call | solution.py:327
  80.9 1.0 %collective-permute-start.13 = (f32[48,512]{1,0:T(8,128)S(1)}, f32[48,512]{1,0:T(8,128)S(1)}, u32[]{:S(2)}, u32[]{:S(2)}) collective-permute-start(f32[48,512]{1,0:T(8,128)S(1)} %get-tuple-element.31), channel_id=1, source_target_pairs={{0,3},{1,2},{2,1},{3,0},{4,7},{5,6},{6,5},{7,4},{8,11},{9,10},{10,... | collective-permute-start | bytes 294920 | tf_op jit(solution)/shard_map/ppermute | solution.py:671
  82.0 0.6 collective-permute-start.14
  82.6 0.3 collective-permute-start.15
  82.9 1.6 %all-to-all-done.3.refs_3_ = f32[8,1,2048]{2,1,0:T(1,128)S(1)} async-done(((f32[8,1,2048]{2,1,0:T(1,128)}), f32[8,1,2048]{2,1,0:T(1,128)S(1)}, u32[]{:S(2)}, u32[]{:S(2)}) %all-to-all-start.3) | async-done | bytes 65568 | tf_op jit(solution)/shard_map/all_to_all | solution.py:701
  84.5 9.5 %repel.1 = (f32[48,384]{1,0:T(8,128)S(1)}, bf16[48,384]{1,0:T(8,128)(2,1)S(1)}, bf16[48,384]{1,0:T(8,128)(2,1)S(1)}, bf16[48,384]{1,0:T(8,128)(2,1)S(1)}) custom-call(s32[2]{0:T(128)S(1)} %pad_add_fusion.refs_0_, bf16[192,256]{1,0:T(8,128)(2,1)S(1)} %get-tuple-element.23.refs_1_, f32[32,1,256]{2,1,0:T(1,128)S(1)} %all-to-all-done.refs_4_.refs_2_, ...), custom_call_target="tpu_custom_call" | custom-call | flops 3221225472 | bytes 8388608 | tf_op jit(solution)/shard_map/repel/pallas_call | solution.py:246
  94.0 0.1 collective-permute-start.18
  94.1 1.5 %collective-permute-start.19 = (bf16[48,384]{1,0:T(8,128)(2,1)S(1)}, bf16[48,384]{1,0:T(8,128)(2,1)S(1)}, u32[]{:S(2)}, u32[]{:S(2)}) collective-permute-start(bf16[48,384]{1,0:T(8,128)(2,1)S(1)} %get-tuple-element.39), channel_id=1, source_target_pairs={{0,2},{1,3},{2,0},{3,1},{4,6},{5,7},{6,4},{7,5},{8,10},{9,11},{10,... | collective-permute-start | bytes 110600 | tf_op jit(solution)/shard_map/ppermute | solution.py:671
  95.6 0.0 collective-permute-done.13.rest_1_
  95.6 0.3 collective-permute-start.20
  95.9 0.0 collective-permute-done.14.rest_2_
  95.9 0.0 collective-permute-done.15.rest_3_
  95.9 1.9 %collective-permute-done.18.rest_5_ = bf16[48,384]{1,0:T(8,128)(2,1)S(1)} collective-permute-done((bf16[48,384]{1,0:T(8,128)(2,1)S(1)}, bf16[48,384]{1,0:T(8,128)(2,1)S(1)}, u32[]{:S(2)}, u32[]{:S(2)}) %collective-permute-start.18) | collective-permute-done | bytes 36896 | tf_op jit(solution)/shard_map/ppermute | solution.py:671
  97.8 0.4 collective-permute-done.19.rest_6_
  98.2 0.0 collective-permute-done.20.rest_7_
  98.2 0.8 finish.1
  (9 shorter events, 0.1 us)
Async XLA Ops:
  1.0 6.7 %collective-permute-start.3 = (bf16[96,256]{1,0:T(8,128)(2,1)S(1)}, bf16[96,256]{1,0:T(8,128)(2,1)S(1)}, u32[]{:S(2)}, u32[]{:S(2)}) collective-permute-start(bf16[96,256]{1,0:T(8,128)(2,1)S(1)} %get-tuple-element.24), channel_id=1, source_target_pairs={{0,16},{4,20},{8,24},{12,28},{16,0},{20,4},{24,8},{28,12},{1,17},{... | collective-permute-start | bytes 147464 | tf_op jit(solution)/shard_map/ppermute | solution.py:671
  5.1 7.0 %collective-permute-start = (bf16[48,1536]{1,0:T(8,128)(2,1)}, bf16[48,1536]{1,0:T(8,128)(2,1)S(1)}, u32[]{:S(2)}, u32[]{:S(2)}) collective-permute-start(bf16[48,1536]{1,0:T(8,128)(2,1)} %refs_3_.1), channel_id=1, source_target_pairs={{0,2},{1,3},{2,0},{3,1},{4,6},{5,7},{6,4},{7,5},{8,10},{9,11},{10,... | collective-permute-start | bytes 442376 | tf_op jit(solution)/shard_map/ppermute | solution.py:671
  6.6 9.6 %collective-permute-start.5 = (bf16[512,256]{1,0:T(8,128)(2,1)}, bf16[512,256]{1,0:T(8,128)(2,1)S(1)}, u32[]{:S(2)}, u32[]{:S(2)}) collective-permute-start(bf16[512,256]{1,0:T(8,128)(2,1)} %own_ref.1), channel_id=1, source_target_pairs={{0,2},{1,3},{2,0},{3,1},{4,6},{5,7},{6,4},{7,5},{8,10},{9,11},{10,... | collective-permute-start | bytes 786440 | tf_op jit(solution)/shard_map/ppermute | solution.py:671
  7.8 4.7 %collective-permute-start.4 = (bf16[192,256]{1,0:T(8,128)(2,1)S(1)}, bf16[192,256]{1,0:T(8,128)(2,1)S(1)}, u32[]{:S(2)}, u32[]{:S(2)}) collective-permute-start(bf16[192,256]{1,0:T(8,128)(2,1)S(1)} %maximum_select_fusion.2), channel_id=1, source_target_pairs={{0,8},{4,12},{8,0},{12,4},{16,24},{20,28},{24,16},{28,20},{1,9},{5... | collective-permute-start | bytes 294920 | tf_op jit(solution)/shard_map/ppermute | solution.py:671
  9.2 3.3 %collective-permute-start.1 = (bf16[48,1536]{1,0:T(8,128)(2,1)}, bf16[48,1536]{1,0:T(8,128)(2,1)S(1)}, u32[]{:S(2)}, u32[]{:S(2)}) collective-permute-start(bf16[48,1536]{1,0:T(8,128)(2,1)} %refs_3_.1), channel_id=1, source_target_pairs={{0,1},{1,0},{2,3},{3,2},{4,5},{5,4},{6,7},{7,6},{8,9},{9,8},{10,11... | collective-permute-start | bytes 442376 | tf_op jit(solution)/shard_map/ppermute | solution.py:671
  12.1 4.2 %collective-permute-start.2 = (bf16[48,1536]{1,0:T(8,128)(2,1)S(1)}, bf16[48,1536]{1,0:T(8,128)(2,1)S(1)}, u32[]{:S(2)}, u32[]{:S(2)}) collective-permute-start(bf16[48,1536]{1,0:T(8,128)(2,1)S(1)} %collective-permute-done.refs_4_), channel_id=1, source_target_pairs={{0,1},{1,0},{2,3},{3,2},{4,5},{5,4},{6,7},{7,6},{8,9},{9,8},{10,11... | collective-permute-start | bytes 442376 | tf_op jit(solution)/shard_map/ppermute | solution.py:671
  24.1 7.6 %collective-permute-start.6 = (f32[96,2048]{1,0:T(8,128)}, f32[96,2048]{1,0:T(8,128)S(1)}, u32[]{:S(2)}, u32[]{:S(2)}) collective-permute-start(f32[96,2048]{1,0:T(8,128)} %get-tuple-element.26), channel_id=1, source_target_pairs={{0,1},{1,0},{2,3},{3,2},{4,5},{5,4},{6,7},{7,6},{8,9},{9,8},{10,11... | collective-permute-start | bytes 2359304 | tf_op jit(solution)/shard_map/ppermute | solution.py:671
  24.1 7.3 %collective-permute-start.16 = (bf16[384,256]{1,0:T(8,128)(2,1)S(1)}, bf16[384,256]{1,0:T(8,128)(2,1)S(1)}, u32[]{:S(2)}, u32[]{:S(2)}) collective-permute-start(bf16[384,256]{1,0:T(8,128)(2,1)S(1)} %maximum_select_fusion.1.refs_10_), channel_id=1, source_target_pairs={{0,4},{4,0},{8,12},{12,8},{16,20},{20,16},{24,28},{28,24},{1,5},{5... | collective-permute-start | bytes 589832 | tf_op jit(solution)/shard_map/ppermute | solution.py:671
  25.7 7.7 %collective-permute-start.8 = (bf16[512,256]{1,0:T(8,128)(2,1)}, bf16[512,256]{1,0:T(8,128)(2,1)S(1)}, u32[]{:S(2)}, u32[]{:S(2)}) collective-permute-start(bf16[512,256]{1,0:T(8,128)(2,1)} %own_ref.1), channel_id=1, source_target_pairs={{0,1},{1,0},{2,3},{3,2},{4,5},{5,4},{6,7},{7,6},{8,9},{9,8},{10,11... | collective-permute-start | bytes 786440 | tf_op jit(solution)/shard_map/ppermute | solution.py:671
  25.9 10.5 %collective-permute-start.9 = (bf16[512,256]{1,0:T(8,128)(2,1)S(1)}, bf16[512,256]{1,0:T(8,128)(2,1)S(1)}, u32[]{:S(2)}, u32[]{:S(2)}) collective-permute-start(bf16[512,256]{1,0:T(8,128)(2,1)S(1)} %collective-permute-done.5.refs_11_.partner_ref), channel_id=1, source_target_pairs={{0,1},{1,0},{2,3},{3,2},{4,5},{5,4},{6,7},{7,6},{8,9},{9,8},{10,11... | collective-permute-start | bytes 786440 | tf_op jit(solution)/shard_map/ppermute | solution.py:671
  26.2 10.1 %all-to-all-start = ((f32[32,1,256]{2,1,0:T(1,128)}), f32[32,1,256]{2,1,0:T(1,128)S(1)}, u32[]{:S(2)}, u32[]{:S(2)}) async-start(f32[32,1,256]{2,1,0:T(1,128)} %get-tuple-element.34), calls=%async_computation | async-start | bytes 65536 | tf_op jit(solution)/shard_map/all_to_all | solution.py:701
  31.6 4.8 %collective-permute-start.17 = (bf16[768,256]{1,0:T(8,128)(2,1)S(1)}, bf16[768,256]{1,0:T(8,128)(2,1)}, u32[]{:S(2)}, u32[]{:S(2)}) collective-permute-start(bf16[768,256]{1,0:T(8,128)(2,1)S(1)} %maximum_select_fusion.refs_2_), channel_id=1, source_target_pairs={{0,1},{1,0},{2,3},{3,2},{4,5},{5,4},{6,7},{7,6},{8,9},{9,8},{10,11... | collective-permute-start | bytes 1179656 | tf_op jit(solution)/shard_map/ppermute | solution.py:671
  31.8 14.0 %collective-permute-start.7 = (f32[48,2048]{1,0:T(8,128)S(1)}, f32[48,2048]{1,0:T(8,128)}, u32[]{:S(2)}, u32[]{:S(2)}) collective-permute-start(f32[48,2048]{1,0:T(8,128)S(1)} %slice_add_fusion.refs_5_), channel_id=1, source_target_pairs={{0,2},{1,3},{2,0},{3,1},{4,6},{5,7},{6,4},{7,5},{8,10},{9,11},{10,... | collective-permute-start | bytes 1179656 | tf_op jit(solution)/shard_map/ppermute | solution.py:671
  43.2 10.8 %all-to-all-start.1 = ((bf16[32,16,128]{2,1,0:T(8,128)(2,1)}), bf16[32,16,128]{2,1,0:T(8,128)(2,1)S(1)}, u32[]{:S(2)}, u32[]{:S(2)}) async-start(bf16[32,16,128]{2,1,0:T(8,128)(2,1)} %get-tuple-element.36), calls=%async_computation.1 | async-start | bytes 262144 | tf_op jit(solution)/shard_map/all_to_all | solution.py:701
  47.4 13.6 %collective-permute-start.12 = (bf16[48,256]{1,0:T(8,128)(2,1)S(1)}, bf16[48,256]{1,0:T(8,128)(2,1)S(1)}, u32[]{:S(2)}, u32[]{:S(2)}) collective-permute-start(bf16[48,256]{1,0:T(8,128)(2,1)S(1)} %get-tuple-element.29.refs_2_), channel_id=1, source_target_pairs={{0,3},{1,2},{2,1},{3,0},{4,7},{5,6},{6,5},{7,4},{8,11},{9,10},{10,... | collective-permute-start | bytes 73736 | tf_op jit(solution)/shard_map/ppermute | solution.py:671
  48.9 12.1 %collective-permute-start.11 = (bf16[48,256]{1,0:T(8,128)(2,1)S(1)}, bf16[48,256]{1,0:T(8,128)(2,1)S(1)}, u32[]{:S(2)}, u32[]{:S(2)}) collective-permute-start(bf16[48,256]{1,0:T(8,128)(2,1)S(1)} %get-tuple-element.29.refs_2_), channel_id=1, source_target_pairs={{0,2},{1,3},{2,0},{3,1},{4,6},{5,7},{6,4},{7,5},{8,10},{9,11},{10,... | collective-permute-start | bytes 73736 | tf_op jit(solution)/shard_map/ppermute | solution.py:671
  49.3 11.7 %collective-permute-start.10 = (bf16[48,256]{1,0:T(8,128)(2,1)S(1)}, bf16[48,256]{1,0:T(8,128)(2,1)S(1)}, u32[]{:S(2)}, u32[]{:S(2)}) collective-permute-start(bf16[48,256]{1,0:T(8,128)(2,1)S(1)} %get-tuple-element.29.refs_2_), channel_id=1, source_target_pairs={{0,1},{1,0},{2,3},{3,2},{4,5},{5,4},{6,7},{7,6},{8,9},{9,8},{10,11... | collective-permute-start | bytes 73736 | tf_op jit(solution)/shard_map/ppermute | solution.py:671
  58.4 10.8 %all-to-all-start.2 = ((bf16[32,16,128]{2,1,0:T(8,128)(2,1)}), bf16[32,16,128]{2,1,0:T(8,128)(2,1)S(1)}, u32[]{:S(2)}, u32[]{:S(2)}) async-start(bf16[32,16,128]{2,1,0:T(8,128)(2,1)} %next_sweep.1), calls=%async_computation.2 | async-start | bytes 262144 | tf_op jit(solution)/shard_map/all_to_all | solution.py:701
  73.0 11.5 %all-to-all-start.3 = ((f32[8,1,2048]{2,1,0:T(1,128)}), f32[8,1,2048]{2,1,0:T(1,128)S(1)}, u32[]{:S(2)}, u32[]{:S(2)}) async-start(f32[8,1,2048]{2,1,0:T(1,128)} %last_scales.1), calls=%async_computation.3 | async-start | bytes 131072 | tf_op jit(solution)/shard_map/all_to_all | solution.py:701
  80.9 14.7 %collective-permute-start.13 = (f32[48,512]{1,0:T(8,128)S(1)}, f32[48,512]{1,0:T(8,128)S(1)}, u32[]{:S(2)}, u32[]{:S(2)}) collective-permute-start(f32[48,512]{1,0:T(8,128)S(1)} %get-tuple-element.31), channel_id=1, source_target_pairs={{0,3},{1,2},{2,1},{3,0},{4,7},{5,6},{6,5},{7,4},{8,11},{9,10},{10,... | collective-permute-start | bytes 294920 | tf_op jit(solution)/shard_map/ppermute | solution.py:671
  82.0 14.0 %collective-permute-start.14 = (f32[48,512]{1,0:T(8,128)S(1)}, f32[48,512]{1,0:T(8,128)S(1)}, u32[]{:S(2)}, u32[]{:S(2)}) collective-permute-start(f32[48,512]{1,0:T(8,128)S(1)} %get-tuple-element.32), channel_id=1, source_target_pairs={{0,2},{1,3},{2,0},{3,1},{4,6},{5,7},{6,4},{7,5},{8,10},{9,11},{10,... | collective-permute-start | bytes 294920 | tf_op jit(solution)/shard_map/ppermute | solution.py:671
  82.6 13.4 %collective-permute-start.15 = (f32[48,512]{1,0:T(8,128)S(1)}, f32[48,512]{1,0:T(8,128)S(1)}, u32[]{:S(2)}, u32[]{:S(2)}) collective-permute-start(f32[48,512]{1,0:T(8,128)S(1)} %get-tuple-element.33), channel_id=1, source_target_pairs={{0,1},{1,0},{2,3},{3,2},{4,5},{5,4},{6,7},{7,6},{8,9},{9,8},{10,11... | collective-permute-start | bytes 294920 | tf_op jit(solution)/shard_map/ppermute | solution.py:671
  94.0 3.8 %collective-permute-start.18 = (bf16[48,384]{1,0:T(8,128)(2,1)S(1)}, bf16[48,384]{1,0:T(8,128)(2,1)S(1)}, u32[]{:S(2)}, u32[]{:S(2)}) collective-permute-start(bf16[48,384]{1,0:T(8,128)(2,1)S(1)} %get-tuple-element.38), channel_id=1, source_target_pairs={{0,3},{1,2},{2,1},{3,0},{4,7},{5,6},{6,5},{7,4},{8,11},{9,10},{10,... | collective-permute-start | bytes 110600 | tf_op jit(solution)/shard_map/ppermute | solution.py:671
  94.1 4.2 %collective-permute-start.19 = (bf16[48,384]{1,0:T(8,128)(2,1)S(1)}, bf16[48,384]{1,0:T(8,128)(2,1)S(1)}, u32[]{:S(2)}, u32[]{:S(2)}) collective-permute-start(bf16[48,384]{1,0:T(8,128)(2,1)S(1)} %get-tuple-element.39), channel_id=1, source_target_pairs={{0,2},{1,3},{2,0},{3,1},{4,6},{5,7},{6,4},{7,5},{8,10},{9,11},{10,... | collective-permute-start | bytes 110600 | tf_op jit(solution)/shard_map/ppermute | solution.py:671
  95.6 2.6 %collective-permute-start.20 = (bf16[48,384]{1,0:T(8,128)(2,1)S(1)}, bf16[48,384]{1,0:T(8,128)(2,1)S(1)}, u32[]{:S(2)}, u32[]{:S(2)}) collective-permute-start(bf16[48,384]{1,0:T(8,128)(2,1)S(1)} %get-tuple-element.40), channel_id=1, source_target_pairs={{0,1},{1,0},{2,3},{3,2},{4,5},{5,4},{6,7},{7,6},{8,9},{9,8},{10,11... | collective-permute-start | bytes 110600 | tf_op jit(solution)/shard_map/ppermute | solution.py:671

commit v21 on v20

--- a/solution.py
+++ b/solution.py
@@ -746,7 +746,7 @@
     slots = attract(student_emb, state, protos, 6 * eighth, 2 * eighth, 2, proto_size)
     attract_parts = send_blocks(slots)
 
-    copies, weights = first_sweep(thin_ref, protos, mine, other, all_tops, (x_sent, *thirds[2:]), devices, thin, protos_total)
+    copies, weights = first_sweep(thin_ref, protos, mine, other, all_tops, (x_sent,), devices, thin, protos_total)
     for _ in range(ITERS - 2):
         copies = next_sweep(weights, all_to_all(copies, BOTH), (rounded,), protos_total)
     scale_copies = last_scales(weights, all_to_all(copies, BOTH), (state,), batch_size, protos_total)

time: 99.5 us -> 99.1 us (level)
  transfers between devices with their start and end apart: 25 -> 25, of which waited for: 11 -> 11; matrix products, arithmetic and copies ran while one was open for 0% -> 0% of each run, Pallas kernels for 33% -> 32%
where the time goes in v21:
time: 99.1 us; the launch traced here: 98.6 us
  Pallas kernels  45.1 us (46%)
  starting transfers between devices  29.7 us (30%)
  waiting for transfers between devices  22.4 us (23%)
    ppermute x21, starting transfers between devices, swap(): lax.ppermute(values, axis, [(i, i ^ flip) for i in range(lax.axis_size(ax...  17 us
    all_to_all x4, starting transfers between devices, all_to_all(): return lax.all_to_all(copies, axes, 0, 0, tiled=True)  12.7 us
    ppermute x21, waiting for transfers between devices, swap(): lax.ppermute(values, axis, [(i, i ^ flip) for i in range(lax.axis_size(ax...  12.6 us
    pallas_call x2, Pallas kernels, attract(): pl.pallas_call(functools.partial(attract_kernel, first_row, outputs > 1),...  10.2 us
    all_to_all x4, waiting for transfers between devices, all_to_all(): return lax.all_to_all(copies, axes, 0, 0, tiled=True)  9.78 us
    pallas_call x1, Pallas kernels, repel(): pl.pallas_call(skipping(functools.partial(repel_kernel, proto_size), 5, l...  9.46 us
    pallas_call x1, Pallas kernels, front(): pl.pallas_call(skipping(front_kernel, 10, len(order)), in_specs=[whole(pl...  7.76 us
    pallas_call x1, Pallas kernels, first_sweep(): pl.pallas_call(skipping(functools.partial(first_sweep_kernel, chunk, prot...  6.02 us
  transfers between devices with their start and end apart: 25, of which 11 were waited for; matrix products, arithmetic and copies ran while one was open for 0% of the time, Pallas kernels for 32%

profile of v21, /device:TPU:0, one launch (start us, length us, event | category | flops | bytes accessed | tf_op | source)
XLA Modules:
  0.0 98.6 jit_solution(16758087209451212437)
XLA Ops:
  0.0 1.0 %teacher_units.1 = (bf16[192,256]{1,0:T(8,128)(2,1)S(1)}, bf16[96,256]{1,0:T(8,128)(2,1)S(1)}) custom-call(s32[1]{0:T(128)} %bitcast.1.core_ref, bf16[192,256]{1,0:T(8,128)(2,1)} %emb_ref.1), custom_call_target="tpu_custom_call" | custom-call | flops 196608 | bytes 393216 | tf_op jit(solution)/shard_map/teacher_units/pallas_call | solution.py:96
  1.0 4.1 %collective-permute-start.3 = (bf16[96,256]{1,0:T(8,128)(2,1)S(1)}, bf16[96,256]{1,0:T(8,128)(2,1)S(1)}, u32[]{:S(2)}, u32[]{:S(2)}) collective-permute-start(bf16[96,256]{1,0:T(8,128)(2,1)S(1)} %get-tuple-element.24), channel_id=1, source_target_pairs={{0,16},{4,20},{8,24},{12,28},{16,0},{20,4},{24,8},{28,12},{1,17},{... | collective-permute-start | bytes 147464 | tf_op jit(solution)/shard_map/ppermute | solution.py:671
  5.1 1.5 %collective-permute-start = (bf16[48,1536]{1,0:T(8,128)(2,1)}, bf16[48,1536]{1,0:T(8,128)(2,1)S(1)}, u32[]{:S(2)}, u32[]{:S(2)}) collective-permute-start(bf16[48,1536]{1,0:T(8,128)(2,1)} %refs_3_.1), channel_id=1, source_target_pairs={{0,2},{1,3},{2,0},{3,1},{4,6},{5,7},{6,4},{7,5},{8,10},{9,11},{10,... | collective-permute-start | bytes 442376 | tf_op jit(solution)/shard_map/ppermute | solution.py:671
  6.6 0.5 collective-permute-start.5
  7.2 0.6 collective-permute-done.3
  7.8 1.4 %collective-permute-start.4 = (bf16[192,256]{1,0:T(8,128)(2,1)S(1)}, bf16[192,256]{1,0:T(8,128)(2,1)S(1)}, u32[]{:S(2)}, u32[]{:S(2)}) collective-permute-start(bf16[192,256]{1,0:T(8,128)(2,1)S(1)} %maximum_select_fusion.2), channel_id=1, source_target_pairs={{0,8},{4,12},{8,0},{12,4},{16,24},{20,28},{24,16},{28,20},{1,9},{5... | collective-permute-start | bytes 294920 | tf_op jit(solution)/shard_map/ppermute | solution.py:671
  9.2 0.0 collective-permute-start.1
  9.2 2.9 %collective-permute-done.refs_4_ = bf16[48,1536]{1,0:T(8,128)(2,1)S(1)} collective-permute-done((bf16[48,1536]{1,0:T(8,128)(2,1)}, bf16[48,1536]{1,0:T(8,128)(2,1)S(1)}, u32[]{:S(2)}, u32[]{:S(2)}) %collective-permute-start) | collective-permute-done | bytes 147488 | tf_op jit(solution)/shard_map/ppermute | solution.py:671
  12.1 0.0 collective-permute-start.2
  12.1 0.3 collective-permute-done.4
  12.4 0.1 maximum_select_fusion.1.refs_10_
  12.5 0.0 collective-permute-done.1.refs_5_
  12.5 3.8 %collective-permute-done.5.refs_11_.partner_ref = bf16[512,256]{1,0:T(8,128)(2,1)S(1)} collective-permute-done((bf16[512,256]{1,0:T(8,128)(2,1)}, bf16[512,256]{1,0:T(8,128)(2,1)S(1)}, u32[]{:S(2)}, u32[]{:S(2)}) %collective-permute-start.5) | collective-permute-done | bytes 262176 | tf_op jit(solution)/shard_map/ppermute | solution.py:671
  16.3 0.0 collective-permute-done.2.refs_6_
  16.3 7.8 %front.1 = (f32[32,1,256]{2,1,0:T(1,128)}, f32[96,2048]{1,0:T(8,128)S(1)}, f32[96,2048]{1,0:T(8,128)}) custom-call(s32[1]{0:T(128)} %bitcast.refs_0_.index_ref, bf16[192,256]{1,0:T(8,128)(2,1)S(1)} %get-tuple-element.23.refs_1_, f32[1,2048]{1,0:T(1,128)} %bitcast.7, bf16[48,1536]{1,0:T(8,128)(2,1)} %refs_3_.1, ...), custom_call_target="tpu_custom_call" | custom-call | flops 2315255808 | bytes 8388608 | tf_op jit(solution)/shard_map/front/pallas_call | solution.py:161
  24.1 0.1 collective-permute-start.6
  24.1 1.6 %collective-permute-start.16 = (bf16[384,256]{1,0:T(8,128)(2,1)S(1)}, bf16[384,256]{1,0:T(8,128)(2,1)S(1)}, u32[]{:S(2)}, u32[]{:S(2)}) collective-permute-start(bf16[384,256]{1,0:T(8,128)(2,1)S(1)} %maximum_select_fusion.1.refs_10_), channel_id=1, source_target_pairs={{0,4},{4,0},{8,12},{12,8},{16,20},{20,16},{24,28},{28,24},{1,5},{5... | collective-permute-start | bytes 589832 | tf_op jit(solution)/shard_map/ppermute | solution.py:671
  25.7 0.2 collective-permute-start.8
  25.9 2.9 %all-to-all-start = ((f32[32,1,256]{2,1,0:T(1,128)}), f32[32,1,256]{2,1,0:T(1,128)S(1)}, u32[]{:S(2)}, u32[]{:S(2)}) async-start(f32[32,1,256]{2,1,0:T(1,128)} %get-tuple-element.34), calls=%async_computation | async-start | bytes 65536 | tf_op jit(solution)/shard_map/all_to_all | solution.py:701
  28.8 2.7 %collective-permute-done.16 = bf16[384,256]{1,0:T(8,128)(2,1)S(1)} collective-permute-done((bf16[384,256]{1,0:T(8,128)(2,1)S(1)}, bf16[384,256]{1,0:T(8,128)(2,1)S(1)}, u32[]{:S(2)}, u32[]{:S(2)}) %collective-permute-start.16) | collective-permute-done | bytes 196640 | tf_op jit(solution)/shard_map/ppermute | solution.py:671
  31.5 0.2 maximum_select_fusion.refs_2_
  31.6 0.1 collective-permute-start.17
  31.7 0.0 collective-permute-done.6.core_ref
  31.8 1.5 %collective-permute-start.7 = (f32[48,2048]{1,0:T(8,128)S(1)}, f32[48,2048]{1,0:T(8,128)S(1)}, u32[]{:S(2)}, u32[]{:S(2)}) collective-permute-start(f32[48,2048]{1,0:T(8,128)S(1)} %slice_add_fusion.refs_5_), channel_id=1, source_target_pairs={{0,2},{1,3},{2,0},{3,1},{4,6},{5,7},{6,4},{7,5},{8,10},{9,11},{10,... | collective-permute-start | bytes 1179656 | tf_op jit(solution)/shard_map/ppermute | solution.py:671
  33.3 0.1 pad_add_fusion.1.refs_0_
  33.4 0.2 collective-permute-start.9
  33.6 2.4 %all-to-all-done.refs_4_.refs_2_ = f32[32,1,256]{2,1,0:T(1,128)S(1)} async-done(((f32[32,1,256]{2,1,0:T(1,128)}), f32[32,1,256]{2,1,0:T(1,128)S(1)}, u32[]{:S(2)}, u32[]{:S(2)}) %all-to-all-start) | async-done | bytes 32800 | tf_op jit(solution)/shard_map/all_to_all | solution.py:701
  36.0 0.0 collective-permute-done.17.refs_3_
  36.0 6.0 %first_sweep.1 = (bf16[32,16,128]{2,1,0:T(8,128)(2,1)S(1)}, bf16[2048,1536]{1,0:T(8,128)(2,1)}) custom-call(s32[2]{0:T(128)S(1)} %pad_add_fusion.1.refs_0_, bf16[16384,256]{1,0:T(8,128)(2,1)} %refs_4_.1, bf16[768,256]{1,0:T(8,128)(2,1)S(1)} %maximum_select_fusion.refs_2_, bf16[768,256]{1,0:T(8,128)(2,1)S(1)} %collective-permute-done.17.refs_3_, ...), custom_call_target="tpu_custom_call" | custom-call | flops 1610612736 | bytes 6291456 | tf_op jit(solution)/shard_map/first_sweep/pallas_call | solution.py:453
  42.1 0.6 copy-done
  42.7 2.6 %all-to-all-start.1 = ((bf16[32,16,128]{2,1,0:T(8,128)(2,1)}), bf16[32,16,128]{2,1,0:T(8,128)(2,1)S(1)}, u32[]{:S(2)}, u32[]{:S(2)}) async-start(bf16[32,16,128]{2,1,0:T(8,128)(2,1)} %copy-done), calls=%async_computation.1 | async-start | bytes 262144 | tf_op jit(solution)/shard_map/all_to_all | solution.py:701
  45.3 0.0 collective-permute-done.8.other_ref
  45.3 0.0 collective-permute-done.9.last_ref
  45.3 0.0 collective-permute-done.7.x_ref
  45.3 1.7 %student_middle.1 = (f32[48,256]{1,0:T(8,128)S(1)}, bf16[48,256]{1,0:T(8,128)(2,1)S(1)}, f32[48,128]{1,0:T(8,128)S(1)}) custom-call(s32[1]{0:T(128)} %bitcast.refs_0_.index_ref, f32[96,2048]{1,0:T(8,128)S(1)} %get-tuple-element.25.keep_ref, f32[96,2048]{1,0:T(8,128)S(1)} %collective-permute-done.6.core_ref, f32[48,2048]{1,0:T(8,128)S(1)} %collective-permute-done.7.x_ref, ...), custom_call_target="tpu_custom_call" | custom-call | flops 50331648 | bytes 2621440 | tf_op jit(solution)/shard_map/student_middle/pallas_call | solution.py:619
  47.0 1.5 %collective-permute-start.12 = (bf16[48,256]{1,0:T(8,128)(2,1)S(1)}, bf16[48,256]{1,0:T(8,128)(2,1)S(1)}, u32[]{:S(2)}, u32[]{:S(2)}) collective-permute-start(bf16[48,256]{1,0:T(8,128)(2,1)S(1)} %get-tuple-element.29.refs_2_), channel_id=1, source_target_pairs={{0,3},{1,2},{2,1},{3,0},{4,7},{5,6},{6,5},{7,4},{8,11},{9,10},{10,... | collective-permute-start | bytes 73736 | tf_op jit(solution)/shard_map/ppermute | solution.py:671
  48.5 0.4 collective-permute-start.11
  48.8 0.1 collective-permute-start.10
  49.0 4.5 %all-to-all-done.1.refs_1_ = bf16[32,16,128]{2,1,0:T(8,128)(2,1)S(1)} async-done(((bf16[32,16,128]{2,1,0:T(8,128)(2,1)}), bf16[32,16,128]{2,1,0:T(8,128)(2,1)S(1)}, u32[]{:S(2)}, u32[]{:S(2)}) %all-to-all-start.1) | async-done | bytes 131104 | tf_op jit(solution)/shard_map/all_to_all | solution.py:701
  53.5 4.4 %next_sweep.1 = bf16[32,16,128]{2,1,0:T(8,128)(2,1)} custom-call(bf16[2048,1536]{1,0:T(8,128)(2,1)} %get-tuple-element.35.refs_0_, bf16[32,16,128]{2,1,0:T(8,128)(2,1)S(1)} %all-to-all-done.1.refs_1_, bf16[48,256]{1,0:T(8,128)(2,1)S(1)} %get-tuple-element.29.refs_2_), custom_call_target="tpu_custom_call" | custom-call | flops 25165824 | bytes 6291456 | tf_op jit(solution)/shard_map/next_sweep/pallas_call | solution.py:539
  57.9 2.6 %all-to-all-start.2 = ((bf16[32,16,128]{2,1,0:T(8,128)(2,1)}), bf16[32,16,128]{2,1,0:T(8,128)(2,1)S(1)}, u32[]{:S(2)}, u32[]{:S(2)}) async-start(bf16[32,16,128]{2,1,0:T(8,128)(2,1)} %next_sweep.1), calls=%async_computation.2 | async-start | bytes 262144 | tf_op jit(solution)/shard_map/all_to_all | solution.py:701
  60.5 0.0 collective-permute-done.10
  60.5 0.0 collective-permute-done.11
  60.5 0.0 collective-permute-done.12
  60.6 6.9 %attract.2.state_ref.refs_2_ = f32[192,512]{1,0:T(8,128)S(1)} custom-call(bf16[192,256]{1,0:T(8,128)(2,1)S(1)} %constant_dynamic-update-slice_fusion.emb_ref, f32[192,512]{1,0:T(8,128)S(1)} %concatenate.32.state_ref, bf16[16384,256]{1,0:T(8,128)(2,1)} %refs_4_.1), custom_call_target="tpu_custom_call" | custom-call | flops 2415919104 | bytes 6291456 | tf_op jit(solution)/shard_map/attract/pallas_call | solution.py:327
  67.5 1.2 %all-to-all-done.2.refs_1_ = bf16[32,16,128]{2,1,0:T(8,128)(2,1)S(1)} async-done(((bf16[32,16,128]{2,1,0:T(8,128)(2,1)}), bf16[32,16,128]{2,1,0:T(8,128)(2,1)S(1)}, u32[]{:S(2)}, u32[]{:S(2)}) %all-to-all-start.2) | async-done | bytes 131104 | tf_op jit(solution)/shard_map/all_to_all | solution.py:701
  68.7 3.8 %last_scales.1 = f32[8,1,2048]{2,1,0:T(1,128)} custom-call(bf16[2048,1536]{1,0:T(8,128)(2,1)} %get-tuple-element.35.refs_0_, bf16[32,16,128]{2,1,0:T(8,128)(2,1)S(1)} %all-to-all-done.2.refs_1_, f32[192,512]{1,0:T(8,128)S(1)} %attract.2.state_ref.refs_2_), custom_call_target="tpu_custom_call" | custom-call | flops 12582912 | bytes 6291456 | tf_op jit(solution)/shard_map/last_scales/pallas_call | solution.py:578
  72.5 4.7 %all-to-all-start.3 = ((f32[8,1,2048]{2,1,0:T(1,128)}), f32[8,1,2048]{2,1,0:T(1,128)S(1)}, u32[]{:S(2)}, u32[]{:S(2)}) async-start(f32[8,1,2048]{2,1,0:T(1,128)} %last_scales.1), calls=%async_computation.3 | async-start | bytes 131072 | tf_op jit(solution)/shard_map/all_to_all | solution.py:701
  77.2 0.1 pad_add_fusion.refs_0_
  77.2 3.3 %attract.3 = (f32[48,512]{1,0:T(8,128)S(1)}, f32[48,512]{1,0:T(8,128)S(1)}, f32[48,512]{1,0:T(8,128)S(1)}, f32[48,512]{1,0:T(8,128)S(1)}) custom-call(bf16[192,256]{1,0:T(8,128)(2,1)S(1)} %constant_dynamic-update-slice_fusion.emb_ref, f32[192,512]{1,0:T(8,128)S(1)} %attract.2.state_ref.refs_2_, bf16[16384,256]{1,0:T(8,128)(2,1)} %refs_4_.1), custom_call_target="tpu_custom_call" | custom-call | flops 805306368 | bytes 2097152 | tf_op jit(solution)/shard_map/attract/pallas_call | solution.py:327
  80.5 1.0 %collective-permute-start.13 = (f32[48,512]{1,0:T(8,128)S(1)}, f32[48,512]{1,0:T(8,128)S(1)}, u32[]{:S(2)}, u32[]{:S(2)}) collective-permute-start(f32[48,512]{1,0:T(8,128)S(1)} %get-tuple-element.31), channel_id=1, source_target_pairs={{0,3},{1,2},{2,1},{3,0},{4,7},{5,6},{6,5},{7,4},{8,11},{9,10},{10,... | collective-permute-start | bytes 294920 | tf_op jit(solution)/shard_map/ppermute | solution.py:671
  81.5 0.6 collective-permute-start.14
  82.1 0.3 collective-permute-start.15
  82.4 1.6 %all-to-all-done.3.refs_3_ = f32[8,1,2048]{2,1,0:T(1,128)S(1)} async-done(((f32[8,1,2048]{2,1,0:T(1,128)}), f32[8,1,2048]{2,1,0:T(1,128)S(1)}, u32[]{:S(2)}, u32[]{:S(2)}) %all-to-all-start.3) | async-done | bytes 65568 | tf_op jit(solution)/shard_map/all_to_all | solution.py:701
  84.1 9.5 %repel.1 = (f32[48,384]{1,0:T(8,128)S(1)}, bf16[48,384]{1,0:T(8,128)(2,1)S(1)}, bf16[48,384]{1,0:T(8,128)(2,1)S(1)}, bf16[48,384]{1,0:T(8,128)(2,1)S(1)}) custom-call(s32[2]{0:T(128)S(1)} %pad_add_fusion.refs_0_, bf16[192,256]{1,0:T(8,128)(2,1)S(1)} %copy-done.2, f32[32,1,256]{2,1,0:T(1,128)S(1)} %all-to-all-done.refs_4_.refs_2_, ...), custom_call_target="tpu_custom_call" | custom-call | flops 3221225472 | bytes 8388608 | tf_op jit(solution)/shard_map/repel/pallas_call | solution.py:246
  93.5 0.1 collective-permute-start.18
  93.6 1.5 %collective-permute-start.19 = (bf16[48,384]{1,0:T(8,128)(2,1)S(1)}, bf16[48,384]{1,0:T(8,128)(2,1)S(1)}, u32[]{:S(2)}, u32[]{:S(2)}) collective-permute-start(bf16[48,384]{1,0:T(8,128)(2,1)S(1)} %get-tuple-element.39), channel_id=1, source_target_pairs={{0,2},{1,3},{2,0},{3,1},{4,6},{5,7},{6,4},{7,5},{8,10},{9,11},{10,... | collective-permute-start | bytes 110600 | tf_op jit(solution)/shard_map/ppermute | solution.py:671
  95.2 0.0 collective-permute-done.13.rest_1_
  95.2 0.3 collective-permute-start.20
  95.5 0.0 collective-permute-done.14.rest_2_
  95.5 0.0 collective-permute-done.15.rest_3_
  95.5 1.9 %collective-permute-done.18.rest_5_ = bf16[48,384]{1,0:T(8,128)(2,1)S(1)} collective-permute-done((bf16[48,384]{1,0:T(8,128)(2,1)S(1)}, bf16[48,384]{1,0:T(8,128)(2,1)S(1)}, u32[]{:S(2)}, u32[]{:S(2)}) %collective-permute-start.18) | collective-permute-done | bytes 36896 | tf_op jit(solution)/shard_map/ppermute | solution.py:671
  97.3 0.4 collective-permute-done.19.rest_6_
  97.8 0.8 finish.1
  (15 shorter events, 0.1 us)
Async XLA Ops:
  1.0 23.0 %copy-start.1 = (bf16[192,256]{1,0:T(8,128)(2,1)}, bf16[192,256]{1,0:T(8,128)(2,1)S(1)}, u32[]{:S(2)}) copy-start(bf16[192,256]{1,0:T(8,128)(2,1)S(1)} %get-tuple-element.23.refs_1_) | copy-start | bytes 294916
  1.0 6.7 %collective-permute-start.3 = (bf16[96,256]{1,0:T(8,128)(2,1)S(1)}, bf16[96,256]{1,0:T(8,128)(2,1)S(1)}, u32[]{:S(2)}, u32[]{:S(2)}) collective-permute-start(bf16[96,256]{1,0:T(8,128)(2,1)S(1)} %get-tuple-element.24), channel_id=1, source_target_pairs={{0,16},{4,20},{8,24},{12,28},{16,0},{20,4},{24,8},{28,12},{1,17},{... | collective-permute-start | bytes 147464 | tf_op jit(solution)/shard_map/ppermute | solution.py:671
  5.1 7.0 %collective-permute-start = (bf16[48,1536]{1,0:T(8,128)(2,1)}, bf16[48,1536]{1,0:T(8,128)(2,1)S(1)}, u32[]{:S(2)}, u32[]{:S(2)}) collective-permute-start(bf16[48,1536]{1,0:T(8,128)(2,1)} %refs_3_.1), channel_id=1, source_target_pairs={{0,2},{1,3},{2,0},{3,1},{4,6},{5,7},{6,4},{7,5},{8,10},{9,11},{10,... | collective-permute-start | bytes 442376 | tf_op jit(solution)/shard_map/ppermute | solution.py:671
  6.6 9.6 %collective-permute-start.5 = (bf16[512,256]{1,0:T(8,128)(2,1)}, bf16[512,256]{1,0:T(8,128)(2,1)S(1)}, u32[]{:S(2)}, u32[]{:S(2)}) collective-permute-start(bf16[512,256]{1,0:T(8,128)(2,1)} %own_ref.1), channel_id=1, source_target_pairs={{0,2},{1,3},{2,0},{3,1},{4,6},{5,7},{6,4},{7,5},{8,10},{9,11},{10,... | collective-permute-start | bytes 786440 | tf_op jit(solution)/shard_map/ppermute | solution.py:671
  7.8 4.7 %collective-permute-start.4 = (bf16[192,256]{1,0:T(8,128)(2,1)S(1)}, bf16[192,256]{1,0:T(8,128)(2,1)S(1)}, u32[]{:S(2)}, u32[]{:S(2)}) collective-permute-start(bf16[192,256]{1,0:T(8,128)(2,1)S(1)} %maximum_select_fusion.2), channel_id=1, source_target_pairs={{0,8},{4,12},{8,0},{12,4},{16,24},{20,28},{24,16},{28,20},{1,9},{5... | collective-permute-start | bytes 294920 | tf_op jit(solution)/shard_map/ppermute | solution.py:671
  9.2 3.3 %collective-permute-start.1 = (bf16[48,1536]{1,0:T(8,128)(2,1)}, bf16[48,1536]{1,0:T(8,128)(2,1)S(1)}, u32[]{:S(2)}, u32[]{:S(2)}) collective-permute-start(bf16[48,1536]{1,0:T(8,128)(2,1)} %refs_3_.1), channel_id=1, source_target_pairs={{0,1},{1,0},{2,3},{3,2},{4,5},{5,4},{6,7},{7,6},{8,9},{9,8},{10,11... | collective-permute-start | bytes 442376 | tf_op jit(solution)/shard_map/ppermute | solution.py:671
  12.1 4.2 %collective-permute-start.2 = (bf16[48,1536]{1,0:T(8,128)(2,1)S(1)}, bf16[48,1536]{1,0:T(8,128)(2,1)S(1)}, u32[]{:S(2)}, u32[]{:S(2)}) collective-permute-start(bf16[48,1536]{1,0:T(8,128)(2,1)S(1)} %collective-permute-done.refs_4_), channel_id=1, source_target_pairs={{0,1},{1,0},{2,3},{3,2},{4,5},{5,4},{6,7},{7,6},{8,9},{9,8},{10,11... | collective-permute-start | bytes 442376 | tf_op jit(solution)/shard_map/ppermute | solution.py:671
  24.1 7.6 %collective-permute-start.6 = (f32[96,2048]{1,0:T(8,128)}, f32[96,2048]{1,0:T(8,128)S(1)}, u32[]{:S(2)}, u32[]{:S(2)}) collective-permute-start(f32[96,2048]{1,0:T(8,128)} %get-tuple-element.26), channel_id=1, source_target_pairs={{0,1},{1,0},{2,3},{3,2},{4,5},{5,4},{6,7},{7,6},{8,9},{9,8},{10,11... | collective-permute-start | bytes 2359304 | tf_op jit(solution)/shard_map/ppermute | solution.py:671
  24.1 7.3 %collective-permute-start.16 = (bf16[384,256]{1,0:T(8,128)(2,1)S(1)}, bf16[384,256]{1,0:T(8,128)(2,1)S(1)}, u32[]{:S(2)}, u32[]{:S(2)}) collective-permute-start(bf16[384,256]{1,0:T(8,128)(2,1)S(1)} %maximum_select_fusion.1.refs_10_), channel_id=1, source_target_pairs={{0,4},{4,0},{8,12},{12,8},{16,20},{20,16},{24,28},{28,24},{1,5},{5... | collective-permute-start | bytes 589832 | tf_op jit(solution)/shard_map/ppermute | solution.py:671
  25.7 19.6 %collective-permute-start.8 = (bf16[512,256]{1,0:T(8,128)(2,1)}, bf16[512,256]{1,0:T(8,128)(2,1)}, u32[]{:S(2)}, u32[]{:S(2)}) collective-permute-start(bf16[512,256]{1,0:T(8,128)(2,1)} %own_ref.1), channel_id=1, source_target_pairs={{0,1},{1,0},{2,3},{3,2},{4,5},{5,4},{6,7},{7,6},{8,9},{9,8},{10,11... | collective-permute-start | bytes 786440 | tf_op jit(solution)/shard_map/ppermute | solution.py:671
  25.9 10.1 %all-to-all-start = ((f32[32,1,256]{2,1,0:T(1,128)}), f32[32,1,256]{2,1,0:T(1,128)S(1)}, u32[]{:S(2)}, u32[]{:S(2)}) async-start(f32[32,1,256]{2,1,0:T(1,128)} %get-tuple-element.34), calls=%async_computation | async-start | bytes 65536 | tf_op jit(solution)/shard_map/all_to_all | solution.py:701
  31.6 4.4 %collective-permute-start.17 = (bf16[768,256]{1,0:T(8,128)(2,1)S(1)}, bf16[768,256]{1,0:T(8,128)(2,1)S(1)}, u32[]{:S(2)}, u32[]{:S(2)}) collective-permute-start(bf16[768,256]{1,0:T(8,128)(2,1)S(1)} %maximum_select_fusion.refs_2_), channel_id=1, source_target_pairs={{0,1},{1,0},{2,3},{3,2},{4,5},{5,4},{6,7},{7,6},{8,9},{9,8},{10,11... | collective-permute-start | bytes 1179656 | tf_op jit(solution)/shard_map/ppermute | solution.py:671
  31.8 13.6 %collective-permute-start.7 = (f32[48,2048]{1,0:T(8,128)S(1)}, f32[48,2048]{1,0:T(8,128)S(1)}, u32[]{:S(2)}, u32[]{:S(2)}) collective-permute-start(f32[48,2048]{1,0:T(8,128)S(1)} %slice_add_fusion.refs_5_), channel_id=1, source_target_pairs={{0,2},{1,3},{2,0},{3,1},{4,6},{5,7},{6,4},{7,5},{8,10},{9,11},{10,... | collective-permute-start | bytes 1179656 | tf_op jit(solution)/shard_map/ppermute | solution.py:671
  33.4 11.9 %collective-permute-start.9 = (bf16[512,256]{1,0:T(8,128)(2,1)S(1)}, bf16[512,256]{1,0:T(8,128)(2,1)}, u32[]{:S(2)}, u32[]{:S(2)}) collective-permute-start(bf16[512,256]{1,0:T(8,128)(2,1)S(1)} %collective-permute-done.5.refs_11_.partner_ref), channel_id=1, source_target_pairs={{0,1},{1,0},{2,3},{3,2},{4,5},{5,4},{6,7},{7,6},{8,9},{9,8},{10,11... | collective-permute-start | bytes 786440 | tf_op jit(solution)/shard_map/ppermute | solution.py:671
  42.0 0.6 copy-start
  42.7 10.8 %all-to-all-start.1 = ((bf16[32,16,128]{2,1,0:T(8,128)(2,1)}), bf16[32,16,128]{2,1,0:T(8,128)(2,1)S(1)}, u32[]{:S(2)}, u32[]{:S(2)}) async-start(bf16[32,16,128]{2,1,0:T(8,128)(2,1)} %copy-done), calls=%async_computation.1 | async-start | bytes 262144 | tf_op jit(solution)/shard_map/all_to_all | solution.py:701
  47.0 13.5 %collective-permute-start.12 = (bf16[48,256]{1,0:T(8,128)(2,1)S(1)}, bf16[48,256]{1,0:T(8,128)(2,1)S(1)}, u32[]{:S(2)}, u32[]{:S(2)}) collective-permute-start(bf16[48,256]{1,0:T(8,128)(2,1)S(1)} %get-tuple-element.29.refs_2_), channel_id=1, source_target_pairs={{0,3},{1,2},{2,1},{3,0},{4,7},{5,6},{6,5},{7,4},{8,11},{9,10},{10,... | collective-permute-start | bytes 73736 | tf_op jit(solution)/shard_map/ppermute | solution.py:671
  48.5 12.0 %collective-permute-start.11 = (bf16[48,256]{1,0:T(8,128)(2,1)S(1)}, bf16[48,256]{1,0:T(8,128)(2,1)S(1)}, u32[]{:S(2)}, u32[]{:S(2)}) collective-permute-start(bf16[48,256]{1,0:T(8,128)(2,1)S(1)} %get-tuple-element.29.refs_2_), channel_id=1, source_target_pairs={{0,2},{1,3},{2,0},{3,1},{4,6},{5,7},{6,4},{7,5},{8,10},{9,11},{10,... | collective-permute-start | bytes 73736 | tf_op jit(solution)/shard_map/ppermute | solution.py:671
  48.8 11.7 %collective-permute-start.10 = (bf16[48,256]{1,0:T(8,128)(2,1)S(1)}, bf16[48,256]{1,0:T(8,128)(2,1)S(1)}, u32[]{:S(2)}, u32[]{:S(2)}) collective-permute-start(bf16[48,256]{1,0:T(8,128)(2,1)S(1)} %get-tuple-element.29.refs_2_), channel_id=1, source_target_pairs={{0,1},{1,0},{2,3},{3,2},{4,5},{5,4},{6,7},{7,6},{8,9},{9,8},{10,11... | collective-permute-start | bytes 73736 | tf_op jit(solution)/shard_map/ppermute | solution.py:671
  57.9 10.8 %all-to-all-start.2 = ((bf16[32,16,128]{2,1,0:T(8,128)(2,1)}), bf16[32,16,128]{2,1,0:T(8,128)(2,1)S(1)}, u32[]{:S(2)}, u32[]{:S(2)}) async-start(bf16[32,16,128]{2,1,0:T(8,128)(2,1)} %next_sweep.1), calls=%async_computation.2 | async-start | bytes 262144 | tf_op jit(solution)/shard_map/all_to_all | solution.py:701
  67.5 16.6 %copy-start.2 = (bf16[192,256]{1,0:T(8,128)(2,1)S(1)}, bf16[192,256]{1,0:T(8,128)(2,1)}, u32[]{:S(2)}) copy-start(bf16[192,256]{1,0:T(8,128)(2,1)} %copy-done.1) | copy-start | bytes 294916
  72.5 11.6 %all-to-all-start.3 = ((f32[8,1,2048]{2,1,0:T(1,128)}), f32[8,1,2048]{2,1,0:T(1,128)S(1)}, u32[]{:S(2)}, u32[]{:S(2)}) async-start(f32[8,1,2048]{2,1,0:T(1,128)} %last_scales.1), calls=%async_computation.3 | async-start | bytes 131072 | tf_op jit(solution)/shard_map/all_to_all | solution.py:701
  80.5 14.7 %collective-permute-start.13 = (f32[48,512]{1,0:T(8,128)S(1)}, f32[48,512]{1,0:T(8,128)S(1)}, u32[]{:S(2)}, u32[]{:S(2)}) collective-permute-start(f32[48,512]{1,0:T(8,128)S(1)} %get-tuple-element.31), channel_id=1, source_target_pairs={{0,3},{1,2},{2,1},{3,0},{4,7},{5,6},{6,5},{7,4},{8,11},{9,10},{10,... | collective-permute-start | bytes 294920 | tf_op jit(solution)/shard_map/ppermute | solution.py:671
  81.5 14.0 %collective-permute-start.14 = (f32[48,512]{1,0:T(8,128)S(1)}, f32[48,512]{1,0:T(8,128)S(1)}, u32[]{:S(2)}, u32[]{:S(2)}) collective-permute-start(f32[48,512]{1,0:T(8,128)S(1)} %get-tuple-element.32), channel_id=1, source_target_pairs={{0,2},{1,3},{2,0},{3,1},{4,6},{5,7},{6,4},{7,5},{8,10},{9,11},{10,... | collective-permute-start | bytes 294920 | tf_op jit(solution)/shard_map/ppermute | solution.py:671
  82.1 13.3 %collective-permute-start.15 = (f32[48,512]{1,0:T(8,128)S(1)}, f32[48,512]{1,0:T(8,128)S(1)}, u32[]{:S(2)}, u32[]{:S(2)}) collective-permute-start(f32[48,512]{1,0:T(8,128)S(1)} %get-tuple-element.33), channel_id=1, source_target_pairs={{0,1},{1,0},{2,3},{3,2},{4,5},{5,4},{6,7},{7,6},{8,9},{9,8},{10,11... | collective-permute-start | bytes 294920 | tf_op jit(solution)/shard_map/ppermute | solution.py:671
  93.5 3.8 %collective-permute-start.18 = (bf16[48,384]{1,0:T(8,128)(2,1)S(1)}, bf16[48,384]{1,0:T(8,128)(2,1)S(1)}, u32[]{:S(2)}, u32[]{:S(2)}) collective-permute-start(bf16[48,384]{1,0:T(8,128)(2,1)S(1)} %get-tuple-element.38), channel_id=1, source_target_pairs={{0,3},{1,2},{2,1},{3,0},{4,7},{5,6},{6,5},{7,4},{8,11},{9,10},{10,... | collective-permute-start | bytes 110600 | tf_op jit(solution)/shard_map/ppermute | solution.py:671
  93.6 4.2 %collective-permute-start.19 = (bf16[48,384]{1,0:T(8,128)(2,1)S(1)}, bf16[48,384]{1,0:T(8,128)(2,1)S(1)}, u32[]{:S(2)}, u32[]{:S(2)}) collective-permute-start(bf16[48,384]{1,0:T(8,128)(2,1)S(1)} %get-tuple-element.39), channel_id=1, source_target_pairs={{0,2},{1,3},{2,0},{3,1},{4,6},{5,7},{6,4},{7,5},{8,10},{9,11},{10,... | collective-permute-start | bytes 110600 | tf_op jit(solution)/shard_map/ppermute | solution.py:671
  95.2 2.6 %collective-permute-start.20 = (bf16[48,384]{1,0:T(8,128)(2,1)S(1)}, bf16[48,384]{1,0:T(8,128)(2,1)S(1)}, u32[]{:S(2)}, u32[]{:S(2)}) collective-permute-start(bf16[48,384]{1,0:T(8,128)(2,1)S(1)} %get-tuple-element.40), channel_id=1, source_target_pairs={{0,1},{1,0},{2,3},{3,2},{4,5},{5,4},{6,7},{7,6},{8,9},{9,8},{10,11... | collective-permute-start | bytes 110600 | tf_op jit(solution)/shard_map/ppermute | solution.py:671
